TPU v7x, 32 devices: a whole 2x2x4 slice. The times are simulated.
32 devices in a mesh: dom: 8 (over z, y), shuf: 4 (over x, core).
Axes of the slice: x: 2, y: 2, z: 4, core: 2. Of those that a mesh axis runs over, the one named last changes fastest.
Arguments:
- features: float32 [8192, 128], P(('dom', 'shuf')), may hold values from -204 to 204
- tile_values: float32 [256, 128, 128], P(('dom', 'shuf')), may hold values from -0.375 to 0.375
- tile_dst: int32 [256], P(('dom', 'shuf')), may hold values from 0 to 1, as said below
- tile_src: int32 [256], P(('dom', 'shuf')), may hold values from 0 to 5
- tile_count: int32 [32], P(('dom', 'shuf')), may hold values from 2 to 8, as said below
- send_left: int32 [64], P(('dom', 'shuf')), may hold values from 0 to 1
- send_right: int32 [64], P(('dom', 'shuf')), may hold values from 0 to 1
- send_count: int32 [32, 2], P(('dom', 'shuf')), may hold values from 1 to 2, as said below
- batch_order: int32 [32, 256], P(('dom', 'shuf')), may hold values from 0 to 255, each once within a row
- labels: int32 [8192], P(('dom', 'shuf')), may hold values from 0 to 171
- w_branch: bfloat16 [4, 128, 1024], replicated, may hold values from -0.5 to 0.5
- w_class: bfloat16 [4096, 172], replicated
Outputs:
- loss_rows: float32 [8192], P(('dom', 'shuf'))
- grad_branch: float32 [4, 128, 1024], P(None, None, 'shuf')
- grad_class: float32 [4096, 172], P('shuf')
Inputs may be any that keep to these rules, and one draw needn't show every extreme that they name: `tile_dst`: in each partition's first 2 tile slots every local block is the destination exactly once. `tile_count`: some partition has all 8 slots live. `send_count`: some list has all 2 slots live.
All inputs are finite; a program needn't handle non-finite values.
Results may differ from a plain program's by a relative error of at most 0.0045.
The roundings to bfloat16 on the way count: a program that leaves them out, or rounds other values in their place, can miss the bound.
Values may be sent and summed in bfloat16 or wider, within the bound.
No kernel may reach another device: no remote copies, remote signals or barrier semaphores. Data moves between devices by JAX's collectives and lax.ppermute only.
A program may use at most 64 MiB of HBM per device.

v0:
```python
import math

import jax
import jax.numpy as jnp
from jax import lax
from jax.sharding import PartitionSpec as P

HOPS = 3


def passed_along(value, axis, steps):
    count = lax.axis_size(axis)
    pairs = [(source, (source + steps) % count) for source in range(count)]
    return lax.ppermute(value, axis, pairs)


def local_terms(batch_rows, labels, w_branch, w_class, row_scale):
    branch_count = batch_rows.shape[0]
    hidden_width = w_branch.shape[2]
    branch_pre = [
        jnp.dot(
            batch_rows[branch_index], w_branch[branch_index], preferred_element_type=jnp.float32
        )
        for branch_index in range(branch_count)
    ]
    hidden = jnp.concatenate(
        [jax.nn.relu(branch_value) for branch_value in branch_pre], axis=1
    ).astype(jnp.bfloat16)
    logits = jnp.dot(hidden, w_class, preferred_element_type=jnp.float32)
    row_max = jnp.max(logits, axis=1, keepdims=True)
    log_total = row_max[:, 0] + jnp.log(jnp.sum(jnp.exp(logits - row_max), axis=1))
    classes = jnp.arange(logits.shape[1], dtype=jnp.int32)
    onehot = (labels[:, None] == classes[None, :]).astype(jnp.float32)
    loss_rows = log_total - jnp.sum(logits * onehot, axis=1)
    softmax_rows = jnp.exp(logits - log_total[:, None])
    dlogits = ((softmax_rows - onehot) * row_scale).astype(jnp.bfloat16)
    grad_class = jnp.dot(hidden.T, dlogits, preferred_element_type=jnp.float32)
    dhidden = (
        jnp.dot(dlogits, w_class.T, preferred_element_type=jnp.float32) * (hidden > 0)
    ).astype(jnp.bfloat16)
    grad_branch = jnp.stack(
        [
            jnp.dot(
                batch_rows[branch_index].T,
                dhidden[:, branch_index * hidden_width : (branch_index + 1) * hidden_width],
                preferred_element_type=jnp.float32,
            )
            for branch_index in range(branch_count)
        ]
    )
    return (loss_rows, grad_branch, grad_class)


def pick_blocks(current, indices, live_count):
    slot_ids = jnp.arange(indices.shape[0], dtype=jnp.int32)
    keep = (slot_ids < live_count).astype(jnp.float32)
    return current[indices] * keep[:, None, None]


def propagate_padded(extended, tile_values, tile_dst, tile_src, live_count, block_count):
    gathered = extended[tile_src]
    products = jnp.einsum("tij,tjf->tif", tile_values, gathered, precision=lax.Precision.HIGHEST)
    live_mask = jnp.arange(tile_values.shape[0], dtype=jnp.int32) < live_count
    onehot = (
        (tile_dst[None, :] == jnp.arange(block_count, dtype=jnp.int32)[:, None])
        & live_mask[None, :]
    ).astype(jnp.float32)
    return jnp.einsum("bt,tif->bif", onehot, products, precision=lax.Precision.HIGHEST)


def body(
    features,
    tile_values,
    tile_dst,
    tile_src,
    tile_count,
    send_left,
    send_right,
    send_count,
    batch_order,
    labels,
    w_branch,
    w_class,
):
    block_size = tile_values.shape[1]
    width = features.shape[1]
    block_count = features.shape[0] // block_size
    current = features.reshape(block_count, block_size, width)
    permute = batch_order[0]
    sorted_list = []
    sorted_list.append(features[permute].astype(jnp.bfloat16))
    for hop_index in range(HOPS):
        to_left = pick_blocks(current, send_left, send_count[0, 0])
        to_right = pick_blocks(current, send_right, send_count[0, 1])
        from_lower = passed_along(to_right, "dom", 1)
        from_upper = passed_along(to_left, "dom", -1)
        extended = jnp.concatenate([current, from_lower, from_upper], axis=0)
        current = propagate_padded(
            extended, tile_values, tile_dst, tile_src, tile_count[0], block_count
        )
        hop_flat = current.reshape(block_count * block_size, width)
        sorted_list.append(hop_flat[permute].astype(jnp.bfloat16))
    batch_rows = lax.all_to_all(
        jnp.stack(sorted_list, axis=0), "shuf", split_axis=1, concat_axis=1, tiled=True
    )
    row_scale = 1.0 / math.sqrt(
        float(batch_rows.shape[1] * lax.axis_size("dom") * lax.axis_size("shuf"))
    )
    loss_rows, grad_branch, grad_class = local_terms(
        batch_rows, labels, w_branch, w_class, row_scale
    )
    shares = (
        lax.psum_scatter(grad_branch, "shuf", scatter_dimension=2, tiled=True),
        lax.psum_scatter(grad_class, "shuf", scatter_dimension=0, tiled=True),
    )
    summed = lax.psum((shares[0], shares[1]), "dom")
    return (loss_rows, summed[0], summed[1])


def solution(mesh):
    return jax.shard_map(
        body,
        mesh=mesh,
        in_specs=(
            P(("dom", "shuf"), None),
            P(("dom", "shuf"), None, None),
            P(("dom", "shuf")),
            P(("dom", "shuf")),
            P(("dom", "shuf")),
            P(("dom", "shuf")),
            P(("dom", "shuf")),
            P(("dom", "shuf"), None),
            P(("dom", "shuf"), None),
            P(("dom", "shuf")),
            P(),
            P(),
        ),
        out_specs=(P(("dom", "shuf")), P(None, None, "shuf"), P("shuf", None)),
        check_vma=False,
    )
```

profile of v0, /device:TPU:0, one launch (start us, length us, event | category | flops | bytes accessed | tf_op | source)
XLA Modules:
  0.0 235.0 jit_solution(1893687365355516177)
XLA Ops:
  7.2 0.8 compare_select_fusion.3
  8.0 1.3 fusion.27
  9.4 0.6 compare_convert_fusion.1
  10.0 1.5 gather_fusion.1
  11.6 3.0 %collective-permute-start = (f32[2,128,128]{2,1,0:T(8,128)S(1)}, f32[2,128,128]{2,1,0:T(8,128)S(1)}, u32[]{:S(2)}, u32[]{:S(2)}) collective-permute-start(f32[2,128,128]{2,1,0:T(8,128)S(1)} %broadcast_multiply_fusion.5), channel_id=1, source_target_pairs={{0,4},{4,8},{8,12},{12,16},{16,20},{20,24},{24,28},{28,0},{1,5},{5... | collective-permute-start | bytes 393224 | tf_op jit(solution)/shard_map/ppermute | solution.py:14
  14.6 0.7 compare_select_fusion.2
  15.3 1.5 gather_fusion.2
  16.7 0.7 compare_convert_fusion
  17.4 0.1 broadcast_multiply_fusion.2
  17.5 3.1 %collective-permute-start.1 = (f32[2,128,128]{2,1,0:T(8,128)S(1)}, f32[2,128,128]{2,1,0:T(8,128)S(1)}, u32[]{:S(2)}, u32[]{:S(2)}) collective-permute-start(f32[2,128,128]{2,1,0:T(8,128)S(1)} %broadcast_multiply_fusion.2), channel_id=1, source_target_pairs={{0,28},{4,0},{8,4},{12,8},{16,12},{20,16},{24,20},{28,24},{1,29},{... | collective-permute-start | bytes 393224 | tf_op jit(solution)/shard_map/ppermute | solution.py:14
  20.6 0.7 compare_select_fusion.1
  21.9 2.0 collective-permute-done.1
  23.9 0.9 pad_maximum_fusion.2
  24.9 0.6 gather_fusion.3
  25.5 1.0 convolution_bitcast_fusion.6
  26.5 0.2 copy.85
  26.7 0.4 fusion.21
  27.1 0.6 gather_fusion.5
  27.7 0.6 gather_fusion.6
  28.2 0.1 broadcast_multiply_fusion.4
  28.3 1.0 collective-permute-start.2
  29.4 3.8 %collective-permute-start.3 = (f32[2,128,128]{2,1,0:T(8,128)S(1)}, f32[2,128,128]{2,1,0:T(8,128)S(1)}, u32[]{:S(2)}, u32[]{:S(2)}) collective-permute-start(f32[2,128,128]{2,1,0:T(8,128)S(1)} %broadcast_multiply_fusion.1), channel_id=1, source_target_pairs={{0,28},{4,0},{8,4},{12,8},{16,12},{20,16},{24,20},{28,24},{1,29},{... | collective-permute-start | bytes 393224 | tf_op jit(solution)/shard_map/ppermute | solution.py:14
  33.2 3.4 %collective-permute-done.2 = f32[2,128,128]{2,1,0:T(8,128)S(1)} collective-permute-done((f32[2,128,128]{2,1,0:T(8,128)S(1)}, f32[2,128,128]{2,1,0:T(8,128)S(1)}, u32[]{:S(2)}, u32[]{:S(2)}) %collective-permute-start.2) | collective-permute-done | bytes 131104 | tf_op jit(solution)/shard_map/ppermute | solution.py:14
  36.6 0.7 collective-permute-done.3
  37.3 0.6 gather_fusion.7
  37.9 1.0 convolution_bitcast_fusion.5
  38.9 0.2 copy.91
  39.2 0.4 fusion.19
  39.5 0.6 gather_fusion.9
  40.1 0.6 gather_fusion.10
  40.7 0.1 broadcast_multiply_fusion.3
  40.9 4.8 %collective-permute-start.5 = (f32[2,128,128]{2,1,0:T(8,128)S(1)}, f32[2,128,128]{2,1,0:T(8,128)S(1)}, u32[]{:S(2)}, u32[]{:S(2)}) collective-permute-start(f32[2,128,128]{2,1,0:T(8,128)S(1)} %broadcast_multiply_fusion), channel_id=1, source_target_pairs={{0,28},{4,0},{8,4},{12,8},{16,12},{20,16},{24,20},{28,24},{1,29},{... | collective-permute-start | bytes 393224 | tf_op jit(solution)/shard_map/ppermute | solution.py:14
  45.7 0.7 gather_fusion
  46.4 0.7 gather_fusion.4
  47.2 1.4 gather_fusion.8
  48.6 0.1 collective-permute-done.5
  48.8 0.6 gather_fusion.11
  49.4 1.0 convolution_bitcast_fusion.4
  50.4 0.2 copy.97
  50.6 0.4 fusion.17
  51.0 0.9 gather_fusion.12
  51.9 0.2 copy.99
  52.1 8.6 %all_to_all.5 = bf16[4,256,128]{2,0,1:T(4,128)(2,1)S(1)} all-to-all(bf16[4,256,128]{2,0,1:T(4,128)(2,1)S(1)} %copy.99), channel_id=1, replica_groups=mesh['dom'=8,'shuf'=4] {'shuf'}, dimensions={1} | all-to-all | bytes 524288 | tf_op jit(solution)/shard_map/all_to_all | solution.py:103
  60.7 0.4 fusion.26
  61.1 0.3 fusion.1
  61.4 0.3 fusion.2
  61.7 0.3 fusion.3
  62.0 0.3 fusion.4
  62.3 0.9 fusion.28
  63.3 0.6 fusion.25
  63.9 1.0 fusion
  64.9 0.2 convolution_bitcast_fusion.3
  65.2 0.3 convolution_bitcast_fusion.2
  65.4 0.3 convolution_bitcast_fusion.1
  65.7 0.2 convolution_bitcast_fusion
  65.9 1.5 pad_maximum_fusion.1
  67.5 1.0 copy-done.5
  68.5 0.2 copy-done.7
  68.6 3.1 %fusion.23 = f32[4096,172]{0,1:T(8,128)} fusion(f32[256,172]{0,1:T(8,128)} %copy-done.9, f32[256]{0:T(256)S(1)} %get-tuple-element.8, s32[256]{0:T(256)S(1)} %copy-done.11, bf16[256,1024]{1,0:T(8,128)(2,1)S(1)} %copy-done.7, bf16[256,1024]{1,0:T(8,128)(2,1)S(1)} %copy-done.5, bf16[256,1024]{1,0:T(8,128)(2,1)S(1)} %fusion.2, bf16[256,1024]{1,0:T(8,128)(2,1)S(1)} %fusion.1), kind=kOutput, calls=%fused_computation.85 | convolution fusion | flops 369362944 | bytes 5093376 | tf_op jit(solution)/shard_map/dot_general | solution.py:37
  71.8 27.7 %reduce-scatter.3.cloned.1.call-done = f32[4,128,256]{2,1,0:T(8,128)} async-done(((f32[4,128,1024]{2,1,0:T(8,128)}), f32[4,128,256]{2,1,0:T(8,128)}) %reduce-scatter.3.cloned.1.call-update) | async-done | bytes 524304 | tf_op jit(solution)/shard_map/reduce_scatter | solution.py:113
  99.4 39.0 %reduce-scatter.5.cloned.1.call-done = f32[1024,172]{0,1:T(8,128)} async-done(((f32[4096,172]{0,1:T(8,128)}), f32[1024,172]{0,1:T(8,128)}) %reduce-scatter.5.cloned.1.call-update) | async-done | bytes 704528 | tf_op jit(solution)/shard_map/reduce_scatter | solution.py:114
  138.5 86.1 %all-reduce.3.cloned.1.call-done = (f32[4,128,256]{2,1,0:T(8,128)}, f32[1024,172]{0,1:T(8,128)}) async-done(((f32[4,128,256]{2,1,0:T(8,128)}, f32[1024,172]{0,1:T(8,128)}), (f32[4,128,256]{2,1,0:T(8,128)}, f32[1024,172]{0,1:T(8,128)})) %all-reduce.3.cloned.1.call-update) | async-done | bytes 1228816 | tf_op jit(solution)/shard_map/psum | solution.py:116
  224.6 1.9 copy.126
  226.4 2.0 copy.127
  (49 shorter events, 0.8 us)
Async XLA Ops:
  7.2 55.2 %copy-start = (bf16[4096,172]{0,1:T(8,128)(2,1)S(1)}, bf16[4096,172]{0,1:T(8,128)(2,1)}, u32[]{:S(2)}) copy-start(bf16[4096,172]{0,1:T(8,128)(2,1)} %param.23) | copy-start | bytes 4227076
  7.2 18.3 %copy-start.2 = (f32[8,128,128]{2,1,0:T(8,128)S(1)}, f32[8,128,128]{2,1,0:T(8,128)}, u32[]{:S(2)}) copy-start(f32[8,128,128]{2,1,0:T(8,128)} %param.13) | copy-start | bytes 1572868
  7.2 92.2 %reduce-scatter.3.cloned.1.call-start = ((), (), s32[]{:S(2)}) async-start(), calls=%async_computation.3 | async-start | bytes 2621440 | tf_op jit(solution)/shard_map/reduce_scatter | solution.py:113
  11.6 10.3 %collective-permute-start = (f32[2,128,128]{2,1,0:T(8,128)S(1)}, f32[2,128,128]{2,1,0:T(8,128)S(1)}, u32[]{:S(2)}, u32[]{:S(2)}) collective-permute-start(f32[2,128,128]{2,1,0:T(8,128)S(1)} %broadcast_multiply_fusion.5), channel_id=1, source_target_pairs={{0,4},{4,8},{8,12},{12,16},{16,20},{20,24},{24,28},{28,0},{1,5},{5... | collective-permute-start | bytes 393224 | tf_op jit(solution)/shard_map/ppermute | solution.py:14
  17.5 6.5 %collective-permute-start.1 = (f32[2,128,128]{2,1,0:T(8,128)S(1)}, f32[2,128,128]{2,1,0:T(8,128)S(1)}, u32[]{:S(2)}, u32[]{:S(2)}) collective-permute-start(f32[2,128,128]{2,1,0:T(8,128)S(1)} %broadcast_multiply_fusion.2), channel_id=1, source_target_pairs={{0,28},{4,0},{8,4},{12,8},{16,12},{20,16},{24,20},{28,24},{1,29},{... | collective-permute-start | bytes 393224 | tf_op jit(solution)/shard_map/ppermute | solution.py:14
  21.9 4.8 %copy-start.10 = (s32[8]{0:T(128)S(1)}, s32[8]{0:T(128)}, u32[]{:S(2)}) copy-start(s32[8]{0:T(128)} %param.14) | copy-start | bytes 100
  28.3 8.3 %collective-permute-start.2 = (f32[2,128,128]{2,1,0:T(8,128)S(1)}, f32[2,128,128]{2,1,0:T(8,128)S(1)}, u32[]{:S(2)}, u32[]{:S(2)}) collective-permute-start(f32[2,128,128]{2,1,0:T(8,128)S(1)} %broadcast_multiply_fusion.4), channel_id=1, source_target_pairs={{0,4},{4,8},{8,12},{12,16},{16,20},{20,24},{24,28},{28,0},{1,5},{5... | collective-permute-start | bytes 393224 | tf_op jit(solution)/shard_map/ppermute | solution.py:14
  29.4 7.8 %collective-permute-start.3 = (f32[2,128,128]{2,1,0:T(8,128)S(1)}, f32[2,128,128]{2,1,0:T(8,128)S(1)}, u32[]{:S(2)}, u32[]{:S(2)}) collective-permute-start(f32[2,128,128]{2,1,0:T(8,128)S(1)} %broadcast_multiply_fusion.1), channel_id=1, source_target_pairs={{0,28},{4,0},{8,4},{12,8},{16,12},{20,16},{24,20},{28,24},{1,29},{... | collective-permute-start | bytes 393224 | tf_op jit(solution)/shard_map/ppermute | solution.py:14
  37.9 7.8 %copy-start.12 = (s32[1,256]{1,0:T(1,128)S(1)}, s32[1,256]{1,0:T(1,128)}, u32[]{:S(2)}) copy-start(s32[1,256]{1,0:T(1,128)} %param.20) | copy-start | bytes 3076
  37.9 7.8 %copy-start.1 = (f32[256,128]{1,0:T(8,128)S(1)}, f32[256,128]{1,0:T(8,128)}, u32[]{:S(2)}) copy-start(f32[256,128]{1,0:T(8,128)} %param.12) | copy-start | bytes 393220
  40.8 7.8 %collective-permute-start.4 = (f32[2,128,128]{2,1,0:T(8,128)S(1)}, f32[2,128,128]{2,1,0:T(8,128)S(1)}, u32[]{:S(2)}, u32[]{:S(2)}) collective-permute-start(f32[2,128,128]{2,1,0:T(8,128)S(1)} %broadcast_multiply_fusion.3), channel_id=1, source_target_pairs={{0,4},{4,8},{8,12},{12,16},{16,20},{20,24},{24,28},{28,0},{1,5},{5... | collective-permute-start | bytes 393224 | tf_op jit(solution)/shard_map/ppermute | solution.py:14
  40.9 7.8 %collective-permute-start.5 = (f32[2,128,128]{2,1,0:T(8,128)S(1)}, f32[2,128,128]{2,1,0:T(8,128)S(1)}, u32[]{:S(2)}, u32[]{:S(2)}) collective-permute-start(f32[2,128,128]{2,1,0:T(8,128)S(1)} %broadcast_multiply_fusion), channel_id=1, source_target_pairs={{0,28},{4,0},{8,4},{12,8},{16,12},{20,16},{24,20},{28,24},{1,29},{... | collective-permute-start | bytes 393224 | tf_op jit(solution)/shard_map/ppermute | solution.py:14
  50.4 1.5 copy-start.8
  50.6 10.5 %copy-start.3 = (bf16[4,128,1024]{2,1,0:T(8,128)(2,1)S(1)}, bf16[4,128,1024]{2,1,0:T(8,128)(2,1)}, u32[]{:S(2)}) copy-start(bf16[4,128,1024]{2,1,0:T(8,128)(2,1)} %param.22) | copy-start | bytes 3145732
  62.0 1.9 copy-start.4
  62.3 1.6 copy-start.6
  62.3 0.9 copy-start.11
  63.2 1.7 copy-start.9
  67.4 1.0 copy-start.5
  67.4 1.2 copy-start.7
  67.5 71.0 %reduce-scatter.5.cloned.1.call-start = ((), (), s32[]{:S(2)}) async-start(), calls=%async_computation.4 | async-start | bytes 3604480 | tf_op jit(solution)/shard_map/reduce_scatter | solution.py:114
  71.7 152.8 %all-reduce.3.cloned.1.call-start = ((), (), s32[]{:S(2)}) async-start(), calls=%async_computation.5 | async-start | bytes 2490368 | tf_op jit(solution)/shard_map/psum | solution.py:116
Sparse Core Ops, SparseCore 0:
  67.6 31.8 reduce-scatter.2
  102.1 36.3 reduce-scatter.4
  142.1 82.4 all-reduce.2
where the time goes:
time: 235 us
  waiting for transfers between devices  159 us (68%)
  local copies, waits for them, and re-layouts  18.3 us (8%)
  starting transfers between devices  15.9 us (7%)
  between operations  14.9 us (6%)
  matrix products  11.2 us (5%)
  blocking collectives  8.6 us (4%)
  other arithmetic  7.1 us (3%)
    psum x1, waiting for transfers between devices, body(): summed = lax.psum((shares[0], shares[1]), 'dom')  86.1 us
    reduce_scatter x1, waiting for transfers between devices, body(): lax.psum_scatter(grad_class, 'shuf', scatter_dimension=0, tiled=True)  39 us
    reduce_scatter x1, waiting for transfers between devices, body(): lax.psum_scatter(grad_branch, 'shuf', scatter_dimension=2, tiled=True)  27.7 us
    ppermute x6, starting transfers between devices, passed_along(): return lax.ppermute(value, axis, pairs)  15.8 us
    all_to_all x1, blocking collectives, body(): lax.all_to_all(jnp.stack(sorted_list, axis=0), 'shuf', split_axis=1, conc...  8.6 us
    ppermute x6, waiting for transfers between devices, passed_along(): return lax.ppermute(value, axis, pairs)  6.23 us
    gather x6, local copies, waits for them, and re-layouts, pick_blocks(): return current[indices] * keep[:, None, None]  5.14 us
    unnamed x28, local copies, waits for them, and re-layouts  5.1 us
  transfers between devices with their start and end apart: 9, of which 8 were waited for; matrix products, arithmetic and copies ran while one was open for 4% of the time, Pallas kernels for 0%

commit v1 on v0

v1 whole, which is shorter than its diff:
```python
import functools
import math

import jax
import jax.numpy as jnp
from jax import lax
from jax.experimental import pallas as pl
from jax.experimental.pallas import tpu as pltpu
from jax.sharding import PartitionSpec as P

HOPS = 3
LANES = 128
VMEM_LIMIT = 24 * 1024 * 1024

IN_VMEM = pl.BlockSpec(memory_space=pltpu.VMEM)
IN_SMEM = pl.BlockSpec(memory_space=pltpu.SMEM)
BF16 = jnp.bfloat16
F32 = jnp.float32


def up_to(value, multiple):
    return -(-value // multiple) * multiple


def passed_along(value, axis, steps):
    count = lax.axis_size(axis)
    pairs = [(source, (source + steps) % count) for source in range(count)]
    return lax.ppermute(value, axis, pairs)


def matmul(left, right, dims=((1,), (0,)), precision=None):
    return lax.dot_general(
        left, right, (dims, ((), ())), precision=precision, preferred_element_type=F32
    )


def call(kernel, out_shape, in_specs, flops, scratch=()):
    outs = out_shape if isinstance(out_shape, (list, tuple)) else [out_shape]
    moved = sum(math.prod(one.shape) * one.dtype.itemsize for one in outs)
    return pl.pallas_call(
        kernel,
        out_shape=out_shape,
        in_specs=in_specs,
        out_specs=[IN_VMEM] * len(out_shape)
        if isinstance(out_shape, (list, tuple))
        else IN_VMEM,
        scratch_shapes=list(scratch),
        compiler_params=pltpu.CompilerParams(vmem_limit_bytes=VMEM_LIMIT),
        cost_estimate=pl.CostEstimate(
            flops=flops, bytes_accessed=3 * moved, transcendentals=0
        ),
    )


def write_sends(blocks, left_ref, right_ref, left_ids, right_ids, counts):
    for slot in range(left_ref.shape[0]):
        for out_ref, ids, live in (
            (left_ref, left_ids, counts(0)),
            (right_ref, right_ids, counts(1)),
        ):
            index = ids(slot)
            picked = blocks[0]
            for number in range(1, len(blocks)):
                picked = jnp.where(index == number, blocks[number], picked)
            out_ref[slot] = jnp.where(slot < live, picked, 0.0)


def first_kernel(sl_ref, sr_ref, sc_ref, feat_ref, left_ref, right_ref, b_ref):
    blocks = [feat_ref[number] for number in range(feat_ref.shape[0])]
    write_sends(
        blocks,
        left_ref,
        right_ref,
        lambda slot: sl_ref[slot],
        lambda slot: sr_ref[slot],
        lambda side: sc_ref[0, side],
    )
    for number, block in enumerate(blocks):
        size = block.shape[0]
        b_ref[number * size : (number + 1) * size] = block.astype(BF16)


def next_blocks(dst_ref, src_ref, count_ref, cur_ref, low_ref, high_ref, tiles_ref, ext_ref):
    local = cur_ref.shape[0]
    slots = low_ref.shape[0]
    ext_ref[:local] = cur_ref[...]
    ext_ref[local : local + slots] = low_ref[...]
    ext_ref[local + slots :] = high_ref[...]
    totals = [jnp.zeros(cur_ref.shape[1:], F32) for _ in range(local)]
    live = count_ref[0]
    for tile in range(tiles_ref.shape[0]):
        product = matmul(
            tiles_ref[tile], ext_ref[src_ref[tile]], precision=lax.Precision.HIGHEST
        )
        wanted = jnp.where(tile < live, dst_ref[tile], -1)
        for number in range(local):
            totals[number] = totals[number] + jnp.where(wanted == number, product, 0.0)
    return totals


def hop_kernel(
    dst_ref, src_ref, count_ref, sl_ref, sr_ref, sc_ref,
    cur_ref, low_ref, high_ref, tiles_ref,
    next_ref, left_ref, right_ref, b_ref, ext_ref,
):
    blocks = next_blocks(
        dst_ref, src_ref, count_ref, cur_ref, low_ref, high_ref, tiles_ref, ext_ref
    )
    write_sends(
        blocks,
        left_ref,
        right_ref,
        lambda slot: sl_ref[slot],
        lambda slot: sr_ref[slot],
        lambda side: sc_ref[0, side],
    )
    for number, block in enumerate(blocks):
        size = block.shape[0]
        next_ref[number] = block
        b_ref[number * size : (number + 1) * size] = block.astype(BF16)


def branch_logits(rows, w_ref, wc_ref):
    hidden = jnp.maximum(matmul(rows, w_ref[...]), 0.0).astype(BF16)
    return matmul(hidden, wc_ref[...])


def forward_kernel(b_ref, w_ref, wc_ref, out_ref):
    out_ref[...] = branch_logits(b_ref[...], w_ref, wc_ref)


def forward_more_kernel(b_ref, w_ref, wc_ref, before_ref, out_ref):
    out_ref[...] = before_ref[...] + branch_logits(b_ref[...], w_ref, wc_ref)


def last_kernel(
    classes, row_scale,
    dst_ref, src_ref, count_ref,
    cur_ref, low_ref, high_ref, tiles_ref,
    before_ref, w_ref, wc_ref, order_ref, label_ref,
    out_ref, ext_ref,
):
    blocks = next_blocks(
        dst_ref, src_ref, count_ref, cur_ref, low_ref, high_ref, tiles_ref, ext_ref
    )
    halves = [block.astype(BF16) for block in blocks]
    rows_b = jnp.concatenate(halves, axis=0)
    size = halves[0].shape[0]
    width = halves[0].shape[1]
    for number, half in enumerate(halves):
        out_ref[:size, number * width : (number + 1) * width] = half
    logits = before_ref[...] + branch_logits(rows_b, w_ref, wc_ref)
    rows, wide = logits.shape
    lane = lax.broadcasted_iota(jnp.int32, (rows, wide), 1)
    logits = jnp.where(lane < classes, logits, -jnp.inf)
    place = order_ref[...] == lax.broadcasted_iota(jnp.int32, (rows, rows), 0)
    label = jnp.sum(
        jnp.where(place, label_ref[...].astype(F32), 0.0), axis=1, keepdims=True
    ).astype(jnp.int32)
    hit = lane == label
    top = jnp.max(logits, axis=1, keepdims=True)
    log_total = top + jnp.log(jnp.sum(jnp.exp(logits - top), axis=1, keepdims=True))
    loss = log_total - jnp.sum(jnp.where(hit, logits, 0.0), axis=1, keepdims=True)
    dlogits = (jnp.exp(logits - log_total) - jnp.where(hit, 1.0, 0.0)) * row_scale
    kept = up_to(classes, 16)
    out_ref[size : size + kept] = dlogits.T[:kept].astype(BF16)
    ordered = jnp.sum(jnp.where(place, loss, 0.0), axis=0, keepdims=True)
    piece = lax.broadcasted_iota(jnp.int32, (16, rows), 0)
    rest = ordered
    packed = jnp.zeros((16, rows), F32)
    for number in range(3):
        part = rest.astype(BF16).astype(F32)
        packed = jnp.where(piece == number, part, packed)
        rest = rest - part
    out_ref[size + kept :] = packed.astype(BF16)


def grad_kernel(
    kept, which_ref, b0_ref, b1_ref, b2_ref, last_ref, wq_ref, wt_ref, wc_ref, out_ref,
):
    group = last_ref.shape[0]
    width = b0_ref.shape[2]
    size = b0_ref.shape[1] // (last_ref.shape[2] // width)
    branches = []
    for b_ref in (b0_ref, b1_ref, b2_ref):
        branches.append(b_ref[...].reshape(group * b_ref.shape[1], width))
    last_rows = []
    for member in range(group):
        for number in range(last_ref.shape[2] // width):
            last_rows.append(last_ref[member, :size, number * width : (number + 1) * width])
    branches.append(jnp.concatenate(last_rows, axis=0))
    dlogits_t = jnp.concatenate(
        [last_ref[member, size : size + kept] for member in range(group)], axis=1
    )
    which = which_ref[0]
    chosen = branches[0]
    for number in range(1, len(branches)):
        chosen = jnp.where(which == number, branches[number], chosen)
    hidden = jnp.maximum(matmul(chosen, wq_ref[...]), 0.0).astype(BF16)
    class_t = matmul(dlogits_t, hidden).astype(BF16)
    for chunk in range(out_ref.shape[0]):
        out_ref[chunk, :kept] = class_t[:, chunk * LANES : (chunk + 1) * LANES]
    per_branch = out_ref.shape[0] // len(branches)
    for number, rows in enumerate(branches):
        live = matmul(wt_ref[number], rows, ((1,), (1,))) > 0.0
        dhidden_t = jnp.where(live, matmul(wc_ref[number], dlogits_t), 0.0).astype(BF16)
        branch_t = matmul(dhidden_t, rows).astype(BF16)
        for part in range(per_branch):
            out_ref[number * per_branch + part, kept:] = branch_t[
                part * LANES : (part + 1) * LANES
            ]


def sum_kernel(in_ref, out_ref):
    total = in_ref[0].astype(F32)
    for number in range(1, in_ref.shape[0]):
        total = total + in_ref[number].astype(F32)
    out_ref[...] = total.astype(BF16)


def out_kernel(kept, in_ref, branch_ref, class_ref):
    chunks = in_ref.shape[0]
    per_branch = chunks // branch_ref.shape[0]
    classes = class_ref.shape[1]
    for chunk in range(chunks):
        turned = in_ref[chunk].astype(F32).T
        class_ref[chunk * LANES : (chunk + 1) * LANES] = turned[:, :classes]
        part = chunk % per_branch
        branch_ref[chunk // per_branch, :, part * LANES : (part + 1) * LANES] = in_ref[
            chunk, kept:
        ].astype(F32).T


def body(
    features, tile_values, tile_dst, tile_src, tile_count, send_left, send_right,
    send_count, batch_order, labels, w_branch, w_class,
):
    block = tile_values.shape[1]
    nodes, width = features.shape
    local = nodes // block
    slots = send_left.shape[0]
    tiles = tile_values.shape[0]
    branches, _, hid = w_branch.shape
    cat, classes = w_class.shape
    dom = lax.axis_size("dom")
    shuf = lax.axis_size("shuf")
    mine = lax.axis_index("shuf")
    share = nodes // shuf
    own = hid // shuf
    own_class = cat // shuf
    kept = up_to(classes, 16)
    wide = up_to(classes, LANES)
    row_scale = 1.0 / math.sqrt(float(nodes * dom * shuf))
    blocks_f32 = jax.ShapeDtypeStruct((local, block, width), F32)
    slots_f32 = jax.ShapeDtypeStruct((slots, block, width), F32)
    rows_b16 = jax.ShapeDtypeStruct((nodes, width), BF16)
    logits_f32 = jax.ShapeDtypeStruct((nodes, wide), F32)

    label_all = lax.all_gather(labels, "shuf").reshape(shuf, shuf, share)
    label_mine = lax.dynamic_index_in_dim(label_all, mine, 1, keepdims=False).reshape(1, nodes)

    wc_wide = jnp.pad(w_class, ((0, 0), (0, wide - classes))).reshape(branches, hid, wide)
    wc_own = jnp.pad(
        lax.dynamic_slice_in_dim(w_class.reshape(branches, hid, classes), mine * own, own, 1),
        ((0, 0), (0, 0), (0, kept - classes)),
    )
    w_own_t = lax.dynamic_slice_in_dim(w_branch, mine * own, own, 2).transpose(0, 2, 1)
    which = (mine * own_class) // hid
    w_class_own = lax.dynamic_slice(
        w_branch, (which, 0, (mine * own_class) % hid), (1, width, own_class)
    )[0]

    current = features.reshape(local, block, width)
    to_left, to_right, rows = call(
        first_kernel,
        [slots_f32, slots_f32, rows_b16],
        [IN_SMEM] * 3 + [IN_VMEM],
        1000,
    )(send_left, send_right, send_count, current)
    gathered = []
    logits = None
    hop_flops = 12 * tiles * block * block * width
    forward_flops = 2 * nodes * hid * (width + wide)
    ext = pltpu.VMEM((local + 2 * slots, block, width), F32)
    for hop in range(HOPS):
        from_lower = passed_along(to_right, "dom", 1)
        from_upper = passed_along(to_left, "dom", -1)
        gathered.append(lax.all_gather(rows, "shuf"))
        if logits is None:
            logits = call(forward_kernel, logits_f32, [IN_VMEM] * 3, forward_flops)(
                rows, w_branch[hop], wc_wide[hop]
            )
        else:
            logits = call(forward_more_kernel, logits_f32, [IN_VMEM] * 4, forward_flops)(
                rows, w_branch[hop], wc_wide[hop], logits
            )
        if hop < HOPS - 1:
            current, to_left, to_right, rows = call(
                hop_kernel,
                [blocks_f32, slots_f32, slots_f32, rows_b16],
                [IN_SMEM] * 6 + [IN_VMEM] * 4,
                hop_flops,
                [ext],
            )(
                tile_dst, tile_src, tile_count, send_left, send_right, send_count,
                current, from_lower, from_upper, tile_values,
            )
    payload = call(
        functools.partial(last_kernel, classes, row_scale),
        jax.ShapeDtypeStruct((block + kept + 16, local * width), BF16),
        [IN_SMEM] * 3 + [IN_VMEM] * 9,
        hop_flops + forward_flops,
        [ext],
    )(
        tile_dst, tile_src, tile_count, current, from_lower, from_upper, tile_values,
        logits, w_branch[HOPS], wc_wide[HOPS], batch_order, label_mine,
    )
    last_all = lax.all_gather(payload, "shuf")
    loss_parts = lax.dynamic_slice(
        last_all, (0, block + kept, mine * share), (shuf, 3, share)
    ).astype(F32)
    loss_rows = (loss_parts[:, 0] + loss_parts[:, 1] + loss_parts[:, 2]).reshape(nodes)

    chunks = own_class // LANES
    height = kept + width
    grads = call(
        functools.partial(grad_kernel, kept),
        jax.ShapeDtypeStruct((chunks, height, LANES), BF16),
        [IN_SMEM] + [IN_VMEM] * 7,
        2 * shuf * nodes * own_class * (2 * width + 2 * wide + width),
    )(
        jnp.reshape(which, (1,)).astype(jnp.int32),
        *gathered, last_all, w_class_own, w_own_t, wc_own,
    )
    if chunks == dom:
        parts = lax.all_to_all(grads, "dom", split_axis=0, concat_axis=0, tiled=True)
        part = call(
            sum_kernel, jax.ShapeDtypeStruct((height, LANES), BF16), [IN_VMEM], 1000
        )(parts)
        summed = lax.all_gather(part, "dom")
    else:
        summed = lax.psum(grads.astype(F32), "dom")
    grad_branch, grad_class = call(
        functools.partial(out_kernel, kept),
        [
            jax.ShapeDtypeStruct((branches, width, own), F32),
            jax.ShapeDtypeStruct((own_class, classes), F32),
        ],
        [IN_VMEM],
        1000,
    )(summed)
    return (loss_rows, grad_branch, grad_class)


def solution(mesh):
    return jax.shard_map(
        body,
        mesh=mesh,
        in_specs=(
            P(("dom", "shuf"), None),
            P(("dom", "shuf"), None, None),
            P(("dom", "shuf")),
            P(("dom", "shuf")),
            P(("dom", "shuf")),
            P(("dom", "shuf")),
            P(("dom", "shuf")),
            P(("dom", "shuf"), None),
            P(("dom", "shuf"), None),
            P(("dom", "shuf")),
            P(),
            P(),
        ),
        out_specs=(P(("dom", "shuf")), P(None, None, "shuf"), P("shuf", None)),
        check_vma=False,
    )
```

time: 235 us -> 138 us (0.59)
  waiting for transfers between devices: 159 us -> 16.6 us
  blocking collectives: 8.6 us -> 62.9 us
  Pallas kernels: 0 us -> 13.6 us
  between operations: 14.9 us -> 1.57 us
  matrix products: 11.2 us -> 0 us
  other arithmetic: 7.1 us -> 0.13 us
  local copies, waits for them, and re-layouts: 18.3 us -> 23.4 us
  starting transfers between devices: 15.9 us -> 19 us
    psum x1 -> x0, waiting for transfers between devices: 86.1 us -> none  [body(): summed = lax.psum((shares[0], shares[1]), 'dom')]
    reduce_scatter x2 -> x0, waiting for transfers between devices: 66.7 us -> none  [the longest x1 39 us: body(): lax.psum_scatter(grad_class, 'shuf', scatter_dimension=0, tiled=True)]
    all_gather x0 -> x6, blocking collectives: none -> 62.9 us  [the longest x1 31.6 us: body(): summed = lax.all_gather(part, 'dom')]
    all_to_all x0 -> x1, waiting for transfers between devices: none -> 16.6 us  [body(): lax.all_to_all(grads, 'dom', split_axis=0, concat_axis=0, tiled=True)]
    pallas_call x0 -> x10, Pallas kernels: none -> 13.6 us  [the longest x2 3.99 us: body(): call(hop_kernel, [blocks_f32, slots_f32, slots_f32, rows_b16], [IN_SMEM]...]
    dot_general x17 -> x0, matrix products: 11.2 us -> none  [the longest x1 3.06 us: local_terms(): grad_class = jnp.dot(hidden.T, dlogits, preferred_element_type=jnp.float32)]
    gather x13 -> x0, local copies, waits for them, and re-layouts: 10.6 us -> none  [the longest x6 5.14 us: pick_blocks(): return current[indices] * keep[:, None, None]]
    unnamed x28 -> x53, local copies, waits for them, and re-layouts: 5.1 us -> 13.7 us
  transfers between devices with their start and end apart: 9 -> 7, of which waited for: 8 -> 1; matrix products, arithmetic and copies ran while one was open for 4% -> 11% of each run, Pallas kernels for 0% -> 1%
where the time goes in v1:
time: 138 us; the launch traced here: 137 us
  blocking collectives  62.9 us (46%)
  local copies, waits for them, and re-layouts  23.4 us (17%)
  starting transfers between devices  19 us (14%)
  waiting for transfers between devices  16.6 us (12%)
  Pallas kernels  13.6 us (10%)
  between operations  1.57 us (1%)
    all_gather x1, blocking collectives, body(): summed = lax.all_gather(part, 'dom')  31.6 us
    all_gather x3, blocking collectives, body(): gathered.append(lax.all_gather(rows, 'shuf'))  18 us
    all_to_all x1, waiting for transfers between devices, body(): lax.all_to_all(grads, 'dom', split_axis=0, concat_axis=0, tiled=True)  16.6 us
    ppermute x6, starting transfers between devices, passed_along(): return lax.ppermute(value, axis, pairs)  15.5 us
    unnamed x53, local copies, waits for them, and re-layouts  13.7 us
    all_gather x1, blocking collectives, body(): last_all = lax.all_gather(payload, 'shuf')  8.01 us
    all_gather x1, blocking collectives, body(): label_all = lax.all_gather(labels, 'shuf').reshape(shuf, shuf, share)  5.27 us
    pallas_call x2, Pallas kernels, body(): call(hop_kernel, [blocks_f32, slots_f32, slots_f32, rows_b16], [IN_SMEM]...  3.99 us
  transfers between devices with their start and end apart: 7, of which 1 were waited for; matrix products, arithmetic and copies ran while one was open for 11% of the time, Pallas kernels for 1%

profile of v1, /device:TPU:0, one launch (start us, length us, event | category | flops | bytes accessed | tf_op | source)
XLA Modules:
  0.0 137.2 jit_solution(11434199857038243384)
XLA Ops:
  0.6 0.0 copy-start.2
  0.6 0.9 copy-done.2
  1.5 0.7 copy-done.14
  2.2 0.7 copy-done.16
  2.9 0.7 copy-done.18
  3.5 1.3 shard_map.139
  4.8 0.6 copy-done.4
  5.4 3.0 %collective-permute-start = (f32[2,128,128]{2,1,0:T(8,128)}, f32[2,128,128]{2,1,0:T(8,128)}, u32[]{:S(2)}, u32[]{:S(2)}) collective-permute-start(f32[2,128,128]{2,1,0:T(8,128)} %get-tuple-element.16), channel_id=1, source_target_pairs={{0,4},{4,8},{8,12},{12,16},{16,20},{20,24},{24,28},{28,0},{1,5},{5... | collective-permute-start | bytes 393224 | tf_op jit(solution)/shard_map/ppermute | solution.py:28
  8.4 3.0 %collective-permute-start.1 = (f32[2,128,128]{2,1,0:T(8,128)}, f32[2,128,128]{2,1,0:T(8,128)}, u32[]{:S(2)}, u32[]{:S(2)}) collective-permute-start(f32[2,128,128]{2,1,0:T(8,128)} %get-tuple-element.17), channel_id=1, source_target_pairs={{0,28},{4,0},{8,4},{12,8},{16,12},{20,16},{24,20},{28,24},{1,29},{... | collective-permute-start | bytes 393224 | tf_op jit(solution)/shard_map/ppermute | solution.py:28
  11.4 3.8 %copy.23 = bf16[4096,172]{1,0:T(8,128)(2,1)} copy(bf16[4096,172]{0,1:T(8,128)(2,1)} %param.23) | data formatting | bytes 2818048 | tf_op args[11]
  15.2 1.9 %pad_slice_fusion = (bf16[1024,256]{1,0:T(8,128)(2,1)S(1)}, bf16[1024,256]{1,0:T(8,128)(2,1)S(1)}, bf16[1024,256]{1,0:T(8,128)(2,1)S(1)}, bf16[1024,256]{1,0:T(8,128)(2,1)S(1)}) fusion(bf16[4096,172]{1,0:T(8,128)(2,1)} %copy.23), kind=kLoop, calls=%fused_computation | loop fusion | bytes 3506176 | tf_op jit(solution)/shard_map/slice | solution.py:316
  17.0 0.0 copy-start
  17.1 0.0 copy-start.3
  17.1 0.0 copy-start.15
  17.1 0.0 copy-start.17
  17.1 0.0 copy-start.19
  17.1 0.0 copy-start.20
  17.1 2.2 %dynamic-slice_bitcast_fusion = (bf16[128,1024]{1,0:T(8,128)(2,1)}, bf16[128,1024]{1,0:T(8,128)(2,1)S(1)}, bf16[128,1024]{1,0:T(8,128)(2,1)S(1)}, bf16[128,1024]{1,0:T(8,128)(2,1)}, bf16[128,1024]{1,0:T(8,128)(2,1)S(1)}) fusion(bf16[4,128,1024]{2,1,0:T(8,128)(2,1)} %param.22, s32[]{:T(128)S(6)} %select_n.27), kind=kLoop, calls=%fused_computation.4 | loop fusion | bytes 2621444 | tf_op jit(solution)/shard_map/squeeze | solution.py:269
  19.4 1.7 %constant_dynamic-slice_fusion.1 = bf16[4,128,256]{2,1,0:T(8,128)(2,1)} fusion(bf16[4,128,1024]{2,1,0:T(8,128)(2,1)} %param.22, s32[]{:T(128)S(6)} %select_n.28), kind=kLoop, calls=%fused_computation.15 | loop fusion | bytes 524292 | tf_op jit(solution)/shard_map/dynamic_slice | solution.py:267
  21.7 1.9 %constant_dynamic-slice_fusion = bf16[4,256,172]{2,1,0:T(8,128)(2,1)} fusion(bf16[4,1024,172]{2,1,0:T(8,128)(2,1)} %bitcast.29, s32[]{:T(128)S(6)} %select_n.28), kind=kLoop, calls=%fused_computation.14 | loop fusion | bytes 704516 | tf_op jit(solution)/shard_map/dynamic_slice | solution.py:264
  23.6 0.0 collective-permute-done.low_ref
  23.6 0.0 collective-permute-done.1.high_ref
  23.7 0.0 copy-start.21
  23.7 0.6 copy-done.21
  24.3 2.4 %shard_map.140 = (f32[2,128,128]{2,1,0:T(8,128)S(1)}, f32[2,128,128]{2,1,0:T(8,128)}, f32[2,128,128]{2,1,0:T(8,128)}, bf16[256,128]{1,0:T(8,128)(2,1)S(1)}) custom-call(s32[8]{0:T(128)S(1)} %copy-done.20, s32[8]{0:T(128)S(1)} %copy-done.21, s32[1]{0:T(128)S(6)} %copy.28.count_ref, s32[2]{0:T(128)S(1)} %copy-done.15, s32[2]{0:T(128)S(1)} %copy-done.17, ...), custom_call_target="tpu_custom_call" | custom-call | flops 201326592 | bytes 1376256 | tf_op jit(solution)/shard_map/pallas_call | solution.py:298
  26.7 0.6 copy-done.10
  27.3 0.6 copy-done.12
  28.0 0.0 collective-permute-start.2
  28.0 4.7 %collective-permute-start.3 = (f32[2,128,128]{2,1,0:T(8,128)}, f32[2,128,128]{2,1,0:T(8,128)}, u32[]{:S(2)}, u32[]{:S(2)}) collective-permute-start(f32[2,128,128]{2,1,0:T(8,128)} %get-tuple-element.20), channel_id=1, source_target_pairs={{0,28},{4,0},{8,4},{12,8},{16,12},{20,16},{24,20},{28,24},{1,29},{... | collective-permute-start | bytes 393224 | tf_op jit(solution)/shard_map/ppermute | solution.py:28
  32.7 6.3 %all-gather.2 = bf16[1024,128]{1,0:T(8,128)(2,1)} all-gather(bf16[256,128]{1,0:T(8,128)(2,1)S(1)} %copy-done.5), channel_id=4, replica_groups=mesh['dom'=8,'shuf'=4] {'shuf'}, dimensions={0}, use_global_device_ids=true | all-gather | bytes 327680 | tf_op jit(solution)/shard_map/all_gather | solution.py:288
  39.0 5.3 %all-gather.6 = s32[4,1,256]{2,1,0:T(1,128)S(1)} all-gather(s32[1,1,256]{2,1,0:T(1,128)} %bitcast.30), channel_id=2, replica_groups=mesh['dom'=8,'shuf'=4] {'shuf'}, dimensions={0}, use_global_device_ids=true | all-gather | bytes 5120 | tf_op jit(solution)/shard_map/all_gather | solution.py:259
  44.3 0.1 reshape.38
  44.4 0.1 reshape.39.label_ref
  44.5 1.8 %copy.27 = bf16[4,128,256]{1,2,0:T(8,128)(2,1)} copy(bf16[4,128,256]{2,1,0:T(8,128)(2,1)} %constant_dynamic-slice_fusion.1) | data formatting | bytes 524288
  46.3 1.2 pad.9.wc_ref
  47.5 0.8 copy-done.6
  48.3 0.5 shard_map.142.before_ref
  48.9 0.0 copy-start.23
  48.9 0.0 copy-start.24
  48.9 5.8 %all-gather.3 = bf16[1024,128]{1,0:T(8,128)(2,1)S(1)} all-gather(bf16[256,128]{1,0:T(8,128)(2,1)S(1)} %copy-done.11), channel_id=5, replica_groups=mesh['dom'=8,'shuf'=4] {'shuf'}, dimensions={0}, use_global_device_ids=true | all-gather | bytes 327680 | tf_op jit(solution)/shard_map/all_gather | solution.py:288
  54.8 0.0 collective-permute-done.2.low_ref
  54.8 0.0 collective-permute-done.3.high_ref
  54.8 0.0 copy-start.22
  54.8 0.6 copy-done.22
  55.4 1.6 %shard_map.141 = (f32[2,128,128]{2,1,0:T(8,128)S(1)}, f32[2,128,128]{2,1,0:T(8,128)S(1)}, f32[2,128,128]{2,1,0:T(8,128)S(1)}, bf16[256,128]{1,0:T(8,128)(2,1)S(1)}) custom-call(s32[8]{0:T(128)S(1)} %copy-done.20, s32[8]{0:T(128)S(1)} %copy-done.22, s32[1]{0:T(128)S(6)} %copy.28.count_ref, s32[2]{0:T(128)S(1)} %copy-done.15, s32[2]{0:T(128)S(1)} %copy-done.17, ...), custom_call_target="tpu_custom_call" | custom-call | flops 201326592 | bytes 1376256 | tf_op jit(solution)/shard_map/pallas_call | solution.py:298
  57.1 0.1 collective-permute-start.4
  57.1 4.7 %collective-permute-start.5 = (f32[2,128,128]{2,1,0:T(8,128)S(1)}, f32[2,128,128]{2,1,0:T(8,128)S(1)}, u32[]{:S(2)}, u32[]{:S(2)}) collective-permute-start(f32[2,128,128]{2,1,0:T(8,128)S(1)} %get-tuple-element.23), channel_id=1, source_target_pairs={{0,28},{4,0},{8,4},{12,8},{16,12},{20,16},{24,20},{28,24},{1,29},{... | collective-permute-start | bytes 393224 | tf_op jit(solution)/shard_map/ppermute | solution.py:28
  61.8 0.5 shard_map.143.before_ref
  62.4 0.0 copy-start.9
  62.4 0.5 shard_map.144.before_ref
  63.0 5.8 %all-gather.4 = bf16[1024,128]{1,0:T(8,128)(2,1)S(1)} all-gather(bf16[256,128]{1,0:T(8,128)(2,1)S(1)} %get-tuple-element.24.b_ref), channel_id=6, replica_groups=mesh['dom'=8,'shuf'=4] {'shuf'}, dimensions={0}, use_global_device_ids=true | all-gather | bytes 327680 | tf_op jit(solution)/shard_map/all_gather | solution.py:288
  68.8 0.0 collective-permute-done.4.low_ref
  68.8 0.0 collective-permute-done.5.high_ref
  68.8 2.0 %shard_map.145 = bf16[320,256]{1,0:T(8,128)(2,1)S(1)} custom-call(s32[8]{0:T(128)S(1)} %copy-done.20, s32[8]{0:T(128)S(1)} %copy-done.23, s32[1]{0:T(128)S(6)} %copy.28.count_ref, f32[2,128,128]{2,1,0:T(8,128)S(1)} %get-tuple-element.21.cur_ref, f32[2,128,128]{2,1,0:T(8,128)S(1)} %collective-permute-done.4.low_ref, ...), custom_call_target="tpu_custom_call" | custom-call | flops 402653184 | bytes 491520 | tf_op jit(solution)/shard_map/pallas_call | solution.py:308
  70.8 8.0 %all-gather.1 = bf16[1280,256]{1,0:T(8,128)(2,1)S(1)} all-gather(bf16[320,256]{1,0:T(8,128)(2,1)S(1)} %shard_map.145), channel_id=3, replica_groups=mesh['dom'=8,'shuf'=4] {'shuf'}, dimensions={0}, use_global_device_ids=true | all-gather | bytes 819200 | tf_op jit(solution)/shard_map/all_gather | solution.py:318
  78.8 3.6 %shard_map.146 = bf16[8,304,128]{2,1,0:T(8,128)(2,1)} custom-call(s32[1]{0:T(128)} %bitcast.7.which_ref, bf16[4,256,128]{2,1,0:T(8,128)(2,1)S(1)} %bitcast.25, bf16[4,256,128]{2,1,0:T(8,128)(2,1)S(1)} %bitcast.26, bf16[4,256,128]{2,1,0:T(8,128)(2,1)S(1)} %bitcast.27, bf16[4,320,256]{2,1,0:T(8,128)(2,1)S(1)} %bitcast.21, bf16[128,1024]{1,0:T(8,128)(2,1)S(1)} %copy-done.9, ...), custom_call_target="tpu_custom_call" | custom-call | flops 1879048192 | bytes 1867776 | tf_op jit(solution)/shard_map/pallas_call | solution.py:326
  82.3 3.5 %all-to-all-start = ((bf16[8,304,128]{2,1,0:T(8,128)(2,1)}), bf16[8,304,128]{2,1,0:T(8,128)(2,1)S(1)}, u32[]{:S(2)}, u32[]{:S(2)}) async-start(bf16[8,304,128]{2,1,0:T(8,128)(2,1)} %shard_map.146), calls=%async_computation | async-start | bytes 1245184 | tf_op jit(solution)/shard_map/all_to_all | solution.py:336
  85.9 0.1 dynamic-slice_convert_fusion
  86.0 0.6 add.38
  86.6 16.6 %all-to-all-done.in_ref = bf16[8,304,128]{2,1,0:T(8,128)(2,1)S(1)} async-done(((bf16[8,304,128]{2,1,0:T(8,128)(2,1)}), bf16[8,304,128]{2,1,0:T(8,128)(2,1)S(1)}, u32[]{:S(2)}, u32[]{:S(2)}) %all-to-all-start) | async-done | bytes 622624 | tf_op jit(solution)/shard_map/all_to_all | solution.py:336
  103.3 0.1 shard_map.147
  103.3 31.6 %all-gather.5 = bf16[2432,128]{1,0:T(8,128)(2,1)S(1)} all-gather(bf16[304,128]{1,0:T(8,128)(2,1)S(1)} %shard_map.147), channel_id=7, replica_groups=mesh['dom'=8,'shuf'=4] {'dom'}, dimensions={0}, use_global_device_ids=true | all-gather | bytes 700416 | tf_op jit(solution)/shard_map/all_gather | solution.py:340
  135.0 1.1 shard_map.148
  136.0 1.2 copy.26
  (31 shorter events, 0.1 us)
Async XLA Ops:
  0.6 0.9 copy-start.2
  1.5 0.7 copy-start.14
  2.2 0.7 copy-start.16
  2.8 0.7 copy-start.18
  4.8 0.6 copy-start.4
  5.4 18.2 %collective-permute-start = (f32[2,128,128]{2,1,0:T(8,128)}, f32[2,128,128]{2,1,0:T(8,128)}, u32[]{:S(2)}, u32[]{:S(2)}) collective-permute-start(f32[2,128,128]{2,1,0:T(8,128)} %get-tuple-element.16), channel_id=1, source_target_pairs={{0,4},{4,8},{8,12},{12,16},{16,20},{20,24},{24,28},{28,0},{1,5},{5... | collective-permute-start | bytes 393224 | tf_op jit(solution)/shard_map/ppermute | solution.py:28
  8.4 15.2 %collective-permute-start.1 = (f32[2,128,128]{2,1,0:T(8,128)}, f32[2,128,128]{2,1,0:T(8,128)}, u32[]{:S(2)}, u32[]{:S(2)}) collective-permute-start(f32[2,128,128]{2,1,0:T(8,128)} %get-tuple-element.17), channel_id=1, source_target_pairs={{0,28},{4,0},{8,4},{12,8},{16,12},{20,16},{24,20},{28,24},{1,29},{... | collective-permute-start | bytes 393224 | tf_op jit(solution)/shard_map/ppermute | solution.py:28
  17.0 6.6 %copy-start = (f32[8,128,128]{2,1,0:T(8,128)S(1)}, f32[8,128,128]{2,1,0:T(8,128)}, u32[]{:S(2)}) copy-start(f32[8,128,128]{2,1,0:T(8,128)} %tiles_ref.5) | copy-start | bytes 1572868
  17.1 6.6 %copy-start.3 = (f32[256,128]{1,0:T(8,128)S(1)}, f32[256,128]{1,0:T(8,128)}, u32[]{:S(2)}) copy-start(f32[256,128]{1,0:T(8,128)} %param.12) | copy-start | bytes 393220
  17.1 6.6 %copy-start.15 = (s32[2]{0:T(128)S(1)}, s32[2]{0:T(128)}, u32[]{:S(2)}) copy-start(s32[2]{0:T(128)} %sl_ref.5) | copy-start | bytes 28
  17.1 6.5 %copy-start.17 = (s32[2]{0:T(128)S(1)}, s32[2]{0:T(128)}, u32[]{:S(2)}) copy-start(s32[2]{0:T(128)} %sr_ref.5) | copy-start | bytes 28
  17.1 6.5 %copy-start.19 = (s32[1,2]{1,0:T(1,128)S(1)}, s32[1,2]{1,0:T(1,128)}, u32[]{:S(2)}) copy-start(s32[1,2]{1,0:T(1,128)} %sc_ref.5) | copy-start | bytes 28
  17.1 6.5 %copy-start.20 = (s32[8]{0:T(128)S(1)}, s32[8]{0:T(128)}, u32[]{:S(2)}) copy-start(s32[8]{0:T(128)} %dst_ref.5) | copy-start | bytes 100
  19.4 13.3 %copy-start.5 = (bf16[256,128]{1,0:T(8,128)(2,1)S(1)}, bf16[256,128]{1,0:T(8,128)(2,1)}, u32[]{:S(2)}) copy-start(bf16[256,128]{1,0:T(8,128)(2,1)} %copy-done.4) | copy-start | bytes 196612
  23.7 0.7 copy-start.21
  26.7 0.6 copy-start.10
  27.3 0.7 copy-start.12
  28.0 20.9 %copy-start.11 = (bf16[256,128]{1,0:T(8,128)(2,1)S(1)}, bf16[256,128]{1,0:T(8,128)(2,1)}, u32[]{:S(2)}) copy-start(bf16[256,128]{1,0:T(8,128)(2,1)} %copy-done.10) | copy-start | bytes 196612
  28.0 26.8 %collective-permute-start.2 = (f32[2,128,128]{2,1,0:T(8,128)}, f32[2,128,128]{2,1,0:T(8,128)}, u32[]{:S(2)}, u32[]{:S(2)}) collective-permute-start(f32[2,128,128]{2,1,0:T(8,128)} %get-tuple-element.19), channel_id=1, source_target_pairs={{0,4},{4,8},{8,12},{12,16},{16,20},{20,24},{24,28},{28,0},{1,5},{5... | collective-permute-start | bytes 393224 | tf_op jit(solution)/shard_map/ppermute | solution.py:28
  28.0 26.8 %collective-permute-start.3 = (f32[2,128,128]{2,1,0:T(8,128)}, f32[2,128,128]{2,1,0:T(8,128)}, u32[]{:S(2)}, u32[]{:S(2)}) collective-permute-start(f32[2,128,128]{2,1,0:T(8,128)} %get-tuple-element.20), channel_id=1, source_target_pairs={{0,28},{4,0},{8,4},{12,8},{16,12},{20,16},{24,20},{28,24},{1,29},{... | collective-permute-start | bytes 393224 | tf_op jit(solution)/shard_map/ppermute | solution.py:28
  46.3 8.5 %copy-start.13 = (f32[2,128,128]{2,1,0:T(8,128)S(1)}, f32[2,128,128]{2,1,0:T(8,128)}, u32[]{:S(2)}) copy-start(f32[2,128,128]{2,1,0:T(8,128)} %copy-done.12) | copy-start | bytes 393220
  46.3 15.5 %copy-start.1 = (bf16[128,1024]{1,0:T(8,128)(2,1)S(1)}, bf16[128,1024]{1,0:T(8,128)(2,1)}, u32[]{:S(2)}) copy-start(bf16[128,1024]{1,0:T(8,128)(2,1)} %get-tuple-element.45.w_ref) | copy-start | bytes 786436
  47.5 0.8 copy-start.6
  48.9 19.9 %copy-start.23 = (s32[8]{0:T(128)S(1)}, s32[8]{0:T(128)}, u32[]{:S(2)}) copy-start(s32[8]{0:T(128)} %src_ref.5) | copy-start | bytes 100
  48.9 19.9 %copy-start.24 = (s32[1,256]{1,0:T(1,128)S(1)}, s32[1,256]{1,0:T(1,128)}, u32[]{:S(2)}) copy-start(s32[1,256]{1,0:T(1,128)} %order_ref.1) | copy-start | bytes 3076
  54.8 0.7 copy-start.22
  57.1 11.7 %collective-permute-start.4 = (f32[2,128,128]{2,1,0:T(8,128)S(1)}, f32[2,128,128]{2,1,0:T(8,128)S(1)}, u32[]{:S(2)}, u32[]{:S(2)}) collective-permute-start(f32[2,128,128]{2,1,0:T(8,128)S(1)} %get-tuple-element.22), channel_id=1, source_target_pairs={{0,4},{4,8},{8,12},{12,16},{16,20},{20,24},{24,28},{28,0},{1,5},{5... | collective-permute-start | bytes 393224 | tf_op jit(solution)/shard_map/ppermute | solution.py:28
  57.1 11.6 %collective-permute-start.5 = (f32[2,128,128]{2,1,0:T(8,128)S(1)}, f32[2,128,128]{2,1,0:T(8,128)S(1)}, u32[]{:S(2)}, u32[]{:S(2)}) collective-permute-start(f32[2,128,128]{2,1,0:T(8,128)S(1)} %get-tuple-element.23), channel_id=1, source_target_pairs={{0,28},{4,0},{8,4},{12,8},{16,12},{20,16},{24,20},{28,24},{1,29},{... | collective-permute-start | bytes 393224 | tf_op jit(solution)/shard_map/ppermute | solution.py:28
  62.4 16.4 %copy-start.7 = (bf16[1024,128]{1,0:T(8,128)(2,1)S(1)}, bf16[1024,128]{1,0:T(8,128)(2,1)}, u32[]{:S(2)}) copy-start(bf16[1024,128]{1,0:T(8,128)(2,1)} %all-gather.2) | copy-start | bytes 786436
  62.4 16.4 %copy-start.8 = (bf16[4,128,256]{1,2,0:T(8,128)(2,1)S(1)}, bf16[4,128,256]{1,2,0:T(8,128)(2,1)}, u32[]{:S(2)}) copy-start(bf16[4,128,256]{1,2,0:T(8,128)(2,1)} %copy.27) | copy-start | bytes 786436
  62.4 16.4 %copy-start.9 = (bf16[128,1024]{1,0:T(8,128)(2,1)S(1)}, bf16[128,1024]{1,0:T(8,128)(2,1)}, u32[]{:S(2)}) copy-start(bf16[128,1024]{1,0:T(8,128)(2,1)} %get-tuple-element.42.wq_ref) | copy-start | bytes 786436
  82.3 20.9 %all-to-all-start = ((bf16[8,304,128]{2,1,0:T(8,128)(2,1)}), bf16[8,304,128]{2,1,0:T(8,128)(2,1)S(1)}, u32[]{:S(2)}, u32[]{:S(2)}) async-start(bf16[8,304,128]{2,1,0:T(8,128)(2,1)} %shard_map.146), calls=%async_computation | async-start | bytes 1245184 | tf_op jit(solution)/shard_map/all_to_all | solution.py:336

commit v2 on v1

v2 whole, which is shorter than its diff:
```python
import functools
import math

import jax
import jax.numpy as jnp
from jax import lax
from jax.experimental import pallas as pl
from jax.experimental.pallas import tpu as pltpu
from jax.sharding import PartitionSpec as P

HOPS = 3
LANES = 128
VMEM_LIMIT = 24 * 1024 * 1024

IN_VMEM = pl.BlockSpec(memory_space=pltpu.VMEM)
IN_SMEM = pl.BlockSpec(memory_space=pltpu.SMEM)
BF16 = jnp.bfloat16
F32 = jnp.float32


def up_to(value, multiple):
    return -(-value // multiple) * multiple


def passed_along(value, axis, steps):
    count = lax.axis_size(axis)
    pairs = [(source, (source + steps) % count) for source in range(count)]
    return lax.ppermute(value, axis, pairs)


def matmul(left, right, dims=((1,), (0,)), precision=None):
    return lax.dot_general(
        left, right, (dims, ((), ())), precision=precision, preferred_element_type=F32
    )


def call(kernel, out_shape, in_specs, flops, scratch=()):
    many = isinstance(out_shape, (list, tuple))
    outs = out_shape if many else [out_shape]
    moved = sum(math.prod(one.shape) * one.dtype.itemsize for one in outs)
    return pl.pallas_call(
        kernel,
        out_shape=out_shape,
        in_specs=in_specs,
        out_specs=[IN_VMEM] * len(outs) if many else IN_VMEM,
        scratch_shapes=list(scratch),
        compiler_params=pltpu.CompilerParams(vmem_limit_bytes=VMEM_LIMIT),
        cost_estimate=pl.CostEstimate(
            flops=flops, bytes_accessed=3 * moved, transcendentals=0
        ),
    )


class Plan:
    def __init__(self, tiles, slots):
        self.tiles = tiles
        self.slots = slots
        self.dst = 0
        self.src = tiles
        self.count = 2 * tiles
        self.left = 2 * tiles + 1
        self.right = self.left + slots
        self.sent = self.right + slots


def write_sends(plan, plan_ref, blocks, left_ref, right_ref):
    for slot in range(plan.slots):
        for out_ref, ids, side in ((left_ref, plan.left, 0), (right_ref, plan.right, 1)):
            index = plan_ref[ids + slot]
            picked = blocks[0]
            for number in range(1, len(blocks)):
                picked = jnp.where(index == number, blocks[number], picked)
            out_ref[slot] = jnp.where(slot < plan_ref[plan.sent + side], picked, 0.0)


def first_kernel(plan, plan_ref, feat_ref, label_ref, left_ref, right_ref, b_ref):
    blocks = [feat_ref[number] for number in range(feat_ref.shape[0])]
    write_sends(plan, plan_ref, blocks, left_ref, right_ref)
    size = blocks[0].shape[0]
    for number, block in enumerate(blocks):
        b_ref[number * size : (number + 1) * size] = block.astype(BF16)
    width = b_ref.shape[1]
    nodes = label_ref.shape[1]
    per_piece = nodes // width
    place = lax.broadcasted_iota(jnp.int32, (16, width), 0)
    packed = jnp.zeros((16, width), F32)
    for piece in range(2):
        value = label_ref[...] & 255 if piece == 0 else label_ref[...] >> 8
        value = value.astype(F32)
        for part in range(per_piece):
            packed = jnp.where(
                place == piece * per_piece + part,
                value[:, part * width : (part + 1) * width],
                packed,
            )
    b_ref[nodes:] = packed.astype(BF16)


def next_blocks(plan, plan_ref, cur_ref, low_ref, high_ref, tiles_ref, ext_ref):
    local = cur_ref.shape[0]
    slots = low_ref.shape[0]
    ext_ref[:local] = cur_ref[...]
    ext_ref[local : local + slots] = low_ref[...]
    ext_ref[local + slots :] = high_ref[...]
    totals = [jnp.zeros(cur_ref.shape[1:], F32) for _ in range(local)]
    live = plan_ref[plan.count]
    for tile in range(plan.tiles):
        product = matmul(
            tiles_ref[tile],
            ext_ref[plan_ref[plan.src + tile]],
            precision=lax.Precision.HIGHEST,
        )
        wanted = jnp.where(tile < live, plan_ref[plan.dst + tile], -1)
        for number in range(local):
            totals[number] = totals[number] + jnp.where(wanted == number, product, 0.0)
    return totals


def hop_kernel(
    plan, plan_ref, cur_ref, low_ref, high_ref, tiles_ref,
    next_ref, left_ref, right_ref, b_ref, ext_ref,
):
    blocks = next_blocks(plan, plan_ref, cur_ref, low_ref, high_ref, tiles_ref, ext_ref)
    write_sends(plan, plan_ref, blocks, left_ref, right_ref)
    for number, block in enumerate(blocks):
        size = block.shape[0]
        next_ref[number] = block
        b_ref[number * size : (number + 1) * size] = block.astype(BF16)


def branch_logits(branch, rows, w_ref, wc_ref):
    hidden = jnp.maximum(matmul(rows, w_ref[branch]), 0.0).astype(BF16)
    hid = hidden.shape[1]
    return matmul(wc_ref[:, branch * hid : (branch + 1) * hid], hidden, ((1,), (1,)))


def forward_kernel(branch, cur_ref, w_ref, wc_ref, *refs):
    rows = cur_ref[...].reshape(-1, cur_ref.shape[2]).astype(BF16)
    part = branch_logits(branch, rows, w_ref, wc_ref)
    if len(refs) == 2:
        part = refs[0][...] + part
    refs[-1][...] = part


def last_kernel(
    plan, row_scale, plan_ref,
    cur_ref, low_ref, high_ref, tiles_ref, before_ref, w_ref, wc_ref, order_ref, label_ref,
    out_ref, ext_ref,
):
    blocks = next_blocks(plan, plan_ref, cur_ref, low_ref, high_ref, tiles_ref, ext_ref)
    halves = [block.astype(BF16) for block in blocks]
    rows_b = jnp.concatenate(halves, axis=0)
    size, width = halves[0].shape
    for number, half in enumerate(halves):
        out_ref[:size, number * width : (number + 1) * width] = half
    logits = before_ref[...] + branch_logits(w_ref.shape[0] - 1, rows_b, w_ref, wc_ref)
    classes, rows = logits.shape
    kept = up_to(classes, 16)
    place = (order_ref[...] == lax.broadcasted_iota(jnp.int32, (rows, rows), 0)).astype(F32)
    place = place.astype(BF16)
    pieces = matmul(label_ref[...], place, ((1,), (1,)))
    label = (pieces[0:1] + 256.0 * pieces[1:2]).astype(jnp.int32)
    hit = lax.broadcasted_iota(jnp.int32, (classes, rows), 0) == label
    top = jnp.max(logits, axis=0, keepdims=True)
    log_total = top + jnp.log(jnp.sum(jnp.exp(logits - top), axis=0, keepdims=True))
    loss = log_total - jnp.sum(jnp.where(hit, logits, 0.0), axis=0, keepdims=True)
    dlogits = (jnp.exp(logits - log_total) - jnp.where(hit, 1.0, 0.0)) * row_scale
    out_ref[size + kept - 16 : size + kept] = jnp.zeros((16, rows), BF16)
    out_ref[size : size + classes] = dlogits.astype(BF16)
    number = lax.broadcasted_iota(jnp.int32, (16, rows), 0)
    packed = jnp.zeros((16, rows), F32)
    rest = loss
    for piece in range(3):
        part = rest.astype(BF16).astype(F32)
        packed = jnp.where(number == piece, part, packed)
        rest = rest - part
    out_ref[size + kept :] = matmul(packed.astype(BF16), place).astype(BF16)


def weights_kernel(w_ref, wc_ref, wt_ref, wct_ref, pad_ref):
    branches, own, kept = wct_ref.shape
    classes = wc_ref.shape[0]
    hid = w_ref.shape[2]
    first = lax.axis_index("shuf") * own
    pad_ref[...] = jnp.zeros_like(pad_ref)
    for branch in range(branches):
        columns = w_ref[branch, :, pl.ds(pl.multiple_of(first, LANES), own)]
        wt_ref[branch] = columns.astype(F32).T.astype(BF16)
        columns = wc_ref[:, pl.ds(pl.multiple_of(branch * hid + first, LANES), own)]
        pad_ref[:classes] = columns.astype(F32)
        wct_ref[branch] = pad_ref[...].T[:, :kept].astype(BF16)


def all_chunks(kept, b0_ref, b1_ref, b2_ref, last_ref, w_ref, wt_ref, wct_ref, chunks_ref):
    group = last_ref.shape[0]
    branches, own, width = wt_ref.shape
    nodes = b1_ref.shape[1]
    hid = w_ref.shape[2]
    parts = last_ref.shape[2] // width
    size = nodes // parts
    all_rows = []
    for b_ref in (b0_ref, b1_ref, b2_ref):
        all_rows.append(
            jnp.concatenate([b_ref[member, :nodes] for member in range(group)], axis=0)
        )
    last_rows = []
    for member in range(group):
        for part in range(parts):
            last_rows.append(last_ref[member, :size, part * width : (part + 1) * width])
    all_rows.append(jnp.concatenate(last_rows, axis=0))
    dlogits_t = jnp.concatenate(
        [last_ref[member, size : size + kept] for member in range(group)], axis=1
    )
    own_class = branches * own
    first = lax.axis_index("shuf") * own_class
    which = first // hid
    columns = pl.ds(pl.multiple_of(first - which * hid, LANES), own_class)
    chosen = all_rows[0]
    for branch in range(1, branches):
        chosen = jnp.where(which == branch, all_rows[branch], chosen)
    hidden = jnp.maximum(matmul(chosen, w_ref[which, :, columns]), 0.0).astype(BF16)
    class_t = matmul(dlogits_t, hidden)
    for chunk in range(chunks_ref.shape[0]):
        chunks_ref[chunk, :kept] = class_t[:, chunk * LANES : (chunk + 1) * LANES]
    per_branch = chunks_ref.shape[0] // branches
    for branch, rows in enumerate(all_rows):
        live = matmul(wt_ref[branch], rows, ((1,), (1,))) > 0.0
        dhidden_t = jnp.where(live, matmul(wct_ref[branch], dlogits_t), 0.0).astype(BF16)
        branch_t = matmul(dhidden_t, rows)
        for part in range(per_branch):
            chunks_ref[branch * per_branch + part, kept:] = branch_t[
                part * LANES : (part + 1) * LANES
            ]


def grad_kernel(kept, *refs):
    ins, outs, chunks_ref = refs[:7], refs[7:-1], refs[-1]
    all_chunks(kept, *ins, chunks_ref)
    dom = lax.axis_index("dom")
    half = len(outs) // 2
    for step in range(half):
        stays = dom ^ (2 * step)
        outs[step][...] = chunks_ref[stays]
        outs[half + step][...] = chunks_ref[stays ^ 1].astype(BF16)


def write_chunk(kept, chunk, value, branch_ref, class_ref):
    per_branch = branch_ref.shape[2] // LANES
    start = pl.multiple_of(chunk * LANES, LANES)
    class_ref[:, pl.ds(start, LANES)] = value[: class_ref.shape[0]]
    branch = chunk // per_branch
    start = pl.multiple_of((chunk - branch * per_branch) * LANES, LANES)
    branch_ref[branch, :, pl.ds(start, LANES)] = value[kept:].T


def out_kernel(kept, *refs):
    ins, branch_ref, class_ref = refs[:-2], refs[-2], refs[-1]
    dom = lax.axis_index("dom")
    half = len(ins) // 2
    for step in range(half):
        for side in range(2):
            value = ins[side * half + step][...].astype(F32)
            write_chunk(kept, dom ^ (2 * step + side), value, branch_ref, class_ref)


def plain_out_kernel(kept, in_ref, branch_ref, class_ref):
    for chunk in range(in_ref.shape[0]):
        write_chunk(kept, chunk, in_ref[chunk], branch_ref, class_ref)


def swapped(value, distance):
    pairs = [(source, source ^ distance) for source in range(lax.axis_size("dom"))]
    return lax.ppermute(value, "dom", pairs)


def body(
    features, tile_values, tile_dst, tile_src, tile_count, send_left, send_right,
    send_count, batch_order, labels, w_branch, w_class,
):
    block = tile_values.shape[1]
    nodes, width = features.shape
    local = nodes // block
    slots = send_left.shape[0]
    tiles = tile_values.shape[0]
    branches, _, hid = w_branch.shape
    cat, classes = w_class.shape
    dom = lax.axis_size("dom")
    shuf = lax.axis_size("shuf")
    mine = lax.axis_index("shuf")
    share = nodes // shuf
    own = hid // shuf
    own_class = cat // shuf
    kept = up_to(classes, 16)
    row_scale = 1.0 / math.sqrt(float(nodes * dom * shuf))
    plan = Plan(tiles, slots)
    small = jnp.concatenate(
        [tile_dst, tile_src, tile_count, send_left, send_right, send_count.reshape(-1)]
    )
    blocks_f32 = jax.ShapeDtypeStruct((local, block, width), F32)
    slots_f32 = jax.ShapeDtypeStruct((slots, block, width), F32)
    rows_b16 = jax.ShapeDtypeStruct((nodes, width), BF16)
    first_b16 = jax.ShapeDtypeStruct((nodes + 16, width), BF16)
    logits_f32 = jax.ShapeDtypeStruct((classes, nodes), F32)
    w_class_t = w_class.T

    current = features.reshape(local, block, width)
    to_left, to_right, rows = call(
        functools.partial(first_kernel, plan),
        [slots_f32, slots_f32, first_b16],
        [IN_SMEM, IN_VMEM, IN_VMEM],
        1000,
    )(small, current, labels.reshape(1, nodes))
    gathered = []
    logits = []
    hop_flops = 12 * tiles * block * block * width
    forward_flops = 2 * nodes * hid * (width + classes)
    ext = pltpu.VMEM((local + 2 * slots, block, width), F32)
    for hop in range(HOPS):
        from_lower = passed_along(to_right, "dom", 1)
        from_upper = passed_along(to_left, "dom", -1)
        gathered.append(lax.all_gather(rows, "shuf"))
        logits = [
            call(
                functools.partial(forward_kernel, hop),
                logits_f32,
                [IN_VMEM] * (3 + len(logits)),
                forward_flops,
            )(current, w_branch, w_class_t, *logits)
        ]
        if hop < HOPS - 1:
            current, to_left, to_right, rows = call(
                functools.partial(hop_kernel, plan),
                [blocks_f32, slots_f32, slots_f32, rows_b16],
                [IN_SMEM] + [IN_VMEM] * 4,
                hop_flops,
                [ext],
            )(small, current, from_lower, from_upper, tile_values)

    pieces = gathered[0][:, nodes : nodes + 2 * nodes // width].reshape(shuf, 2, shuf, share)
    pieces = lax.dynamic_index_in_dim(pieces, mine, 2, keepdims=False)
    label_mine = jnp.pad(pieces.transpose(1, 0, 2).reshape(2, nodes), ((0, 14), (0, 0)))

    wt_own, wct_own = call(
        weights_kernel,
        [
            jax.ShapeDtypeStruct((branches, own, width), BF16),
            jax.ShapeDtypeStruct((branches, own, kept), BF16),
        ],
        [IN_VMEM] * 2,
        1000,
        [pltpu.VMEM((up_to(classes, LANES), own), F32)],
    )(w_branch, w_class_t)

    payload = call(
        functools.partial(last_kernel, plan, row_scale),
        jax.ShapeDtypeStruct((block + kept + 16, local * width), BF16),
        [IN_SMEM] + [IN_VMEM] * 9,
        hop_flops + forward_flops,
        [ext],
    )(
        small, current, from_lower, from_upper, tile_values,
        *logits, w_branch, w_class_t, batch_order, label_mine,
    )
    last_all = lax.all_gather(payload, "shuf")
    loss_parts = lax.dynamic_slice(
        last_all, (0, block + kept, mine * share), (shuf, 3, share)
    ).astype(F32)
    loss_rows = (loss_parts[:, 0] + loss_parts[:, 1] + loss_parts[:, 2]).reshape(nodes)

    chunks = own_class // LANES
    height = kept + width
    grad_flops = 2 * shuf * nodes * own_class * (3 * width + 2 * kept)
    grad_ins = (*gathered, last_all, w_branch, wt_own, wct_own)
    outs = [
        jax.ShapeDtypeStruct((branches, width, own), F32),
        jax.ShapeDtypeStruct((classes, own_class), F32),
    ]
    chunks_f32 = pltpu.VMEM((chunks, height, LANES), F32)
    if chunks == dom and dom % 2 == 0 and dom & (dom - 1) == 0:
        half = dom // 2
        one_f32 = jax.ShapeDtypeStruct((height, LANES), F32)
        one_b16 = jax.ShapeDtypeStruct((height, LANES), BF16)
        made = call(
            functools.partial(grad_kernel, kept),
            [one_f32] * half + [one_b16] * half,
            [IN_VMEM] * 7,
            grad_flops,
            [chunks_f32],
        )(*grad_ins)
        order = list(range(1, half)) + [0]
        arrived = {step: swapped(made[half + step], 1) for step in order}
        total = {step: made[step] + arrived[step].astype(F32) for step in order}
        far = [swapped(total[step].astype(BF16), 2 * step) for step in range(1, half)]
        summed = total[0]
        for value in far:
            summed = summed + value.astype(F32)
        near = [summed.astype(BF16)]
        for step in range(1, half):
            near.append(swapped(near[0], 2 * step))
        other = [swapped(value, 1) for value in near]
        grad_branch, grad_class_t = call(
            functools.partial(out_kernel, kept), outs, [IN_VMEM] * dom, 1000
        )(*near, *other)
    else:
        grads = call(
            functools.partial(all_chunks, kept),
            jax.ShapeDtypeStruct((chunks, height, LANES), F32),
            [IN_VMEM] * 7,
            grad_flops,
        )(*grad_ins)
        grad_branch, grad_class_t = call(
            functools.partial(plain_out_kernel, kept), outs, [IN_VMEM], 1000
        )(lax.psum(grads, "dom"))
    return (loss_rows, grad_branch, grad_class_t.T)


def solution(mesh):
    return jax.shard_map(
        body,
        mesh=mesh,
        in_specs=(
            P(("dom", "shuf"), None),
            P(("dom", "shuf"), None, None),
            P(("dom", "shuf")),
            P(("dom", "shuf")),
            P(("dom", "shuf")),
            P(("dom", "shuf")),
            P(("dom", "shuf")),
            P(("dom", "shuf"), None),
            P(("dom", "shuf"), None),
            P(("dom", "shuf")),
            P(),
            P(),
        ),
        out_specs=(P(("dom", "shuf")), P(None, None, "shuf"), P("shuf", None)),
        check_vma=False,
    )
```

time: 138 us -> 100 us (0.72)
  blocking collectives: 62.9 us -> 25.6 us
  local copies, waits for them, and re-layouts: 23.4 us -> 12.2 us
  starting transfers between devices: 19 us -> 29.7 us
  waiting for transfers between devices: 16.6 us -> 18.6 us
  Pallas kernels: 13.6 us -> 12.1 us
    all_gather x2 -> x0, blocking collectives: 36.9 us -> none  [the longest x1 31.6 us: body(): summed = lax.all_gather(part, 'dom')]
    all_to_all x1 -> x0, waiting for transfers between devices: 16.6 us -> none  [body(): lax.all_to_all(grads, 'dom', split_axis=0, concat_axis=0, tiled=True)]
    ppermute x0 -> x14, starting transfers between devices: none -> 14.1 us  [swapped(): return lax.ppermute(value, 'dom', pairs)]
    ppermute x0 -> x14, waiting for transfers between devices: none -> 13.9 us  [swapped(): return lax.ppermute(value, 'dom', pairs)]
    unnamed x53 -> x35, local copies, waits for them, and re-layouts: 13.7 us -> 5.53 us
    ppermute x6, waiting for transfers between devices: 0.02 us -> 4.68 us  [passed_along(): return lax.ppermute(value, axis, pairs)]
    all_to_all x1 -> x0, starting transfers between devices: 3.54 us -> none  [body(): lax.all_to_all(grads, 'dom', split_axis=0, concat_axis=0, tiled=True)]
    dynamic_slice x3 -> x1, local copies, waits for them, and re-layouts: 3.61 us -> 0.7 us  [body(): pieces = lax.dynamic_index_in_dim(pieces, mine, 2, keepdims=False)]
  transfers between devices with their start and end apart: 7 -> 20, of which waited for: 1 -> 10; matrix products, arithmetic and copies ran while one was open for 11% -> 6% of each run, Pallas kernels for 1% -> 2%
where the time goes in v2:
time: 100 us
  starting transfers between devices  29.7 us (30%)
  blocking collectives  25.6 us (26%)
  waiting for transfers between devices  18.6 us (19%)
  local copies, waits for them, and re-layouts  12.2 us (12%)
  Pallas kernels  12.1 us (12%)
  between operations  1.59 us (2%)
    all_gather x3, blocking collectives, body(): gathered.append(lax.all_gather(rows, 'shuf'))  17.6 us
    ppermute x6, starting transfers between devices, passed_along(): return lax.ppermute(value, axis, pairs)  15.6 us
    ppermute x14, starting transfers between devices, swapped(): return lax.ppermute(value, 'dom', pairs)  14.1 us
    ppermute x14, waiting for transfers between devices, swapped(): return lax.ppermute(value, 'dom', pairs)  13.9 us
    all_gather x1, blocking collectives, body(): last_all = lax.all_gather(payload, 'shuf')  7.99 us
    unnamed x35, local copies, waits for them, and re-layouts  5.53 us
    ppermute x6, waiting for transfers between devices, passed_along(): return lax.ppermute(value, axis, pairs)  4.68 us
    pallas_call x2, Pallas kernels, body(): call(functools.partial(hop_kernel, plan), [blocks_f32, slots_f32, slots_f...  3.53 us
  transfers between devices with their start and end apart: 20, of which 10 were waited for; matrix products, arithmetic and copies ran while one was open for 6% of the time, Pallas kernels for 2%

profile of v2, /device:TPU:0, one launch (start us, length us, event | category | flops | bytes accessed | tf_op | source)
XLA Modules:
  0.0 100.0 jit_solution(9457011099168086530)
XLA Ops:
  1.4 0.8 concatenate.3.plan_ref
  2.2 0.9 copy-done.5
  3.1 0.7 copy-done.11
  3.8 0.6 shard_map.139
  4.3 3.0 %collective-permute-start = (f32[2,128,128]{2,1,0:T(8,128)S(1)}, f32[2,128,128]{2,1,0:T(8,128)S(1)}, u32[]{:S(2)}, u32[]{:S(2)}) collective-permute-start(f32[2,128,128]{2,1,0:T(8,128)S(1)} %get-tuple-element.26), channel_id=1, source_target_pairs={{0,4},{4,8},{8,12},{12,16},{16,20},{20,24},{24,28},{28,0},{1,5},{5... | collective-permute-start | bytes 393224 | tf_op jit(solution)/shard_map/ppermute | solution.py:28
  7.4 3.1 %collective-permute-start.1 = (f32[2,128,128]{2,1,0:T(8,128)S(1)}, f32[2,128,128]{2,1,0:T(8,128)S(1)}, u32[]{:S(2)}, u32[]{:S(2)}) collective-permute-start(f32[2,128,128]{2,1,0:T(8,128)S(1)} %get-tuple-element.27), channel_id=1, source_target_pairs={{0,28},{4,0},{8,4},{12,8},{16,12},{20,16},{24,20},{28,24},{1,29},{... | collective-permute-start | bytes 393224 | tf_op jit(solution)/shard_map/ppermute | solution.py:28
  10.5 3.5 %collective-permute-done.low_ref = f32[2,128,128]{2,1,0:T(8,128)S(1)} collective-permute-done((f32[2,128,128]{2,1,0:T(8,128)S(1)}, f32[2,128,128]{2,1,0:T(8,128)S(1)}, u32[]{:S(2)}, u32[]{:S(2)}) %collective-permute-start) | collective-permute-done | bytes 131104 | tf_op jit(solution)/shard_map/ppermute | solution.py:28
  14.0 1.1 %collective-permute-done.1.high_ref = f32[2,128,128]{2,1,0:T(8,128)S(1)} collective-permute-done((f32[2,128,128]{2,1,0:T(8,128)S(1)}, f32[2,128,128]{2,1,0:T(8,128)S(1)}, u32[]{:S(2)}, u32[]{:S(2)}) %collective-permute-start.1) | collective-permute-done | bytes 131104 | tf_op jit(solution)/shard_map/ppermute | solution.py:28
  15.1 1.0 %copy-done.3 = f32[8,128,128]{2,1,0:T(8,128)S(1)} copy-done((f32[8,128,128]{2,1,0:T(8,128)S(1)}, f32[8,128,128]{2,1,0:T(8,128)}, u32[]{:S(2)}) %copy-start.3) | copy-done | bytes 524312
  16.2 1.9 %shard_map.140 = (f32[2,128,128]{2,1,0:T(8,128)S(1)}, f32[2,128,128]{2,1,0:T(8,128)}, f32[2,128,128]{2,1,0:T(8,128)}, bf16[256,128]{1,0:T(8,128)(2,1)S(1)}) custom-call(s32[23]{0:T(128)S(1)} %concatenate.3.plan_ref, f32[2,128,128]{2,1,0:T(8,128)S(1)} %bitcast.20, f32[2,128,128]{2,1,0:T(8,128)S(1)} %collective-permute-done.low_ref, ...), custom_call_target="tpu_custom_call" | custom-call | flops 201326592 | bytes 1376256 | tf_op jit(solution)/shard_map/pallas_call | solution.py:331
  18.1 0.3 collective-permute-start.2
  18.4 4.5 %collective-permute-start.3 = (f32[2,128,128]{2,1,0:T(8,128)}, f32[2,128,128]{2,1,0:T(8,128)}, u32[]{:S(2)}, u32[]{:S(2)}) collective-permute-start(f32[2,128,128]{2,1,0:T(8,128)} %get-tuple-element.30), channel_id=1, source_target_pairs={{0,28},{4,0},{8,4},{12,8},{16,12},{20,16},{24,20},{28,24},{1,29},{... | collective-permute-start | bytes 393224 | tf_op jit(solution)/shard_map/ppermute | solution.py:28
  22.8 5.9 %all-gather = bf16[1088,128]{1,0:T(8,128)(2,1)S(1)} all-gather(bf16[272,128]{1,0:T(8,128)(2,1)S(1)} %get-tuple-element.34), channel_id=2, replica_groups=mesh['dom'=8,'shuf'=4] {'shuf'}, dimensions={0}, use_global_device_ids=true | all-gather | bytes 348160 | tf_op jit(solution)/shard_map/all_gather | solution.py:321
  28.8 1.4 %copy-done = bf16[4096,172]{0,1:T(8,128)(2,1)S(1)} copy-done((bf16[4096,172]{0,1:T(8,128)(2,1)S(1)}, bf16[4096,172]{0,1:T(8,128)(2,1)}, u32[]{:S(2)}) %copy-start) | copy-done | bytes 1409048
  30.1 0.3 shard_map.146
  30.4 0.0 copy-start.13
  30.4 0.8 copy-done.13
  31.2 0.7 copy-done.15
  31.9 0.6 slice.16
  32.5 1.3 %reshape.30 = bf16[4,2,4,64]{3,2,1,0:T(4,128)(2,1)} reshape(bf16[4,4,128]{2,1,0:T(4,128)(2,1)} %slice.16) | data formatting | bytes 8192 | tf_op jit(solution)/shard_map/reshape | solution.py:339
  33.9 0.7 constant_dynamic-slice_fusion
  34.6 0.6 copy.16
  35.2 1.3 %reshape.31 = bf16[2,256]{1,0:T(2,128)(2,1)} reshape(bf16[2,4,64]{2,1,0:T(4,128)(2,1)} %copy.16) | data formatting | bytes 2048 | tf_op jit(solution)/shard_map/reshape | solution.py:341
  36.5 0.7 pad.4.label_ref
  37.2 0.6 shard_map.142.refs_0_
  37.8 0.0 collective-permute-done.2.low_ref
  37.8 0.0 collective-permute-done.3.high_ref
  37.8 1.6 %shard_map.141 = (f32[2,128,128]{2,1,0:T(8,128)S(1)}, f32[2,128,128]{2,1,0:T(8,128)S(1)}, f32[2,128,128]{2,1,0:T(8,128)S(1)}, bf16[256,128]{1,0:T(8,128)(2,1)S(1)}) custom-call(s32[23]{0:T(128)S(1)} %copy-done.10, f32[2,128,128]{2,1,0:T(8,128)S(1)} %get-tuple-element.28.cur_ref, f32[2,128,128]{2,1,0:T(8,128)} %collective-permute-done.2.low_ref, ...), custom_call_target="tpu_custom_call" | custom-call | flops 201326592 | bytes 1376256 | tf_op jit(solution)/shard_map/pallas_call | solution.py:331
  39.5 0.1 collective-permute-start.4
  39.5 4.7 %collective-permute-start.5 = (f32[2,128,128]{2,1,0:T(8,128)S(1)}, f32[2,128,128]{2,1,0:T(8,128)S(1)}, u32[]{:S(2)}, u32[]{:S(2)}) collective-permute-start(f32[2,128,128]{2,1,0:T(8,128)S(1)} %get-tuple-element.33), channel_id=1, source_target_pairs={{0,28},{4,0},{8,4},{12,8},{16,12},{20,16},{24,20},{28,24},{1,29},{... | collective-permute-start | bytes 393224 | tf_op jit(solution)/shard_map/ppermute | solution.py:28
  44.2 5.8 %all-gather.2 = bf16[1024,128]{1,0:T(8,128)(2,1)S(1)} all-gather(bf16[256,128]{1,0:T(8,128)(2,1)S(1)} %copy-done.8), channel_id=4, replica_groups=mesh['dom'=8,'shuf'=4] {'shuf'}, dimensions={0}, use_global_device_ids=true | all-gather | bytes 327680 | tf_op jit(solution)/shard_map/all_gather | solution.py:321
  50.0 0.6 shard_map.143.refs_0_
  50.6 0.0 copy-start.12
  50.6 0.6 shard_map.144.before_ref
  51.2 5.9 %all-gather.3 = bf16[1024,128]{1,0:T(8,128)(2,1)S(1)} all-gather(bf16[256,128]{1,0:T(8,128)(2,1)S(1)} %get-tuple-element.36), channel_id=5, replica_groups=mesh['dom'=8,'shuf'=4] {'shuf'}, dimensions={0}, use_global_device_ids=true | all-gather | bytes 327680 | tf_op jit(solution)/shard_map/all_gather | solution.py:321
  57.1 2.0 %shard_map.145 = bf16[320,256]{1,0:T(8,128)(2,1)S(1)} custom-call(s32[23]{0:T(128)S(1)} %copy-done.10, f32[2,128,128]{2,1,0:T(8,128)S(1)} %get-tuple-element.31.cur_ref, f32[2,128,128]{2,1,0:T(8,128)S(1)} %collective-permute-done.4.low_ref, f32[2,128,128]{2,1,0:T(8,128)S(1)} %collective-permute-done.5.high_ref, f32[8,128,128]{2,1,0:T(8,128)S(1)} %copy-done.4, ...), custom_call_target="tpu_custom_call" | custom-call | flops 358612992 | bytes 491520 | tf_op jit(solution)/shard_map/pallas_call | solution.py:354
  59.1 8.0 %all-gather.1 = bf16[1280,256]{1,0:T(8,128)(2,1)S(1)} all-gather(bf16[320,256]{1,0:T(8,128)(2,1)S(1)} %shard_map.145), channel_id=3, replica_groups=mesh['dom'=8,'shuf'=4] {'shuf'}, dimensions={0}, use_global_device_ids=true | all-gather | bytes 819200 | tf_op jit(solution)/shard_map/all_gather | solution.py:364
  67.1 2.8 %shard_map.147 = (f32[304,128]{1,0:T(8,128)S(1)}, f32[304,128]{1,0:T(8,128)S(1)}, f32[304,128]{1,0:T(8,128)S(1)}, f32[304,128]{1,0:T(8,128)S(1)}, bf16[304,128]{...) custom-call(bf16[4,272,128]{2,1,0:T(8,128)(2,1)S(1)} %bitcast.25, ...), custom_call_target="tpu_custom_call" | custom-call | flops 1543503872 | bytes 2801664 | tf_op jit(solution)/shard_map/pallas_call | solution.py:383
  69.9 0.1 collective-permute-start.7
  70.0 2.0 %collective-permute-start.9 = (bf16[304,128]{1,0:T(8,128)(2,1)S(1)}, bf16[304,128]{1,0:T(8,128)(2,1)S(1)}, u32[]{:S(2)}, u32[]{:S(2)}) collective-permute-start(bf16[304,128]{1,0:T(8,128)(2,1)S(1)} %get-tuple-element.44), channel_id=1, source_target_pairs={{0,4},{4,0},{8,12},{12,8},{16,20},{20,16},{24,28},{28,24},{1,5},{5... | collective-permute-start | bytes 233480 | tf_op jit(solution)/shard_map/ppermute | solution.py:273
  72.0 0.1 collective-permute-start.11
  72.1 1.9 %collective-permute-start.6 = (bf16[304,128]{1,0:T(8,128)(2,1)S(1)}, bf16[304,128]{1,0:T(8,128)(2,1)S(1)}, u32[]{:S(2)}, u32[]{:S(2)}) collective-permute-start(bf16[304,128]{1,0:T(8,128)(2,1)S(1)} %get-tuple-element.40), channel_id=1, source_target_pairs={{0,4},{4,0},{8,12},{12,8},{16,20},{20,16},{24,28},{28,24},{1,5},{5... | collective-permute-start | bytes 233480 | tf_op jit(solution)/shard_map/ppermute | solution.py:273
  74.0 1.1 %collective-permute-done.7 = bf16[304,128]{1,0:T(8,128)(2,1)S(1)} collective-permute-done((bf16[304,128]{1,0:T(8,128)(2,1)S(1)}, bf16[304,128]{1,0:T(8,128)(2,1)S(1)}, u32[]{:S(2)}, u32[]{:S(2)}) %collective-permute-start.7) | collective-permute-done | bytes 77856 | tf_op jit(solution)/shard_map/ppermute | solution.py:273
  75.2 0.1 collective-permute-start.8
  75.2 1.6 %collective-permute-done.9 = bf16[304,128]{1,0:T(8,128)(2,1)S(1)} collective-permute-done((bf16[304,128]{1,0:T(8,128)(2,1)S(1)}, bf16[304,128]{1,0:T(8,128)(2,1)S(1)}, u32[]{:S(2)}, u32[]{:S(2)}) %collective-permute-start.9) | collective-permute-done | bytes 77856 | tf_op jit(solution)/shard_map/ppermute | solution.py:273
  76.8 0.1 collective-permute-start.10
  76.9 1.6 %collective-permute-done.11 = bf16[304,128]{1,0:T(8,128)(2,1)S(1)} collective-permute-done((bf16[304,128]{1,0:T(8,128)(2,1)S(1)}, bf16[304,128]{1,0:T(8,128)(2,1)S(1)}, u32[]{:S(2)}, u32[]{:S(2)}) %collective-permute-start.11) | collective-permute-done | bytes 77856 | tf_op jit(solution)/shard_map/ppermute | solution.py:273
  78.5 1.3 %collective-permute-start.12 = (bf16[304,128]{1,0:T(8,128)(2,1)S(1)}, bf16[304,128]{1,0:T(8,128)(2,1)S(1)}, u32[]{:S(2)}, u32[]{:S(2)}) collective-permute-start(bf16[304,128]{1,0:T(8,128)(2,1)S(1)} %add_convert_fusion.1), channel_id=1, source_target_pairs={{0,24},{4,28},{8,16},{12,20},{16,8},{20,12},{24,0},{28,4},{1,25},{... | collective-permute-start | bytes 233480 | tf_op jit(solution)/shard_map/ppermute | solution.py:273
  79.8 4.2 %collective-permute-done.10 = bf16[304,128]{1,0:T(8,128)(2,1)S(1)} collective-permute-done((bf16[304,128]{1,0:T(8,128)(2,1)S(1)}, bf16[304,128]{1,0:T(8,128)(2,1)S(1)}, u32[]{:S(2)}, u32[]{:S(2)}) %collective-permute-start.10) | collective-permute-done | bytes 77856 | tf_op jit(solution)/shard_map/ppermute | solution.py:273
  84.0 0.9 collective-permute-done.12
  84.9 0.1 add_convert_fusion.refs_0_
  84.9 1.4 %collective-permute-start.13 = (bf16[304,128]{1,0:T(8,128)(2,1)S(1)}, bf16[304,128]{1,0:T(8,128)(2,1)S(1)}, u32[]{:S(2)}, u32[]{:S(2)}) collective-permute-start(bf16[304,128]{1,0:T(8,128)(2,1)S(1)} %add_convert_fusion.refs_0_), channel_id=1, source_target_pairs={{0,8},{4,12},{8,0},{12,4},{16,24},{20,28},{24,16},{28,20},{1,9},{5... | collective-permute-start | bytes 233480 | tf_op jit(solution)/shard_map/ppermute | solution.py:273
  86.3 0.5 collective-permute-start.14
  86.8 2.6 %collective-permute-start.15 = (bf16[304,128]{1,0:T(8,128)(2,1)S(1)}, bf16[304,128]{1,0:T(8,128)(2,1)S(1)}, u32[]{:S(2)}, u32[]{:S(2)}) collective-permute-start(bf16[304,128]{1,0:T(8,128)(2,1)S(1)} %add_convert_fusion.refs_0_), channel_id=1, source_target_pairs={{0,24},{4,28},{8,16},{12,20},{16,8},{20,12},{24,0},{28,4},{1,25},{... | collective-permute-start | bytes 233480 | tf_op jit(solution)/shard_map/ppermute | solution.py:273
  89.4 0.1 dynamic-slice_convert_fusion
  89.5 0.5 collective-permute-start.16
  89.9 1.6 %collective-permute-start.17 = (bf16[304,128]{1,0:T(8,128)(2,1)S(1)}, bf16[304,128]{1,0:T(8,128)(2,1)S(1)}, u32[]{:S(2)}, u32[]{:S(2)}) collective-permute-start(bf16[304,128]{1,0:T(8,128)(2,1)S(1)} %collective-permute-done.13.refs_1_), channel_id=1, source_target_pairs={{0,4},{4,0},{8,12},{12,8},{16,20},{20,16},{24,28},{28,24},{1,5},{5... | collective-permute-start | bytes 233480 | tf_op jit(solution)/shard_map/ppermute | solution.py:273
  91.5 2.1 %collective-permute-done.14.refs_2_ = bf16[304,128]{1,0:T(8,128)(2,1)S(1)} collective-permute-done((bf16[304,128]{1,0:T(8,128)(2,1)S(1)}, bf16[304,128]{1,0:T(8,128)(2,1)S(1)}, u32[]{:S(2)}, u32[]{:S(2)}) %collective-permute-start.14) | collective-permute-done | bytes 77856 | tf_op jit(solution)/shard_map/ppermute | solution.py:273
  93.6 0.3 collective-permute-start.18
  93.9 1.7 %collective-permute-start.19 = (bf16[304,128]{1,0:T(8,128)(2,1)S(1)}, bf16[304,128]{1,0:T(8,128)(2,1)S(1)}, u32[]{:S(2)}, u32[]{:S(2)}) collective-permute-start(bf16[304,128]{1,0:T(8,128)(2,1)S(1)} %collective-permute-done.15.refs_3_), channel_id=1, source_target_pairs={{0,4},{4,0},{8,12},{12,8},{16,20},{20,16},{24,28},{28,24},{1,5},{5... | collective-permute-start | bytes 233480 | tf_op jit(solution)/shard_map/ppermute | solution.py:273
  95.6 0.6 add.46
  96.3 1.7 %collective-permute-done.18.refs_6_ = bf16[304,128]{1,0:T(8,128)(2,1)S(1)} collective-permute-done((bf16[304,128]{1,0:T(8,128)(2,1)S(1)}, bf16[304,128]{1,0:T(8,128)(2,1)S(1)}, u32[]{:S(2)}, u32[]{:S(2)}) %collective-permute-start.18) | collective-permute-done | bytes 77856 | tf_op jit(solution)/shard_map/ppermute | solution.py:273
  98.0 0.8 collective-permute-done.19.refs_7_
  98.8 1.2 %shard_map.148 = (f32[4,128,256]{2,1,0:T(8,128)}, f32[172,1024]{1,0:T(8,128)}) custom-call(bf16[304,128]{1,0:T(8,128)(2,1)S(1)} %add_convert_fusion.refs_0_, bf16[304,128]{1,0:T(8,128)(2,1)S(1)} %collective-permute-done.13.refs_1_, bf16[304,128]{1,0:T(8,128)(2,1)S(1)} %collective-permute-done.14.refs_2_, ...), custom_call_target="tpu_custom_call" | custom-call | flops 1000 | bytes 3686400 | tf_op jit(solution)/shard_map/pallas_call | solution.py:401
  (39 shorter events, 0.2 us)
Async XLA Ops:
  0.6 28.1 %copy-start.2 = (bf16[4,128,1024]{2,1,0:T(8,128)(2,1)S(1)}, bf16[4,128,1024]{2,1,0:T(8,128)(2,1)}, u32[]{:S(2)}) copy-start(bf16[4,128,1024]{2,1,0:T(8,128)(2,1)} %refs_4_.1) | copy-start | bytes 3145732
  2.2 26.6 %copy-start.9 = (s32[23]{0:T(128)}, s32[23]{0:T(128)S(1)}, u32[]{:S(2)}) copy-start(s32[23]{0:T(128)S(1)} %concatenate.3.plan_ref) | copy-start | bytes 280
  2.2 0.9 copy-start.5
  3.1 0.7 copy-start.11
  4.3 9.7 %collective-permute-start = (f32[2,128,128]{2,1,0:T(8,128)S(1)}, f32[2,128,128]{2,1,0:T(8,128)S(1)}, u32[]{:S(2)}, u32[]{:S(2)}) collective-permute-start(f32[2,128,128]{2,1,0:T(8,128)S(1)} %get-tuple-element.26), channel_id=1, source_target_pairs={{0,4},{4,8},{8,12},{12,16},{16,20},{20,24},{24,28},{28,0},{1,5},{5... | collective-permute-start | bytes 393224 | tf_op jit(solution)/shard_map/ppermute | solution.py:28
  7.4 7.8 %collective-permute-start.1 = (f32[2,128,128]{2,1,0:T(8,128)S(1)}, f32[2,128,128]{2,1,0:T(8,128)S(1)}, u32[]{:S(2)}, u32[]{:S(2)}) collective-permute-start(f32[2,128,128]{2,1,0:T(8,128)S(1)} %get-tuple-element.27), channel_id=1, source_target_pairs={{0,28},{4,0},{8,4},{12,8},{16,12},{20,16},{24,20},{28,24},{1,29},{... | collective-permute-start | bytes 393224 | tf_op jit(solution)/shard_map/ppermute | solution.py:28
  15.1 1.0 %copy-start.3 = (f32[8,128,128]{2,1,0:T(8,128)S(1)}, f32[8,128,128]{2,1,0:T(8,128)}, u32[]{:S(2)}) copy-start(f32[8,128,128]{2,1,0:T(8,128)} %tiles_ref.5) | copy-start | bytes 1572868
  18.1 12.3 %copy-start.7 = (bf16[256,128]{1,0:T(8,128)(2,1)}, bf16[256,128]{1,0:T(8,128)(2,1)S(1)}, u32[]{:S(2)}) copy-start(bf16[256,128]{1,0:T(8,128)(2,1)S(1)} %get-tuple-element.35) | copy-start | bytes 196612
  18.1 19.7 %collective-permute-start.2 = (f32[2,128,128]{2,1,0:T(8,128)}, f32[2,128,128]{2,1,0:T(8,128)}, u32[]{:S(2)}, u32[]{:S(2)}) collective-permute-start(f32[2,128,128]{2,1,0:T(8,128)} %get-tuple-element.29), channel_id=1, source_target_pairs={{0,4},{4,8},{8,12},{12,16},{16,20},{20,24},{24,28},{28,0},{1,5},{5... | collective-permute-start | bytes 393224 | tf_op jit(solution)/shard_map/ppermute | solution.py:28
  18.4 19.4 %collective-permute-start.3 = (f32[2,128,128]{2,1,0:T(8,128)}, f32[2,128,128]{2,1,0:T(8,128)}, u32[]{:S(2)}, u32[]{:S(2)}) collective-permute-start(f32[2,128,128]{2,1,0:T(8,128)} %get-tuple-element.30), channel_id=1, source_target_pairs={{0,28},{4,0},{8,4},{12,8},{16,12},{20,16},{24,20},{28,24},{1,29},{... | collective-permute-start | bytes 393224 | tf_op jit(solution)/shard_map/ppermute | solution.py:28
  22.8 14.4 %copy-start.6 = (f32[256,128]{1,0:T(8,128)S(1)}, f32[256,128]{1,0:T(8,128)}, u32[]{:S(2)}) copy-start(f32[256,128]{1,0:T(8,128)} %param.12) | copy-start | bytes 393220
  28.8 1.4 %copy-start = (bf16[4096,172]{0,1:T(8,128)(2,1)S(1)}, bf16[4096,172]{0,1:T(8,128)(2,1)}, u32[]{:S(2)}) copy-start(bf16[4096,172]{0,1:T(8,128)(2,1)} %param.23) | copy-start | bytes 4227076
  30.1 7.0 %copy-start.1 = (bf16[4096,172]{0,1:T(8,128)(2,1)S(1)}, bf16[4096,172]{0,1:T(8,128)(2,1)}, u32[]{:S(2)}) copy-start(bf16[4096,172]{0,1:T(8,128)(2,1)} %param.23) | copy-start | bytes 4227076
  30.4 0.8 copy-start.13
  31.2 0.7 copy-start.15
  31.9 5.9 %copy-start.4 = (f32[8,128,128]{2,1,0:T(8,128)S(1)}, f32[8,128,128]{2,1,0:T(8,128)}, u32[]{:S(2)}) copy-start(f32[8,128,128]{2,1,0:T(8,128)} %tiles_ref.5) | copy-start | bytes 1572868
  36.5 1.3 %copy-start.10 = (s32[23]{0:T(128)S(1)}, s32[23]{0:T(128)}, u32[]{:S(2)}) copy-start(s32[23]{0:T(128)} %copy-done.9) | copy-start | bytes 280
  37.2 7.1 %copy-start.8 = (bf16[256,128]{1,0:T(8,128)(2,1)S(1)}, bf16[256,128]{1,0:T(8,128)(2,1)}, u32[]{:S(2)}) copy-start(bf16[256,128]{1,0:T(8,128)(2,1)} %copy-done.7) | copy-start | bytes 196612
  39.5 17.7 %collective-permute-start.4 = (f32[2,128,128]{2,1,0:T(8,128)S(1)}, f32[2,128,128]{2,1,0:T(8,128)S(1)}, u32[]{:S(2)}, u32[]{:S(2)}) collective-permute-start(f32[2,128,128]{2,1,0:T(8,128)S(1)} %get-tuple-element.32), channel_id=1, source_target_pairs={{0,4},{4,8},{8,12},{12,16},{16,20},{20,24},{24,28},{28,0},{1,5},{5... | collective-permute-start | bytes 393224 | tf_op jit(solution)/shard_map/ppermute | solution.py:28
  39.5 17.6 %collective-permute-start.5 = (f32[2,128,128]{2,1,0:T(8,128)S(1)}, f32[2,128,128]{2,1,0:T(8,128)S(1)}, u32[]{:S(2)}, u32[]{:S(2)}) collective-permute-start(f32[2,128,128]{2,1,0:T(8,128)S(1)} %get-tuple-element.33), channel_id=1, source_target_pairs={{0,28},{4,0},{8,4},{12,8},{16,12},{20,16},{24,20},{28,24},{1,29},{... | collective-permute-start | bytes 393224 | tf_op jit(solution)/shard_map/ppermute | solution.py:28
  50.6 6.5 %copy-start.12 = (s32[1,256]{1,0:T(1,128)S(1)}, s32[1,256]{1,0:T(1,128)}, u32[]{:S(2)}) copy-start(s32[1,256]{1,0:T(1,128)} %order_ref.1) | copy-start | bytes 3076
  57.1 10.0 %copy-start.14 = (bf16[4,256,176]{2,1,0:T(8,128)(2,1)S(1)}, bf16[4,256,176]{2,1,0:T(8,128)(2,1)}, u32[]{:S(2)}) copy-start(bf16[4,256,176]{2,1,0:T(8,128)(2,1)} %copy-done.13) | copy-start | bytes 1081348
  57.1 10.0 %copy-start.16 = (bf16[4,256,128]{2,1,0:T(8,128)(2,1)S(1)}, bf16[4,256,128]{2,1,0:T(8,128)(2,1)}, u32[]{:S(2)}) copy-start(bf16[4,256,128]{2,1,0:T(8,128)(2,1)} %copy-done.15) | copy-start | bytes 786436
  69.9 5.2 %collective-permute-start.7 = (bf16[304,128]{1,0:T(8,128)(2,1)S(1)}, bf16[304,128]{1,0:T(8,128)(2,1)S(1)}, u32[]{:S(2)}, u32[]{:S(2)}) collective-permute-start(bf16[304,128]{1,0:T(8,128)(2,1)S(1)} %get-tuple-element.42), channel_id=1, source_target_pairs={{0,4},{4,0},{8,12},{12,8},{16,20},{20,16},{24,28},{28,24},{1,5},{5... | collective-permute-start | bytes 233480 | tf_op jit(solution)/shard_map/ppermute | solution.py:273
  70.0 6.8 %collective-permute-start.9 = (bf16[304,128]{1,0:T(8,128)(2,1)S(1)}, bf16[304,128]{1,0:T(8,128)(2,1)S(1)}, u32[]{:S(2)}, u32[]{:S(2)}) collective-permute-start(bf16[304,128]{1,0:T(8,128)(2,1)S(1)} %get-tuple-element.44), channel_id=1, source_target_pairs={{0,4},{4,0},{8,12},{12,8},{16,20},{20,16},{24,28},{28,24},{1,5},{5... | collective-permute-start | bytes 233480 | tf_op jit(solution)/shard_map/ppermute | solution.py:273
  72.0 6.5 %collective-permute-start.11 = (bf16[304,128]{1,0:T(8,128)(2,1)S(1)}, bf16[304,128]{1,0:T(8,128)(2,1)S(1)}, u32[]{:S(2)}, u32[]{:S(2)}) collective-permute-start(bf16[304,128]{1,0:T(8,128)(2,1)S(1)} %get-tuple-element.46), channel_id=1, source_target_pairs={{0,4},{4,0},{8,12},{12,8},{16,20},{20,16},{24,28},{28,24},{1,5},{5... | collective-permute-start | bytes 233480 | tf_op jit(solution)/shard_map/ppermute | solution.py:273
  72.1 7.7 %collective-permute-start.6 = (bf16[304,128]{1,0:T(8,128)(2,1)S(1)}, bf16[304,128]{1,0:T(8,128)(2,1)S(1)}, u32[]{:S(2)}, u32[]{:S(2)}) collective-permute-start(bf16[304,128]{1,0:T(8,128)(2,1)S(1)} %get-tuple-element.40), channel_id=1, source_target_pairs={{0,4},{4,0},{8,12},{12,8},{16,20},{20,16},{24,28},{28,24},{1,5},{5... | collective-permute-start | bytes 233480 | tf_op jit(solution)/shard_map/ppermute | solution.py:273
  75.2 4.6 %collective-permute-start.8 = (bf16[304,128]{1,0:T(8,128)(2,1)S(1)}, bf16[304,128]{1,0:T(8,128)(2,1)S(1)}, u32[]{:S(2)}, u32[]{:S(2)}) collective-permute-start(bf16[304,128]{1,0:T(8,128)(2,1)S(1)} %add_convert_fusion.3), channel_id=1, source_target_pairs={{0,8},{4,12},{8,0},{12,4},{16,24},{20,28},{24,16},{28,20},{1,9},{5... | collective-permute-start | bytes 233480 | tf_op jit(solution)/shard_map/ppermute | solution.py:273
  76.8 7.2 %collective-permute-start.10 = (bf16[304,128]{1,0:T(8,128)(2,1)S(1)}, bf16[304,128]{1,0:T(8,128)(2,1)S(1)}, u32[]{:S(2)}, u32[]{:S(2)}) collective-permute-start(bf16[304,128]{1,0:T(8,128)(2,1)S(1)} %add_convert_fusion.2), channel_id=1, source_target_pairs={{0,16},{4,20},{8,24},{12,28},{16,0},{20,4},{24,8},{28,12},{1,17},{... | collective-permute-start | bytes 233480 | tf_op jit(solution)/shard_map/ppermute | solution.py:273
  78.5 6.4 %collective-permute-start.12 = (bf16[304,128]{1,0:T(8,128)(2,1)S(1)}, bf16[304,128]{1,0:T(8,128)(2,1)S(1)}, u32[]{:S(2)}, u32[]{:S(2)}) collective-permute-start(bf16[304,128]{1,0:T(8,128)(2,1)S(1)} %add_convert_fusion.1), channel_id=1, source_target_pairs={{0,24},{4,28},{8,16},{12,20},{16,8},{20,12},{24,0},{28,4},{1,25},{... | collective-permute-start | bytes 233480 | tf_op jit(solution)/shard_map/ppermute | solution.py:273
  84.9 5.0 %collective-permute-start.13 = (bf16[304,128]{1,0:T(8,128)(2,1)S(1)}, bf16[304,128]{1,0:T(8,128)(2,1)S(1)}, u32[]{:S(2)}, u32[]{:S(2)}) collective-permute-start(bf16[304,128]{1,0:T(8,128)(2,1)S(1)} %add_convert_fusion.refs_0_), channel_id=1, source_target_pairs={{0,8},{4,12},{8,0},{12,4},{16,24},{20,28},{24,16},{28,20},{1,9},{5... | collective-permute-start | bytes 233480 | tf_op jit(solution)/shard_map/ppermute | solution.py:273
  86.3 7.2 %collective-permute-start.14 = (bf16[304,128]{1,0:T(8,128)(2,1)S(1)}, bf16[304,128]{1,0:T(8,128)(2,1)S(1)}, u32[]{:S(2)}, u32[]{:S(2)}) collective-permute-start(bf16[304,128]{1,0:T(8,128)(2,1)S(1)} %add_convert_fusion.refs_0_), channel_id=1, source_target_pairs={{0,16},{4,20},{8,24},{12,28},{16,0},{20,4},{24,8},{28,12},{1,17},{... | collective-permute-start | bytes 233480 | tf_op jit(solution)/shard_map/ppermute | solution.py:273
  86.8 7.1 %collective-permute-start.15 = (bf16[304,128]{1,0:T(8,128)(2,1)S(1)}, bf16[304,128]{1,0:T(8,128)(2,1)S(1)}, u32[]{:S(2)}, u32[]{:S(2)}) collective-permute-start(bf16[304,128]{1,0:T(8,128)(2,1)S(1)} %add_convert_fusion.refs_0_), channel_id=1, source_target_pairs={{0,24},{4,28},{8,16},{12,20},{16,8},{20,12},{24,0},{28,4},{1,25},{... | collective-permute-start | bytes 233480 | tf_op jit(solution)/shard_map/ppermute | solution.py:273
  89.5 6.8 %collective-permute-start.16 = (bf16[304,128]{1,0:T(8,128)(2,1)S(1)}, bf16[304,128]{1,0:T(8,128)(2,1)S(1)}, u32[]{:S(2)}, u32[]{:S(2)}) collective-permute-start(bf16[304,128]{1,0:T(8,128)(2,1)S(1)} %add_convert_fusion.refs_0_), channel_id=1, source_target_pairs={{0,4},{4,0},{8,12},{12,8},{16,20},{20,16},{24,28},{28,24},{1,5},{5... | collective-permute-start | bytes 233480 | tf_op jit(solution)/shard_map/ppermute | solution.py:273
  89.9 6.3 %collective-permute-start.17 = (bf16[304,128]{1,0:T(8,128)(2,1)S(1)}, bf16[304,128]{1,0:T(8,128)(2,1)S(1)}, u32[]{:S(2)}, u32[]{:S(2)}) collective-permute-start(bf16[304,128]{1,0:T(8,128)(2,1)S(1)} %collective-permute-done.13.refs_1_), channel_id=1, source_target_pairs={{0,4},{4,0},{8,12},{12,8},{16,20},{20,16},{24,28},{28,24},{1,5},{5... | collective-permute-start | bytes 233480 | tf_op jit(solution)/shard_map/ppermute | solution.py:273
  93.6 4.4 %collective-permute-start.18 = (bf16[304,128]{1,0:T(8,128)(2,1)S(1)}, bf16[304,128]{1,0:T(8,128)(2,1)S(1)}, u32[]{:S(2)}, u32[]{:S(2)}) collective-permute-start(bf16[304,128]{1,0:T(8,128)(2,1)S(1)} %collective-permute-done.14.refs_2_), channel_id=1, source_target_pairs={{0,4},{4,0},{8,12},{12,8},{16,20},{20,16},{24,28},{28,24},{1,5},{5... | collective-permute-start | bytes 233480 | tf_op jit(solution)/shard_map/ppermute | solution.py:273
  93.9 4.9 %collective-permute-start.19 = (bf16[304,128]{1,0:T(8,128)(2,1)S(1)}, bf16[304,128]{1,0:T(8,128)(2,1)S(1)}, u32[]{:S(2)}, u32[]{:S(2)}) collective-permute-start(bf16[304,128]{1,0:T(8,128)(2,1)S(1)} %collective-permute-done.15.refs_3_), channel_id=1, source_target_pairs={{0,4},{4,0},{8,12},{12,8},{16,20},{20,16},{24,28},{28,24},{1,5},{5... | collective-permute-start | bytes 233480 | tf_op jit(solution)/shard_map/ppermute | solution.py:273

commit v3 on v2

--- a/solution.py
+++ b/solution.py
@@ -73,27 +73,12 @@
             out_ref[slot] = jnp.where(slot < plan_ref[plan.sent + side], picked, 0.0)
 
 
-def first_kernel(plan, plan_ref, feat_ref, label_ref, left_ref, right_ref, b_ref):
-    blocks = [feat_ref[number] for number in range(feat_ref.shape[0])]
+def first_kernel(plan, plan_ref, feat_ref, left_ref, right_ref, held_ref, sem):
+    copy = pltpu.make_async_copy(feat_ref, held_ref, sem)
+    copy.start()
+    copy.wait()
+    blocks = [held_ref[number] for number in range(held_ref.shape[0])]
     write_sends(plan, plan_ref, blocks, left_ref, right_ref)
-    size = blocks[0].shape[0]
-    for number, block in enumerate(blocks):
-        b_ref[number * size : (number + 1) * size] = block.astype(BF16)
-    width = b_ref.shape[1]
-    nodes = label_ref.shape[1]
-    per_piece = nodes // width
-    place = lax.broadcasted_iota(jnp.int32, (16, width), 0)
-    packed = jnp.zeros((16, width), F32)
-    for piece in range(2):
-        value = label_ref[...] & 255 if piece == 0 else label_ref[...] >> 8
-        value = value.astype(F32)
-        for part in range(per_piece):
-            packed = jnp.where(
-                place == piece * per_piece + part,
-                value[:, part * width : (part + 1) * width],
-                packed,
-            )
-    b_ref[nodes:] = packed.astype(BF16)
 
 
 def next_blocks(plan, plan_ref, cur_ref, low_ref, high_ref, tiles_ref, ext_ref):
@@ -118,14 +103,12 @@
 
 def hop_kernel(
     plan, plan_ref, cur_ref, low_ref, high_ref, tiles_ref,
-    next_ref, left_ref, right_ref, b_ref, ext_ref,
+    next_ref, left_ref, right_ref, ext_ref,
 ):
     blocks = next_blocks(plan, plan_ref, cur_ref, low_ref, high_ref, tiles_ref, ext_ref)
     write_sends(plan, plan_ref, blocks, left_ref, right_ref)
     for number, block in enumerate(blocks):
-        size = block.shape[0]
         next_ref[number] = block
-        b_ref[number * size : (number + 1) * size] = block.astype(BF16)
 
 
 def branch_logits(branch, rows, w_ref, wc_ref):
@@ -137,9 +120,61 @@
 def forward_kernel(branch, cur_ref, w_ref, wc_ref, *refs):
     rows = cur_ref[...].reshape(-1, cur_ref.shape[2]).astype(BF16)
     part = branch_logits(branch, rows, w_ref, wc_ref)
-    if len(refs) == 2:
+    if len(refs) == 3:
         part = refs[0][...] + part
-    refs[-1][...] = part
+    refs[-2][...] = part
+    refs[-1][...] = rows
+
+
+def forward_first_kernel(cur_ref, w_ref, wc_ref, label_ref, tiles_ref, part_ref, b_ref):
+    nodes = label_ref.shape[1]
+    forward_kernel(0, cur_ref, w_ref, wc_ref, part_ref, b_ref.at[:nodes])
+    width = b_ref.shape[1]
+    per_piece = nodes // width
+    place = lax.broadcasted_iota(jnp.int32, (16, width), 0)
+    packed = jnp.zeros((16, width), F32)
+    for piece in range(2):
+        value = label_ref[...] & 255 if piece == 0 else label_ref[...] >> 8
+        value = value.astype(F32)
+        for part in range(per_piece):
+            packed = jnp.where(
+                place == piece * per_piece + part,
+                value[:, part * width : (part + 1) * width],
+                packed,
+            )
+    b_ref[nodes:] = packed.astype(BF16)
+
+
+def places(order_ref):
+    nodes = order_ref.shape[1]
+    rows = lax.broadcasted_iota(jnp.int32, (nodes, nodes), 0)
+    return (order_ref[...] == rows).astype(F32).astype(BF16)
+
+
+def label_kernel(order_ref, *refs):
+    nodes = order_ref.shape[1]
+    group = len(refs) - 1
+    share = nodes // group
+    mine = lax.axis_index("shuf")
+    width = refs[0].shape[1]
+    per_piece = nodes // width
+    ordered = [jnp.zeros((1, nodes), F32) for _ in range(2)]
+    for step in range(group):
+        tail = refs[step][nodes:]
+        away = ((mine ^ step) - mine) * share
+        for part in range(per_piece):
+            source = lax.broadcasted_iota(jnp.int32, (width, nodes), 0) + part * width
+            target = lax.broadcasted_iota(jnp.int32, (width, nodes), 1)
+            first = mine * share
+            wanted = (target == source + away) & (source >= first) & (source < first + share)
+            moved = matmul(tail, wanted.astype(F32).astype(BF16))
+            for piece in range(2):
+                row = piece * per_piece + part
+                ordered[piece] = ordered[piece] + moved[row : row + 1]
+    number = lax.broadcasted_iota(jnp.int32, (16, nodes), 0)
+    packed = jnp.where(number == 0, ordered[0], jnp.where(number == 1, ordered[1], 0.0))
+    pieces = matmul(packed.astype(BF16), places(order_ref), ((1,), (1,)))
+    refs[-1][...] = (pieces[0:1] + 256.0 * pieces[1:2]).astype(jnp.int32)
 
 
 def last_kernel(
@@ -156,11 +191,7 @@
     logits = before_ref[...] + branch_logits(w_ref.shape[0] - 1, rows_b, w_ref, wc_ref)
     classes, rows = logits.shape
     kept = up_to(classes, 16)
-    place = (order_ref[...] == lax.broadcasted_iota(jnp.int32, (rows, rows), 0)).astype(F32)
-    place = place.astype(BF16)
-    pieces = matmul(label_ref[...], place, ((1,), (1,)))
-    label = (pieces[0:1] + 256.0 * pieces[1:2]).astype(jnp.int32)
-    hit = lax.broadcasted_iota(jnp.int32, (classes, rows), 0) == label
+    hit = lax.broadcasted_iota(jnp.int32, (classes, rows), 0) == label_ref[...]
     top = jnp.max(logits, axis=0, keepdims=True)
     log_total = top + jnp.log(jnp.sum(jnp.exp(logits - top), axis=0, keepdims=True))
     loss = log_total - jnp.sum(jnp.where(hit, logits, 0.0), axis=0, keepdims=True)
@@ -174,7 +205,7 @@
         part = rest.astype(BF16).astype(F32)
         packed = jnp.where(number == piece, part, packed)
         rest = rest - part
-    out_ref[size + kept :] = matmul(packed.astype(BF16), place).astype(BF16)
+    out_ref[size + kept :] = matmul(packed.astype(BF16), places(order_ref)).astype(BF16)
 
 
 def weights_kernel(w_ref, wc_ref, wt_ref, wct_ref, pad_ref):
@@ -191,25 +222,25 @@
         wct_ref[branch] = pad_ref[...].T[:, :kept].astype(BF16)
 
 
-def all_chunks(kept, b0_ref, b1_ref, b2_ref, last_ref, w_ref, wt_ref, wct_ref, chunks_ref):
+def all_chunks(kept, row_refs, last_ref, w_ref, wt_ref, wct_ref, chunks_ref):
     group = last_ref.shape[0]
     branches, own, width = wt_ref.shape
-    nodes = b1_ref.shape[1]
+    nodes = row_refs[-1].shape[0]
     hid = w_ref.shape[2]
     parts = last_ref.shape[2] // width
     size = nodes // parts
+    mine = lax.axis_index("shuf")
     all_rows = []
-    for b_ref in (b0_ref, b1_ref, b2_ref):
-        all_rows.append(
-            jnp.concatenate([b_ref[member, :nodes] for member in range(group)], axis=0)
-        )
+    for branch in range(branches - 1):
+        ours = row_refs[branch * group : (branch + 1) * group]
+        all_rows.append(jnp.concatenate([ref[:nodes] for ref in ours], axis=0))
     last_rows = []
-    for member in range(group):
+    for step in range(group):
         for part in range(parts):
-            last_rows.append(last_ref[member, :size, part * width : (part + 1) * width])
+            last_rows.append(last_ref[mine ^ step, :size, part * width : (part + 1) * width])
     all_rows.append(jnp.concatenate(last_rows, axis=0))
     dlogits_t = jnp.concatenate(
-        [last_ref[member, size : size + kept] for member in range(group)], axis=1
+        [last_ref[mine ^ step, size : size + kept] for step in range(group)], axis=1
     )
     own_class = branches * own
     first = lax.axis_index("shuf") * own_class
@@ -233,15 +264,19 @@
             ]
 
 
-def grad_kernel(kept, *refs):
-    ins, outs, chunks_ref = refs[:7], refs[7:-1], refs[-1]
-    all_chunks(kept, *ins, chunks_ref)
+def grad_kernel(kept, row_count, half, *refs):
+    outs = refs[row_count + 4 : -1]
+    chunks_ref = refs[-1]
+    all_chunks(kept, refs[:row_count], *refs[row_count : row_count + 4], chunks_ref)
     dom = lax.axis_index("dom")
-    half = len(outs) // 2
     for step in range(half):
         stays = dom ^ (2 * step)
         outs[step][...] = chunks_ref[stays]
-        outs[half + step][...] = chunks_ref[stays ^ 1].astype(BF16)
+        outs[half + step // 2][step % 2] = chunks_ref[stays ^ 1].astype(BF16)
+
+
+def plain_grad_kernel(kept, row_count, *refs):
+    all_chunks(kept, refs[:row_count], *refs[row_count:])
 
 
 def write_chunk(kept, chunk, value, branch_ref, class_ref):
@@ -268,9 +303,24 @@
         write_chunk(kept, chunk, in_ref[chunk], branch_ref, class_ref)
 
 
-def swapped(value, distance):
-    pairs = [(source, source ^ distance) for source in range(lax.axis_size("dom"))]
-    return lax.ppermute(value, "dom", pairs)
+def swapped(value, distance, axis="dom"):
+    pairs = [(source, source ^ distance) for source in range(lax.axis_size(axis))]
+    return lax.ppermute(value, axis, pairs)
+
+
+def in_group(value):
+    members = [value]
+    distance = lax.axis_size("shuf") // 2
+    while distance:
+        members += [swapped(member, distance, "shuf") for member in members]
+        distance //= 2
+    count = len(members)
+    steps = [0]
+    distance = count // 2
+    while distance:
+        steps += [step + distance for step in steps]
+        distance //= 2
+    return [members[steps.index(step)] for step in range(count)]
 
 
 def body(
@@ -304,41 +354,48 @@
     w_class_t = w_class.T
 
     current = features.reshape(local, block, width)
-    to_left, to_right, rows = call(
+    to_left, to_right = call(
         functools.partial(first_kernel, plan),
-        [slots_f32, slots_f32, first_b16],
-        [IN_SMEM, IN_VMEM, IN_VMEM],
+        [slots_f32, slots_f32],
+        [IN_SMEM, pl.BlockSpec(memory_space=pl.ANY)],
         1000,
-    )(small, current, labels.reshape(1, nodes))
+        [pltpu.VMEM((local, block, width), F32), pltpu.SemaphoreType.DMA],
+    )(small, current)
     gathered = []
-    logits = []
+    logits = None
     hop_flops = 12 * tiles * block * block * width
     forward_flops = 2 * nodes * hid * (width + classes)
     ext = pltpu.VMEM((local + 2 * slots, block, width), F32)
     for hop in range(HOPS):
         from_lower = passed_along(to_right, "dom", 1)
         from_upper = passed_along(to_left, "dom", -1)
-        gathered.append(lax.all_gather(rows, "shuf"))
-        logits = [
-            call(
+        if hop == 0:
+            logits, rows = call(
+                forward_first_kernel, [logits_f32, first_b16], [IN_VMEM] * 5, forward_flops
+            )(current, w_branch, w_class_t, labels.reshape(1, nodes), tile_values)
+        else:
+            logits, rows = call(
                 functools.partial(forward_kernel, hop),
-                logits_f32,
-                [IN_VMEM] * (3 + len(logits)),
+                [logits_f32, rows_b16],
+                [IN_VMEM] * 4,
                 forward_flops,
-            )(current, w_branch, w_class_t, *logits)
-        ]
+            )(current, w_branch, w_class_t, logits)
+        gathered += in_group(rows)
         if hop < HOPS - 1:
-            current, to_left, to_right, rows = call(
+            current, to_left, to_right = call(
                 functools.partial(hop_kernel, plan),
-                [blocks_f32, slots_f32, slots_f32, rows_b16],
+                [blocks_f32, slots_f32, slots_f32],
                 [IN_SMEM] + [IN_VMEM] * 4,
                 hop_flops,
                 [ext],
             )(small, current, from_lower, from_upper, tile_values)
 
-    pieces = gathered[0][:, nodes : nodes + 2 * nodes // width].reshape(shuf, 2, shuf, share)
-    pieces = lax.dynamic_index_in_dim(pieces, mine, 2, keepdims=False)
-    label_mine = jnp.pad(pieces.transpose(1, 0, 2).reshape(2, nodes), ((0, 14), (0, 0)))
+    label_mine = call(
+        label_kernel,
+        jax.ShapeDtypeStruct((1, nodes), jnp.int32),
+        [IN_VMEM] * (1 + shuf),
+        1000,
+    )(batch_order, *gathered[:shuf])
 
     wt_own, wct_own = call(
         weights_kernel,
@@ -359,7 +416,7 @@
         [ext],
     )(
         small, current, from_lower, from_upper, tile_values,
-        *logits, w_branch, w_class_t, batch_order, label_mine,
+        logits, w_branch, w_class_t, batch_order, label_mine,
     )
     last_all = lax.all_gather(payload, "shuf")
     loss_parts = lax.dynamic_slice(
@@ -376,36 +433,42 @@
         jax.ShapeDtypeStruct((classes, own_class), F32),
     ]
     chunks_f32 = pltpu.VMEM((chunks, height, LANES), F32)
-    if chunks == dom and dom % 2 == 0 and dom & (dom - 1) == 0:
+    if chunks == dom and dom % 4 == 0 and dom & (dom - 1) == 0:
         half = dom // 2
         one_f32 = jax.ShapeDtypeStruct((height, LANES), F32)
-        one_b16 = jax.ShapeDtypeStruct((height, LANES), BF16)
+        two_b16 = jax.ShapeDtypeStruct((2, height, LANES), BF16)
         made = call(
-            functools.partial(grad_kernel, kept),
-            [one_f32] * half + [one_b16] * half,
-            [IN_VMEM] * 7,
+            functools.partial(grad_kernel, kept, len(gathered), half),
+            [one_f32] * half + [two_b16] * (half // 2),
+            [IN_VMEM] * len(grad_ins),
             grad_flops,
             [chunks_f32],
         )(*grad_ins)
-        order = list(range(1, half)) + [0]
-        arrived = {step: swapped(made[half + step], 1) for step in order}
-        total = {step: made[step] + arrived[step].astype(F32) for step in order}
-        far = [swapped(total[step].astype(BF16), 2 * step) for step in range(1, half)]
+        order = list(range(half - 1, -1, -1))
+        arrived = {pair: swapped(made[half + pair], 1) for pair in range(half // 2 - 1, -1, -1)}
+        total = {
+            step: made[step] + arrived[step // 2][step % 2].astype(F32) for step in order
+        }
+        far = [swapped(total[step].astype(BF16), 2 * step) for step in order[:-1]]
         summed = total[0]
         for value in far:
             summed = summed + value.astype(F32)
-        near = [summed.astype(BF16)]
+        near = {0: summed.astype(BF16)}
+        other = {0: swapped(near[0], 1)}
+        for step in order[:-1]:
+            near[step] = swapped(near[0], 2 * step)
         for step in range(1, half):
-            near.append(swapped(near[0], 2 * step))
-        other = [swapped(value, 1) for value in near]
+            other[step] = swapped(near[step], 1)
+        near = [near[step] for step in range(half)]
+        other = [other[step] for step in range(half)]
         grad_branch, grad_class_t = call(
             functools.partial(out_kernel, kept), outs, [IN_VMEM] * dom, 1000
         )(*near, *other)
     else:
         grads = call(
-            functools.partial(all_chunks, kept),
+            functools.partial(plain_grad_kernel, kept, len(gathered)),
             jax.ShapeDtypeStruct((chunks, height, LANES), F32),
-            [IN_VMEM] * 7,
+            [IN_VMEM] * len(grad_ins),
             grad_flops,
         )(*grad_ins)
         grad_branch, grad_class_t = call(

time: 100 us -> 83.3 us (0.83)
  blocking collectives: 25.6 us -> 7.66 us
  local copies, waits for them, and re-layouts: 12.2 us -> 5.45 us
  waiting for transfers between devices: 18.6 us -> 22.9 us
  starting transfers between devices: 29.7 us -> 33.7 us
    all_gather x3 -> x0, blocking collectives: 17.6 us -> none  [body(): gathered.append(lax.all_gather(rows, 'shuf'))]
    ppermute x14 -> x21, waiting for transfers between devices: 13.9 us -> 18.2 us  [swapped(): return lax.ppermute(value, axis, pairs)]
    ppermute x14 -> x21, starting transfers between devices: 14.1 us -> 18 us  [swapped(): return lax.ppermute(value, axis, pairs)]
    reshape x2 -> x0, local copies, waits for them, and re-layouts: 2.66 us -> none  [the longest x1 1.34 us: body(): gathered[0][:, nodes:nodes + 2 * nodes // width]]
    unnamed x35 -> x16, local copies, waits for them, and re-layouts: 5.53 us -> 4 us
    pallas_call x2, Pallas kernels: 3.53 us -> 2.4 us  [body(): call(functools.partial(hop_kernel, plan), [blocks_f32, slots_f32, slots_f...]
    pallas_call x5 -> x6, Pallas kernels: 5.15 us -> 5.72 us  [the longest x1 2.81 us: body(): call(functools.partial(grad_kernel, kept, len(gathered), half), [one_f32]...]
  transfers between devices with their start and end apart: 20 -> 27, of which waited for: 10 -> 12; matrix products, arithmetic and copies ran while one was open for 6% -> 1% of each run, Pallas kernels for 2% -> 7%
where the time goes in v3:
time: 83.3 us; the launch traced here: 83 us
  starting transfers between devices  33.7 us (40%)
  waiting for transfers between devices  22.9 us (27%)
  Pallas kernels  11.6 us (14%)
  blocking collectives  7.66 us (9%)
  local copies, waits for them, and re-layouts  5.45 us (7%)
  between operations  1.56 us (2%)
    ppermute x21, waiting for transfers between devices, swapped(): return lax.ppermute(value, axis, pairs)  18.2 us
    ppermute x21, starting transfers between devices, swapped(): return lax.ppermute(value, axis, pairs)  18 us
    ppermute x6, starting transfers between devices, passed_along(): return lax.ppermute(value, axis, pairs)  15.7 us
    all_gather x1, blocking collectives, body(): last_all = lax.all_gather(payload, 'shuf')  7.66 us
    ppermute x6, waiting for transfers between devices, passed_along(): return lax.ppermute(value, axis, pairs)  4.68 us
    unnamed x16, local copies, waits for them, and re-layouts  4 us
    pallas_call x1, Pallas kernels, body(): call(functools.partial(grad_kernel, kept, len(gathered), half), [one_f32]...  2.81 us
    pallas_call x2, Pallas kernels, body(): call(functools.partial(hop_kernel, plan), [blocks_f32, slots_f32, slots_f...  2.4 us
  transfers between devices with their start and end apart: 27, of which 12 were waited for; matrix products, arithmetic and copies ran while one was open for 1% of the time, Pallas kernels for 7%

profile of v3, /device:TPU:0, one launch (start us, length us, event | category | flops | bytes accessed | tf_op | source)
XLA Modules:
  0.0 83.0 jit_solution(9335307902163101352)
XLA Ops:
  1.4 0.8 concatenate.3.plan_ref
  2.2 0.9 %copy-done.5 = f32[256,128]{1,0:T(8,128)S(1)} copy-done((f32[256,128]{1,0:T(8,128)S(1)}, f32[256,128]{1,0:T(8,128)}, u32[]{:S(2)}) %copy-start.5) | copy-done | bytes 131096
  3.1 0.7 shard_map.139
  3.8 3.0 %collective-permute-start = (f32[2,128,128]{2,1,0:T(8,128)S(1)}, f32[2,128,128]{2,1,0:T(8,128)S(1)}, u32[]{:S(2)}, u32[]{:S(2)}) collective-permute-start(f32[2,128,128]{2,1,0:T(8,128)S(1)} %get-tuple-element.27), channel_id=1, source_target_pairs={{0,4},{4,8},{8,12},{12,16},{16,20},{20,24},{24,28},{28,0},{1,5},{5... | collective-permute-start | bytes 393224 | tf_op jit(solution)/shard_map/ppermute | solution.py:28
  6.9 3.1 %collective-permute-start.1 = (f32[2,128,128]{2,1,0:T(8,128)S(1)}, f32[2,128,128]{2,1,0:T(8,128)S(1)}, u32[]{:S(2)}, u32[]{:S(2)}) collective-permute-start(f32[2,128,128]{2,1,0:T(8,128)S(1)} %get-tuple-element.28), channel_id=1, source_target_pairs={{0,28},{4,0},{8,4},{12,8},{16,12},{20,16},{24,20},{28,24},{1,29},{... | collective-permute-start | bytes 393224 | tf_op jit(solution)/shard_map/ppermute | solution.py:28
  10.0 3.5 %collective-permute-done.low_ref = f32[2,128,128]{2,1,0:T(8,128)S(1)} collective-permute-done((f32[2,128,128]{2,1,0:T(8,128)S(1)}, f32[2,128,128]{2,1,0:T(8,128)S(1)}, u32[]{:S(2)}, u32[]{:S(2)}) %collective-permute-start) | collective-permute-done | bytes 131104 | tf_op jit(solution)/shard_map/ppermute | solution.py:28
  13.5 1.1 %collective-permute-done.1.high_ref = f32[2,128,128]{2,1,0:T(8,128)S(1)} collective-permute-done((f32[2,128,128]{2,1,0:T(8,128)S(1)}, f32[2,128,128]{2,1,0:T(8,128)S(1)}, u32[]{:S(2)}, u32[]{:S(2)}) %collective-permute-start.1) | collective-permute-done | bytes 131104 | tf_op jit(solution)/shard_map/ppermute | solution.py:28
  14.6 1.0 %copy-done.3 = f32[8,128,128]{2,1,0:T(8,128)S(1)} copy-done((f32[8,128,128]{2,1,0:T(8,128)S(1)}, f32[8,128,128]{2,1,0:T(8,128)}, u32[]{:S(2)}) %copy-start.3) | copy-done | bytes 524312
  15.7 1.2 %shard_map.140 = (f32[2,128,128]{2,1,0:T(8,128)S(1)}, f32[2,128,128]{2,1,0:T(8,128)S(1)}, f32[2,128,128]{2,1,0:T(8,128)S(1)}) custom-call(s32[23]{0:T(128)S(1)} %concatenate.3.plan_ref, f32[2,128,128]{2,1,0:T(8,128)S(1)} %bitcast.32, f32[2,128,128]{2,1,0:T(8,128)S(1)} %collective-permute-done.low_ref, f32[2,128,128]{2,1,0:T(8,128)S(1)} %collective-permute-done.1.high_ref, ...), custom_call_target="tpu_custom_call" | custom-call | flops 201326592 | bytes 1179648 | tf_op jit(solution)/shard_map/pallas_call | solution.py:385
  16.9 0.3 collective-permute-start.2
  17.2 4.4 %collective-permute-start.3 = (f32[2,128,128]{2,1,0:T(8,128)S(1)}, f32[2,128,128]{2,1,0:T(8,128)S(1)}, u32[]{:S(2)}, u32[]{:S(2)}) collective-permute-start(f32[2,128,128]{2,1,0:T(8,128)S(1)} %get-tuple-element.31), channel_id=1, source_target_pairs={{0,28},{4,0},{8,4},{12,8},{16,12},{20,16},{24,20},{28,24},{1,29},{... | collective-permute-start | bytes 393224 | tf_op jit(solution)/shard_map/ppermute | solution.py:28
  21.7 1.4 %copy-done = bf16[4096,172]{0,1:T(8,128)(2,1)S(1)} copy-done((bf16[4096,172]{0,1:T(8,128)(2,1)S(1)}, bf16[4096,172]{0,1:T(8,128)(2,1)}, u32[]{:S(2)}) %copy-start) | copy-done | bytes 1409048
  23.0 0.7 copy-done.7
  23.7 0.6 shard_map.142
  24.3 1.6 %collective-permute-start.7 = (bf16[272,128]{1,0:T(8,128)(2,1)S(1)}, bf16[272,128]{1,0:T(8,128)(2,1)S(1)}, u32[]{:S(2)}, u32[]{:S(2)}) collective-permute-start(bf16[272,128]{1,0:T(8,128)(2,1)S(1)} %get-tuple-element.38.refs_0_), channel_id=1, source_target_pairs={{0,2},{1,3},{2,0},{3,1},{4,6},{5,7},{6,4},{7,5},{8,10},{9,11},{10,... | collective-permute-start | bytes 208904 | tf_op jit(solution)/shard_map/ppermute | solution.py:308
  25.9 0.0 collective-permute-done.3.high_ref
  25.9 1.2 %shard_map.141 = (f32[2,128,128]{2,1,0:T(8,128)S(1)}, f32[2,128,128]{2,1,0:T(8,128)S(1)}, f32[2,128,128]{2,1,0:T(8,128)S(1)}) custom-call(s32[23]{0:T(128)S(1)} %concatenate.3.plan_ref, f32[2,128,128]{2,1,0:T(8,128)S(1)} %get-tuple-element.29.cur_ref, f32[2,128,128]{2,1,0:T(8,128)S(1)} %collective-permute-done.2.low_ref, ...), custom_call_target="tpu_custom_call" | custom-call | flops 201326592 | bytes 1179648 | tf_op jit(solution)/shard_map/pallas_call | solution.py:385
  27.1 0.1 collective-permute-start.4
  27.2 4.7 %collective-permute-start.5 = (f32[2,128,128]{2,1,0:T(8,128)S(1)}, f32[2,128,128]{2,1,0:T(8,128)S(1)}, u32[]{:S(2)}, u32[]{:S(2)}) collective-permute-start(f32[2,128,128]{2,1,0:T(8,128)S(1)} %get-tuple-element.34), channel_id=1, source_target_pairs={{0,28},{4,0},{8,4},{12,8},{16,12},{20,16},{24,20},{28,24},{1,29},{... | collective-permute-start | bytes 393224 | tf_op jit(solution)/shard_map/ppermute | solution.py:28
  31.9 0.0 collective-permute-done.7.refs_2_
  31.9 0.6 shard_map.143
  32.5 1.4 %collective-permute-start.10 = (bf16[256,128]{1,0:T(8,128)(2,1)S(1)}, bf16[256,128]{1,0:T(8,128)(2,1)S(1)}, u32[]{:S(2)}, u32[]{:S(2)}) collective-permute-start(bf16[256,128]{1,0:T(8,128)(2,1)S(1)} %get-tuple-element.39.refs_4_), channel_id=1, source_target_pairs={{0,2},{1,3},{2,0},{3,1},{4,6},{5,7},{6,4},{7,5},{8,10},{9,11},{10,... | collective-permute-start | bytes 196616 | tf_op jit(solution)/shard_map/ppermute | solution.py:308
  33.9 0.6 shard_map.144
  34.5 0.0 copy-start.6
  34.5 0.0 collective-permute-done.6.refs_1_
  34.5 0.8 collective-permute-start.13
  35.3 0.3 shard_map.147
  35.6 0.0 collective-permute-done.8.refs_3_
  35.6 0.1 collective-permute-start.9
  35.7 0.4 shard_map.145.label_ref
  36.0 1.0 %collective-permute-done.10.refs_6_ = bf16[256,128]{1,0:T(8,128)(2,1)S(1)} collective-permute-done((bf16[256,128]{1,0:T(8,128)(2,1)S(1)}, bf16[256,128]{1,0:T(8,128)(2,1)S(1)}, u32[]{:S(2)}, u32[]{:S(2)}) %collective-permute-start.10) | collective-permute-done | bytes 65568 | tf_op jit(solution)/shard_map/ppermute | solution.py:308
  37.1 0.0 collective-permute-start.11
  37.1 1.8 %collective-permute-done.13.refs_10_ = bf16[256,128]{1,0:T(8,128)(2,1)S(1)} collective-permute-done((bf16[256,128]{1,0:T(8,128)(2,1)S(1)}, bf16[256,128]{1,0:T(8,128)(2,1)S(1)}, u32[]{:S(2)}, u32[]{:S(2)}) %collective-permute-start.13) | collective-permute-done | bytes 65568 | tf_op jit(solution)/shard_map/ppermute | solution.py:308
  38.8 0.5 collective-permute-start.14
  39.3 2.0 %shard_map.146 = bf16[320,256]{1,0:T(8,128)(2,1)S(1)} custom-call(s32[23]{0:T(128)S(1)} %concatenate.3.plan_ref, f32[2,128,128]{2,1,0:T(8,128)S(1)} %get-tuple-element.32.cur_ref, f32[2,128,128]{2,1,0:T(8,128)S(1)} %collective-permute-done.4.low_ref, f32[2,128,128]{2,1,0:T(8,128)S(1)} %collective-permute-done.5.high_ref, f32[8,128,128]{2,1,0:T(8,128)S(1)} %copy-done.4, ...), custom_call_target="tpu_custom_call" | custom-call | flops 358612992 | bytes 491520 | tf_op jit(solution)/shard_map/pallas_call | solution.py:411
  41.3 7.7 %all-gather = bf16[1280,256]{1,0:T(8,128)(2,1)S(1)} all-gather(bf16[320,256]{1,0:T(8,128)(2,1)S(1)} %shard_map.146), channel_id=2, replica_groups=mesh['dom'=8,'shuf'=4] {'shuf'}, dimensions={0}, use_global_device_ids=true | all-gather | bytes 819200 | tf_op jit(solution)/shard_map/all_gather | solution.py:421
  49.0 0.0 collective-permute-done.9.refs_5_
  49.0 0.0 collective-permute-done.11.refs_7_
  49.0 0.0 collective-permute-done.14.refs_11_
  49.0 2.8 %shard_map.148 = (f32[304,128]{1,0:T(8,128)S(1)}, f32[304,128]{1,0:T(8,128)S(1)}, f32[304,128]{1,0:T(8,128)S(1)}, f32[304,128]{1,0:T(8,128)S(1)}, bf16[2,304,128...) custom-call(bf16[272,128]{1,0:T(8,128)(2,1)S(1)} %get-tuple-element.38.refs_0_, ...), custom_call_target="tpu_custom_call" | custom-call | flops 1543503872 | bytes 2801664 | tf_op jit(solution)/shard_map/pallas_call | solution.py:440
  51.8 0.1 collective-permute-start.16
  51.9 2.0 %collective-permute-start.15 = (bf16[2,304,128]{2,1,0:T(8,128)(2,1)S(1)}, bf16[2,304,128]{2,1,0:T(8,128)(2,1)S(1)}, u32[]{:S(2)}, u32[]{:S(2)}) collective-permute-start(bf16[2,304,128]{2,1,0:T(8,128)(2,1)S(1)} %get-tuple-element.44), channel_id=1, source_target_pairs={{0,4},{4,0},{8,12},{12,8},{16,20},{20,16},{24,28},{28,24},{1,5},{5... | collective-permute-start | bytes 466952 | tf_op jit(solution)/shard_map/ppermute | solution.py:308
  53.9 4.8 %collective-permute-done.16 = bf16[2,304,128]{2,1,0:T(8,128)(2,1)S(1)} collective-permute-done((bf16[2,304,128]{2,1,0:T(8,128)(2,1)S(1)}, bf16[2,304,128]{2,1,0:T(8,128)(2,1)S(1)}, u32[]{:S(2)}, u32[]{:S(2)}) %collective-permute-start.16) | collective-permute-done | bytes 155680 | tf_op jit(solution)/shard_map/ppermute | solution.py:308
  58.8 1.0 %collective-permute-start.17 = (bf16[304,128]{1,0:T(8,128)(2,1)S(1)}, bf16[304,128]{1,0:T(8,128)(2,1)S(1)}, u32[]{:S(2)}, u32[]{:S(2)}) collective-permute-start(bf16[304,128]{1,0:T(8,128)(2,1)S(1)} %get-tuple-element.51), channel_id=1, source_target_pairs={{0,24},{4,28},{8,16},{12,20},{16,8},{20,12},{24,0},{28,4},{1,25},{... | collective-permute-start | bytes 233480 | tf_op jit(solution)/shard_map/ppermute | solution.py:308
  59.8 0.3 collective-permute-start.18
  60.1 1.4 %collective-permute-done.15 = bf16[2,304,128]{2,1,0:T(8,128)(2,1)S(1)} collective-permute-done((bf16[2,304,128]{2,1,0:T(8,128)(2,1)S(1)}, bf16[2,304,128]{2,1,0:T(8,128)(2,1)S(1)}, u32[]{:S(2)}, u32[]{:S(2)}) %collective-permute-start.15) | collective-permute-done | bytes 155680 | tf_op jit(solution)/shard_map/ppermute | solution.py:308
  61.5 1.8 %collective-permute-start.19 = (bf16[304,128]{1,0:T(8,128)(2,1)S(1)}, bf16[304,128]{1,0:T(8,128)(2,1)S(1)}, u32[]{:S(2)}, u32[]{:S(2)}) collective-permute-start(bf16[304,128]{1,0:T(8,128)(2,1)S(1)} %fusion), channel_id=1, source_target_pairs={{0,8},{4,12},{8,0},{12,4},{16,24},{20,28},{24,16},{28,20},{1,9},{5... | collective-permute-start | bytes 233480 | tf_op jit(solution)/shard_map/ppermute | solution.py:308
  63.3 2.4 %collective-permute-done.17 = bf16[304,128]{1,0:T(8,128)(2,1)S(1)} collective-permute-done((bf16[304,128]{1,0:T(8,128)(2,1)S(1)}, bf16[304,128]{1,0:T(8,128)(2,1)S(1)}, u32[]{:S(2)}, u32[]{:S(2)}) %collective-permute-start.17) | collective-permute-done | bytes 77856 | tf_op jit(solution)/shard_map/ppermute | solution.py:308
  65.7 1.9 %collective-permute-done.18 = bf16[304,128]{1,0:T(8,128)(2,1)S(1)} collective-permute-done((bf16[304,128]{1,0:T(8,128)(2,1)S(1)}, bf16[304,128]{1,0:T(8,128)(2,1)S(1)}, u32[]{:S(2)}, u32[]{:S(2)}) %collective-permute-start.18) | collective-permute-done | bytes 77856 | tf_op jit(solution)/shard_map/ppermute | solution.py:308
  67.6 0.1 collective-permute-done.19
  67.7 0.1 fusion.6.refs_0_
  67.8 0.1 collective-permute-start.20
  67.8 1.9 %collective-permute-start.21 = (bf16[304,128]{1,0:T(8,128)(2,1)S(1)}, bf16[304,128]{1,0:T(8,128)(2,1)S(1)}, u32[]{:S(2)}, u32[]{:S(2)}) collective-permute-start(bf16[304,128]{1,0:T(8,128)(2,1)S(1)} %fusion.6.refs_0_), channel_id=1, source_target_pairs={{0,16},{4,20},{8,24},{12,28},{16,0},{20,4},{24,8},{28,12},{1,17},{... | collective-permute-start | bytes 233480 | tf_op jit(solution)/shard_map/ppermute | solution.py:308
  69.7 2.5 %collective-permute-start.22 = (bf16[304,128]{1,0:T(8,128)(2,1)S(1)}, bf16[304,128]{1,0:T(8,128)(2,1)S(1)}, u32[]{:S(2)}, u32[]{:S(2)}) collective-permute-start(bf16[304,128]{1,0:T(8,128)(2,1)S(1)} %fusion.6.refs_0_), channel_id=1, source_target_pairs={{0,24},{4,28},{8,16},{12,20},{16,8},{20,12},{24,0},{28,4},{1,25},{... | collective-permute-start | bytes 233480 | tf_op jit(solution)/shard_map/ppermute | solution.py:308
  72.2 0.1 dynamic-slice_convert_fusion
  72.3 0.5 collective-permute-start.23
  72.8 1.6 %collective-permute-start.24 = (bf16[304,128]{1,0:T(8,128)(2,1)S(1)}, bf16[304,128]{1,0:T(8,128)(2,1)S(1)}, u32[]{:S(2)}, u32[]{:S(2)}) collective-permute-start(bf16[304,128]{1,0:T(8,128)(2,1)S(1)} %collective-permute-done.20.refs_1_), channel_id=1, source_target_pairs={{0,4},{4,0},{8,12},{12,8},{16,20},{20,16},{24,28},{28,24},{1,5},{5... | collective-permute-start | bytes 233480 | tf_op jit(solution)/shard_map/ppermute | solution.py:308
  74.3 2.3 %collective-permute-done.21.refs_2_ = bf16[304,128]{1,0:T(8,128)(2,1)S(1)} collective-permute-done((bf16[304,128]{1,0:T(8,128)(2,1)S(1)}, bf16[304,128]{1,0:T(8,128)(2,1)S(1)}, u32[]{:S(2)}, u32[]{:S(2)}) %collective-permute-start.21) | collective-permute-done | bytes 77856 | tf_op jit(solution)/shard_map/ppermute | solution.py:308
  76.6 0.8 %collective-permute-start.25 = (bf16[304,128]{1,0:T(8,128)(2,1)S(1)}, bf16[304,128]{1,0:T(8,128)(2,1)S(1)}, u32[]{:S(2)}, u32[]{:S(2)}) collective-permute-start(bf16[304,128]{1,0:T(8,128)(2,1)S(1)} %collective-permute-done.21.refs_2_), channel_id=1, source_target_pairs={{0,4},{4,0},{8,12},{12,8},{16,20},{20,16},{24,28},{28,24},{1,5},{5... | collective-permute-start | bytes 233480 | tf_op jit(solution)/shard_map/ppermute | solution.py:308
  77.4 1.2 %collective-permute-start.26 = (bf16[304,128]{1,0:T(8,128)(2,1)S(1)}, bf16[304,128]{1,0:T(8,128)(2,1)S(1)}, u32[]{:S(2)}, u32[]{:S(2)}) collective-permute-start(bf16[304,128]{1,0:T(8,128)(2,1)S(1)} %collective-permute-done.22.refs_3_), channel_id=1, source_target_pairs={{0,4},{4,0},{8,12},{12,8},{16,20},{20,16},{24,28},{28,24},{1,5},{5... | collective-permute-start | bytes 233480 | tf_op jit(solution)/shard_map/ppermute | solution.py:308
  78.6 0.6 add.39
  79.3 1.7 %collective-permute-done.25.refs_6_ = bf16[304,128]{1,0:T(8,128)(2,1)S(1)} collective-permute-done((bf16[304,128]{1,0:T(8,128)(2,1)S(1)}, bf16[304,128]{1,0:T(8,128)(2,1)S(1)}, u32[]{:S(2)}, u32[]{:S(2)}) %collective-permute-start.25) | collective-permute-done | bytes 77856 | tf_op jit(solution)/shard_map/ppermute | solution.py:308
  81.0 0.8 %collective-permute-done.26.refs_7_ = bf16[304,128]{1,0:T(8,128)(2,1)S(1)} collective-permute-done((bf16[304,128]{1,0:T(8,128)(2,1)S(1)}, bf16[304,128]{1,0:T(8,128)(2,1)S(1)}, u32[]{:S(2)}, u32[]{:S(2)}) %collective-permute-start.26) | collective-permute-done | bytes 77856 | tf_op jit(solution)/shard_map/ppermute | solution.py:308
  81.8 1.2 %shard_map.149 = (f32[4,128,256]{2,1,0:T(8,128)}, f32[172,1024]{1,0:T(8,128)}) custom-call(bf16[304,128]{1,0:T(8,128)(2,1)S(1)} %fusion.6.refs_0_, bf16[304,128]{1,0:T(8,128)(2,1)S(1)} %collective-permute-done.20.refs_1_, bf16[304,128]{1,0:T(8,128)(2,1)S(1)} %collective-permute-done.21.refs_2_, bf16[304,128]{1,0:T(8,128)(2,1)S(1)} %collective-permute-done.22.refs_3_, ...), custom_call_target="tpu_custom_call" | custom-call | flops 1000 | bytes 3686400 | tf_op jit(solution)/shard_map/pallas_call | solution.py:464
  (25 shorter events, 0.1 us)
Async XLA Ops:
  0.6 21.0 %copy-start.2 = (bf16[4,128,1024]{2,1,0:T(8,128)(2,1)S(1)}, bf16[4,128,1024]{2,1,0:T(8,128)(2,1)}, u32[]{:S(2)}) copy-start(bf16[4,128,1024]{2,1,0:T(8,128)(2,1)} %refs_13_.1) | copy-start | bytes 3145732
  2.2 0.9 %copy-start.5 = (f32[256,128]{1,0:T(8,128)S(1)}, f32[256,128]{1,0:T(8,128)}, u32[]{:S(2)}) copy-start(f32[256,128]{1,0:T(8,128)} %param.12) | copy-start | bytes 393220
  3.8 9.7 %collective-permute-start = (f32[2,128,128]{2,1,0:T(8,128)S(1)}, f32[2,128,128]{2,1,0:T(8,128)S(1)}, u32[]{:S(2)}, u32[]{:S(2)}) collective-permute-start(f32[2,128,128]{2,1,0:T(8,128)S(1)} %get-tuple-element.27), channel_id=1, source_target_pairs={{0,4},{4,8},{8,12},{12,16},{16,20},{20,24},{24,28},{28,0},{1,5},{5... | collective-permute-start | bytes 393224 | tf_op jit(solution)/shard_map/ppermute | solution.py:28
  6.9 7.8 %collective-permute-start.1 = (f32[2,128,128]{2,1,0:T(8,128)S(1)}, f32[2,128,128]{2,1,0:T(8,128)S(1)}, u32[]{:S(2)}, u32[]{:S(2)}) collective-permute-start(f32[2,128,128]{2,1,0:T(8,128)S(1)} %get-tuple-element.28), channel_id=1, source_target_pairs={{0,28},{4,0},{8,4},{12,8},{16,12},{20,16},{24,20},{28,24},{1,29},{... | collective-permute-start | bytes 393224 | tf_op jit(solution)/shard_map/ppermute | solution.py:28
  14.6 1.0 %copy-start.3 = (f32[8,128,128]{2,1,0:T(8,128)S(1)}, f32[8,128,128]{2,1,0:T(8,128)}, u32[]{:S(2)}) copy-start(f32[8,128,128]{2,1,0:T(8,128)} %tiles_ref.7) | copy-start | bytes 1572868
  16.9 9.0 %collective-permute-start.2 = (f32[2,128,128]{2,1,0:T(8,128)S(1)}, f32[2,128,128]{2,1,0:T(8,128)S(1)}, u32[]{:S(2)}, u32[]{:S(2)}) collective-permute-start(f32[2,128,128]{2,1,0:T(8,128)S(1)} %get-tuple-element.30), channel_id=1, source_target_pairs={{0,4},{4,8},{8,12},{12,16},{16,20},{20,24},{24,28},{28,0},{1,5},{5... | collective-permute-start | bytes 393224 | tf_op jit(solution)/shard_map/ppermute | solution.py:28
  17.2 8.7 %collective-permute-start.3 = (f32[2,128,128]{2,1,0:T(8,128)S(1)}, f32[2,128,128]{2,1,0:T(8,128)S(1)}, u32[]{:S(2)}, u32[]{:S(2)}) collective-permute-start(f32[2,128,128]{2,1,0:T(8,128)S(1)} %get-tuple-element.31), channel_id=1, source_target_pairs={{0,28},{4,0},{8,4},{12,8},{16,12},{20,16},{24,20},{28,24},{1,29},{... | collective-permute-start | bytes 393224 | tf_op jit(solution)/shard_map/ppermute | solution.py:28
  21.7 1.4 %copy-start = (bf16[4096,172]{0,1:T(8,128)(2,1)S(1)}, bf16[4096,172]{0,1:T(8,128)(2,1)}, u32[]{:S(2)}) copy-start(bf16[4096,172]{0,1:T(8,128)(2,1)} %param.23) | copy-start | bytes 4227076
  23.0 0.7 copy-start.7
  23.7 2.2 %copy-start.4 = (f32[8,128,128]{2,1,0:T(8,128)S(1)}, f32[8,128,128]{2,1,0:T(8,128)}, u32[]{:S(2)}) copy-start(f32[8,128,128]{2,1,0:T(8,128)} %tiles_ref.7) | copy-start | bytes 1572868
  23.7 8.2 %copy-start.1 = (bf16[4096,172]{0,1:T(8,128)(2,1)S(1)}, bf16[4096,172]{0,1:T(8,128)(2,1)}, u32[]{:S(2)}) copy-start(bf16[4096,172]{0,1:T(8,128)(2,1)} %param.23) | copy-start | bytes 4227076
  24.3 7.6 %collective-permute-start.7 = (bf16[272,128]{1,0:T(8,128)(2,1)S(1)}, bf16[272,128]{1,0:T(8,128)(2,1)S(1)}, u32[]{:S(2)}, u32[]{:S(2)}) collective-permute-start(bf16[272,128]{1,0:T(8,128)(2,1)S(1)} %get-tuple-element.38.refs_0_), channel_id=1, source_target_pairs={{0,2},{1,3},{2,0},{3,1},{4,6},{5,7},{6,4},{7,5},{8,10},{9,11},{10,... | collective-permute-start | bytes 208904 | tf_op jit(solution)/shard_map/ppermute | solution.py:308
  25.9 8.6 %collective-permute-start.6 = (bf16[272,128]{1,0:T(8,128)(2,1)S(1)}, bf16[272,128]{1,0:T(8,128)(2,1)S(1)}, u32[]{:S(2)}, u32[]{:S(2)}) collective-permute-start(bf16[272,128]{1,0:T(8,128)(2,1)S(1)} %get-tuple-element.38.refs_0_), channel_id=1, source_target_pairs={{0,1},{1,0},{2,3},{3,2},{4,5},{5,4},{6,7},{7,6},{8,9},{9,8},{10,11... | collective-permute-start | bytes 208904 | tf_op jit(solution)/shard_map/ppermute | solution.py:308
  27.1 11.7 %collective-permute-start.4 = (f32[2,128,128]{2,1,0:T(8,128)S(1)}, f32[2,128,128]{2,1,0:T(8,128)S(1)}, u32[]{:S(2)}, u32[]{:S(2)}) collective-permute-start(f32[2,128,128]{2,1,0:T(8,128)S(1)} %get-tuple-element.33), channel_id=1, source_target_pairs={{0,4},{4,8},{8,12},{12,16},{16,20},{20,24},{24,28},{28,0},{1,5},{5... | collective-permute-start | bytes 393224 | tf_op jit(solution)/shard_map/ppermute | solution.py:28
  27.2 12.2 %collective-permute-start.5 = (f32[2,128,128]{2,1,0:T(8,128)S(1)}, f32[2,128,128]{2,1,0:T(8,128)S(1)}, u32[]{:S(2)}, u32[]{:S(2)}) collective-permute-start(f32[2,128,128]{2,1,0:T(8,128)S(1)} %get-tuple-element.34), channel_id=1, source_target_pairs={{0,28},{4,0},{8,4},{12,8},{16,12},{20,16},{24,20},{28,24},{1,29},{... | collective-permute-start | bytes 393224 | tf_op jit(solution)/shard_map/ppermute | solution.py:28
  31.9 3.7 %collective-permute-start.8 = (bf16[272,128]{1,0:T(8,128)(2,1)S(1)}, bf16[272,128]{1,0:T(8,128)(2,1)S(1)}, u32[]{:S(2)}, u32[]{:S(2)}) collective-permute-start(bf16[272,128]{1,0:T(8,128)(2,1)S(1)} %collective-permute-done.7.refs_2_), channel_id=1, source_target_pairs={{0,1},{1,0},{2,3},{3,2},{4,5},{5,4},{6,7},{7,6},{8,9},{9,8},{10,11... | collective-permute-start | bytes 208904 | tf_op jit(solution)/shard_map/ppermute | solution.py:308
  32.5 4.6 %collective-permute-start.10 = (bf16[256,128]{1,0:T(8,128)(2,1)S(1)}, bf16[256,128]{1,0:T(8,128)(2,1)S(1)}, u32[]{:S(2)}, u32[]{:S(2)}) collective-permute-start(bf16[256,128]{1,0:T(8,128)(2,1)S(1)} %get-tuple-element.39.refs_4_), channel_id=1, source_target_pairs={{0,2},{1,3},{2,0},{3,1},{4,6},{5,7},{6,4},{7,5},{8,10},{9,11},{10,... | collective-permute-start | bytes 196616 | tf_op jit(solution)/shard_map/ppermute | solution.py:308
  34.5 1.2 %copy-start.6 = (s32[1,256]{1,0:T(1,128)S(1)}, s32[1,256]{1,0:T(1,128)}, u32[]{:S(2)}) copy-start(s32[1,256]{1,0:T(1,128)} %order_ref.3) | copy-start | bytes 3076
  34.5 4.3 %collective-permute-start.13 = (bf16[256,128]{1,0:T(8,128)(2,1)S(1)}, bf16[256,128]{1,0:T(8,128)(2,1)S(1)}, u32[]{:S(2)}, u32[]{:S(2)}) collective-permute-start(bf16[256,128]{1,0:T(8,128)(2,1)S(1)} %get-tuple-element.40.refs_8_), channel_id=1, source_target_pairs={{0,2},{1,3},{2,0},{3,1},{4,6},{5,7},{6,4},{7,5},{8,10},{9,11},{10,... | collective-permute-start | bytes 196616 | tf_op jit(solution)/shard_map/ppermute | solution.py:308
  35.6 13.4 %collective-permute-start.9 = (bf16[256,128]{1,0:T(8,128)(2,1)S(1)}, bf16[256,128]{1,0:T(8,128)(2,1)S(1)}, u32[]{:S(2)}, u32[]{:S(2)}) collective-permute-start(bf16[256,128]{1,0:T(8,128)(2,1)S(1)} %get-tuple-element.39.refs_4_), channel_id=1, source_target_pairs={{0,1},{1,0},{2,3},{3,2},{4,5},{5,4},{6,7},{7,6},{8,9},{9,8},{10,11... | collective-permute-start | bytes 196616 | tf_op jit(solution)/shard_map/ppermute | solution.py:308
  37.1 11.9 %collective-permute-start.11 = (bf16[256,128]{1,0:T(8,128)(2,1)S(1)}, bf16[256,128]{1,0:T(8,128)(2,1)S(1)}, u32[]{:S(2)}, u32[]{:S(2)}) collective-permute-start(bf16[256,128]{1,0:T(8,128)(2,1)S(1)} %collective-permute-done.10.refs_6_), channel_id=1, source_target_pairs={{0,1},{1,0},{2,3},{3,2},{4,5},{5,4},{6,7},{7,6},{8,9},{9,8},{10,11... | collective-permute-start | bytes 196616 | tf_op jit(solution)/shard_map/ppermute | solution.py:308
  38.8 10.2 %collective-permute-start.12 = (bf16[256,128]{1,0:T(8,128)(2,1)S(1)}, bf16[256,128]{1,0:T(8,128)(2,1)S(1)}, u32[]{:S(2)}, u32[]{:S(2)}) collective-permute-start(bf16[256,128]{1,0:T(8,128)(2,1)S(1)} %get-tuple-element.40.refs_8_), channel_id=1, source_target_pairs={{0,1},{1,0},{2,3},{3,2},{4,5},{5,4},{6,7},{7,6},{8,9},{9,8},{10,11... | collective-permute-start | bytes 196616 | tf_op jit(solution)/shard_map/ppermute | solution.py:308
  38.8 10.2 %collective-permute-start.14 = (bf16[256,128]{1,0:T(8,128)(2,1)S(1)}, bf16[256,128]{1,0:T(8,128)(2,1)S(1)}, u32[]{:S(2)}, u32[]{:S(2)}) collective-permute-start(bf16[256,128]{1,0:T(8,128)(2,1)S(1)} %collective-permute-done.13.refs_10_), channel_id=1, source_target_pairs={{0,1},{1,0},{2,3},{3,2},{4,5},{5,4},{6,7},{7,6},{8,9},{9,8},{10,11... | collective-permute-start | bytes 196616 | tf_op jit(solution)/shard_map/ppermute | solution.py:308
  51.8 6.9 %collective-permute-start.16 = (bf16[2,304,128]{2,1,0:T(8,128)(2,1)S(1)}, bf16[2,304,128]{2,1,0:T(8,128)(2,1)S(1)}, u32[]{:S(2)}, u32[]{:S(2)}) collective-permute-start(bf16[2,304,128]{2,1,0:T(8,128)(2,1)S(1)} %get-tuple-element.46), channel_id=1, source_target_pairs={{0,4},{4,0},{8,12},{12,8},{16,20},{20,16},{24,28},{28,24},{1,5},{5... | collective-permute-start | bytes 466952 | tf_op jit(solution)/shard_map/ppermute | solution.py:308
  51.9 9.6 %collective-permute-start.15 = (bf16[2,304,128]{2,1,0:T(8,128)(2,1)S(1)}, bf16[2,304,128]{2,1,0:T(8,128)(2,1)S(1)}, u32[]{:S(2)}, u32[]{:S(2)}) collective-permute-start(bf16[2,304,128]{2,1,0:T(8,128)(2,1)S(1)} %get-tuple-element.44), channel_id=1, source_target_pairs={{0,4},{4,0},{8,12},{12,8},{16,20},{20,16},{24,28},{28,24},{1,5},{5... | collective-permute-start | bytes 466952 | tf_op jit(solution)/shard_map/ppermute | solution.py:308
  58.8 6.9 %collective-permute-start.17 = (bf16[304,128]{1,0:T(8,128)(2,1)S(1)}, bf16[304,128]{1,0:T(8,128)(2,1)S(1)}, u32[]{:S(2)}, u32[]{:S(2)}) collective-permute-start(bf16[304,128]{1,0:T(8,128)(2,1)S(1)} %get-tuple-element.51), channel_id=1, source_target_pairs={{0,24},{4,28},{8,16},{12,20},{16,8},{20,12},{24,0},{28,4},{1,25},{... | collective-permute-start | bytes 233480 | tf_op jit(solution)/shard_map/ppermute | solution.py:308
  59.8 7.7 %collective-permute-start.18 = (bf16[304,128]{1,0:T(8,128)(2,1)S(1)}, bf16[304,128]{1,0:T(8,128)(2,1)S(1)}, u32[]{:S(2)}, u32[]{:S(2)}) collective-permute-start(bf16[304,128]{1,0:T(8,128)(2,1)S(1)} %get-tuple-element.52), channel_id=1, source_target_pairs={{0,16},{4,20},{8,24},{12,28},{16,0},{20,4},{24,8},{28,12},{1,17},{... | collective-permute-start | bytes 233480 | tf_op jit(solution)/shard_map/ppermute | solution.py:308
  61.5 6.2 %collective-permute-start.19 = (bf16[304,128]{1,0:T(8,128)(2,1)S(1)}, bf16[304,128]{1,0:T(8,128)(2,1)S(1)}, u32[]{:S(2)}, u32[]{:S(2)}) collective-permute-start(bf16[304,128]{1,0:T(8,128)(2,1)S(1)} %fusion), channel_id=1, source_target_pairs={{0,8},{4,12},{8,0},{12,4},{16,24},{20,28},{24,16},{28,20},{1,9},{5... | collective-permute-start | bytes 233480 | tf_op jit(solution)/shard_map/ppermute | solution.py:308
  67.8 5.0 %collective-permute-start.20 = (bf16[304,128]{1,0:T(8,128)(2,1)S(1)}, bf16[304,128]{1,0:T(8,128)(2,1)S(1)}, u32[]{:S(2)}, u32[]{:S(2)}) collective-permute-start(bf16[304,128]{1,0:T(8,128)(2,1)S(1)} %fusion.6.refs_0_), channel_id=1, source_target_pairs={{0,8},{4,12},{8,0},{12,4},{16,24},{20,28},{24,16},{28,20},{1,9},{5... | collective-permute-start | bytes 233480 | tf_op jit(solution)/shard_map/ppermute | solution.py:308
  67.8 8.7 %collective-permute-start.21 = (bf16[304,128]{1,0:T(8,128)(2,1)S(1)}, bf16[304,128]{1,0:T(8,128)(2,1)S(1)}, u32[]{:S(2)}, u32[]{:S(2)}) collective-permute-start(bf16[304,128]{1,0:T(8,128)(2,1)S(1)} %fusion.6.refs_0_), channel_id=1, source_target_pairs={{0,16},{4,20},{8,24},{12,28},{16,0},{20,4},{24,8},{28,12},{1,17},{... | collective-permute-start | bytes 233480 | tf_op jit(solution)/shard_map/ppermute | solution.py:308
  69.7 7.7 %collective-permute-start.22 = (bf16[304,128]{1,0:T(8,128)(2,1)S(1)}, bf16[304,128]{1,0:T(8,128)(2,1)S(1)}, u32[]{:S(2)}, u32[]{:S(2)}) collective-permute-start(bf16[304,128]{1,0:T(8,128)(2,1)S(1)} %fusion.6.refs_0_), channel_id=1, source_target_pairs={{0,24},{4,28},{8,16},{12,20},{16,8},{20,12},{24,0},{28,4},{1,25},{... | collective-permute-start | bytes 233480 | tf_op jit(solution)/shard_map/ppermute | solution.py:308
  72.3 7.0 %collective-permute-start.23 = (bf16[304,128]{1,0:T(8,128)(2,1)S(1)}, bf16[304,128]{1,0:T(8,128)(2,1)S(1)}, u32[]{:S(2)}, u32[]{:S(2)}) collective-permute-start(bf16[304,128]{1,0:T(8,128)(2,1)S(1)} %fusion.6.refs_0_), channel_id=1, source_target_pairs={{0,4},{4,0},{8,12},{12,8},{16,20},{20,16},{24,28},{28,24},{1,5},{5... | collective-permute-start | bytes 233480 | tf_op jit(solution)/shard_map/ppermute | solution.py:308
  72.8 6.5 %collective-permute-start.24 = (bf16[304,128]{1,0:T(8,128)(2,1)S(1)}, bf16[304,128]{1,0:T(8,128)(2,1)S(1)}, u32[]{:S(2)}, u32[]{:S(2)}) collective-permute-start(bf16[304,128]{1,0:T(8,128)(2,1)S(1)} %collective-permute-done.20.refs_1_), channel_id=1, source_target_pairs={{0,4},{4,0},{8,12},{12,8},{16,20},{20,16},{24,28},{28,24},{1,5},{5... | collective-permute-start | bytes 233480 | tf_op jit(solution)/shard_map/ppermute | solution.py:308
  76.6 4.4 %collective-permute-start.25 = (bf16[304,128]{1,0:T(8,128)(2,1)S(1)}, bf16[304,128]{1,0:T(8,128)(2,1)S(1)}, u32[]{:S(2)}, u32[]{:S(2)}) collective-permute-start(bf16[304,128]{1,0:T(8,128)(2,1)S(1)} %collective-permute-done.21.refs_2_), channel_id=1, source_target_pairs={{0,4},{4,0},{8,12},{12,8},{16,20},{20,16},{24,28},{28,24},{1,5},{5... | collective-permute-start | bytes 233480 | tf_op jit(solution)/shard_map/ppermute | solution.py:308
  77.4 4.4 %collective-permute-start.26 = (bf16[304,128]{1,0:T(8,128)(2,1)S(1)}, bf16[304,128]{1,0:T(8,128)(2,1)S(1)}, u32[]{:S(2)}, u32[]{:S(2)}) collective-permute-start(bf16[304,128]{1,0:T(8,128)(2,1)S(1)} %collective-permute-done.22.refs_3_), channel_id=1, source_target_pairs={{0,4},{4,0},{8,12},{12,8},{16,20},{20,16},{24,28},{28,24},{1,5},{5... | collective-permute-start | bytes 233480 | tf_op jit(solution)/shard_map/ppermute | solution.py:308

commit v4 on v3

--- a/solution.py
+++ b/solution.py
@@ -34,14 +34,19 @@
     )
 
 
-def call(kernel, out_shape, in_specs, flops, scratch=()):
+def call(kernel, out_shape, in_specs, flops, scratch=(), after=()):
     many = isinstance(out_shape, (list, tuple))
     outs = out_shape if many else [out_shape]
     moved = sum(math.prod(one.shape) * one.dtype.itemsize for one in outs)
-    return pl.pallas_call(
-        kernel,
+    waited = len(after)
+
+    def run(*refs):
+        kernel(*refs[waited:])
+
+    made = pl.pallas_call(
+        run,
         out_shape=out_shape,
-        in_specs=in_specs,
+        in_specs=[pl.BlockSpec(memory_space=pl.ANY)] * waited + in_specs,
         out_specs=[IN_VMEM] * len(outs) if many else IN_VMEM,
         scratch_shapes=list(scratch),
         compiler_params=pltpu.CompilerParams(vmem_limit_bytes=VMEM_LIMIT),
@@ -49,6 +54,7 @@
             flops=flops, bytes_accessed=3 * moved, transcendentals=0
         ),
     )
+    return functools.partial(made, *after)
 
 
 class Plan:
@@ -73,20 +79,9 @@
             out_ref[slot] = jnp.where(slot < plan_ref[plan.sent + side], picked, 0.0)
 
 
-def first_kernel(plan, plan_ref, feat_ref, left_ref, right_ref, held_ref, sem):
-    copy = pltpu.make_async_copy(feat_ref, held_ref, sem)
-    copy.start()
-    copy.wait()
-    blocks = [held_ref[number] for number in range(held_ref.shape[0])]
-    write_sends(plan, plan_ref, blocks, left_ref, right_ref)
-
-
-def next_blocks(plan, plan_ref, cur_ref, low_ref, high_ref, tiles_ref, ext_ref):
+def next_blocks(plan, plan_ref, cur_ref, tiles_ref, ext_ref):
     local = cur_ref.shape[0]
-    slots = low_ref.shape[0]
     ext_ref[:local] = cur_ref[...]
-    ext_ref[local : local + slots] = low_ref[...]
-    ext_ref[local + slots :] = high_ref[...]
     totals = [jnp.zeros(cur_ref.shape[1:], F32) for _ in range(local)]
     live = plan_ref[plan.count]
     for tile in range(plan.tiles):
@@ -101,14 +96,41 @@
     return totals
 
 
+def extend(cur_ref, low_ref, high_ref, ext_ref):
+    local = cur_ref.shape[0]
+    slots = low_ref.shape[0]
+    ext_ref[local : local + slots] = low_ref[...]
+    ext_ref[local + slots :] = high_ref[...]
+
+
+def write_hop(plan, plan_ref, cur_ref, tiles_ref, next_ref, left_ref, right_ref, ext_ref):
+    blocks = next_blocks(plan, plan_ref, cur_ref, tiles_ref, ext_ref)
+    write_sends(plan, plan_ref, blocks, left_ref, right_ref)
+    for number, block in enumerate(blocks):
+        next_ref[number] = block
+
+
+def first_hop_kernel(
+    plan, plan_ref, low_plan_ref, high_plan_ref, cur_ref, low_ref, high_ref, tiles_ref,
+    next_ref, left_ref, right_ref, ext_ref,
+):
+    local = cur_ref.shape[0]
+    for slot in range(plan.slots):
+        low = low_ref[low_plan_ref[plan.right + slot]]
+        high = high_ref[high_plan_ref[plan.left + slot]]
+        live_low = slot < low_plan_ref[plan.sent + 1]
+        live_high = slot < high_plan_ref[plan.sent]
+        ext_ref[local + slot] = jnp.where(live_low, low, 0.0)
+        ext_ref[local + plan.slots + slot] = jnp.where(live_high, high, 0.0)
+    write_hop(plan, plan_ref, cur_ref, tiles_ref, next_ref, left_ref, right_ref, ext_ref)
+
+
 def hop_kernel(
     plan, plan_ref, cur_ref, low_ref, high_ref, tiles_ref,
     next_ref, left_ref, right_ref, ext_ref,
 ):
-    blocks = next_blocks(plan, plan_ref, cur_ref, low_ref, high_ref, tiles_ref, ext_ref)
-    write_sends(plan, plan_ref, blocks, left_ref, right_ref)
-    for number, block in enumerate(blocks):
-        next_ref[number] = block
+    extend(cur_ref, low_ref, high_ref, ext_ref)
+    write_hop(plan, plan_ref, cur_ref, tiles_ref, next_ref, left_ref, right_ref, ext_ref)
 
 
 def branch_logits(branch, rows, w_ref, wc_ref):
@@ -151,23 +173,27 @@
     return (order_ref[...] == rows).astype(F32).astype(BF16)
 
 
+def wanted_places(nodes, group, step, offset, count):
+    share = nodes // group
+    mine = lax.axis_index("shuf")
+    first = mine * share
+    source = lax.broadcasted_iota(jnp.int32, (count, nodes), 0) + offset
+    target = lax.broadcasted_iota(jnp.int32, (count, nodes), 1)
+    moved = source + ((mine ^ step) - mine) * share
+    wanted = (target == moved) & (source >= first) & (source < first + share)
+    return wanted.astype(F32).astype(BF16)
+
+
 def label_kernel(order_ref, *refs):
     nodes = order_ref.shape[1]
     group = len(refs) - 1
-    share = nodes // group
-    mine = lax.axis_index("shuf")
     width = refs[0].shape[1]
     per_piece = nodes // width
     ordered = [jnp.zeros((1, nodes), F32) for _ in range(2)]
     for step in range(group):
         tail = refs[step][nodes:]
-        away = ((mine ^ step) - mine) * share
         for part in range(per_piece):
-            source = lax.broadcasted_iota(jnp.int32, (width, nodes), 0) + part * width
-            target = lax.broadcasted_iota(jnp.int32, (width, nodes), 1)
-            first = mine * share
-            wanted = (target == source + away) & (source >= first) & (source < first + share)
-            moved = matmul(tail, wanted.astype(F32).astype(BF16))
+            moved = matmul(tail, wanted_places(nodes, group, step, part * width, width))
             for piece in range(2):
                 row = piece * per_piece + part
                 ordered[piece] = ordered[piece] + moved[row : row + 1]
@@ -177,12 +203,23 @@
     refs[-1][...] = (pieces[0:1] + 256.0 * pieces[1:2]).astype(jnp.int32)
 
 
+def loss_kernel(*refs):
+    group = len(refs) - 1
+    height, nodes = refs[0].shape
+    total = jnp.zeros((16, nodes), F32)
+    for step in range(group):
+        wanted = wanted_places(nodes, group, step, 0, nodes)
+        total = total + matmul(refs[step][height - 16 :], wanted)
+    refs[-1][...] = total[0:1] + total[1:2] + total[2:3]
+
+
 def last_kernel(
     plan, row_scale, plan_ref,
     cur_ref, low_ref, high_ref, tiles_ref, before_ref, w_ref, wc_ref, order_ref, label_ref,
     out_ref, ext_ref,
 ):
-    blocks = next_blocks(plan, plan_ref, cur_ref, low_ref, high_ref, tiles_ref, ext_ref)
+    extend(cur_ref, low_ref, high_ref, ext_ref)
+    blocks = next_blocks(plan, plan_ref, cur_ref, tiles_ref, ext_ref)
     halves = [block.astype(BF16) for block in blocks]
     rows_b = jnp.concatenate(halves, axis=0)
     size, width = halves[0].shape
@@ -222,26 +259,23 @@
         wct_ref[branch] = pad_ref[...].T[:, :kept].astype(BF16)
 
 
-def all_chunks(kept, row_refs, last_ref, w_ref, wt_ref, wct_ref, chunks_ref):
-    group = last_ref.shape[0]
+def all_chunks(kept, row_refs, last_refs, w_ref, wt_ref, wct_ref, chunks_ref):
+    group = len(last_refs)
     branches, own, width = wt_ref.shape
     nodes = row_refs[-1].shape[0]
     hid = w_ref.shape[2]
-    parts = last_ref.shape[2] // width
+    parts = last_refs[0].shape[1] // width
     size = nodes // parts
-    mine = lax.axis_index("shuf")
     all_rows = []
     for branch in range(branches - 1):
         ours = row_refs[branch * group : (branch + 1) * group]
         all_rows.append(jnp.concatenate([ref[:nodes] for ref in ours], axis=0))
     last_rows = []
-    for step in range(group):
+    for ref in last_refs:
         for part in range(parts):
-            last_rows.append(last_ref[mine ^ step, :size, part * width : (part + 1) * width])
+            last_rows.append(ref[:size, part * width : (part + 1) * width])
     all_rows.append(jnp.concatenate(last_rows, axis=0))
-    dlogits_t = jnp.concatenate(
-        [last_ref[mine ^ step, size : size + kept] for step in range(group)], axis=1
-    )
+    dlogits_t = jnp.concatenate([ref[size : size + kept] for ref in last_refs], axis=1)
     own_class = branches * own
     first = lax.axis_index("shuf") * own_class
     which = first // hid
@@ -264,10 +298,11 @@
             ]
 
 
-def grad_kernel(kept, row_count, half, *refs):
-    outs = refs[row_count + 4 : -1]
+def grad_kernel(kept, group, row_count, half, *refs):
+    ins = row_count + group + 3
+    outs = refs[ins:-1]
     chunks_ref = refs[-1]
-    all_chunks(kept, refs[:row_count], *refs[row_count : row_count + 4], chunks_ref)
+    plain_grad_kernel(kept, group, row_count, *refs[:ins], chunks_ref)
     dom = lax.axis_index("dom")
     for step in range(half):
         stays = dom ^ (2 * step)
@@ -275,8 +310,9 @@
         outs[half + step // 2][step % 2] = chunks_ref[stays ^ 1].astype(BF16)
 
 
-def plain_grad_kernel(kept, row_count, *refs):
-    all_chunks(kept, refs[:row_count], *refs[row_count:])
+def plain_grad_kernel(kept, group, row_count, *refs):
+    last = row_count + group
+    all_chunks(kept, refs[:row_count], refs[row_count:last], *refs[last:])
 
 
 def write_chunk(kept, chunk, value, branch_ref, class_ref):
@@ -354,18 +390,12 @@
     w_class_t = w_class.T
 
     current = features.reshape(local, block, width)
-    to_left, to_right = call(
-        functools.partial(first_kernel, plan),
-        [slots_f32, slots_f32],
-        [IN_SMEM, pl.BlockSpec(memory_space=pl.ANY)],
-        1000,
-        [pltpu.VMEM((local, block, width), F32), pltpu.SemaphoreType.DMA],
-    )(small, current)
     gathered = []
     logits = None
     hop_flops = 12 * tiles * block * block * width
     forward_flops = 2 * nodes * hid * (width + classes)
     ext = pltpu.VMEM((local + 2 * slots, block, width), F32)
+    to_left = to_right = current
     for hop in range(HOPS):
         from_lower = passed_along(to_right, "dom", 1)
         from_upper = passed_along(to_left, "dom", -1)
@@ -380,22 +410,30 @@
                 [IN_VMEM] * 4,
                 forward_flops,
             )(current, w_branch, w_class_t, logits)
-        gathered += in_group(rows)
+        gathered.append(in_group(rows))
         if hop < HOPS - 1:
+            out_shape = [blocks_f32, slots_f32, slots_f32]
+            if hop == 0:
+                kernel = first_hop_kernel
+                plans = (small, passed_along(small, "dom", 1), passed_along(small, "dom", -1))
+            else:
+                kernel = hop_kernel
+                plans = (small,)
             current, to_left, to_right = call(
-                functools.partial(hop_kernel, plan),
-                [blocks_f32, slots_f32, slots_f32],
-                [IN_SMEM] + [IN_VMEM] * 4,
+                functools.partial(kernel, plan),
+                out_shape,
+                [IN_SMEM] * len(plans) + [IN_VMEM] * 4,
                 hop_flops,
                 [ext],
-            )(small, current, from_lower, from_upper, tile_values)
+                [logits] + [members[shuf // 2] for members in gathered[:hop]],
+            )(*plans, current, from_lower, from_upper, tile_values)
 
     label_mine = call(
         label_kernel,
         jax.ShapeDtypeStruct((1, nodes), jnp.int32),
         [IN_VMEM] * (1 + shuf),
         1000,
-    )(batch_order, *gathered[:shuf])
+    )(batch_order, *gathered[0])
 
     wt_own, wct_own = call(
         weights_kernel,
@@ -414,20 +452,21 @@
         [IN_SMEM] + [IN_VMEM] * 9,
         hop_flops + forward_flops,
         [ext],
+        [*gathered[1][1:], gathered[2][shuf // 2]],
     )(
         small, current, from_lower, from_upper, tile_values,
         logits, w_branch, w_class_t, batch_order, label_mine,
     )
-    last_all = lax.all_gather(payload, "shuf")
-    loss_parts = lax.dynamic_slice(
-        last_all, (0, block + kept, mine * share), (shuf, 3, share)
-    ).astype(F32)
-    loss_rows = (loss_parts[:, 0] + loss_parts[:, 1] + loss_parts[:, 2]).reshape(nodes)
+    gathered = [member for members in gathered for member in members]
+    last_all = in_group(payload)
+    loss_rows = call(
+        loss_kernel, jax.ShapeDtypeStruct((1, nodes), F32), [IN_VMEM] * shuf, 1000
+    )(*last_all).reshape(nodes)
 
     chunks = own_class // LANES
     height = kept + width
     grad_flops = 2 * shuf * nodes * own_class * (3 * width + 2 * kept)
-    grad_ins = (*gathered, last_all, w_branch, wt_own, wct_own)
+    grad_ins = (*gathered, *last_all, w_branch, wt_own, wct_own)
     outs = [
         jax.ShapeDtypeStruct((branches, width, own), F32),
         jax.ShapeDtypeStruct((classes, own_class), F32),
@@ -438,7 +477,7 @@
         one_f32 = jax.ShapeDtypeStruct((height, LANES), F32)
         two_b16 = jax.ShapeDtypeStruct((2, height, LANES), BF16)
         made = call(
-            functools.partial(grad_kernel, kept, len(gathered), half),
+            functools.partial(grad_kernel, kept, shuf, len(gathered), half),
             [one_f32] * half + [two_b16] * (half // 2),
             [IN_VMEM] * len(grad_ins),
             grad_flops,
@@ -466,7 +505,7 @@
         )(*near, *other)
     else:
         grads = call(
-            functools.partial(plain_grad_kernel, kept, len(gathered)),
+            functools.partial(plain_grad_kernel, kept, shuf, len(gathered)),
             jax.ShapeDtypeStruct((chunks, height, LANES), F32),
             [IN_VMEM] * len(grad_ins),
             grad_flops,

time: 83.3 us -> 86.3 us (1.036)
  blocking collectives: 7.66 us -> 0 us
  starting transfers between devices: 33.7 us -> 39.4 us
  waiting for transfers between devices: 22.9 us -> 27.4 us
    ppermute x21 -> x24, waiting for transfers between devices: 18.2 us -> 27.4 us  [swapped(): return lax.ppermute(value, axis, pairs)]
    all_gather x1 -> x0, blocking collectives: 7.66 us -> none  [body(): last_all = lax.all_gather(payload, 'shuf')]
    ppermute x6 -> x8, starting transfers between devices: 15.7 us -> 20.4 us  [passed_along(): return lax.ppermute(value, axis, pairs)]
    ppermute x6 -> x8, waiting for transfers between devices: 4.68 us -> 0.02 us  [passed_along(): return lax.ppermute(value, axis, pairs)]
    unnamed x16 -> x18, local copies, waits for them, and re-layouts: 4 us -> 5.23 us
    ppermute x21 -> x24, starting transfers between devices: 18 us -> 19 us  [swapped(): return lax.ppermute(value, axis, pairs)]
  transfers between devices with their start and end apart: 27 -> 32, of which waited for: 12 -> 14; matrix products, arithmetic and copies ran while one was open for 1% -> 1% of each run, Pallas kernels for 7% -> 5%
where the time goes in v4:
time: 86.3 us; the launch traced here: 86 us
  starting transfers between devices  39.4 us (46%)
  waiting for transfers between devices  27.4 us (32%)
  Pallas kernels  11.7 us (14%)
  local copies, waits for them, and re-layouts  6.03 us (7%)
  between operations  1.49 us (2%)
    ppermute x24, waiting for transfers between devices, swapped(): return lax.ppermute(value, axis, pairs)  27.4 us
    ppermute x8, starting transfers between devices, passed_along(): return lax.ppermute(value, axis, pairs)  20.4 us
    ppermute x24, starting transfers between devices, swapped(): return lax.ppermute(value, axis, pairs)  19 us
    unnamed x18, local copies, waits for them, and re-layouts  5.23 us
    pallas_call x1, Pallas kernels, body(): call(functools.partial(grad_kernel, kept, shuf, len(gathered), half), [on...  2.82 us
    pallas_call x2, Pallas kernels, body(): call(functools.partial(kernel, plan), out_shape, [IN_SMEM] * len(plans) +...  2.43 us
    pallas_call x1, Pallas kernels, body(): call(functools.partial(last_kernel, plan, row_scale), jax.ShapeDtypeStruc...  1.99 us
  transfers between devices with their start and end apart: 32, of which 14 were waited for; matrix products, arithmetic and copies ran while one was open for 1% of the time, Pallas kernels for 5%

profile of v4, /device:TPU:0, one launch (start us, length us, event | category | flops | bytes accessed | tf_op | source)
XLA Modules:
  0.0 86.0 jit_solution(4834501253715601419)
XLA Ops:
  0.6 3.0 %collective-permute-start.2 = (f32[2,128,128]{2,1,0:T(8,128)}, f32[2,128,128]{2,1,0:T(8,128)S(1)}, u32[]{:S(2)}, u32[]{:S(2)}) collective-permute-start(f32[2,128,128]{2,1,0:T(8,128)} %bitcast.31), channel_id=1, source_target_pairs={{0,4},{4,8},{8,12},{12,16},{16,20},{20,24},{24,28},{28,0},{1,5},{5... | collective-permute-start | bytes 393224 | tf_op jit(solution)/shard_map/ppermute | solution.py:28
  3.7 3.1 %collective-permute-start.3 = (f32[2,128,128]{2,1,0:T(8,128)}, f32[2,128,128]{2,1,0:T(8,128)S(1)}, u32[]{:S(2)}, u32[]{:S(2)}) collective-permute-start(f32[2,128,128]{2,1,0:T(8,128)} %bitcast.32), channel_id=1, source_target_pairs={{0,28},{4,0},{8,4},{12,8},{16,12},{20,16},{24,20},{28,24},{1,29},{... | collective-permute-start | bytes 393224 | tf_op jit(solution)/shard_map/ppermute | solution.py:28
  7.4 0.8 concatenate.3.refs_1_.refs_2_.refs_4_
  8.2 0.0 collective-permute-start
  8.2 4.7 %collective-permute-start.1 = (s32[23]{0:T(128)S(1)}, s32[23]{0:T(128)S(1)}, u32[]{:S(2)}, u32[]{:S(2)}) collective-permute-start(s32[23]{0:T(128)S(1)} %concatenate.3.refs_1_.refs_2_.refs_4_), channel_id=1, source_target_pairs={{0,28},{4,0},{8,4},{12,8},{16,12},{20,16},{24,20},{28,24},{1,29},{... | collective-permute-start | bytes 284 | tf_op jit(solution)/shard_map/ppermute | solution.py:28
  12.9 1.4 %copy-done = bf16[4096,172]{0,1:T(8,128)(2,1)S(1)} copy-done((bf16[4096,172]{0,1:T(8,128)(2,1)S(1)}, bf16[4096,172]{0,1:T(8,128)(2,1)}, u32[]{:S(2)}) %copy-start) | copy-done | bytes 1409048
  14.3 1.2 %copy-done.2 = bf16[4,128,1024]{2,1,0:T(8,128)(2,1)S(1)} copy-done((bf16[4,128,1024]{2,1,0:T(8,128)(2,1)S(1)}, bf16[4,128,1024]{2,1,0:T(8,128)(2,1)}, u32[]{:S(2)}) %copy-start.2) | copy-done | bytes 1048600
  15.5 1.0 %copy-done.4 = f32[8,128,128]{2,1,0:T(8,128)S(1)} copy-done((f32[8,128,128]{2,1,0:T(8,128)S(1)}, f32[8,128,128]{2,1,0:T(8,128)}, u32[]{:S(2)}) %copy-start.4) | copy-done | bytes 524312
  16.6 0.9 %copy-done.6 = f32[256,128]{1,0:T(8,128)S(1)} copy-done((f32[256,128]{1,0:T(8,128)S(1)}, f32[256,128]{1,0:T(8,128)}, u32[]{:S(2)}) %copy-start.6) | copy-done | bytes 131096
  17.5 0.7 copy-done.8
  18.1 0.6 shard_map.139
  18.7 0.0 collective-permute-done.refs_2_
  18.8 0.0 collective-permute-done.2.refs_5_
  18.8 0.0 collective-permute-done.3.refs_6_
  18.8 1.2 %shard_map.140 = (f32[2,128,128]{2,1,0:T(8,128)S(1)}, f32[2,128,128]{2,1,0:T(8,128)S(1)}, f32[2,128,128]{2,1,0:T(8,128)S(1)}) custom-call(f32[172,256]{1,0:T(8,128)S(1)} %get-tuple-element.25.refs_0_.refs_3_, s32[23]{0:T(128)S(1)} %concatenate.3.refs_1_.refs_2_.refs_4_, s32[23]{0:T(128)S(1)} %collective-permute-done.refs_2_, ...), custom_call_target="tpu_custom_call" | custom-call | flops 201326592 | bytes 1179648 | tf_op jit(solution)/shard_map/pallas_call | solution.py:422
  20.0 0.0 copy-start.5
  20.0 0.1 collective-permute-start.8
  20.1 4.7 %collective-permute-start.9 = (f32[2,128,128]{2,1,0:T(8,128)S(1)}, f32[2,128,128]{2,1,0:T(8,128)S(1)}, u32[]{:S(2)}, u32[]{:S(2)}) collective-permute-start(f32[2,128,128]{2,1,0:T(8,128)S(1)} %get-tuple-element.31), channel_id=1, source_target_pairs={{0,28},{4,0},{8,4},{12,8},{16,12},{20,16},{24,20},{28,24},{1,29},{... | collective-permute-start | bytes 393224 | tf_op jit(solution)/shard_map/ppermute | solution.py:28
  24.8 1.6 %collective-permute-start.7 = (bf16[272,128]{1,0:T(8,128)(2,1)S(1)}, bf16[272,128]{1,0:T(8,128)(2,1)S(1)}, u32[]{:S(2)}, u32[]{:S(2)}) collective-permute-start(bf16[272,128]{1,0:T(8,128)(2,1)S(1)} %get-tuple-element.29.refs_1_.refs_0_), channel_id=1, source_target_pairs={{0,2},{1,3},{2,0},{3,1},{4,6},{5,7},{6,4},{7,5},{8,10},{9,11},{10,... | collective-permute-start | bytes 208904 | tf_op jit(solution)/shard_map/ppermute | solution.py:344
  26.4 2.7 %collective-permute-done.7.refs_1_.refs_3_.refs_2_ = bf16[272,128]{1,0:T(8,128)(2,1)S(1)} collective-permute-done((bf16[272,128]{1,0:T(8,128)(2,1)S(1)}, bf16[272,128]{1,0:T(8,128)(2,1)S(1)}, u32[]{:S(2)}, u32[]{:S(2)}) %collective-permute-start.7) | collective-permute-done | bytes 69664 | tf_op jit(solution)/shard_map/ppermute | solution.py:344
  29.1 0.6 shard_map.141
  29.7 1.7 %collective-permute-start.5 = (bf16[256,128]{1,0:T(8,128)(2,1)S(1)}, bf16[256,128]{1,0:T(8,128)(2,1)S(1)}, u32[]{:S(2)}, u32[]{:S(2)}) collective-permute-start(bf16[256,128]{1,0:T(8,128)(2,1)S(1)} %get-tuple-element.27.refs_4_), channel_id=1, source_target_pairs={{0,2},{1,3},{2,0},{3,1},{4,6},{5,7},{6,4},{7,5},{8,10},{9,11},{10,... | collective-permute-start | bytes 196616 | tf_op jit(solution)/shard_map/ppermute | solution.py:344
  31.4 1.2 %shard_map.142 = (f32[2,128,128]{2,1,0:T(8,128)S(1)}, f32[2,128,128]{2,1,0:T(8,128)S(1)}, f32[2,128,128]{2,1,0:T(8,128)S(1)}) custom-call(f32[172,256]{1,0:T(8,128)S(1)} %get-tuple-element.28.refs_0_.refs_3_, bf16[272,128]{1,0:T(8,128)(2,1)S(1)} %collective-permute-done.7.refs_1_.refs_3_.refs_2_, s32[23]{0:T(128)S(1)} %concatenate.3.refs_1_.refs_2_.refs_4_, ...), custom_call_target="tpu_custom_call" | custom-call | flops 201326592 | bytes 1179648 | tf_op jit(solution)/shard_map/pallas_call | solution.py:422
  32.6 0.0 copy-start.7
  32.6 0.1 collective-permute-start.11
  32.7 4.7 %collective-permute-start.12 = (f32[2,128,128]{2,1,0:T(8,128)S(1)}, f32[2,128,128]{2,1,0:T(8,128)S(1)}, u32[]{:S(2)}, u32[]{:S(2)}) collective-permute-start(f32[2,128,128]{2,1,0:T(8,128)S(1)} %get-tuple-element.35), channel_id=1, source_target_pairs={{0,28},{4,0},{8,4},{12,8},{16,12},{20,16},{24,20},{28,24},{1,29},{... | collective-permute-start | bytes 393224 | tf_op jit(solution)/shard_map/ppermute | solution.py:28
  37.4 0.6 shard_map.143
  38.0 0.1 collective-permute-start.4
  38.1 0.5 collective-permute-start.6
  38.6 0.4 collective-permute-start.10
  39.0 0.4 shard_map.144.refs_13_
  39.4 0.0 collective-permute-done.4.refs_0_.refs_5_
  39.4 0.1 collective-permute-done.6.refs_2_.refs_7_
  39.5 3.4 %collective-permute-done.10.refs_3_.refs_10_ = bf16[256,128]{1,0:T(8,128)(2,1)S(1)} collective-permute-done((bf16[256,128]{1,0:T(8,128)(2,1)S(1)}, bf16[256,128]{1,0:T(8,128)(2,1)S(1)}, u32[]{:S(2)}, u32[]{:S(2)}) %collective-permute-start.10) | collective-permute-done | bytes 65568 | tf_op jit(solution)/shard_map/ppermute | solution.py:344
  42.9 2.0 %shard_map.145.refs_0_.refs_12_ = bf16[320,256]{1,0:T(8,128)(2,1)S(1)} custom-call(bf16[256,128]{1,0:T(8,128)(2,1)S(1)} %collective-permute-done.4.refs_0_.refs_5_, bf16[256,128]{1,0:T(8,128)(2,1)S(1)} %collective-permute-done.5.refs_1_.refs_6_, bf16[256,128]{1,0:T(8,128)(2,1)S(1)} %collective-permute-done.6.refs_2_.refs_7_, ...), custom_call_target="tpu_custom_call" | custom-call | flops 358612992 | bytes 491520 | tf_op jit(solution)/shard_map/pallas_call | solution.py:449
  44.9 0.4 collective-permute-start.16
  45.3 4.9 %collective-permute-done.16.refs_2_.refs_14_ = bf16[320,256]{1,0:T(8,128)(2,1)S(1)} collective-permute-done((bf16[320,256]{1,0:T(8,128)(2,1)S(1)}, bf16[320,256]{1,0:T(8,128)(2,1)S(1)}, u32[]{:S(2)}, u32[]{:S(2)}) %collective-permute-start.16) | collective-permute-done | bytes 163872 | tf_op jit(solution)/shard_map/ppermute | solution.py:344
  50.2 0.5 collective-permute-start.18
  50.7 0.0 collective-permute-start.19
  50.7 0.3 shard_map.147
  51.0 0.7 collective-permute-done.18.refs_9_
  51.7 0.3 collective-permute-done.19.refs_11_
  52.0 2.8 %shard_map.148 = (f32[304,128]{1,0:T(8,128)S(1)}, f32[304,128]{1,0:T(8,128)S(1)}, f32[304,128]{1,0:T(8,128)S(1)}, f32[304,128]{1,0:T(8,128)S(1)}, bf16[2,304,128...) custom-call(bf16[272,128]{1,0:T(8,128)(2,1)S(1)} %get-tuple-element.29.refs_1_.refs_0_, ...), custom_call_target="tpu_custom_call" | custom-call | flops 1543503872 | bytes 2801664 | tf_op jit(solution)/shard_map/pallas_call | solution.py:479
  54.8 0.1 collective-permute-start.21
  54.9 2.0 %collective-permute-start.20 = (bf16[2,304,128]{2,1,0:T(8,128)(2,1)S(1)}, bf16[2,304,128]{2,1,0:T(8,128)(2,1)S(1)}, u32[]{:S(2)}, u32[]{:S(2)}) collective-permute-start(bf16[2,304,128]{2,1,0:T(8,128)(2,1)S(1)} %get-tuple-element.40), channel_id=1, source_target_pairs={{0,4},{4,0},{8,12},{12,8},{16,20},{20,16},{24,28},{28,24},{1,5},{5... | collective-permute-start | bytes 466952 | tf_op jit(solution)/shard_map/ppermute | solution.py:344
  56.9 4.8 %collective-permute-done.21 = bf16[2,304,128]{2,1,0:T(8,128)(2,1)S(1)} collective-permute-done((bf16[2,304,128]{2,1,0:T(8,128)(2,1)S(1)}, bf16[2,304,128]{2,1,0:T(8,128)(2,1)S(1)}, u32[]{:S(2)}, u32[]{:S(2)}) %collective-permute-start.21) | collective-permute-done | bytes 155680 | tf_op jit(solution)/shard_map/ppermute | solution.py:344
  61.8 1.1 %collective-permute-start.22 = (bf16[304,128]{1,0:T(8,128)(2,1)S(1)}, bf16[304,128]{1,0:T(8,128)(2,1)S(1)}, u32[]{:S(2)}, u32[]{:S(2)}) collective-permute-start(bf16[304,128]{1,0:T(8,128)(2,1)S(1)} %get-tuple-element.47), channel_id=1, source_target_pairs={{0,24},{4,28},{8,16},{12,20},{16,8},{20,12},{24,0},{28,4},{1,25},{... | collective-permute-start | bytes 233480 | tf_op jit(solution)/shard_map/ppermute | solution.py:344
  62.9 1.3 %collective-permute-done.20 = bf16[2,304,128]{2,1,0:T(8,128)(2,1)S(1)} collective-permute-done((bf16[2,304,128]{2,1,0:T(8,128)(2,1)S(1)}, bf16[2,304,128]{2,1,0:T(8,128)(2,1)S(1)}, u32[]{:S(2)}, u32[]{:S(2)}) %collective-permute-start.20) | collective-permute-done | bytes 155680 | tf_op jit(solution)/shard_map/ppermute | solution.py:344
  64.3 2.0 %collective-permute-start.24 = (bf16[304,128]{1,0:T(8,128)(2,1)S(1)}, bf16[304,128]{1,0:T(8,128)(2,1)S(1)}, u32[]{:S(2)}, u32[]{:S(2)}) collective-permute-start(bf16[304,128]{1,0:T(8,128)(2,1)S(1)} %fusion), channel_id=1, source_target_pairs={{0,8},{4,12},{8,0},{12,4},{16,24},{20,28},{24,16},{28,20},{1,9},{5... | collective-permute-start | bytes 233480 | tf_op jit(solution)/shard_map/ppermute | solution.py:344
  66.3 2.0 %collective-permute-done.22 = bf16[304,128]{1,0:T(8,128)(2,1)S(1)} collective-permute-done((bf16[304,128]{1,0:T(8,128)(2,1)S(1)}, bf16[304,128]{1,0:T(8,128)(2,1)S(1)}, u32[]{:S(2)}, u32[]{:S(2)}) %collective-permute-start.22) | collective-permute-done | bytes 77856 | tf_op jit(solution)/shard_map/ppermute | solution.py:344
  68.3 1.6 %collective-permute-done.23 = bf16[304,128]{1,0:T(8,128)(2,1)S(1)} collective-permute-done((bf16[304,128]{1,0:T(8,128)(2,1)S(1)}, bf16[304,128]{1,0:T(8,128)(2,1)S(1)}, u32[]{:S(2)}, u32[]{:S(2)}) %collective-permute-start.23) | collective-permute-done | bytes 77856 | tf_op jit(solution)/shard_map/ppermute | solution.py:344
  69.9 0.4 collective-permute-done.24
  70.3 0.1 fusion.6.refs_0_
  70.4 0.5 collective-permute-start.25
  70.8 1.9 %collective-permute-start.26 = (bf16[304,128]{1,0:T(8,128)(2,1)S(1)}, bf16[304,128]{1,0:T(8,128)(2,1)S(1)}, u32[]{:S(2)}, u32[]{:S(2)}) collective-permute-start(bf16[304,128]{1,0:T(8,128)(2,1)S(1)} %fusion.6.refs_0_), channel_id=1, source_target_pairs={{0,16},{4,20},{8,24},{12,28},{16,0},{20,4},{24,8},{28,12},{1,17},{... | collective-permute-start | bytes 233480 | tf_op jit(solution)/shard_map/ppermute | solution.py:344
  72.8 2.1 %collective-permute-start.27 = (bf16[304,128]{1,0:T(8,128)(2,1)S(1)}, bf16[304,128]{1,0:T(8,128)(2,1)S(1)}, u32[]{:S(2)}, u32[]{:S(2)}) collective-permute-start(bf16[304,128]{1,0:T(8,128)(2,1)S(1)} %fusion.6.refs_0_), channel_id=1, source_target_pairs={{0,24},{4,28},{8,16},{12,20},{16,8},{20,12},{24,0},{28,4},{1,25},{... | collective-permute-start | bytes 233480 | tf_op jit(solution)/shard_map/ppermute | solution.py:344
  74.8 0.7 collective-permute-start.28
  75.5 1.3 %collective-permute-start.29 = (bf16[304,128]{1,0:T(8,128)(2,1)S(1)}, bf16[304,128]{1,0:T(8,128)(2,1)S(1)}, u32[]{:S(2)}, u32[]{:S(2)}) collective-permute-start(bf16[304,128]{1,0:T(8,128)(2,1)S(1)} %collective-permute-done.25.refs_1_), channel_id=1, source_target_pairs={{0,4},{4,0},{8,12},{12,8},{16,20},{20,16},{24,28},{28,24},{1,5},{5... | collective-permute-start | bytes 233480 | tf_op jit(solution)/shard_map/ppermute | solution.py:344
  76.9 2.8 %collective-permute-done.26.refs_2_ = bf16[304,128]{1,0:T(8,128)(2,1)S(1)} collective-permute-done((bf16[304,128]{1,0:T(8,128)(2,1)S(1)}, bf16[304,128]{1,0:T(8,128)(2,1)S(1)}, u32[]{:S(2)}, u32[]{:S(2)}) %collective-permute-start.26) | collective-permute-done | bytes 77856 | tf_op jit(solution)/shard_map/ppermute | solution.py:344
  79.6 2.0 %collective-permute-start.31 = (bf16[304,128]{1,0:T(8,128)(2,1)S(1)}, bf16[304,128]{1,0:T(8,128)(2,1)S(1)}, u32[]{:S(2)}, u32[]{:S(2)}) collective-permute-start(bf16[304,128]{1,0:T(8,128)(2,1)S(1)} %collective-permute-done.27.refs_3_), channel_id=1, source_target_pairs={{0,4},{4,0},{8,12},{12,8},{16,20},{20,16},{24,28},{28,24},{1,5},{5... | collective-permute-start | bytes 233480 | tf_op jit(solution)/shard_map/ppermute | solution.py:344
  81.7 0.8 shard_map.146
  82.5 1.5 %collective-permute-done.30.refs_6_ = bf16[304,128]{1,0:T(8,128)(2,1)S(1)} collective-permute-done((bf16[304,128]{1,0:T(8,128)(2,1)S(1)}, bf16[304,128]{1,0:T(8,128)(2,1)S(1)}, u32[]{:S(2)}, u32[]{:S(2)}) %collective-permute-start.30) | collective-permute-done | bytes 77856 | tf_op jit(solution)/shard_map/ppermute | solution.py:344
  84.0 0.8 collective-permute-done.31.refs_7_
  84.9 1.2 %shard_map.149 = (f32[4,128,256]{2,1,0:T(8,128)}, f32[172,1024]{1,0:T(8,128)}) custom-call(bf16[304,128]{1,0:T(8,128)(2,1)S(1)} %fusion.6.refs_0_, bf16[304,128]{1,0:T(8,128)(2,1)S(1)} %collective-permute-done.25.refs_1_, bf16[304,128]{1,0:T(8,128)(2,1)S(1)} %collective-permute-done.26.refs_2_, bf16[304,128]{1,0:T(8,128)(2,1)S(1)} %collective-permute-done.27.refs_3_, ...), custom_call_target="tpu_custom_call" | custom-call | flops 1000 | bytes 3686400 | tf_op jit(solution)/shard_map/pallas_call | solution.py:503
  (33 shorter events, 0.1 us)
Async XLA Ops:
  0.6 18.1 %collective-permute-start.2 = (f32[2,128,128]{2,1,0:T(8,128)}, f32[2,128,128]{2,1,0:T(8,128)S(1)}, u32[]{:S(2)}, u32[]{:S(2)}) collective-permute-start(f32[2,128,128]{2,1,0:T(8,128)} %bitcast.31), channel_id=1, source_target_pairs={{0,4},{4,8},{8,12},{12,16},{16,20},{20,24},{24,28},{28,0},{1,5},{5... | collective-permute-start | bytes 393224 | tf_op jit(solution)/shard_map/ppermute | solution.py:28
  3.7 15.1 %collective-permute-start.3 = (f32[2,128,128]{2,1,0:T(8,128)}, f32[2,128,128]{2,1,0:T(8,128)S(1)}, u32[]{:S(2)}, u32[]{:S(2)}) collective-permute-start(f32[2,128,128]{2,1,0:T(8,128)} %bitcast.32), channel_id=1, source_target_pairs={{0,28},{4,0},{8,4},{12,8},{16,12},{20,16},{24,20},{28,24},{1,29},{... | collective-permute-start | bytes 393224 | tf_op jit(solution)/shard_map/ppermute | solution.py:28
  8.2 10.5 %collective-permute-start = (s32[23]{0:T(128)S(1)}, s32[23]{0:T(128)S(1)}, u32[]{:S(2)}, u32[]{:S(2)}) collective-permute-start(s32[23]{0:T(128)S(1)} %concatenate.3.refs_1_.refs_2_.refs_4_), channel_id=1, source_target_pairs={{0,4},{4,8},{8,12},{12,16},{16,20},{20,24},{24,28},{28,0},{1,5},{5... | collective-permute-start | bytes 284 | tf_op jit(solution)/shard_map/ppermute | solution.py:28
  8.2 10.5 %collective-permute-start.1 = (s32[23]{0:T(128)S(1)}, s32[23]{0:T(128)S(1)}, u32[]{:S(2)}, u32[]{:S(2)}) collective-permute-start(s32[23]{0:T(128)S(1)} %concatenate.3.refs_1_.refs_2_.refs_4_), channel_id=1, source_target_pairs={{0,28},{4,0},{8,4},{12,8},{16,12},{20,16},{24,20},{28,24},{1,29},{... | collective-permute-start | bytes 284 | tf_op jit(solution)/shard_map/ppermute | solution.py:28
  12.9 1.4 %copy-start = (bf16[4096,172]{0,1:T(8,128)(2,1)S(1)}, bf16[4096,172]{0,1:T(8,128)(2,1)}, u32[]{:S(2)}) copy-start(bf16[4096,172]{0,1:T(8,128)(2,1)} %param.23) | copy-start | bytes 4227076
  14.3 1.2 %copy-start.2 = (bf16[4,128,1024]{2,1,0:T(8,128)(2,1)S(1)}, bf16[4,128,1024]{2,1,0:T(8,128)(2,1)}, u32[]{:S(2)}) copy-start(bf16[4,128,1024]{2,1,0:T(8,128)(2,1)} %refs_16_.1) | copy-start | bytes 3145732
  15.5 1.0 %copy-start.4 = (f32[8,128,128]{2,1,0:T(8,128)S(1)}, f32[8,128,128]{2,1,0:T(8,128)}, u32[]{:S(2)}) copy-start(f32[8,128,128]{2,1,0:T(8,128)} %refs_8_.1) | copy-start | bytes 1572868
  16.6 0.9 %copy-start.6 = (f32[256,128]{1,0:T(8,128)S(1)}, f32[256,128]{1,0:T(8,128)}, u32[]{:S(2)}) copy-start(f32[256,128]{1,0:T(8,128)} %param.12) | copy-start | bytes 393220
  17.5 0.7 copy-start.8
  18.1 11.0 %copy-start.1 = (bf16[4096,172]{0,1:T(8,128)(2,1)S(1)}, bf16[4096,172]{0,1:T(8,128)(2,1)}, u32[]{:S(2)}) copy-start(bf16[4096,172]{0,1:T(8,128)(2,1)} %param.23) | copy-start | bytes 4227076
  18.1 11.0 %copy-start.3 = (bf16[4,128,1024]{2,1,0:T(8,128)(2,1)S(1)}, bf16[4,128,1024]{2,1,0:T(8,128)(2,1)}, u32[]{:S(2)}) copy-start(bf16[4,128,1024]{2,1,0:T(8,128)(2,1)} %refs_16_.1) | copy-start | bytes 3145732
  20.0 11.4 %copy-start.5 = (f32[8,128,128]{2,1,0:T(8,128)S(1)}, f32[8,128,128]{2,1,0:T(8,128)}, u32[]{:S(2)}) copy-start(f32[8,128,128]{2,1,0:T(8,128)} %refs_8_.1) | copy-start | bytes 1572868
  20.0 11.4 %collective-permute-start.8 = (f32[2,128,128]{2,1,0:T(8,128)S(1)}, f32[2,128,128]{2,1,0:T(8,128)S(1)}, u32[]{:S(2)}, u32[]{:S(2)}) collective-permute-start(f32[2,128,128]{2,1,0:T(8,128)S(1)} %get-tuple-element.30), channel_id=1, source_target_pairs={{0,4},{4,8},{8,12},{12,16},{16,20},{20,24},{24,28},{28,0},{1,5},{5... | collective-permute-start | bytes 393224 | tf_op jit(solution)/shard_map/ppermute | solution.py:28
  20.1 11.3 %collective-permute-start.9 = (f32[2,128,128]{2,1,0:T(8,128)S(1)}, f32[2,128,128]{2,1,0:T(8,128)S(1)}, u32[]{:S(2)}, u32[]{:S(2)}) collective-permute-start(f32[2,128,128]{2,1,0:T(8,128)S(1)} %get-tuple-element.31), channel_id=1, source_target_pairs={{0,28},{4,0},{8,4},{12,8},{16,12},{20,16},{24,20},{28,24},{1,29},{... | collective-permute-start | bytes 393224 | tf_op jit(solution)/shard_map/ppermute | solution.py:28
  24.8 4.3 %collective-permute-start.7 = (bf16[272,128]{1,0:T(8,128)(2,1)S(1)}, bf16[272,128]{1,0:T(8,128)(2,1)S(1)}, u32[]{:S(2)}, u32[]{:S(2)}) collective-permute-start(bf16[272,128]{1,0:T(8,128)(2,1)S(1)} %get-tuple-element.29.refs_1_.refs_0_), channel_id=1, source_target_pairs={{0,2},{1,3},{2,0},{3,1},{4,6},{5,7},{6,4},{7,5},{8,10},{9,11},{10,... | collective-permute-start | bytes 208904 | tf_op jit(solution)/shard_map/ppermute | solution.py:344
  26.4 11.6 %collective-permute-start.13 = (bf16[272,128]{1,0:T(8,128)(2,1)S(1)}, bf16[272,128]{1,0:T(8,128)(2,1)S(1)}, u32[]{:S(2)}, u32[]{:S(2)}) collective-permute-start(bf16[272,128]{1,0:T(8,128)(2,1)S(1)} %get-tuple-element.29.refs_1_.refs_0_), channel_id=1, source_target_pairs={{0,1},{1,0},{2,3},{3,2},{4,5},{5,4},{6,7},{7,6},{8,9},{9,8},{10,11... | collective-permute-start | bytes 208904 | tf_op jit(solution)/shard_map/ppermute | solution.py:344
  29.1 9.5 %collective-permute-start.14 = (bf16[272,128]{1,0:T(8,128)(2,1)S(1)}, bf16[272,128]{1,0:T(8,128)(2,1)S(1)}, u32[]{:S(2)}, u32[]{:S(2)}) collective-permute-start(bf16[272,128]{1,0:T(8,128)(2,1)S(1)} %collective-permute-done.7.refs_1_.refs_3_.refs_2_), channel_id=1, source_target_pairs={{0,1},{1,0},{2,3},{3,2},{4,5},{5,4},{6,7},{7,6},{8,9},{9,8},{10,11... | collective-permute-start | bytes 208904 | tf_op jit(solution)/shard_map/ppermute | solution.py:344
  29.7 8.4 %collective-permute-start.5 = (bf16[256,128]{1,0:T(8,128)(2,1)S(1)}, bf16[256,128]{1,0:T(8,128)(2,1)S(1)}, u32[]{:S(2)}, u32[]{:S(2)}) collective-permute-start(bf16[256,128]{1,0:T(8,128)(2,1)S(1)} %get-tuple-element.27.refs_4_), channel_id=1, source_target_pairs={{0,2},{1,3},{2,0},{3,1},{4,6},{5,7},{6,4},{7,5},{8,10},{9,11},{10,... | collective-permute-start | bytes 196616 | tf_op jit(solution)/shard_map/ppermute | solution.py:344
  32.6 6.4 %copy-start.7 = (s32[1,256]{1,0:T(1,128)S(1)}, s32[1,256]{1,0:T(1,128)}, u32[]{:S(2)}) copy-start(s32[1,256]{1,0:T(1,128)} %refs_12_.1) | copy-start | bytes 3076
  32.6 10.2 %collective-permute-start.11 = (f32[2,128,128]{2,1,0:T(8,128)S(1)}, f32[2,128,128]{2,1,0:T(8,128)S(1)}, u32[]{:S(2)}, u32[]{:S(2)}) collective-permute-start(f32[2,128,128]{2,1,0:T(8,128)S(1)} %get-tuple-element.34), channel_id=1, source_target_pairs={{0,4},{4,8},{8,12},{12,16},{16,20},{20,24},{24,28},{28,0},{1,5},{5... | collective-permute-start | bytes 393224 | tf_op jit(solution)/shard_map/ppermute | solution.py:28
  32.7 10.2 %collective-permute-start.12 = (f32[2,128,128]{2,1,0:T(8,128)S(1)}, f32[2,128,128]{2,1,0:T(8,128)S(1)}, u32[]{:S(2)}, u32[]{:S(2)}) collective-permute-start(f32[2,128,128]{2,1,0:T(8,128)S(1)} %get-tuple-element.35), channel_id=1, source_target_pairs={{0,28},{4,0},{8,4},{12,8},{16,12},{20,16},{24,20},{28,24},{1,29},{... | collective-permute-start | bytes 393224 | tf_op jit(solution)/shard_map/ppermute | solution.py:28
  38.0 1.4 %collective-permute-start.4 = (bf16[256,128]{1,0:T(8,128)(2,1)S(1)}, bf16[256,128]{1,0:T(8,128)(2,1)S(1)}, u32[]{:S(2)}, u32[]{:S(2)}) collective-permute-start(bf16[256,128]{1,0:T(8,128)(2,1)S(1)} %get-tuple-element.27.refs_4_), channel_id=1, source_target_pairs={{0,1},{1,0},{2,3},{3,2},{4,5},{5,4},{6,7},{7,6},{8,9},{9,8},{10,11... | collective-permute-start | bytes 196616 | tf_op jit(solution)/shard_map/ppermute | solution.py:344
  38.1 1.4 %collective-permute-start.6 = (bf16[256,128]{1,0:T(8,128)(2,1)S(1)}, bf16[256,128]{1,0:T(8,128)(2,1)S(1)}, u32[]{:S(2)}, u32[]{:S(2)}) collective-permute-start(bf16[256,128]{1,0:T(8,128)(2,1)S(1)} %collective-permute-done.5.refs_1_.refs_6_), channel_id=1, source_target_pairs={{0,1},{1,0},{2,3},{3,2},{4,5},{5,4},{6,7},{7,6},{8,9},{9,8},{10,11... | collective-permute-start | bytes 196616 | tf_op jit(solution)/shard_map/ppermute | solution.py:344
  38.6 4.3 %collective-permute-start.10 = (bf16[256,128]{1,0:T(8,128)(2,1)S(1)}, bf16[256,128]{1,0:T(8,128)(2,1)S(1)}, u32[]{:S(2)}, u32[]{:S(2)}) collective-permute-start(bf16[256,128]{1,0:T(8,128)(2,1)S(1)} %get-tuple-element.33.refs_8_), channel_id=1, source_target_pairs={{0,2},{1,3},{2,0},{3,1},{4,6},{5,7},{6,4},{7,5},{8,10},{9,11},{10,... | collective-permute-start | bytes 196616 | tf_op jit(solution)/shard_map/ppermute | solution.py:344
  44.9 5.3 %collective-permute-start.16 = (bf16[320,256]{1,0:T(8,128)(2,1)S(1)}, bf16[320,256]{1,0:T(8,128)(2,1)S(1)}, u32[]{:S(2)}, u32[]{:S(2)}) collective-permute-start(bf16[320,256]{1,0:T(8,128)(2,1)S(1)} %shard_map.145.refs_0_.refs_12_), channel_id=1, source_target_pairs={{0,2},{1,3},{2,0},{3,1},{4,6},{5,7},{6,4},{7,5},{8,10},{9,11},{10,... | collective-permute-start | bytes 491528 | tf_op jit(solution)/shard_map/ppermute | solution.py:344
  45.3 6.7 %collective-permute-start.15 = (bf16[320,256]{1,0:T(8,128)(2,1)S(1)}, bf16[320,256]{1,0:T(8,128)(2,1)S(1)}, u32[]{:S(2)}, u32[]{:S(2)}) collective-permute-start(bf16[320,256]{1,0:T(8,128)(2,1)S(1)} %shard_map.145.refs_0_.refs_12_), channel_id=1, source_target_pairs={{0,1},{1,0},{2,3},{3,2},{4,5},{5,4},{6,7},{7,6},{8,9},{9,8},{10,11... | collective-permute-start | bytes 491528 | tf_op jit(solution)/shard_map/ppermute | solution.py:344
  50.2 1.8 %collective-permute-start.17 = (bf16[320,256]{1,0:T(8,128)(2,1)S(1)}, bf16[320,256]{1,0:T(8,128)(2,1)S(1)}, u32[]{:S(2)}, u32[]{:S(2)}) collective-permute-start(bf16[320,256]{1,0:T(8,128)(2,1)S(1)} %collective-permute-done.16.refs_2_.refs_14_), channel_id=1, source_target_pairs={{0,1},{1,0},{2,3},{3,2},{4,5},{5,4},{6,7},{7,6},{8,9},{9,8},{10,11... | collective-permute-start | bytes 491528 | tf_op jit(solution)/shard_map/ppermute | solution.py:344
  50.2 1.5 %collective-permute-start.18 = (bf16[256,128]{1,0:T(8,128)(2,1)S(1)}, bf16[256,128]{1,0:T(8,128)(2,1)S(1)}, u32[]{:S(2)}, u32[]{:S(2)}) collective-permute-start(bf16[256,128]{1,0:T(8,128)(2,1)S(1)} %get-tuple-element.33.refs_8_), channel_id=1, source_target_pairs={{0,1},{1,0},{2,3},{3,2},{4,5},{5,4},{6,7},{7,6},{8,9},{9,8},{10,11... | collective-permute-start | bytes 196616 | tf_op jit(solution)/shard_map/ppermute | solution.py:344
  50.7 1.3 %collective-permute-start.19 = (bf16[256,128]{1,0:T(8,128)(2,1)S(1)}, bf16[256,128]{1,0:T(8,128)(2,1)S(1)}, u32[]{:S(2)}, u32[]{:S(2)}) collective-permute-start(bf16[256,128]{1,0:T(8,128)(2,1)S(1)} %collective-permute-done.10.refs_3_.refs_10_), channel_id=1, source_target_pairs={{0,1},{1,0},{2,3},{3,2},{4,5},{5,4},{6,7},{7,6},{8,9},{9,8},{10,11... | collective-permute-start | bytes 196616 | tf_op jit(solution)/shard_map/ppermute | solution.py:344
  54.8 6.9 %collective-permute-start.21 = (bf16[2,304,128]{2,1,0:T(8,128)(2,1)S(1)}, bf16[2,304,128]{2,1,0:T(8,128)(2,1)S(1)}, u32[]{:S(2)}, u32[]{:S(2)}) collective-permute-start(bf16[2,304,128]{2,1,0:T(8,128)(2,1)S(1)} %get-tuple-element.42), channel_id=1, source_target_pairs={{0,4},{4,0},{8,12},{12,8},{16,20},{20,16},{24,28},{28,24},{1,5},{5... | collective-permute-start | bytes 466952 | tf_op jit(solution)/shard_map/ppermute | solution.py:344
  54.9 9.4 %collective-permute-start.20 = (bf16[2,304,128]{2,1,0:T(8,128)(2,1)S(1)}, bf16[2,304,128]{2,1,0:T(8,128)(2,1)S(1)}, u32[]{:S(2)}, u32[]{:S(2)}) collective-permute-start(bf16[2,304,128]{2,1,0:T(8,128)(2,1)S(1)} %get-tuple-element.40), channel_id=1, source_target_pairs={{0,4},{4,0},{8,12},{12,8},{16,20},{20,16},{24,28},{28,24},{1,5},{5... | collective-permute-start | bytes 466952 | tf_op jit(solution)/shard_map/ppermute | solution.py:344
  61.8 6.5 %collective-permute-start.22 = (bf16[304,128]{1,0:T(8,128)(2,1)S(1)}, bf16[304,128]{1,0:T(8,128)(2,1)S(1)}, u32[]{:S(2)}, u32[]{:S(2)}) collective-permute-start(bf16[304,128]{1,0:T(8,128)(2,1)S(1)} %get-tuple-element.47), channel_id=1, source_target_pairs={{0,24},{4,28},{8,16},{12,20},{16,8},{20,12},{24,0},{28,4},{1,25},{... | collective-permute-start | bytes 233480 | tf_op jit(solution)/shard_map/ppermute | solution.py:344
  62.9 7.0 %collective-permute-start.23 = (bf16[304,128]{1,0:T(8,128)(2,1)S(1)}, bf16[304,128]{1,0:T(8,128)(2,1)S(1)}, u32[]{:S(2)}, u32[]{:S(2)}) collective-permute-start(bf16[304,128]{1,0:T(8,128)(2,1)S(1)} %get-tuple-element.48), channel_id=1, source_target_pairs={{0,16},{4,20},{8,24},{12,28},{16,0},{20,4},{24,8},{28,12},{1,17},{... | collective-permute-start | bytes 233480 | tf_op jit(solution)/shard_map/ppermute | solution.py:344
  64.3 6.0 %collective-permute-start.24 = (bf16[304,128]{1,0:T(8,128)(2,1)S(1)}, bf16[304,128]{1,0:T(8,128)(2,1)S(1)}, u32[]{:S(2)}, u32[]{:S(2)}) collective-permute-start(bf16[304,128]{1,0:T(8,128)(2,1)S(1)} %fusion), channel_id=1, source_target_pairs={{0,8},{4,12},{8,0},{12,4},{16,24},{20,28},{24,16},{28,20},{1,9},{5... | collective-permute-start | bytes 233480 | tf_op jit(solution)/shard_map/ppermute | solution.py:344
  70.4 5.1 %collective-permute-start.25 = (bf16[304,128]{1,0:T(8,128)(2,1)S(1)}, bf16[304,128]{1,0:T(8,128)(2,1)S(1)}, u32[]{:S(2)}, u32[]{:S(2)}) collective-permute-start(bf16[304,128]{1,0:T(8,128)(2,1)S(1)} %fusion.6.refs_0_), channel_id=1, source_target_pairs={{0,8},{4,12},{8,0},{12,4},{16,24},{20,28},{24,16},{28,20},{1,9},{5... | collective-permute-start | bytes 233480 | tf_op jit(solution)/shard_map/ppermute | solution.py:344
  70.8 8.8 %collective-permute-start.26 = (bf16[304,128]{1,0:T(8,128)(2,1)S(1)}, bf16[304,128]{1,0:T(8,128)(2,1)S(1)}, u32[]{:S(2)}, u32[]{:S(2)}) collective-permute-start(bf16[304,128]{1,0:T(8,128)(2,1)S(1)} %fusion.6.refs_0_), channel_id=1, source_target_pairs={{0,16},{4,20},{8,24},{12,28},{16,0},{20,4},{24,8},{28,12},{1,17},{... | collective-permute-start | bytes 233480 | tf_op jit(solution)/shard_map/ppermute | solution.py:344
  72.8 6.9 %collective-permute-start.27 = (bf16[304,128]{1,0:T(8,128)(2,1)S(1)}, bf16[304,128]{1,0:T(8,128)(2,1)S(1)}, u32[]{:S(2)}, u32[]{:S(2)}) collective-permute-start(bf16[304,128]{1,0:T(8,128)(2,1)S(1)} %fusion.6.refs_0_), channel_id=1, source_target_pairs={{0,24},{4,28},{8,16},{12,20},{16,8},{20,12},{24,0},{28,4},{1,25},{... | collective-permute-start | bytes 233480 | tf_op jit(solution)/shard_map/ppermute | solution.py:344
  74.8 7.6 %collective-permute-start.28 = (bf16[304,128]{1,0:T(8,128)(2,1)S(1)}, bf16[304,128]{1,0:T(8,128)(2,1)S(1)}, u32[]{:S(2)}, u32[]{:S(2)}) collective-permute-start(bf16[304,128]{1,0:T(8,128)(2,1)S(1)} %fusion.6.refs_0_), channel_id=1, source_target_pairs={{0,4},{4,0},{8,12},{12,8},{16,20},{20,16},{24,28},{28,24},{1,5},{5... | collective-permute-start | bytes 233480 | tf_op jit(solution)/shard_map/ppermute | solution.py:344
  75.5 7.0 %collective-permute-start.29 = (bf16[304,128]{1,0:T(8,128)(2,1)S(1)}, bf16[304,128]{1,0:T(8,128)(2,1)S(1)}, u32[]{:S(2)}, u32[]{:S(2)}) collective-permute-start(bf16[304,128]{1,0:T(8,128)(2,1)S(1)} %collective-permute-done.25.refs_1_), channel_id=1, source_target_pairs={{0,4},{4,0},{8,12},{12,8},{16,20},{20,16},{24,28},{28,24},{1,5},{5... | collective-permute-start | bytes 233480 | tf_op jit(solution)/shard_map/ppermute | solution.py:344
  79.6 4.4 %collective-permute-start.30 = (bf16[304,128]{1,0:T(8,128)(2,1)S(1)}, bf16[304,128]{1,0:T(8,128)(2,1)S(1)}, u32[]{:S(2)}, u32[]{:S(2)}) collective-permute-start(bf16[304,128]{1,0:T(8,128)(2,1)S(1)} %collective-permute-done.26.refs_2_), channel_id=1, source_target_pairs={{0,4},{4,0},{8,12},{12,8},{16,20},{20,16},{24,28},{28,24},{1,5},{5... | collective-permute-start | bytes 233480 | tf_op jit(solution)/shard_map/ppermute | solution.py:344
  79.6 5.2 %collective-permute-start.31 = (bf16[304,128]{1,0:T(8,128)(2,1)S(1)}, bf16[304,128]{1,0:T(8,128)(2,1)S(1)}, u32[]{:S(2)}, u32[]{:S(2)}) collective-permute-start(bf16[304,128]{1,0:T(8,128)(2,1)S(1)} %collective-permute-done.27.refs_3_), channel_id=1, source_target_pairs={{0,4},{4,0},{8,12},{12,8},{16,20},{20,16},{24,28},{28,24},{1,5},{5... | collective-permute-start | bytes 233480 | tf_op jit(solution)/shard_map/ppermute | solution.py:344

commit v5 on v4

--- a/solution.py
+++ b/solution.py
@@ -11,9 +11,11 @@
 HOPS = 3
 LANES = 128
 VMEM_LIMIT = 24 * 1024 * 1024
+VMEM_ALL = 56 * 1024 * 1024
 
 IN_VMEM = pl.BlockSpec(memory_space=pltpu.VMEM)
 IN_SMEM = pl.BlockSpec(memory_space=pltpu.SMEM)
+ANYWHERE = pl.BlockSpec(memory_space=pl.ANY)
 BF16 = jnp.bfloat16
 F32 = jnp.float32
 
@@ -34,7 +36,7 @@
     )
 
 
-def call(kernel, out_shape, in_specs, flops, scratch=(), after=()):
+def call(kernel, out_shape, in_specs, flops, scratch=(), after=(), limit=VMEM_LIMIT):
     many = isinstance(out_shape, (list, tuple))
     outs = out_shape if many else [out_shape]
     moved = sum(math.prod(one.shape) * one.dtype.itemsize for one in outs)
@@ -46,10 +48,10 @@
     made = pl.pallas_call(
         run,
         out_shape=out_shape,
-        in_specs=[pl.BlockSpec(memory_space=pl.ANY)] * waited + in_specs,
+        in_specs=[ANYWHERE] * waited + in_specs,
         out_specs=[IN_VMEM] * len(outs) if many else IN_VMEM,
         scratch_shapes=list(scratch),
-        compiler_params=pltpu.CompilerParams(vmem_limit_bytes=VMEM_LIMIT),
+        compiler_params=pltpu.CompilerParams(vmem_limit_bytes=limit),
         cost_estimate=pl.CostEstimate(
             flops=flops, bytes_accessed=3 * moved, transcendentals=0
         ),
@@ -69,14 +71,42 @@
         self.sent = self.right + slots
 
 
-def write_sends(plan, plan_ref, blocks, left_ref, right_ref):
-    for slot in range(plan.slots):
-        for out_ref, ids, side in ((left_ref, plan.left, 0), (right_ref, plan.right, 1)):
-            index = plan_ref[ids + slot]
+def write_sends(blocks, left_ref, right_ref, left_ids, right_ids, counts):
+    for slot in range(left_ref.shape[0]):
+        for out_ref, ids, side in ((left_ref, left_ids, 0), (right_ref, right_ids, 1)):
+            index = ids(slot)
             picked = blocks[0]
             for number in range(1, len(blocks)):
                 picked = jnp.where(index == number, blocks[number], picked)
-            out_ref[slot] = jnp.where(slot < plan_ref[plan.sent + side], picked, 0.0)
+            out_ref[slot] = jnp.where(slot < counts(side), picked, 0.0)
+
+
+def copied(sources, targets, sems):
+    copies = [
+        pltpu.make_async_copy(source, target, sems.at[number])
+        for number, (source, target) in enumerate(zip(sources, targets))
+    ]
+    for copy in copies:
+        copy.start()
+    for copy in copies:
+        copy.wait()
+
+
+def first_kernel(
+    sl_ref, sr_ref, sc_ref, feat_ref, left_ref, right_ref, held_ref,
+    sl_here, sr_here, sc_here, sems,
+):
+    copied(
+        (sl_ref, sr_ref, sc_ref, feat_ref), (sl_here, sr_here, sc_here, held_ref), sems
+    )
+    write_sends(
+        [held_ref[number] for number in range(held_ref.shape[0])],
+        left_ref,
+        right_ref,
+        lambda slot: sl_here[slot],
+        lambda slot: sr_here[slot],
+        lambda side: sc_here[0, side],
+    )
 
 
 def next_blocks(plan, plan_ref, cur_ref, tiles_ref, ext_ref):
@@ -105,24 +135,16 @@
 
 def write_hop(plan, plan_ref, cur_ref, tiles_ref, next_ref, left_ref, right_ref, ext_ref):
     blocks = next_blocks(plan, plan_ref, cur_ref, tiles_ref, ext_ref)
-    write_sends(plan, plan_ref, blocks, left_ref, right_ref)
+    write_sends(
+        blocks,
+        left_ref,
+        right_ref,
+        lambda slot: plan_ref[plan.left + slot],
+        lambda slot: plan_ref[plan.right + slot],
+        lambda side: plan_ref[plan.sent + side],
+    )
     for number, block in enumerate(blocks):
         next_ref[number] = block
-
-
-def first_hop_kernel(
-    plan, plan_ref, low_plan_ref, high_plan_ref, cur_ref, low_ref, high_ref, tiles_ref,
-    next_ref, left_ref, right_ref, ext_ref,
-):
-    local = cur_ref.shape[0]
-    for slot in range(plan.slots):
-        low = low_ref[low_plan_ref[plan.right + slot]]
-        high = high_ref[high_plan_ref[plan.left + slot]]
-        live_low = slot < low_plan_ref[plan.sent + 1]
-        live_high = slot < high_plan_ref[plan.sent]
-        ext_ref[local + slot] = jnp.where(live_low, low, 0.0)
-        ext_ref[local + plan.slots + slot] = jnp.where(live_high, high, 0.0)
-    write_hop(plan, plan_ref, cur_ref, tiles_ref, next_ref, left_ref, right_ref, ext_ref)
 
 
 def hop_kernel(
@@ -148,7 +170,7 @@
     refs[-1][...] = rows
 
 
-def forward_first_kernel(cur_ref, w_ref, wc_ref, label_ref, tiles_ref, part_ref, b_ref):
+def forward_first_kernel(cur_ref, w_ref, wc_ref, tiles_ref, label_ref, part_ref, b_ref):
     nodes = label_ref.shape[1]
     forward_kernel(0, cur_ref, w_ref, wc_ref, part_ref, b_ref.at[:nodes])
     width = b_ref.shape[1]
@@ -224,7 +246,10 @@
     rows_b = jnp.concatenate(halves, axis=0)
     size, width = halves[0].shape
     for number, half in enumerate(halves):
-        out_ref[:size, number * width : (number + 1) * width] = half
+        columns = slice(number * width, (number + 1) * width)
+        out_ref[:size, columns] = half
+        out_ref[size : 2 * size, columns] = cur_ref[number].astype(BF16)
+    size = 2 * size
     logits = before_ref[...] + branch_logits(w_ref.shape[0] - 1, rows_b, w_ref, wc_ref)
     classes, rows = logits.shape
     kept = up_to(classes, 16)
@@ -262,19 +287,22 @@
 def all_chunks(kept, row_refs, last_refs, w_ref, wt_ref, wct_ref, chunks_ref):
     group = len(last_refs)
     branches, own, width = wt_ref.shape
-    nodes = row_refs[-1].shape[0]
+    nodes = last_refs[0].shape[1]
     hid = w_ref.shape[2]
     parts = last_refs[0].shape[1] // width
     size = nodes // parts
     all_rows = []
-    for branch in range(branches - 1):
+    for branch in range(branches - 2):
         ours = row_refs[branch * group : (branch + 1) * group]
         all_rows.append(jnp.concatenate([ref[:nodes] for ref in ours], axis=0))
-    last_rows = []
-    for ref in last_refs:
-        for part in range(parts):
-            last_rows.append(ref[:size, part * width : (part + 1) * width])
-    all_rows.append(jnp.concatenate(last_rows, axis=0))
+    for place in (1, 0):
+        last_rows = []
+        for ref in last_refs:
+            for part in range(parts):
+                columns = slice(part * width, (part + 1) * width)
+                last_rows.append(ref[place * size : (place + 1) * size, columns])
+        all_rows.append(jnp.concatenate(last_rows, axis=0))
+    size = 2 * size
     dlogits_t = jnp.concatenate([ref[size : size + kept] for ref in last_refs], axis=1)
     own_class = branches * own
     first = lax.axis_index("shuf") * own_class
@@ -395,38 +423,47 @@
     hop_flops = 12 * tiles * block * block * width
     forward_flops = 2 * nodes * hid * (width + classes)
     ext = pltpu.VMEM((local + 2 * slots, block, width), F32)
-    to_left = to_right = current
+    to_left, to_right, current = call(
+        first_kernel,
+        [slots_f32, slots_f32, blocks_f32],
+        [ANYWHERE] * 4,
+        1000,
+        [
+            pltpu.SMEM((slots,), jnp.int32),
+            pltpu.SMEM((slots,), jnp.int32),
+            pltpu.SMEM((1, 2), jnp.int32),
+            pltpu.SemaphoreType.DMA((4,)),
+        ],
+        limit=VMEM_ALL,
+    )(send_left, send_right, send_count, current)
     for hop in range(HOPS):
         from_lower = passed_along(to_right, "dom", 1)
         from_upper = passed_along(to_left, "dom", -1)
         if hop == 0:
             logits, rows = call(
                 forward_first_kernel, [logits_f32, first_b16], [IN_VMEM] * 5, forward_flops
-            )(current, w_branch, w_class_t, labels.reshape(1, nodes), tile_values)
+            )(current, w_branch, w_class_t, tile_values, labels.reshape(1, nodes))
+            gathered.append(in_group(rows))
         else:
             logits, rows = call(
                 functools.partial(forward_kernel, hop),
                 [logits_f32, rows_b16],
                 [IN_VMEM] * 4,
                 forward_flops,
+                (),
+                [members[shuf // 2] for members in gathered] if hop == 2 else [],
             )(current, w_branch, w_class_t, logits)
-        gathered.append(in_group(rows))
+            if hop < HOPS - 1:
+                gathered.append(in_group(rows))
         if hop < HOPS - 1:
-            out_shape = [blocks_f32, slots_f32, slots_f32]
-            if hop == 0:
-                kernel = first_hop_kernel
-                plans = (small, passed_along(small, "dom", 1), passed_along(small, "dom", -1))
-            else:
-                kernel = hop_kernel
-                plans = (small,)
             current, to_left, to_right = call(
-                functools.partial(kernel, plan),
-                out_shape,
-                [IN_SMEM] * len(plans) + [IN_VMEM] * 4,
+                functools.partial(hop_kernel, plan),
+                [blocks_f32, slots_f32, slots_f32],
+                [IN_SMEM] + [IN_VMEM] * 4,
                 hop_flops,
                 [ext],
-                [logits] + [members[shuf // 2] for members in gathered[:hop]],
-            )(*plans, current, from_lower, from_upper, tile_values)
+                [logits],
+            )(small, current, from_lower, from_upper, tile_values)
 
     label_mine = call(
         label_kernel,
@@ -448,11 +485,11 @@
 
     payload = call(
         functools.partial(last_kernel, plan, row_scale),
-        jax.ShapeDtypeStruct((block + kept + 16, local * width), BF16),
+        jax.ShapeDtypeStruct((2 * block + kept + 16, local * width), BF16),
         [IN_SMEM] + [IN_VMEM] * 9,
         hop_flops + forward_flops,
         [ext],
-        [*gathered[1][1:], gathered[2][shuf // 2]],
+        gathered[1][1:],
     )(
         small, current, from_lower, from_upper, tile_values,
         logits, w_branch, w_class_t, batch_order, label_mine,

time: 86.3 us -> 79 us (0.915)
  starting transfers between devices: 39.4 us -> 34.4 us
  waiting for transfers between devices: 27.4 us -> 22.9 us
  Pallas kernels: 11.7 us -> 13.8 us
    ppermute x24 -> x21, waiting for transfers between devices: 27.4 us -> 21.8 us  [swapped(): return lax.ppermute(value, axis, pairs)]
    ppermute x8 -> x6, starting transfers between devices: 20.4 us -> 15.7 us  [passed_along(): return lax.ppermute(value, axis, pairs)]
    pallas_call x2 -> x3, Pallas kernels: 2.43 us -> 4.09 us  [the longest x2 2.39 us: body(): call(functools.partial(hop_kernel, plan), [blocks_f32, slots_f32, slots_f...]
    ppermute x8 -> x6, waiting for transfers between devices: 0.02 us -> 1.06 us  [passed_along(): return lax.ppermute(value, axis, pairs)]
    ppermute x24 -> x21, starting transfers between devices: 19 us -> 18.8 us  [swapped(): return lax.ppermute(value, axis, pairs)]
  transfers between devices with their start and end apart: 32 -> 27, of which waited for: 14 -> 14; matrix products, arithmetic and copies ran while one was open for 1% -> 1% of each run, Pallas kernels for 5% -> 6%
where the time goes in v5:
time: 79 us; the launch traced here: 78.7 us
  starting transfers between devices  34.4 us (44%)
  waiting for transfers between devices  22.9 us (29%)
  Pallas kernels  13.8 us (17%)
  local copies, waits for them, and re-layouts  6.03 us (8%)
  between operations  1.44 us (2%)
    ppermute x21, waiting for transfers between devices, swapped(): return lax.ppermute(value, axis, pairs)  21.8 us
    ppermute x21, starting transfers between devices, swapped(): return lax.ppermute(value, axis, pairs)  18.8 us
    ppermute x6, starting transfers between devices, passed_along(): return lax.ppermute(value, axis, pairs)  15.7 us
    unnamed x18, local copies, waits for them, and re-layouts  5.23 us
    pallas_call x1, Pallas kernels, body(): call(functools.partial(grad_kernel, kept, shuf, len(gathered), half), [on...  2.79 us
    pallas_call x2, Pallas kernels, body(): call(functools.partial(hop_kernel, plan), [blocks_f32, slots_f32, slots_f...  2.39 us
    pallas_call x1, Pallas kernels, body(): call(functools.partial(last_kernel, plan, row_scale), jax.ShapeDtypeStruc...  1.99 us
    pallas_call x1, Pallas kernels, body(): call(first_kernel, [slots_f32, slots_f32, blocks_f32], [ANYWHERE] * 4, 10...  1.7 us
  transfers between devices with their start and end apart: 27, of which 14 were waited for; matrix products, arithmetic and copies ran while one was open for 1% of the time, Pallas kernels for 6%

profile of v5, /device:TPU:0, one launch (start us, length us, event | category | flops | bytes accessed | tf_op | source)
XLA Modules:
  0.0 78.7 jit_solution(7441126177477190988)
XLA Ops:
  0.6 1.7 %shard_map.139 = (f32[2,128,128]{2,1,0:T(8,128)}, f32[2,128,128]{2,1,0:T(8,128)}, f32[2,128,128]{2,1,0:T(8,128)}) custom-call(s32[2]{0:T(128)} %refs_0_.3, s32[2]{0:T(128)} %refs_1_.3, s32[1,2]{1,0:T(1,128)} %refs_2_.1, f32[2,128,128]{2,1,0:T(8,128)} %bitcast.32), custom_call_target="tpu_custom_call" | custom-call | flops 1000 | bytes 1179648 | tf_op jit(solution)/shard_map/pallas_call | solution.py:426
  2.3 3.0 %collective-permute-start = (f32[2,128,128]{2,1,0:T(8,128)}, f32[2,128,128]{2,1,0:T(8,128)S(1)}, u32[]{:S(2)}, u32[]{:S(2)}) collective-permute-start(f32[2,128,128]{2,1,0:T(8,128)} %get-tuple-element.29), channel_id=1, source_target_pairs={{0,4},{4,8},{8,12},{12,16},{16,20},{20,24},{24,28},{28,0},{1,5},{5... | collective-permute-start | bytes 393224 | tf_op jit(solution)/shard_map/ppermute | solution.py:30
  5.4 3.1 %collective-permute-start.1 = (f32[2,128,128]{2,1,0:T(8,128)}, f32[2,128,128]{2,1,0:T(8,128)S(1)}, u32[]{:S(2)}, u32[]{:S(2)}) collective-permute-start(f32[2,128,128]{2,1,0:T(8,128)} %get-tuple-element.30), channel_id=1, source_target_pairs={{0,28},{4,0},{8,4},{12,8},{16,12},{20,16},{24,20},{28,24},{1,29},{... | collective-permute-start | bytes 393224 | tf_op jit(solution)/shard_map/ppermute | solution.py:30
  9.1 0.8 %concatenate.3.refs_1_.refs_3_ = s32[23]{0:T(128)S(1)} concatenate(s32[8]{0:T(128)} %param.14, s32[8]{0:T(128)} %param.15, s32[1]{0:T(128)S(6)} %copy.15, s32[2]{0:T(128)} %refs_0_.3, s32[2]{0:T(128)} %refs_1_.3, s32[2]{0:T(128)} %bitcast.33), dimensions={0} | concatenate | bytes 184 | tf_op jit(solution)/shard_map/concatenate | solution.py:410
  9.9 1.4 %copy-done = bf16[4096,172]{0,1:T(8,128)(2,1)S(1)} copy-done((bf16[4096,172]{0,1:T(8,128)(2,1)S(1)}, bf16[4096,172]{0,1:T(8,128)(2,1)}, u32[]{:S(2)}) %copy-start) | copy-done | bytes 1409048
  11.3 1.2 %copy-done.2 = bf16[4,128,1024]{2,1,0:T(8,128)(2,1)S(1)} copy-done((bf16[4,128,1024]{2,1,0:T(8,128)(2,1)S(1)}, bf16[4,128,1024]{2,1,0:T(8,128)(2,1)}, u32[]{:S(2)}) %copy-start.2) | copy-done | bytes 1048600
  12.5 1.0 %copy-done.4 = f32[8,128,128]{2,1,0:T(8,128)S(1)} copy-done((f32[8,128,128]{2,1,0:T(8,128)S(1)}, f32[8,128,128]{2,1,0:T(8,128)}, u32[]{:S(2)}) %copy-start.4) | copy-done | bytes 524312
  13.5 0.9 %copy-done.6 = f32[2,128,128]{2,1,0:T(8,128)S(1)} copy-done((f32[2,128,128]{2,1,0:T(8,128)S(1)}, f32[2,128,128]{2,1,0:T(8,128)}, u32[]{:S(2)}) %copy-start.6) | copy-done | bytes 131096
  14.5 0.7 copy-done.8
  15.1 0.6 shard_map.140
  15.7 0.0 collective-permute-done.refs_3_
  15.8 1.2 %shard_map.141 = (f32[2,128,128]{2,1,0:T(8,128)S(1)}, f32[2,128,128]{2,1,0:T(8,128)S(1)}, f32[2,128,128]{2,1,0:T(8,128)S(1)}) custom-call(f32[172,256]{1,0:T(8,128)S(1)} %get-tuple-element.28.refs_0_.refs_3_, s32[23]{0:T(128)S(1)} %concatenate.3.refs_1_.refs_3_, f32[2,128,128]{2,1,0:T(8,128)S(1)} %copy-done.6, ...), custom_call_target="tpu_custom_call" | custom-call | flops 201326592 | bytes 1179648 | tf_op jit(solution)/shard_map/pallas_call | solution.py:459
  17.0 0.0 copy-start.5
  17.0 0.1 collective-permute-start.5
  17.0 4.7 %collective-permute-start.6 = (f32[2,128,128]{2,1,0:T(8,128)S(1)}, f32[2,128,128]{2,1,0:T(8,128)S(1)}, u32[]{:S(2)}, u32[]{:S(2)}) collective-permute-start(f32[2,128,128]{2,1,0:T(8,128)S(1)} %get-tuple-element.35), channel_id=1, source_target_pairs={{0,28},{4,0},{8,4},{12,8},{16,12},{20,16},{24,20},{28,24},{1,29},{... | collective-permute-start | bytes 393224 | tf_op jit(solution)/shard_map/ppermute | solution.py:30
  21.7 1.6 %collective-permute-start.9 = (bf16[272,128]{1,0:T(8,128)(2,1)S(1)}, bf16[272,128]{1,0:T(8,128)(2,1)S(1)}, u32[]{:S(2)}, u32[]{:S(2)}) collective-permute-start(bf16[272,128]{1,0:T(8,128)(2,1)S(1)} %get-tuple-element.39.refs_1_.refs_0_), channel_id=1, source_target_pairs={{0,2},{1,3},{2,0},{3,1},{4,6},{5,7},{6,4},{7,5},{8,10},{9,11},{10,... | collective-permute-start | bytes 208904 | tf_op jit(solution)/shard_map/ppermute | solution.py:372
  23.3 0.0 collective-permute-start.10
  23.4 0.0 copy-start.7
  23.4 0.6 shard_map.142
  24.0 0.5 collective-permute-start.3
  24.5 0.3 collective-permute-done.5.refs_3_
  24.8 0.1 collective-permute-done.6.refs_4_
  24.9 1.2 %shard_map.143 = (f32[2,128,128]{2,1,0:T(8,128)S(1)}, f32[2,128,128]{2,1,0:T(8,128)S(1)}, f32[2,128,128]{2,1,0:T(8,128)S(1)}) custom-call(f32[172,256]{1,0:T(8,128)S(1)} %get-tuple-element.33.refs_0_.refs_5_, s32[23]{0:T(128)S(1)} %concatenate.3.refs_1_.refs_3_, f32[2,128,128]{2,1,0:T(8,128)S(1)} %get-tuple-element.31.refs_0_.refs_2_, ...), custom_call_target="tpu_custom_call" | custom-call | flops 201326592 | bytes 1179648 | tf_op jit(solution)/shard_map/pallas_call | solution.py:459
  26.1 0.3 collective-permute-start.7
  26.3 4.5 %collective-permute-start.8 = (f32[2,128,128]{2,1,0:T(8,128)S(1)}, f32[2,128,128]{2,1,0:T(8,128)S(1)}, u32[]{:S(2)}, u32[]{:S(2)}) collective-permute-start(f32[2,128,128]{2,1,0:T(8,128)S(1)} %get-tuple-element.38), channel_id=1, source_target_pairs={{0,28},{4,0},{8,4},{12,8},{16,12},{20,16},{24,20},{28,24},{1,29},{... | collective-permute-start | bytes 393224 | tf_op jit(solution)/shard_map/ppermute | solution.py:30
  30.8 0.0 collective-permute-start.11
  30.9 0.0 collective-permute-done.10.refs_2_.refs_1_
  30.9 0.5 collective-permute-start.2
  31.4 0.1 collective-permute-start.4
  31.4 0.7 collective-permute-done.11.refs_4_.refs_3_
  32.1 0.4 shard_map.145.refs_12_
  32.5 1.1 %shard_map.144 = (f32[172,256]{1,0:T(8,128)S(1)}, bf16[256,128]{1,0:T(8,128)(2,1)}) custom-call(bf16[272,128]{1,0:T(8,128)(2,1)S(1)} %collective-permute-done.9.refs_0_.refs_3_.refs_2_, bf16[256,128]{1,0:T(8,128)(2,1)S(1)} %collective-permute-done.3.refs_1_.refs_6_, f32[2,128,128]{2,1,0:T(8,128)S(1)} %get-tuple-element.36.refs_2_.refs_4_, ...), custom_call_target="tpu_custom_call" | custom-call | flops 157286400 | bytes 724992 | tf_op jit(solution)/shard_map/pallas_call | solution.py:448
  33.6 0.6 collective-permute-done.7.refs_5_
  34.2 0.1 collective-permute-done.8.refs_6_
  34.2 2.0 %shard_map.146.refs_0_.refs_8_ = bf16[448,256]{1,0:T(8,128)(2,1)S(1)} custom-call(bf16[256,128]{1,0:T(8,128)(2,1)S(1)} %collective-permute-done.2.refs_0_.refs_5_, bf16[256,128]{1,0:T(8,128)(2,1)S(1)} %collective-permute-done.3.refs_1_.refs_6_, bf16[256,128]{1,0:T(8,128)(2,1)S(1)} %collective-permute-done.4.refs_2_.refs_7_, ...), custom_call_target="tpu_custom_call" | custom-call | flops 358612992 | bytes 688128 | tf_op jit(solution)/shard_map/pallas_call | solution.py:486
  36.2 1.6 %collective-permute-start.13 = (bf16[448,256]{1,0:T(8,128)(2,1)S(1)}, bf16[448,256]{1,0:T(8,128)(2,1)S(1)}, u32[]{:S(2)}, u32[]{:S(2)}) collective-permute-start(bf16[448,256]{1,0:T(8,128)(2,1)S(1)} %shard_map.146.refs_0_.refs_8_), channel_id=1, source_target_pairs={{0,2},{1,3},{2,0},{3,1},{4,6},{5,7},{6,4},{7,5},{8,10},{9,11},{10,... | collective-permute-start | bytes 688136 | tf_op jit(solution)/shard_map/ppermute | solution.py:372
  37.8 0.0 collective-permute-start.12
  37.8 5.4 %collective-permute-done.13.refs_2_.refs_10_ = bf16[448,256]{1,0:T(8,128)(2,1)S(1)} collective-permute-done((bf16[448,256]{1,0:T(8,128)(2,1)S(1)}, bf16[448,256]{1,0:T(8,128)(2,1)S(1)}, u32[]{:S(2)}, u32[]{:S(2)}) %collective-permute-start.13) | collective-permute-done | bytes 229408 | tf_op jit(solution)/shard_map/ppermute | solution.py:372
  43.3 0.0 collective-permute-start.14
  43.3 0.3 shard_map.148
  43.5 0.0 collective-permute-done.12.refs_1_.refs_9_
  43.6 1.2 %collective-permute-done.14.refs_3_.refs_11_ = bf16[448,256]{1,0:T(8,128)(2,1)S(1)} collective-permute-done((bf16[448,256]{1,0:T(8,128)(2,1)S(1)}, bf16[448,256]{1,0:T(8,128)(2,1)S(1)}, u32[]{:S(2)}, u32[]{:S(2)}) %collective-permute-start.14) | collective-permute-done | bytes 229408 | tf_op jit(solution)/shard_map/ppermute | solution.py:372
  44.7 2.8 %shard_map.149 = (f32[304,128]{1,0:T(8,128)S(1)}, f32[304,128]{1,0:T(8,128)S(1)}, f32[304,128]{1,0:T(8,128)S(1)}, f32[304,128]{1,0:T(8,128)S(1)}, bf16[2,304,128...) custom-call(bf16[272,128]{1,0:T(8,128)(2,1)S(1)} %get-tuple-element.39.refs_1_.refs_0_, ...), custom_call_target="tpu_custom_call" | custom-call | flops 1543503872 | bytes 2801664 | tf_op jit(solution)/shard_map/pallas_call | solution.py:516
  47.5 0.1 collective-permute-start.16
  47.6 2.0 %collective-permute-start.15 = (bf16[2,304,128]{2,1,0:T(8,128)(2,1)S(1)}, bf16[2,304,128]{2,1,0:T(8,128)(2,1)S(1)}, u32[]{:S(2)}, u32[]{:S(2)}) collective-permute-start(bf16[2,304,128]{2,1,0:T(8,128)(2,1)S(1)} %get-tuple-element.44), channel_id=1, source_target_pairs={{0,4},{4,0},{8,12},{12,8},{16,20},{20,16},{24,28},{28,24},{1,5},{5... | collective-permute-start | bytes 466952 | tf_op jit(solution)/shard_map/ppermute | solution.py:372
  49.6 4.8 %collective-permute-done.16 = bf16[2,304,128]{2,1,0:T(8,128)(2,1)S(1)} collective-permute-done((bf16[2,304,128]{2,1,0:T(8,128)(2,1)S(1)}, bf16[2,304,128]{2,1,0:T(8,128)(2,1)S(1)}, u32[]{:S(2)}, u32[]{:S(2)}) %collective-permute-start.16) | collective-permute-done | bytes 155680 | tf_op jit(solution)/shard_map/ppermute | solution.py:372
  54.5 3.7 %collective-permute-start.17 = (bf16[304,128]{1,0:T(8,128)(2,1)S(1)}, bf16[304,128]{1,0:T(8,128)(2,1)S(1)}, u32[]{:S(2)}, u32[]{:S(2)}) collective-permute-start(bf16[304,128]{1,0:T(8,128)(2,1)S(1)} %get-tuple-element.51), channel_id=1, source_target_pairs={{0,24},{4,28},{8,16},{12,20},{16,8},{20,12},{24,0},{28,4},{1,25},{... | collective-permute-start | bytes 233480 | tf_op jit(solution)/shard_map/ppermute | solution.py:372
  58.2 0.8 %collective-permute-start.19 = (bf16[304,128]{1,0:T(8,128)(2,1)S(1)}, bf16[304,128]{1,0:T(8,128)(2,1)S(1)}, u32[]{:S(2)}, u32[]{:S(2)}) collective-permute-start(bf16[304,128]{1,0:T(8,128)(2,1)S(1)} %fusion), channel_id=1, source_target_pairs={{0,8},{4,12},{8,0},{12,4},{16,24},{20,28},{24,16},{28,20},{1,9},{5... | collective-permute-start | bytes 233480 | tf_op jit(solution)/shard_map/ppermute | solution.py:372
  59.1 1.7 %collective-permute-done.17 = bf16[304,128]{1,0:T(8,128)(2,1)S(1)} collective-permute-done((bf16[304,128]{1,0:T(8,128)(2,1)S(1)}, bf16[304,128]{1,0:T(8,128)(2,1)S(1)}, u32[]{:S(2)}, u32[]{:S(2)}) %collective-permute-start.17) | collective-permute-done | bytes 77856 | tf_op jit(solution)/shard_map/ppermute | solution.py:372
  60.8 3.2 %collective-permute-done.18 = bf16[304,128]{1,0:T(8,128)(2,1)S(1)} collective-permute-done((bf16[304,128]{1,0:T(8,128)(2,1)S(1)}, bf16[304,128]{1,0:T(8,128)(2,1)S(1)}, u32[]{:S(2)}, u32[]{:S(2)}) %collective-permute-start.18) | collective-permute-done | bytes 77856 | tf_op jit(solution)/shard_map/ppermute | solution.py:372
  64.0 0.1 fusion.6.refs_0_
  64.1 0.4 collective-permute-start.20
  64.5 2.3 %collective-permute-start.21 = (bf16[304,128]{1,0:T(8,128)(2,1)S(1)}, bf16[304,128]{1,0:T(8,128)(2,1)S(1)}, u32[]{:S(2)}, u32[]{:S(2)}) collective-permute-start(bf16[304,128]{1,0:T(8,128)(2,1)S(1)} %fusion.6.refs_0_), channel_id=1, source_target_pairs={{0,16},{4,20},{8,24},{12,28},{16,0},{20,4},{24,8},{28,12},{1,17},{... | collective-permute-start | bytes 233480 | tf_op jit(solution)/shard_map/ppermute | solution.py:372
  66.8 1.7 %collective-permute-start.22 = (bf16[304,128]{1,0:T(8,128)(2,1)S(1)}, bf16[304,128]{1,0:T(8,128)(2,1)S(1)}, u32[]{:S(2)}, u32[]{:S(2)}) collective-permute-start(bf16[304,128]{1,0:T(8,128)(2,1)S(1)} %fusion.6.refs_0_), channel_id=1, source_target_pairs={{0,24},{4,28},{8,16},{12,20},{16,8},{20,12},{24,0},{28,4},{1,25},{... | collective-permute-start | bytes 233480 | tf_op jit(solution)/shard_map/ppermute | solution.py:372
  68.6 0.3 collective-permute-start.23
  68.8 1.7 %collective-permute-start.24 = (bf16[304,128]{1,0:T(8,128)(2,1)S(1)}, bf16[304,128]{1,0:T(8,128)(2,1)S(1)}, u32[]{:S(2)}, u32[]{:S(2)}) collective-permute-start(bf16[304,128]{1,0:T(8,128)(2,1)S(1)} %collective-permute-done.20.refs_1_), channel_id=1, source_target_pairs={{0,4},{4,0},{8,12},{12,8},{16,20},{20,16},{24,28},{28,24},{1,5},{5... | collective-permute-start | bytes 233480 | tf_op jit(solution)/shard_map/ppermute | solution.py:372
  70.6 1.5 %collective-permute-done.21.refs_2_ = bf16[304,128]{1,0:T(8,128)(2,1)S(1)} collective-permute-done((bf16[304,128]{1,0:T(8,128)(2,1)S(1)}, bf16[304,128]{1,0:T(8,128)(2,1)S(1)}, u32[]{:S(2)}, u32[]{:S(2)}) %collective-permute-start.21) | collective-permute-done | bytes 77856 | tf_op jit(solution)/shard_map/ppermute | solution.py:372
  72.1 0.4 collective-permute-start.25
  72.5 0.6 collective-permute-done.22.refs_3_
  73.1 1.0 %collective-permute-start.26 = (bf16[304,128]{1,0:T(8,128)(2,1)S(1)}, bf16[304,128]{1,0:T(8,128)(2,1)S(1)}, u32[]{:S(2)}, u32[]{:S(2)}) collective-permute-start(bf16[304,128]{1,0:T(8,128)(2,1)S(1)} %collective-permute-done.22.refs_3_), channel_id=1, source_target_pairs={{0,4},{4,0},{8,12},{12,8},{16,20},{20,16},{24,28},{28,24},{1,5},{5... | collective-permute-start | bytes 233480 | tf_op jit(solution)/shard_map/ppermute | solution.py:372
  74.1 0.8 %shard_map.147 = f32[1,256]{1,0:T(1,128)} custom-call(bf16[448,256]{1,0:T(8,128)(2,1)S(1)} %shard_map.146.refs_0_.refs_8_, bf16[448,256]{1,0:T(8,128)(2,1)S(1)} %collective-permute-done.12.refs_1_.refs_9_, bf16[448,256]{1,0:T(8,128)(2,1)S(1)} %collective-permute-done.13.refs_2_.refs_10_, bf16[448,256]{1,0:T(8,128)(2,1)S(1)} %collective-permute-done.14.refs_3_.refs_11_), custom_call_target="tpu_custom_call" | custom-call | flops 1000 | bytes 3072 | tf_op jit(solution)/shard_map/pallas_call | solution.py:499
  74.9 1.5 %collective-permute-done.25.refs_6_ = bf16[304,128]{1,0:T(8,128)(2,1)S(1)} collective-permute-done((bf16[304,128]{1,0:T(8,128)(2,1)S(1)}, bf16[304,128]{1,0:T(8,128)(2,1)S(1)}, u32[]{:S(2)}, u32[]{:S(2)}) %collective-permute-start.25) | collective-permute-done | bytes 77856 | tf_op jit(solution)/shard_map/ppermute | solution.py:372
  76.5 1.0 %collective-permute-done.26.refs_7_ = bf16[304,128]{1,0:T(8,128)(2,1)S(1)} collective-permute-done((bf16[304,128]{1,0:T(8,128)(2,1)S(1)}, bf16[304,128]{1,0:T(8,128)(2,1)S(1)}, u32[]{:S(2)}, u32[]{:S(2)}) %collective-permute-start.26) | collective-permute-done | bytes 77856 | tf_op jit(solution)/shard_map/ppermute | solution.py:372
  77.5 1.2 %shard_map.150 = (f32[4,128,256]{2,1,0:T(8,128)}, f32[172,1024]{1,0:T(8,128)}) custom-call(bf16[304,128]{1,0:T(8,128)(2,1)S(1)} %fusion.6.refs_0_, bf16[304,128]{1,0:T(8,128)(2,1)S(1)} %collective-permute-done.20.refs_1_, bf16[304,128]{1,0:T(8,128)(2,1)S(1)} %collective-permute-done.21.refs_2_, bf16[304,128]{1,0:T(8,128)(2,1)S(1)} %collective-permute-done.22.refs_3_, ...), custom_call_target="tpu_custom_call" | custom-call | flops 1000 | bytes 3686400 | tf_op jit(solution)/shard_map/pallas_call | solution.py:540
  (24 shorter events, 0.1 us)
Async XLA Ops:
  2.3 13.4 %collective-permute-start = (f32[2,128,128]{2,1,0:T(8,128)}, f32[2,128,128]{2,1,0:T(8,128)S(1)}, u32[]{:S(2)}, u32[]{:S(2)}) collective-permute-start(f32[2,128,128]{2,1,0:T(8,128)} %get-tuple-element.29), channel_id=1, source_target_pairs={{0,4},{4,8},{8,12},{12,16},{16,20},{20,24},{24,28},{28,0},{1,5},{5... | collective-permute-start | bytes 393224 | tf_op jit(solution)/shard_map/ppermute | solution.py:30
  5.4 10.4 %collective-permute-start.1 = (f32[2,128,128]{2,1,0:T(8,128)}, f32[2,128,128]{2,1,0:T(8,128)S(1)}, u32[]{:S(2)}, u32[]{:S(2)}) collective-permute-start(f32[2,128,128]{2,1,0:T(8,128)} %get-tuple-element.30), channel_id=1, source_target_pairs={{0,28},{4,0},{8,4},{12,8},{16,12},{20,16},{24,20},{28,24},{1,29},{... | collective-permute-start | bytes 393224 | tf_op jit(solution)/shard_map/ppermute | solution.py:30
  9.9 1.4 %copy-start = (bf16[4096,172]{0,1:T(8,128)(2,1)S(1)}, bf16[4096,172]{0,1:T(8,128)(2,1)}, u32[]{:S(2)}) copy-start(bf16[4096,172]{0,1:T(8,128)(2,1)} %param.23) | copy-start | bytes 4227076
  11.3 1.2 %copy-start.2 = (bf16[4,128,1024]{2,1,0:T(8,128)(2,1)S(1)}, bf16[4,128,1024]{2,1,0:T(8,128)(2,1)}, u32[]{:S(2)}) copy-start(bf16[4,128,1024]{2,1,0:T(8,128)(2,1)} %refs_12_.1) | copy-start | bytes 3145732
  12.5 1.0 %copy-start.4 = (f32[8,128,128]{2,1,0:T(8,128)S(1)}, f32[8,128,128]{2,1,0:T(8,128)}, u32[]{:S(2)}) copy-start(f32[8,128,128]{2,1,0:T(8,128)} %refs_7_.1) | copy-start | bytes 1572868
  13.5 0.9 %copy-start.6 = (f32[2,128,128]{2,1,0:T(8,128)S(1)}, f32[2,128,128]{2,1,0:T(8,128)}, u32[]{:S(2)}) copy-start(f32[2,128,128]{2,1,0:T(8,128)} %get-tuple-element.27.refs_0_.refs_2_) | copy-start | bytes 393220
  14.5 0.7 copy-start.8
  15.1 8.2 %copy-start.1 = (bf16[4096,172]{0,1:T(8,128)(2,1)S(1)}, bf16[4096,172]{0,1:T(8,128)(2,1)}, u32[]{:S(2)}) copy-start(bf16[4096,172]{0,1:T(8,128)(2,1)} %param.23) | copy-start | bytes 4227076
  15.1 8.2 %copy-start.3 = (bf16[4,128,1024]{2,1,0:T(8,128)(2,1)S(1)}, bf16[4,128,1024]{2,1,0:T(8,128)(2,1)}, u32[]{:S(2)}) copy-start(bf16[4,128,1024]{2,1,0:T(8,128)(2,1)} %refs_12_.1) | copy-start | bytes 3145732
  17.0 7.9 %copy-start.5 = (f32[8,128,128]{2,1,0:T(8,128)S(1)}, f32[8,128,128]{2,1,0:T(8,128)}, u32[]{:S(2)}) copy-start(f32[8,128,128]{2,1,0:T(8,128)} %refs_7_.1) | copy-start | bytes 1572868
  17.0 7.8 %collective-permute-start.5 = (f32[2,128,128]{2,1,0:T(8,128)S(1)}, f32[2,128,128]{2,1,0:T(8,128)S(1)}, u32[]{:S(2)}, u32[]{:S(2)}) collective-permute-start(f32[2,128,128]{2,1,0:T(8,128)S(1)} %get-tuple-element.34), channel_id=1, source_target_pairs={{0,4},{4,8},{8,12},{12,16},{16,20},{20,24},{24,28},{28,0},{1,5},{5... | collective-permute-start | bytes 393224 | tf_op jit(solution)/shard_map/ppermute | solution.py:30
  17.0 7.8 %collective-permute-start.6 = (f32[2,128,128]{2,1,0:T(8,128)S(1)}, f32[2,128,128]{2,1,0:T(8,128)S(1)}, u32[]{:S(2)}, u32[]{:S(2)}) collective-permute-start(f32[2,128,128]{2,1,0:T(8,128)S(1)} %get-tuple-element.35), channel_id=1, source_target_pairs={{0,28},{4,0},{8,4},{12,8},{16,12},{20,16},{24,20},{28,24},{1,29},{... | collective-permute-start | bytes 393224 | tf_op jit(solution)/shard_map/ppermute | solution.py:30
  21.7 9.1 %collective-permute-start.9 = (bf16[272,128]{1,0:T(8,128)(2,1)S(1)}, bf16[272,128]{1,0:T(8,128)(2,1)S(1)}, u32[]{:S(2)}, u32[]{:S(2)}) collective-permute-start(bf16[272,128]{1,0:T(8,128)(2,1)S(1)} %get-tuple-element.39.refs_1_.refs_0_), channel_id=1, source_target_pairs={{0,2},{1,3},{2,0},{3,1},{4,6},{5,7},{6,4},{7,5},{8,10},{9,11},{10,... | collective-permute-start | bytes 208904 | tf_op jit(solution)/shard_map/ppermute | solution.py:372
  23.3 7.5 %collective-permute-start.10 = (bf16[272,128]{1,0:T(8,128)(2,1)S(1)}, bf16[272,128]{1,0:T(8,128)(2,1)S(1)}, u32[]{:S(2)}, u32[]{:S(2)}) collective-permute-start(bf16[272,128]{1,0:T(8,128)(2,1)S(1)} %get-tuple-element.39.refs_1_.refs_0_), channel_id=1, source_target_pairs={{0,1},{1,0},{2,3},{3,2},{4,5},{5,4},{6,7},{7,6},{8,9},{9,8},{10,11... | collective-permute-start | bytes 208904 | tf_op jit(solution)/shard_map/ppermute | solution.py:372
  23.4 8.8 %copy-start.7 = (s32[1,256]{1,0:T(1,128)S(1)}, s32[1,256]{1,0:T(1,128)}, u32[]{:S(2)}) copy-start(s32[1,256]{1,0:T(1,128)} %refs_11_.1) | copy-start | bytes 3076
  24.0 7.4 %collective-permute-start.3 = (bf16[256,128]{1,0:T(8,128)(2,1)S(1)}, bf16[256,128]{1,0:T(8,128)(2,1)S(1)}, u32[]{:S(2)}, u32[]{:S(2)}) collective-permute-start(bf16[256,128]{1,0:T(8,128)(2,1)S(1)} %get-tuple-element.32.refs_4_), channel_id=1, source_target_pairs={{0,2},{1,3},{2,0},{3,1},{4,6},{5,7},{6,4},{7,5},{8,10},{9,11},{10,... | collective-permute-start | bytes 196616 | tf_op jit(solution)/shard_map/ppermute | solution.py:372
  26.1 8.1 %collective-permute-start.7 = (f32[2,128,128]{2,1,0:T(8,128)S(1)}, f32[2,128,128]{2,1,0:T(8,128)S(1)}, u32[]{:S(2)}, u32[]{:S(2)}) collective-permute-start(f32[2,128,128]{2,1,0:T(8,128)S(1)} %get-tuple-element.37), channel_id=1, source_target_pairs={{0,4},{4,8},{8,12},{12,16},{16,20},{20,24},{24,28},{28,0},{1,5},{5... | collective-permute-start | bytes 393224 | tf_op jit(solution)/shard_map/ppermute | solution.py:30
  26.3 7.9 %collective-permute-start.8 = (f32[2,128,128]{2,1,0:T(8,128)S(1)}, f32[2,128,128]{2,1,0:T(8,128)S(1)}, u32[]{:S(2)}, u32[]{:S(2)}) collective-permute-start(f32[2,128,128]{2,1,0:T(8,128)S(1)} %get-tuple-element.38), channel_id=1, source_target_pairs={{0,28},{4,0},{8,4},{12,8},{16,12},{20,16},{24,20},{28,24},{1,29},{... | collective-permute-start | bytes 393224 | tf_op jit(solution)/shard_map/ppermute | solution.py:30
  30.8 1.3 %collective-permute-start.11 = (bf16[272,128]{1,0:T(8,128)(2,1)S(1)}, bf16[272,128]{1,0:T(8,128)(2,1)S(1)}, u32[]{:S(2)}, u32[]{:S(2)}) collective-permute-start(bf16[272,128]{1,0:T(8,128)(2,1)S(1)} %collective-permute-done.9.refs_0_.refs_3_.refs_2_), channel_id=1, source_target_pairs={{0,1},{1,0},{2,3},{3,2},{4,5},{5,4},{6,7},{7,6},{8,9},{9,8},{10,11... | collective-permute-start | bytes 208904 | tf_op jit(solution)/shard_map/ppermute | solution.py:372
  30.9 2.7 %collective-permute-start.2 = (bf16[256,128]{1,0:T(8,128)(2,1)S(1)}, bf16[256,128]{1,0:T(8,128)(2,1)S(1)}, u32[]{:S(2)}, u32[]{:S(2)}) collective-permute-start(bf16[256,128]{1,0:T(8,128)(2,1)S(1)} %get-tuple-element.32.refs_4_), channel_id=1, source_target_pairs={{0,1},{1,0},{2,3},{3,2},{4,5},{5,4},{6,7},{7,6},{8,9},{9,8},{10,11... | collective-permute-start | bytes 196616 | tf_op jit(solution)/shard_map/ppermute | solution.py:372
  31.4 2.2 %collective-permute-start.4 = (bf16[256,128]{1,0:T(8,128)(2,1)S(1)}, bf16[256,128]{1,0:T(8,128)(2,1)S(1)}, u32[]{:S(2)}, u32[]{:S(2)}) collective-permute-start(bf16[256,128]{1,0:T(8,128)(2,1)S(1)} %collective-permute-done.3.refs_1_.refs_6_), channel_id=1, source_target_pairs={{0,1},{1,0},{2,3},{3,2},{4,5},{5,4},{6,7},{7,6},{8,9},{9,8},{10,11... | collective-permute-start | bytes 196616 | tf_op jit(solution)/shard_map/ppermute | solution.py:372
  36.2 7.0 %collective-permute-start.13 = (bf16[448,256]{1,0:T(8,128)(2,1)S(1)}, bf16[448,256]{1,0:T(8,128)(2,1)S(1)}, u32[]{:S(2)}, u32[]{:S(2)}) collective-permute-start(bf16[448,256]{1,0:T(8,128)(2,1)S(1)} %shard_map.146.refs_0_.refs_8_), channel_id=1, source_target_pairs={{0,2},{1,3},{2,0},{3,1},{4,6},{5,7},{6,4},{7,5},{8,10},{9,11},{10,... | collective-permute-start | bytes 688136 | tf_op jit(solution)/shard_map/ppermute | solution.py:372
  37.8 5.7 %collective-permute-start.12 = (bf16[448,256]{1,0:T(8,128)(2,1)S(1)}, bf16[448,256]{1,0:T(8,128)(2,1)S(1)}, u32[]{:S(2)}, u32[]{:S(2)}) collective-permute-start(bf16[448,256]{1,0:T(8,128)(2,1)S(1)} %shard_map.146.refs_0_.refs_8_), channel_id=1, source_target_pairs={{0,1},{1,0},{2,3},{3,2},{4,5},{5,4},{6,7},{7,6},{8,9},{9,8},{10,11... | collective-permute-start | bytes 688136 | tf_op jit(solution)/shard_map/ppermute | solution.py:372
  43.3 1.5 %collective-permute-start.14 = (bf16[448,256]{1,0:T(8,128)(2,1)S(1)}, bf16[448,256]{1,0:T(8,128)(2,1)S(1)}, u32[]{:S(2)}, u32[]{:S(2)}) collective-permute-start(bf16[448,256]{1,0:T(8,128)(2,1)S(1)} %collective-permute-done.13.refs_2_.refs_10_), channel_id=1, source_target_pairs={{0,1},{1,0},{2,3},{3,2},{4,5},{5,4},{6,7},{7,6},{8,9},{9,8},{10,11... | collective-permute-start | bytes 688136 | tf_op jit(solution)/shard_map/ppermute | solution.py:372
  47.5 6.9 %collective-permute-start.16 = (bf16[2,304,128]{2,1,0:T(8,128)(2,1)S(1)}, bf16[2,304,128]{2,1,0:T(8,128)(2,1)S(1)}, u32[]{:S(2)}, u32[]{:S(2)}) collective-permute-start(bf16[2,304,128]{2,1,0:T(8,128)(2,1)S(1)} %get-tuple-element.46), channel_id=1, source_target_pairs={{0,4},{4,0},{8,12},{12,8},{16,20},{20,16},{24,28},{28,24},{1,5},{5... | collective-permute-start | bytes 466952 | tf_op jit(solution)/shard_map/ppermute | solution.py:372
  47.6 10.6 %collective-permute-start.15 = (bf16[2,304,128]{2,1,0:T(8,128)(2,1)S(1)}, bf16[2,304,128]{2,1,0:T(8,128)(2,1)S(1)}, u32[]{:S(2)}, u32[]{:S(2)}) collective-permute-start(bf16[2,304,128]{2,1,0:T(8,128)(2,1)S(1)} %get-tuple-element.44), channel_id=1, source_target_pairs={{0,4},{4,0},{8,12},{12,8},{16,20},{20,16},{24,28},{28,24},{1,5},{5... | collective-permute-start | bytes 466952 | tf_op jit(solution)/shard_map/ppermute | solution.py:372
  54.5 6.3 %collective-permute-start.17 = (bf16[304,128]{1,0:T(8,128)(2,1)S(1)}, bf16[304,128]{1,0:T(8,128)(2,1)S(1)}, u32[]{:S(2)}, u32[]{:S(2)}) collective-permute-start(bf16[304,128]{1,0:T(8,128)(2,1)S(1)} %get-tuple-element.51), channel_id=1, source_target_pairs={{0,24},{4,28},{8,16},{12,20},{16,8},{20,12},{24,0},{28,4},{1,25},{... | collective-permute-start | bytes 233480 | tf_op jit(solution)/shard_map/ppermute | solution.py:372
  58.2 5.8 %collective-permute-start.18 = (bf16[304,128]{1,0:T(8,128)(2,1)S(1)}, bf16[304,128]{1,0:T(8,128)(2,1)S(1)}, u32[]{:S(2)}, u32[]{:S(2)}) collective-permute-start(bf16[304,128]{1,0:T(8,128)(2,1)S(1)} %get-tuple-element.52), channel_id=1, source_target_pairs={{0,16},{4,20},{8,24},{12,28},{16,0},{20,4},{24,8},{28,12},{1,17},{... | collective-permute-start | bytes 233480 | tf_op jit(solution)/shard_map/ppermute | solution.py:372
  58.2 5.8 %collective-permute-start.19 = (bf16[304,128]{1,0:T(8,128)(2,1)S(1)}, bf16[304,128]{1,0:T(8,128)(2,1)S(1)}, u32[]{:S(2)}, u32[]{:S(2)}) collective-permute-start(bf16[304,128]{1,0:T(8,128)(2,1)S(1)} %fusion), channel_id=1, source_target_pairs={{0,8},{4,12},{8,0},{12,4},{16,24},{20,28},{24,16},{28,20},{1,9},{5... | collective-permute-start | bytes 233480 | tf_op jit(solution)/shard_map/ppermute | solution.py:372
  64.1 4.7 %collective-permute-start.20 = (bf16[304,128]{1,0:T(8,128)(2,1)S(1)}, bf16[304,128]{1,0:T(8,128)(2,1)S(1)}, u32[]{:S(2)}, u32[]{:S(2)}) collective-permute-start(bf16[304,128]{1,0:T(8,128)(2,1)S(1)} %fusion.6.refs_0_), channel_id=1, source_target_pairs={{0,8},{4,12},{8,0},{12,4},{16,24},{20,28},{24,16},{28,20},{1,9},{5... | collective-permute-start | bytes 233480 | tf_op jit(solution)/shard_map/ppermute | solution.py:372
  64.5 7.6 %collective-permute-start.21 = (bf16[304,128]{1,0:T(8,128)(2,1)S(1)}, bf16[304,128]{1,0:T(8,128)(2,1)S(1)}, u32[]{:S(2)}, u32[]{:S(2)}) collective-permute-start(bf16[304,128]{1,0:T(8,128)(2,1)S(1)} %fusion.6.refs_0_), channel_id=1, source_target_pairs={{0,16},{4,20},{8,24},{12,28},{16,0},{20,4},{24,8},{28,12},{1,17},{... | collective-permute-start | bytes 233480 | tf_op jit(solution)/shard_map/ppermute | solution.py:372
  66.8 6.3 %collective-permute-start.22 = (bf16[304,128]{1,0:T(8,128)(2,1)S(1)}, bf16[304,128]{1,0:T(8,128)(2,1)S(1)}, u32[]{:S(2)}, u32[]{:S(2)}) collective-permute-start(bf16[304,128]{1,0:T(8,128)(2,1)S(1)} %fusion.6.refs_0_), channel_id=1, source_target_pairs={{0,24},{4,28},{8,16},{12,20},{16,8},{20,12},{24,0},{28,4},{1,25},{... | collective-permute-start | bytes 233480 | tf_op jit(solution)/shard_map/ppermute | solution.py:372
  68.6 6.4 %collective-permute-start.23 = (bf16[304,128]{1,0:T(8,128)(2,1)S(1)}, bf16[304,128]{1,0:T(8,128)(2,1)S(1)}, u32[]{:S(2)}, u32[]{:S(2)}) collective-permute-start(bf16[304,128]{1,0:T(8,128)(2,1)S(1)} %fusion.6.refs_0_), channel_id=1, source_target_pairs={{0,4},{4,0},{8,12},{12,8},{16,20},{20,16},{24,28},{28,24},{1,5},{5... | collective-permute-start | bytes 233480 | tf_op jit(solution)/shard_map/ppermute | solution.py:372
  68.8 6.1 %collective-permute-start.24 = (bf16[304,128]{1,0:T(8,128)(2,1)S(1)}, bf16[304,128]{1,0:T(8,128)(2,1)S(1)}, u32[]{:S(2)}, u32[]{:S(2)}) collective-permute-start(bf16[304,128]{1,0:T(8,128)(2,1)S(1)} %collective-permute-done.20.refs_1_), channel_id=1, source_target_pairs={{0,4},{4,0},{8,12},{12,8},{16,20},{20,16},{24,28},{28,24},{1,5},{5... | collective-permute-start | bytes 233480 | tf_op jit(solution)/shard_map/ppermute | solution.py:372
  72.1 4.4 %collective-permute-start.25 = (bf16[304,128]{1,0:T(8,128)(2,1)S(1)}, bf16[304,128]{1,0:T(8,128)(2,1)S(1)}, u32[]{:S(2)}, u32[]{:S(2)}) collective-permute-start(bf16[304,128]{1,0:T(8,128)(2,1)S(1)} %collective-permute-done.21.refs_2_), channel_id=1, source_target_pairs={{0,4},{4,0},{8,12},{12,8},{16,20},{20,16},{24,28},{28,24},{1,5},{5... | collective-permute-start | bytes 233480 | tf_op jit(solution)/shard_map/ppermute | solution.py:372
  73.1 4.4 %collective-permute-start.26 = (bf16[304,128]{1,0:T(8,128)(2,1)S(1)}, bf16[304,128]{1,0:T(8,128)(2,1)S(1)}, u32[]{:S(2)}, u32[]{:S(2)}) collective-permute-start(bf16[304,128]{1,0:T(8,128)(2,1)S(1)} %collective-permute-done.22.refs_3_), channel_id=1, source_target_pairs={{0,4},{4,0},{8,12},{12,8},{16,20},{20,16},{24,28},{28,24},{1,5},{5... | collective-permute-start | bytes 233480 | tf_op jit(solution)/shard_map/ppermute | solution.py:372

commit v6 on v5

--- a/solution.py
+++ b/solution.py
@@ -24,9 +24,18 @@
     return -(-value // multiple) * multiple
 
 
-def passed_along(value, axis, steps):
-    count = lax.axis_size(axis)
-    pairs = [(source, (source + steps) % count) for source in range(count)]
+def near_pairs(value):
+    return swapped(value, 1)
+
+
+def far_pairs(value):
+    count = lax.axis_size("dom")
+    pairs = [(d, (d + 1 if d % 2 else d - 1) % count) for d in range(count)]
+    return lax.ppermute(value, "dom", pairs)
+
+
+def swapped(value, distance, axis="dom"):
+    pairs = [(source, source ^ distance) for source in range(lax.axis_size(axis))]
     return lax.ppermute(value, axis, pairs)
 
 
@@ -71,10 +80,11 @@
         self.sent = self.right + slots
 
 
-def write_sends(blocks, left_ref, right_ref, left_ids, right_ids, counts):
-    for slot in range(left_ref.shape[0]):
-        for out_ref, ids, side in ((left_ref, left_ids, 0), (right_ref, right_ids, 1)):
-            index = ids(slot)
+def write_sends(blocks, far_ref, near_ref, ids, counts):
+    odd = lax.axis_index("dom") % 2
+    for slot in range(far_ref.shape[0]):
+        for out_ref, side in ((far_ref, odd), (near_ref, 1 - odd)):
+            index = ids(side, slot)
             picked = blocks[0]
             for number in range(1, len(blocks)):
                 picked = jnp.where(index == number, blocks[number], picked)
@@ -93,20 +103,45 @@
 
 
 def first_kernel(
-    sl_ref, sr_ref, sc_ref, feat_ref, left_ref, right_ref, held_ref,
-    sl_here, sr_here, sc_here, sems,
+    sl_ref, sr_ref, sc_ref, feat_ref, label_from,
+    far_ref, near_ref, held_ref, b_ref,
+    sl_here, sr_here, sc_here, label_ref, sems,
 ):
     copied(
-        (sl_ref, sr_ref, sc_ref, feat_ref), (sl_here, sr_here, sc_here, held_ref), sems
-    )
+        (sl_ref, sr_ref, sc_ref, feat_ref, label_from),
+        (sl_here, sr_here, sc_here, held_ref, label_ref),
+        sems,
+    )
+    blocks = [held_ref[number] for number in range(held_ref.shape[0])]
     write_sends(
-        [held_ref[number] for number in range(held_ref.shape[0])],
-        left_ref,
-        right_ref,
-        lambda slot: sl_here[slot],
-        lambda slot: sr_here[slot],
+        blocks,
+        far_ref,
+        near_ref,
+        lambda side, slot: jnp.where(side == 0, sl_here[slot], sr_here[slot]),
         lambda side: sc_here[0, side],
     )
+    write_rows(blocks, b_ref)
+    nodes = label_ref.shape[1]
+    width = b_ref.shape[1]
+    per_piece = nodes // width
+    place = lax.broadcasted_iota(jnp.int32, (16, width), 0)
+    packed = jnp.zeros((16, width), F32)
+    for piece in range(2):
+        value = label_ref[...] & 255 if piece == 0 else label_ref[...] >> 8
+        value = value.astype(F32)
+        for part in range(per_piece):
+            packed = jnp.where(
+                place == piece * per_piece + part,
+                value[:, part * width : (part + 1) * width],
+                packed,
+            )
+    b_ref[nodes:] = packed.astype(BF16)
+
+
+def write_rows(blocks, b_ref):
+    for number, block in enumerate(blocks):
+        size = block.shape[0]
+        b_ref[number * size : (number + 1) * size] = block.astype(BF16)
 
 
 def next_blocks(plan, plan_ref, cur_ref, tiles_ref, ext_ref):
@@ -126,33 +161,35 @@
     return totals
 
 
-def extend(cur_ref, low_ref, high_ref, ext_ref):
+def extend(cur_ref, far_ref, near_ref, ext_ref):
     local = cur_ref.shape[0]
-    slots = low_ref.shape[0]
-    ext_ref[local : local + slots] = low_ref[...]
-    ext_ref[local + slots :] = high_ref[...]
-
-
-def write_hop(plan, plan_ref, cur_ref, tiles_ref, next_ref, left_ref, right_ref, ext_ref):
+    slots = far_ref.shape[0]
+    odd = lax.axis_index("dom") % 2
+    ext_ref[pl.ds(local + odd * slots, slots)] = far_ref[...]
+    ext_ref[pl.ds(local + (1 - odd) * slots, slots)] = near_ref[...]
+
+
+def hop_kernel(
+    plan, plan_ref, cur_ref, far_in_ref, near_in_ref, tiles_ref,
+    next_ref, far_ref, near_ref, b_ref, ext_ref,
+):
+    extend(cur_ref, far_in_ref, near_in_ref, ext_ref)
     blocks = next_blocks(plan, plan_ref, cur_ref, tiles_ref, ext_ref)
     write_sends(
         blocks,
-        left_ref,
-        right_ref,
-        lambda slot: plan_ref[plan.left + slot],
-        lambda slot: plan_ref[plan.right + slot],
+        far_ref,
+        near_ref,
+        lambda side, slot: plan_ref[plan.left + side * plan.slots + slot],
         lambda side: plan_ref[plan.sent + side],
     )
     for number, block in enumerate(blocks):
         next_ref[number] = block
-
-
-def hop_kernel(
-    plan, plan_ref, cur_ref, low_ref, high_ref, tiles_ref,
-    next_ref, left_ref, right_ref, ext_ref,
-):
-    extend(cur_ref, low_ref, high_ref, ext_ref)
-    write_hop(plan, plan_ref, cur_ref, tiles_ref, next_ref, left_ref, right_ref, ext_ref)
+    write_rows(blocks, b_ref)
+
+
+def ready_kernel(cur_ref, tiles_ref, cur_out, tiles_out):
+    cur_out[...] = cur_ref[...]
+    tiles_out[...] = tiles_ref[...]
 
 
 def branch_logits(branch, rows, w_ref, wc_ref):
@@ -164,29 +201,9 @@
 def forward_kernel(branch, cur_ref, w_ref, wc_ref, *refs):
     rows = cur_ref[...].reshape(-1, cur_ref.shape[2]).astype(BF16)
     part = branch_logits(branch, rows, w_ref, wc_ref)
-    if len(refs) == 3:
+    if len(refs) == 2:
         part = refs[0][...] + part
-    refs[-2][...] = part
-    refs[-1][...] = rows
-
-
-def forward_first_kernel(cur_ref, w_ref, wc_ref, tiles_ref, label_ref, part_ref, b_ref):
-    nodes = label_ref.shape[1]
-    forward_kernel(0, cur_ref, w_ref, wc_ref, part_ref, b_ref.at[:nodes])
-    width = b_ref.shape[1]
-    per_piece = nodes // width
-    place = lax.broadcasted_iota(jnp.int32, (16, width), 0)
-    packed = jnp.zeros((16, width), F32)
-    for piece in range(2):
-        value = label_ref[...] & 255 if piece == 0 else label_ref[...] >> 8
-        value = value.astype(F32)
-        for part in range(per_piece):
-            packed = jnp.where(
-                place == piece * per_piece + part,
-                value[:, part * width : (part + 1) * width],
-                packed,
-            )
-    b_ref[nodes:] = packed.astype(BF16)
+    refs[-1][...] = part
 
 
 def places(order_ref):
@@ -237,10 +254,10 @@
 
 def last_kernel(
     plan, row_scale, plan_ref,
-    cur_ref, low_ref, high_ref, tiles_ref, before_ref, w_ref, wc_ref, order_ref, label_ref,
+    cur_ref, far_ref, near_ref, tiles_ref, before_ref, w_ref, wc_ref, order_ref, label_ref,
     out_ref, ext_ref,
 ):
-    extend(cur_ref, low_ref, high_ref, ext_ref)
+    extend(cur_ref, far_ref, near_ref, ext_ref)
     blocks = next_blocks(plan, plan_ref, cur_ref, tiles_ref, ext_ref)
     halves = [block.astype(BF16) for block in blocks]
     rows_b = jnp.concatenate(halves, axis=0)
@@ -284,8 +301,8 @@
         wct_ref[branch] = pad_ref[...].T[:, :kept].astype(BF16)
 
 
-def all_chunks(kept, row_refs, last_refs, w_ref, wt_ref, wct_ref, chunks_ref):
-    group = len(last_refs)
+def add_chunks(kept, more, row_refs, last_refs, w_ref, wt_ref, wct_ref, chunks_ref):
+    members = len(last_refs)
     branches, own, width = wt_ref.shape
     nodes = last_refs[0].shape[1]
     hid = w_ref.shape[2]
@@ -293,7 +310,7 @@
     size = nodes // parts
     all_rows = []
     for branch in range(branches - 2):
-        ours = row_refs[branch * group : (branch + 1) * group]
+        ours = row_refs[branch * members : (branch + 1) * members]
         all_rows.append(jnp.concatenate([ref[:nodes] for ref in ours], axis=0))
     for place in (1, 0):
         last_rows = []
@@ -311,26 +328,45 @@
     chosen = all_rows[0]
     for branch in range(1, branches):
         chosen = jnp.where(which == branch, all_rows[branch], chosen)
+
+    def put(chunk, rows, value):
+        chunks_ref[chunk, rows] = chunks_ref[chunk, rows] + value if more else value
+
     hidden = jnp.maximum(matmul(chosen, w_ref[which, :, columns]), 0.0).astype(BF16)
     class_t = matmul(dlogits_t, hidden)
     for chunk in range(chunks_ref.shape[0]):
-        chunks_ref[chunk, :kept] = class_t[:, chunk * LANES : (chunk + 1) * LANES]
+        put(chunk, slice(0, kept), class_t[:, chunk * LANES : (chunk + 1) * LANES])
     per_branch = chunks_ref.shape[0] // branches
     for branch, rows in enumerate(all_rows):
         live = matmul(wt_ref[branch], rows, ((1,), (1,))) > 0.0
         dhidden_t = jnp.where(live, matmul(wct_ref[branch], dlogits_t), 0.0).astype(BF16)
         branch_t = matmul(dhidden_t, rows)
         for part in range(per_branch):
-            chunks_ref[branch * per_branch + part, kept:] = branch_t[
-                part * LANES : (part + 1) * LANES
-            ]
-
-
-def grad_kernel(kept, group, row_count, half, *refs):
-    ins = row_count + group + 3
+            put(
+                branch * per_branch + part,
+                slice(kept, kept + width),
+                branch_t[part * LANES : (part + 1) * LANES],
+            )
+
+
+def early_kernel(kept, members, *refs):
+    last = len(refs) - 4 - members
+    add_chunks(kept, False, refs[:last], refs[last : last + members], *refs[last + members :])
+
+
+def late_chunks(kept, members, early_ref, refs, chunks_ref):
+    last = len(refs) - 3 - members
+    chunks_ref[...] = early_ref[...]
+    add_chunks(
+        kept, True, refs[:last], refs[last : last + members], *refs[last + members :], chunks_ref
+    )
+
+
+def late_kernel(kept, members, half, early_ref, *refs):
+    ins = len(refs) - 1 - half - half // 2
     outs = refs[ins:-1]
     chunks_ref = refs[-1]
-    plain_grad_kernel(kept, group, row_count, *refs[:ins], chunks_ref)
+    late_chunks(kept, members, early_ref, refs[:ins], chunks_ref)
     dom = lax.axis_index("dom")
     for step in range(half):
         stays = dom ^ (2 * step)
@@ -338,9 +374,8 @@
         outs[half + step // 2][step % 2] = chunks_ref[stays ^ 1].astype(BF16)
 
 
-def plain_grad_kernel(kept, group, row_count, *refs):
-    last = row_count + group
-    all_chunks(kept, refs[:row_count], refs[row_count:last], *refs[last:])
+def plain_late_kernel(kept, members, early_ref, *refs):
+    late_chunks(kept, members, early_ref, refs[:-1], refs[-1])
 
 
 def write_chunk(kept, chunk, value, branch_ref, class_ref):
@@ -367,24 +402,15 @@
         write_chunk(kept, chunk, in_ref[chunk], branch_ref, class_ref)
 
 
-def swapped(value, distance, axis="dom"):
-    pairs = [(source, source ^ distance) for source in range(lax.axis_size(axis))]
-    return lax.ppermute(value, axis, pairs)
-
-
-def in_group(value):
+def in_group(value, distance=None):
     members = [value]
-    distance = lax.axis_size("shuf") // 2
+    steps = [0]
+    distance = lax.axis_size("shuf") // 2 if distance is None else distance
     while distance:
         members += [swapped(member, distance, "shuf") for member in members]
-        distance //= 2
-    count = len(members)
-    steps = [0]
-    distance = count // 2
-    while distance:
         steps += [step + distance for step in steps]
         distance //= 2
-    return [members[steps.index(step)] for step in range(count)]
+    return [members[steps.index(step)] for step in range(len(steps))]
 
 
 def body(
@@ -423,47 +449,53 @@
     hop_flops = 12 * tiles * block * block * width
     forward_flops = 2 * nodes * hid * (width + classes)
     ext = pltpu.VMEM((local + 2 * slots, block, width), F32)
-    to_left, to_right, current = call(
+    to_far, to_near, current, rows = call(
         first_kernel,
-        [slots_f32, slots_f32, blocks_f32],
-        [ANYWHERE] * 4,
+        [slots_f32, slots_f32, blocks_f32, first_b16],
+        [ANYWHERE] * 5,
         1000,
         [
             pltpu.SMEM((slots,), jnp.int32),
             pltpu.SMEM((slots,), jnp.int32),
             pltpu.SMEM((1, 2), jnp.int32),
-            pltpu.SemaphoreType.DMA((4,)),
+            pltpu.VMEM((1, nodes), jnp.int32),
+            pltpu.SemaphoreType.DMA((5,)),
         ],
         limit=VMEM_ALL,
-    )(send_left, send_right, send_count, current)
+    )(send_left, send_right, send_count, current, labels.reshape(1, nodes))
+    current, tile_values = call(
+        ready_kernel,
+        [blocks_f32, jax.ShapeDtypeStruct(tile_values.shape, F32)],
+        [IN_VMEM] * 2,
+        1000,
+    )(current, tile_values)
     for hop in range(HOPS):
-        from_lower = passed_along(to_right, "dom", 1)
-        from_upper = passed_along(to_left, "dom", -1)
+        from_far = far_pairs(to_far)
+        from_near = near_pairs(to_near)
+        if hop < HOPS - 1:
+            gathered.append(in_group(rows))
+        before = [] if logits is None else [logits]
+        logits = call(
+            functools.partial(forward_kernel, hop),
+            logits_f32,
+            [IN_VMEM] * (3 + len(before)),
+            forward_flops,
+            after=[members[shuf // 2] for members in gathered] if hop == HOPS - 1 else [],
+        )(current, w_branch, w_class_t, *before)
         if hop == 0:
-            logits, rows = call(
-                forward_first_kernel, [logits_f32, first_b16], [IN_VMEM] * 5, forward_flops
-            )(current, w_branch, w_class_t, tile_values, labels.reshape(1, nodes))
-            gathered.append(in_group(rows))
+            first_logits = logits
+            after = []
         else:
-            logits, rows = call(
-                functools.partial(forward_kernel, hop),
-                [logits_f32, rows_b16],
-                [IN_VMEM] * 4,
-                forward_flops,
-                (),
-                [members[shuf // 2] for members in gathered] if hop == 2 else [],
-            )(current, w_branch, w_class_t, logits)
-            if hop < HOPS - 1:
-                gathered.append(in_group(rows))
+            after = [first_logits]
         if hop < HOPS - 1:
-            current, to_left, to_right = call(
+            current, to_far, to_near, rows = call(
                 functools.partial(hop_kernel, plan),
-                [blocks_f32, slots_f32, slots_f32],
+                [blocks_f32, slots_f32, slots_f32, rows_b16],
                 [IN_SMEM] + [IN_VMEM] * 4,
                 hop_flops,
                 [ext],
-                [logits],
-            )(small, current, from_lower, from_upper, tile_values)
+                after,
+            )(small, current, from_far, from_near, tile_values)
 
     label_mine = call(
         label_kernel,
@@ -491,35 +523,48 @@
         [ext],
         gathered[1][1:],
     )(
-        small, current, from_lower, from_upper, tile_values,
+        small, current, from_far, from_near, tile_values,
         logits, w_branch, w_class_t, batch_order, label_mine,
     )
-    gathered = [member for members in gathered for member in members]
-    last_all = in_group(payload)
+    chunks = own_class // LANES
+    height = kept + width
+    ahead = shuf // 2
+    chunks_f32 = jax.ShapeDtypeStruct((chunks, height, LANES), F32)
+    grad_flops = shuf * nodes * own_class * (3 * width + 2 * kept)
+    weights = (w_branch, wt_own, wct_own)
+    across = swapped(payload, ahead, "shuf")
+    close = in_group(payload, ahead // 2)
+    early = call(
+        functools.partial(early_kernel, kept, ahead),
+        chunks_f32,
+        [IN_VMEM] * (3 * ahead + 3),
+        grad_flops,
+    )(*[member for members in gathered for member in members[:ahead]], *close, *weights)
+    across, early = lax.optimization_barrier((across, early))
+    distant = in_group(across, ahead // 2)
+    late_ins = (
+        early, *[member for members in gathered for member in members[ahead:]], *distant, *weights
+    )
+    last_all = close + distant
     loss_rows = call(
         loss_kernel, jax.ShapeDtypeStruct((1, nodes), F32), [IN_VMEM] * shuf, 1000
     )(*last_all).reshape(nodes)
 
-    chunks = own_class // LANES
-    height = kept + width
-    grad_flops = 2 * shuf * nodes * own_class * (3 * width + 2 * kept)
-    grad_ins = (*gathered, *last_all, w_branch, wt_own, wct_own)
     outs = [
         jax.ShapeDtypeStruct((branches, width, own), F32),
         jax.ShapeDtypeStruct((classes, own_class), F32),
     ]
-    chunks_f32 = pltpu.VMEM((chunks, height, LANES), F32)
     if chunks == dom and dom % 4 == 0 and dom & (dom - 1) == 0:
         half = dom // 2
         one_f32 = jax.ShapeDtypeStruct((height, LANES), F32)
         two_b16 = jax.ShapeDtypeStruct((2, height, LANES), BF16)
         made = call(
-            functools.partial(grad_kernel, kept, shuf, len(gathered), half),
+            functools.partial(late_kernel, kept, ahead, half),
             [one_f32] * half + [two_b16] * (half // 2),
-            [IN_VMEM] * len(grad_ins),
+            [IN_VMEM] * len(late_ins),
             grad_flops,
-            [chunks_f32],
-        )(*grad_ins)
+            [pltpu.VMEM(chunks_f32.shape, F32)],
+        )(*late_ins)
         order = list(range(half - 1, -1, -1))
         arrived = {pair: swapped(made[half + pair], 1) for pair in range(half // 2 - 1, -1, -1)}
         total = {
@@ -542,11 +587,11 @@
         )(*near, *other)
     else:
         grads = call(
-            functools.partial(plain_grad_kernel, kept, shuf, len(gathered)),
-            jax.ShapeDtypeStruct((chunks, height, LANES), F32),
-            [IN_VMEM] * len(grad_ins),
+            functools.partial(plain_late_kernel, kept, ahead),
+            chunks_f32,
+            [IN_VMEM] * len(late_ins),
             grad_flops,
-        )(*grad_ins)
+        )(*late_ins)
         grad_branch, grad_class_t = call(
             functools.partial(plain_out_kernel, kept), outs, [IN_VMEM], 1000
         )(lax.psum(grads, "dom"))

time: 79 us -> 84.6 us (1.071)
  waiting for transfers between devices: 22.9 us -> 36.4 us
  starting transfers between devices: 34.4 us -> 27.2 us
  local copies, waits for them, and re-layouts: 6.03 us -> 4.12 us
  Pallas kernels: 13.8 us -> 15 us
    ppermute x21 -> x24, waiting for transfers between devices: 21.8 us -> 30.5 us  [swapped(): return lax.ppermute(value, axis, pairs)]
    ppermute x6 -> x3, starting transfers between devices: 15.7 us -> 10.1 us  [far_pairs(): return lax.ppermute(value, 'dom', pairs)]
    ppermute x6 -> x3, waiting for transfers between devices: 1.06 us -> 5.93 us  [far_pairs(): return lax.ppermute(value, 'dom', pairs)]
    unnamed x18 -> x14, local copies, waits for them, and re-layouts: 5.23 us -> 3.32 us
    ppermute x21 -> x24, starting transfers between devices: 18.8 us -> 17.1 us  [swapped(): return lax.ppermute(value, axis, pairs)]
    pallas_call x5 -> x7, Pallas kernels: 6.77 us -> 7.28 us  [the longest x1 1.85 us: body(): call(functools.partial(late_kernel, kept, ahead, half), [one_f32] * half...]
  transfers between devices with their start and end apart: 27 -> 27, of which waited for: 14 -> 14; matrix products, arithmetic and copies ran while one was open for 1% -> 1% of each run, Pallas kernels for 6% -> 8%
where the time goes in v6:
time: 84.6 us; the launch traced here: 84.3 us
  waiting for transfers between devices  36.4 us (43%)
  starting transfers between devices  27.2 us (32%)
  Pallas kernels  15 us (18%)
  local copies, waits for them, and re-layouts  4.12 us (5%)
  between operations  1.45 us (2%)
    ppermute x24, waiting for transfers between devices, swapped(): return lax.ppermute(value, axis, pairs)  30.5 us
    ppermute x24, starting transfers between devices, swapped(): return lax.ppermute(value, axis, pairs)  17.1 us
    ppermute x3, starting transfers between devices, far_pairs(): return lax.ppermute(value, 'dom', pairs)  10.1 us
    ppermute x3, waiting for transfers between devices, far_pairs(): return lax.ppermute(value, 'dom', pairs)  5.93 us
    unnamed x14, local copies, waits for them, and re-layouts  3.32 us
    pallas_call x2, Pallas kernels, body(): call(functools.partial(hop_kernel, plan), [blocks_f32, slots_f32, slots_f...  3.06 us
    pallas_call x1, Pallas kernels, body(): call(functools.partial(last_kernel, plan, row_scale), jax.ShapeDtypeStruc...  2 us
    pallas_call x1, Pallas kernels, body(): call(functools.partial(late_kernel, kept, ahead, half), [one_f32] * half...  1.85 us
  transfers between devices with their start and end apart: 27, of which 14 were waited for; matrix products, arithmetic and copies ran while one was open for 1% of the time, Pallas kernels for 8%

profile of v6, /device:TPU:0, one launch (start us, length us, event | category | flops | bytes accessed | tf_op | source)
XLA Modules:
  0.0 84.3 jit_solution(6198053396473352007)
XLA Ops:
  0.6 1.8 %shard_map.139 = (f32[2,128,128]{2,1,0:T(8,128)}, f32[2,128,128]{2,1,0:T(8,128)}, f32[2,128,128]{2,1,0:T(8,128)}, bf16[272,128]{1,0:T(8,128)(2,1)}) custom-call(s32[2]{0:T(128)} %refs_0_.3, s32[2]{0:T(128)} %refs_1_.4, s32[1,2]{1,0:T(1,128)} %refs_2_.1, f32[2,128,128]{2,1,0:T(8,128)} %bitcast.31, s32[1,256]{1,0:T(1,128)} %bitcast.33), custom_call_target="tpu_custom_call" | custom-call | flops 1000 | bytes 1388544 | tf_op jit(solution)/shard_map/pallas_call | solution.py:452
  2.5 6.1 %collective-permute-start = (f32[2,128,128]{2,1,0:T(8,128)}, f32[2,128,128]{2,1,0:T(8,128)S(1)}, u32[]{:S(2)}, u32[]{:S(2)}) collective-permute-start(f32[2,128,128]{2,1,0:T(8,128)} %get-tuple-element.30), channel_id=1, source_target_pairs={{0,28},{4,8},{8,4},{12,16},{16,12},{20,24},{24,20},{28,0},{1,29},{... | collective-permute-start | bytes 393224 | tf_op jit(solution)/shard_map/ppermute | solution.py:34
  8.5 0.0 collective-permute-start.1
  8.6 1.0 %copy-done.3 = f32[8,128,128]{2,1,0:T(8,128)S(1)} copy-done((f32[8,128,128]{2,1,0:T(8,128)S(1)}, f32[8,128,128]{2,1,0:T(8,128)}, u32[]{:S(2)}) %copy-start.3) | copy-done | bytes 524312
  9.6 0.9 %copy-done.5 = f32[2,128,128]{2,1,0:T(8,128)S(1)} copy-done((f32[2,128,128]{2,1,0:T(8,128)S(1)}, f32[2,128,128]{2,1,0:T(8,128)}, u32[]{:S(2)}) %copy-start.5) | copy-done | bytes 131096
  11.2 0.8 concatenate.3.refs_0_.refs_1_.refs_3_
  12.0 0.4 collective-permute-done.refs_2_
  12.4 2.7 %collective-permute-done.1.refs_3_ = f32[2,128,128]{2,1,0:T(8,128)S(1)} collective-permute-done((f32[2,128,128]{2,1,0:T(8,128)}, f32[2,128,128]{2,1,0:T(8,128)S(1)}, u32[]{:S(2)}, u32[]{:S(2)}) %collective-permute-start.1) | collective-permute-done | bytes 131104 | tf_op jit(solution)/shard_map/ppermute | solution.py:39
  15.1 1.2 %shard_map.141 = (f32[2,128,128]{2,1,0:T(8,128)S(1)}, f32[2,128,128]{2,1,0:T(8,128)S(1)}, f32[2,128,128]{2,1,0:T(8,128)S(1)}, bf16[256,128]{1,0:T(8,128)(2,1)S(1)}) custom-call(s32[23]{0:T(128)S(1)} %concatenate.3.refs_0_.refs_1_.refs_3_, f32[2,128,128]{2,1,0:T(8,128)S(1)} %get-tuple-element.29.refs_1_.refs_0_, ...), custom_call_target="tpu_custom_call" | custom-call | flops 201326592 | bytes 1376256 | tf_op jit(solution)/shard_map/pallas_call | solution.py:491
  16.3 1.9 %collective-permute-start.5 = (f32[2,128,128]{2,1,0:T(8,128)S(1)}, f32[2,128,128]{2,1,0:T(8,128)S(1)}, u32[]{:S(2)}, u32[]{:S(2)}) collective-permute-start(f32[2,128,128]{2,1,0:T(8,128)S(1)} %get-tuple-element.35), channel_id=1, source_target_pairs={{0,28},{4,8},{8,4},{12,16},{16,12},{20,24},{24,20},{28,0},{1,29},{... | collective-permute-start | bytes 393224 | tf_op jit(solution)/shard_map/ppermute | solution.py:34
  18.2 0.0 collective-permute-start.6
  18.2 1.5 %collective-permute-start.9 = (bf16[272,128]{1,0:T(8,128)(2,1)S(1)}, bf16[272,128]{1,0:T(8,128)(2,1)S(1)}, u32[]{:S(2)}, u32[]{:S(2)}) collective-permute-start(bf16[272,128]{1,0:T(8,128)(2,1)S(1)} %copy-done.4), channel_id=1, source_target_pairs={{0,2},{1,3},{2,0},{3,1},{4,6},{5,7},{6,4},{7,5},{8,10},{9,11},{10,... | collective-permute-start | bytes 208904 | tf_op jit(solution)/shard_map/ppermute | solution.py:39
  19.7 0.0 collective-permute-start.10
  19.7 1.4 %copy-done.1 = bf16[4096,172]{0,1:T(8,128)(2,1)S(1)} copy-done((bf16[4096,172]{0,1:T(8,128)(2,1)S(1)}, bf16[4096,172]{0,1:T(8,128)(2,1)}, u32[]{:S(2)}) %copy-start.1) | copy-done | bytes 1409048
  21.0 0.6 shard_map.142.refs_0_.refs_3_
  21.6 0.6 collective-permute-start.3
  22.2 2.3 %collective-permute-done.5.refs_3_ = f32[2,128,128]{2,1,0:T(8,128)S(1)} collective-permute-done((f32[2,128,128]{2,1,0:T(8,128)S(1)}, f32[2,128,128]{2,1,0:T(8,128)S(1)}, u32[]{:S(2)}, u32[]{:S(2)}) %collective-permute-start.5) | collective-permute-done | bytes 131104 | tf_op jit(solution)/shard_map/ppermute | solution.py:34
  24.6 1.3 %collective-permute-done.6.refs_4_ = f32[2,128,128]{2,1,0:T(8,128)S(1)} collective-permute-done((f32[2,128,128]{2,1,0:T(8,128)S(1)}, f32[2,128,128]{2,1,0:T(8,128)S(1)}, u32[]{:S(2)}, u32[]{:S(2)}) %collective-permute-start.6) | collective-permute-done | bytes 131104 | tf_op jit(solution)/shard_map/ppermute | solution.py:39
  25.9 1.8 %shard_map.143 = (f32[2,128,128]{2,1,0:T(8,128)S(1)}, f32[2,128,128]{2,1,0:T(8,128)S(1)}, f32[2,128,128]{2,1,0:T(8,128)S(1)}, bf16[256,128]{1,0:T(8,128)(2,1)}) custom-call(f32[172,256]{1,0:T(8,128)S(1)} %shard_map.142.refs_0_.refs_3_, s32[23]{0:T(128)S(1)} %concatenate.3.refs_0_.refs_1_.refs_3_, f32[2,128,128]{2,1,0:T(8,128)S(1)} %get-tuple-element.34.refs_2_.refs_0_, ...), custom_call_target="tpu_custom_call" | custom-call | flops 201326592 | bytes 1376256 | tf_op jit(solution)/shard_map/pallas_call | solution.py:491
  27.7 2.2 %collective-permute-start.7 = (f32[2,128,128]{2,1,0:T(8,128)S(1)}, f32[2,128,128]{2,1,0:T(8,128)S(1)}, u32[]{:S(2)}, u32[]{:S(2)}) collective-permute-start(f32[2,128,128]{2,1,0:T(8,128)S(1)} %get-tuple-element.38), channel_id=1, source_target_pairs={{0,28},{4,8},{8,4},{12,16},{16,12},{20,24},{24,20},{28,0},{1,29},{... | collective-permute-start | bytes 393224 | tf_op jit(solution)/shard_map/ppermute | solution.py:34
  29.9 0.0 collective-permute-start.8
  29.9 0.1 collective-permute-start.11
  30.0 0.5 collective-permute-start.2
  30.5 0.0 collective-permute-done.3.refs_1_.refs_3_
  30.5 0.1 collective-permute-start.4
  30.6 0.6 shard_map.144.refs_5_
  31.2 0.1 collective-permute-done.11.refs_4_.refs_2_
  31.2 0.4 shard_map.146.refs_12_
  31.6 0.6 shard_map.145.refs_8_
  32.2 0.0 collective-permute-done.4.refs_2_.refs_4_
  32.2 3.2 %collective-permute-done.7.refs_5_ = f32[2,128,128]{2,1,0:T(8,128)S(1)} collective-permute-done((f32[2,128,128]{2,1,0:T(8,128)S(1)}, f32[2,128,128]{2,1,0:T(8,128)S(1)}, u32[]{:S(2)}, u32[]{:S(2)}) %collective-permute-start.7) | collective-permute-done | bytes 131104 | tf_op jit(solution)/shard_map/ppermute | solution.py:34
  35.5 0.9 %collective-permute-done.8.refs_6_ = f32[2,128,128]{2,1,0:T(8,128)S(1)} collective-permute-done((f32[2,128,128]{2,1,0:T(8,128)S(1)}, f32[2,128,128]{2,1,0:T(8,128)S(1)}, u32[]{:S(2)}, u32[]{:S(2)}) %collective-permute-start.8) | collective-permute-done | bytes 131104 | tf_op jit(solution)/shard_map/ppermute | solution.py:39
  36.4 2.0 %shard_map.147.refs_4_.refs_0_ = bf16[448,256]{1,0:T(8,128)(2,1)S(1)} custom-call(bf16[256,128]{1,0:T(8,128)(2,1)S(1)} %collective-permute-done.2.refs_0_.refs_3_, bf16[256,128]{1,0:T(8,128)(2,1)S(1)} %collective-permute-done.3.refs_1_.refs_3_, bf16[256,128]{1,0:T(8,128)(2,1)S(1)} %collective-permute-done.4.refs_2_.refs_4_, ...), custom_call_target="tpu_custom_call" | custom-call | flops 358612992 | bytes 688128 | tf_op jit(solution)/shard_map/pallas_call | solution.py:518
  38.4 0.0 collective-permute-start.12
  38.4 1.5 %collective-permute-start.13 = (bf16[448,256]{1,0:T(8,128)(2,1)S(1)}, bf16[448,256]{1,0:T(8,128)(2,1)S(1)}, u32[]{:S(2)}, u32[]{:S(2)}) collective-permute-start(bf16[448,256]{1,0:T(8,128)(2,1)S(1)} %shard_map.147.refs_4_.refs_0_), channel_id=1, source_target_pairs={{0,2},{1,3},{2,0},{3,1},{4,6},{5,7},{6,4},{7,5},{8,10},{9,11},{10,... | collective-permute-start | bytes 688136 | tf_op jit(solution)/shard_map/ppermute | solution.py:39
  39.9 0.3 shard_map.148
  40.2 1.8 %shard_map.149.refs_0_ = f32[8,304,128]{2,1,0:T(8,128)S(1)} custom-call(bf16[272,128]{1,0:T(8,128)(2,1)S(1)} %copy-done.4, bf16[272,128]{1,0:T(8,128)(2,1)S(1)} %collective-permute-done.10.refs_2_.refs_1_, bf16[256,128]{1,0:T(8,128)(2,1)S(1)} %get-tuple-element.33.refs_2_, bf16[256,128]{1,0:T(8,128)(2,1)S(1)} %collective-permute-done.2.refs_0_.refs_3_, ...), custom_call_target="tpu_custom_call" | custom-call | flops 771751936 | bytes 3735552 | tf_op jit(solution)/shard_map/pallas_call | solution.py:537
  42.0 4.4 %collective-permute-done.13.refs_2_.refs_5_ = bf16[448,256]{1,0:T(8,128)(2,1)S(1)} collective-permute-done((bf16[448,256]{1,0:T(8,128)(2,1)S(1)}, bf16[448,256]{1,0:T(8,128)(2,1)S(1)}, u32[]{:S(2)}, u32[]{:S(2)}) %collective-permute-start.13) | collective-permute-done | bytes 229408 | tf_op jit(solution)/shard_map/ppermute | solution.py:39
  46.4 1.5 %collective-permute-done.14.refs_3_.refs_6_ = bf16[448,256]{1,0:T(8,128)(2,1)S(1)} collective-permute-done((bf16[448,256]{1,0:T(8,128)(2,1)S(1)}, bf16[448,256]{1,0:T(8,128)(2,1)S(1)}, u32[]{:S(2)}, u32[]{:S(2)}) %collective-permute-start.14) | collective-permute-done | bytes 229408 | tf_op jit(solution)/shard_map/ppermute | solution.py:39
  47.9 1.9 %shard_map.151 = (f32[304,128]{1,0:T(8,128)S(1)}, f32[304,128]{1,0:T(8,128)S(1)}, f32[304,128]{1,0:T(8,128)S(1)}, f32[304,128]{1,0:T(8,128)S(1)}, bf16[2,304,128...) custom-call(f32[8,304,128]{2,1,0:T(8,128)S(1)} %shard_map.149.refs_0_, ...), custom_call_target="tpu_custom_call" | custom-call | flops 771751936 | bytes 2801664 | tf_op jit(solution)/shard_map/pallas_call | solution.py:561
  49.8 0.1 collective-permute-start.15
  49.8 2.0 %collective-permute-start.16 = (bf16[2,304,128]{2,1,0:T(8,128)(2,1)S(1)}, bf16[2,304,128]{2,1,0:T(8,128)(2,1)S(1)}, u32[]{:S(2)}, u32[]{:S(2)}) collective-permute-start(bf16[2,304,128]{2,1,0:T(8,128)(2,1)S(1)} %get-tuple-element.48), channel_id=1, source_target_pairs={{0,4},{4,0},{8,12},{12,8},{16,20},{20,16},{24,28},{28,24},{1,5},{5... | collective-permute-start | bytes 466952 | tf_op jit(solution)/shard_map/ppermute | solution.py:39
  51.9 4.8 %collective-permute-done.15 = bf16[2,304,128]{2,1,0:T(8,128)(2,1)S(1)} collective-permute-done((bf16[2,304,128]{2,1,0:T(8,128)(2,1)S(1)}, bf16[2,304,128]{2,1,0:T(8,128)(2,1)S(1)}, u32[]{:S(2)}, u32[]{:S(2)}) %collective-permute-start.15) | collective-permute-done | bytes 155680 | tf_op jit(solution)/shard_map/ppermute | solution.py:39
  56.7 0.1 collective-permute-start.19
  56.8 2.4 %collective-permute-done.16 = bf16[2,304,128]{2,1,0:T(8,128)(2,1)S(1)} collective-permute-done((bf16[2,304,128]{2,1,0:T(8,128)(2,1)S(1)}, bf16[2,304,128]{2,1,0:T(8,128)(2,1)S(1)}, u32[]{:S(2)}, u32[]{:S(2)}) %collective-permute-start.16) | collective-permute-done | bytes 155680 | tf_op jit(solution)/shard_map/ppermute | solution.py:39
  59.3 0.8 collective-permute-start.18
  60.1 1.3 %collective-permute-start.17 = (bf16[304,128]{1,0:T(8,128)(2,1)S(1)}, bf16[304,128]{1,0:T(8,128)(2,1)S(1)}, u32[]{:S(2)}, u32[]{:S(2)}) collective-permute-start(bf16[304,128]{1,0:T(8,128)(2,1)S(1)} %get-tuple-element.53), channel_id=1, source_target_pairs={{0,24},{4,28},{8,16},{12,20},{16,8},{20,12},{24,0},{28,4},{1,25},{... | collective-permute-start | bytes 233480 | tf_op jit(solution)/shard_map/ppermute | solution.py:39
  61.4 0.0 collective-permute-done.19
  61.4 5.8 %collective-permute-done.18 = bf16[304,128]{1,0:T(8,128)(2,1)S(1)} collective-permute-done((bf16[304,128]{1,0:T(8,128)(2,1)S(1)}, bf16[304,128]{1,0:T(8,128)(2,1)S(1)}, u32[]{:S(2)}, u32[]{:S(2)}) %collective-permute-start.18) | collective-permute-done | bytes 77856 | tf_op jit(solution)/shard_map/ppermute | solution.py:39
  67.2 0.0 collective-permute-done.17
  67.2 0.1 fusion.6.refs_0_
  67.3 1.5 %collective-permute-start.20 = (bf16[304,128]{1,0:T(8,128)(2,1)S(1)}, bf16[304,128]{1,0:T(8,128)(2,1)S(1)}, u32[]{:S(2)}, u32[]{:S(2)}) collective-permute-start(bf16[304,128]{1,0:T(8,128)(2,1)S(1)} %fusion.6.refs_0_), channel_id=1, source_target_pairs={{0,8},{4,12},{8,0},{12,4},{16,24},{20,28},{24,16},{28,20},{1,9},{5... | collective-permute-start | bytes 233480 | tf_op jit(solution)/shard_map/ppermute | solution.py:39
  68.7 1.0 %collective-permute-start.21 = (bf16[304,128]{1,0:T(8,128)(2,1)S(1)}, bf16[304,128]{1,0:T(8,128)(2,1)S(1)}, u32[]{:S(2)}, u32[]{:S(2)}) collective-permute-start(bf16[304,128]{1,0:T(8,128)(2,1)S(1)} %fusion.6.refs_0_), channel_id=1, source_target_pairs={{0,16},{4,20},{8,24},{12,28},{16,0},{20,4},{24,8},{28,12},{1,17},{... | collective-permute-start | bytes 233480 | tf_op jit(solution)/shard_map/ppermute | solution.py:39
  69.7 2.0 %collective-permute-start.22 = (bf16[304,128]{1,0:T(8,128)(2,1)S(1)}, bf16[304,128]{1,0:T(8,128)(2,1)S(1)}, u32[]{:S(2)}, u32[]{:S(2)}) collective-permute-start(bf16[304,128]{1,0:T(8,128)(2,1)S(1)} %fusion.6.refs_0_), channel_id=1, source_target_pairs={{0,24},{4,28},{8,16},{12,20},{16,8},{20,12},{24,0},{28,4},{1,25},{... | collective-permute-start | bytes 233480 | tf_op jit(solution)/shard_map/ppermute | solution.py:39
  71.7 1.1 %collective-permute-start.23 = (bf16[304,128]{1,0:T(8,128)(2,1)S(1)}, bf16[304,128]{1,0:T(8,128)(2,1)S(1)}, u32[]{:S(2)}, u32[]{:S(2)}) collective-permute-start(bf16[304,128]{1,0:T(8,128)(2,1)S(1)} %fusion.6.refs_0_), channel_id=1, source_target_pairs={{0,4},{4,0},{8,12},{12,8},{16,20},{20,16},{24,28},{28,24},{1,5},{5... | collective-permute-start | bytes 233480 | tf_op jit(solution)/shard_map/ppermute | solution.py:39
  72.8 0.9 %collective-permute-start.24 = (bf16[304,128]{1,0:T(8,128)(2,1)S(1)}, bf16[304,128]{1,0:T(8,128)(2,1)S(1)}, u32[]{:S(2)}, u32[]{:S(2)}) collective-permute-start(bf16[304,128]{1,0:T(8,128)(2,1)S(1)} %collective-permute-done.20.refs_1_), channel_id=1, source_target_pairs={{0,4},{4,0},{8,12},{12,8},{16,20},{20,16},{24,28},{28,24},{1,5},{5... | collective-permute-start | bytes 233480 | tf_op jit(solution)/shard_map/ppermute | solution.py:39
  73.8 3.8 %collective-permute-done.21.refs_2_ = bf16[304,128]{1,0:T(8,128)(2,1)S(1)} collective-permute-done((bf16[304,128]{1,0:T(8,128)(2,1)S(1)}, bf16[304,128]{1,0:T(8,128)(2,1)S(1)}, u32[]{:S(2)}, u32[]{:S(2)}) %collective-permute-start.21) | collective-permute-done | bytes 77856 | tf_op jit(solution)/shard_map/ppermute | solution.py:39
  77.5 1.2 %collective-permute-start.25 = (bf16[304,128]{1,0:T(8,128)(2,1)S(1)}, bf16[304,128]{1,0:T(8,128)(2,1)S(1)}, u32[]{:S(2)}, u32[]{:S(2)}) collective-permute-start(bf16[304,128]{1,0:T(8,128)(2,1)S(1)} %collective-permute-done.21.refs_2_), channel_id=1, source_target_pairs={{0,4},{4,0},{8,12},{12,8},{16,20},{20,16},{24,28},{28,24},{1,5},{5... | collective-permute-start | bytes 233480 | tf_op jit(solution)/shard_map/ppermute | solution.py:39
  78.7 0.0 collective-permute-done.22.refs_3_
  78.7 0.8 collective-permute-start.26
  79.6 0.8 shard_map.150
  80.4 1.5 %collective-permute-done.25.refs_6_ = bf16[304,128]{1,0:T(8,128)(2,1)S(1)} collective-permute-done((bf16[304,128]{1,0:T(8,128)(2,1)S(1)}, bf16[304,128]{1,0:T(8,128)(2,1)S(1)}, u32[]{:S(2)}, u32[]{:S(2)}) %collective-permute-start.25) | collective-permute-done | bytes 77856 | tf_op jit(solution)/shard_map/ppermute | solution.py:39
  81.9 1.2 %collective-permute-done.26.refs_7_ = bf16[304,128]{1,0:T(8,128)(2,1)S(1)} collective-permute-done((bf16[304,128]{1,0:T(8,128)(2,1)S(1)}, bf16[304,128]{1,0:T(8,128)(2,1)S(1)}, u32[]{:S(2)}, u32[]{:S(2)}) %collective-permute-start.26) | collective-permute-done | bytes 77856 | tf_op jit(solution)/shard_map/ppermute | solution.py:39
  83.1 1.2 %shard_map.152 = (f32[4,128,256]{2,1,0:T(8,128)}, f32[172,1024]{1,0:T(8,128)}) custom-call(bf16[304,128]{1,0:T(8,128)(2,1)S(1)} %fusion.6.refs_0_, bf16[304,128]{1,0:T(8,128)(2,1)S(1)} %collective-permute-done.20.refs_1_, bf16[304,128]{1,0:T(8,128)(2,1)S(1)} %collective-permute-done.21.refs_2_, bf16[304,128]{1,0:T(8,128)(2,1)S(1)} %collective-permute-done.22.refs_3_, ...), custom_call_target="tpu_custom_call" | custom-call | flops 1000 | bytes 3686400 | tf_op jit(solution)/shard_map/pallas_call | solution.py:585
  (22 shorter events, 0.2 us)
Async XLA Ops:
  0.6 19.0 %copy-start = (bf16[4,128,1024]{2,1,0:T(8,128)(2,1)S(1)}, bf16[4,128,1024]{2,1,0:T(8,128)(2,1)}, u32[]{:S(2)}) copy-start(bf16[4,128,1024]{2,1,0:T(8,128)(2,1)} %refs_7_.1) | copy-start | bytes 3145732
  2.5 9.9 %collective-permute-start = (f32[2,128,128]{2,1,0:T(8,128)}, f32[2,128,128]{2,1,0:T(8,128)S(1)}, u32[]{:S(2)}, u32[]{:S(2)}) collective-permute-start(f32[2,128,128]{2,1,0:T(8,128)} %get-tuple-element.30), channel_id=1, source_target_pairs={{0,28},{4,8},{8,4},{12,16},{16,12},{20,24},{24,20},{28,0},{1,29},{... | collective-permute-start | bytes 393224 | tf_op jit(solution)/shard_map/ppermute | solution.py:34
  8.5 6.5 %collective-permute-start.1 = (f32[2,128,128]{2,1,0:T(8,128)}, f32[2,128,128]{2,1,0:T(8,128)S(1)}, u32[]{:S(2)}, u32[]{:S(2)}) collective-permute-start(f32[2,128,128]{2,1,0:T(8,128)} %get-tuple-element.31), channel_id=1, source_target_pairs={{0,4},{4,0},{8,12},{12,8},{16,20},{20,16},{24,28},{28,24},{1,5},{5... | collective-permute-start | bytes 393224 | tf_op jit(solution)/shard_map/ppermute | solution.py:39
  8.5 1.0 %copy-start.3 = (f32[8,128,128]{2,1,0:T(8,128)S(1)}, f32[8,128,128]{2,1,0:T(8,128)}, u32[]{:S(2)}) copy-start(f32[8,128,128]{2,1,0:T(8,128)} %refs_1_.5) | copy-start | bytes 1572868
  9.6 0.9 %copy-start.5 = (f32[2,128,128]{2,1,0:T(8,128)S(1)}, f32[2,128,128]{2,1,0:T(8,128)}, u32[]{:S(2)}) copy-start(f32[2,128,128]{2,1,0:T(8,128)} %get-tuple-element.28.refs_0_) | copy-start | bytes 393220
  10.5 7.7 %copy-start.4 = (bf16[272,128]{1,0:T(8,128)(2,1)S(1)}, bf16[272,128]{1,0:T(8,128)(2,1)}, u32[]{:S(2)}) copy-start(bf16[272,128]{1,0:T(8,128)(2,1)} %get-tuple-element.40.refs_1_.refs_0_) | copy-start | bytes 208900
  16.3 8.3 %collective-permute-start.5 = (f32[2,128,128]{2,1,0:T(8,128)S(1)}, f32[2,128,128]{2,1,0:T(8,128)S(1)}, u32[]{:S(2)}, u32[]{:S(2)}) collective-permute-start(f32[2,128,128]{2,1,0:T(8,128)S(1)} %get-tuple-element.35), channel_id=1, source_target_pairs={{0,28},{4,8},{8,4},{12,16},{16,12},{20,24},{24,20},{28,0},{1,29},{... | collective-permute-start | bytes 393224 | tf_op jit(solution)/shard_map/ppermute | solution.py:34
  18.2 7.7 %collective-permute-start.6 = (f32[2,128,128]{2,1,0:T(8,128)S(1)}, f32[2,128,128]{2,1,0:T(8,128)S(1)}, u32[]{:S(2)}, u32[]{:S(2)}) collective-permute-start(f32[2,128,128]{2,1,0:T(8,128)S(1)} %get-tuple-element.36), channel_id=1, source_target_pairs={{0,4},{4,0},{8,12},{12,8},{16,20},{20,16},{24,28},{28,24},{1,5},{5... | collective-permute-start | bytes 393224 | tf_op jit(solution)/shard_map/ppermute | solution.py:39
  18.2 11.7 %collective-permute-start.9 = (bf16[272,128]{1,0:T(8,128)(2,1)S(1)}, bf16[272,128]{1,0:T(8,128)(2,1)S(1)}, u32[]{:S(2)}, u32[]{:S(2)}) collective-permute-start(bf16[272,128]{1,0:T(8,128)(2,1)S(1)} %copy-done.4), channel_id=1, source_target_pairs={{0,2},{1,3},{2,0},{3,1},{4,6},{5,7},{6,4},{7,5},{8,10},{9,11},{10,... | collective-permute-start | bytes 208904 | tf_op jit(solution)/shard_map/ppermute | solution.py:39
  19.7 10.3 %collective-permute-start.10 = (bf16[272,128]{1,0:T(8,128)(2,1)S(1)}, bf16[272,128]{1,0:T(8,128)(2,1)S(1)}, u32[]{:S(2)}, u32[]{:S(2)}) collective-permute-start(bf16[272,128]{1,0:T(8,128)(2,1)S(1)} %copy-done.4), channel_id=1, source_target_pairs={{0,1},{1,0},{2,3},{3,2},{4,5},{5,4},{6,7},{7,6},{8,9},{9,8},{10,11... | collective-permute-start | bytes 208904 | tf_op jit(solution)/shard_map/ppermute | solution.py:39
  19.7 1.4 %copy-start.1 = (bf16[4096,172]{0,1:T(8,128)(2,1)S(1)}, bf16[4096,172]{0,1:T(8,128)(2,1)}, u32[]{:S(2)}) copy-start(bf16[4096,172]{0,1:T(8,128)(2,1)} %param.23) | copy-start | bytes 4227076
  21.0 9.5 %copy-start.2 = (bf16[4096,172]{0,1:T(8,128)(2,1)S(1)}, bf16[4096,172]{0,1:T(8,128)(2,1)}, u32[]{:S(2)}) copy-start(bf16[4096,172]{0,1:T(8,128)(2,1)} %param.23) | copy-start | bytes 4227076
  21.6 8.9 %collective-permute-start.3 = (bf16[256,128]{1,0:T(8,128)(2,1)S(1)}, bf16[256,128]{1,0:T(8,128)(2,1)S(1)}, u32[]{:S(2)}, u32[]{:S(2)}) collective-permute-start(bf16[256,128]{1,0:T(8,128)(2,1)S(1)} %get-tuple-element.33.refs_2_), channel_id=1, source_target_pairs={{0,2},{1,3},{2,0},{3,1},{4,6},{5,7},{6,4},{7,5},{8,10},{9,11},{10,... | collective-permute-start | bytes 196616 | tf_op jit(solution)/shard_map/ppermute | solution.py:39
  27.7 7.8 %collective-permute-start.7 = (f32[2,128,128]{2,1,0:T(8,128)S(1)}, f32[2,128,128]{2,1,0:T(8,128)S(1)}, u32[]{:S(2)}, u32[]{:S(2)}) collective-permute-start(f32[2,128,128]{2,1,0:T(8,128)S(1)} %get-tuple-element.38), channel_id=1, source_target_pairs={{0,28},{4,8},{8,4},{12,16},{16,12},{20,24},{24,20},{28,0},{1,29},{... | collective-permute-start | bytes 393224 | tf_op jit(solution)/shard_map/ppermute | solution.py:34
  29.9 1.3 %copy-start.6 = (s32[1,256]{1,0:T(1,128)S(1)}, s32[1,256]{1,0:T(1,128)}, u32[]{:S(2)}) copy-start(s32[1,256]{1,0:T(1,128)} %refs_11_.1) | copy-start | bytes 3076
  29.9 6.5 %collective-permute-start.8 = (f32[2,128,128]{2,1,0:T(8,128)S(1)}, f32[2,128,128]{2,1,0:T(8,128)S(1)}, u32[]{:S(2)}, u32[]{:S(2)}) collective-permute-start(f32[2,128,128]{2,1,0:T(8,128)S(1)} %get-tuple-element.39), channel_id=1, source_target_pairs={{0,4},{4,0},{8,12},{12,8},{16,20},{20,16},{24,28},{28,24},{1,5},{5... | collective-permute-start | bytes 393224 | tf_op jit(solution)/shard_map/ppermute | solution.py:39
  29.9 1.3 %collective-permute-start.11 = (bf16[272,128]{1,0:T(8,128)(2,1)S(1)}, bf16[272,128]{1,0:T(8,128)(2,1)S(1)}, u32[]{:S(2)}, u32[]{:S(2)}) collective-permute-start(bf16[272,128]{1,0:T(8,128)(2,1)S(1)} %collective-permute-done.9.refs_0_.refs_3_.refs_1_), channel_id=1, source_target_pairs={{0,1},{1,0},{2,3},{3,2},{4,5},{5,4},{6,7},{7,6},{8,9},{9,8},{10,11... | collective-permute-start | bytes 208904 | tf_op jit(solution)/shard_map/ppermute | solution.py:39
  30.0 2.2 %collective-permute-start.2 = (bf16[256,128]{1,0:T(8,128)(2,1)S(1)}, bf16[256,128]{1,0:T(8,128)(2,1)S(1)}, u32[]{:S(2)}, u32[]{:S(2)}) collective-permute-start(bf16[256,128]{1,0:T(8,128)(2,1)S(1)} %get-tuple-element.33.refs_2_), channel_id=1, source_target_pairs={{0,1},{1,0},{2,3},{3,2},{4,5},{5,4},{6,7},{7,6},{8,9},{9,8},{10,11... | collective-permute-start | bytes 196616 | tf_op jit(solution)/shard_map/ppermute | solution.py:39
  30.5 1.8 %collective-permute-start.4 = (bf16[256,128]{1,0:T(8,128)(2,1)S(1)}, bf16[256,128]{1,0:T(8,128)(2,1)S(1)}, u32[]{:S(2)}, u32[]{:S(2)}) collective-permute-start(bf16[256,128]{1,0:T(8,128)(2,1)S(1)} %collective-permute-done.3.refs_1_.refs_3_), channel_id=1, source_target_pairs={{0,1},{1,0},{2,3},{3,2},{4,5},{5,4},{6,7},{7,6},{8,9},{9,8},{10,11... | collective-permute-start | bytes 196616 | tf_op jit(solution)/shard_map/ppermute | solution.py:39
  38.4 1.8 %collective-permute-start.12 = (bf16[448,256]{1,0:T(8,128)(2,1)S(1)}, bf16[448,256]{1,0:T(8,128)(2,1)S(1)}, u32[]{:S(2)}, u32[]{:S(2)}) collective-permute-start(bf16[448,256]{1,0:T(8,128)(2,1)S(1)} %shard_map.147.refs_4_.refs_0_), channel_id=1, source_target_pairs={{0,1},{1,0},{2,3},{3,2},{4,5},{5,4},{6,7},{7,6},{8,9},{9,8},{10,11... | collective-permute-start | bytes 688136 | tf_op jit(solution)/shard_map/ppermute | solution.py:39
  38.4 8.0 %collective-permute-start.13 = (bf16[448,256]{1,0:T(8,128)(2,1)S(1)}, bf16[448,256]{1,0:T(8,128)(2,1)S(1)}, u32[]{:S(2)}, u32[]{:S(2)}) collective-permute-start(bf16[448,256]{1,0:T(8,128)(2,1)S(1)} %shard_map.147.refs_4_.refs_0_), channel_id=1, source_target_pairs={{0,2},{1,3},{2,0},{3,1},{4,6},{5,7},{6,4},{7,5},{8,10},{9,11},{10,... | collective-permute-start | bytes 688136 | tf_op jit(solution)/shard_map/ppermute | solution.py:39
  46.4 1.5 %collective-permute-start.14 = (bf16[448,256]{1,0:T(8,128)(2,1)S(1)}, bf16[448,256]{1,0:T(8,128)(2,1)S(1)}, u32[]{:S(2)}, u32[]{:S(2)}) collective-permute-start(bf16[448,256]{1,0:T(8,128)(2,1)S(1)} %collective-permute-done.13.refs_2_.refs_5_), channel_id=1, source_target_pairs={{0,1},{1,0},{2,3},{3,2},{4,5},{5,4},{6,7},{7,6},{8,9},{9,8},{10,11... | collective-permute-start | bytes 688136 | tf_op jit(solution)/shard_map/ppermute | solution.py:39
  49.8 6.9 %collective-permute-start.15 = (bf16[2,304,128]{2,1,0:T(8,128)(2,1)S(1)}, bf16[2,304,128]{2,1,0:T(8,128)(2,1)S(1)}, u32[]{:S(2)}, u32[]{:S(2)}) collective-permute-start(bf16[2,304,128]{2,1,0:T(8,128)(2,1)S(1)} %get-tuple-element.46), channel_id=1, source_target_pairs={{0,4},{4,0},{8,12},{12,8},{16,20},{20,16},{24,28},{28,24},{1,5},{5... | collective-permute-start | bytes 466952 | tf_op jit(solution)/shard_map/ppermute | solution.py:39
  49.8 9.4 %collective-permute-start.16 = (bf16[2,304,128]{2,1,0:T(8,128)(2,1)S(1)}, bf16[2,304,128]{2,1,0:T(8,128)(2,1)S(1)}, u32[]{:S(2)}, u32[]{:S(2)}) collective-permute-start(bf16[2,304,128]{2,1,0:T(8,128)(2,1)S(1)} %get-tuple-element.48), channel_id=1, source_target_pairs={{0,4},{4,0},{8,12},{12,8},{16,20},{20,16},{24,28},{28,24},{1,5},{5... | collective-permute-start | bytes 466952 | tf_op jit(solution)/shard_map/ppermute | solution.py:39
  56.7 4.7 %collective-permute-start.19 = (bf16[304,128]{1,0:T(8,128)(2,1)S(1)}, bf16[304,128]{1,0:T(8,128)(2,1)S(1)}, u32[]{:S(2)}, u32[]{:S(2)}) collective-permute-start(bf16[304,128]{1,0:T(8,128)(2,1)S(1)} %fusion), channel_id=1, source_target_pairs={{0,8},{4,12},{8,0},{12,4},{16,24},{20,28},{24,16},{28,20},{1,9},{5... | collective-permute-start | bytes 233480 | tf_op jit(solution)/shard_map/ppermute | solution.py:39
  59.3 7.9 %collective-permute-start.18 = (bf16[304,128]{1,0:T(8,128)(2,1)S(1)}, bf16[304,128]{1,0:T(8,128)(2,1)S(1)}, u32[]{:S(2)}, u32[]{:S(2)}) collective-permute-start(bf16[304,128]{1,0:T(8,128)(2,1)S(1)} %get-tuple-element.54), channel_id=1, source_target_pairs={{0,16},{4,20},{8,24},{12,28},{16,0},{20,4},{24,8},{28,12},{1,17},{... | collective-permute-start | bytes 233480 | tf_op jit(solution)/shard_map/ppermute | solution.py:39
  60.1 7.1 %collective-permute-start.17 = (bf16[304,128]{1,0:T(8,128)(2,1)S(1)}, bf16[304,128]{1,0:T(8,128)(2,1)S(1)}, u32[]{:S(2)}, u32[]{:S(2)}) collective-permute-start(bf16[304,128]{1,0:T(8,128)(2,1)S(1)} %get-tuple-element.53), channel_id=1, source_target_pairs={{0,24},{4,28},{8,16},{12,20},{16,8},{20,12},{24,0},{28,4},{1,25},{... | collective-permute-start | bytes 233480 | tf_op jit(solution)/shard_map/ppermute | solution.py:39
  67.3 5.6 %collective-permute-start.20 = (bf16[304,128]{1,0:T(8,128)(2,1)S(1)}, bf16[304,128]{1,0:T(8,128)(2,1)S(1)}, u32[]{:S(2)}, u32[]{:S(2)}) collective-permute-start(bf16[304,128]{1,0:T(8,128)(2,1)S(1)} %fusion.6.refs_0_), channel_id=1, source_target_pairs={{0,8},{4,12},{8,0},{12,4},{16,24},{20,28},{24,16},{28,20},{1,9},{5... | collective-permute-start | bytes 233480 | tf_op jit(solution)/shard_map/ppermute | solution.py:39
  68.7 8.8 %collective-permute-start.21 = (bf16[304,128]{1,0:T(8,128)(2,1)S(1)}, bf16[304,128]{1,0:T(8,128)(2,1)S(1)}, u32[]{:S(2)}, u32[]{:S(2)}) collective-permute-start(bf16[304,128]{1,0:T(8,128)(2,1)S(1)} %fusion.6.refs_0_), channel_id=1, source_target_pairs={{0,16},{4,20},{8,24},{12,28},{16,0},{20,4},{24,8},{28,12},{1,17},{... | collective-permute-start | bytes 233480 | tf_op jit(solution)/shard_map/ppermute | solution.py:39
  69.7 9.0 %collective-permute-start.22 = (bf16[304,128]{1,0:T(8,128)(2,1)S(1)}, bf16[304,128]{1,0:T(8,128)(2,1)S(1)}, u32[]{:S(2)}, u32[]{:S(2)}) collective-permute-start(bf16[304,128]{1,0:T(8,128)(2,1)S(1)} %fusion.6.refs_0_), channel_id=1, source_target_pairs={{0,24},{4,28},{8,16},{12,20},{16,8},{20,12},{24,0},{28,4},{1,25},{... | collective-permute-start | bytes 233480 | tf_op jit(solution)/shard_map/ppermute | solution.py:39
  71.7 8.7 %collective-permute-start.23 = (bf16[304,128]{1,0:T(8,128)(2,1)S(1)}, bf16[304,128]{1,0:T(8,128)(2,1)S(1)}, u32[]{:S(2)}, u32[]{:S(2)}) collective-permute-start(bf16[304,128]{1,0:T(8,128)(2,1)S(1)} %fusion.6.refs_0_), channel_id=1, source_target_pairs={{0,4},{4,0},{8,12},{12,8},{16,20},{20,16},{24,28},{28,24},{1,5},{5... | collective-permute-start | bytes 233480 | tf_op jit(solution)/shard_map/ppermute | solution.py:39
  72.8 7.6 %collective-permute-start.24 = (bf16[304,128]{1,0:T(8,128)(2,1)S(1)}, bf16[304,128]{1,0:T(8,128)(2,1)S(1)}, u32[]{:S(2)}, u32[]{:S(2)}) collective-permute-start(bf16[304,128]{1,0:T(8,128)(2,1)S(1)} %collective-permute-done.20.refs_1_), channel_id=1, source_target_pairs={{0,4},{4,0},{8,12},{12,8},{16,20},{20,16},{24,28},{28,24},{1,5},{5... | collective-permute-start | bytes 233480 | tf_op jit(solution)/shard_map/ppermute | solution.py:39
  77.5 4.4 %collective-permute-start.25 = (bf16[304,128]{1,0:T(8,128)(2,1)S(1)}, bf16[304,128]{1,0:T(8,128)(2,1)S(1)}, u32[]{:S(2)}, u32[]{:S(2)}) collective-permute-start(bf16[304,128]{1,0:T(8,128)(2,1)S(1)} %collective-permute-done.21.refs_2_), channel_id=1, source_target_pairs={{0,4},{4,0},{8,12},{12,8},{16,20},{20,16},{24,28},{28,24},{1,5},{5... | collective-permute-start | bytes 233480 | tf_op jit(solution)/shard_map/ppermute | solution.py:39
  78.7 4.4 %collective-permute-start.26 = (bf16[304,128]{1,0:T(8,128)(2,1)S(1)}, bf16[304,128]{1,0:T(8,128)(2,1)S(1)}, u32[]{:S(2)}, u32[]{:S(2)}) collective-permute-start(bf16[304,128]{1,0:T(8,128)(2,1)S(1)} %collective-permute-done.22.refs_3_), channel_id=1, source_target_pairs={{0,4},{4,0},{8,12},{12,8},{16,20},{20,16},{24,28},{28,24},{1,5},{5... | collective-permute-start | bytes 233480 | tf_op jit(solution)/shard_map/ppermute | solution.py:39

commit v7 on v6

--- a/solution.py
+++ b/solution.py
@@ -24,14 +24,10 @@
     return -(-value // multiple) * multiple
 
 
-def near_pairs(value):
-    return swapped(value, 1)
-
-
-def far_pairs(value):
-    count = lax.axis_size("dom")
-    pairs = [(d, (d + 1 if d % 2 else d - 1) % count) for d in range(count)]
-    return lax.ppermute(value, "dom", pairs)
+def passed_along(value, axis, steps):
+    count = lax.axis_size(axis)
+    pairs = [(source, (source + steps) % count) for source in range(count)]
+    return lax.ppermute(value, axis, pairs)
 
 
 def swapped(value, distance, axis="dom"):
@@ -80,10 +76,9 @@
         self.sent = self.right + slots
 
 
-def write_sends(blocks, far_ref, near_ref, ids, counts):
-    odd = lax.axis_index("dom") % 2
-    for slot in range(far_ref.shape[0]):
-        for out_ref, side in ((far_ref, odd), (near_ref, 1 - odd)):
+def write_sends(blocks, left_ref, right_ref, ids, counts):
+    for slot in range(left_ref.shape[0]):
+        for side, out_ref in enumerate((left_ref, right_ref)):
             index = ids(side, slot)
             picked = blocks[0]
             for number in range(1, len(blocks)):
@@ -104,7 +99,7 @@
 
 def first_kernel(
     sl_ref, sr_ref, sc_ref, feat_ref, label_from,
-    far_ref, near_ref, held_ref, b_ref,
+    left_ref, right_ref, held_ref, b_ref,
     sl_here, sr_here, sc_here, label_ref, sems,
 ):
     copied(
@@ -115,9 +110,9 @@
     blocks = [held_ref[number] for number in range(held_ref.shape[0])]
     write_sends(
         blocks,
-        far_ref,
-        near_ref,
-        lambda side, slot: jnp.where(side == 0, sl_here[slot], sr_here[slot]),
+        left_ref,
+        right_ref,
+        lambda side, slot: (sl_here, sr_here)[side][slot],
         lambda side: sc_here[0, side],
     )
     write_rows(blocks, b_ref)
@@ -161,25 +156,24 @@
     return totals
 
 
-def extend(cur_ref, far_ref, near_ref, ext_ref):
+def extend(cur_ref, low_ref, high_ref, ext_ref):
     local = cur_ref.shape[0]
-    slots = far_ref.shape[0]
-    odd = lax.axis_index("dom") % 2
-    ext_ref[pl.ds(local + odd * slots, slots)] = far_ref[...]
-    ext_ref[pl.ds(local + (1 - odd) * slots, slots)] = near_ref[...]
+    slots = low_ref.shape[0]
+    ext_ref[local : local + slots] = low_ref[...]
+    ext_ref[local + slots :] = high_ref[...]
 
 
 def hop_kernel(
-    plan, plan_ref, cur_ref, far_in_ref, near_in_ref, tiles_ref,
-    next_ref, far_ref, near_ref, b_ref, ext_ref,
+    plan, plan_ref, cur_ref, low_ref, high_ref, tiles_ref,
+    next_ref, left_ref, right_ref, b_ref, ext_ref,
 ):
-    extend(cur_ref, far_in_ref, near_in_ref, ext_ref)
+    extend(cur_ref, low_ref, high_ref, ext_ref)
     blocks = next_blocks(plan, plan_ref, cur_ref, tiles_ref, ext_ref)
     write_sends(
         blocks,
-        far_ref,
-        near_ref,
-        lambda side, slot: plan_ref[plan.left + side * plan.slots + slot],
+        left_ref,
+        right_ref,
+        lambda side, slot: plan_ref[(plan.left, plan.right)[side] + slot],
         lambda side: plan_ref[plan.sent + side],
     )
     for number, block in enumerate(blocks):
@@ -252,21 +246,29 @@
     refs[-1][...] = total[0:1] + total[1:2] + total[2:3]
 
 
-def last_kernel(
-    plan, row_scale, plan_ref,
-    cur_ref, far_ref, near_ref, tiles_ref, before_ref, w_ref, wc_ref, order_ref, label_ref,
-    out_ref, ext_ref,
+def last_hop_kernel(plan, plan_ref, cur_ref, low_ref, high_ref, tiles_ref, out_ref, ext_ref):
+    extend(cur_ref, low_ref, high_ref, ext_ref)
+    blocks = next_blocks(plan, plan_ref, cur_ref, tiles_ref, ext_ref)
+    for number, block in enumerate(blocks):
+        size, width = block.shape
+        columns = slice(number * width, (number + 1) * width)
+        out_ref[:size, columns] = block.astype(BF16)
+        out_ref[size:, columns] = cur_ref[number].astype(BF16)
+
+
+def stacked(ref, place, width):
+    size = ref.shape[0] // 2
+    parts = ref.shape[1] // width
+    return [
+        ref[place * size : (place + 1) * size, part * width : (part + 1) * width]
+        for part in range(parts)
+    ]
+
+
+def loss_and_gradient_kernel(
+    row_scale, rows_ref, before_ref, w_ref, wc_ref, order_ref, label_ref, out_ref
 ):
-    extend(cur_ref, far_ref, near_ref, ext_ref)
-    blocks = next_blocks(plan, plan_ref, cur_ref, tiles_ref, ext_ref)
-    halves = [block.astype(BF16) for block in blocks]
-    rows_b = jnp.concatenate(halves, axis=0)
-    size, width = halves[0].shape
-    for number, half in enumerate(halves):
-        columns = slice(number * width, (number + 1) * width)
-        out_ref[:size, columns] = half
-        out_ref[size : 2 * size, columns] = cur_ref[number].astype(BF16)
-    size = 2 * size
+    rows_b = jnp.concatenate(stacked(rows_ref, 0, w_ref.shape[1]), axis=0)
     logits = before_ref[...] + branch_logits(w_ref.shape[0] - 1, rows_b, w_ref, wc_ref)
     classes, rows = logits.shape
     kept = up_to(classes, 16)
@@ -275,8 +277,8 @@
     log_total = top + jnp.log(jnp.sum(jnp.exp(logits - top), axis=0, keepdims=True))
     loss = log_total - jnp.sum(jnp.where(hit, logits, 0.0), axis=0, keepdims=True)
     dlogits = (jnp.exp(logits - log_total) - jnp.where(hit, 1.0, 0.0)) * row_scale
-    out_ref[size + kept - 16 : size + kept] = jnp.zeros((16, rows), BF16)
-    out_ref[size : size + classes] = dlogits.astype(BF16)
+    out_ref[kept - 16 : kept] = jnp.zeros((16, rows), BF16)
+    out_ref[:classes] = dlogits.astype(BF16)
     number = lax.broadcasted_iota(jnp.int32, (16, rows), 0)
     packed = jnp.zeros((16, rows), F32)
     rest = loss
@@ -284,7 +286,7 @@
         part = rest.astype(BF16).astype(F32)
         packed = jnp.where(number == piece, part, packed)
         rest = rest - part
-    out_ref[size + kept :] = matmul(packed.astype(BF16), places(order_ref)).astype(BF16)
+    out_ref[kept:] = matmul(packed.astype(BF16), places(order_ref)).astype(BF16)
 
 
 def weights_kernel(w_ref, wc_ref, wt_ref, wct_ref, pad_ref):
@@ -301,26 +303,19 @@
         wct_ref[branch] = pad_ref[...].T[:, :kept].astype(BF16)
 
 
-def add_chunks(kept, more, row_refs, last_refs, w_ref, wt_ref, wct_ref, chunks_ref):
+def add_chunks(kept, more, row_refs, last_refs, dlogit_refs, w_ref, wt_ref, wct_ref, chunks_ref):
     members = len(last_refs)
     branches, own, width = wt_ref.shape
     nodes = last_refs[0].shape[1]
     hid = w_ref.shape[2]
-    parts = last_refs[0].shape[1] // width
-    size = nodes // parts
     all_rows = []
     for branch in range(branches - 2):
         ours = row_refs[branch * members : (branch + 1) * members]
         all_rows.append(jnp.concatenate([ref[:nodes] for ref in ours], axis=0))
     for place in (1, 0):
-        last_rows = []
-        for ref in last_refs:
-            for part in range(parts):
-                columns = slice(part * width, (part + 1) * width)
-                last_rows.append(ref[place * size : (place + 1) * size, columns])
-        all_rows.append(jnp.concatenate(last_rows, axis=0))
-    size = 2 * size
-    dlogits_t = jnp.concatenate([ref[size : size + kept] for ref in last_refs], axis=1)
+        ours = [rows for ref in last_refs for rows in stacked(ref, place, width)]
+        all_rows.append(jnp.concatenate(ours, axis=0))
+    dlogits_t = jnp.concatenate([ref[:kept] for ref in dlogit_refs], axis=1)
     own_class = branches * own
     first = lax.axis_index("shuf") * own_class
     which = first // hid
@@ -349,17 +344,21 @@
             )
 
 
+def split_refs(members, refs):
+    last = len(refs) - 3 - 2 * members
+    return (
+        refs[:last], refs[last : last + members], refs[last + members : last + 2 * members],
+        *refs[last + 2 * members :],
+    )
+
+
 def early_kernel(kept, members, *refs):
-    last = len(refs) - 4 - members
-    add_chunks(kept, False, refs[:last], refs[last : last + members], *refs[last + members :])
+    add_chunks(kept, False, *split_refs(members, refs[:-1]), refs[-1])
 
 
 def late_chunks(kept, members, early_ref, refs, chunks_ref):
-    last = len(refs) - 3 - members
     chunks_ref[...] = early_ref[...]
-    add_chunks(
-        kept, True, refs[:last], refs[last : last + members], *refs[last + members :], chunks_ref
-    )
+    add_chunks(kept, True, *split_refs(members, refs), chunks_ref)
 
 
 def late_kernel(kept, members, half, early_ref, *refs):
@@ -449,7 +448,7 @@
     hop_flops = 12 * tiles * block * block * width
     forward_flops = 2 * nodes * hid * (width + classes)
     ext = pltpu.VMEM((local + 2 * slots, block, width), F32)
-    to_far, to_near, current, rows = call(
+    to_left, to_right, current, rows = call(
         first_kernel,
         [slots_f32, slots_f32, blocks_f32, first_b16],
         [ANYWHERE] * 5,
@@ -470,8 +469,8 @@
         1000,
     )(current, tile_values)
     for hop in range(HOPS):
-        from_far = far_pairs(to_far)
-        from_near = near_pairs(to_near)
+        from_lower = passed_along(to_right, "dom", 1)
+        from_upper = passed_along(to_left, "dom", -1)
         if hop < HOPS - 1:
             gathered.append(in_group(rows))
         before = [] if logits is None else [logits]
@@ -488,14 +487,14 @@
         else:
             after = [first_logits]
         if hop < HOPS - 1:
-            current, to_far, to_near, rows = call(
+            current, to_left, to_right, rows = call(
                 functools.partial(hop_kernel, plan),
                 [blocks_f32, slots_f32, slots_f32, rows_b16],
                 [IN_SMEM] + [IN_VMEM] * 4,
                 hop_flops,
                 [ext],
                 after,
-            )(small, current, from_far, from_near, tile_values)
+            )(small, current, from_lower, from_upper, tile_values)
 
     label_mine = call(
         label_kernel,
@@ -515,35 +514,45 @@
         [pltpu.VMEM((up_to(classes, LANES), own), F32)],
     )(w_branch, w_class_t)
 
-    payload = call(
-        functools.partial(last_kernel, plan, row_scale),
-        jax.ShapeDtypeStruct((2 * block + kept + 16, local * width), BF16),
-        [IN_SMEM] + [IN_VMEM] * 9,
-        hop_flops + forward_flops,
+    last_rows = call(
+        functools.partial(last_hop_kernel, plan),
+        jax.ShapeDtypeStruct((2 * block, local * width), BF16),
+        [IN_SMEM] + [IN_VMEM] * 4,
+        hop_flops,
         [ext],
-        gathered[1][1:],
-    )(
-        small, current, from_far, from_near, tile_values,
-        logits, w_branch, w_class_t, batch_order, label_mine,
-    )
+        [logits, label_mine, *gathered[1][1:]],
+    )(small, current, from_lower, from_upper, tile_values)
+    dlogits = call(
+        functools.partial(loss_and_gradient_kernel, row_scale),
+        jax.ShapeDtypeStruct((kept + 16, nodes), BF16),
+        [IN_VMEM] * 6,
+        forward_flops,
+    )(last_rows, logits, w_branch, w_class_t, batch_order, label_mine)
     chunks = own_class // LANES
     height = kept + width
     ahead = shuf // 2
     chunks_f32 = jax.ShapeDtypeStruct((chunks, height, LANES), F32)
     grad_flops = shuf * nodes * own_class * (3 * width + 2 * kept)
     weights = (w_branch, wt_own, wct_own)
-    across = swapped(payload, ahead, "shuf")
-    close = in_group(payload, ahead // 2)
+    across_rows = swapped(last_rows, ahead, "shuf")
+    across = swapped(dlogits, ahead, "shuf")
+    close_rows = in_group(last_rows, ahead // 2)
+    close = in_group(dlogits, ahead // 2)
     early = call(
         functools.partial(early_kernel, kept, ahead),
         chunks_f32,
-        [IN_VMEM] * (3 * ahead + 3),
+        [IN_VMEM] * (4 * ahead + 3),
         grad_flops,
-    )(*[member for members in gathered for member in members[:ahead]], *close, *weights)
-    across, early = lax.optimization_barrier((across, early))
+    )(
+        *[member for members in gathered for member in members[:ahead]],
+        *close_rows, *close, *weights,
+    )
+    across, across_rows, early = lax.optimization_barrier((across, across_rows, early))
+    distant_rows = in_group(across_rows, ahead // 2)
     distant = in_group(across, ahead // 2)
     late_ins = (
-        early, *[member for members in gathered for member in members[ahead:]], *distant, *weights
+        early, *[member for members in gathered for member in members[ahead:]],
+        *distant_rows, *distant, *weights,
     )
     last_all = close + distant
     loss_rows = call(
@@ -566,7 +575,12 @@
             [pltpu.VMEM(chunks_f32.shape, F32)],
         )(*late_ins)
         order = list(range(half - 1, -1, -1))
-        arrived = {pair: swapped(made[half + pair], 1) for pair in range(half // 2 - 1, -1, -1)}
+        arrived = {}
+        for pair in range(half // 2 - 1, -1, -1):
+            going = made[half + pair]
+            if arrived:
+                arrived[pair + 1], going = lax.optimization_barrier((arrived[pair + 1], going))
+            arrived[pair] = swapped(going, 1)
         total = {
             step: made[step] + arrived[step // 2][step % 2].astype(F32) for step in order
         }

time: 84.6 us -> 81.2 us (0.960)
  waiting for transfers between devices: 36.4 us -> 24.8 us
  starting transfers between devices: 27.2 us -> 35.5 us
    ppermute x24, waiting for transfers between devices: 30.5 us -> 21.1 us  [swapped(): return lax.ppermute(value, axis, pairs)]
    ppermute x3 -> x6, starting transfers between devices: 10.1 us -> 15.6 us  [passed_along(): return lax.ppermute(value, axis, pairs)]
    ppermute x24, starting transfers between devices: 17.1 us -> 19.9 us  [swapped(): return lax.ppermute(value, axis, pairs)]
    ppermute x3 -> x6, waiting for transfers between devices: 5.93 us -> 3.67 us  [passed_along(): return lax.ppermute(value, axis, pairs)]
    pallas_call x1 -> x2, Pallas kernels: 2 us -> 2.01 us  [the longest x1 1.18 us: body(): call(functools.partial(last_hop_kernel, plan), jax.ShapeDtypeStruct((2 *...]
  transfers between devices with their start and end apart: 27 -> 30, of which waited for: 14 -> 16; matrix products, arithmetic and copies ran while one was open for 1% -> 1% of each run, Pallas kernels for 8% -> 10%
where the time goes in v7:
time: 81.2 us; the launch traced here: 80.9 us
  starting transfers between devices  35.5 us (44%)
  waiting for transfers between devices  24.8 us (31%)
  Pallas kernels  14.9 us (18%)
  local copies, waits for them, and re-layouts  4.12 us (5%)
  between operations  1.45 us (2%)
    ppermute x24, waiting for transfers between devices, swapped(): return lax.ppermute(value, axis, pairs)  21.1 us
    ppermute x24, starting transfers between devices, swapped(): return lax.ppermute(value, axis, pairs)  19.9 us
    ppermute x6, starting transfers between devices, passed_along(): return lax.ppermute(value, axis, pairs)  15.6 us
    ppermute x6, waiting for transfers between devices, passed_along(): return lax.ppermute(value, axis, pairs)  3.67 us
    unnamed x14, local copies, waits for them, and re-layouts  3.32 us
    pallas_call x2, Pallas kernels, body(): call(functools.partial(hop_kernel, plan), [blocks_f32, slots_f32, slots_f...  3.01 us
    pallas_call x1, Pallas kernels, body(): call(functools.partial(late_kernel, kept, ahead, half), [one_f32] * half...  1.82 us
    pallas_call x1, Pallas kernels, body(): call(first_kernel, [slots_f32, slots_f32, blocks_f32, first_b16], [ANYWHE...  1.81 us
  transfers between devices with their start and end apart: 30, of which 16 were waited for; matrix products, arithmetic and copies ran while one was open for 1% of the time, Pallas kernels for 10%

profile of v7, /device:TPU:0, one launch (start us, length us, event | category | flops | bytes accessed | tf_op | source)
XLA Modules:
  0.0 80.9 jit_solution(8618950602738311655)
XLA Ops:
  0.6 1.8 %shard_map.139 = (f32[2,128,128]{2,1,0:T(8,128)}, f32[2,128,128]{2,1,0:T(8,128)}, f32[2,128,128]{2,1,0:T(8,128)}, bf16[272,128]{1,0:T(8,128)(2,1)}) custom-call(s32[2]{0:T(128)} %refs_0_.3, s32[2]{0:T(128)} %refs_1_.4, s32[1,2]{1,0:T(1,128)} %refs_2_.2, f32[2,128,128]{2,1,0:T(8,128)} %bitcast.27, s32[1,256]{1,0:T(1,128)} %bitcast.29), custom_call_target="tpu_custom_call" | custom-call | flops 1000 | bytes 1388544 | tf_op jit(solution)/shard_map/pallas_call | solution.py:451
  2.5 3.0 %collective-permute-start.1 = (f32[2,128,128]{2,1,0:T(8,128)}, f32[2,128,128]{2,1,0:T(8,128)S(1)}, u32[]{:S(2)}, u32[]{:S(2)}) collective-permute-start(f32[2,128,128]{2,1,0:T(8,128)} %get-tuple-element.34), channel_id=1, source_target_pairs={{0,4},{4,8},{8,12},{12,16},{16,20},{20,24},{24,28},{28,0},{1,5},{5... | collective-permute-start | bytes 393224 | tf_op jit(solution)/shard_map/ppermute | solution.py:30
  5.5 3.1 %collective-permute-start.2 = (f32[2,128,128]{2,1,0:T(8,128)}, f32[2,128,128]{2,1,0:T(8,128)S(1)}, u32[]{:S(2)}, u32[]{:S(2)}) collective-permute-start(f32[2,128,128]{2,1,0:T(8,128)} %get-tuple-element.35), channel_id=1, source_target_pairs={{0,28},{4,0},{8,4},{12,8},{16,12},{20,16},{24,20},{28,24},{1,29},{... | collective-permute-start | bytes 393224 | tf_op jit(solution)/shard_map/ppermute | solution.py:30
  8.6 1.0 %copy-done.3 = f32[8,128,128]{2,1,0:T(8,128)S(1)} copy-done((f32[8,128,128]{2,1,0:T(8,128)S(1)}, f32[8,128,128]{2,1,0:T(8,128)}, u32[]{:S(2)}) %copy-start.3) | copy-done | bytes 524312
  9.6 0.9 %copy-done.5 = f32[2,128,128]{2,1,0:T(8,128)S(1)} copy-done((f32[2,128,128]{2,1,0:T(8,128)S(1)}, f32[2,128,128]{2,1,0:T(8,128)}, u32[]{:S(2)}) %copy-start.5) | copy-done | bytes 131096
  11.2 0.8 concatenate.3.refs_0_.refs_1_.refs_5_
  12.0 0.3 collective-permute-done.1.refs_2_
  12.3 1.1 %collective-permute-done.2.refs_3_ = f32[2,128,128]{2,1,0:T(8,128)S(1)} collective-permute-done((f32[2,128,128]{2,1,0:T(8,128)}, f32[2,128,128]{2,1,0:T(8,128)S(1)}, u32[]{:S(2)}, u32[]{:S(2)}) %collective-permute-start.2) | collective-permute-done | bytes 131104 | tf_op jit(solution)/shard_map/ppermute | solution.py:30
  13.5 1.2 %shard_map.141 = (f32[2,128,128]{2,1,0:T(8,128)S(1)}, f32[2,128,128]{2,1,0:T(8,128)S(1)}, f32[2,128,128]{2,1,0:T(8,128)S(1)}, bf16[256,128]{1,0:T(8,128)(2,1)S(1)}) custom-call(s32[23]{0:T(128)S(1)} %concatenate.3.refs_0_.refs_1_.refs_5_, f32[2,128,128]{2,1,0:T(8,128)S(1)} %get-tuple-element.33.refs_1_.refs_0_, ...), custom_call_target="tpu_custom_call" | custom-call | flops 201326592 | bytes 1376256 | tf_op jit(solution)/shard_map/pallas_call | solution.py:490
  14.7 0.3 collective-permute-start.4
  15.0 4.4 %collective-permute-start.5 = (f32[2,128,128]{2,1,0:T(8,128)S(1)}, f32[2,128,128]{2,1,0:T(8,128)S(1)}, u32[]{:S(2)}, u32[]{:S(2)}) collective-permute-start(f32[2,128,128]{2,1,0:T(8,128)S(1)} %get-tuple-element.40), channel_id=1, source_target_pairs={{0,28},{4,0},{8,4},{12,8},{16,12},{20,16},{24,20},{28,24},{1,29},{... | collective-permute-start | bytes 393224 | tf_op jit(solution)/shard_map/ppermute | solution.py:30
  19.4 0.0 collective-permute-start.6
  19.4 1.5 %collective-permute-start = (bf16[272,128]{1,0:T(8,128)(2,1)S(1)}, bf16[272,128]{1,0:T(8,128)(2,1)S(1)}, u32[]{:S(2)}, u32[]{:S(2)}) collective-permute-start(bf16[272,128]{1,0:T(8,128)(2,1)S(1)} %copy-done.4), channel_id=1, source_target_pairs={{0,2},{1,3},{2,0},{3,1},{4,6},{5,7},{6,4},{7,5},{8,10},{9,11},{10,... | collective-permute-start | bytes 208904 | tf_op jit(solution)/shard_map/ppermute | solution.py:35
  20.9 1.4 %copy-done.1 = bf16[4096,172]{0,1:T(8,128)(2,1)S(1)} copy-done((bf16[4096,172]{0,1:T(8,128)(2,1)S(1)}, bf16[4096,172]{0,1:T(8,128)(2,1)}, u32[]{:S(2)}) %copy-start.1) | copy-done | bytes 1409048
  22.3 0.6 shard_map.142.refs_0_.refs_3_
  22.9 0.6 collective-permute-start.3
  23.5 0.0 collective-permute-done.4.refs_3_
  23.5 0.1 collective-permute-done.5.refs_4_
  23.6 1.8 %shard_map.143 = (f32[2,128,128]{2,1,0:T(8,128)S(1)}, f32[2,128,128]{2,1,0:T(8,128)S(1)}, f32[2,128,128]{2,1,0:T(8,128)S(1)}, bf16[256,128]{1,0:T(8,128)(2,1)}) custom-call(f32[172,256]{1,0:T(8,128)S(1)} %shard_map.142.refs_0_.refs_3_, s32[23]{0:T(128)S(1)} %concatenate.3.refs_0_.refs_1_.refs_5_, f32[2,128,128]{2,1,0:T(8,128)S(1)} %get-tuple-element.38.refs_2_.refs_0_, ...), custom_call_target="tpu_custom_call" | custom-call | flops 201326592 | bytes 1376256 | tf_op jit(solution)/shard_map/pallas_call | solution.py:490
  25.4 0.0 collective-permute-start.10
  25.4 4.7 %collective-permute-start.11 = (f32[2,128,128]{2,1,0:T(8,128)S(1)}, f32[2,128,128]{2,1,0:T(8,128)S(1)}, u32[]{:S(2)}, u32[]{:S(2)}) collective-permute-start(f32[2,128,128]{2,1,0:T(8,128)S(1)} %get-tuple-element.43), channel_id=1, source_target_pairs={{0,28},{4,0},{8,4},{12,8},{16,12},{20,16},{24,20},{28,24},{1,29},{... | collective-permute-start | bytes 393224 | tf_op jit(solution)/shard_map/ppermute | solution.py:30
  30.2 0.5 collective-permute-start.8
  30.7 0.0 collective-permute-done.3.refs_1_.refs_3_
  30.7 0.1 collective-permute-start.9
  30.8 0.6 shard_map.144.refs_5_
  31.4 0.1 collective-permute-done.7.refs_4_.refs_2_
  31.4 0.4 shard_map.146.refs_1_.refs_5_
  31.8 0.6 shard_map.145.refs_0_.refs_1_
  32.4 0.0 collective-permute-done.8.refs_2_.refs_3_
  32.4 1.1 %collective-permute-done.10.refs_7_ = f32[2,128,128]{2,1,0:T(8,128)S(1)} collective-permute-done((f32[2,128,128]{2,1,0:T(8,128)S(1)}, f32[2,128,128]{2,1,0:T(8,128)S(1)}, u32[]{:S(2)}, u32[]{:S(2)}) %collective-permute-start.10) | collective-permute-done | bytes 131104 | tf_op jit(solution)/shard_map/ppermute | solution.py:30
  33.5 1.0 %collective-permute-done.11.refs_8_ = f32[2,128,128]{2,1,0:T(8,128)S(1)} collective-permute-done((f32[2,128,128]{2,1,0:T(8,128)S(1)}, f32[2,128,128]{2,1,0:T(8,128)S(1)}, u32[]{:S(2)}, u32[]{:S(2)}) %collective-permute-start.11) | collective-permute-done | bytes 131104 | tf_op jit(solution)/shard_map/ppermute | solution.py:30
  34.6 1.2 %shard_map.147.refs_0_.refs_4_ = bf16[256,256]{1,0:T(8,128)(2,1)S(1)} custom-call(f32[172,256]{1,0:T(8,128)S(1)} %shard_map.145.refs_0_.refs_1_, s32[1,256]{1,0:T(1,128)S(1)} %shard_map.146.refs_1_.refs_5_, bf16[256,128]{1,0:T(8,128)(2,1)S(1)} %collective-permute-done.8.refs_2_.refs_3_, bf16[256,128]{1,0:T(8,128)(2,1)S(1)} %collective-permute-done.3.refs_1_.refs_3_, ...), custom_call_target="tpu_custom_call" | custom-call | flops 201326592 | bytes 393216 | tf_op jit(solution)/shard_map/pallas_call | solution.py:517
  35.8 0.1 collective-permute-start.15
  35.8 0.8 %shard_map.148.refs_6_.refs_0_ = bf16[192,256]{1,0:T(8,128)(2,1)S(1)} custom-call(bf16[256,256]{1,0:T(8,128)(2,1)S(1)} %shard_map.147.refs_0_.refs_4_, f32[172,256]{1,0:T(8,128)S(1)} %shard_map.145.refs_0_.refs_1_, bf16[4,128,1024]{2,1,0:T(8,128)(2,1)S(1)} %copy-done, bf16[172,4096]{1,0:T(8,128)(2,1)S(1)} %bitcast.25, s32[1,256]{1,0:T(1,128)S(1)} %copy-done.6, ...), custom_call_target="tpu_custom_call" | custom-call | flops 157286400 | bytes 294912 | tf_op jit(solution)/shard_map/pallas_call | solution.py:525
  36.7 0.5 collective-permute-start.12
  37.2 1.5 %collective-permute-start.14 = (bf16[256,256]{1,0:T(8,128)(2,1)S(1)}, bf16[256,256]{1,0:T(8,128)(2,1)S(1)}, u32[]{:S(2)}, u32[]{:S(2)}) collective-permute-start(bf16[256,256]{1,0:T(8,128)(2,1)S(1)} %shard_map.147.refs_0_.refs_4_), channel_id=1, source_target_pairs={{0,2},{1,3},{2,0},{3,1},{4,6},{5,7},{6,4},{7,5},{8,10},{9,11},{10,... | collective-permute-start | bytes 393224 | tf_op jit(solution)/shard_map/ppermute | solution.py:35
  38.7 0.5 collective-permute-start.13
  39.2 0.3 shard_map.149
  39.5 1.8 %shard_map.150.refs_0_ = f32[8,304,128]{2,1,0:T(8,128)S(1)} custom-call(bf16[272,128]{1,0:T(8,128)(2,1)S(1)} %copy-done.4, bf16[272,128]{1,0:T(8,128)(2,1)S(1)} %collective-permute-done.6.refs_2_.refs_1_, bf16[256,128]{1,0:T(8,128)(2,1)S(1)} %get-tuple-element.37.refs_2_, bf16[256,128]{1,0:T(8,128)(2,1)S(1)} %collective-permute-done.8.refs_2_.refs_3_, ...), custom_call_target="tpu_custom_call" | custom-call | flops 771751936 | bytes 3735552 | tf_op jit(solution)/shard_map/pallas_call | solution.py:541
  41.3 3.5 %collective-permute-done.13.refs_2_.refs_7_ = bf16[192,256]{1,0:T(8,128)(2,1)S(1)} collective-permute-done((bf16[192,256]{1,0:T(8,128)(2,1)S(1)}, bf16[192,256]{1,0:T(8,128)(2,1)S(1)}, u32[]{:S(2)}, u32[]{:S(2)}) %collective-permute-start.13) | collective-permute-done | bytes 98336 | tf_op jit(solution)/shard_map/ppermute | solution.py:35
  44.7 0.5 collective-permute-start.16
  45.2 1.0 %collective-permute-done.16.refs_3_.refs_8_ = bf16[192,256]{1,0:T(8,128)(2,1)S(1)} collective-permute-done((bf16[192,256]{1,0:T(8,128)(2,1)S(1)}, bf16[192,256]{1,0:T(8,128)(2,1)S(1)}, u32[]{:S(2)}, u32[]{:S(2)}) %collective-permute-start.16) | collective-permute-done | bytes 98336 | tf_op jit(solution)/shard_map/ppermute | solution.py:35
  46.2 1.8 %shard_map.152 = (f32[304,128]{1,0:T(8,128)S(1)}, f32[304,128]{1,0:T(8,128)S(1)}, f32[304,128]{1,0:T(8,128)S(1)}, f32[304,128]{1,0:T(8,128)S(1)}, bf16[2,304,128...) custom-call(f32[8,304,128]{2,1,0:T(8,128)S(1)} %shard_map.150.refs_0_, ...), custom_call_target="tpu_custom_call" | custom-call | flops 771751936 | bytes 2801664 | tf_op jit(solution)/shard_map/pallas_call | solution.py:570
  48.0 0.1 collective-permute-start.18
  48.1 6.2 %collective-permute-done.18 = bf16[2,304,128]{2,1,0:T(8,128)(2,1)S(1)} collective-permute-done((bf16[2,304,128]{2,1,0:T(8,128)(2,1)S(1)}, bf16[2,304,128]{2,1,0:T(8,128)(2,1)S(1)}, u32[]{:S(2)}, u32[]{:S(2)}) %collective-permute-start.18) | collective-permute-done | bytes 155680 | tf_op jit(solution)/shard_map/ppermute | solution.py:35
  54.4 0.3 collective-permute-start.19
  54.7 3.6 %collective-permute-start.20 = (bf16[304,128]{1,0:T(8,128)(2,1)S(1)}, bf16[304,128]{1,0:T(8,128)(2,1)S(1)}, u32[]{:S(2)}, u32[]{:S(2)}) collective-permute-start(bf16[304,128]{1,0:T(8,128)(2,1)S(1)} %get-tuple-element.59), channel_id=1, source_target_pairs={{0,24},{4,28},{8,16},{12,20},{16,8},{20,12},{24,0},{28,4},{1,25},{... | collective-permute-start | bytes 233480 | tf_op jit(solution)/shard_map/ppermute | solution.py:35
  58.3 1.5 %collective-permute-done.19 = bf16[2,304,128]{2,1,0:T(8,128)(2,1)S(1)} collective-permute-done((bf16[2,304,128]{2,1,0:T(8,128)(2,1)S(1)}, bf16[2,304,128]{2,1,0:T(8,128)(2,1)S(1)}, u32[]{:S(2)}, u32[]{:S(2)}) %collective-permute-start.19) | collective-permute-done | bytes 155680 | tf_op jit(solution)/shard_map/ppermute | solution.py:35
  59.8 1.5 %collective-permute-start.22 = (bf16[304,128]{1,0:T(8,128)(2,1)S(1)}, bf16[304,128]{1,0:T(8,128)(2,1)S(1)}, u32[]{:S(2)}, u32[]{:S(2)}) collective-permute-start(bf16[304,128]{1,0:T(8,128)(2,1)S(1)} %fusion), channel_id=1, source_target_pairs={{0,8},{4,12},{8,0},{12,4},{16,24},{20,28},{24,16},{28,20},{1,9},{5... | collective-permute-start | bytes 233480 | tf_op jit(solution)/shard_map/ppermute | solution.py:35
  61.3 3.3 %collective-permute-done.21 = bf16[304,128]{1,0:T(8,128)(2,1)S(1)} collective-permute-done((bf16[304,128]{1,0:T(8,128)(2,1)S(1)}, bf16[304,128]{1,0:T(8,128)(2,1)S(1)}, u32[]{:S(2)}, u32[]{:S(2)}) %collective-permute-start.21) | collective-permute-done | bytes 77856 | tf_op jit(solution)/shard_map/ppermute | solution.py:35
  64.7 0.6 collective-permute-done.22
  65.3 0.1 fusion.6.refs_0_
  65.4 2.2 %collective-permute-start.25 = (bf16[304,128]{1,0:T(8,128)(2,1)S(1)}, bf16[304,128]{1,0:T(8,128)(2,1)S(1)}, u32[]{:S(2)}, u32[]{:S(2)}) collective-permute-start(bf16[304,128]{1,0:T(8,128)(2,1)S(1)} %fusion.6.refs_0_), channel_id=1, source_target_pairs={{0,24},{4,28},{8,16},{12,20},{16,8},{20,12},{24,0},{28,4},{1,25},{... | collective-permute-start | bytes 233480 | tf_op jit(solution)/shard_map/ppermute | solution.py:35
  67.6 2.2 %collective-permute-start.23 = (bf16[304,128]{1,0:T(8,128)(2,1)S(1)}, bf16[304,128]{1,0:T(8,128)(2,1)S(1)}, u32[]{:S(2)}, u32[]{:S(2)}) collective-permute-start(bf16[304,128]{1,0:T(8,128)(2,1)S(1)} %fusion.6.refs_0_), channel_id=1, source_target_pairs={{0,8},{4,12},{8,0},{12,4},{16,24},{20,28},{24,16},{28,20},{1,9},{5... | collective-permute-start | bytes 233480 | tf_op jit(solution)/shard_map/ppermute | solution.py:35
  69.8 1.0 %collective-permute-start.26 = (bf16[304,128]{1,0:T(8,128)(2,1)S(1)}, bf16[304,128]{1,0:T(8,128)(2,1)S(1)}, u32[]{:S(2)}, u32[]{:S(2)}) collective-permute-start(bf16[304,128]{1,0:T(8,128)(2,1)S(1)} %fusion.6.refs_0_), channel_id=1, source_target_pairs={{0,4},{4,0},{8,12},{12,8},{16,20},{20,16},{24,28},{28,24},{1,5},{5... | collective-permute-start | bytes 233480 | tf_op jit(solution)/shard_map/ppermute | solution.py:35
  70.8 1.0 %collective-permute-done.25.refs_3_ = bf16[304,128]{1,0:T(8,128)(2,1)S(1)} collective-permute-done((bf16[304,128]{1,0:T(8,128)(2,1)S(1)}, bf16[304,128]{1,0:T(8,128)(2,1)S(1)}, u32[]{:S(2)}, u32[]{:S(2)}) %collective-permute-start.25) | collective-permute-done | bytes 77856 | tf_op jit(solution)/shard_map/ppermute | solution.py:35
  71.8 1.2 %collective-permute-start.29 = (bf16[304,128]{1,0:T(8,128)(2,1)S(1)}, bf16[304,128]{1,0:T(8,128)(2,1)S(1)}, u32[]{:S(2)}, u32[]{:S(2)}) collective-permute-start(bf16[304,128]{1,0:T(8,128)(2,1)S(1)} %collective-permute-done.25.refs_3_), channel_id=1, source_target_pairs={{0,4},{4,0},{8,12},{12,8},{16,20},{20,16},{24,28},{28,24},{1,5},{5... | collective-permute-start | bytes 233480 | tf_op jit(solution)/shard_map/ppermute | solution.py:35
  73.0 1.3 %collective-permute-done.24.refs_2_ = bf16[304,128]{1,0:T(8,128)(2,1)S(1)} collective-permute-done((bf16[304,128]{1,0:T(8,128)(2,1)S(1)}, bf16[304,128]{1,0:T(8,128)(2,1)S(1)}, u32[]{:S(2)}, u32[]{:S(2)}) %collective-permute-start.24) | collective-permute-done | bytes 77856 | tf_op jit(solution)/shard_map/ppermute | solution.py:35
  74.3 1.0 %collective-permute-start.28 = (bf16[304,128]{1,0:T(8,128)(2,1)S(1)}, bf16[304,128]{1,0:T(8,128)(2,1)S(1)}, u32[]{:S(2)}, u32[]{:S(2)}) collective-permute-start(bf16[304,128]{1,0:T(8,128)(2,1)S(1)} %collective-permute-done.24.refs_2_), channel_id=1, source_target_pairs={{0,4},{4,0},{8,12},{12,8},{16,20},{20,16},{24,28},{28,24},{1,5},{5... | collective-permute-start | bytes 233480 | tf_op jit(solution)/shard_map/ppermute | solution.py:35
  75.3 1.0 %collective-permute-start.27 = (bf16[304,128]{1,0:T(8,128)(2,1)S(1)}, bf16[304,128]{1,0:T(8,128)(2,1)S(1)}, u32[]{:S(2)}, u32[]{:S(2)}) collective-permute-start(bf16[304,128]{1,0:T(8,128)(2,1)S(1)} %collective-permute-done.23.refs_1_), channel_id=1, source_target_pairs={{0,4},{4,0},{8,12},{12,8},{16,20},{20,16},{24,28},{28,24},{1,5},{5... | collective-permute-start | bytes 233480 | tf_op jit(solution)/shard_map/ppermute | solution.py:35
  76.3 0.8 %shard_map.151 = f32[1,256]{1,0:T(1,128)} custom-call(bf16[192,256]{1,0:T(8,128)(2,1)S(1)} %shard_map.148.refs_6_.refs_0_, bf16[192,256]{1,0:T(8,128)(2,1)S(1)} %collective-permute-done.12.refs_7_.refs_1_, bf16[192,256]{1,0:T(8,128)(2,1)S(1)} %collective-permute-done.13.refs_2_.refs_7_, bf16[192,256]{1,0:T(8,128)(2,1)S(1)} %collective-permute-done.16.refs_3_.refs_8_), custom_call_target="tpu_custom_call" | custom-call | flops 1000 | bytes 3072 | tf_op jit(solution)/shard_map/pallas_call | solution.py:558
  77.1 1.7 %collective-permute-done.28.refs_6_ = bf16[304,128]{1,0:T(8,128)(2,1)S(1)} collective-permute-done((bf16[304,128]{1,0:T(8,128)(2,1)S(1)}, bf16[304,128]{1,0:T(8,128)(2,1)S(1)}, u32[]{:S(2)}, u32[]{:S(2)}) %collective-permute-start.28) | collective-permute-done | bytes 77856 | tf_op jit(solution)/shard_map/ppermute | solution.py:35
  78.8 0.9 %collective-permute-done.27.refs_5_ = bf16[304,128]{1,0:T(8,128)(2,1)S(1)} collective-permute-done((bf16[304,128]{1,0:T(8,128)(2,1)S(1)}, bf16[304,128]{1,0:T(8,128)(2,1)S(1)}, u32[]{:S(2)}, u32[]{:S(2)}) %collective-permute-start.27) | collective-permute-done | bytes 77856 | tf_op jit(solution)/shard_map/ppermute | solution.py:35
  79.7 1.2 %shard_map.153 = (f32[4,128,256]{2,1,0:T(8,128)}, f32[172,1024]{1,0:T(8,128)}) custom-call(bf16[304,128]{1,0:T(8,128)(2,1)S(1)} %fusion.6.refs_0_, bf16[304,128]{1,0:T(8,128)(2,1)S(1)} %collective-permute-done.23.refs_1_, bf16[304,128]{1,0:T(8,128)(2,1)S(1)} %collective-permute-done.24.refs_2_, bf16[304,128]{1,0:T(8,128)(2,1)S(1)} %collective-permute-done.25.refs_3_, ...), custom_call_target="tpu_custom_call" | custom-call | flops 1000 | bytes 3686400 | tf_op jit(solution)/shard_map/pallas_call | solution.py:599
  (29 shorter events, 0.2 us)
Async XLA Ops:
  0.6 20.3 %copy-start = (bf16[4,128,1024]{2,1,0:T(8,128)(2,1)S(1)}, bf16[4,128,1024]{2,1,0:T(8,128)(2,1)}, u32[]{:S(2)}) copy-start(bf16[4,128,1024]{2,1,0:T(8,128)(2,1)} %refs_9_.1) | copy-start | bytes 3145732
  2.5 9.9 %collective-permute-start.1 = (f32[2,128,128]{2,1,0:T(8,128)}, f32[2,128,128]{2,1,0:T(8,128)S(1)}, u32[]{:S(2)}, u32[]{:S(2)}) collective-permute-start(f32[2,128,128]{2,1,0:T(8,128)} %get-tuple-element.34), channel_id=1, source_target_pairs={{0,4},{4,8},{8,12},{12,16},{16,20},{20,24},{24,28},{28,0},{1,5},{5... | collective-permute-start | bytes 393224 | tf_op jit(solution)/shard_map/ppermute | solution.py:30
  5.5 8.0 %collective-permute-start.2 = (f32[2,128,128]{2,1,0:T(8,128)}, f32[2,128,128]{2,1,0:T(8,128)S(1)}, u32[]{:S(2)}, u32[]{:S(2)}) collective-permute-start(f32[2,128,128]{2,1,0:T(8,128)} %get-tuple-element.35), channel_id=1, source_target_pairs={{0,28},{4,0},{8,4},{12,8},{16,12},{20,16},{24,20},{28,24},{1,29},{... | collective-permute-start | bytes 393224 | tf_op jit(solution)/shard_map/ppermute | solution.py:30
  8.6 1.0 %copy-start.3 = (f32[8,128,128]{2,1,0:T(8,128)S(1)}, f32[8,128,128]{2,1,0:T(8,128)}, u32[]{:S(2)}) copy-start(f32[8,128,128]{2,1,0:T(8,128)} %refs_1_.5) | copy-start | bytes 1572868
  9.6 0.9 %copy-start.5 = (f32[2,128,128]{2,1,0:T(8,128)S(1)}, f32[2,128,128]{2,1,0:T(8,128)}, u32[]{:S(2)}) copy-start(f32[2,128,128]{2,1,0:T(8,128)} %get-tuple-element.32.refs_0_) | copy-start | bytes 393220
  10.5 8.9 %copy-start.4 = (bf16[272,128]{1,0:T(8,128)(2,1)S(1)}, bf16[272,128]{1,0:T(8,128)(2,1)}, u32[]{:S(2)}) copy-start(bf16[272,128]{1,0:T(8,128)(2,1)} %get-tuple-element.31.refs_1_.refs_0_) | copy-start | bytes 208900
  14.7 8.8 %collective-permute-start.4 = (f32[2,128,128]{2,1,0:T(8,128)S(1)}, f32[2,128,128]{2,1,0:T(8,128)S(1)}, u32[]{:S(2)}, u32[]{:S(2)}) collective-permute-start(f32[2,128,128]{2,1,0:T(8,128)S(1)} %get-tuple-element.39), channel_id=1, source_target_pairs={{0,4},{4,8},{8,12},{12,16},{16,20},{20,24},{24,28},{28,0},{1,5},{5... | collective-permute-start | bytes 393224 | tf_op jit(solution)/shard_map/ppermute | solution.py:30
  15.0 8.6 %collective-permute-start.5 = (f32[2,128,128]{2,1,0:T(8,128)S(1)}, f32[2,128,128]{2,1,0:T(8,128)S(1)}, u32[]{:S(2)}, u32[]{:S(2)}) collective-permute-start(f32[2,128,128]{2,1,0:T(8,128)S(1)} %get-tuple-element.40), channel_id=1, source_target_pairs={{0,28},{4,0},{8,4},{12,8},{16,12},{20,16},{24,20},{28,24},{1,29},{... | collective-permute-start | bytes 393224 | tf_op jit(solution)/shard_map/ppermute | solution.py:30
  19.4 10.7 %collective-permute-start.6 = (bf16[272,128]{1,0:T(8,128)(2,1)S(1)}, bf16[272,128]{1,0:T(8,128)(2,1)S(1)}, u32[]{:S(2)}, u32[]{:S(2)}) collective-permute-start(bf16[272,128]{1,0:T(8,128)(2,1)S(1)} %copy-done.4), channel_id=1, source_target_pairs={{0,1},{1,0},{2,3},{3,2},{4,5},{5,4},{6,7},{7,6},{8,9},{9,8},{10,11... | collective-permute-start | bytes 208904 | tf_op jit(solution)/shard_map/ppermute | solution.py:35
  19.4 10.7 %collective-permute-start = (bf16[272,128]{1,0:T(8,128)(2,1)S(1)}, bf16[272,128]{1,0:T(8,128)(2,1)S(1)}, u32[]{:S(2)}, u32[]{:S(2)}) collective-permute-start(bf16[272,128]{1,0:T(8,128)(2,1)S(1)} %copy-done.4), channel_id=1, source_target_pairs={{0,2},{1,3},{2,0},{3,1},{4,6},{5,7},{6,4},{7,5},{8,10},{9,11},{10,... | collective-permute-start | bytes 208904 | tf_op jit(solution)/shard_map/ppermute | solution.py:35
  20.9 1.4 %copy-start.1 = (bf16[4096,172]{0,1:T(8,128)(2,1)S(1)}, bf16[4096,172]{0,1:T(8,128)(2,1)}, u32[]{:S(2)}) copy-start(bf16[4096,172]{0,1:T(8,128)(2,1)} %param.23) | copy-start | bytes 4227076
  22.3 8.5 %copy-start.2 = (bf16[4096,172]{0,1:T(8,128)(2,1)S(1)}, bf16[4096,172]{0,1:T(8,128)(2,1)}, u32[]{:S(2)}) copy-start(bf16[4096,172]{0,1:T(8,128)(2,1)} %param.23) | copy-start | bytes 4227076
  22.9 7.8 %collective-permute-start.3 = (bf16[256,128]{1,0:T(8,128)(2,1)S(1)}, bf16[256,128]{1,0:T(8,128)(2,1)S(1)}, u32[]{:S(2)}, u32[]{:S(2)}) collective-permute-start(bf16[256,128]{1,0:T(8,128)(2,1)S(1)} %get-tuple-element.37.refs_2_), channel_id=1, source_target_pairs={{0,2},{1,3},{2,0},{3,1},{4,6},{5,7},{6,4},{7,5},{8,10},{9,11},{10,... | collective-permute-start | bytes 196616 | tf_op jit(solution)/shard_map/ppermute | solution.py:35
  25.4 8.1 %collective-permute-start.10 = (f32[2,128,128]{2,1,0:T(8,128)S(1)}, f32[2,128,128]{2,1,0:T(8,128)S(1)}, u32[]{:S(2)}, u32[]{:S(2)}) collective-permute-start(f32[2,128,128]{2,1,0:T(8,128)S(1)} %get-tuple-element.42), channel_id=1, source_target_pairs={{0,4},{4,8},{8,12},{12,16},{16,20},{20,24},{24,28},{28,0},{1,5},{5... | collective-permute-start | bytes 393224 | tf_op jit(solution)/shard_map/ppermute | solution.py:30
  25.4 6.0 %copy-start.6 = (s32[1,256]{1,0:T(1,128)S(1)}, s32[1,256]{1,0:T(1,128)}, u32[]{:S(2)}) copy-start(s32[1,256]{1,0:T(1,128)} %refs_4_.1) | copy-start | bytes 3076
  25.4 9.1 %collective-permute-start.11 = (f32[2,128,128]{2,1,0:T(8,128)S(1)}, f32[2,128,128]{2,1,0:T(8,128)S(1)}, u32[]{:S(2)}, u32[]{:S(2)}) collective-permute-start(f32[2,128,128]{2,1,0:T(8,128)S(1)} %get-tuple-element.43), channel_id=1, source_target_pairs={{0,28},{4,0},{8,4},{12,8},{16,12},{20,16},{24,20},{28,24},{1,29},{... | collective-permute-start | bytes 393224 | tf_op jit(solution)/shard_map/ppermute | solution.py:30
  30.2 1.3 %collective-permute-start.7 = (bf16[272,128]{1,0:T(8,128)(2,1)S(1)}, bf16[272,128]{1,0:T(8,128)(2,1)S(1)}, u32[]{:S(2)}, u32[]{:S(2)}) collective-permute-start(bf16[272,128]{1,0:T(8,128)(2,1)S(1)} %collective-permute-done.refs_0_.refs_3_.refs_1_), channel_id=1, source_target_pairs={{0,1},{1,0},{2,3},{3,2},{4,5},{5,4},{6,7},{7,6},{8,9},{9,8},{10,11... | collective-permute-start | bytes 208904 | tf_op jit(solution)/shard_map/ppermute | solution.py:35
  30.2 2.3 %collective-permute-start.8 = (bf16[256,128]{1,0:T(8,128)(2,1)S(1)}, bf16[256,128]{1,0:T(8,128)(2,1)S(1)}, u32[]{:S(2)}, u32[]{:S(2)}) collective-permute-start(bf16[256,128]{1,0:T(8,128)(2,1)S(1)} %get-tuple-element.37.refs_2_), channel_id=1, source_target_pairs={{0,1},{1,0},{2,3},{3,2},{4,5},{5,4},{6,7},{7,6},{8,9},{9,8},{10,11... | collective-permute-start | bytes 196616 | tf_op jit(solution)/shard_map/ppermute | solution.py:35
  30.7 1.8 %collective-permute-start.9 = (bf16[256,128]{1,0:T(8,128)(2,1)S(1)}, bf16[256,128]{1,0:T(8,128)(2,1)S(1)}, u32[]{:S(2)}, u32[]{:S(2)}) collective-permute-start(bf16[256,128]{1,0:T(8,128)(2,1)S(1)} %collective-permute-done.3.refs_1_.refs_3_), channel_id=1, source_target_pairs={{0,1},{1,0},{2,3},{3,2},{4,5},{5,4},{6,7},{7,6},{8,9},{9,8},{10,11... | collective-permute-start | bytes 196616 | tf_op jit(solution)/shard_map/ppermute | solution.py:35
  35.8 3.7 %collective-permute-start.15 = (bf16[256,256]{1,0:T(8,128)(2,1)S(1)}, bf16[256,256]{1,0:T(8,128)(2,1)S(1)}, u32[]{:S(2)}, u32[]{:S(2)}) collective-permute-start(bf16[256,256]{1,0:T(8,128)(2,1)S(1)} %shard_map.147.refs_0_.refs_4_), channel_id=1, source_target_pairs={{0,1},{1,0},{2,3},{3,2},{4,5},{5,4},{6,7},{7,6},{8,9},{9,8},{10,11... | collective-permute-start | bytes 393224 | tf_op jit(solution)/shard_map/ppermute | solution.py:35
  36.7 2.8 %collective-permute-start.12 = (bf16[192,256]{1,0:T(8,128)(2,1)S(1)}, bf16[192,256]{1,0:T(8,128)(2,1)S(1)}, u32[]{:S(2)}, u32[]{:S(2)}) collective-permute-start(bf16[192,256]{1,0:T(8,128)(2,1)S(1)} %shard_map.148.refs_6_.refs_0_), channel_id=1, source_target_pairs={{0,1},{1,0},{2,3},{3,2},{4,5},{5,4},{6,7},{7,6},{8,9},{9,8},{10,11... | collective-permute-start | bytes 294920 | tf_op jit(solution)/shard_map/ppermute | solution.py:35
  37.2 7.6 %collective-permute-start.14 = (bf16[256,256]{1,0:T(8,128)(2,1)S(1)}, bf16[256,256]{1,0:T(8,128)(2,1)S(1)}, u32[]{:S(2)}, u32[]{:S(2)}) collective-permute-start(bf16[256,256]{1,0:T(8,128)(2,1)S(1)} %shard_map.147.refs_0_.refs_4_), channel_id=1, source_target_pairs={{0,2},{1,3},{2,0},{3,1},{4,6},{5,7},{6,4},{7,5},{8,10},{9,11},{10,... | collective-permute-start | bytes 393224 | tf_op jit(solution)/shard_map/ppermute | solution.py:35
  38.7 6.1 %collective-permute-start.13 = (bf16[192,256]{1,0:T(8,128)(2,1)S(1)}, bf16[192,256]{1,0:T(8,128)(2,1)S(1)}, u32[]{:S(2)}, u32[]{:S(2)}) collective-permute-start(bf16[192,256]{1,0:T(8,128)(2,1)S(1)} %shard_map.148.refs_6_.refs_0_), channel_id=1, source_target_pairs={{0,2},{1,3},{2,0},{3,1},{4,6},{5,7},{6,4},{7,5},{8,10},{9,11},{10,... | collective-permute-start | bytes 294920 | tf_op jit(solution)/shard_map/ppermute | solution.py:35
  44.7 1.5 %collective-permute-start.17 = (bf16[256,256]{1,0:T(8,128)(2,1)S(1)}, bf16[256,256]{1,0:T(8,128)(2,1)S(1)}, u32[]{:S(2)}, u32[]{:S(2)}) collective-permute-start(bf16[256,256]{1,0:T(8,128)(2,1)S(1)} %collective-permute-done.14.refs_5_), channel_id=1, source_target_pairs={{0,1},{1,0},{2,3},{3,2},{4,5},{5,4},{6,7},{7,6},{8,9},{9,8},{10,11... | collective-permute-start | bytes 393224 | tf_op jit(solution)/shard_map/ppermute | solution.py:35
  44.7 1.5 %collective-permute-start.16 = (bf16[192,256]{1,0:T(8,128)(2,1)S(1)}, bf16[192,256]{1,0:T(8,128)(2,1)S(1)}, u32[]{:S(2)}, u32[]{:S(2)}) collective-permute-start(bf16[192,256]{1,0:T(8,128)(2,1)S(1)} %collective-permute-done.13.refs_2_.refs_7_), channel_id=1, source_target_pairs={{0,1},{1,0},{2,3},{3,2},{4,5},{5,4},{6,7},{7,6},{8,9},{9,8},{10,11... | collective-permute-start | bytes 294920 | tf_op jit(solution)/shard_map/ppermute | solution.py:35
  48.0 6.3 %collective-permute-start.18 = (bf16[2,304,128]{2,1,0:T(8,128)(2,1)S(1)}, bf16[2,304,128]{2,1,0:T(8,128)(2,1)S(1)}, u32[]{:S(2)}, u32[]{:S(2)}) collective-permute-start(bf16[2,304,128]{2,1,0:T(8,128)(2,1)S(1)} %get-tuple-element.50), channel_id=1, source_target_pairs={{0,4},{4,0},{8,12},{12,8},{16,20},{20,16},{24,28},{28,24},{1,5},{5... | collective-permute-start | bytes 466952 | tf_op jit(solution)/shard_map/ppermute | solution.py:35
  54.4 5.4 %collective-permute-start.19 = (bf16[2,304,128]{2,1,0:T(8,128)(2,1)S(1)}, bf16[2,304,128]{2,1,0:T(8,128)(2,1)S(1)}, u32[]{:S(2)}, u32[]{:S(2)}) collective-permute-start(bf16[2,304,128]{2,1,0:T(8,128)(2,1)S(1)} %get-tuple-element.52), channel_id=1, source_target_pairs={{0,4},{4,0},{8,12},{12,8},{16,20},{20,16},{24,28},{28,24},{1,5},{5... | collective-permute-start | bytes 466952 | tf_op jit(solution)/shard_map/ppermute | solution.py:35
  54.7 6.6 %collective-permute-start.20 = (bf16[304,128]{1,0:T(8,128)(2,1)S(1)}, bf16[304,128]{1,0:T(8,128)(2,1)S(1)}, u32[]{:S(2)}, u32[]{:S(2)}) collective-permute-start(bf16[304,128]{1,0:T(8,128)(2,1)S(1)} %get-tuple-element.59), channel_id=1, source_target_pairs={{0,24},{4,28},{8,16},{12,20},{16,8},{20,12},{24,0},{28,4},{1,25},{... | collective-permute-start | bytes 233480 | tf_op jit(solution)/shard_map/ppermute | solution.py:35
  58.3 6.3 %collective-permute-start.21 = (bf16[304,128]{1,0:T(8,128)(2,1)S(1)}, bf16[304,128]{1,0:T(8,128)(2,1)S(1)}, u32[]{:S(2)}, u32[]{:S(2)}) collective-permute-start(bf16[304,128]{1,0:T(8,128)(2,1)S(1)} %get-tuple-element.60), channel_id=1, source_target_pairs={{0,16},{4,20},{8,24},{12,28},{16,0},{20,4},{24,8},{28,12},{1,17},{... | collective-permute-start | bytes 233480 | tf_op jit(solution)/shard_map/ppermute | solution.py:35
  59.8 5.5 %collective-permute-start.22 = (bf16[304,128]{1,0:T(8,128)(2,1)S(1)}, bf16[304,128]{1,0:T(8,128)(2,1)S(1)}, u32[]{:S(2)}, u32[]{:S(2)}) collective-permute-start(bf16[304,128]{1,0:T(8,128)(2,1)S(1)} %fusion), channel_id=1, source_target_pairs={{0,8},{4,12},{8,0},{12,4},{16,24},{20,28},{24,16},{28,20},{1,9},{5... | collective-permute-start | bytes 233480 | tf_op jit(solution)/shard_map/ppermute | solution.py:35
  65.4 6.5 %collective-permute-start.25 = (bf16[304,128]{1,0:T(8,128)(2,1)S(1)}, bf16[304,128]{1,0:T(8,128)(2,1)S(1)}, u32[]{:S(2)}, u32[]{:S(2)}) collective-permute-start(bf16[304,128]{1,0:T(8,128)(2,1)S(1)} %fusion.6.refs_0_), channel_id=1, source_target_pairs={{0,24},{4,28},{8,16},{12,20},{16,8},{20,12},{24,0},{28,4},{1,25},{... | collective-permute-start | bytes 233480 | tf_op jit(solution)/shard_map/ppermute | solution.py:35
  67.6 6.7 %collective-permute-start.24 = (bf16[304,128]{1,0:T(8,128)(2,1)S(1)}, bf16[304,128]{1,0:T(8,128)(2,1)S(1)}, u32[]{:S(2)}, u32[]{:S(2)}) collective-permute-start(bf16[304,128]{1,0:T(8,128)(2,1)S(1)} %fusion.6.refs_0_), channel_id=1, source_target_pairs={{0,16},{4,20},{8,24},{12,28},{16,0},{20,4},{24,8},{28,12},{1,17},{... | collective-permute-start | bytes 233480 | tf_op jit(solution)/shard_map/ppermute | solution.py:35
  67.6 7.7 %collective-permute-start.23 = (bf16[304,128]{1,0:T(8,128)(2,1)S(1)}, bf16[304,128]{1,0:T(8,128)(2,1)S(1)}, u32[]{:S(2)}, u32[]{:S(2)}) collective-permute-start(bf16[304,128]{1,0:T(8,128)(2,1)S(1)} %fusion.6.refs_0_), channel_id=1, source_target_pairs={{0,8},{4,12},{8,0},{12,4},{16,24},{20,28},{24,16},{28,20},{1,9},{5... | collective-permute-start | bytes 233480 | tf_op jit(solution)/shard_map/ppermute | solution.py:35
  69.8 7.3 %collective-permute-start.26 = (bf16[304,128]{1,0:T(8,128)(2,1)S(1)}, bf16[304,128]{1,0:T(8,128)(2,1)S(1)}, u32[]{:S(2)}, u32[]{:S(2)}) collective-permute-start(bf16[304,128]{1,0:T(8,128)(2,1)S(1)} %fusion.6.refs_0_), channel_id=1, source_target_pairs={{0,4},{4,0},{8,12},{12,8},{16,20},{20,16},{24,28},{28,24},{1,5},{5... | collective-permute-start | bytes 233480 | tf_op jit(solution)/shard_map/ppermute | solution.py:35
  71.8 5.3 %collective-permute-start.29 = (bf16[304,128]{1,0:T(8,128)(2,1)S(1)}, bf16[304,128]{1,0:T(8,128)(2,1)S(1)}, u32[]{:S(2)}, u32[]{:S(2)}) collective-permute-start(bf16[304,128]{1,0:T(8,128)(2,1)S(1)} %collective-permute-done.25.refs_3_), channel_id=1, source_target_pairs={{0,4},{4,0},{8,12},{12,8},{16,20},{20,16},{24,28},{28,24},{1,5},{5... | collective-permute-start | bytes 233480 | tf_op jit(solution)/shard_map/ppermute | solution.py:35
  74.3 4.5 %collective-permute-start.28 = (bf16[304,128]{1,0:T(8,128)(2,1)S(1)}, bf16[304,128]{1,0:T(8,128)(2,1)S(1)}, u32[]{:S(2)}, u32[]{:S(2)}) collective-permute-start(bf16[304,128]{1,0:T(8,128)(2,1)S(1)} %collective-permute-done.24.refs_2_), channel_id=1, source_target_pairs={{0,4},{4,0},{8,12},{12,8},{16,20},{20,16},{24,28},{28,24},{1,5},{5... | collective-permute-start | bytes 233480 | tf_op jit(solution)/shard_map/ppermute | solution.py:35
  75.3 4.4 %collective-permute-start.27 = (bf16[304,128]{1,0:T(8,128)(2,1)S(1)}, bf16[304,128]{1,0:T(8,128)(2,1)S(1)}, u32[]{:S(2)}, u32[]{:S(2)}) collective-permute-start(bf16[304,128]{1,0:T(8,128)(2,1)S(1)} %collective-permute-done.23.refs_1_), channel_id=1, source_target_pairs={{0,4},{4,0},{8,12},{12,8},{16,20},{20,16},{24,28},{28,24},{1,5},{5... | collective-permute-start | bytes 233480 | tf_op jit(solution)/shard_map/ppermute | solution.py:35

commit v8 on v7

--- a/solution.py
+++ b/solution.py
@@ -58,7 +58,7 @@
         scratch_shapes=list(scratch),
         compiler_params=pltpu.CompilerParams(vmem_limit_bytes=limit),
         cost_estimate=pl.CostEstimate(
-            flops=flops, bytes_accessed=3 * moved, transcendentals=0
+            flops=flops, bytes_accessed=3 * moved if flops > 1000 else 1000, transcendentals=0
         ),
     )
     return functools.partial(made, *after)
@@ -164,9 +164,9 @@
 
 
 def hop_kernel(
-    plan, plan_ref, cur_ref, low_ref, high_ref, tiles_ref,
-    next_ref, left_ref, right_ref, b_ref, ext_ref,
+    plan, plan_ref, cur_ref, low_ref, high_ref, tiles_ref, next_ref, left_ref, right_ref, *refs
 ):
+    ext_ref = refs[-1]
     extend(cur_ref, low_ref, high_ref, ext_ref)
     blocks = next_blocks(plan, plan_ref, cur_ref, tiles_ref, ext_ref)
     write_sends(
@@ -178,12 +178,14 @@
     )
     for number, block in enumerate(blocks):
         next_ref[number] = block
-    write_rows(blocks, b_ref)
-
-
-def ready_kernel(cur_ref, tiles_ref, cur_out, tiles_out):
+    for b_ref in refs[:-1]:
+        write_rows(blocks, b_ref)
+
+
+def ready_kernel(cur_ref, tiles_ref, wc_ref, cur_out, tiles_out, wc_out):
     cur_out[...] = cur_ref[...]
     tiles_out[...] = tiles_ref[...]
+    wc_out[...] = wc_ref[...]
 
 
 def branch_logits(branch, rows, w_ref, wc_ref):
@@ -362,7 +364,7 @@
 
 
 def late_kernel(kept, members, half, early_ref, *refs):
-    ins = len(refs) - 1 - half - half // 2
+    ins = len(refs) - 2 - half
     outs = refs[ins:-1]
     chunks_ref = refs[-1]
     late_chunks(kept, members, early_ref, refs[:ins], chunks_ref)
@@ -370,7 +372,7 @@
     for step in range(half):
         stays = dom ^ (2 * step)
         outs[step][...] = chunks_ref[stays]
-        outs[half + step // 2][step % 2] = chunks_ref[stays ^ 1].astype(BF16)
+        outs[half][step] = chunks_ref[stays ^ 1].astype(BF16)
 
 
 def plain_late_kernel(kept, members, early_ref, *refs):
@@ -448,7 +450,7 @@
     hop_flops = 12 * tiles * block * block * width
     forward_flops = 2 * nodes * hid * (width + classes)
     ext = pltpu.VMEM((local + 2 * slots, block, width), F32)
-    to_left, to_right, current, rows = call(
+    to_left, to_right, current, *rows = call(
         first_kernel,
         [slots_f32, slots_f32, blocks_f32, first_b16],
         [ANYWHERE] * 5,
@@ -462,17 +464,21 @@
         ],
         limit=VMEM_ALL,
     )(send_left, send_right, send_count, current, labels.reshape(1, nodes))
-    current, tile_values = call(
+    current, tile_values, w_class_t = call(
         ready_kernel,
-        [blocks_f32, jax.ShapeDtypeStruct(tile_values.shape, F32)],
-        [IN_VMEM] * 2,
+        [
+            blocks_f32,
+            jax.ShapeDtypeStruct(tile_values.shape, F32),
+            jax.ShapeDtypeStruct(w_class_t.shape, BF16),
+        ],
+        [IN_VMEM] * 3,
         1000,
-    )(current, tile_values)
+    )(current, tile_values, w_class_t)
     for hop in range(HOPS):
         from_lower = passed_along(to_right, "dom", 1)
         from_upper = passed_along(to_left, "dom", -1)
-        if hop < HOPS - 1:
-            gathered.append(in_group(rows))
+        for value in rows:
+            gathered.append(in_group(value))
         before = [] if logits is None else [logits]
         logits = call(
             functools.partial(forward_kernel, hop),
@@ -487,9 +493,9 @@
         else:
             after = [first_logits]
         if hop < HOPS - 1:
-            current, to_left, to_right, rows = call(
+            current, to_left, to_right, *rows = call(
                 functools.partial(hop_kernel, plan),
-                [blocks_f32, slots_f32, slots_f32, rows_b16],
+                [blocks_f32, slots_f32, slots_f32] + [rows_b16] * (hop < HOPS - 2),
                 [IN_SMEM] + [IN_VMEM] * 4,
                 hop_flops,
                 [ext],
@@ -526,7 +532,7 @@
         functools.partial(loss_and_gradient_kernel, row_scale),
         jax.ShapeDtypeStruct((kept + 16, nodes), BF16),
         [IN_VMEM] * 6,
-        forward_flops,
+        1000,
     )(last_rows, logits, w_branch, w_class_t, batch_order, label_mine)
     chunks = own_class // LANES
     height = kept + width
@@ -542,7 +548,7 @@
         functools.partial(early_kernel, kept, ahead),
         chunks_f32,
         [IN_VMEM] * (4 * ahead + 3),
-        grad_flops,
+        1000,
     )(
         *[member for members in gathered for member in members[:ahead]],
         *close_rows, *close, *weights,
@@ -563,27 +569,19 @@
         jax.ShapeDtypeStruct((branches, width, own), F32),
         jax.ShapeDtypeStruct((classes, own_class), F32),
     ]
-    if chunks == dom and dom % 4 == 0 and dom & (dom - 1) == 0:
+    if chunks == dom and dom % 2 == 0 and dom & (dom - 1) == 0:
         half = dom // 2
         one_f32 = jax.ShapeDtypeStruct((height, LANES), F32)
-        two_b16 = jax.ShapeDtypeStruct((2, height, LANES), BF16)
         made = call(
             functools.partial(late_kernel, kept, ahead, half),
-            [one_f32] * half + [two_b16] * (half // 2),
+            [one_f32] * half + [jax.ShapeDtypeStruct((half, height, LANES), BF16)],
             [IN_VMEM] * len(late_ins),
             grad_flops,
             [pltpu.VMEM(chunks_f32.shape, F32)],
         )(*late_ins)
         order = list(range(half - 1, -1, -1))
-        arrived = {}
-        for pair in range(half // 2 - 1, -1, -1):
-            going = made[half + pair]
-            if arrived:
-                arrived[pair + 1], going = lax.optimization_barrier((arrived[pair + 1], going))
-            arrived[pair] = swapped(going, 1)
-        total = {
-            step: made[step] + arrived[step // 2][step % 2].astype(F32) for step in order
-        }
+        arrived = swapped(made[half], 1)
+        total = {step: made[step] + arrived[step].astype(F32) for step in order}
         far = [swapped(total[step].astype(BF16), 2 * step) for step in order[:-1]]
         summed = total[0]
         for value in far:

time: 81.2 us -> 82.5 us (1.016)
  waiting for transfers between devices: 24.8 us -> 30.5 us
  starting transfers between devices: 35.5 us -> 32.3 us
    ppermute x24 -> x23, waiting for transfers between devices: 21.1 us -> 26.4 us  [swapped(): return lax.ppermute(value, axis, pairs)]
    ppermute x24 -> x23, starting transfers between devices: 19.9 us -> 16.6 us  [swapped(): return lax.ppermute(value, axis, pairs)]
    unnamed x14 -> x22, local copies, waits for them, and re-layouts: 3.32 us -> 3.34 us
  transfers between devices with their start and end apart: 30 -> 29, of which waited for: 16 -> 17; matrix products, arithmetic and copies ran while one was open for 1% -> 0% of each run, Pallas kernels for 10% -> 9%
where the time goes in v8:
time: 82.5 us; the launch traced here: 82.3 us
  starting transfers between devices  32.3 us (39%)
  waiting for transfers between devices  30.5 us (37%)
  Pallas kernels  14.3 us (17%)
  local copies, waits for them, and re-layouts  3.42 us (4%)
  between operations  1.62 us (2%)
    ppermute x23, waiting for transfers between devices, swapped(): return lax.ppermute(value, axis, pairs)  26.4 us
    ppermute x23, starting transfers between devices, swapped(): return lax.ppermute(value, axis, pairs)  16.6 us
    ppermute x6, starting transfers between devices, passed_along(): return lax.ppermute(value, axis, pairs)  15.7 us
    ppermute x6, waiting for transfers between devices, passed_along(): return lax.ppermute(value, axis, pairs)  4.17 us
    unnamed x22, local copies, waits for them, and re-layouts  3.34 us
    pallas_call x2, Pallas kernels, body(): call(functools.partial(hop_kernel, plan), [blocks_f32, slots_f32, slots_f...  2.37 us
    pallas_call x1, Pallas kernels, body(): call(functools.partial(late_kernel, kept, ahead, half), [one_f32] * half...  1.85 us
    pallas_call x3, Pallas kernels, body(): call(functools.partial(forward_kernel, hop), logits_f32, [IN_VMEM] * (3 +...  1.8 us
  transfers between devices with their start and end apart: 29, of which 17 were waited for; matrix products, arithmetic and copies ran while one was open for 0% of the time, Pallas kernels for 9%

profile of v8, /device:TPU:0, one launch (start us, length us, event | category | flops | bytes accessed | tf_op | source)
XLA Modules:
  0.0 82.3 jit_solution(7809995917790927880)
XLA Ops:
  0.7 1.8 %shard_map.139 = (f32[2,128,128]{2,1,0:T(8,128)}, f32[2,128,128]{2,1,0:T(8,128)}, f32[2,128,128]{2,1,0:T(8,128)}, bf16[272,128]{1,0:T(8,128)(2,1)}) custom-call(s32[2]{0:T(128)} %refs_0_.3, s32[2]{0:T(128)} %refs_1_.4, s32[1,2]{1,0:T(1,128)} %refs_2_.2, f32[2,128,128]{2,1,0:T(8,128)} %bitcast.27, s32[1,256]{1,0:T(1,128)} %bitcast.29), custom_call_target="tpu_custom_call" | custom-call | flops 1000 | bytes 1000 | tf_op jit(solution)/shard_map/pallas_call | solution.py:453
  2.4 3.0 %collective-permute-start.1 = (f32[2,128,128]{2,1,0:T(8,128)}, f32[2,128,128]{2,1,0:T(8,128)S(1)}, u32[]{:S(2)}, u32[]{:S(2)}) collective-permute-start(f32[2,128,128]{2,1,0:T(8,128)} %get-tuple-element.32), channel_id=1, source_target_pairs={{0,4},{4,8},{8,12},{12,16},{16,20},{20,24},{24,28},{28,0},{1,5},{5... | collective-permute-start | bytes 393224 | tf_op jit(solution)/shard_map/ppermute | solution.py:30
  5.5 3.1 %collective-permute-start.2 = (f32[2,128,128]{2,1,0:T(8,128)}, f32[2,128,128]{2,1,0:T(8,128)S(1)}, u32[]{:S(2)}, u32[]{:S(2)}) collective-permute-start(f32[2,128,128]{2,1,0:T(8,128)} %get-tuple-element.33), channel_id=1, source_target_pairs={{0,28},{4,0},{8,4},{12,8},{16,12},{20,16},{24,20},{28,24},{1,29},{... | collective-permute-start | bytes 393224 | tf_op jit(solution)/shard_map/ppermute | solution.py:30
  8.6 1.4 %copy-done.1 = bf16[4096,172]{0,1:T(8,128)(2,1)S(1)} copy-done((bf16[4096,172]{0,1:T(8,128)(2,1)S(1)}, bf16[4096,172]{0,1:T(8,128)(2,1)}, u32[]{:S(2)}) %copy-start.1) | copy-done | bytes 1409048
  9.9 1.0 %copy-done.2 = f32[8,128,128]{2,1,0:T(8,128)S(1)} copy-done((f32[8,128,128]{2,1,0:T(8,128)S(1)}, f32[8,128,128]{2,1,0:T(8,128)}, u32[]{:S(2)}) %copy-start.2) | copy-done | bytes 524312
  11.0 0.9 %copy-done.4 = f32[2,128,128]{2,1,0:T(8,128)S(1)} copy-done((f32[2,128,128]{2,1,0:T(8,128)S(1)}, f32[2,128,128]{2,1,0:T(8,128)}, u32[]{:S(2)}) %copy-start.4) | copy-done | bytes 131096
  11.9 0.1 shard_map.140
  12.8 0.1 concatenate.3.refs_0_.refs_1_.refs_5_
  12.9 0.0 collective-permute-done.1.refs_2_
  12.9 0.6 collective-permute-done.2.refs_3_
  13.5 1.2 %shard_map.141 = (f32[2,128,128]{2,1,0:T(8,128)S(1)}, f32[2,128,128]{2,1,0:T(8,128)S(1)}, f32[2,128,128]{2,1,0:T(8,128)S(1)}, bf16[256,128]{1,0:T(8,128)(2,1)S(1)}) custom-call(s32[23]{0:T(128)S(1)} %concatenate.3.refs_0_.refs_1_.refs_5_, f32[2,128,128]{2,1,0:T(8,128)S(1)} %get-tuple-element.31.refs_1_.refs_0_, ...), custom_call_target="tpu_custom_call" | custom-call | flops 201326592 | bytes 1376256 | tf_op jit(solution)/shard_map/pallas_call | solution.py:496
  14.6 0.3 collective-permute-start.4
  15.0 4.4 %collective-permute-start.5 = (f32[2,128,128]{2,1,0:T(8,128)S(1)}, f32[2,128,128]{2,1,0:T(8,128)S(1)}, u32[]{:S(2)}, u32[]{:S(2)}) collective-permute-start(f32[2,128,128]{2,1,0:T(8,128)S(1)} %get-tuple-element.39), channel_id=1, source_target_pairs={{0,28},{4,0},{8,4},{12,8},{16,12},{20,16},{24,20},{28,24},{1,29},{... | collective-permute-start | bytes 393224 | tf_op jit(solution)/shard_map/ppermute | solution.py:30
  19.4 0.0 collective-permute-start.6
  19.4 1.5 %collective-permute-start = (bf16[272,128]{1,0:T(8,128)(2,1)S(1)}, bf16[272,128]{1,0:T(8,128)(2,1)S(1)}, u32[]{:S(2)}, u32[]{:S(2)}) collective-permute-start(bf16[272,128]{1,0:T(8,128)(2,1)S(1)} %copy-done.3), channel_id=1, source_target_pairs={{0,2},{1,3},{2,0},{3,1},{4,6},{5,7},{6,4},{7,5},{8,10},{9,11},{10,... | collective-permute-start | bytes 208904 | tf_op jit(solution)/shard_map/ppermute | solution.py:35
  20.9 0.6 shard_map.142.refs_0_.refs_3_
  21.5 0.6 collective-permute-start.3
  22.1 0.3 collective-permute-done.4.refs_3_
  22.5 1.1 %collective-permute-done.5.refs_4_ = f32[2,128,128]{2,1,0:T(8,128)S(1)} collective-permute-done((f32[2,128,128]{2,1,0:T(8,128)S(1)}, f32[2,128,128]{2,1,0:T(8,128)S(1)}, u32[]{:S(2)}, u32[]{:S(2)}) %collective-permute-start.5) | collective-permute-done | bytes 131104 | tf_op jit(solution)/shard_map/ppermute | solution.py:30
  23.6 1.2 %shard_map.143 = (f32[2,128,128]{2,1,0:T(8,128)S(1)}, f32[2,128,128]{2,1,0:T(8,128)S(1)}, f32[2,128,128]{2,1,0:T(8,128)S(1)}) custom-call(f32[172,256]{1,0:T(8,128)S(1)} %shard_map.142.refs_0_.refs_3_, s32[23]{0:T(128)S(1)} %concatenate.3.refs_0_.refs_1_.refs_5_, f32[2,128,128]{2,1,0:T(8,128)S(1)} %get-tuple-element.37.refs_2_.refs_0_, ...), custom_call_target="tpu_custom_call" | custom-call | flops 201326592 | bytes 1179648 | tf_op jit(solution)/shard_map/pallas_call | solution.py:496
  24.8 0.1 collective-permute-start.10
  24.9 0.0 copy-start.5
  24.9 4.7 %collective-permute-start.11 = (f32[2,128,128]{2,1,0:T(8,128)S(1)}, f32[2,128,128]{2,1,0:T(8,128)S(1)}, u32[]{:S(2)}, u32[]{:S(2)}) collective-permute-start(f32[2,128,128]{2,1,0:T(8,128)S(1)} %get-tuple-element.42), channel_id=1, source_target_pairs={{0,28},{4,0},{8,4},{12,8},{16,12},{20,16},{24,20},{28,24},{1,29},{... | collective-permute-start | bytes 393224 | tf_op jit(solution)/shard_map/ppermute | solution.py:30
  29.6 0.5 collective-permute-start.8
  30.1 0.1 collective-permute-start.9
  30.2 0.6 shard_map.144.refs_5_
  30.8 0.1 collective-permute-done.7.refs_4_.refs_2_
  30.8 0.4 shard_map.146.refs_1_.refs_5_
  31.2 0.6 shard_map.145.refs_0_.refs_1_
  31.8 0.7 collective-permute-done.10.refs_7_
  32.6 1.4 %collective-permute-done.11.refs_8_ = f32[2,128,128]{2,1,0:T(8,128)S(1)} collective-permute-done((f32[2,128,128]{2,1,0:T(8,128)S(1)}, f32[2,128,128]{2,1,0:T(8,128)S(1)}, u32[]{:S(2)}, u32[]{:S(2)}) %collective-permute-start.11) | collective-permute-done | bytes 131104 | tf_op jit(solution)/shard_map/ppermute | solution.py:30
  34.0 1.2 %shard_map.147.refs_0_.refs_4_ = bf16[256,256]{1,0:T(8,128)(2,1)S(1)} custom-call(f32[172,256]{1,0:T(8,128)S(1)} %shard_map.145.refs_0_.refs_1_, s32[1,256]{1,0:T(1,128)S(1)} %shard_map.146.refs_1_.refs_5_, bf16[256,128]{1,0:T(8,128)(2,1)S(1)} %collective-permute-done.8.refs_2_.refs_3_, bf16[256,128]{1,0:T(8,128)(2,1)S(1)} %collective-permute-done.3.refs_1_.refs_3_, ...), custom_call_target="tpu_custom_call" | custom-call | flops 201326592 | bytes 393216 | tf_op jit(solution)/shard_map/pallas_call | solution.py:523
  35.2 0.1 collective-permute-start.15
  35.2 1.6 %collective-permute-start.14 = (bf16[256,256]{1,0:T(8,128)(2,1)S(1)}, bf16[256,256]{1,0:T(8,128)(2,1)S(1)}, u32[]{:S(2)}, u32[]{:S(2)}) collective-permute-start(bf16[256,256]{1,0:T(8,128)(2,1)S(1)} %shard_map.147.refs_0_.refs_4_), channel_id=1, source_target_pairs={{0,2},{1,3},{2,0},{3,1},{4,6},{5,7},{6,4},{7,5},{8,10},{9,11},{10,... | collective-permute-start | bytes 393224 | tf_op jit(solution)/shard_map/ppermute | solution.py:35
  36.8 0.8 %shard_map.148.refs_6_.refs_0_ = bf16[192,256]{1,0:T(8,128)(2,1)S(1)} custom-call(bf16[256,256]{1,0:T(8,128)(2,1)S(1)} %shard_map.147.refs_0_.refs_4_, f32[172,256]{1,0:T(8,128)S(1)} %shard_map.145.refs_0_.refs_1_, bf16[4,128,1024]{2,1,0:T(8,128)(2,1)S(1)} %copy-done, bf16[172,4096]{1,0:T(8,128)(2,1)S(1)} %get-tuple-element.36.refs_2_.refs_4_.refs_3_.refs_1_, ...), custom_call_target="tpu_custom_call" | custom-call | flops 1000 | bytes 1000 | tf_op jit(solution)/shard_map/pallas_call | solution.py:531
  37.6 0.2 collective-permute-start.12
  37.8 0.5 collective-permute-start.13
  38.3 0.3 shard_map.149
  38.6 0.3 collective-permute-done.12.refs_7_.refs_1_
  38.9 1.8 %shard_map.150.refs_0_ = f32[8,304,128]{2,1,0:T(8,128)S(1)} custom-call(bf16[272,128]{1,0:T(8,128)(2,1)S(1)} %copy-done.3, bf16[272,128]{1,0:T(8,128)(2,1)S(1)} %collective-permute-done.6.refs_2_.refs_1_, bf16[256,128]{1,0:T(8,128)(2,1)S(1)} %get-tuple-element.35.refs_2_, bf16[256,128]{1,0:T(8,128)(2,1)S(1)} %collective-permute-done.8.refs_2_.refs_3_, ...), custom_call_target="tpu_custom_call" | custom-call | flops 1000 | bytes 1000 | tf_op jit(solution)/shard_map/pallas_call | solution.py:547
  40.7 2.6 %collective-permute-done.13.refs_2_.refs_7_ = bf16[192,256]{1,0:T(8,128)(2,1)S(1)} collective-permute-done((bf16[192,256]{1,0:T(8,128)(2,1)S(1)}, bf16[192,256]{1,0:T(8,128)(2,1)S(1)}, u32[]{:S(2)}, u32[]{:S(2)}) %collective-permute-start.13) | collective-permute-done | bytes 98336 | tf_op jit(solution)/shard_map/ppermute | solution.py:35
  43.3 0.5 collective-permute-start.16
  43.8 1.0 %collective-permute-done.16.refs_3_.refs_8_ = bf16[192,256]{1,0:T(8,128)(2,1)S(1)} collective-permute-done((bf16[192,256]{1,0:T(8,128)(2,1)S(1)}, bf16[192,256]{1,0:T(8,128)(2,1)S(1)}, u32[]{:S(2)}, u32[]{:S(2)}) %collective-permute-start.16) | collective-permute-done | bytes 98336 | tf_op jit(solution)/shard_map/ppermute | solution.py:35
  44.8 1.8 %shard_map.152 = (f32[304,128]{1,0:T(8,128)S(1)}, f32[304,128]{1,0:T(8,128)S(1)}, f32[304,128]{1,0:T(8,128)S(1)}, f32[304,128]{1,0:T(8,128)S(1)}, bf16[4,304,128]{2,1,0:T(8,128)(2,1)S(1)}) custom-call(f32[8,304,128]{2,1,0:T(8,128)S(1)} %shard_map.150.refs_0_, bf16[272,128]{1,0:T(8,128)(2,1)S(1)} %collective-permute-done.refs_0_.refs_3_.refs_1_, ...), custom_call_target="tpu_custom_call" | custom-call | flops 771751936 | bytes 2801664 | tf_op jit(solution)/shard_map/pallas_call | solution.py:575
  46.6 0.1 collective-permute-start.18
  46.7 9.6 %collective-permute-done.18 = bf16[4,304,128]{2,1,0:T(8,128)(2,1)S(1)} collective-permute-done((bf16[4,304,128]{2,1,0:T(8,128)(2,1)S(1)}, bf16[4,304,128]{2,1,0:T(8,128)(2,1)S(1)}, u32[]{:S(2)}, u32[]{:S(2)}) %collective-permute-start.18) | collective-permute-done | bytes 311328 | tf_op jit(solution)/shard_map/ppermute | solution.py:35
  56.3 0.1 fusion.2
  56.3 2.2 %collective-permute-start.19 = (bf16[304,128]{1,0:T(8,128)(2,1)S(1)}, bf16[304,128]{1,0:T(8,128)(2,1)S(1)}, u32[]{:S(2)}, u32[]{:S(2)}) collective-permute-start(bf16[304,128]{1,0:T(8,128)(2,1)S(1)} %get-tuple-element.55), channel_id=1, source_target_pairs={{0,24},{4,28},{8,16},{12,20},{16,8},{20,12},{24,0},{28,4},{1,25},{... | collective-permute-start | bytes 233480 | tf_op jit(solution)/shard_map/ppermute | solution.py:35
  58.5 0.1 collective-permute-start.21
  58.6 2.2 %collective-permute-start.20 = (bf16[304,128]{1,0:T(8,128)(2,1)S(1)}, bf16[304,128]{1,0:T(8,128)(2,1)S(1)}, u32[]{:S(2)}, u32[]{:S(2)}) collective-permute-start(bf16[304,128]{1,0:T(8,128)(2,1)S(1)} %get-tuple-element.57), channel_id=1, source_target_pairs={{0,16},{4,20},{8,24},{12,28},{16,0},{20,4},{24,8},{28,12},{1,17},{... | collective-permute-start | bytes 233480 | tf_op jit(solution)/shard_map/ppermute | solution.py:35
  60.8 2.2 %collective-permute-done.19 = bf16[304,128]{1,0:T(8,128)(2,1)S(1)} collective-permute-done((bf16[304,128]{1,0:T(8,128)(2,1)S(1)}, bf16[304,128]{1,0:T(8,128)(2,1)S(1)}, u32[]{:S(2)}, u32[]{:S(2)}) %collective-permute-start.19) | collective-permute-done | bytes 77856 | tf_op jit(solution)/shard_map/ppermute | solution.py:35
  63.0 1.4 %collective-permute-done.21 = bf16[304,128]{1,0:T(8,128)(2,1)S(1)} collective-permute-done((bf16[304,128]{1,0:T(8,128)(2,1)S(1)}, bf16[304,128]{1,0:T(8,128)(2,1)S(1)}, u32[]{:S(2)}, u32[]{:S(2)}) %collective-permute-start.21) | collective-permute-done | bytes 77856 | tf_op jit(solution)/shard_map/ppermute | solution.py:35
  64.4 1.8 %collective-permute-done.20 = bf16[304,128]{1,0:T(8,128)(2,1)S(1)} collective-permute-done((bf16[304,128]{1,0:T(8,128)(2,1)S(1)}, bf16[304,128]{1,0:T(8,128)(2,1)S(1)}, u32[]{:S(2)}, u32[]{:S(2)}) %collective-permute-start.20) | collective-permute-done | bytes 77856 | tf_op jit(solution)/shard_map/ppermute | solution.py:35
  66.1 0.1 fusion.6.refs_0_
  66.2 2.3 %collective-permute-start.24 = (bf16[304,128]{1,0:T(8,128)(2,1)S(1)}, bf16[304,128]{1,0:T(8,128)(2,1)S(1)}, u32[]{:S(2)}, u32[]{:S(2)}) collective-permute-start(bf16[304,128]{1,0:T(8,128)(2,1)S(1)} %fusion.6.refs_0_), channel_id=1, source_target_pairs={{0,24},{4,28},{8,16},{12,20},{16,8},{20,12},{24,0},{28,4},{1,25},{... | collective-permute-start | bytes 233480 | tf_op jit(solution)/shard_map/ppermute | solution.py:35
  68.5 2.2 %collective-permute-start.22 = (bf16[304,128]{1,0:T(8,128)(2,1)S(1)}, bf16[304,128]{1,0:T(8,128)(2,1)S(1)}, u32[]{:S(2)}, u32[]{:S(2)}) collective-permute-start(bf16[304,128]{1,0:T(8,128)(2,1)S(1)} %fusion.6.refs_0_), channel_id=1, source_target_pairs={{0,8},{4,12},{8,0},{12,4},{16,24},{20,28},{24,16},{28,20},{1,9},{5... | collective-permute-start | bytes 233480 | tf_op jit(solution)/shard_map/ppermute | solution.py:35
  70.7 0.1 collective-permute-start.25
  70.7 2.5 %collective-permute-done.24.refs_3_ = bf16[304,128]{1,0:T(8,128)(2,1)S(1)} collective-permute-done((bf16[304,128]{1,0:T(8,128)(2,1)S(1)}, bf16[304,128]{1,0:T(8,128)(2,1)S(1)}, u32[]{:S(2)}, u32[]{:S(2)}) %collective-permute-start.24) | collective-permute-done | bytes 77856 | tf_op jit(solution)/shard_map/ppermute | solution.py:35
  73.2 2.1 %collective-permute-done.23.refs_2_ = bf16[304,128]{1,0:T(8,128)(2,1)S(1)} collective-permute-done((bf16[304,128]{1,0:T(8,128)(2,1)S(1)}, bf16[304,128]{1,0:T(8,128)(2,1)S(1)}, u32[]{:S(2)}, u32[]{:S(2)}) %collective-permute-start.23) | collective-permute-done | bytes 77856 | tf_op jit(solution)/shard_map/ppermute | solution.py:35
  75.3 2.0 %collective-permute-start.26 = (bf16[304,128]{1,0:T(8,128)(2,1)S(1)}, bf16[304,128]{1,0:T(8,128)(2,1)S(1)}, u32[]{:S(2)}, u32[]{:S(2)}) collective-permute-start(bf16[304,128]{1,0:T(8,128)(2,1)S(1)} %collective-permute-done.22.refs_1_), channel_id=1, source_target_pairs={{0,4},{4,0},{8,12},{12,8},{16,20},{20,16},{24,28},{28,24},{1,5},{5... | collective-permute-start | bytes 233480 | tf_op jit(solution)/shard_map/ppermute | solution.py:35
  77.3 0.8 shard_map.151
  78.1 2.1 %collective-permute-done.27.refs_6_ = bf16[304,128]{1,0:T(8,128)(2,1)S(1)} collective-permute-done((bf16[304,128]{1,0:T(8,128)(2,1)S(1)}, bf16[304,128]{1,0:T(8,128)(2,1)S(1)}, u32[]{:S(2)}, u32[]{:S(2)}) %collective-permute-start.27) | collective-permute-done | bytes 77856 | tf_op jit(solution)/shard_map/ppermute | solution.py:35
  80.2 0.8 %collective-permute-done.26.refs_5_ = bf16[304,128]{1,0:T(8,128)(2,1)S(1)} collective-permute-done((bf16[304,128]{1,0:T(8,128)(2,1)S(1)}, bf16[304,128]{1,0:T(8,128)(2,1)S(1)}, u32[]{:S(2)}, u32[]{:S(2)}) %collective-permute-start.26) | collective-permute-done | bytes 77856 | tf_op jit(solution)/shard_map/ppermute | solution.py:35
  81.1 1.2 %shard_map.153 = (f32[4,128,256]{2,1,0:T(8,128)}, f32[172,1024]{1,0:T(8,128)}) custom-call(bf16[304,128]{1,0:T(8,128)(2,1)S(1)} %fusion.6.refs_0_, bf16[304,128]{1,0:T(8,128)(2,1)S(1)} %collective-permute-done.22.refs_1_, bf16[304,128]{1,0:T(8,128)(2,1)S(1)} %collective-permute-done.23.refs_2_, bf16[304,128]{1,0:T(8,128)(2,1)S(1)} %collective-permute-done.24.refs_3_, ...), custom_call_target="tpu_custom_call" | custom-call | flops 1000 | bytes 1000 | tf_op jit(solution)/shard_map/pallas_call | solution.py:597
  (34 shorter events, 0.1 us)
Async XLA Ops:
  0.6 12.1 %copy-start.8 = (s32[1,2]{1,0:T(1,128)S(1)}, s32[1,2]{1,0:T(1,128)}, u32[]{:S(2)}) copy-start(s32[1,2]{1,0:T(1,128)} %refs_2_.2) | copy-start | bytes 28
  0.6 12.1 %copy-start.7 = (s32[2]{0:T(128)S(1)}, s32[2]{0:T(128)}, u32[]{:S(2)}) copy-start(s32[2]{0:T(128)} %refs_1_.4) | copy-start | bytes 28
  0.7 12.1 %copy-start.6 = (s32[2]{0:T(128)S(1)}, s32[2]{0:T(128)}, u32[]{:S(2)}) copy-start(s32[2]{0:T(128)} %refs_0_.3) | copy-start | bytes 28
  0.7 12.1 %copy-start.10 = (s32[8]{0:T(128)S(1)}, s32[8]{0:T(128)}, u32[]{:S(2)}) copy-start(s32[8]{0:T(128)} %param.15) | copy-start | bytes 100
  0.7 12.1 %copy-start.9 = (s32[8]{0:T(128)S(1)}, s32[8]{0:T(128)}, u32[]{:S(2)}) copy-start(s32[8]{0:T(128)} %param.14) | copy-start | bytes 100
  2.4 10.4 %collective-permute-start.1 = (f32[2,128,128]{2,1,0:T(8,128)}, f32[2,128,128]{2,1,0:T(8,128)S(1)}, u32[]{:S(2)}, u32[]{:S(2)}) collective-permute-start(f32[2,128,128]{2,1,0:T(8,128)} %get-tuple-element.32), channel_id=1, source_target_pairs={{0,4},{4,8},{8,12},{12,16},{16,20},{20,24},{24,28},{28,0},{1,5},{5... | collective-permute-start | bytes 393224 | tf_op jit(solution)/shard_map/ppermute | solution.py:30
  5.5 8.0 %collective-permute-start.2 = (f32[2,128,128]{2,1,0:T(8,128)}, f32[2,128,128]{2,1,0:T(8,128)S(1)}, u32[]{:S(2)}, u32[]{:S(2)}) collective-permute-start(f32[2,128,128]{2,1,0:T(8,128)} %get-tuple-element.33), channel_id=1, source_target_pairs={{0,28},{4,0},{8,4},{12,8},{16,12},{20,16},{24,20},{28,24},{1,29},{... | collective-permute-start | bytes 393224 | tf_op jit(solution)/shard_map/ppermute | solution.py:30
  8.6 1.4 %copy-start.1 = (bf16[4096,172]{0,1:T(8,128)(2,1)S(1)}, bf16[4096,172]{0,1:T(8,128)(2,1)}, u32[]{:S(2)}) copy-start(bf16[4096,172]{0,1:T(8,128)(2,1)} %param.23) | copy-start | bytes 4227076
  9.9 1.0 %copy-start.2 = (f32[8,128,128]{2,1,0:T(8,128)S(1)}, f32[8,128,128]{2,1,0:T(8,128)}, u32[]{:S(2)}) copy-start(f32[8,128,128]{2,1,0:T(8,128)} %refs_1_.5) | copy-start | bytes 1572868
  11.0 0.9 %copy-start.4 = (f32[2,128,128]{2,1,0:T(8,128)S(1)}, f32[2,128,128]{2,1,0:T(8,128)}, u32[]{:S(2)}) copy-start(f32[2,128,128]{2,1,0:T(8,128)} %get-tuple-element.30.refs_0_) | copy-start | bytes 393220
  11.9 7.5 %copy-start.3 = (bf16[272,128]{1,0:T(8,128)(2,1)S(1)}, bf16[272,128]{1,0:T(8,128)(2,1)}, u32[]{:S(2)}) copy-start(bf16[272,128]{1,0:T(8,128)(2,1)} %get-tuple-element.29.refs_1_.refs_0_) | copy-start | bytes 208900
  11.9 9.0 %copy-start = (bf16[4,128,1024]{2,1,0:T(8,128)(2,1)S(1)}, bf16[4,128,1024]{2,1,0:T(8,128)(2,1)}, u32[]{:S(2)}) copy-start(bf16[4,128,1024]{2,1,0:T(8,128)(2,1)} %refs_9_.1) | copy-start | bytes 3145732
  14.6 7.8 %collective-permute-start.4 = (f32[2,128,128]{2,1,0:T(8,128)S(1)}, f32[2,128,128]{2,1,0:T(8,128)S(1)}, u32[]{:S(2)}, u32[]{:S(2)}) collective-permute-start(f32[2,128,128]{2,1,0:T(8,128)S(1)} %get-tuple-element.38), channel_id=1, source_target_pairs={{0,4},{4,8},{8,12},{12,16},{16,20},{20,24},{24,28},{28,0},{1,5},{5... | collective-permute-start | bytes 393224 | tf_op jit(solution)/shard_map/ppermute | solution.py:30
  15.0 8.6 %collective-permute-start.5 = (f32[2,128,128]{2,1,0:T(8,128)S(1)}, f32[2,128,128]{2,1,0:T(8,128)S(1)}, u32[]{:S(2)}, u32[]{:S(2)}) collective-permute-start(f32[2,128,128]{2,1,0:T(8,128)S(1)} %get-tuple-element.39), channel_id=1, source_target_pairs={{0,28},{4,0},{8,4},{12,8},{16,12},{20,16},{24,20},{28,24},{1,29},{... | collective-permute-start | bytes 393224 | tf_op jit(solution)/shard_map/ppermute | solution.py:30
  19.4 10.2 %collective-permute-start.6 = (bf16[272,128]{1,0:T(8,128)(2,1)S(1)}, bf16[272,128]{1,0:T(8,128)(2,1)S(1)}, u32[]{:S(2)}, u32[]{:S(2)}) collective-permute-start(bf16[272,128]{1,0:T(8,128)(2,1)S(1)} %copy-done.3), channel_id=1, source_target_pairs={{0,1},{1,0},{2,3},{3,2},{4,5},{5,4},{6,7},{7,6},{8,9},{9,8},{10,11... | collective-permute-start | bytes 208904 | tf_op jit(solution)/shard_map/ppermute | solution.py:35
  19.4 10.1 %collective-permute-start = (bf16[272,128]{1,0:T(8,128)(2,1)S(1)}, bf16[272,128]{1,0:T(8,128)(2,1)S(1)}, u32[]{:S(2)}, u32[]{:S(2)}) collective-permute-start(bf16[272,128]{1,0:T(8,128)(2,1)S(1)} %copy-done.3), channel_id=1, source_target_pairs={{0,2},{1,3},{2,0},{3,1},{4,6},{5,7},{6,4},{7,5},{8,10},{9,11},{10,... | collective-permute-start | bytes 208904 | tf_op jit(solution)/shard_map/ppermute | solution.py:35
  21.5 8.6 %collective-permute-start.3 = (bf16[256,128]{1,0:T(8,128)(2,1)S(1)}, bf16[256,128]{1,0:T(8,128)(2,1)S(1)}, u32[]{:S(2)}, u32[]{:S(2)}) collective-permute-start(bf16[256,128]{1,0:T(8,128)(2,1)S(1)} %get-tuple-element.35.refs_2_), channel_id=1, source_target_pairs={{0,2},{1,3},{2,0},{3,1},{4,6},{5,7},{6,4},{7,5},{8,10},{9,11},{10,... | collective-permute-start | bytes 196616 | tf_op jit(solution)/shard_map/ppermute | solution.py:35
  24.8 7.8 %collective-permute-start.10 = (f32[2,128,128]{2,1,0:T(8,128)S(1)}, f32[2,128,128]{2,1,0:T(8,128)S(1)}, u32[]{:S(2)}, u32[]{:S(2)}) collective-permute-start(f32[2,128,128]{2,1,0:T(8,128)S(1)} %get-tuple-element.41), channel_id=1, source_target_pairs={{0,4},{4,8},{8,12},{12,16},{16,20},{20,24},{24,28},{28,0},{1,5},{5... | collective-permute-start | bytes 393224 | tf_op jit(solution)/shard_map/ppermute | solution.py:30
  24.9 6.0 %copy-start.5 = (s32[1,256]{1,0:T(1,128)S(1)}, s32[1,256]{1,0:T(1,128)}, u32[]{:S(2)}) copy-start(s32[1,256]{1,0:T(1,128)} %refs_4_.1) | copy-start | bytes 3076
  24.9 9.1 %collective-permute-start.11 = (f32[2,128,128]{2,1,0:T(8,128)S(1)}, f32[2,128,128]{2,1,0:T(8,128)S(1)}, u32[]{:S(2)}, u32[]{:S(2)}) collective-permute-start(f32[2,128,128]{2,1,0:T(8,128)S(1)} %get-tuple-element.42), channel_id=1, source_target_pairs={{0,28},{4,0},{8,4},{12,8},{16,12},{20,16},{24,20},{28,24},{1,29},{... | collective-permute-start | bytes 393224 | tf_op jit(solution)/shard_map/ppermute | solution.py:30
  29.6 1.3 %collective-permute-start.7 = (bf16[272,128]{1,0:T(8,128)(2,1)S(1)}, bf16[272,128]{1,0:T(8,128)(2,1)S(1)}, u32[]{:S(2)}, u32[]{:S(2)}) collective-permute-start(bf16[272,128]{1,0:T(8,128)(2,1)S(1)} %collective-permute-done.refs_0_.refs_3_.refs_1_), channel_id=1, source_target_pairs={{0,1},{1,0},{2,3},{3,2},{4,5},{5,4},{6,7},{7,6},{8,9},{9,8},{10,11... | collective-permute-start | bytes 208904 | tf_op jit(solution)/shard_map/ppermute | solution.py:35
  29.6 2.2 %collective-permute-start.8 = (bf16[256,128]{1,0:T(8,128)(2,1)S(1)}, bf16[256,128]{1,0:T(8,128)(2,1)S(1)}, u32[]{:S(2)}, u32[]{:S(2)}) collective-permute-start(bf16[256,128]{1,0:T(8,128)(2,1)S(1)} %get-tuple-element.35.refs_2_), channel_id=1, source_target_pairs={{0,1},{1,0},{2,3},{3,2},{4,5},{5,4},{6,7},{7,6},{8,9},{9,8},{10,11... | collective-permute-start | bytes 196616 | tf_op jit(solution)/shard_map/ppermute | solution.py:35
  30.1 1.7 %collective-permute-start.9 = (bf16[256,128]{1,0:T(8,128)(2,1)S(1)}, bf16[256,128]{1,0:T(8,128)(2,1)S(1)}, u32[]{:S(2)}, u32[]{:S(2)}) collective-permute-start(bf16[256,128]{1,0:T(8,128)(2,1)S(1)} %collective-permute-done.3.refs_1_.refs_3_), channel_id=1, source_target_pairs={{0,1},{1,0},{2,3},{3,2},{4,5},{5,4},{6,7},{7,6},{8,9},{9,8},{10,11... | collective-permute-start | bytes 196616 | tf_op jit(solution)/shard_map/ppermute | solution.py:35
  35.2 3.8 %collective-permute-start.15 = (bf16[256,256]{1,0:T(8,128)(2,1)S(1)}, bf16[256,256]{1,0:T(8,128)(2,1)S(1)}, u32[]{:S(2)}, u32[]{:S(2)}) collective-permute-start(bf16[256,256]{1,0:T(8,128)(2,1)S(1)} %shard_map.147.refs_0_.refs_4_), channel_id=1, source_target_pairs={{0,1},{1,0},{2,3},{3,2},{4,5},{5,4},{6,7},{7,6},{8,9},{9,8},{10,11... | collective-permute-start | bytes 393224 | tf_op jit(solution)/shard_map/ppermute | solution.py:35
  35.2 8.0 %collective-permute-start.14 = (bf16[256,256]{1,0:T(8,128)(2,1)S(1)}, bf16[256,256]{1,0:T(8,128)(2,1)S(1)}, u32[]{:S(2)}, u32[]{:S(2)}) collective-permute-start(bf16[256,256]{1,0:T(8,128)(2,1)S(1)} %shard_map.147.refs_0_.refs_4_), channel_id=1, source_target_pairs={{0,2},{1,3},{2,0},{3,1},{4,6},{5,7},{6,4},{7,5},{8,10},{9,11},{10,... | collective-permute-start | bytes 393224 | tf_op jit(solution)/shard_map/ppermute | solution.py:35
  37.6 1.3 %collective-permute-start.12 = (bf16[192,256]{1,0:T(8,128)(2,1)S(1)}, bf16[192,256]{1,0:T(8,128)(2,1)S(1)}, u32[]{:S(2)}, u32[]{:S(2)}) collective-permute-start(bf16[192,256]{1,0:T(8,128)(2,1)S(1)} %shard_map.148.refs_6_.refs_0_), channel_id=1, source_target_pairs={{0,1},{1,0},{2,3},{3,2},{4,5},{5,4},{6,7},{7,6},{8,9},{9,8},{10,11... | collective-permute-start | bytes 294920 | tf_op jit(solution)/shard_map/ppermute | solution.py:35
  37.8 5.5 %collective-permute-start.13 = (bf16[192,256]{1,0:T(8,128)(2,1)S(1)}, bf16[192,256]{1,0:T(8,128)(2,1)S(1)}, u32[]{:S(2)}, u32[]{:S(2)}) collective-permute-start(bf16[192,256]{1,0:T(8,128)(2,1)S(1)} %shard_map.148.refs_6_.refs_0_), channel_id=1, source_target_pairs={{0,2},{1,3},{2,0},{3,1},{4,6},{5,7},{6,4},{7,5},{8,10},{9,11},{10,... | collective-permute-start | bytes 294920 | tf_op jit(solution)/shard_map/ppermute | solution.py:35
  43.3 1.5 %collective-permute-start.17 = (bf16[256,256]{1,0:T(8,128)(2,1)S(1)}, bf16[256,256]{1,0:T(8,128)(2,1)S(1)}, u32[]{:S(2)}, u32[]{:S(2)}) collective-permute-start(bf16[256,256]{1,0:T(8,128)(2,1)S(1)} %collective-permute-done.14.refs_5_), channel_id=1, source_target_pairs={{0,1},{1,0},{2,3},{3,2},{4,5},{5,4},{6,7},{7,6},{8,9},{9,8},{10,11... | collective-permute-start | bytes 393224 | tf_op jit(solution)/shard_map/ppermute | solution.py:35
  43.3 1.5 %collective-permute-start.16 = (bf16[192,256]{1,0:T(8,128)(2,1)S(1)}, bf16[192,256]{1,0:T(8,128)(2,1)S(1)}, u32[]{:S(2)}, u32[]{:S(2)}) collective-permute-start(bf16[192,256]{1,0:T(8,128)(2,1)S(1)} %collective-permute-done.13.refs_2_.refs_7_), channel_id=1, source_target_pairs={{0,1},{1,0},{2,3},{3,2},{4,5},{5,4},{6,7},{7,6},{8,9},{9,8},{10,11... | collective-permute-start | bytes 294920 | tf_op jit(solution)/shard_map/ppermute | solution.py:35
  46.6 9.7 %collective-permute-start.18 = (bf16[4,304,128]{2,1,0:T(8,128)(2,1)S(1)}, bf16[4,304,128]{2,1,0:T(8,128)(2,1)S(1)}, u32[]{:S(2)}, u32[]{:S(2)}) collective-permute-start(bf16[4,304,128]{2,1,0:T(8,128)(2,1)S(1)} %get-tuple-element.49), channel_id=1, source_target_pairs={{0,4},{4,0},{8,12},{12,8},{16,20},{20,16},{24,28},{28,24},{1,5},{5... | collective-permute-start | bytes 933896 | tf_op jit(solution)/shard_map/ppermute | solution.py:35
  56.3 6.7 %collective-permute-start.19 = (bf16[304,128]{1,0:T(8,128)(2,1)S(1)}, bf16[304,128]{1,0:T(8,128)(2,1)S(1)}, u32[]{:S(2)}, u32[]{:S(2)}) collective-permute-start(bf16[304,128]{1,0:T(8,128)(2,1)S(1)} %get-tuple-element.55), channel_id=1, source_target_pairs={{0,24},{4,28},{8,16},{12,20},{16,8},{20,12},{24,0},{28,4},{1,25},{... | collective-permute-start | bytes 233480 | tf_op jit(solution)/shard_map/ppermute | solution.py:35
  58.5 5.9 %collective-permute-start.21 = (bf16[304,128]{1,0:T(8,128)(2,1)S(1)}, bf16[304,128]{1,0:T(8,128)(2,1)S(1)}, u32[]{:S(2)}, u32[]{:S(2)}) collective-permute-start(bf16[304,128]{1,0:T(8,128)(2,1)S(1)} %get-tuple-element.56), channel_id=1, source_target_pairs={{0,8},{4,12},{8,0},{12,4},{16,24},{20,28},{24,16},{28,20},{1,9},{5... | collective-permute-start | bytes 233480 | tf_op jit(solution)/shard_map/ppermute | solution.py:35
  58.6 7.5 %collective-permute-start.20 = (bf16[304,128]{1,0:T(8,128)(2,1)S(1)}, bf16[304,128]{1,0:T(8,128)(2,1)S(1)}, u32[]{:S(2)}, u32[]{:S(2)}) collective-permute-start(bf16[304,128]{1,0:T(8,128)(2,1)S(1)} %get-tuple-element.57), channel_id=1, source_target_pairs={{0,16},{4,20},{8,24},{12,28},{16,0},{20,4},{24,8},{28,12},{1,17},{... | collective-permute-start | bytes 233480 | tf_op jit(solution)/shard_map/ppermute | solution.py:35
  66.2 7.0 %collective-permute-start.24 = (bf16[304,128]{1,0:T(8,128)(2,1)S(1)}, bf16[304,128]{1,0:T(8,128)(2,1)S(1)}, u32[]{:S(2)}, u32[]{:S(2)}) collective-permute-start(bf16[304,128]{1,0:T(8,128)(2,1)S(1)} %fusion.6.refs_0_), channel_id=1, source_target_pairs={{0,24},{4,28},{8,16},{12,20},{16,8},{20,12},{24,0},{28,4},{1,25},{... | collective-permute-start | bytes 233480 | tf_op jit(solution)/shard_map/ppermute | solution.py:35
  68.5 6.8 %collective-permute-start.23 = (bf16[304,128]{1,0:T(8,128)(2,1)S(1)}, bf16[304,128]{1,0:T(8,128)(2,1)S(1)}, u32[]{:S(2)}, u32[]{:S(2)}) collective-permute-start(bf16[304,128]{1,0:T(8,128)(2,1)S(1)} %fusion.6.refs_0_), channel_id=1, source_target_pairs={{0,16},{4,20},{8,24},{12,28},{16,0},{20,4},{24,8},{28,12},{1,17},{... | collective-permute-start | bytes 233480 | tf_op jit(solution)/shard_map/ppermute | solution.py:35
  68.5 6.8 %collective-permute-start.22 = (bf16[304,128]{1,0:T(8,128)(2,1)S(1)}, bf16[304,128]{1,0:T(8,128)(2,1)S(1)}, u32[]{:S(2)}, u32[]{:S(2)}) collective-permute-start(bf16[304,128]{1,0:T(8,128)(2,1)S(1)} %fusion.6.refs_0_), channel_id=1, source_target_pairs={{0,8},{4,12},{8,0},{12,4},{16,24},{20,28},{24,16},{28,20},{1,9},{5... | collective-permute-start | bytes 233480 | tf_op jit(solution)/shard_map/ppermute | solution.py:35
  70.7 7.5 %collective-permute-start.25 = (bf16[304,128]{1,0:T(8,128)(2,1)S(1)}, bf16[304,128]{1,0:T(8,128)(2,1)S(1)}, u32[]{:S(2)}, u32[]{:S(2)}) collective-permute-start(bf16[304,128]{1,0:T(8,128)(2,1)S(1)} %fusion.6.refs_0_), channel_id=1, source_target_pairs={{0,4},{4,0},{8,12},{12,8},{16,20},{20,16},{24,28},{28,24},{1,5},{5... | collective-permute-start | bytes 233480 | tf_op jit(solution)/shard_map/ppermute | solution.py:35
  73.2 4.9 %collective-permute-start.28 = (bf16[304,128]{1,0:T(8,128)(2,1)S(1)}, bf16[304,128]{1,0:T(8,128)(2,1)S(1)}, u32[]{:S(2)}, u32[]{:S(2)}) collective-permute-start(bf16[304,128]{1,0:T(8,128)(2,1)S(1)} %collective-permute-done.24.refs_3_), channel_id=1, source_target_pairs={{0,4},{4,0},{8,12},{12,8},{16,20},{20,16},{24,28},{28,24},{1,5},{5... | collective-permute-start | bytes 233480 | tf_op jit(solution)/shard_map/ppermute | solution.py:35
  75.3 5.0 %collective-permute-start.27 = (bf16[304,128]{1,0:T(8,128)(2,1)S(1)}, bf16[304,128]{1,0:T(8,128)(2,1)S(1)}, u32[]{:S(2)}, u32[]{:S(2)}) collective-permute-start(bf16[304,128]{1,0:T(8,128)(2,1)S(1)} %collective-permute-done.23.refs_2_), channel_id=1, source_target_pairs={{0,4},{4,0},{8,12},{12,8},{16,20},{20,16},{24,28},{28,24},{1,5},{5... | collective-permute-start | bytes 233480 | tf_op jit(solution)/shard_map/ppermute | solution.py:35
  75.3 5.8 %collective-permute-start.26 = (bf16[304,128]{1,0:T(8,128)(2,1)S(1)}, bf16[304,128]{1,0:T(8,128)(2,1)S(1)}, u32[]{:S(2)}, u32[]{:S(2)}) collective-permute-start(bf16[304,128]{1,0:T(8,128)(2,1)S(1)} %collective-permute-done.22.refs_1_), channel_id=1, source_target_pairs={{0,4},{4,0},{8,12},{12,8},{16,20},{20,16},{24,28},{28,24},{1,5},{5... | collective-permute-start | bytes 233480 | tf_op jit(solution)/shard_map/ppermute | solution.py:35

commit v9 on v8

--- a/solution.py
+++ b/solution.py
@@ -364,7 +364,7 @@
 
 
 def late_kernel(kept, members, half, early_ref, *refs):
-    ins = len(refs) - 2 - half
+    ins = len(refs) - 1 - 2 * half
     outs = refs[ins:-1]
     chunks_ref = refs[-1]
     late_chunks(kept, members, early_ref, refs[:ins], chunks_ref)
@@ -372,7 +372,7 @@
     for step in range(half):
         stays = dom ^ (2 * step)
         outs[step][...] = chunks_ref[stays]
-        outs[half][step] = chunks_ref[stays ^ 1].astype(BF16)
+        outs[half + step][...] = chunks_ref[stays ^ 1].astype(BF16)
 
 
 def plain_late_kernel(kept, members, early_ref, *refs):
@@ -388,14 +388,55 @@
     branch_ref[branch, :, pl.ds(start, LANES)] = value[kept:].T
 
 
-def out_kernel(kept, *refs):
-    ins, branch_ref, class_ref = refs[:-2], refs[-2], refs[-1]
+def out_kernel(kept, distances, *refs):
+    count = len(distances)
+    ins = refs[-5 - count : -5]
+    branch_ref, class_ref, branch_here, class_here, sems = refs[-5:]
     dom = lax.axis_index("dom")
-    half = len(ins) // 2
-    for step in range(half):
-        for side in range(2):
-            value = ins[side * half + step][...].astype(F32)
-            write_chunk(kept, dom ^ (2 * step + side), value, branch_ref, class_ref)
+    per_branch = branch_ref.shape[2] // LANES
+    copies = []
+    for number, distance in enumerate(distances):
+        chunk = dom ^ distance
+        value = ins[number][...].astype(F32)
+        class_here[number] = value[: class_ref.shape[0]]
+        start = pl.multiple_of(chunk * LANES, LANES)
+        copies.append(
+            pltpu.make_async_copy(
+                class_here.at[number], class_ref.at[:, pl.ds(start, LANES)], sems.at[2 * number]
+            )
+        )
+        copies[-1].start()
+        branch_here[number] = value[kept:].T
+        branch = chunk // per_branch
+        start = pl.multiple_of((chunk - branch * per_branch) * LANES, LANES)
+        copies.append(
+            pltpu.make_async_copy(
+                branch_here.at[number],
+                branch_ref.at[branch, :, pl.ds(start, LANES)],
+                sems.at[2 * number + 1],
+            )
+        )
+        copies[-1].start()
+    for copy in copies:
+        copy.wait()
+
+
+def write_out(kept, distances, values, outs, before):
+    count = len(distances)
+    return pl.pallas_call(
+        functools.partial(out_kernel, kept, distances),
+        out_shape=outs,
+        in_specs=[ANYWHERE] * len(before) + [IN_VMEM] * count,
+        out_specs=[pl.BlockSpec(memory_space=pltpu.HBM)] * 2,
+        scratch_shapes=[
+            pltpu.VMEM((count, outs[0].shape[1], LANES), F32),
+            pltpu.VMEM((count, outs[1].shape[0], LANES), F32),
+            pltpu.SemaphoreType.DMA((2 * count,)),
+        ],
+        input_output_aliases={0: 0, 1: 1} if before else {},
+        compiler_params=pltpu.CompilerParams(vmem_limit_bytes=VMEM_LIMIT),
+        cost_estimate=pl.CostEstimate(flops=1000, bytes_accessed=1000, transcendentals=0),
+    )(*before, *values)
 
 
 def plain_out_kernel(kept, in_ref, branch_ref, class_ref):
@@ -574,29 +615,28 @@
         one_f32 = jax.ShapeDtypeStruct((height, LANES), F32)
         made = call(
             functools.partial(late_kernel, kept, ahead, half),
-            [one_f32] * half + [jax.ShapeDtypeStruct((half, height, LANES), BF16)],
+            [one_f32] * half + [jax.ShapeDtypeStruct((height, LANES), BF16)] * half,
             [IN_VMEM] * len(late_ins),
             grad_flops,
             [pltpu.VMEM(chunks_f32.shape, F32)],
         )(*late_ins)
         order = list(range(half - 1, -1, -1))
-        arrived = swapped(made[half], 1)
+        arrived = {step: swapped(made[half + step], 1) for step in order}
         total = {step: made[step] + arrived[step].astype(F32) for step in order}
-        far = [swapped(total[step].astype(BF16), 2 * step) for step in order[:-1]]
+        far = {step: swapped(total[step].astype(BF16), 2 * step) for step in order[:-1]}
         summed = total[0]
-        for value in far:
-            summed = summed + value.astype(F32)
-        near = {0: summed.astype(BF16)}
-        other = {0: swapped(near[0], 1)}
         for step in order[:-1]:
-            near[step] = swapped(near[0], 2 * step)
-        for step in range(1, half):
-            other[step] = swapped(near[step], 1)
-        near = [near[step] for step in range(half)]
-        other = [other[step] for step in range(half)]
-        grad_branch, grad_class_t = call(
-            functools.partial(out_kernel, kept), outs, [IN_VMEM] * dom, 1000
-        )(*near, *other)
+            summed = lax.optimization_barrier(summed + far[step].astype(F32))
+        near = [summed.astype(BF16)]
+        near += [swapped(near[0], 2 * step) for step in range(1, half)]
+        other = [swapped(value, 1) for value in near]
+        results = []
+        for first in range(0, half, 2):
+            results = write_out(
+                kept, [2 * first, 2 * first + 2, 2 * first + 1, 2 * first + 3],
+                near[first : first + 2] + other[first : first + 2], outs, results,
+            )
+        grad_branch, grad_class_t = results
     else:
         grads = call(
             functools.partial(plain_late_kernel, kept, ahead),

time: 82.5 us -> 76.6 us (0.928)
  waiting for transfers between devices: 30.5 us -> 16.6 us
  starting transfers between devices: 32.3 us -> 39.4 us
    ppermute x23 -> x26, waiting for transfers between devices: 26.4 us -> 12.5 us  [swapped(): return lax.ppermute(value, axis, pairs)]
    ppermute x23 -> x26, starting transfers between devices: 16.6 us -> 23.8 us  [swapped(): return lax.ppermute(value, axis, pairs)]
    pallas_call x1 -> x2, Pallas kernels: 1.19 us -> 1.93 us  [write_out(): pl.pallas_call(functools.partial(out_kernel, kept, distances), out_shape=...]
  transfers between devices with their start and end apart: 29 -> 32, of which waited for: 17 -> 16; matrix products, arithmetic and copies ran while one was open for 0% -> 0% of each run, Pallas kernels for 9% -> 11%
where the time goes in v9:
time: 76.6 us; the launch traced here: 76.3 us
  starting transfers between devices  39.4 us (51%)
  waiting for transfers between devices  16.6 us (22%)
  Pallas kernels  15.1 us (20%)
  local copies, waits for them, and re-layouts  3.42 us (4%)
  between operations  1.64 us (2%)
    ppermute x26, starting transfers between devices, swapped(): return lax.ppermute(value, axis, pairs)  23.8 us
    ppermute x6, starting transfers between devices, passed_along(): return lax.ppermute(value, axis, pairs)  15.7 us
    ppermute x26, waiting for transfers between devices, swapped(): return lax.ppermute(value, axis, pairs)  12.5 us
    ppermute x6, waiting for transfers between devices, passed_along(): return lax.ppermute(value, axis, pairs)  4.16 us
    unnamed x22, local copies, waits for them, and re-layouts  3.34 us
    pallas_call x2, Pallas kernels, body(): call(functools.partial(hop_kernel, plan), [blocks_f32, slots_f32, slots_f...  2.37 us
    pallas_call x2, Pallas kernels, write_out(): pl.pallas_call(functools.partial(out_kernel, kept, distances), out_shape=...  1.93 us
    pallas_call x1, Pallas kernels, body(): call(functools.partial(late_kernel, kept, ahead, half), [one_f32] * half...  1.86 us
  transfers between devices with their start and end apart: 32, of which 16 were waited for; matrix products, arithmetic and copies ran while one was open for 0% of the time, Pallas kernels for 11%

profile of v9, /device:TPU:0, one launch (start us, length us, event | category | flops | bytes accessed | tf_op | source)
XLA Modules:
  0.0 76.3 jit_solution(15194130384139884093)
XLA Ops:
  0.7 1.8 %shard_map.139 = (f32[2,128,128]{2,1,0:T(8,128)}, f32[2,128,128]{2,1,0:T(8,128)}, f32[2,128,128]{2,1,0:T(8,128)}, bf16[272,128]{1,0:T(8,128)(2,1)}) custom-call(s32[2]{0:T(128)} %refs_0_.3, s32[2]{0:T(128)} %refs_1_.4, s32[1,2]{1,0:T(1,128)} %refs_2_.2, f32[2,128,128]{2,1,0:T(8,128)} %bitcast.8, s32[1,256]{1,0:T(1,128)} %bitcast.10), custom_call_target="tpu_custom_call" | custom-call | flops 1000 | bytes 1000 | tf_op jit(solution)/shard_map/pallas_call | solution.py:494
  2.4 3.0 %collective-permute-start.1 = (f32[2,128,128]{2,1,0:T(8,128)}, f32[2,128,128]{2,1,0:T(8,128)S(1)}, u32[]{:S(2)}, u32[]{:S(2)}) collective-permute-start(f32[2,128,128]{2,1,0:T(8,128)} %get-tuple-element.37), channel_id=1, source_target_pairs={{0,4},{4,8},{8,12},{12,16},{16,20},{20,24},{24,28},{28,0},{1,5},{5... | collective-permute-start | bytes 393224 | tf_op jit(solution)/shard_map/ppermute | solution.py:30
  5.5 3.1 %collective-permute-start.2 = (f32[2,128,128]{2,1,0:T(8,128)}, f32[2,128,128]{2,1,0:T(8,128)S(1)}, u32[]{:S(2)}, u32[]{:S(2)}) collective-permute-start(f32[2,128,128]{2,1,0:T(8,128)} %get-tuple-element.38), channel_id=1, source_target_pairs={{0,28},{4,0},{8,4},{12,8},{16,12},{20,16},{24,20},{28,24},{1,29},{... | collective-permute-start | bytes 393224 | tf_op jit(solution)/shard_map/ppermute | solution.py:30
  8.6 1.4 %copy-done.1 = bf16[4096,172]{0,1:T(8,128)(2,1)S(1)} copy-done((bf16[4096,172]{0,1:T(8,128)(2,1)S(1)}, bf16[4096,172]{0,1:T(8,128)(2,1)}, u32[]{:S(2)}) %copy-start.1) | copy-done | bytes 1409048
  9.9 1.0 %copy-done.2 = f32[8,128,128]{2,1,0:T(8,128)S(1)} copy-done((f32[8,128,128]{2,1,0:T(8,128)S(1)}, f32[8,128,128]{2,1,0:T(8,128)}, u32[]{:S(2)}) %copy-start.2) | copy-done | bytes 524312
  11.0 0.9 %copy-done.4 = f32[2,128,128]{2,1,0:T(8,128)S(1)} copy-done((f32[2,128,128]{2,1,0:T(8,128)S(1)}, f32[2,128,128]{2,1,0:T(8,128)}, u32[]{:S(2)}) %copy-start.4) | copy-done | bytes 131096
  11.9 0.1 shard_map.140
  12.8 0.1 concatenate.3.refs_0_.refs_1_.refs_5_
  12.9 0.6 collective-permute-done.2.refs_3_
  13.5 1.2 %shard_map.141 = (f32[2,128,128]{2,1,0:T(8,128)S(1)}, f32[2,128,128]{2,1,0:T(8,128)S(1)}, f32[2,128,128]{2,1,0:T(8,128)S(1)}, bf16[256,128]{1,0:T(8,128)(2,1)S(1)}) custom-call(s32[23]{0:T(128)S(1)} %concatenate.3.refs_0_.refs_1_.refs_5_, f32[2,128,128]{2,1,0:T(8,128)S(1)} %get-tuple-element.36.refs_1_.refs_0_, ...), custom_call_target="tpu_custom_call" | custom-call | flops 201326592 | bytes 1376256 | tf_op jit(solution)/shard_map/pallas_call | solution.py:537
  14.7 0.3 collective-permute-start.4
  15.0 4.5 %collective-permute-start.5 = (f32[2,128,128]{2,1,0:T(8,128)S(1)}, f32[2,128,128]{2,1,0:T(8,128)S(1)}, u32[]{:S(2)}, u32[]{:S(2)}) collective-permute-start(f32[2,128,128]{2,1,0:T(8,128)S(1)} %get-tuple-element.44), channel_id=1, source_target_pairs={{0,28},{4,0},{8,4},{12,8},{16,12},{20,16},{24,20},{28,24},{1,29},{... | collective-permute-start | bytes 393224 | tf_op jit(solution)/shard_map/ppermute | solution.py:30
  19.4 1.5 %collective-permute-start = (bf16[272,128]{1,0:T(8,128)(2,1)S(1)}, bf16[272,128]{1,0:T(8,128)(2,1)S(1)}, u32[]{:S(2)}, u32[]{:S(2)}) collective-permute-start(bf16[272,128]{1,0:T(8,128)(2,1)S(1)} %copy-done.3), channel_id=1, source_target_pairs={{0,2},{1,3},{2,0},{3,1},{4,6},{5,7},{6,4},{7,5},{8,10},{9,11},{10,... | collective-permute-start | bytes 208904 | tf_op jit(solution)/shard_map/ppermute | solution.py:35
  20.9 0.6 shard_map.142.refs_0_.refs_3_
  21.5 0.6 collective-permute-start.3
  22.1 0.3 collective-permute-done.4.refs_3_
  22.5 1.1 %collective-permute-done.5.refs_4_ = f32[2,128,128]{2,1,0:T(8,128)S(1)} collective-permute-done((f32[2,128,128]{2,1,0:T(8,128)S(1)}, f32[2,128,128]{2,1,0:T(8,128)S(1)}, u32[]{:S(2)}, u32[]{:S(2)}) %collective-permute-start.5) | collective-permute-done | bytes 131104 | tf_op jit(solution)/shard_map/ppermute | solution.py:30
  23.6 1.2 %shard_map.143 = (f32[2,128,128]{2,1,0:T(8,128)S(1)}, f32[2,128,128]{2,1,0:T(8,128)S(1)}, f32[2,128,128]{2,1,0:T(8,128)S(1)}) custom-call(f32[172,256]{1,0:T(8,128)S(1)} %shard_map.142.refs_0_.refs_3_, s32[23]{0:T(128)S(1)} %concatenate.3.refs_0_.refs_1_.refs_5_, f32[2,128,128]{2,1,0:T(8,128)S(1)} %get-tuple-element.42.refs_2_.refs_0_, ...), custom_call_target="tpu_custom_call" | custom-call | flops 201326592 | bytes 1179648 | tf_op jit(solution)/shard_map/pallas_call | solution.py:537
  24.8 0.1 collective-permute-start.10
  24.9 4.7 %collective-permute-start.11 = (f32[2,128,128]{2,1,0:T(8,128)S(1)}, f32[2,128,128]{2,1,0:T(8,128)S(1)}, u32[]{:S(2)}, u32[]{:S(2)}) collective-permute-start(f32[2,128,128]{2,1,0:T(8,128)S(1)} %get-tuple-element.47), channel_id=1, source_target_pairs={{0,28},{4,0},{8,4},{12,8},{16,12},{20,16},{24,20},{28,24},{1,29},{... | collective-permute-start | bytes 393224 | tf_op jit(solution)/shard_map/ppermute | solution.py:30
  29.6 0.5 collective-permute-start.8
  30.1 0.1 collective-permute-start.9
  30.2 0.6 shard_map.144.refs_5_
  30.8 0.1 collective-permute-done.7.refs_4_.refs_2_
  30.8 0.4 shard_map.146.refs_1_.refs_5_
  31.2 0.6 shard_map.145.refs_0_.refs_1_
  31.8 0.7 collective-permute-done.10.refs_7_
  32.6 1.4 %collective-permute-done.11.refs_8_ = f32[2,128,128]{2,1,0:T(8,128)S(1)} collective-permute-done((f32[2,128,128]{2,1,0:T(8,128)S(1)}, f32[2,128,128]{2,1,0:T(8,128)S(1)}, u32[]{:S(2)}, u32[]{:S(2)}) %collective-permute-start.11) | collective-permute-done | bytes 131104 | tf_op jit(solution)/shard_map/ppermute | solution.py:30
  34.0 1.2 %shard_map.147.refs_0_.refs_4_ = bf16[256,256]{1,0:T(8,128)(2,1)S(1)} custom-call(f32[172,256]{1,0:T(8,128)S(1)} %shard_map.145.refs_0_.refs_1_, s32[1,256]{1,0:T(1,128)S(1)} %shard_map.146.refs_1_.refs_5_, bf16[256,128]{1,0:T(8,128)(2,1)S(1)} %collective-permute-done.8.refs_2_.refs_3_, bf16[256,128]{1,0:T(8,128)(2,1)S(1)} %collective-permute-done.3.refs_1_.refs_3_, ...), custom_call_target="tpu_custom_call" | custom-call | flops 201326592 | bytes 393216 | tf_op jit(solution)/shard_map/pallas_call | solution.py:564
  35.2 0.1 collective-permute-start.15
  35.2 1.6 %collective-permute-start.14 = (bf16[256,256]{1,0:T(8,128)(2,1)S(1)}, bf16[256,256]{1,0:T(8,128)(2,1)S(1)}, u32[]{:S(2)}, u32[]{:S(2)}) collective-permute-start(bf16[256,256]{1,0:T(8,128)(2,1)S(1)} %shard_map.147.refs_0_.refs_4_), channel_id=1, source_target_pairs={{0,2},{1,3},{2,0},{3,1},{4,6},{5,7},{6,4},{7,5},{8,10},{9,11},{10,... | collective-permute-start | bytes 393224 | tf_op jit(solution)/shard_map/ppermute | solution.py:35
  36.8 0.8 %shard_map.148.refs_6_.refs_0_ = bf16[192,256]{1,0:T(8,128)(2,1)S(1)} custom-call(bf16[256,256]{1,0:T(8,128)(2,1)S(1)} %shard_map.147.refs_0_.refs_4_, f32[172,256]{1,0:T(8,128)S(1)} %shard_map.145.refs_0_.refs_1_, bf16[4,128,1024]{2,1,0:T(8,128)(2,1)S(1)} %copy-done, bf16[172,4096]{1,0:T(8,128)(2,1)S(1)} %get-tuple-element.41.refs_2_.refs_4_.refs_3_.refs_1_, ...), custom_call_target="tpu_custom_call" | custom-call | flops 1000 | bytes 1000 | tf_op jit(solution)/shard_map/pallas_call | solution.py:572
  37.6 0.2 collective-permute-start.12
  37.8 0.5 collective-permute-start.13
  38.3 0.3 shard_map.149
  38.6 0.3 collective-permute-done.12.refs_7_.refs_1_
  38.9 1.8 %shard_map.150.refs_0_ = f32[8,304,128]{2,1,0:T(8,128)S(1)} custom-call(bf16[272,128]{1,0:T(8,128)(2,1)S(1)} %copy-done.3, bf16[272,128]{1,0:T(8,128)(2,1)S(1)} %collective-permute-done.6.refs_2_.refs_1_, bf16[256,128]{1,0:T(8,128)(2,1)S(1)} %get-tuple-element.40.refs_2_, bf16[256,128]{1,0:T(8,128)(2,1)S(1)} %collective-permute-done.8.refs_2_.refs_3_, ...), custom_call_target="tpu_custom_call" | custom-call | flops 1000 | bytes 1000 | tf_op jit(solution)/shard_map/pallas_call | solution.py:588
  40.7 2.6 %collective-permute-done.13.refs_2_.refs_7_ = bf16[192,256]{1,0:T(8,128)(2,1)S(1)} collective-permute-done((bf16[192,256]{1,0:T(8,128)(2,1)S(1)}, bf16[192,256]{1,0:T(8,128)(2,1)S(1)}, u32[]{:S(2)}, u32[]{:S(2)}) %collective-permute-start.13) | collective-permute-done | bytes 98336 | tf_op jit(solution)/shard_map/ppermute | solution.py:35
  43.3 0.5 collective-permute-start.16
  43.8 1.0 %collective-permute-done.16.refs_3_.refs_8_ = bf16[192,256]{1,0:T(8,128)(2,1)S(1)} collective-permute-done((bf16[192,256]{1,0:T(8,128)(2,1)S(1)}, bf16[192,256]{1,0:T(8,128)(2,1)S(1)}, u32[]{:S(2)}, u32[]{:S(2)}) %collective-permute-start.16) | collective-permute-done | bytes 98336 | tf_op jit(solution)/shard_map/ppermute | solution.py:35
  44.8 1.9 %shard_map.152 = (f32[304,128]{1,0:T(8,128)S(1)}, f32[304,128]{1,0:T(8,128)S(1)}, f32[304,128]{1,0:T(8,128)S(1)}, f32[304,128]{1,0:T(8,128)S(1)}, bf16[304,128]{...) custom-call(f32[8,304,128]{2,1,0:T(8,128)S(1)} %shard_map.150.refs_0, ...), custom_call_target="tpu_custom_call" | custom-call | flops 771751936 | bytes 2801664 | tf_op jit(solution)/shard_map/pallas_call | solution.py:616
  46.6 0.1 collective-permute-start.19
  46.7 2.0 %collective-permute-start.18 = (bf16[304,128]{1,0:T(8,128)(2,1)S(1)}, bf16[304,128]{1,0:T(8,128)(2,1)S(1)}, u32[]{:S(2)}, u32[]{:S(2)}) collective-permute-start(bf16[304,128]{1,0:T(8,128)(2,1)S(1)} %get-tuple-element.54), channel_id=1, source_target_pairs={{0,4},{4,0},{8,12},{12,8},{16,20},{20,16},{24,28},{28,24},{1,5},{5... | collective-permute-start | bytes 233480 | tf_op jit(solution)/shard_map/ppermute | solution.py:35
  48.8 2.0 %collective-permute-start.23 = (bf16[304,128]{1,0:T(8,128)(2,1)S(1)}, bf16[304,128]{1,0:T(8,128)(2,1)S(1)}, u32[]{:S(2)}, u32[]{:S(2)}) collective-permute-start(bf16[304,128]{1,0:T(8,128)(2,1)S(1)} %get-tuple-element.60), channel_id=1, source_target_pairs={{0,4},{4,0},{8,12},{12,8},{16,20},{20,16},{24,28},{28,24},{1,5},{5... | collective-permute-start | bytes 233480 | tf_op jit(solution)/shard_map/ppermute | solution.py:35
  50.8 1.1 %collective-permute-done.19 = bf16[304,128]{1,0:T(8,128)(2,1)S(1)} collective-permute-done((bf16[304,128]{1,0:T(8,128)(2,1)S(1)}, bf16[304,128]{1,0:T(8,128)(2,1)S(1)}, u32[]{:S(2)}, u32[]{:S(2)}) %collective-permute-start.19) | collective-permute-done | bytes 77856 | tf_op jit(solution)/shard_map/ppermute | solution.py:35
  51.9 1.7 %collective-permute-start.20 = (bf16[304,128]{1,0:T(8,128)(2,1)S(1)}, bf16[304,128]{1,0:T(8,128)(2,1)S(1)}, u32[]{:S(2)}, u32[]{:S(2)}) collective-permute-start(bf16[304,128]{1,0:T(8,128)(2,1)S(1)} %add_convert_fusion.2), channel_id=1, source_target_pairs={{0,24},{4,28},{8,16},{12,20},{16,8},{20,12},{24,0},{28,4},{1,25},{... | collective-permute-start | bytes 233480 | tf_op jit(solution)/shard_map/ppermute | solution.py:35
  53.6 1.6 %collective-permute-done.21 = bf16[304,128]{1,0:T(8,128)(2,1)S(1)} collective-permute-done((bf16[304,128]{1,0:T(8,128)(2,1)S(1)}, bf16[304,128]{1,0:T(8,128)(2,1)S(1)}, u32[]{:S(2)}, u32[]{:S(2)}) %collective-permute-start.21) | collective-permute-done | bytes 77856 | tf_op jit(solution)/shard_map/ppermute | solution.py:35
  55.3 1.7 %collective-permute-start.22 = (bf16[304,128]{1,0:T(8,128)(2,1)S(1)}, bf16[304,128]{1,0:T(8,128)(2,1)S(1)}, u32[]{:S(2)}, u32[]{:S(2)}) collective-permute-start(bf16[304,128]{1,0:T(8,128)(2,1)S(1)} %add_convert_fusion.1), channel_id=1, source_target_pairs={{0,16},{4,20},{8,24},{12,28},{16,0},{20,4},{24,8},{28,12},{1,17},{... | collective-permute-start | bytes 233480 | tf_op jit(solution)/shard_map/ppermute | solution.py:35
  57.0 1.2 %collective-permute-start.24 = (bf16[304,128]{1,0:T(8,128)(2,1)S(1)}, bf16[304,128]{1,0:T(8,128)(2,1)S(1)}, u32[]{:S(2)}, u32[]{:S(2)}) collective-permute-start(bf16[304,128]{1,0:T(8,128)(2,1)S(1)} %add_convert_fusion), channel_id=1, source_target_pairs={{0,8},{4,12},{8,0},{12,4},{16,24},{20,28},{24,16},{28,20},{1,9},{5... | collective-permute-start | bytes 233480 | tf_op jit(solution)/shard_map/ppermute | solution.py:35
  58.1 0.1 collective-permute-done.20
  58.3 2.4 %collective-permute-done.22 = bf16[304,128]{1,0:T(8,128)(2,1)S(1)} collective-permute-done((bf16[304,128]{1,0:T(8,128)(2,1)S(1)}, bf16[304,128]{1,0:T(8,128)(2,1)S(1)}, u32[]{:S(2)}, u32[]{:S(2)}) %collective-permute-start.22) | collective-permute-done | bytes 77856 | tf_op jit(solution)/shard_map/ppermute | solution.py:35
  60.7 0.8 %collective-permute-done.24 = bf16[304,128]{1,0:T(8,128)(2,1)S(1)} collective-permute-done((bf16[304,128]{1,0:T(8,128)(2,1)S(1)}, bf16[304,128]{1,0:T(8,128)(2,1)S(1)}, u32[]{:S(2)}, u32[]{:S(2)}) %collective-permute-start.24) | collective-permute-done | bytes 77856 | tf_op jit(solution)/shard_map/ppermute | solution.py:35
  61.6 1.1 %collective-permute-start.25 = (bf16[304,128]{1,0:T(8,128)(2,1)S(1)}, bf16[304,128]{1,0:T(8,128)(2,1)S(1)}, u32[]{:S(2)}, u32[]{:S(2)}) collective-permute-start(bf16[304,128]{1,0:T(8,128)(2,1)S(1)} %convert_add_fusion.refs_0_), channel_id=1, source_target_pairs={{0,8},{4,12},{8,0},{12,4},{16,24},{20,28},{24,16},{28,20},{1,9},{5... | collective-permute-start | bytes 233480 | tf_op jit(solution)/shard_map/ppermute | solution.py:35
  62.6 1.9 %collective-permute-start.28 = (bf16[304,128]{1,0:T(8,128)(2,1)S(1)}, bf16[304,128]{1,0:T(8,128)(2,1)S(1)}, u32[]{:S(2)}, u32[]{:S(2)}) collective-permute-start(bf16[304,128]{1,0:T(8,128)(2,1)S(1)} %convert_add_fusion.refs_0_), channel_id=1, source_target_pairs={{0,16},{4,20},{8,24},{12,28},{16,0},{20,4},{24,8},{28,12},{1,17},{... | collective-permute-start | bytes 233480 | tf_op jit(solution)/shard_map/ppermute | solution.py:35
  64.5 1.5 %collective-permute-start.29 = (bf16[304,128]{1,0:T(8,128)(2,1)S(1)}, bf16[304,128]{1,0:T(8,128)(2,1)S(1)}, u32[]{:S(2)}, u32[]{:S(2)}) collective-permute-start(bf16[304,128]{1,0:T(8,128)(2,1)S(1)} %convert_add_fusion.refs_0_), channel_id=1, source_target_pairs={{0,24},{4,28},{8,16},{12,20},{16,8},{20,12},{24,0},{28,4},{1,25},{... | collective-permute-start | bytes 233480 | tf_op jit(solution)/shard_map/ppermute | solution.py:35
  66.0 0.7 collective-permute-start.26
  66.7 1.3 %collective-permute-start.27 = (bf16[304,128]{1,0:T(8,128)(2,1)S(1)}, bf16[304,128]{1,0:T(8,128)(2,1)S(1)}, u32[]{:S(2)}, u32[]{:S(2)}) collective-permute-start(bf16[304,128]{1,0:T(8,128)(2,1)S(1)} %collective-permute-done.25.refs_1_), channel_id=1, source_target_pairs={{0,4},{4,0},{8,12},{12,8},{16,20},{20,16},{24,28},{28,24},{1,5},{5... | collective-permute-start | bytes 233480 | tf_op jit(solution)/shard_map/ppermute | solution.py:35
  68.0 1.3 %collective-permute-done.28.refs_2_ = bf16[304,128]{1,0:T(8,128)(2,1)S(1)} collective-permute-done((bf16[304,128]{1,0:T(8,128)(2,1)S(1)}, bf16[304,128]{1,0:T(8,128)(2,1)S(1)}, u32[]{:S(2)}, u32[]{:S(2)}) %collective-permute-start.28) | collective-permute-done | bytes 77856 | tf_op jit(solution)/shard_map/ppermute | solution.py:35
  69.3 1.6 %collective-permute-start.30 = (bf16[304,128]{1,0:T(8,128)(2,1)S(1)}, bf16[304,128]{1,0:T(8,128)(2,1)S(1)}, u32[]{:S(2)}, u32[]{:S(2)}) collective-permute-start(bf16[304,128]{1,0:T(8,128)(2,1)S(1)} %collective-permute-done.28.refs_2_), channel_id=1, source_target_pairs={{0,4},{4,0},{8,12},{12,8},{16,20},{20,16},{24,28},{28,24},{1,5},{5... | collective-permute-start | bytes 233480 | tf_op jit(solution)/shard_map/ppermute | solution.py:35
  71.0 1.4 %collective-permute-start.31 = (bf16[304,128]{1,0:T(8,128)(2,1)S(1)}, bf16[304,128]{1,0:T(8,128)(2,1)S(1)}, u32[]{:S(2)}, u32[]{:S(2)}) collective-permute-start(bf16[304,128]{1,0:T(8,128)(2,1)S(1)} %collective-permute-done.29.refs_3_), channel_id=1, source_target_pairs={{0,4},{4,0},{8,12},{12,8},{16,20},{20,16},{24,28},{28,24},{1,5},{5... | collective-permute-start | bytes 233480 | tf_op jit(solution)/shard_map/ppermute | solution.py:35
  72.4 0.8 %shard_map.151 = f32[1,256]{1,0:T(1,128)} custom-call(bf16[192,256]{1,0:T(8,128)(2,1)S(1)} %shard_map.148.refs_6_.refs_0_, bf16[192,256]{1,0:T(8,128)(2,1)S(1)} %collective-permute-done.12.refs_7_.refs_1_, bf16[192,256]{1,0:T(8,128)(2,1)S(1)} %collective-permute-done.13.refs_2_.refs_7_, bf16[192,256]{1,0:T(8,128)(2,1)S(1)} %collective-permute-done.16.refs_3_.refs_8_), custom_call_target="tpu_custom_call" | custom-call | flops 1000 | bytes 1000 | tf_op jit(solution)/shard_map/pallas_call | solution.py:605
  73.2 1.0 %shard_map.153 = (f32[4,128,256]{2,1,0:T(8,128)}, f32[172,1024]{1,0:T(8,128)}) custom-call(bf16[304,128]{1,0:T(8,128)(2,1)S(1)} %convert_add_fusion.refs_0_, bf16[304,128]{1,0:T(8,128)(2,1)S(1)} %collective-permute-done.25.refs_1_, bf16[304,128]{1,0:T(8,128)(2,1)S(1)} %collective-permute-done.26.refs_2_, bf16[304,128]{1,0:T(8,128)(2,1)S(1)} %collective-permute-done.27.refs_3_), custom_call_target="tpu_custom_call" | custom-call | flops 1000 | bytes 1000 | tf_op jit(solution)/shard_map/pallas_call | solution.py:426
  74.2 1.2 %collective-permute-done.31.refs_5_ = bf16[304,128]{1,0:T(8,128)(2,1)S(1)} collective-permute-done((bf16[304,128]{1,0:T(8,128)(2,1)S(1)}, bf16[304,128]{1,0:T(8,128)(2,1)S(1)}, u32[]{:S(2)}, u32[]{:S(2)}) %collective-permute-start.31) | collective-permute-done | bytes 77856 | tf_op jit(solution)/shard_map/ppermute | solution.py:35
  75.3 1.0 %shard_map.154 = (f32[4,128,256]{2,1,0:T(8,128)}, f32[172,1024]{1,0:T(8,128)}) custom-call(f32[4,128,256]{2,1,0:T(8,128)} %get-tuple-element.61.refs_0_, f32[172,1024]{1,0:T(8,128)} %get-tuple-element.62.refs_1_, bf16[304,128]{1,0:T(8,128)(2,1)S(1)} %collective-permute-done.28.refs_2_, ...), custom_call_target="tpu_custom_call", output_to_operand_aliasing={{0}: (0, {}), {1}: (1, {})} | custom-call | flops 1000 | bytes 1000 | tf_op jit(solution)/shard_map/pallas_call | solution.py:426
  (45 shorter events, 0.3 us)
Async XLA Ops:
  0.6 12.1 %copy-start.8 = (s32[1,2]{1,0:T(1,128)S(1)}, s32[1,2]{1,0:T(1,128)}, u32[]{:S(2)}) copy-start(s32[1,2]{1,0:T(1,128)} %refs_2_.2) | copy-start | bytes 28
  0.6 12.1 %copy-start.7 = (s32[2]{0:T(128)S(1)}, s32[2]{0:T(128)}, u32[]{:S(2)}) copy-start(s32[2]{0:T(128)} %refs_1_.4) | copy-start | bytes 28
  0.7 12.1 %copy-start.6 = (s32[2]{0:T(128)S(1)}, s32[2]{0:T(128)}, u32[]{:S(2)}) copy-start(s32[2]{0:T(128)} %refs_0_.3) | copy-start | bytes 28
  0.7 12.1 %copy-start.10 = (s32[8]{0:T(128)S(1)}, s32[8]{0:T(128)}, u32[]{:S(2)}) copy-start(s32[8]{0:T(128)} %param.15) | copy-start | bytes 100
  0.7 12.1 %copy-start.9 = (s32[8]{0:T(128)S(1)}, s32[8]{0:T(128)}, u32[]{:S(2)}) copy-start(s32[8]{0:T(128)} %param.14) | copy-start | bytes 100
  2.4 10.4 %collective-permute-start.1 = (f32[2,128,128]{2,1,0:T(8,128)}, f32[2,128,128]{2,1,0:T(8,128)S(1)}, u32[]{:S(2)}, u32[]{:S(2)}) collective-permute-start(f32[2,128,128]{2,1,0:T(8,128)} %get-tuple-element.37), channel_id=1, source_target_pairs={{0,4},{4,8},{8,12},{12,16},{16,20},{20,24},{24,28},{28,0},{1,5},{5... | collective-permute-start | bytes 393224 | tf_op jit(solution)/shard_map/ppermute | solution.py:30
  5.5 8.0 %collective-permute-start.2 = (f32[2,128,128]{2,1,0:T(8,128)}, f32[2,128,128]{2,1,0:T(8,128)S(1)}, u32[]{:S(2)}, u32[]{:S(2)}) collective-permute-start(f32[2,128,128]{2,1,0:T(8,128)} %get-tuple-element.38), channel_id=1, source_target_pairs={{0,28},{4,0},{8,4},{12,8},{16,12},{20,16},{24,20},{28,24},{1,29},{... | collective-permute-start | bytes 393224 | tf_op jit(solution)/shard_map/ppermute | solution.py:30
  8.6 1.4 %copy-start.1 = (bf16[4096,172]{0,1:T(8,128)(2,1)S(1)}, bf16[4096,172]{0,1:T(8,128)(2,1)}, u32[]{:S(2)}) copy-start(bf16[4096,172]{0,1:T(8,128)(2,1)} %param.23) | copy-start | bytes 4227076
  9.9 1.0 %copy-start.2 = (f32[8,128,128]{2,1,0:T(8,128)S(1)}, f32[8,128,128]{2,1,0:T(8,128)}, u32[]{:S(2)}) copy-start(f32[8,128,128]{2,1,0:T(8,128)} %refs_1_.5) | copy-start | bytes 1572868
  11.0 0.9 %copy-start.4 = (f32[2,128,128]{2,1,0:T(8,128)S(1)}, f32[2,128,128]{2,1,0:T(8,128)}, u32[]{:S(2)}) copy-start(f32[2,128,128]{2,1,0:T(8,128)} %get-tuple-element.35.refs_0_) | copy-start | bytes 393220
  11.9 7.5 %copy-start.3 = (bf16[272,128]{1,0:T(8,128)(2,1)S(1)}, bf16[272,128]{1,0:T(8,128)(2,1)}, u32[]{:S(2)}) copy-start(bf16[272,128]{1,0:T(8,128)(2,1)} %get-tuple-element.34.refs_1_.refs_0_) | copy-start | bytes 208900
  11.9 9.0 %copy-start = (bf16[4,128,1024]{2,1,0:T(8,128)(2,1)S(1)}, bf16[4,128,1024]{2,1,0:T(8,128)(2,1)}, u32[]{:S(2)}) copy-start(bf16[4,128,1024]{2,1,0:T(8,128)(2,1)} %refs_9_.1) | copy-start | bytes 3145732
  14.7 7.8 %collective-permute-start.4 = (f32[2,128,128]{2,1,0:T(8,128)S(1)}, f32[2,128,128]{2,1,0:T(8,128)S(1)}, u32[]{:S(2)}, u32[]{:S(2)}) collective-permute-start(f32[2,128,128]{2,1,0:T(8,128)S(1)} %get-tuple-element.43), channel_id=1, source_target_pairs={{0,4},{4,8},{8,12},{12,16},{16,20},{20,24},{24,28},{28,0},{1,5},{5... | collective-permute-start | bytes 393224 | tf_op jit(solution)/shard_map/ppermute | solution.py:30
  15.0 8.6 %collective-permute-start.5 = (f32[2,128,128]{2,1,0:T(8,128)S(1)}, f32[2,128,128]{2,1,0:T(8,128)S(1)}, u32[]{:S(2)}, u32[]{:S(2)}) collective-permute-start(f32[2,128,128]{2,1,0:T(8,128)S(1)} %get-tuple-element.44), channel_id=1, source_target_pairs={{0,28},{4,0},{8,4},{12,8},{16,12},{20,16},{24,20},{28,24},{1,29},{... | collective-permute-start | bytes 393224 | tf_op jit(solution)/shard_map/ppermute | solution.py:30
  19.4 10.1 %collective-permute-start.6 = (bf16[272,128]{1,0:T(8,128)(2,1)S(1)}, bf16[272,128]{1,0:T(8,128)(2,1)S(1)}, u32[]{:S(2)}, u32[]{:S(2)}) collective-permute-start(bf16[272,128]{1,0:T(8,128)(2,1)S(1)} %copy-done.3), channel_id=1, source_target_pairs={{0,1},{1,0},{2,3},{3,2},{4,5},{5,4},{6,7},{7,6},{8,9},{9,8},{10,11... | collective-permute-start | bytes 208904 | tf_op jit(solution)/shard_map/ppermute | solution.py:35
  19.4 10.1 %collective-permute-start = (bf16[272,128]{1,0:T(8,128)(2,1)S(1)}, bf16[272,128]{1,0:T(8,128)(2,1)S(1)}, u32[]{:S(2)}, u32[]{:S(2)}) collective-permute-start(bf16[272,128]{1,0:T(8,128)(2,1)S(1)} %copy-done.3), channel_id=1, source_target_pairs={{0,2},{1,3},{2,0},{3,1},{4,6},{5,7},{6,4},{7,5},{8,10},{9,11},{10,... | collective-permute-start | bytes 208904 | tf_op jit(solution)/shard_map/ppermute | solution.py:35
  21.5 8.6 %collective-permute-start.3 = (bf16[256,128]{1,0:T(8,128)(2,1)S(1)}, bf16[256,128]{1,0:T(8,128)(2,1)S(1)}, u32[]{:S(2)}, u32[]{:S(2)}) collective-permute-start(bf16[256,128]{1,0:T(8,128)(2,1)S(1)} %get-tuple-element.40.refs_2_), channel_id=1, source_target_pairs={{0,2},{1,3},{2,0},{3,1},{4,6},{5,7},{6,4},{7,5},{8,10},{9,11},{10,... | collective-permute-start | bytes 196616 | tf_op jit(solution)/shard_map/ppermute | solution.py:35
  24.8 7.8 %collective-permute-start.10 = (f32[2,128,128]{2,1,0:T(8,128)S(1)}, f32[2,128,128]{2,1,0:T(8,128)S(1)}, u32[]{:S(2)}, u32[]{:S(2)}) collective-permute-start(f32[2,128,128]{2,1,0:T(8,128)S(1)} %get-tuple-element.46), channel_id=1, source_target_pairs={{0,4},{4,8},{8,12},{12,16},{16,20},{20,24},{24,28},{28,0},{1,5},{5... | collective-permute-start | bytes 393224 | tf_op jit(solution)/shard_map/ppermute | solution.py:30
  24.9 6.0 %copy-start.5 = (s32[1,256]{1,0:T(1,128)S(1)}, s32[1,256]{1,0:T(1,128)}, u32[]{:S(2)}) copy-start(s32[1,256]{1,0:T(1,128)} %refs_4_.1) | copy-start | bytes 3076
  24.9 9.1 %collective-permute-start.11 = (f32[2,128,128]{2,1,0:T(8,128)S(1)}, f32[2,128,128]{2,1,0:T(8,128)S(1)}, u32[]{:S(2)}, u32[]{:S(2)}) collective-permute-start(f32[2,128,128]{2,1,0:T(8,128)S(1)} %get-tuple-element.47), channel_id=1, source_target_pairs={{0,28},{4,0},{8,4},{12,8},{16,12},{20,16},{24,20},{28,24},{1,29},{... | collective-permute-start | bytes 393224 | tf_op jit(solution)/shard_map/ppermute | solution.py:30
  29.6 1.3 %collective-permute-start.7 = (bf16[272,128]{1,0:T(8,128)(2,1)S(1)}, bf16[272,128]{1,0:T(8,128)(2,1)S(1)}, u32[]{:S(2)}, u32[]{:S(2)}) collective-permute-start(bf16[272,128]{1,0:T(8,128)(2,1)S(1)} %collective-permute-done.refs_0_.refs_3_.refs_1_), channel_id=1, source_target_pairs={{0,1},{1,0},{2,3},{3,2},{4,5},{5,4},{6,7},{7,6},{8,9},{9,8},{10,11... | collective-permute-start | bytes 208904 | tf_op jit(solution)/shard_map/ppermute | solution.py:35
  29.6 2.2 %collective-permute-start.8 = (bf16[256,128]{1,0:T(8,128)(2,1)S(1)}, bf16[256,128]{1,0:T(8,128)(2,1)S(1)}, u32[]{:S(2)}, u32[]{:S(2)}) collective-permute-start(bf16[256,128]{1,0:T(8,128)(2,1)S(1)} %get-tuple-element.40.refs_2_), channel_id=1, source_target_pairs={{0,1},{1,0},{2,3},{3,2},{4,5},{5,4},{6,7},{7,6},{8,9},{9,8},{10,11... | collective-permute-start | bytes 196616 | tf_op jit(solution)/shard_map/ppermute | solution.py:35
  30.1 1.7 %collective-permute-start.9 = (bf16[256,128]{1,0:T(8,128)(2,1)S(1)}, bf16[256,128]{1,0:T(8,128)(2,1)S(1)}, u32[]{:S(2)}, u32[]{:S(2)}) collective-permute-start(bf16[256,128]{1,0:T(8,128)(2,1)S(1)} %collective-permute-done.3.refs_1_.refs_3_), channel_id=1, source_target_pairs={{0,1},{1,0},{2,3},{3,2},{4,5},{5,4},{6,7},{7,6},{8,9},{9,8},{10,11... | collective-permute-start | bytes 196616 | tf_op jit(solution)/shard_map/ppermute | solution.py:35
  35.2 3.8 %collective-permute-start.15 = (bf16[256,256]{1,0:T(8,128)(2,1)S(1)}, bf16[256,256]{1,0:T(8,128)(2,1)S(1)}, u32[]{:S(2)}, u32[]{:S(2)}) collective-permute-start(bf16[256,256]{1,0:T(8,128)(2,1)S(1)} %shard_map.147.refs_0_.refs_4_), channel_id=1, source_target_pairs={{0,1},{1,0},{2,3},{3,2},{4,5},{5,4},{6,7},{7,6},{8,9},{9,8},{10,11... | collective-permute-start | bytes 393224 | tf_op jit(solution)/shard_map/ppermute | solution.py:35
  35.2 8.0 %collective-permute-start.14 = (bf16[256,256]{1,0:T(8,128)(2,1)S(1)}, bf16[256,256]{1,0:T(8,128)(2,1)S(1)}, u32[]{:S(2)}, u32[]{:S(2)}) collective-permute-start(bf16[256,256]{1,0:T(8,128)(2,1)S(1)} %shard_map.147.refs_0_.refs_4_), channel_id=1, source_target_pairs={{0,2},{1,3},{2,0},{3,1},{4,6},{5,7},{6,4},{7,5},{8,10},{9,11},{10,... | collective-permute-start | bytes 393224 | tf_op jit(solution)/shard_map/ppermute | solution.py:35
  37.6 1.3 %collective-permute-start.12 = (bf16[192,256]{1,0:T(8,128)(2,1)S(1)}, bf16[192,256]{1,0:T(8,128)(2,1)S(1)}, u32[]{:S(2)}, u32[]{:S(2)}) collective-permute-start(bf16[192,256]{1,0:T(8,128)(2,1)S(1)} %shard_map.148.refs_6_.refs_0_), channel_id=1, source_target_pairs={{0,1},{1,0},{2,3},{3,2},{4,5},{5,4},{6,7},{7,6},{8,9},{9,8},{10,11... | collective-permute-start | bytes 294920 | tf_op jit(solution)/shard_map/ppermute | solution.py:35
  37.8 5.5 %collective-permute-start.13 = (bf16[192,256]{1,0:T(8,128)(2,1)S(1)}, bf16[192,256]{1,0:T(8,128)(2,1)S(1)}, u32[]{:S(2)}, u32[]{:S(2)}) collective-permute-start(bf16[192,256]{1,0:T(8,128)(2,1)S(1)} %shard_map.148.refs_6_.refs_0_), channel_id=1, source_target_pairs={{0,2},{1,3},{2,0},{3,1},{4,6},{5,7},{6,4},{7,5},{8,10},{9,11},{10,... | collective-permute-start | bytes 294920 | tf_op jit(solution)/shard_map/ppermute | solution.py:35
  43.3 1.5 %collective-permute-start.17 = (bf16[256,256]{1,0:T(8,128)(2,1)S(1)}, bf16[256,256]{1,0:T(8,128)(2,1)S(1)}, u32[]{:S(2)}, u32[]{:S(2)}) collective-permute-start(bf16[256,256]{1,0:T(8,128)(2,1)S(1)} %collective-permute-done.14.refs_5_), channel_id=1, source_target_pairs={{0,1},{1,0},{2,3},{3,2},{4,5},{5,4},{6,7},{7,6},{8,9},{9,8},{10,11... | collective-permute-start | bytes 393224 | tf_op jit(solution)/shard_map/ppermute | solution.py:35
  43.3 1.5 %collective-permute-start.16 = (bf16[192,256]{1,0:T(8,128)(2,1)S(1)}, bf16[192,256]{1,0:T(8,128)(2,1)S(1)}, u32[]{:S(2)}, u32[]{:S(2)}) collective-permute-start(bf16[192,256]{1,0:T(8,128)(2,1)S(1)} %collective-permute-done.13.refs_2_.refs_7_), channel_id=1, source_target_pairs={{0,1},{1,0},{2,3},{3,2},{4,5},{5,4},{6,7},{7,6},{8,9},{9,8},{10,11... | collective-permute-start | bytes 294920 | tf_op jit(solution)/shard_map/ppermute | solution.py:35
  46.6 5.3 %collective-permute-start.19 = (bf16[304,128]{1,0:T(8,128)(2,1)S(1)}, bf16[304,128]{1,0:T(8,128)(2,1)S(1)}, u32[]{:S(2)}, u32[]{:S(2)}) collective-permute-start(bf16[304,128]{1,0:T(8,128)(2,1)S(1)} %get-tuple-element.56), channel_id=1, source_target_pairs={{0,4},{4,0},{8,12},{12,8},{16,20},{20,16},{24,28},{28,24},{1,5},{5... | collective-permute-start | bytes 233480 | tf_op jit(solution)/shard_map/ppermute | solution.py:35
  46.7 11.4 %collective-permute-start.18 = (bf16[304,128]{1,0:T(8,128)(2,1)S(1)}, bf16[304,128]{1,0:T(8,128)(2,1)S(1)}, u32[]{:S(2)}, u32[]{:S(2)}) collective-permute-start(bf16[304,128]{1,0:T(8,128)(2,1)S(1)} %get-tuple-element.54), channel_id=1, source_target_pairs={{0,4},{4,0},{8,12},{12,8},{16,20},{20,16},{24,28},{28,24},{1,5},{5... | collective-permute-start | bytes 233480 | tf_op jit(solution)/shard_map/ppermute | solution.py:35
  48.7 6.5 %collective-permute-start.21 = (bf16[304,128]{1,0:T(8,128)(2,1)S(1)}, bf16[304,128]{1,0:T(8,128)(2,1)S(1)}, u32[]{:S(2)}, u32[]{:S(2)}) collective-permute-start(bf16[304,128]{1,0:T(8,128)(2,1)S(1)} %get-tuple-element.58), channel_id=1, source_target_pairs={{0,4},{4,0},{8,12},{12,8},{16,20},{20,16},{24,28},{28,24},{1,5},{5... | collective-permute-start | bytes 233480 | tf_op jit(solution)/shard_map/ppermute | solution.py:35
  48.8 8.1 %collective-permute-start.23 = (bf16[304,128]{1,0:T(8,128)(2,1)S(1)}, bf16[304,128]{1,0:T(8,128)(2,1)S(1)}, u32[]{:S(2)}, u32[]{:S(2)}) collective-permute-start(bf16[304,128]{1,0:T(8,128)(2,1)S(1)} %get-tuple-element.60), channel_id=1, source_target_pairs={{0,4},{4,0},{8,12},{12,8},{16,20},{20,16},{24,28},{28,24},{1,5},{5... | collective-permute-start | bytes 233480 | tf_op jit(solution)/shard_map/ppermute | solution.py:35
  51.9 6.3 %collective-permute-start.20 = (bf16[304,128]{1,0:T(8,128)(2,1)S(1)}, bf16[304,128]{1,0:T(8,128)(2,1)S(1)}, u32[]{:S(2)}, u32[]{:S(2)}) collective-permute-start(bf16[304,128]{1,0:T(8,128)(2,1)S(1)} %add_convert_fusion.2), channel_id=1, source_target_pairs={{0,24},{4,28},{8,16},{12,20},{16,8},{20,12},{24,0},{28,4},{1,25},{... | collective-permute-start | bytes 233480 | tf_op jit(solution)/shard_map/ppermute | solution.py:35
  55.3 5.4 %collective-permute-start.22 = (bf16[304,128]{1,0:T(8,128)(2,1)S(1)}, bf16[304,128]{1,0:T(8,128)(2,1)S(1)}, u32[]{:S(2)}, u32[]{:S(2)}) collective-permute-start(bf16[304,128]{1,0:T(8,128)(2,1)S(1)} %add_convert_fusion.1), channel_id=1, source_target_pairs={{0,16},{4,20},{8,24},{12,28},{16,0},{20,4},{24,8},{28,12},{1,17},{... | collective-permute-start | bytes 233480 | tf_op jit(solution)/shard_map/ppermute | solution.py:35
  57.0 4.6 %collective-permute-start.24 = (bf16[304,128]{1,0:T(8,128)(2,1)S(1)}, bf16[304,128]{1,0:T(8,128)(2,1)S(1)}, u32[]{:S(2)}, u32[]{:S(2)}) collective-permute-start(bf16[304,128]{1,0:T(8,128)(2,1)S(1)} %add_convert_fusion), channel_id=1, source_target_pairs={{0,8},{4,12},{8,0},{12,4},{16,24},{20,28},{24,16},{28,20},{1,9},{5... | collective-permute-start | bytes 233480 | tf_op jit(solution)/shard_map/ppermute | solution.py:35
  61.6 5.1 %collective-permute-start.25 = (bf16[304,128]{1,0:T(8,128)(2,1)S(1)}, bf16[304,128]{1,0:T(8,128)(2,1)S(1)}, u32[]{:S(2)}, u32[]{:S(2)}) collective-permute-start(bf16[304,128]{1,0:T(8,128)(2,1)S(1)} %convert_add_fusion.refs_0_), channel_id=1, source_target_pairs={{0,8},{4,12},{8,0},{12,4},{16,24},{20,28},{24,16},{28,20},{1,9},{5... | collective-permute-start | bytes 233480 | tf_op jit(solution)/shard_map/ppermute | solution.py:35
  62.6 6.7 %collective-permute-start.28 = (bf16[304,128]{1,0:T(8,128)(2,1)S(1)}, bf16[304,128]{1,0:T(8,128)(2,1)S(1)}, u32[]{:S(2)}, u32[]{:S(2)}) collective-permute-start(bf16[304,128]{1,0:T(8,128)(2,1)S(1)} %convert_add_fusion.refs_0_), channel_id=1, source_target_pairs={{0,16},{4,20},{8,24},{12,28},{16,0},{20,4},{24,8},{28,12},{1,17},{... | collective-permute-start | bytes 233480 | tf_op jit(solution)/shard_map/ppermute | solution.py:35
  64.5 6.4 %collective-permute-start.29 = (bf16[304,128]{1,0:T(8,128)(2,1)S(1)}, bf16[304,128]{1,0:T(8,128)(2,1)S(1)}, u32[]{:S(2)}, u32[]{:S(2)}) collective-permute-start(bf16[304,128]{1,0:T(8,128)(2,1)S(1)} %convert_add_fusion.refs_0_), channel_id=1, source_target_pairs={{0,24},{4,28},{8,16},{12,20},{16,8},{20,12},{24,0},{28,4},{1,25},{... | collective-permute-start | bytes 233480 | tf_op jit(solution)/shard_map/ppermute | solution.py:35
  66.0 7.2 %collective-permute-start.26 = (bf16[304,128]{1,0:T(8,128)(2,1)S(1)}, bf16[304,128]{1,0:T(8,128)(2,1)S(1)}, u32[]{:S(2)}, u32[]{:S(2)}) collective-permute-start(bf16[304,128]{1,0:T(8,128)(2,1)S(1)} %convert_add_fusion.refs_0_), channel_id=1, source_target_pairs={{0,4},{4,0},{8,12},{12,8},{16,20},{20,16},{24,28},{28,24},{1,5},{5... | collective-permute-start | bytes 233480 | tf_op jit(solution)/shard_map/ppermute | solution.py:35
  66.7 6.5 %collective-permute-start.27 = (bf16[304,128]{1,0:T(8,128)(2,1)S(1)}, bf16[304,128]{1,0:T(8,128)(2,1)S(1)}, u32[]{:S(2)}, u32[]{:S(2)}) collective-permute-start(bf16[304,128]{1,0:T(8,128)(2,1)S(1)} %collective-permute-done.25.refs_1_), channel_id=1, source_target_pairs={{0,4},{4,0},{8,12},{12,8},{16,20},{20,16},{24,28},{28,24},{1,5},{5... | collective-permute-start | bytes 233480 | tf_op jit(solution)/shard_map/ppermute | solution.py:35
  69.3 4.9 %collective-permute-start.30 = (bf16[304,128]{1,0:T(8,128)(2,1)S(1)}, bf16[304,128]{1,0:T(8,128)(2,1)S(1)}, u32[]{:S(2)}, u32[]{:S(2)}) collective-permute-start(bf16[304,128]{1,0:T(8,128)(2,1)S(1)} %collective-permute-done.28.refs_2_), channel_id=1, source_target_pairs={{0,4},{4,0},{8,12},{12,8},{16,20},{20,16},{24,28},{28,24},{1,5},{5... | collective-permute-start | bytes 233480 | tf_op jit(solution)/shard_map/ppermute | solution.py:35
  71.0 4.4 %collective-permute-start.31 = (bf16[304,128]{1,0:T(8,128)(2,1)S(1)}, bf16[304,128]{1,0:T(8,128)(2,1)S(1)}, u32[]{:S(2)}, u32[]{:S(2)}) collective-permute-start(bf16[304,128]{1,0:T(8,128)(2,1)S(1)} %collective-permute-done.29.refs_3_), channel_id=1, source_target_pairs={{0,4},{4,0},{8,12},{12,8},{16,20},{20,16},{24,28},{28,24},{1,5},{5... | collective-permute-start | bytes 233480 | tf_op jit(solution)/shard_map/ppermute | solution.py:35

commit v10 on v9

--- a/solution.py
+++ b/solution.py
@@ -252,25 +252,20 @@
     extend(cur_ref, low_ref, high_ref, ext_ref)
     blocks = next_blocks(plan, plan_ref, cur_ref, tiles_ref, ext_ref)
     for number, block in enumerate(blocks):
-        size, width = block.shape
+        width = block.shape[1]
         columns = slice(number * width, (number + 1) * width)
-        out_ref[:size, columns] = block.astype(BF16)
-        out_ref[size:, columns] = cur_ref[number].astype(BF16)
-
-
-def stacked(ref, place, width):
-    size = ref.shape[0] // 2
+        out_ref[:, columns] = block.astype(BF16)
+
+
+def stacked(ref, width):
     parts = ref.shape[1] // width
-    return [
-        ref[place * size : (place + 1) * size, part * width : (part + 1) * width]
-        for part in range(parts)
-    ]
+    return [ref[:, part * width : (part + 1) * width] for part in range(parts)]
 
 
 def loss_and_gradient_kernel(
     row_scale, rows_ref, before_ref, w_ref, wc_ref, order_ref, label_ref, out_ref
 ):
-    rows_b = jnp.concatenate(stacked(rows_ref, 0, w_ref.shape[1]), axis=0)
+    rows_b = jnp.concatenate(stacked(rows_ref, w_ref.shape[1]), axis=0)
     logits = before_ref[...] + branch_logits(w_ref.shape[0] - 1, rows_b, w_ref, wc_ref)
     classes, rows = logits.shape
     kept = up_to(classes, 16)
@@ -305,18 +300,17 @@
         wct_ref[branch] = pad_ref[...].T[:, :kept].astype(BF16)
 
 
-def add_chunks(kept, more, row_refs, last_refs, dlogit_refs, w_ref, wt_ref, wct_ref, chunks_ref):
+def add_chunks(kept, before_ref, row_refs, last_refs, dlogit_refs, w_ref, wt_ref, wct_ref, chunks_ref):
     members = len(last_refs)
     branches, own, width = wt_ref.shape
     nodes = last_refs[0].shape[1]
     hid = w_ref.shape[2]
     all_rows = []
-    for branch in range(branches - 2):
+    for branch in range(branches - 1):
         ours = row_refs[branch * members : (branch + 1) * members]
         all_rows.append(jnp.concatenate([ref[:nodes] for ref in ours], axis=0))
-    for place in (1, 0):
-        ours = [rows for ref in last_refs for rows in stacked(ref, place, width)]
-        all_rows.append(jnp.concatenate(ours, axis=0))
+    ours = [rows for ref in last_refs for rows in stacked(ref, width)]
+    all_rows.append(jnp.concatenate(ours, axis=0))
     dlogits_t = jnp.concatenate([ref[:kept] for ref in dlogit_refs], axis=1)
     own_class = branches * own
     first = lax.axis_index("shuf") * own_class
@@ -327,7 +321,7 @@
         chosen = jnp.where(which == branch, all_rows[branch], chosen)
 
     def put(chunk, rows, value):
-        chunks_ref[chunk, rows] = chunks_ref[chunk, rows] + value if more else value
+        chunks_ref[chunk, rows] = value if before_ref is None else before_ref[chunk, rows] + value
 
     hidden = jnp.maximum(matmul(chosen, w_ref[which, :, columns]), 0.0).astype(BF16)
     class_t = matmul(dlogits_t, hidden)
@@ -355,12 +349,11 @@
 
 
 def early_kernel(kept, members, *refs):
-    add_chunks(kept, False, *split_refs(members, refs[:-1]), refs[-1])
+    add_chunks(kept, None, *split_refs(members, refs[:-1]), refs[-1])
 
 
 def late_chunks(kept, members, early_ref, refs, chunks_ref):
-    chunks_ref[...] = early_ref[...]
-    add_chunks(kept, True, *split_refs(members, refs), chunks_ref)
+    add_chunks(kept, early_ref, *split_refs(members, refs), chunks_ref)
 
 
 def late_kernel(kept, members, half, early_ref, *refs):
@@ -526,7 +519,7 @@
             logits_f32,
             [IN_VMEM] * (3 + len(before)),
             forward_flops,
-            after=[members[shuf // 2] for members in gathered] if hop == HOPS - 1 else [],
+            after=[members[shuf // 2] for members in gathered[:2]] if hop == HOPS - 1 else [],
         )(current, w_branch, w_class_t, *before)
         if hop == 0:
             first_logits = logits
@@ -536,7 +529,7 @@
         if hop < HOPS - 1:
             current, to_left, to_right, *rows = call(
                 functools.partial(hop_kernel, plan),
-                [blocks_f32, slots_f32, slots_f32] + [rows_b16] * (hop < HOPS - 2),
+                [blocks_f32, slots_f32, slots_f32, rows_b16],
                 [IN_SMEM] + [IN_VMEM] * 4,
                 hop_flops,
                 [ext],
@@ -563,7 +556,7 @@
 
     last_rows = call(
         functools.partial(last_hop_kernel, plan),
-        jax.ShapeDtypeStruct((2 * block, local * width), BF16),
+        jax.ShapeDtypeStruct((block, local * width), BF16),
         [IN_SMEM] + [IN_VMEM] * 4,
         hop_flops,
         [ext],
@@ -574,6 +567,7 @@
         jax.ShapeDtypeStruct((kept + 16, nodes), BF16),
         [IN_VMEM] * 6,
         1000,
+        after=[gathered[2][shuf // 2]],
     )(last_rows, logits, w_branch, w_class_t, batch_order, label_mine)
     chunks = own_class // LANES
     height = kept + width
@@ -588,8 +582,9 @@
     early = call(
         functools.partial(early_kernel, kept, ahead),
         chunks_f32,
-        [IN_VMEM] * (4 * ahead + 3),
+        [IN_VMEM] * (5 * ahead + 3),
         1000,
+        after=[across_rows],
     )(
         *[member for members in gathered for member in members[:ahead]],
         *close_rows, *close, *weights,
@@ -620,22 +615,27 @@
             grad_flops,
             [pltpu.VMEM(chunks_f32.shape, F32)],
         )(*late_ins)
-        order = list(range(half - 1, -1, -1))
+        order = sorted(range(half), key=lambda step: (step % 2 == 0, -step))
         arrived = {step: swapped(made[half + step], 1) for step in order}
         total = {step: made[step] + arrived[step].astype(F32) for step in order}
-        far = {step: swapped(total[step].astype(BF16), 2 * step) for step in order[:-1]}
+        distance = 1
+        while distance < half:
+            far = [step for step in total if step & distance]
+            for step in far:
+                came = swapped(total.pop(step).astype(BF16), 2 * distance)
+                kept_step = step ^ distance
+                total[kept_step] = lax.optimization_barrier(
+                    total[kept_step] + came.astype(F32)
+                )
+            distance *= 2
         summed = total[0]
-        for step in order[:-1]:
-            summed = lax.optimization_barrier(summed + far[step].astype(F32))
         near = [summed.astype(BF16)]
         near += [swapped(near[0], 2 * step) for step in range(1, half)]
         other = [swapped(value, 1) for value in near]
         results = []
-        for first in range(0, half, 2):
-            results = write_out(
-                kept, [2 * first, 2 * first + 2, 2 * first + 1, 2 * first + 3],
-                near[first : first + 2] + other[first : first + 2], outs, results,
-            )
+        places = [2 * step for step in range(half)] + [2 * step + 1 for step in range(half)]
+        for part in (slice(0, -half // 2), slice(-half // 2, None)):
+            results = write_out(kept, places[part], (near + other)[part], outs, results)
         grad_branch, grad_class_t = results
     else:
         grads = call(

time: 76.6 us -> 78.5 us (1.025)
  starting transfers between devices: 39.4 us -> 40.4 us
  waiting for transfers between devices: 16.6 us -> 17.5 us
    ppermute x26 -> x29, waiting for transfers between devices: 12.5 us -> 15.4 us  [swapped(): return lax.ppermute(value, axis, pairs)]
    ppermute x6, waiting for transfers between devices: 4.16 us -> 2.04 us  [passed_along(): return lax.ppermute(value, axis, pairs)]
    ppermute x26 -> x29, starting transfers between devices: 23.8 us -> 24.8 us  [swapped(): return lax.ppermute(value, axis, pairs)]
  transfers between devices with their start and end apart: 32 -> 35, of which waited for: 16 -> 16; matrix products, arithmetic and copies ran while one was open for 0% -> 0% of each run, Pallas kernels for 11% -> 11%
where the time goes in v10:
time: 78.5 us; the launch traced here: 78.2 us
  starting transfers between devices  40.4 us (51%)
  waiting for transfers between devices  17.5 us (22%)
  Pallas kernels  15.1 us (19%)
  local copies, waits for them, and re-layouts  3.42 us (4%)
  between operations  1.67 us (2%)
    ppermute x29, starting transfers between devices, swapped(): return lax.ppermute(value, axis, pairs)  24.8 us
    ppermute x6, starting transfers between devices, passed_along(): return lax.ppermute(value, axis, pairs)  15.7 us
    ppermute x29, waiting for transfers between devices, swapped(): return lax.ppermute(value, axis, pairs)  15.4 us
    unnamed x22, local copies, waits for them, and re-layouts  3.34 us
    pallas_call x2, Pallas kernels, body(): call(functools.partial(hop_kernel, plan), [blocks_f32, slots_f32, slots_f...  2.38 us
    ppermute x6, waiting for transfers between devices, passed_along(): return lax.ppermute(value, axis, pairs)  2.04 us
    pallas_call x2, Pallas kernels, write_out(): pl.pallas_call(functools.partial(out_kernel, kept, distances), out_shape=...  1.93 us
    pallas_call x1, Pallas kernels, body(): call(functools.partial(late_kernel, kept, ahead, half), [one_f32] * half...  1.85 us
  transfers between devices with their start and end apart: 35, of which 16 were waited for; matrix products, arithmetic and copies ran while one was open for 0% of the time, Pallas kernels for 11%

profile of v10, /device:TPU:0, one launch (start us, length us, event | category | flops | bytes accessed | tf_op | source)
XLA Modules:
  0.0 78.2 jit_solution(13236213325060363607)
XLA Ops:
  0.7 1.7 %shard_map.139 = (f32[2,128,128]{2,1,0:T(8,128)}, f32[2,128,128]{2,1,0:T(8,128)}, f32[2,128,128]{2,1,0:T(8,128)}, bf16[272,128]{1,0:T(8,128)(2,1)}) custom-call(s32[2]{0:T(128)} %refs_0_.3, s32[2]{0:T(128)} %refs_1_.4, s32[1,2]{1,0:T(1,128)} %refs_2_.1, f32[2,128,128]{2,1,0:T(8,128)} %bitcast.8, s32[1,256]{1,0:T(1,128)} %bitcast.10), custom_call_target="tpu_custom_call" | custom-call | flops 1000 | bytes 1000 | tf_op jit(solution)/shard_map/pallas_call | solution.py:487
  2.4 3.0 %collective-permute-start = (f32[2,128,128]{2,1,0:T(8,128)}, f32[2,128,128]{2,1,0:T(8,128)S(1)}, u32[]{:S(2)}, u32[]{:S(2)}) collective-permute-start(f32[2,128,128]{2,1,0:T(8,128)} %get-tuple-element.38), channel_id=1, source_target_pairs={{0,4},{4,8},{8,12},{12,16},{16,20},{20,24},{24,28},{28,0},{1,5},{5... | collective-permute-start | bytes 393224 | tf_op jit(solution)/shard_map/ppermute | solution.py:30
  5.5 3.1 %collective-permute-start.1 = (f32[2,128,128]{2,1,0:T(8,128)}, f32[2,128,128]{2,1,0:T(8,128)S(1)}, u32[]{:S(2)}, u32[]{:S(2)}) collective-permute-start(f32[2,128,128]{2,1,0:T(8,128)} %get-tuple-element.39), channel_id=1, source_target_pairs={{0,28},{4,0},{8,4},{12,8},{16,12},{20,16},{24,20},{28,24},{1,29},{... | collective-permute-start | bytes 393224 | tf_op jit(solution)/shard_map/ppermute | solution.py:30
  8.6 1.4 %copy-done.1 = bf16[4096,172]{0,1:T(8,128)(2,1)S(1)} copy-done((bf16[4096,172]{0,1:T(8,128)(2,1)S(1)}, bf16[4096,172]{0,1:T(8,128)(2,1)}, u32[]{:S(2)}) %copy-start.1) | copy-done | bytes 1409048
  9.9 1.0 %copy-done.2 = f32[8,128,128]{2,1,0:T(8,128)S(1)} copy-done((f32[8,128,128]{2,1,0:T(8,128)S(1)}, f32[8,128,128]{2,1,0:T(8,128)}, u32[]{:S(2)}) %copy-start.2) | copy-done | bytes 524312
  11.0 0.9 %copy-done.4 = f32[2,128,128]{2,1,0:T(8,128)S(1)} copy-done((f32[2,128,128]{2,1,0:T(8,128)S(1)}, f32[2,128,128]{2,1,0:T(8,128)}, u32[]{:S(2)}) %copy-start.4) | copy-done | bytes 131096
  11.9 0.1 shard_map.140
  12.8 0.1 concatenate.3.refs_0_.refs_1_.refs_5_
  12.9 0.6 collective-permute-done.1.refs_3_
  13.4 1.2 %shard_map.142 = (f32[2,128,128]{2,1,0:T(8,128)S(1)}, f32[2,128,128]{2,1,0:T(8,128)S(1)}, f32[2,128,128]{2,1,0:T(8,128)S(1)}, bf16[256,128]{1,0:T(8,128)(2,1)S(1)}) custom-call(s32[23]{0:T(128)S(1)} %concatenate.3.refs_0_.refs_1_.refs_5_, f32[2,128,128]{2,1,0:T(8,128)S(1)} %get-tuple-element.36.refs_0_.refs_1_, ...), custom_call_target="tpu_custom_call" | custom-call | flops 201326592 | bytes 1376256 | tf_op jit(solution)/shard_map/pallas_call | solution.py:530
  14.6 0.3 collective-permute-start.2
  15.0 4.4 %collective-permute-start.3 = (f32[2,128,128]{2,1,0:T(8,128)S(1)}, f32[2,128,128]{2,1,0:T(8,128)S(1)}, u32[]{:S(2)}, u32[]{:S(2)}) collective-permute-start(f32[2,128,128]{2,1,0:T(8,128)S(1)} %get-tuple-element.43), channel_id=1, source_target_pairs={{0,28},{4,0},{8,4},{12,8},{16,12},{20,16},{24,20},{28,24},{1,29},{... | collective-permute-start | bytes 393224 | tf_op jit(solution)/shard_map/ppermute | solution.py:30
  19.4 1.5 %collective-permute-start.5 = (bf16[272,128]{1,0:T(8,128)(2,1)S(1)}, bf16[272,128]{1,0:T(8,128)(2,1)S(1)}, u32[]{:S(2)}, u32[]{:S(2)}) collective-permute-start(bf16[272,128]{1,0:T(8,128)(2,1)S(1)} %copy-done.3), channel_id=1, source_target_pairs={{0,2},{1,3},{2,0},{3,1},{4,6},{5,7},{6,4},{7,5},{8,10},{9,11},{10,... | collective-permute-start | bytes 208904 | tf_op jit(solution)/shard_map/ppermute | solution.py:35
  20.9 0.6 shard_map.141.refs_0_.refs_3_
  21.5 0.6 collective-permute-start.6
  22.1 0.3 collective-permute-done.2.refs_3_
  22.5 1.1 %collective-permute-done.3.refs_4_ = f32[2,128,128]{2,1,0:T(8,128)S(1)} collective-permute-done((f32[2,128,128]{2,1,0:T(8,128)S(1)}, f32[2,128,128]{2,1,0:T(8,128)S(1)}, u32[]{:S(2)}, u32[]{:S(2)}) %collective-permute-start.3) | collective-permute-done | bytes 131104 | tf_op jit(solution)/shard_map/ppermute | solution.py:30
  23.6 1.2 %shard_map.143 = (f32[2,128,128]{2,1,0:T(8,128)S(1)}, f32[2,128,128]{2,1,0:T(8,128)S(1)}, f32[2,128,128]{2,1,0:T(8,128)S(1)}, bf16[256,128]{1,0:T(8,128)(2,1)S(1)}) custom-call(f32[172,256]{1,0:T(8,128)S(1)} %shard_map.141.refs_0_.refs_3_, s32[23]{0:T(128)S(1)} %concatenate.3.refs_0_.refs_1_.refs_5_, f32[2,128,128]{2,1,0:T(8,128)S(1)} %get-tuple-element.41.refs_2_.refs_0_, ...), custom_call_target="tpu_custom_call" | custom-call | flops 201326592 | bytes 1376256 | tf_op jit(solution)/shard_map/pallas_call | solution.py:530
  24.8 4.7 %collective-permute-start.12 = (f32[2,128,128]{2,1,0:T(8,128)S(1)}, f32[2,128,128]{2,1,0:T(8,128)S(1)}, u32[]{:S(2)}, u32[]{:S(2)}) collective-permute-start(f32[2,128,128]{2,1,0:T(8,128)S(1)} %get-tuple-element.49), channel_id=1, source_target_pairs={{0,28},{4,0},{8,4},{12,8},{16,12},{20,16},{24,20},{28,24},{1,29},{... | collective-permute-start | bytes 393224 | tf_op jit(solution)/shard_map/ppermute | solution.py:30
  29.6 0.5 collective-permute-start.9
  30.2 0.7 collective-permute-done.8.refs_4_.refs_2_
  30.8 1.5 %collective-permute-start.4 = (bf16[256,128]{1,0:T(8,128)(2,1)S(1)}, bf16[256,128]{1,0:T(8,128)(2,1)S(1)}, u32[]{:S(2)}, u32[]{:S(2)}) collective-permute-start(bf16[256,128]{1,0:T(8,128)(2,1)S(1)} %get-tuple-element.44.refs_5_), channel_id=1, source_target_pairs={{0,2},{1,3},{2,0},{3,1},{4,6},{5,7},{6,4},{7,5},{8,10},{9,11},{10,... | collective-permute-start | bytes 196616 | tf_op jit(solution)/shard_map/ppermute | solution.py:35
  32.3 0.6 shard_map.144.refs_5_
  32.9 0.4 shard_map.146.refs_1_.refs_6_
  33.3 0.6 shard_map.145.refs_0_.refs_2_
  34.0 1.2 %shard_map.147.refs_1_.refs_7_ = bf16[128,256]{1,0:T(8,128)(2,1)S(1)} custom-call(f32[172,256]{1,0:T(8,128)S(1)} %shard_map.145.refs_0_.refs_2_, s32[1,256]{1,0:T(1,128)S(1)} %shard_map.146.refs_1_.refs_6_, bf16[256,128]{1,0:T(8,128)(2,1)S(1)} %collective-permute-done.9.refs_2_.refs_4_, bf16[256,128]{1,0:T(8,128)(2,1)S(1)} %collective-permute-done.6.refs_1_.refs_3_, ...), custom_call_target="tpu_custom_call" | custom-call | flops 201326592 | bytes 196608 | tf_op jit(solution)/shard_map/pallas_call | solution.py:557
  35.2 0.8 %shard_map.148.refs_9_.refs_0_ = bf16[192,256]{1,0:T(8,128)(2,1)S(1)} custom-call(bf16[256,128]{1,0:T(8,128)(2,1)S(1)} %collective-permute-done.4.refs_0_.refs_5_, bf16[128,256]{1,0:T(8,128)(2,1)S(1)} %shard_map.147.refs_1_.refs_7_, f32[172,256]{1,0:T(8,128)S(1)} %shard_map.145.refs_0_.refs_2_, bf16[4,128,1024]{2,1,0:T(8,128)(2,1)S(1)} %copy-done, ...), custom_call_target="tpu_custom_call" | custom-call | flops 1000 | bytes 1000 | tf_op jit(solution)/shard_map/pallas_call | solution.py:565
  36.0 1.5 %collective-permute-start.14 = (bf16[192,256]{1,0:T(8,128)(2,1)S(1)}, bf16[192,256]{1,0:T(8,128)(2,1)S(1)}, u32[]{:S(2)}, u32[]{:S(2)}) collective-permute-start(bf16[192,256]{1,0:T(8,128)(2,1)S(1)} %shard_map.148.refs_9_.refs_0_), channel_id=1, source_target_pairs={{0,2},{1,3},{2,0},{3,1},{4,6},{5,7},{6,4},{7,5},{8,10},{9,11},{10,... | collective-permute-start | bytes 294920 | tf_op jit(solution)/shard_map/ppermute | solution.py:35
  37.5 0.2 collective-permute-start.16
  37.7 0.5 collective-permute-start.15
  38.3 0.3 shard_map.149
  38.6 0.2 collective-permute-done.16.refs_6_
  38.8 3.8 %collective-permute-done.15.refs_0_.refs_7_ = bf16[128,256]{1,0:T(8,128)(2,1)S(1)} collective-permute-done((bf16[128,256]{1,0:T(8,128)(2,1)S(1)}, bf16[128,256]{1,0:T(8,128)(2,1)S(1)}, u32[]{:S(2)}, u32[]{:S(2)}) %collective-permute-start.15) | collective-permute-done | bytes 65568 | tf_op jit(solution)/shard_map/ppermute | solution.py:35
  42.6 1.8 %shard_map.150.refs_0_ = f32[8,304,128]{2,1,0:T(8,128)S(1)} custom-call(bf16[128,256]{1,0:T(8,128)(2,1)S(1)} %collective-permute-done.15.refs_0_.refs_7_, bf16[272,128]{1,0:T(8,128)(2,1)S(1)} %copy-done.3, bf16[272,128]{1,0:T(8,128)(2,1)S(1)} %collective-permute-done.7.refs_2_, bf16[256,128]{1,0:T(8,128)(2,1)S(1)} %get-tuple-element.46.refs_3_, ...), custom_call_target="tpu_custom_call" | custom-call | flops 1000 | bytes 1000 | tf_op jit(solution)/shard_map/pallas_call | solution.py:582
  44.4 0.1 collective-permute-start.18
  44.5 0.5 collective-permute-start.19
  45.0 0.1 collective-permute-start.20
  45.1 0.8 %collective-permute-done.19.refs_6_ = bf16[256,128]{1,0:T(8,128)(2,1)S(1)} collective-permute-done((bf16[256,128]{1,0:T(8,128)(2,1)S(1)}, bf16[256,128]{1,0:T(8,128)(2,1)S(1)}, u32[]{:S(2)}, u32[]{:S(2)}) %collective-permute-start.19) | collective-permute-done | bytes 65568 | tf_op jit(solution)/shard_map/ppermute | solution.py:35
  45.9 0.4 collective-permute-done.20.refs_8_
  46.3 1.8 %shard_map.152 = (f32[304,128]{1,0:T(8,128)S(1)}, f32[304,128]{1,0:T(8,128)S(1)}, f32[304,128]{1,0:T(8,128)S(1)}, f32[304,128]{1,0:T(8,128)S(1)}, bf16[304,128]{...) custom-call(f32[8,304,128]{2,1,0:T(8,128)S(1)} %shard_map.150.refs_0, ...), custom_call_target="tpu_custom_call" | custom-call | flops 771751936 | bytes 2801664 | tf_op jit(solution)/shard_map/pallas_call | solution.py:611
  48.1 0.1 collective-permute-start.25
  48.2 2.0 %collective-permute-start.22 = (bf16[304,128]{1,0:T(8,128)(2,1)S(1)}, bf16[304,128]{1,0:T(8,128)(2,1)S(1)}, u32[]{:S(2)}, u32[]{:S(2)}) collective-permute-start(bf16[304,128]{1,0:T(8,128)(2,1)S(1)} %get-tuple-element.58), channel_id=1, source_target_pairs={{0,4},{4,0},{8,12},{12,8},{16,20},{20,16},{24,28},{28,24},{1,5},{5... | collective-permute-start | bytes 233480 | tf_op jit(solution)/shard_map/ppermute | solution.py:35
  50.2 0.1 collective-permute-start.21
  50.3 1.9 %collective-permute-start.24 = (bf16[304,128]{1,0:T(8,128)(2,1)S(1)}, bf16[304,128]{1,0:T(8,128)(2,1)S(1)}, u32[]{:S(2)}, u32[]{:S(2)}) collective-permute-start(bf16[304,128]{1,0:T(8,128)(2,1)S(1)} %get-tuple-element.60), channel_id=1, source_target_pairs={{0,4},{4,0},{8,12},{12,8},{16,20},{20,16},{24,28},{28,24},{1,5},{5... | collective-permute-start | bytes 233480 | tf_op jit(solution)/shard_map/ppermute | solution.py:35
  52.2 1.1 %collective-permute-done.25 = bf16[304,128]{1,0:T(8,128)(2,1)S(1)} collective-permute-done((bf16[304,128]{1,0:T(8,128)(2,1)S(1)}, bf16[304,128]{1,0:T(8,128)(2,1)S(1)}, u32[]{:S(2)}, u32[]{:S(2)}) %collective-permute-start.25) | collective-permute-done | bytes 77856 | tf_op jit(solution)/shard_map/ppermute | solution.py:35
  53.4 1.5 %collective-permute-start.26 = (bf16[304,128]{1,0:T(8,128)(2,1)S(1)}, bf16[304,128]{1,0:T(8,128)(2,1)S(1)}, u32[]{:S(2)}, u32[]{:S(2)}) collective-permute-start(bf16[304,128]{1,0:T(8,128)(2,1)S(1)} %add_convert_fusion), channel_id=1, source_target_pairs={{0,8},{4,12},{8,0},{12,4},{16,24},{20,28},{24,16},{28,20},{1,9},{5... | collective-permute-start | bytes 233480 | tf_op jit(solution)/shard_map/ppermute | solution.py:35
  54.9 0.1 collective-permute-done.22
  55.1 1.5 %collective-permute-start.23 = (bf16[304,128]{1,0:T(8,128)(2,1)S(1)}, bf16[304,128]{1,0:T(8,128)(2,1)S(1)}, u32[]{:S(2)}, u32[]{:S(2)}) collective-permute-start(bf16[304,128]{1,0:T(8,128)(2,1)S(1)} %add_convert_fusion.1), channel_id=1, source_target_pairs={{0,8},{4,12},{8,0},{12,4},{16,24},{20,28},{24,16},{28,20},{1,9},{5... | collective-permute-start | bytes 233480 | tf_op jit(solution)/shard_map/ppermute | solution.py:35
  56.6 1.0 %collective-permute-done.24 = bf16[304,128]{1,0:T(8,128)(2,1)S(1)} collective-permute-done((bf16[304,128]{1,0:T(8,128)(2,1)S(1)}, bf16[304,128]{1,0:T(8,128)(2,1)S(1)}, u32[]{:S(2)}, u32[]{:S(2)}) %collective-permute-start.24) | collective-permute-done | bytes 77856 | tf_op jit(solution)/shard_map/ppermute | solution.py:35
  57.6 0.3 collective-permute-done.26
  58.0 1.7 %collective-permute-start.27 = (bf16[304,128]{1,0:T(8,128)(2,1)S(1)}, bf16[304,128]{1,0:T(8,128)(2,1)S(1)}, u32[]{:S(2)}, u32[]{:S(2)}) collective-permute-start(bf16[304,128]{1,0:T(8,128)(2,1)S(1)} %convert_add_fusion.1), channel_id=1, source_target_pairs={{0,16},{4,20},{8,24},{12,28},{16,0},{20,4},{24,8},{28,12},{1,17},{... | collective-permute-start | bytes 233480 | tf_op jit(solution)/shard_map/ppermute | solution.py:35
  59.7 3.6 %collective-permute-done.27 = bf16[304,128]{1,0:T(8,128)(2,1)S(1)} collective-permute-done((bf16[304,128]{1,0:T(8,128)(2,1)S(1)}, bf16[304,128]{1,0:T(8,128)(2,1)S(1)}, u32[]{:S(2)}, u32[]{:S(2)}) %collective-permute-start.27) | collective-permute-done | bytes 77856 | tf_op jit(solution)/shard_map/ppermute | solution.py:35
  63.4 1.5 %collective-permute-start.28 = (bf16[304,128]{1,0:T(8,128)(2,1)S(1)}, bf16[304,128]{1,0:T(8,128)(2,1)S(1)}, u32[]{:S(2)}, u32[]{:S(2)}) collective-permute-start(bf16[304,128]{1,0:T(8,128)(2,1)S(1)} %convert_add_fusion.refs_0_), channel_id=1, source_target_pairs={{0,8},{4,12},{8,0},{12,4},{16,24},{20,28},{24,16},{28,20},{1,9},{5... | collective-permute-start | bytes 233480 | tf_op jit(solution)/shard_map/ppermute | solution.py:35
  64.9 0.8 %collective-permute-start.29 = (bf16[304,128]{1,0:T(8,128)(2,1)S(1)}, bf16[304,128]{1,0:T(8,128)(2,1)S(1)}, u32[]{:S(2)}, u32[]{:S(2)}) collective-permute-start(bf16[304,128]{1,0:T(8,128)(2,1)S(1)} %convert_add_fusion.refs_0_), channel_id=1, source_target_pairs={{0,16},{4,20},{8,24},{12,28},{16,0},{20,4},{24,8},{28,12},{1,17},{... | collective-permute-start | bytes 233480 | tf_op jit(solution)/shard_map/ppermute | solution.py:35
  65.7 2.1 %collective-permute-start.30 = (bf16[304,128]{1,0:T(8,128)(2,1)S(1)}, bf16[304,128]{1,0:T(8,128)(2,1)S(1)}, u32[]{:S(2)}, u32[]{:S(2)}) collective-permute-start(bf16[304,128]{1,0:T(8,128)(2,1)S(1)} %convert_add_fusion.refs_0_), channel_id=1, source_target_pairs={{0,24},{4,28},{8,16},{12,20},{16,8},{20,12},{24,0},{28,4},{1,25},{... | collective-permute-start | bytes 233480 | tf_op jit(solution)/shard_map/ppermute | solution.py:35
  67.8 1.1 %collective-permute-start.31 = (bf16[304,128]{1,0:T(8,128)(2,1)S(1)}, bf16[304,128]{1,0:T(8,128)(2,1)S(1)}, u32[]{:S(2)}, u32[]{:S(2)}) collective-permute-start(bf16[304,128]{1,0:T(8,128)(2,1)S(1)} %convert_add_fusion.refs_0_), channel_id=1, source_target_pairs={{0,4},{4,0},{8,12},{12,8},{16,20},{20,16},{24,28},{28,24},{1,5},{5... | collective-permute-start | bytes 233480 | tf_op jit(solution)/shard_map/ppermute | solution.py:35
  69.0 0.9 %collective-permute-start.32 = (bf16[304,128]{1,0:T(8,128)(2,1)S(1)}, bf16[304,128]{1,0:T(8,128)(2,1)S(1)}, u32[]{:S(2)}, u32[]{:S(2)}) collective-permute-start(bf16[304,128]{1,0:T(8,128)(2,1)S(1)} %collective-permute-done.28.refs_1_), channel_id=1, source_target_pairs={{0,4},{4,0},{8,12},{12,8},{16,20},{20,16},{24,28},{28,24},{1,5},{5... | collective-permute-start | bytes 233480 | tf_op jit(solution)/shard_map/ppermute | solution.py:35
  69.9 2.3 %collective-permute-done.29.refs_2_ = bf16[304,128]{1,0:T(8,128)(2,1)S(1)} collective-permute-done((bf16[304,128]{1,0:T(8,128)(2,1)S(1)}, bf16[304,128]{1,0:T(8,128)(2,1)S(1)}, u32[]{:S(2)}, u32[]{:S(2)}) %collective-permute-start.29) | collective-permute-done | bytes 77856 | tf_op jit(solution)/shard_map/ppermute | solution.py:35
  72.2 2.4 %collective-permute-start.34 = (bf16[304,128]{1,0:T(8,128)(2,1)S(1)}, bf16[304,128]{1,0:T(8,128)(2,1)S(1)}, u32[]{:S(2)}, u32[]{:S(2)}) collective-permute-start(bf16[304,128]{1,0:T(8,128)(2,1)S(1)} %collective-permute-done.30.refs_3_), channel_id=1, source_target_pairs={{0,4},{4,0},{8,12},{12,8},{16,20},{20,16},{24,28},{28,24},{1,5},{5... | collective-permute-start | bytes 233480 | tf_op jit(solution)/shard_map/ppermute | solution.py:35
  74.6 0.8 %shard_map.151 = f32[1,256]{1,0:T(1,128)} custom-call(bf16[192,256]{1,0:T(8,128)(2,1)S(1)} %shard_map.148.refs_9_.refs_0_, bf16[192,256]{1,0:T(8,128)(2,1)S(1)} %collective-permute-done.13.refs_10_.refs_1_, bf16[192,256]{1,0:T(8,128)(2,1)S(1)} %collective-permute-done.14.refs_2_.refs_9_, bf16[192,256]{1,0:T(8,128)(2,1)S(1)} %collective-permute-done.18.refs_3_.refs_10_), custom_call_target="tpu_custom_call" | custom-call | flops 1000 | bytes 1000 | tf_op jit(solution)/shard_map/pallas_call | solution.py:600
  75.4 1.1 %shard_map.153 = (f32[4,128,256]{2,1,0:T(8,128)}, f32[172,1024]{1,0:T(8,128)}) custom-call(bf16[304,128]{1,0:T(8,128)(2,1)S(1)} %convert_add_fusion.refs_0_, bf16[304,128]{1,0:T(8,128)(2,1)S(1)} %collective-permute-done.28.refs_1_, bf16[304,128]{1,0:T(8,128)(2,1)S(1)} %collective-permute-done.29.refs_2_, ...), custom_call_target="tpu_custom_call" | custom-call | flops 1000 | bytes 1000 | tf_op jit(solution)/shard_map/pallas_call | solution.py:419
  76.5 0.1 collective-permute-done.33.refs_2_
  76.6 0.8 %collective-permute-done.34.refs_3_ = bf16[304,128]{1,0:T(8,128)(2,1)S(1)} collective-permute-done((bf16[304,128]{1,0:T(8,128)(2,1)S(1)}, bf16[304,128]{1,0:T(8,128)(2,1)S(1)}, u32[]{:S(2)}, u32[]{:S(2)}) %collective-permute-start.34) | collective-permute-done | bytes 77856 | tf_op jit(solution)/shard_map/ppermute | solution.py:35
  77.4 0.8 %shard_map.154 = (f32[4,128,256]{2,1,0:T(8,128)}, f32[172,1024]{1,0:T(8,128)}) custom-call(f32[4,128,256]{2,1,0:T(8,128)} %get-tuple-element.63.refs_0_, f32[172,1024]{1,0:T(8,128)} %get-tuple-element.64.refs_1_, bf16[304,128]{1,0:T(8,128)(2,1)S(1)} %collective-permute-done.33.refs_2_, ...), custom_call_target="tpu_custom_call", output_to_operand_aliasing={{0}: (0, {}), {1}: (1, {})} | custom-call | flops 1000 | bytes 1000 | tf_op jit(solution)/shard_map/pallas_call | solution.py:419
  (50 shorter events, 0.4 us)
Async XLA Ops:
  0.6 12.1 %copy-start.6 = (s32[2]{0:T(128)S(1)}, s32[2]{0:T(128)}, u32[]{:S(2)}) copy-start(s32[2]{0:T(128)} %refs_0_.3) | copy-start | bytes 28
  0.6 12.1 %copy-start.7 = (s32[2]{0:T(128)S(1)}, s32[2]{0:T(128)}, u32[]{:S(2)}) copy-start(s32[2]{0:T(128)} %refs_1_.4) | copy-start | bytes 28
  0.7 12.1 %copy-start.8 = (s32[1,2]{1,0:T(1,128)S(1)}, s32[1,2]{1,0:T(1,128)}, u32[]{:S(2)}) copy-start(s32[1,2]{1,0:T(1,128)} %refs_2_.1) | copy-start | bytes 28
  0.7 12.1 %copy-start.9 = (s32[8]{0:T(128)S(1)}, s32[8]{0:T(128)}, u32[]{:S(2)}) copy-start(s32[8]{0:T(128)} %param.14) | copy-start | bytes 100
  0.7 12.1 %copy-start.10 = (s32[8]{0:T(128)S(1)}, s32[8]{0:T(128)}, u32[]{:S(2)}) copy-start(s32[8]{0:T(128)} %param.15) | copy-start | bytes 100
  2.4 10.4 %collective-permute-start = (f32[2,128,128]{2,1,0:T(8,128)}, f32[2,128,128]{2,1,0:T(8,128)S(1)}, u32[]{:S(2)}, u32[]{:S(2)}) collective-permute-start(f32[2,128,128]{2,1,0:T(8,128)} %get-tuple-element.38), channel_id=1, source_target_pairs={{0,4},{4,8},{8,12},{12,16},{16,20},{20,24},{24,28},{28,0},{1,5},{5... | collective-permute-start | bytes 393224 | tf_op jit(solution)/shard_map/ppermute | solution.py:30
  5.5 8.0 %collective-permute-start.1 = (f32[2,128,128]{2,1,0:T(8,128)}, f32[2,128,128]{2,1,0:T(8,128)S(1)}, u32[]{:S(2)}, u32[]{:S(2)}) collective-permute-start(f32[2,128,128]{2,1,0:T(8,128)} %get-tuple-element.39), channel_id=1, source_target_pairs={{0,28},{4,0},{8,4},{12,8},{16,12},{20,16},{24,20},{28,24},{1,29},{... | collective-permute-start | bytes 393224 | tf_op jit(solution)/shard_map/ppermute | solution.py:30
  8.6 1.4 %copy-start.1 = (bf16[4096,172]{0,1:T(8,128)(2,1)S(1)}, bf16[4096,172]{0,1:T(8,128)(2,1)}, u32[]{:S(2)}) copy-start(bf16[4096,172]{0,1:T(8,128)(2,1)} %param.23) | copy-start | bytes 4227076
  9.9 1.0 %copy-start.2 = (f32[8,128,128]{2,1,0:T(8,128)S(1)}, f32[8,128,128]{2,1,0:T(8,128)}, u32[]{:S(2)}) copy-start(f32[8,128,128]{2,1,0:T(8,128)} %refs_1_.5) | copy-start | bytes 1572868
  11.0 0.9 %copy-start.4 = (f32[2,128,128]{2,1,0:T(8,128)S(1)}, f32[2,128,128]{2,1,0:T(8,128)}, u32[]{:S(2)}) copy-start(f32[2,128,128]{2,1,0:T(8,128)} %get-tuple-element.35.refs_0_) | copy-start | bytes 393220
  11.9 7.5 %copy-start.3 = (bf16[272,128]{1,0:T(8,128)(2,1)S(1)}, bf16[272,128]{1,0:T(8,128)(2,1)}, u32[]{:S(2)}) copy-start(bf16[272,128]{1,0:T(8,128)(2,1)} %get-tuple-element.45.refs_1_) | copy-start | bytes 208900
  11.9 9.0 %copy-start = (bf16[4,128,1024]{2,1,0:T(8,128)(2,1)S(1)}, bf16[4,128,1024]{2,1,0:T(8,128)(2,1)}, u32[]{:S(2)}) copy-start(bf16[4,128,1024]{2,1,0:T(8,128)(2,1)} %refs_11_.3) | copy-start | bytes 3145732
  14.6 7.8 %collective-permute-start.2 = (f32[2,128,128]{2,1,0:T(8,128)S(1)}, f32[2,128,128]{2,1,0:T(8,128)S(1)}, u32[]{:S(2)}, u32[]{:S(2)}) collective-permute-start(f32[2,128,128]{2,1,0:T(8,128)S(1)} %get-tuple-element.42), channel_id=1, source_target_pairs={{0,4},{4,8},{8,12},{12,16},{16,20},{20,24},{24,28},{28,0},{1,5},{5... | collective-permute-start | bytes 393224 | tf_op jit(solution)/shard_map/ppermute | solution.py:30
  15.0 8.6 %collective-permute-start.3 = (f32[2,128,128]{2,1,0:T(8,128)S(1)}, f32[2,128,128]{2,1,0:T(8,128)S(1)}, u32[]{:S(2)}, u32[]{:S(2)}) collective-permute-start(f32[2,128,128]{2,1,0:T(8,128)S(1)} %get-tuple-element.43), channel_id=1, source_target_pairs={{0,28},{4,0},{8,4},{12,8},{16,12},{20,16},{24,20},{28,24},{1,29},{... | collective-permute-start | bytes 393224 | tf_op jit(solution)/shard_map/ppermute | solution.py:30
  19.4 10.1 %collective-permute-start.5 = (bf16[272,128]{1,0:T(8,128)(2,1)S(1)}, bf16[272,128]{1,0:T(8,128)(2,1)S(1)}, u32[]{:S(2)}, u32[]{:S(2)}) collective-permute-start(bf16[272,128]{1,0:T(8,128)(2,1)S(1)} %copy-done.3), channel_id=1, source_target_pairs={{0,2},{1,3},{2,0},{3,1},{4,6},{5,7},{6,4},{7,5},{8,10},{9,11},{10,... | collective-permute-start | bytes 208904 | tf_op jit(solution)/shard_map/ppermute | solution.py:35
  20.9 8.7 %collective-permute-start.7 = (bf16[272,128]{1,0:T(8,128)(2,1)S(1)}, bf16[272,128]{1,0:T(8,128)(2,1)S(1)}, u32[]{:S(2)}, u32[]{:S(2)}) collective-permute-start(bf16[272,128]{1,0:T(8,128)(2,1)S(1)} %copy-done.3), channel_id=1, source_target_pairs={{0,1},{1,0},{2,3},{3,2},{4,5},{5,4},{6,7},{7,6},{8,9},{9,8},{10,11... | collective-permute-start | bytes 208904 | tf_op jit(solution)/shard_map/ppermute | solution.py:35
  21.5 8.6 %collective-permute-start.6 = (bf16[256,128]{1,0:T(8,128)(2,1)S(1)}, bf16[256,128]{1,0:T(8,128)(2,1)S(1)}, u32[]{:S(2)}, u32[]{:S(2)}) collective-permute-start(bf16[256,128]{1,0:T(8,128)(2,1)S(1)} %get-tuple-element.46.refs_3_), channel_id=1, source_target_pairs={{0,2},{1,3},{2,0},{3,1},{4,6},{5,7},{6,4},{7,5},{8,10},{9,11},{10,... | collective-permute-start | bytes 196616 | tf_op jit(solution)/shard_map/ppermute | solution.py:35
  24.8 9.2 %collective-permute-start.11 = (f32[2,128,128]{2,1,0:T(8,128)S(1)}, f32[2,128,128]{2,1,0:T(8,128)S(1)}, u32[]{:S(2)}, u32[]{:S(2)}) collective-permute-start(f32[2,128,128]{2,1,0:T(8,128)S(1)} %get-tuple-element.48), channel_id=1, source_target_pairs={{0,4},{4,8},{8,12},{12,16},{16,20},{20,24},{24,28},{28,0},{1,5},{5... | collective-permute-start | bytes 393224 | tf_op jit(solution)/shard_map/ppermute | solution.py:30
  24.8 9.1 %collective-permute-start.12 = (f32[2,128,128]{2,1,0:T(8,128)S(1)}, f32[2,128,128]{2,1,0:T(8,128)S(1)}, u32[]{:S(2)}, u32[]{:S(2)}) collective-permute-start(f32[2,128,128]{2,1,0:T(8,128)S(1)} %get-tuple-element.49), channel_id=1, source_target_pairs={{0,28},{4,0},{8,4},{12,8},{16,12},{20,16},{24,20},{28,24},{1,29},{... | collective-permute-start | bytes 393224 | tf_op jit(solution)/shard_map/ppermute | solution.py:30
  29.6 1.3 %collective-permute-start.8 = (bf16[272,128]{1,0:T(8,128)(2,1)S(1)}, bf16[272,128]{1,0:T(8,128)(2,1)S(1)}, u32[]{:S(2)}, u32[]{:S(2)}) collective-permute-start(bf16[272,128]{1,0:T(8,128)(2,1)S(1)} %collective-permute-done.5.refs_0_.refs_3_.refs_1_), channel_id=1, source_target_pairs={{0,1},{1,0},{2,3},{3,2},{4,5},{5,4},{6,7},{7,6},{8,9},{9,8},{10,11... | collective-permute-start | bytes 208904 | tf_op jit(solution)/shard_map/ppermute | solution.py:35
  29.6 4.4 %collective-permute-start.9 = (bf16[256,128]{1,0:T(8,128)(2,1)S(1)}, bf16[256,128]{1,0:T(8,128)(2,1)S(1)}, u32[]{:S(2)}, u32[]{:S(2)}) collective-permute-start(bf16[256,128]{1,0:T(8,128)(2,1)S(1)} %get-tuple-element.46.refs_3_), channel_id=1, source_target_pairs={{0,1},{1,0},{2,3},{3,2},{4,5},{5,4},{6,7},{7,6},{8,9},{9,8},{10,11... | collective-permute-start | bytes 196616 | tf_op jit(solution)/shard_map/ppermute | solution.py:35
  30.1 3.9 %collective-permute-start.10 = (bf16[256,128]{1,0:T(8,128)(2,1)S(1)}, bf16[256,128]{1,0:T(8,128)(2,1)S(1)}, u32[]{:S(2)}, u32[]{:S(2)}) collective-permute-start(bf16[256,128]{1,0:T(8,128)(2,1)S(1)} %collective-permute-done.6.refs_1_.refs_3_), channel_id=1, source_target_pairs={{0,1},{1,0},{2,3},{3,2},{4,5},{5,4},{6,7},{7,6},{8,9},{9,8},{10,11... | collective-permute-start | bytes 196616 | tf_op jit(solution)/shard_map/ppermute | solution.py:35
  30.8 2.1 %copy-start.5 = (s32[1,256]{1,0:T(1,128)S(1)}, s32[1,256]{1,0:T(1,128)}, u32[]{:S(2)}) copy-start(s32[1,256]{1,0:T(1,128)} %refs_5_.1) | copy-start | bytes 3076
  30.8 4.3 %collective-permute-start.4 = (bf16[256,128]{1,0:T(8,128)(2,1)S(1)}, bf16[256,128]{1,0:T(8,128)(2,1)S(1)}, u32[]{:S(2)}, u32[]{:S(2)}) collective-permute-start(bf16[256,128]{1,0:T(8,128)(2,1)S(1)} %get-tuple-element.44.refs_5_), channel_id=1, source_target_pairs={{0,2},{1,3},{2,0},{3,1},{4,6},{5,7},{6,4},{7,5},{8,10},{9,11},{10,... | collective-permute-start | bytes 196616 | tf_op jit(solution)/shard_map/ppermute | solution.py:35
  36.0 6.6 %collective-permute-start.13 = (bf16[192,256]{1,0:T(8,128)(2,1)S(1)}, bf16[192,256]{1,0:T(8,128)(2,1)S(1)}, u32[]{:S(2)}, u32[]{:S(2)}) collective-permute-start(bf16[192,256]{1,0:T(8,128)(2,1)S(1)} %shard_map.148.refs_9_.refs_0_), channel_id=1, source_target_pairs={{0,1},{1,0},{2,3},{3,2},{4,5},{5,4},{6,7},{7,6},{8,9},{9,8},{10,11... | collective-permute-start | bytes 294920 | tf_op jit(solution)/shard_map/ppermute | solution.py:35
  36.0 8.4 %collective-permute-start.14 = (bf16[192,256]{1,0:T(8,128)(2,1)S(1)}, bf16[192,256]{1,0:T(8,128)(2,1)S(1)}, u32[]{:S(2)}, u32[]{:S(2)}) collective-permute-start(bf16[192,256]{1,0:T(8,128)(2,1)S(1)} %shard_map.148.refs_9_.refs_0_), channel_id=1, source_target_pairs={{0,2},{1,3},{2,0},{3,1},{4,6},{5,7},{6,4},{7,5},{8,10},{9,11},{10,... | collective-permute-start | bytes 294920 | tf_op jit(solution)/shard_map/ppermute | solution.py:35
  37.5 1.3 %collective-permute-start.16 = (bf16[256,128]{1,0:T(8,128)(2,1)S(1)}, bf16[256,128]{1,0:T(8,128)(2,1)S(1)}, u32[]{:S(2)}, u32[]{:S(2)}) collective-permute-start(bf16[256,128]{1,0:T(8,128)(2,1)S(1)} %get-tuple-element.44.refs_5_), channel_id=1, source_target_pairs={{0,1},{1,0},{2,3},{3,2},{4,5},{5,4},{6,7},{7,6},{8,9},{9,8},{10,11... | collective-permute-start | bytes 196616 | tf_op jit(solution)/shard_map/ppermute | solution.py:35
  37.7 4.9 %collective-permute-start.15 = (bf16[128,256]{1,0:T(8,128)(2,1)S(1)}, bf16[128,256]{1,0:T(8,128)(2,1)S(1)}, u32[]{:S(2)}, u32[]{:S(2)}) collective-permute-start(bf16[128,256]{1,0:T(8,128)(2,1)S(1)} %shard_map.147.refs_1_.refs_7_), channel_id=1, source_target_pairs={{0,2},{1,3},{2,0},{3,1},{4,6},{5,7},{6,4},{7,5},{8,10},{9,11},{10,... | collective-permute-start | bytes 196616 | tf_op jit(solution)/shard_map/ppermute | solution.py:35
  38.3 4.4 %collective-permute-start.17 = (bf16[128,256]{1,0:T(8,128)(2,1)S(1)}, bf16[128,256]{1,0:T(8,128)(2,1)S(1)}, u32[]{:S(2)}, u32[]{:S(2)}) collective-permute-start(bf16[128,256]{1,0:T(8,128)(2,1)S(1)} %shard_map.147.refs_1_.refs_7_), channel_id=1, source_target_pairs={{0,1},{1,0},{2,3},{3,2},{4,5},{5,4},{6,7},{7,6},{8,9},{9,8},{10,11... | collective-permute-start | bytes 196616 | tf_op jit(solution)/shard_map/ppermute | solution.py:35
  44.4 1.8 %collective-permute-start.18 = (bf16[192,256]{1,0:T(8,128)(2,1)S(1)}, bf16[192,256]{1,0:T(8,128)(2,1)S(1)}, u32[]{:S(2)}, u32[]{:S(2)}) collective-permute-start(bf16[192,256]{1,0:T(8,128)(2,1)S(1)} %collective-permute-done.14.refs_2_.refs_9_), channel_id=1, source_target_pairs={{0,1},{1,0},{2,3},{3,2},{4,5},{5,4},{6,7},{7,6},{8,9},{9,8},{10,11... | collective-permute-start | bytes 294920 | tf_op jit(solution)/shard_map/ppermute | solution.py:35
  44.5 1.4 %collective-permute-start.19 = (bf16[256,128]{1,0:T(8,128)(2,1)S(1)}, bf16[256,128]{1,0:T(8,128)(2,1)S(1)}, u32[]{:S(2)}, u32[]{:S(2)}) collective-permute-start(bf16[256,128]{1,0:T(8,128)(2,1)S(1)} %collective-permute-done.4.refs_0_.refs_5_), channel_id=1, source_target_pairs={{0,1},{1,0},{2,3},{3,2},{4,5},{5,4},{6,7},{7,6},{8,9},{9,8},{10,11... | collective-permute-start | bytes 196616 | tf_op jit(solution)/shard_map/ppermute | solution.py:35
  45.0 1.3 %collective-permute-start.20 = (bf16[128,256]{1,0:T(8,128)(2,1)S(1)}, bf16[128,256]{1,0:T(8,128)(2,1)S(1)}, u32[]{:S(2)}, u32[]{:S(2)}) collective-permute-start(bf16[128,256]{1,0:T(8,128)(2,1)S(1)} %collective-permute-done.15.refs_0_.refs_7_), channel_id=1, source_target_pairs={{0,1},{1,0},{2,3},{3,2},{4,5},{5,4},{6,7},{7,6},{8,9},{9,8},{10,11... | collective-permute-start | bytes 196616 | tf_op jit(solution)/shard_map/ppermute | solution.py:35
  48.1 5.3 %collective-permute-start.25 = (bf16[304,128]{1,0:T(8,128)(2,1)S(1)}, bf16[304,128]{1,0:T(8,128)(2,1)S(1)}, u32[]{:S(2)}, u32[]{:S(2)}) collective-permute-start(bf16[304,128]{1,0:T(8,128)(2,1)S(1)} %get-tuple-element.62), channel_id=1, source_target_pairs={{0,4},{4,0},{8,12},{12,8},{16,20},{20,16},{24,28},{28,24},{1,5},{5... | collective-permute-start | bytes 233480 | tf_op jit(solution)/shard_map/ppermute | solution.py:35
  48.2 6.9 %collective-permute-start.22 = (bf16[304,128]{1,0:T(8,128)(2,1)S(1)}, bf16[304,128]{1,0:T(8,128)(2,1)S(1)}, u32[]{:S(2)}, u32[]{:S(2)}) collective-permute-start(bf16[304,128]{1,0:T(8,128)(2,1)S(1)} %get-tuple-element.58), channel_id=1, source_target_pairs={{0,4},{4,0},{8,12},{12,8},{16,20},{20,16},{24,28},{28,24},{1,5},{5... | collective-permute-start | bytes 233480 | tf_op jit(solution)/shard_map/ppermute | solution.py:35
  50.2 9.5 %collective-permute-start.21 = (bf16[304,128]{1,0:T(8,128)(2,1)S(1)}, bf16[304,128]{1,0:T(8,128)(2,1)S(1)}, u32[]{:S(2)}, u32[]{:S(2)}) collective-permute-start(bf16[304,128]{1,0:T(8,128)(2,1)S(1)} %get-tuple-element.56), channel_id=1, source_target_pairs={{0,4},{4,0},{8,12},{12,8},{16,20},{20,16},{24,28},{28,24},{1,5},{5... | collective-permute-start | bytes 233480 | tf_op jit(solution)/shard_map/ppermute | solution.py:35
  50.3 7.3 %collective-permute-start.24 = (bf16[304,128]{1,0:T(8,128)(2,1)S(1)}, bf16[304,128]{1,0:T(8,128)(2,1)S(1)}, u32[]{:S(2)}, u32[]{:S(2)}) collective-permute-start(bf16[304,128]{1,0:T(8,128)(2,1)S(1)} %get-tuple-element.60), channel_id=1, source_target_pairs={{0,4},{4,0},{8,12},{12,8},{16,20},{20,16},{24,28},{28,24},{1,5},{5... | collective-permute-start | bytes 233480 | tf_op jit(solution)/shard_map/ppermute | solution.py:35
  53.4 4.5 %collective-permute-start.26 = (bf16[304,128]{1,0:T(8,128)(2,1)S(1)}, bf16[304,128]{1,0:T(8,128)(2,1)S(1)}, u32[]{:S(2)}, u32[]{:S(2)}) collective-permute-start(bf16[304,128]{1,0:T(8,128)(2,1)S(1)} %add_convert_fusion), channel_id=1, source_target_pairs={{0,8},{4,12},{8,0},{12,4},{16,24},{20,28},{24,16},{28,20},{1,9},{5... | collective-permute-start | bytes 233480 | tf_op jit(solution)/shard_map/ppermute | solution.py:35
  55.1 4.6 %collective-permute-start.23 = (bf16[304,128]{1,0:T(8,128)(2,1)S(1)}, bf16[304,128]{1,0:T(8,128)(2,1)S(1)}, u32[]{:S(2)}, u32[]{:S(2)}) collective-permute-start(bf16[304,128]{1,0:T(8,128)(2,1)S(1)} %add_convert_fusion.1), channel_id=1, source_target_pairs={{0,8},{4,12},{8,0},{12,4},{16,24},{20,28},{24,16},{28,20},{1,9},{5... | collective-permute-start | bytes 233480 | tf_op jit(solution)/shard_map/ppermute | solution.py:35
  58.0 5.4 %collective-permute-start.27 = (bf16[304,128]{1,0:T(8,128)(2,1)S(1)}, bf16[304,128]{1,0:T(8,128)(2,1)S(1)}, u32[]{:S(2)}, u32[]{:S(2)}) collective-permute-start(bf16[304,128]{1,0:T(8,128)(2,1)S(1)} %convert_add_fusion.1), channel_id=1, source_target_pairs={{0,16},{4,20},{8,24},{12,28},{16,0},{20,4},{24,8},{28,12},{1,17},{... | collective-permute-start | bytes 233480 | tf_op jit(solution)/shard_map/ppermute | solution.py:35
  63.4 5.6 %collective-permute-start.28 = (bf16[304,128]{1,0:T(8,128)(2,1)S(1)}, bf16[304,128]{1,0:T(8,128)(2,1)S(1)}, u32[]{:S(2)}, u32[]{:S(2)}) collective-permute-start(bf16[304,128]{1,0:T(8,128)(2,1)S(1)} %convert_add_fusion.refs_0_), channel_id=1, source_target_pairs={{0,8},{4,12},{8,0},{12,4},{16,24},{20,28},{24,16},{28,20},{1,9},{5... | collective-permute-start | bytes 233480 | tf_op jit(solution)/shard_map/ppermute | solution.py:35
  64.9 7.3 %collective-permute-start.29 = (bf16[304,128]{1,0:T(8,128)(2,1)S(1)}, bf16[304,128]{1,0:T(8,128)(2,1)S(1)}, u32[]{:S(2)}, u32[]{:S(2)}) collective-permute-start(bf16[304,128]{1,0:T(8,128)(2,1)S(1)} %convert_add_fusion.refs_0_), channel_id=1, source_target_pairs={{0,16},{4,20},{8,24},{12,28},{16,0},{20,4},{24,8},{28,12},{1,17},{... | collective-permute-start | bytes 233480 | tf_op jit(solution)/shard_map/ppermute | solution.py:35
  65.7 6.5 %collective-permute-start.30 = (bf16[304,128]{1,0:T(8,128)(2,1)S(1)}, bf16[304,128]{1,0:T(8,128)(2,1)S(1)}, u32[]{:S(2)}, u32[]{:S(2)}) collective-permute-start(bf16[304,128]{1,0:T(8,128)(2,1)S(1)} %convert_add_fusion.refs_0_), channel_id=1, source_target_pairs={{0,24},{4,28},{8,16},{12,20},{16,8},{20,12},{24,0},{28,4},{1,25},{... | collective-permute-start | bytes 233480 | tf_op jit(solution)/shard_map/ppermute | solution.py:35
  67.8 7.5 %collective-permute-start.31 = (bf16[304,128]{1,0:T(8,128)(2,1)S(1)}, bf16[304,128]{1,0:T(8,128)(2,1)S(1)}, u32[]{:S(2)}, u32[]{:S(2)}) collective-permute-start(bf16[304,128]{1,0:T(8,128)(2,1)S(1)} %convert_add_fusion.refs_0_), channel_id=1, source_target_pairs={{0,4},{4,0},{8,12},{12,8},{16,20},{20,16},{24,28},{28,24},{1,5},{5... | collective-permute-start | bytes 233480 | tf_op jit(solution)/shard_map/ppermute | solution.py:35
  69.0 6.4 %collective-permute-start.32 = (bf16[304,128]{1,0:T(8,128)(2,1)S(1)}, bf16[304,128]{1,0:T(8,128)(2,1)S(1)}, u32[]{:S(2)}, u32[]{:S(2)}) collective-permute-start(bf16[304,128]{1,0:T(8,128)(2,1)S(1)} %collective-permute-done.28.refs_1_), channel_id=1, source_target_pairs={{0,4},{4,0},{8,12},{12,8},{16,20},{20,16},{24,28},{28,24},{1,5},{5... | collective-permute-start | bytes 233480 | tf_op jit(solution)/shard_map/ppermute | solution.py:35
  72.2 4.4 %collective-permute-start.33 = (bf16[304,128]{1,0:T(8,128)(2,1)S(1)}, bf16[304,128]{1,0:T(8,128)(2,1)S(1)}, u32[]{:S(2)}, u32[]{:S(2)}) collective-permute-start(bf16[304,128]{1,0:T(8,128)(2,1)S(1)} %collective-permute-done.29.refs_2_), channel_id=1, source_target_pairs={{0,4},{4,0},{8,12},{12,8},{16,20},{20,16},{24,28},{28,24},{1,5},{5... | collective-permute-start | bytes 233480 | tf_op jit(solution)/shard_map/ppermute | solution.py:35
  72.2 5.2 %collective-permute-start.34 = (bf16[304,128]{1,0:T(8,128)(2,1)S(1)}, bf16[304,128]{1,0:T(8,128)(2,1)S(1)}, u32[]{:S(2)}, u32[]{:S(2)}) collective-permute-start(bf16[304,128]{1,0:T(8,128)(2,1)S(1)} %collective-permute-done.30.refs_3_), channel_id=1, source_target_pairs={{0,4},{4,0},{8,12},{12,8},{16,20},{20,16},{24,28},{28,24},{1,5},{5... | collective-permute-start | bytes 233480 | tf_op jit(solution)/shard_map/ppermute | solution.py:35

commit v11 on v10

--- a/solution.py
+++ b/solution.py
@@ -584,7 +584,6 @@
         chunks_f32,
         [IN_VMEM] * (5 * ahead + 3),
         1000,
-        after=[across_rows],
     )(
         *[member for members in gathered for member in members[:ahead]],
         *close_rows, *close, *weights,
@@ -615,20 +614,13 @@
             grad_flops,
             [pltpu.VMEM(chunks_f32.shape, F32)],
         )(*late_ins)
-        order = sorted(range(half), key=lambda step: (step % 2 == 0, -step))
+        order = list(range(half - 1, -1, -1))
         arrived = {step: swapped(made[half + step], 1) for step in order}
         total = {step: made[step] + arrived[step].astype(F32) for step in order}
-        distance = 1
-        while distance < half:
-            far = [step for step in total if step & distance]
-            for step in far:
-                came = swapped(total.pop(step).astype(BF16), 2 * distance)
-                kept_step = step ^ distance
-                total[kept_step] = lax.optimization_barrier(
-                    total[kept_step] + came.astype(F32)
-                )
-            distance *= 2
+        far = {step: swapped(total[step].astype(BF16), 2 * step) for step in order[:-1]}
         summed = total[0]
+        for step in order[:-1]:
+            summed = lax.optimization_barrier(summed + far[step].astype(F32))
         near = [summed.astype(BF16)]
         near += [swapped(near[0], 2 * step) for step in range(1, half)]
         other = [swapped(value, 1) for value in near]

time: 78.5 us -> 75.9 us (0.967)
  waiting for transfers between devices: 17.5 us -> 14.2 us
    ppermute x29, waiting for transfers between devices: 15.4 us -> 12.2 us  [swapped(): return lax.ppermute(value, axis, pairs)]
where the time goes in v11:
time: 75.9 us; the launch traced here: 75.6 us
  starting transfers between devices  41.1 us (54%)
  Pallas kernels  15.1 us (20%)
  waiting for transfers between devices  14.2 us (19%)
  local copies, waits for them, and re-layouts  3.42 us (5%)
  between operations  1.67 us (2%)
    ppermute x29, starting transfers between devices, swapped(): return lax.ppermute(value, axis, pairs)  25.5 us
    ppermute x6, starting transfers between devices, passed_along(): return lax.ppermute(value, axis, pairs)  15.7 us
    ppermute x29, waiting for transfers between devices, swapped(): return lax.ppermute(value, axis, pairs)  12.2 us
    unnamed x22, local copies, waits for them, and re-layouts  3.34 us
    pallas_call x2, Pallas kernels, body(): call(functools.partial(hop_kernel, plan), [blocks_f32, slots_f32, slots_f...  2.38 us
    ppermute x6, waiting for transfers between devices, passed_along(): return lax.ppermute(value, axis, pairs)  2.04 us
    pallas_call x2, Pallas kernels, write_out(): pl.pallas_call(functools.partial(out_kernel, kept, distances), out_shape=...  1.93 us
    pallas_call x1, Pallas kernels, body(): call(functools.partial(late_kernel, kept, ahead, half), [one_f32] * half...  1.85 us
  transfers between devices with their start and end apart: 35, of which 16 were waited for; matrix products, arithmetic and copies ran while one was open for 0% of the time, Pallas kernels for 11%

profile of v11, /device:TPU:0, one launch (start us, length us, event | category | flops | bytes accessed | tf_op | source)
XLA Modules:
  0.0 75.6 jit_solution(11595302527855533267)
XLA Ops:
  0.7 1.7 %shard_map.139 = (f32[2,128,128]{2,1,0:T(8,128)}, f32[2,128,128]{2,1,0:T(8,128)}, f32[2,128,128]{2,1,0:T(8,128)}, bf16[272,128]{1,0:T(8,128)(2,1)}) custom-call(s32[2]{0:T(128)} %refs_0_.3, s32[2]{0:T(128)} %refs_1_.4, s32[1,2]{1,0:T(1,128)} %refs_2_.1, f32[2,128,128]{2,1,0:T(8,128)} %bitcast.8, s32[1,256]{1,0:T(1,128)} %bitcast.10), custom_call_target="tpu_custom_call" | custom-call | flops 1000 | bytes 1000 | tf_op jit(solution)/shard_map/pallas_call | solution.py:487
  2.4 3.0 %collective-permute-start = (f32[2,128,128]{2,1,0:T(8,128)}, f32[2,128,128]{2,1,0:T(8,128)S(1)}, u32[]{:S(2)}, u32[]{:S(2)}) collective-permute-start(f32[2,128,128]{2,1,0:T(8,128)} %get-tuple-element.38), channel_id=1, source_target_pairs={{0,4},{4,8},{8,12},{12,16},{16,20},{20,24},{24,28},{28,0},{1,5},{5... | collective-permute-start | bytes 393224 | tf_op jit(solution)/shard_map/ppermute | solution.py:30
  5.5 3.1 %collective-permute-start.1 = (f32[2,128,128]{2,1,0:T(8,128)}, f32[2,128,128]{2,1,0:T(8,128)S(1)}, u32[]{:S(2)}, u32[]{:S(2)}) collective-permute-start(f32[2,128,128]{2,1,0:T(8,128)} %get-tuple-element.39), channel_id=1, source_target_pairs={{0,28},{4,0},{8,4},{12,8},{16,12},{20,16},{24,20},{28,24},{1,29},{... | collective-permute-start | bytes 393224 | tf_op jit(solution)/shard_map/ppermute | solution.py:30
  8.6 1.4 %copy-done.1 = bf16[4096,172]{0,1:T(8,128)(2,1)S(1)} copy-done((bf16[4096,172]{0,1:T(8,128)(2,1)S(1)}, bf16[4096,172]{0,1:T(8,128)(2,1)}, u32[]{:S(2)}) %copy-start.1) | copy-done | bytes 1409048
  9.9 1.0 %copy-done.2 = f32[8,128,128]{2,1,0:T(8,128)S(1)} copy-done((f32[8,128,128]{2,1,0:T(8,128)S(1)}, f32[8,128,128]{2,1,0:T(8,128)}, u32[]{:S(2)}) %copy-start.2) | copy-done | bytes 524312
  11.0 0.9 %copy-done.4 = f32[2,128,128]{2,1,0:T(8,128)S(1)} copy-done((f32[2,128,128]{2,1,0:T(8,128)S(1)}, f32[2,128,128]{2,1,0:T(8,128)}, u32[]{:S(2)}) %copy-start.4) | copy-done | bytes 131096
  11.9 0.1 shard_map.140
  12.8 0.1 concatenate.3.refs_0_.refs_1_.refs_5_
  12.9 0.6 collective-permute-done.1.refs_3_
  13.4 1.2 %shard_map.142 = (f32[2,128,128]{2,1,0:T(8,128)S(1)}, f32[2,128,128]{2,1,0:T(8,128)S(1)}, f32[2,128,128]{2,1,0:T(8,128)S(1)}, bf16[256,128]{1,0:T(8,128)(2,1)S(1)}) custom-call(s32[23]{0:T(128)S(1)} %concatenate.3.refs_0_.refs_1_.refs_5_, f32[2,128,128]{2,1,0:T(8,128)S(1)} %get-tuple-element.36.refs_0_.refs_1_, ...), custom_call_target="tpu_custom_call" | custom-call | flops 201326592 | bytes 1376256 | tf_op jit(solution)/shard_map/pallas_call | solution.py:530
  14.6 0.3 collective-permute-start.2
  15.0 4.4 %collective-permute-start.3 = (f32[2,128,128]{2,1,0:T(8,128)S(1)}, f32[2,128,128]{2,1,0:T(8,128)S(1)}, u32[]{:S(2)}, u32[]{:S(2)}) collective-permute-start(f32[2,128,128]{2,1,0:T(8,128)S(1)} %get-tuple-element.43), channel_id=1, source_target_pairs={{0,28},{4,0},{8,4},{12,8},{16,12},{20,16},{24,20},{28,24},{1,29},{... | collective-permute-start | bytes 393224 | tf_op jit(solution)/shard_map/ppermute | solution.py:30
  19.4 1.5 %collective-permute-start.5 = (bf16[272,128]{1,0:T(8,128)(2,1)S(1)}, bf16[272,128]{1,0:T(8,128)(2,1)S(1)}, u32[]{:S(2)}, u32[]{:S(2)}) collective-permute-start(bf16[272,128]{1,0:T(8,128)(2,1)S(1)} %copy-done.3), channel_id=1, source_target_pairs={{0,2},{1,3},{2,0},{3,1},{4,6},{5,7},{6,4},{7,5},{8,10},{9,11},{10,... | collective-permute-start | bytes 208904 | tf_op jit(solution)/shard_map/ppermute | solution.py:35
  20.9 0.6 shard_map.141.refs_0_.refs_3_
  21.5 0.6 collective-permute-start.6
  22.1 0.3 collective-permute-done.2.refs_3_
  22.5 1.1 %collective-permute-done.3.refs_4_ = f32[2,128,128]{2,1,0:T(8,128)S(1)} collective-permute-done((f32[2,128,128]{2,1,0:T(8,128)S(1)}, f32[2,128,128]{2,1,0:T(8,128)S(1)}, u32[]{:S(2)}, u32[]{:S(2)}) %collective-permute-start.3) | collective-permute-done | bytes 131104 | tf_op jit(solution)/shard_map/ppermute | solution.py:30
  23.6 1.2 %shard_map.143 = (f32[2,128,128]{2,1,0:T(8,128)S(1)}, f32[2,128,128]{2,1,0:T(8,128)S(1)}, f32[2,128,128]{2,1,0:T(8,128)S(1)}, bf16[256,128]{1,0:T(8,128)(2,1)S(1)}) custom-call(f32[172,256]{1,0:T(8,128)S(1)} %shard_map.141.refs_0_.refs_3_, s32[23]{0:T(128)S(1)} %concatenate.3.refs_0_.refs_1_.refs_5_, f32[2,128,128]{2,1,0:T(8,128)S(1)} %get-tuple-element.41.refs_2_.refs_0_, ...), custom_call_target="tpu_custom_call" | custom-call | flops 201326592 | bytes 1376256 | tf_op jit(solution)/shard_map/pallas_call | solution.py:530
  24.8 4.7 %collective-permute-start.12 = (f32[2,128,128]{2,1,0:T(8,128)S(1)}, f32[2,128,128]{2,1,0:T(8,128)S(1)}, u32[]{:S(2)}, u32[]{:S(2)}) collective-permute-start(f32[2,128,128]{2,1,0:T(8,128)S(1)} %get-tuple-element.49), channel_id=1, source_target_pairs={{0,28},{4,0},{8,4},{12,8},{16,12},{20,16},{24,20},{28,24},{1,29},{... | collective-permute-start | bytes 393224 | tf_op jit(solution)/shard_map/ppermute | solution.py:30
  29.6 0.5 collective-permute-start.9
  30.1 0.1 collective-permute-start.10
  30.2 0.7 collective-permute-done.8.refs_4_.refs_2_
  30.8 1.5 %collective-permute-start.4 = (bf16[256,128]{1,0:T(8,128)(2,1)S(1)}, bf16[256,128]{1,0:T(8,128)(2,1)S(1)}, u32[]{:S(2)}, u32[]{:S(2)}) collective-permute-start(bf16[256,128]{1,0:T(8,128)(2,1)S(1)} %get-tuple-element.44.refs_4_), channel_id=1, source_target_pairs={{0,2},{1,3},{2,0},{3,1},{4,6},{5,7},{6,4},{7,5},{8,10},{9,11},{10,... | collective-permute-start | bytes 196616 | tf_op jit(solution)/shard_map/ppermute | solution.py:35
  32.3 0.6 shard_map.144.refs_5_
  32.9 0.4 shard_map.146.refs_1_.refs_6_
  33.3 0.6 shard_map.145.refs_0_.refs_2_
  34.0 1.2 %shard_map.147.refs_1_.refs_6_ = bf16[128,256]{1,0:T(8,128)(2,1)S(1)} custom-call(f32[172,256]{1,0:T(8,128)S(1)} %shard_map.145.refs_0_.refs_2_, s32[1,256]{1,0:T(1,128)S(1)} %shard_map.146.refs_1_.refs_6_, bf16[256,128]{1,0:T(8,128)(2,1)S(1)} %collective-permute-done.9.refs_2_.refs_3_, bf16[256,128]{1,0:T(8,128)(2,1)S(1)} %collective-permute-done.6.refs_1_.refs_3_, ...), custom_call_target="tpu_custom_call" | custom-call | flops 201326592 | bytes 196608 | tf_op jit(solution)/shard_map/pallas_call | solution.py:557
  35.2 0.8 %shard_map.148.refs_8_.refs_0_ = bf16[192,256]{1,0:T(8,128)(2,1)S(1)} custom-call(bf16[256,128]{1,0:T(8,128)(2,1)S(1)} %collective-permute-done.4.refs_0_.refs_5_, bf16[128,256]{1,0:T(8,128)(2,1)S(1)} %shard_map.147.refs_1_.refs_6_, f32[172,256]{1,0:T(8,128)S(1)} %shard_map.145.refs_0_.refs_2_, bf16[4,128,1024]{2,1,0:T(8,128)(2,1)S(1)} %copy-done, ...), custom_call_target="tpu_custom_call" | custom-call | flops 1000 | bytes 1000 | tf_op jit(solution)/shard_map/pallas_call | solution.py:565
  36.0 1.5 %collective-permute-start.14 = (bf16[192,256]{1,0:T(8,128)(2,1)S(1)}, bf16[192,256]{1,0:T(8,128)(2,1)S(1)}, u32[]{:S(2)}, u32[]{:S(2)}) collective-permute-start(bf16[192,256]{1,0:T(8,128)(2,1)S(1)} %shard_map.148.refs_8_.refs_0_), channel_id=1, source_target_pairs={{0,2},{1,3},{2,0},{3,1},{4,6},{5,7},{6,4},{7,5},{8,10},{9,11},{10,... | collective-permute-start | bytes 294920 | tf_op jit(solution)/shard_map/ppermute | solution.py:35
  37.5 0.2 collective-permute-start.16
  37.7 0.3 collective-permute-start.17
  38.0 0.5 collective-permute-start.15
  38.6 0.3 shard_map.149
  38.9 0.1 collective-permute-done.17.refs_7_
  39.0 1.8 %shard_map.150.refs_0_ = f32[8,304,128]{2,1,0:T(8,128)S(1)} custom-call(bf16[272,128]{1,0:T(8,128)(2,1)S(1)} %copy-done.3, bf16[272,128]{1,0:T(8,128)(2,1)S(1)} %collective-permute-done.7.refs_2_.refs_1_, bf16[256,128]{1,0:T(8,128)(2,1)S(1)} %get-tuple-element.46.refs_2_, bf16[256,128]{1,0:T(8,128)(2,1)S(1)} %collective-permute-done.9.refs_2_.refs_3_, ...), custom_call_target="tpu_custom_call" | custom-call | flops 1000 | bytes 1000 | tf_op jit(solution)/shard_map/pallas_call | solution.py:582
  40.8 1.9 %collective-permute-done.15.refs_7_ = bf16[128,256]{1,0:T(8,128)(2,1)S(1)} collective-permute-done((bf16[128,256]{1,0:T(8,128)(2,1)S(1)}, bf16[128,256]{1,0:T(8,128)(2,1)S(1)}, u32[]{:S(2)}, u32[]{:S(2)}) %collective-permute-start.15) | collective-permute-done | bytes 65568 | tf_op jit(solution)/shard_map/ppermute | solution.py:35
  42.6 0.5 collective-permute-start.19
  43.1 0.9 %collective-permute-done.19.refs_6_ = bf16[256,128]{1,0:T(8,128)(2,1)S(1)} collective-permute-done((bf16[256,128]{1,0:T(8,128)(2,1)S(1)}, bf16[256,128]{1,0:T(8,128)(2,1)S(1)}, u32[]{:S(2)}, u32[]{:S(2)}) %collective-permute-start.19) | collective-permute-done | bytes 65568 | tf_op jit(solution)/shard_map/ppermute | solution.py:35
  44.0 0.4 collective-permute-done.20.refs_8_
  44.4 1.9 %shard_map.152 = (f32[304,128]{1,0:T(8,128)S(1)}, f32[304,128]{1,0:T(8,128)S(1)}, f32[304,128]{1,0:T(8,128)S(1)}, f32[304,128]{1,0:T(8,128)S(1)}, bf16[304,128]{...) custom-call(f32[8,304,128]{2,1,0:T(8,128)S(1)} %shard_map.150.refs_0, ...), custom_call_target="tpu_custom_call" | custom-call | flops 771751936 | bytes 2801664 | tf_op jit(solution)/shard_map/pallas_call | solution.py:610
  46.2 0.1 collective-permute-start.22
  46.3 2.0 %collective-permute-start.21 = (bf16[304,128]{1,0:T(8,128)(2,1)S(1)}, bf16[304,128]{1,0:T(8,128)(2,1)S(1)}, u32[]{:S(2)}, u32[]{:S(2)}) collective-permute-start(bf16[304,128]{1,0:T(8,128)(2,1)S(1)} %get-tuple-element.56), channel_id=1, source_target_pairs={{0,4},{4,0},{8,12},{12,8},{16,20},{20,16},{24,28},{28,24},{1,5},{5... | collective-permute-start | bytes 233480 | tf_op jit(solution)/shard_map/ppermute | solution.py:35
  48.3 0.1 collective-permute-start.24
  48.4 1.9 %collective-permute-start.26 = (bf16[304,128]{1,0:T(8,128)(2,1)S(1)}, bf16[304,128]{1,0:T(8,128)(2,1)S(1)}, u32[]{:S(2)}, u32[]{:S(2)}) collective-permute-start(bf16[304,128]{1,0:T(8,128)(2,1)S(1)} %get-tuple-element.62), channel_id=1, source_target_pairs={{0,4},{4,0},{8,12},{12,8},{16,20},{20,16},{24,28},{28,24},{1,5},{5... | collective-permute-start | bytes 233480 | tf_op jit(solution)/shard_map/ppermute | solution.py:35
  50.4 1.1 %collective-permute-done.22 = bf16[304,128]{1,0:T(8,128)(2,1)S(1)} collective-permute-done((bf16[304,128]{1,0:T(8,128)(2,1)S(1)}, bf16[304,128]{1,0:T(8,128)(2,1)S(1)}, u32[]{:S(2)}, u32[]{:S(2)}) %collective-permute-start.22) | collective-permute-done | bytes 77856 | tf_op jit(solution)/shard_map/ppermute | solution.py:35
  51.5 1.6 %collective-permute-start.23 = (bf16[304,128]{1,0:T(8,128)(2,1)S(1)}, bf16[304,128]{1,0:T(8,128)(2,1)S(1)}, u32[]{:S(2)}, u32[]{:S(2)}) collective-permute-start(bf16[304,128]{1,0:T(8,128)(2,1)S(1)} %add_convert_fusion.2), channel_id=1, source_target_pairs={{0,24},{4,28},{8,16},{12,20},{16,8},{20,12},{24,0},{28,4},{1,25},{... | collective-permute-start | bytes 233480 | tf_op jit(solution)/shard_map/ppermute | solution.py:35
  53.1 1.7 %collective-permute-done.24 = bf16[304,128]{1,0:T(8,128)(2,1)S(1)} collective-permute-done((bf16[304,128]{1,0:T(8,128)(2,1)S(1)}, bf16[304,128]{1,0:T(8,128)(2,1)S(1)}, u32[]{:S(2)}, u32[]{:S(2)}) %collective-permute-start.24) | collective-permute-done | bytes 77856 | tf_op jit(solution)/shard_map/ppermute | solution.py:35
  54.9 1.7 %collective-permute-start.25 = (bf16[304,128]{1,0:T(8,128)(2,1)S(1)}, bf16[304,128]{1,0:T(8,128)(2,1)S(1)}, u32[]{:S(2)}, u32[]{:S(2)}) collective-permute-start(bf16[304,128]{1,0:T(8,128)(2,1)S(1)} %add_convert_fusion.1), channel_id=1, source_target_pairs={{0,16},{4,20},{8,24},{12,28},{16,0},{20,4},{24,8},{28,12},{1,17},{... | collective-permute-start | bytes 233480 | tf_op jit(solution)/shard_map/ppermute | solution.py:35
  56.6 1.1 %collective-permute-start.27 = (bf16[304,128]{1,0:T(8,128)(2,1)S(1)}, bf16[304,128]{1,0:T(8,128)(2,1)S(1)}, u32[]{:S(2)}, u32[]{:S(2)}) collective-permute-start(bf16[304,128]{1,0:T(8,128)(2,1)S(1)} %add_convert_fusion), channel_id=1, source_target_pairs={{0,8},{4,12},{8,0},{12,4},{16,24},{20,28},{24,16},{28,20},{1,9},{5... | collective-permute-start | bytes 233480 | tf_op jit(solution)/shard_map/ppermute | solution.py:35
  57.7 0.2 collective-permute-done.23
  57.9 2.4 %collective-permute-done.25 = bf16[304,128]{1,0:T(8,128)(2,1)S(1)} collective-permute-done((bf16[304,128]{1,0:T(8,128)(2,1)S(1)}, bf16[304,128]{1,0:T(8,128)(2,1)S(1)}, u32[]{:S(2)}, u32[]{:S(2)}) %collective-permute-start.25) | collective-permute-done | bytes 77856 | tf_op jit(solution)/shard_map/ppermute | solution.py:35
  60.3 0.8 %collective-permute-done.27 = bf16[304,128]{1,0:T(8,128)(2,1)S(1)} collective-permute-done((bf16[304,128]{1,0:T(8,128)(2,1)S(1)}, bf16[304,128]{1,0:T(8,128)(2,1)S(1)}, u32[]{:S(2)}, u32[]{:S(2)}) %collective-permute-start.27) | collective-permute-done | bytes 77856 | tf_op jit(solution)/shard_map/ppermute | solution.py:35
  61.2 1.1 %collective-permute-start.28 = (bf16[304,128]{1,0:T(8,128)(2,1)S(1)}, bf16[304,128]{1,0:T(8,128)(2,1)S(1)}, u32[]{:S(2)}, u32[]{:S(2)}) collective-permute-start(bf16[304,128]{1,0:T(8,128)(2,1)S(1)} %convert_add_fusion.refs_0_), channel_id=1, source_target_pairs={{0,8},{4,12},{8,0},{12,4},{16,24},{20,28},{24,16},{28,20},{1,9},{5... | collective-permute-start | bytes 233480 | tf_op jit(solution)/shard_map/ppermute | solution.py:35
  62.2 2.0 %collective-permute-start.29 = (bf16[304,128]{1,0:T(8,128)(2,1)S(1)}, bf16[304,128]{1,0:T(8,128)(2,1)S(1)}, u32[]{:S(2)}, u32[]{:S(2)}) collective-permute-start(bf16[304,128]{1,0:T(8,128)(2,1)S(1)} %convert_add_fusion.refs_0_), channel_id=1, source_target_pairs={{0,16},{4,20},{8,24},{12,28},{16,0},{20,4},{24,8},{28,12},{1,17},{... | collective-permute-start | bytes 233480 | tf_op jit(solution)/shard_map/ppermute | solution.py:35
  64.2 1.4 %collective-permute-start.30 = (bf16[304,128]{1,0:T(8,128)(2,1)S(1)}, bf16[304,128]{1,0:T(8,128)(2,1)S(1)}, u32[]{:S(2)}, u32[]{:S(2)}) collective-permute-start(bf16[304,128]{1,0:T(8,128)(2,1)S(1)} %convert_add_fusion.refs_0_), channel_id=1, source_target_pairs={{0,24},{4,28},{8,16},{12,20},{16,8},{20,12},{24,0},{28,4},{1,25},{... | collective-permute-start | bytes 233480 | tf_op jit(solution)/shard_map/ppermute | solution.py:35
  65.6 0.7 collective-permute-start.31
  66.3 1.3 %collective-permute-start.32 = (bf16[304,128]{1,0:T(8,128)(2,1)S(1)}, bf16[304,128]{1,0:T(8,128)(2,1)S(1)}, u32[]{:S(2)}, u32[]{:S(2)}) collective-permute-start(bf16[304,128]{1,0:T(8,128)(2,1)S(1)} %collective-permute-done.28.refs_1_), channel_id=1, source_target_pairs={{0,4},{4,0},{8,12},{12,8},{16,20},{20,16},{24,28},{28,24},{1,5},{5... | collective-permute-start | bytes 233480 | tf_op jit(solution)/shard_map/ppermute | solution.py:35
  67.6 1.0 %collective-permute-done.29.refs_2_ = bf16[304,128]{1,0:T(8,128)(2,1)S(1)} collective-permute-done((bf16[304,128]{1,0:T(8,128)(2,1)S(1)}, bf16[304,128]{1,0:T(8,128)(2,1)S(1)}, u32[]{:S(2)}, u32[]{:S(2)}) %collective-permute-start.29) | collective-permute-done | bytes 77856 | tf_op jit(solution)/shard_map/ppermute | solution.py:35
  68.6 1.7 %collective-permute-start.33 = (bf16[304,128]{1,0:T(8,128)(2,1)S(1)}, bf16[304,128]{1,0:T(8,128)(2,1)S(1)}, u32[]{:S(2)}, u32[]{:S(2)}) collective-permute-start(bf16[304,128]{1,0:T(8,128)(2,1)S(1)} %collective-permute-done.29.refs_2_), channel_id=1, source_target_pairs={{0,4},{4,0},{8,12},{12,8},{16,20},{20,16},{24,28},{28,24},{1,5},{5... | collective-permute-start | bytes 233480 | tf_op jit(solution)/shard_map/ppermute | solution.py:35
  70.4 1.5 %collective-permute-start.34 = (bf16[304,128]{1,0:T(8,128)(2,1)S(1)}, bf16[304,128]{1,0:T(8,128)(2,1)S(1)}, u32[]{:S(2)}, u32[]{:S(2)}) collective-permute-start(bf16[304,128]{1,0:T(8,128)(2,1)S(1)} %collective-permute-done.30.refs_3_), channel_id=1, source_target_pairs={{0,4},{4,0},{8,12},{12,8},{16,20},{20,16},{24,28},{28,24},{1,5},{5... | collective-permute-start | bytes 233480 | tf_op jit(solution)/shard_map/ppermute | solution.py:35
  71.9 0.8 %shard_map.151 = f32[1,256]{1,0:T(1,128)} custom-call(bf16[192,256]{1,0:T(8,128)(2,1)S(1)} %shard_map.148.refs_8_.refs_0_, bf16[192,256]{1,0:T(8,128)(2,1)S(1)} %collective-permute-done.13.refs_9_.refs_1_, bf16[192,256]{1,0:T(8,128)(2,1)S(1)} %collective-permute-done.14.refs_2_.refs_9_, bf16[192,256]{1,0:T(8,128)(2,1)S(1)} %collective-permute-done.18.refs_3_.refs_10_), custom_call_target="tpu_custom_call" | custom-call | flops 1000 | bytes 1000 | tf_op jit(solution)/shard_map/pallas_call | solution.py:599
  72.7 1.1 %shard_map.153 = (f32[4,128,256]{2,1,0:T(8,128)}, f32[172,1024]{1,0:T(8,128)}) custom-call(bf16[304,128]{1,0:T(8,128)(2,1)S(1)} %convert_add_fusion.refs_0_, bf16[304,128]{1,0:T(8,128)(2,1)S(1)} %collective-permute-done.28.refs_1_, bf16[304,128]{1,0:T(8,128)(2,1)S(1)} %collective-permute-done.29.refs_2_, ...), custom_call_target="tpu_custom_call" | custom-call | flops 1000 | bytes 1000 | tf_op jit(solution)/shard_map/pallas_call | solution.py:419
  73.9 1.0 %collective-permute-done.34.refs_3_ = bf16[304,128]{1,0:T(8,128)(2,1)S(1)} collective-permute-done((bf16[304,128]{1,0:T(8,128)(2,1)S(1)}, bf16[304,128]{1,0:T(8,128)(2,1)S(1)}, u32[]{:S(2)}, u32[]{:S(2)}) %collective-permute-start.34) | collective-permute-done | bytes 77856 | tf_op jit(solution)/shard_map/ppermute | solution.py:35
  74.8 0.8 %shard_map.154 = (f32[4,128,256]{2,1,0:T(8,128)}, f32[172,1024]{1,0:T(8,128)}) custom-call(f32[4,128,256]{2,1,0:T(8,128)} %get-tuple-element.63.refs_0_, f32[172,1024]{1,0:T(8,128)} %get-tuple-element.64.refs_1_, bf16[304,128]{1,0:T(8,128)(2,1)S(1)} %collective-permute-done.33.refs_2_, ...), custom_call_target="tpu_custom_call", output_to_operand_aliasing={{0}: (0, {}), {1}: (1, {})} | custom-call | flops 1000 | bytes 1000 | tf_op jit(solution)/shard_map/pallas_call | solution.py:419
  (51 shorter events, 0.4 us)
Async XLA Ops:
  0.6 12.1 %copy-start.6 = (s32[2]{0:T(128)S(1)}, s32[2]{0:T(128)}, u32[]{:S(2)}) copy-start(s32[2]{0:T(128)} %refs_0_.3) | copy-start | bytes 28
  0.6 12.1 %copy-start.7 = (s32[2]{0:T(128)S(1)}, s32[2]{0:T(128)}, u32[]{:S(2)}) copy-start(s32[2]{0:T(128)} %refs_1_.4) | copy-start | bytes 28
  0.7 12.1 %copy-start.8 = (s32[1,2]{1,0:T(1,128)S(1)}, s32[1,2]{1,0:T(1,128)}, u32[]{:S(2)}) copy-start(s32[1,2]{1,0:T(1,128)} %refs_2_.1) | copy-start | bytes 28
  0.7 12.1 %copy-start.9 = (s32[8]{0:T(128)S(1)}, s32[8]{0:T(128)}, u32[]{:S(2)}) copy-start(s32[8]{0:T(128)} %param.14) | copy-start | bytes 100
  0.7 12.1 %copy-start.10 = (s32[8]{0:T(128)S(1)}, s32[8]{0:T(128)}, u32[]{:S(2)}) copy-start(s32[8]{0:T(128)} %param.15) | copy-start | bytes 100
  2.4 10.4 %collective-permute-start = (f32[2,128,128]{2,1,0:T(8,128)}, f32[2,128,128]{2,1,0:T(8,128)S(1)}, u32[]{:S(2)}, u32[]{:S(2)}) collective-permute-start(f32[2,128,128]{2,1,0:T(8,128)} %get-tuple-element.38), channel_id=1, source_target_pairs={{0,4},{4,8},{8,12},{12,16},{16,20},{20,24},{24,28},{28,0},{1,5},{5... | collective-permute-start | bytes 393224 | tf_op jit(solution)/shard_map/ppermute | solution.py:30
  5.5 8.0 %collective-permute-start.1 = (f32[2,128,128]{2,1,0:T(8,128)}, f32[2,128,128]{2,1,0:T(8,128)S(1)}, u32[]{:S(2)}, u32[]{:S(2)}) collective-permute-start(f32[2,128,128]{2,1,0:T(8,128)} %get-tuple-element.39), channel_id=1, source_target_pairs={{0,28},{4,0},{8,4},{12,8},{16,12},{20,16},{24,20},{28,24},{1,29},{... | collective-permute-start | bytes 393224 | tf_op jit(solution)/shard_map/ppermute | solution.py:30
  8.6 1.4 %copy-start.1 = (bf16[4096,172]{0,1:T(8,128)(2,1)S(1)}, bf16[4096,172]{0,1:T(8,128)(2,1)}, u32[]{:S(2)}) copy-start(bf16[4096,172]{0,1:T(8,128)(2,1)} %param.23) | copy-start | bytes 4227076
  9.9 1.0 %copy-start.2 = (f32[8,128,128]{2,1,0:T(8,128)S(1)}, f32[8,128,128]{2,1,0:T(8,128)}, u32[]{:S(2)}) copy-start(f32[8,128,128]{2,1,0:T(8,128)} %refs_1_.5) | copy-start | bytes 1572868
  11.0 0.9 %copy-start.4 = (f32[2,128,128]{2,1,0:T(8,128)S(1)}, f32[2,128,128]{2,1,0:T(8,128)}, u32[]{:S(2)}) copy-start(f32[2,128,128]{2,1,0:T(8,128)} %get-tuple-element.35.refs_0_) | copy-start | bytes 393220
  11.9 7.5 %copy-start.3 = (bf16[272,128]{1,0:T(8,128)(2,1)S(1)}, bf16[272,128]{1,0:T(8,128)(2,1)}, u32[]{:S(2)}) copy-start(bf16[272,128]{1,0:T(8,128)(2,1)} %get-tuple-element.45.refs_1_.refs_0_) | copy-start | bytes 208900
  11.9 9.0 %copy-start = (bf16[4,128,1024]{2,1,0:T(8,128)(2,1)S(1)}, bf16[4,128,1024]{2,1,0:T(8,128)(2,1)}, u32[]{:S(2)}) copy-start(bf16[4,128,1024]{2,1,0:T(8,128)(2,1)} %refs_11_.1) | copy-start | bytes 3145732
  14.6 7.8 %collective-permute-start.2 = (f32[2,128,128]{2,1,0:T(8,128)S(1)}, f32[2,128,128]{2,1,0:T(8,128)S(1)}, u32[]{:S(2)}, u32[]{:S(2)}) collective-permute-start(f32[2,128,128]{2,1,0:T(8,128)S(1)} %get-tuple-element.42), channel_id=1, source_target_pairs={{0,4},{4,8},{8,12},{12,16},{16,20},{20,24},{24,28},{28,0},{1,5},{5... | collective-permute-start | bytes 393224 | tf_op jit(solution)/shard_map/ppermute | solution.py:30
  15.0 8.6 %collective-permute-start.3 = (f32[2,128,128]{2,1,0:T(8,128)S(1)}, f32[2,128,128]{2,1,0:T(8,128)S(1)}, u32[]{:S(2)}, u32[]{:S(2)}) collective-permute-start(f32[2,128,128]{2,1,0:T(8,128)S(1)} %get-tuple-element.43), channel_id=1, source_target_pairs={{0,28},{4,0},{8,4},{12,8},{16,12},{20,16},{24,20},{28,24},{1,29},{... | collective-permute-start | bytes 393224 | tf_op jit(solution)/shard_map/ppermute | solution.py:30
  19.4 10.1 %collective-permute-start.5 = (bf16[272,128]{1,0:T(8,128)(2,1)S(1)}, bf16[272,128]{1,0:T(8,128)(2,1)S(1)}, u32[]{:S(2)}, u32[]{:S(2)}) collective-permute-start(bf16[272,128]{1,0:T(8,128)(2,1)S(1)} %copy-done.3), channel_id=1, source_target_pairs={{0,2},{1,3},{2,0},{3,1},{4,6},{5,7},{6,4},{7,5},{8,10},{9,11},{10,... | collective-permute-start | bytes 208904 | tf_op jit(solution)/shard_map/ppermute | solution.py:35
  20.9 8.7 %collective-permute-start.7 = (bf16[272,128]{1,0:T(8,128)(2,1)S(1)}, bf16[272,128]{1,0:T(8,128)(2,1)S(1)}, u32[]{:S(2)}, u32[]{:S(2)}) collective-permute-start(bf16[272,128]{1,0:T(8,128)(2,1)S(1)} %copy-done.3), channel_id=1, source_target_pairs={{0,1},{1,0},{2,3},{3,2},{4,5},{5,4},{6,7},{7,6},{8,9},{9,8},{10,11... | collective-permute-start | bytes 208904 | tf_op jit(solution)/shard_map/ppermute | solution.py:35
  21.5 8.6 %collective-permute-start.6 = (bf16[256,128]{1,0:T(8,128)(2,1)S(1)}, bf16[256,128]{1,0:T(8,128)(2,1)S(1)}, u32[]{:S(2)}, u32[]{:S(2)}) collective-permute-start(bf16[256,128]{1,0:T(8,128)(2,1)S(1)} %get-tuple-element.46.refs_2_), channel_id=1, source_target_pairs={{0,2},{1,3},{2,0},{3,1},{4,6},{5,7},{6,4},{7,5},{8,10},{9,11},{10,... | collective-permute-start | bytes 196616 | tf_op jit(solution)/shard_map/ppermute | solution.py:35
  24.8 9.2 %collective-permute-start.11 = (f32[2,128,128]{2,1,0:T(8,128)S(1)}, f32[2,128,128]{2,1,0:T(8,128)S(1)}, u32[]{:S(2)}, u32[]{:S(2)}) collective-permute-start(f32[2,128,128]{2,1,0:T(8,128)S(1)} %get-tuple-element.48), channel_id=1, source_target_pairs={{0,4},{4,8},{8,12},{12,16},{16,20},{20,24},{24,28},{28,0},{1,5},{5... | collective-permute-start | bytes 393224 | tf_op jit(solution)/shard_map/ppermute | solution.py:30
  24.8 9.1 %collective-permute-start.12 = (f32[2,128,128]{2,1,0:T(8,128)S(1)}, f32[2,128,128]{2,1,0:T(8,128)S(1)}, u32[]{:S(2)}, u32[]{:S(2)}) collective-permute-start(f32[2,128,128]{2,1,0:T(8,128)S(1)} %get-tuple-element.49), channel_id=1, source_target_pairs={{0,28},{4,0},{8,4},{12,8},{16,12},{20,16},{24,20},{28,24},{1,29},{... | collective-permute-start | bytes 393224 | tf_op jit(solution)/shard_map/ppermute | solution.py:30
  29.6 1.3 %collective-permute-start.8 = (bf16[272,128]{1,0:T(8,128)(2,1)S(1)}, bf16[272,128]{1,0:T(8,128)(2,1)S(1)}, u32[]{:S(2)}, u32[]{:S(2)}) collective-permute-start(bf16[272,128]{1,0:T(8,128)(2,1)S(1)} %collective-permute-done.5.refs_0_.refs_3_.refs_1_), channel_id=1, source_target_pairs={{0,1},{1,0},{2,3},{3,2},{4,5},{5,4},{6,7},{7,6},{8,9},{9,8},{10,11... | collective-permute-start | bytes 208904 | tf_op jit(solution)/shard_map/ppermute | solution.py:35
  29.6 4.4 %collective-permute-start.9 = (bf16[256,128]{1,0:T(8,128)(2,1)S(1)}, bf16[256,128]{1,0:T(8,128)(2,1)S(1)}, u32[]{:S(2)}, u32[]{:S(2)}) collective-permute-start(bf16[256,128]{1,0:T(8,128)(2,1)S(1)} %get-tuple-element.46.refs_2_), channel_id=1, source_target_pairs={{0,1},{1,0},{2,3},{3,2},{4,5},{5,4},{6,7},{7,6},{8,9},{9,8},{10,11... | collective-permute-start | bytes 196616 | tf_op jit(solution)/shard_map/ppermute | solution.py:35
  30.1 3.9 %collective-permute-start.10 = (bf16[256,128]{1,0:T(8,128)(2,1)S(1)}, bf16[256,128]{1,0:T(8,128)(2,1)S(1)}, u32[]{:S(2)}, u32[]{:S(2)}) collective-permute-start(bf16[256,128]{1,0:T(8,128)(2,1)S(1)} %collective-permute-done.6.refs_1_.refs_3_), channel_id=1, source_target_pairs={{0,1},{1,0},{2,3},{3,2},{4,5},{5,4},{6,7},{7,6},{8,9},{9,8},{10,11... | collective-permute-start | bytes 196616 | tf_op jit(solution)/shard_map/ppermute | solution.py:35
  30.8 2.1 %copy-start.5 = (s32[1,256]{1,0:T(1,128)S(1)}, s32[1,256]{1,0:T(1,128)}, u32[]{:S(2)}) copy-start(s32[1,256]{1,0:T(1,128)} %refs_5_.1) | copy-start | bytes 3076
  30.8 4.3 %collective-permute-start.4 = (bf16[256,128]{1,0:T(8,128)(2,1)S(1)}, bf16[256,128]{1,0:T(8,128)(2,1)S(1)}, u32[]{:S(2)}, u32[]{:S(2)}) collective-permute-start(bf16[256,128]{1,0:T(8,128)(2,1)S(1)} %get-tuple-element.44.refs_4_), channel_id=1, source_target_pairs={{0,2},{1,3},{2,0},{3,1},{4,6},{5,7},{6,4},{7,5},{8,10},{9,11},{10,... | collective-permute-start | bytes 196616 | tf_op jit(solution)/shard_map/ppermute | solution.py:35
  36.0 3.0 %collective-permute-start.13 = (bf16[192,256]{1,0:T(8,128)(2,1)S(1)}, bf16[192,256]{1,0:T(8,128)(2,1)S(1)}, u32[]{:S(2)}, u32[]{:S(2)}) collective-permute-start(bf16[192,256]{1,0:T(8,128)(2,1)S(1)} %shard_map.148.refs_8_.refs_0_), channel_id=1, source_target_pairs={{0,1},{1,0},{2,3},{3,2},{4,5},{5,4},{6,7},{7,6},{8,9},{9,8},{10,11... | collective-permute-start | bytes 294920 | tf_op jit(solution)/shard_map/ppermute | solution.py:35
  36.0 6.6 %collective-permute-start.14 = (bf16[192,256]{1,0:T(8,128)(2,1)S(1)}, bf16[192,256]{1,0:T(8,128)(2,1)S(1)}, u32[]{:S(2)}, u32[]{:S(2)}) collective-permute-start(bf16[192,256]{1,0:T(8,128)(2,1)S(1)} %shard_map.148.refs_8_.refs_0_), channel_id=1, source_target_pairs={{0,2},{1,3},{2,0},{3,1},{4,6},{5,7},{6,4},{7,5},{8,10},{9,11},{10,... | collective-permute-start | bytes 294920 | tf_op jit(solution)/shard_map/ppermute | solution.py:35
  37.5 1.3 %collective-permute-start.16 = (bf16[256,128]{1,0:T(8,128)(2,1)S(1)}, bf16[256,128]{1,0:T(8,128)(2,1)S(1)}, u32[]{:S(2)}, u32[]{:S(2)}) collective-permute-start(bf16[256,128]{1,0:T(8,128)(2,1)S(1)} %get-tuple-element.44.refs_4_), channel_id=1, source_target_pairs={{0,1},{1,0},{2,3},{3,2},{4,5},{5,4},{6,7},{7,6},{8,9},{9,8},{10,11... | collective-permute-start | bytes 196616 | tf_op jit(solution)/shard_map/ppermute | solution.py:35
  37.7 1.3 %collective-permute-start.17 = (bf16[128,256]{1,0:T(8,128)(2,1)S(1)}, bf16[128,256]{1,0:T(8,128)(2,1)S(1)}, u32[]{:S(2)}, u32[]{:S(2)}) collective-permute-start(bf16[128,256]{1,0:T(8,128)(2,1)S(1)} %shard_map.147.refs_1_.refs_6_), channel_id=1, source_target_pairs={{0,1},{1,0},{2,3},{3,2},{4,5},{5,4},{6,7},{7,6},{8,9},{9,8},{10,11... | collective-permute-start | bytes 196616 | tf_op jit(solution)/shard_map/ppermute | solution.py:35
  38.0 4.6 %collective-permute-start.15 = (bf16[128,256]{1,0:T(8,128)(2,1)S(1)}, bf16[128,256]{1,0:T(8,128)(2,1)S(1)}, u32[]{:S(2)}, u32[]{:S(2)}) collective-permute-start(bf16[128,256]{1,0:T(8,128)(2,1)S(1)} %shard_map.147.refs_1_.refs_6_), channel_id=1, source_target_pairs={{0,2},{1,3},{2,0},{3,1},{4,6},{5,7},{6,4},{7,5},{8,10},{9,11},{10,... | collective-permute-start | bytes 196616 | tf_op jit(solution)/shard_map/ppermute | solution.py:35
  42.6 1.8 %collective-permute-start.18 = (bf16[192,256]{1,0:T(8,128)(2,1)S(1)}, bf16[192,256]{1,0:T(8,128)(2,1)S(1)}, u32[]{:S(2)}, u32[]{:S(2)}) collective-permute-start(bf16[192,256]{1,0:T(8,128)(2,1)S(1)} %collective-permute-done.14.refs_2_.refs_9_), channel_id=1, source_target_pairs={{0,1},{1,0},{2,3},{3,2},{4,5},{5,4},{6,7},{7,6},{8,9},{9,8},{10,11... | collective-permute-start | bytes 294920 | tf_op jit(solution)/shard_map/ppermute | solution.py:35
  42.6 1.4 %collective-permute-start.19 = (bf16[256,128]{1,0:T(8,128)(2,1)S(1)}, bf16[256,128]{1,0:T(8,128)(2,1)S(1)}, u32[]{:S(2)}, u32[]{:S(2)}) collective-permute-start(bf16[256,128]{1,0:T(8,128)(2,1)S(1)} %collective-permute-done.4.refs_0_.refs_5_), channel_id=1, source_target_pairs={{0,1},{1,0},{2,3},{3,2},{4,5},{5,4},{6,7},{7,6},{8,9},{9,8},{10,11... | collective-permute-start | bytes 196616 | tf_op jit(solution)/shard_map/ppermute | solution.py:35
  43.1 1.3 %collective-permute-start.20 = (bf16[128,256]{1,0:T(8,128)(2,1)S(1)}, bf16[128,256]{1,0:T(8,128)(2,1)S(1)}, u32[]{:S(2)}, u32[]{:S(2)}) collective-permute-start(bf16[128,256]{1,0:T(8,128)(2,1)S(1)} %collective-permute-done.15.refs_7_), channel_id=1, source_target_pairs={{0,1},{1,0},{2,3},{3,2},{4,5},{5,4},{6,7},{7,6},{8,9},{9,8},{10,11... | collective-permute-start | bytes 196616 | tf_op jit(solution)/shard_map/ppermute | solution.py:35
  46.2 5.3 %collective-permute-start.22 = (bf16[304,128]{1,0:T(8,128)(2,1)S(1)}, bf16[304,128]{1,0:T(8,128)(2,1)S(1)}, u32[]{:S(2)}, u32[]{:S(2)}) collective-permute-start(bf16[304,128]{1,0:T(8,128)(2,1)S(1)} %get-tuple-element.58), channel_id=1, source_target_pairs={{0,4},{4,0},{8,12},{12,8},{16,20},{20,16},{24,28},{28,24},{1,5},{5... | collective-permute-start | bytes 233480 | tf_op jit(solution)/shard_map/ppermute | solution.py:35
  46.3 11.4 %collective-permute-start.21 = (bf16[304,128]{1,0:T(8,128)(2,1)S(1)}, bf16[304,128]{1,0:T(8,128)(2,1)S(1)}, u32[]{:S(2)}, u32[]{:S(2)}) collective-permute-start(bf16[304,128]{1,0:T(8,128)(2,1)S(1)} %get-tuple-element.56), channel_id=1, source_target_pairs={{0,4},{4,0},{8,12},{12,8},{16,20},{20,16},{24,28},{28,24},{1,5},{5... | collective-permute-start | bytes 233480 | tf_op jit(solution)/shard_map/ppermute | solution.py:35
  48.3 6.5 %collective-permute-start.24 = (bf16[304,128]{1,0:T(8,128)(2,1)S(1)}, bf16[304,128]{1,0:T(8,128)(2,1)S(1)}, u32[]{:S(2)}, u32[]{:S(2)}) collective-permute-start(bf16[304,128]{1,0:T(8,128)(2,1)S(1)} %get-tuple-element.60), channel_id=1, source_target_pairs={{0,4},{4,0},{8,12},{12,8},{16,20},{20,16},{24,28},{28,24},{1,5},{5... | collective-permute-start | bytes 233480 | tf_op jit(solution)/shard_map/ppermute | solution.py:35
  48.4 8.2 %collective-permute-start.26 = (bf16[304,128]{1,0:T(8,128)(2,1)S(1)}, bf16[304,128]{1,0:T(8,128)(2,1)S(1)}, u32[]{:S(2)}, u32[]{:S(2)}) collective-permute-start(bf16[304,128]{1,0:T(8,128)(2,1)S(1)} %get-tuple-element.62), channel_id=1, source_target_pairs={{0,4},{4,0},{8,12},{12,8},{16,20},{20,16},{24,28},{28,24},{1,5},{5... | collective-permute-start | bytes 233480 | tf_op jit(solution)/shard_map/ppermute | solution.py:35
  51.5 6.4 %collective-permute-start.23 = (bf16[304,128]{1,0:T(8,128)(2,1)S(1)}, bf16[304,128]{1,0:T(8,128)(2,1)S(1)}, u32[]{:S(2)}, u32[]{:S(2)}) collective-permute-start(bf16[304,128]{1,0:T(8,128)(2,1)S(1)} %add_convert_fusion.2), channel_id=1, source_target_pairs={{0,24},{4,28},{8,16},{12,20},{16,8},{20,12},{24,0},{28,4},{1,25},{... | collective-permute-start | bytes 233480 | tf_op jit(solution)/shard_map/ppermute | solution.py:35
  54.9 5.4 %collective-permute-start.25 = (bf16[304,128]{1,0:T(8,128)(2,1)S(1)}, bf16[304,128]{1,0:T(8,128)(2,1)S(1)}, u32[]{:S(2)}, u32[]{:S(2)}) collective-permute-start(bf16[304,128]{1,0:T(8,128)(2,1)S(1)} %add_convert_fusion.1), channel_id=1, source_target_pairs={{0,16},{4,20},{8,24},{12,28},{16,0},{20,4},{24,8},{28,12},{1,17},{... | collective-permute-start | bytes 233480 | tf_op jit(solution)/shard_map/ppermute | solution.py:35
  56.6 4.5 %collective-permute-start.27 = (bf16[304,128]{1,0:T(8,128)(2,1)S(1)}, bf16[304,128]{1,0:T(8,128)(2,1)S(1)}, u32[]{:S(2)}, u32[]{:S(2)}) collective-permute-start(bf16[304,128]{1,0:T(8,128)(2,1)S(1)} %add_convert_fusion), channel_id=1, source_target_pairs={{0,8},{4,12},{8,0},{12,4},{16,24},{20,28},{24,16},{28,20},{1,9},{5... | collective-permute-start | bytes 233480 | tf_op jit(solution)/shard_map/ppermute | solution.py:35
  61.2 5.2 %collective-permute-start.28 = (bf16[304,128]{1,0:T(8,128)(2,1)S(1)}, bf16[304,128]{1,0:T(8,128)(2,1)S(1)}, u32[]{:S(2)}, u32[]{:S(2)}) collective-permute-start(bf16[304,128]{1,0:T(8,128)(2,1)S(1)} %convert_add_fusion.refs_0_), channel_id=1, source_target_pairs={{0,8},{4,12},{8,0},{12,4},{16,24},{20,28},{24,16},{28,20},{1,9},{5... | collective-permute-start | bytes 233480 | tf_op jit(solution)/shard_map/ppermute | solution.py:35
  62.2 6.4 %collective-permute-start.29 = (bf16[304,128]{1,0:T(8,128)(2,1)S(1)}, bf16[304,128]{1,0:T(8,128)(2,1)S(1)}, u32[]{:S(2)}, u32[]{:S(2)}) collective-permute-start(bf16[304,128]{1,0:T(8,128)(2,1)S(1)} %convert_add_fusion.refs_0_), channel_id=1, source_target_pairs={{0,16},{4,20},{8,24},{12,28},{16,0},{20,4},{24,8},{28,12},{1,17},{... | collective-permute-start | bytes 233480 | tf_op jit(solution)/shard_map/ppermute | solution.py:35
  64.2 6.2 %collective-permute-start.30 = (bf16[304,128]{1,0:T(8,128)(2,1)S(1)}, bf16[304,128]{1,0:T(8,128)(2,1)S(1)}, u32[]{:S(2)}, u32[]{:S(2)}) collective-permute-start(bf16[304,128]{1,0:T(8,128)(2,1)S(1)} %convert_add_fusion.refs_0_), channel_id=1, source_target_pairs={{0,24},{4,28},{8,16},{12,20},{16,8},{20,12},{24,0},{28,4},{1,25},{... | collective-permute-start | bytes 233480 | tf_op jit(solution)/shard_map/ppermute | solution.py:35
  65.6 7.1 %collective-permute-start.31 = (bf16[304,128]{1,0:T(8,128)(2,1)S(1)}, bf16[304,128]{1,0:T(8,128)(2,1)S(1)}, u32[]{:S(2)}, u32[]{:S(2)}) collective-permute-start(bf16[304,128]{1,0:T(8,128)(2,1)S(1)} %convert_add_fusion.refs_0_), channel_id=1, source_target_pairs={{0,4},{4,0},{8,12},{12,8},{16,20},{20,16},{24,28},{28,24},{1,5},{5... | collective-permute-start | bytes 233480 | tf_op jit(solution)/shard_map/ppermute | solution.py:35
  66.3 6.4 %collective-permute-start.32 = (bf16[304,128]{1,0:T(8,128)(2,1)S(1)}, bf16[304,128]{1,0:T(8,128)(2,1)S(1)}, u32[]{:S(2)}, u32[]{:S(2)}) collective-permute-start(bf16[304,128]{1,0:T(8,128)(2,1)S(1)} %collective-permute-done.28.refs_1_), channel_id=1, source_target_pairs={{0,4},{4,0},{8,12},{12,8},{16,20},{20,16},{24,28},{28,24},{1,5},{5... | collective-permute-start | bytes 233480 | tf_op jit(solution)/shard_map/ppermute | solution.py:35
  68.6 5.2 %collective-permute-start.33 = (bf16[304,128]{1,0:T(8,128)(2,1)S(1)}, bf16[304,128]{1,0:T(8,128)(2,1)S(1)}, u32[]{:S(2)}, u32[]{:S(2)}) collective-permute-start(bf16[304,128]{1,0:T(8,128)(2,1)S(1)} %collective-permute-done.29.refs_2_), channel_id=1, source_target_pairs={{0,4},{4,0},{8,12},{12,8},{16,20},{20,16},{24,28},{28,24},{1,5},{5... | collective-permute-start | bytes 233480 | tf_op jit(solution)/shard_map/ppermute | solution.py:35
  70.4 4.4 %collective-permute-start.34 = (bf16[304,128]{1,0:T(8,128)(2,1)S(1)}, bf16[304,128]{1,0:T(8,128)(2,1)S(1)}, u32[]{:S(2)}, u32[]{:S(2)}) collective-permute-start(bf16[304,128]{1,0:T(8,128)(2,1)S(1)} %collective-permute-done.30.refs_3_), channel_id=1, source_target_pairs={{0,4},{4,0},{8,12},{12,8},{16,20},{20,16},{24,28},{28,24},{1,5},{5... | collective-permute-start | bytes 233480 | tf_op jit(solution)/shard_map/ppermute | solution.py:35

commit v12 on v11

--- a/solution.py
+++ b/solution.py
@@ -357,7 +357,7 @@
 
 
 def late_kernel(kept, members, half, early_ref, *refs):
-    ins = len(refs) - 1 - 2 * half
+    ins = len(refs) - 2 * half
     outs = refs[ins:-1]
     chunks_ref = refs[-1]
     late_chunks(kept, members, early_ref, refs[:ins], chunks_ref)
@@ -365,7 +365,11 @@
     for step in range(half):
         stays = dom ^ (2 * step)
         outs[step][...] = chunks_ref[stays]
-        outs[half + step][...] = chunks_ref[stays ^ 1].astype(BF16)
+        going = chunks_ref[stays ^ 1].astype(BF16)
+        if step < 2:
+            outs[half][step] = going
+        else:
+            outs[half + step - 1][...] = going
 
 
 def plain_late_kernel(kept, members, early_ref, *refs):
@@ -381,16 +385,17 @@
     branch_ref[branch, :, pl.ds(start, LANES)] = value[kept:].T
 
 
-def out_kernel(kept, distances, *refs):
-    count = len(distances)
-    ins = refs[-5 - count : -5]
+def out_kernel(kept, distances, count, *refs):
+    values = []
+    for ref in refs[-5 - count : -5]:
+        values += [ref[...]] if len(ref.shape) == 2 else [ref[n] for n in range(ref.shape[0])]
     branch_ref, class_ref, branch_here, class_here, sems = refs[-5:]
     dom = lax.axis_index("dom")
     per_branch = branch_ref.shape[2] // LANES
     copies = []
     for number, distance in enumerate(distances):
         chunk = dom ^ distance
-        value = ins[number][...].astype(F32)
+        value = values[number].astype(F32)
         class_here[number] = value[: class_ref.shape[0]]
         start = pl.multiple_of(chunk * LANES, LANES)
         copies.append(
@@ -417,9 +422,9 @@
 def write_out(kept, distances, values, outs, before):
     count = len(distances)
     return pl.pallas_call(
-        functools.partial(out_kernel, kept, distances),
+        functools.partial(out_kernel, kept, distances, len(values)),
         out_shape=outs,
-        in_specs=[ANYWHERE] * len(before) + [IN_VMEM] * count,
+        in_specs=[ANYWHERE] * len(before) + [IN_VMEM] * len(values),
         out_specs=[pl.BlockSpec(memory_space=pltpu.HBM)] * 2,
         scratch_shapes=[
             pltpu.VMEM((count, outs[0].shape[1], LANES), F32),
@@ -522,10 +527,9 @@
             after=[members[shuf // 2] for members in gathered[:2]] if hop == HOPS - 1 else [],
         )(current, w_branch, w_class_t, *before)
         if hop == 0:
-            first_logits = logits
             after = []
         else:
-            after = [first_logits]
+            after = [logits]
         if hop < HOPS - 1:
             current, to_left, to_right, *rows = call(
                 functools.partial(hop_kernel, plan),
@@ -604,18 +608,22 @@
         jax.ShapeDtypeStruct((branches, width, own), F32),
         jax.ShapeDtypeStruct((classes, own_class), F32),
     ]
-    if chunks == dom and dom % 2 == 0 and dom & (dom - 1) == 0:
+    if chunks == dom and dom % 8 == 0 and dom & (dom - 1) == 0:
         half = dom // 2
         one_f32 = jax.ShapeDtypeStruct((height, LANES), F32)
         made = call(
             functools.partial(late_kernel, kept, ahead, half),
-            [one_f32] * half + [jax.ShapeDtypeStruct((height, LANES), BF16)] * half,
+            [one_f32] * half
+            + [jax.ShapeDtypeStruct((2, height, LANES), BF16)]
+            + [jax.ShapeDtypeStruct((height, LANES), BF16)] * (half - 2),
             [IN_VMEM] * len(late_ins),
             grad_flops,
             [pltpu.VMEM(chunks_f32.shape, F32)],
         )(*late_ins)
         order = list(range(half - 1, -1, -1))
-        arrived = {step: swapped(made[half + step], 1) for step in order}
+        arrived = {step: swapped(made[half + step - 1], 1) for step in order if step > 1}
+        together = swapped(made[half], 1)
+        arrived |= {step: together[step] for step in range(2)}
         total = {step: made[step] + arrived[step].astype(F32) for step in order}
         far = {step: swapped(total[step].astype(BF16), 2 * step) for step in order[:-1]}
         summed = total[0]
@@ -626,8 +634,11 @@
         other = [swapped(value, 1) for value in near]
         results = []
         places = [2 * step for step in range(half)] + [2 * step + 1 for step in range(half)]
-        for part in (slice(0, -half // 2), slice(-half // 2, None)):
-            results = write_out(kept, places[part], (near + other)[part], outs, results)
+        for values, part in (
+            (near + other[: half // 2], slice(0, half + half // 2)),
+            (other[half // 2 :], slice(half + half // 2, None)),
+        ):
+            results = write_out(kept, places[part], values, outs, results)
         grad_branch, grad_class_t = results
     else:
         grads = call(

time: 75.9 us -> 76.8 us (1.012)
  waiting for transfers between devices: 14.2 us -> 17.4 us
  starting transfers between devices: 41.1 us -> 39 us
    ppermute x29 -> x28, waiting for transfers between devices: 12.2 us -> 15.3 us  [swapped(): return lax.ppermute(value, axis, pairs)]
    ppermute x29 -> x28, starting transfers between devices: 25.5 us -> 23.3 us  [swapped(): return lax.ppermute(value, axis, pairs)]
  transfers between devices with their start and end apart: 35 -> 34, of which waited for: 16 -> 15; matrix products, arithmetic and copies ran while one was open for 0% -> 0% of each run, Pallas kernels for 11% -> 11%
where the time goes in v12:
time: 76.8 us; the launch traced here: 76.6 us
  starting transfers between devices  39 us (51%)
  waiting for transfers between devices  17.4 us (23%)
  Pallas kernels  15.1 us (20%)
  local copies, waits for them, and re-layouts  3.42 us (4%)
  between operations  1.66 us (2%)
    ppermute x28, starting transfers between devices, swapped(): return lax.ppermute(value, axis, pairs)  23.3 us
    ppermute x6, starting transfers between devices, passed_along(): return lax.ppermute(value, axis, pairs)  15.7 us
    ppermute x28, waiting for transfers between devices, swapped(): return lax.ppermute(value, axis, pairs)  15.3 us
    unnamed x22, local copies, waits for them, and re-layouts  3.34 us
    pallas_call x2, Pallas kernels, body(): call(functools.partial(hop_kernel, plan), [blocks_f32, slots_f32, slots_f...  2.38 us
    ppermute x6, waiting for transfers between devices, passed_along(): return lax.ppermute(value, axis, pairs)  2.04 us
    pallas_call x2, Pallas kernels, write_out(): pl.pallas_call(functools.partial(out_kernel, kept, distances, len(values)...  1.93 us
    pallas_call x1, Pallas kernels, body(): call(functools.partial(late_kernel, kept, ahead, half), [one_f32] * half...  1.85 us
  transfers between devices with their start and end apart: 34, of which 15 were waited for; matrix products, arithmetic and copies ran while one was open for 0% of the time, Pallas kernels for 11%

profile of v12, /device:TPU:0, one launch (start us, length us, event | category | flops | bytes accessed | tf_op | source)
XLA Modules:
  0.0 76.6 jit_solution(9406386947675883659)
XLA Ops:
  0.7 1.7 %shard_map.139 = (f32[2,128,128]{2,1,0:T(8,128)}, f32[2,128,128]{2,1,0:T(8,128)}, f32[2,128,128]{2,1,0:T(8,128)}, bf16[272,128]{1,0:T(8,128)(2,1)}) custom-call(s32[2]{0:T(128)} %refs_0_.3, s32[2]{0:T(128)} %refs_1_.4, s32[1,2]{1,0:T(1,128)} %refs_2_.1, f32[2,128,128]{2,1,0:T(8,128)} %bitcast.18, s32[1,256]{1,0:T(1,128)} %bitcast.20), custom_call_target="tpu_custom_call" | custom-call | flops 1000 | bytes 1000 | tf_op jit(solution)/shard_map/pallas_call | solution.py:492
  2.4 3.0 %collective-permute-start = (f32[2,128,128]{2,1,0:T(8,128)}, f32[2,128,128]{2,1,0:T(8,128)S(1)}, u32[]{:S(2)}, u32[]{:S(2)}) collective-permute-start(f32[2,128,128]{2,1,0:T(8,128)} %get-tuple-element.36), channel_id=1, source_target_pairs={{0,4},{4,8},{8,12},{12,16},{16,20},{20,24},{24,28},{28,0},{1,5},{5... | collective-permute-start | bytes 393224 | tf_op jit(solution)/shard_map/ppermute | solution.py:30
  5.5 3.1 %collective-permute-start.1 = (f32[2,128,128]{2,1,0:T(8,128)}, f32[2,128,128]{2,1,0:T(8,128)S(1)}, u32[]{:S(2)}, u32[]{:S(2)}) collective-permute-start(f32[2,128,128]{2,1,0:T(8,128)} %get-tuple-element.37), channel_id=1, source_target_pairs={{0,28},{4,0},{8,4},{12,8},{16,12},{20,16},{24,20},{28,24},{1,29},{... | collective-permute-start | bytes 393224 | tf_op jit(solution)/shard_map/ppermute | solution.py:30
  8.6 1.4 %copy-done.1 = bf16[4096,172]{0,1:T(8,128)(2,1)S(1)} copy-done((bf16[4096,172]{0,1:T(8,128)(2,1)S(1)}, bf16[4096,172]{0,1:T(8,128)(2,1)}, u32[]{:S(2)}) %copy-start.1) | copy-done | bytes 1409048
  9.9 1.0 %copy-done.2 = f32[8,128,128]{2,1,0:T(8,128)S(1)} copy-done((f32[8,128,128]{2,1,0:T(8,128)S(1)}, f32[8,128,128]{2,1,0:T(8,128)}, u32[]{:S(2)}) %copy-start.2) | copy-done | bytes 524312
  11.0 0.9 %copy-done.4 = f32[2,128,128]{2,1,0:T(8,128)S(1)} copy-done((f32[2,128,128]{2,1,0:T(8,128)S(1)}, f32[2,128,128]{2,1,0:T(8,128)}, u32[]{:S(2)}) %copy-start.4) | copy-done | bytes 131096
  11.9 0.1 shard_map.140
  12.8 0.1 concatenate.3.refs_0_.refs_1_.refs_5_
  12.9 0.6 collective-permute-done.1.refs_3_
  13.4 1.2 %shard_map.141 = (f32[2,128,128]{2,1,0:T(8,128)S(1)}, f32[2,128,128]{2,1,0:T(8,128)S(1)}, f32[2,128,128]{2,1,0:T(8,128)S(1)}, bf16[256,128]{1,0:T(8,128)(2,1)S(1)}) custom-call(s32[23]{0:T(128)S(1)} %concatenate.3.refs_0_.refs_1_.refs_5_, f32[2,128,128]{2,1,0:T(8,128)S(1)} %get-tuple-element.35.refs_1_.refs_0_, ...), custom_call_target="tpu_custom_call" | custom-call | flops 201326592 | bytes 1376256 | tf_op jit(solution)/shard_map/pallas_call | solution.py:534
  14.6 0.3 collective-permute-start.2
  15.0 4.4 %collective-permute-start.3 = (f32[2,128,128]{2,1,0:T(8,128)S(1)}, f32[2,128,128]{2,1,0:T(8,128)S(1)}, u32[]{:S(2)}, u32[]{:S(2)}) collective-permute-start(f32[2,128,128]{2,1,0:T(8,128)S(1)} %get-tuple-element.42), channel_id=1, source_target_pairs={{0,28},{4,0},{8,4},{12,8},{16,12},{20,16},{24,20},{28,24},{1,29},{... | collective-permute-start | bytes 393224 | tf_op jit(solution)/shard_map/ppermute | solution.py:30
  19.4 1.5 %collective-permute-start.5 = (bf16[272,128]{1,0:T(8,128)(2,1)S(1)}, bf16[272,128]{1,0:T(8,128)(2,1)S(1)}, u32[]{:S(2)}, u32[]{:S(2)}) collective-permute-start(bf16[272,128]{1,0:T(8,128)(2,1)S(1)} %copy-done.3), channel_id=1, source_target_pairs={{0,2},{1,3},{2,0},{3,1},{4,6},{5,7},{6,4},{7,5},{8,10},{9,11},{10,... | collective-permute-start | bytes 208904 | tf_op jit(solution)/shard_map/ppermute | solution.py:35
  20.9 0.6 shard_map.142.refs_3_
  21.5 0.6 collective-permute-start.6
  22.1 0.6 shard_map.143.refs_0_.refs_5_
  22.7 0.9 %collective-permute-done.3.refs_4_ = f32[2,128,128]{2,1,0:T(8,128)S(1)} collective-permute-done((f32[2,128,128]{2,1,0:T(8,128)S(1)}, f32[2,128,128]{2,1,0:T(8,128)S(1)}, u32[]{:S(2)}, u32[]{:S(2)}) %collective-permute-start.3) | collective-permute-done | bytes 131104 | tf_op jit(solution)/shard_map/ppermute | solution.py:30
  23.6 1.2 %shard_map.144 = (f32[2,128,128]{2,1,0:T(8,128)S(1)}, f32[2,128,128]{2,1,0:T(8,128)S(1)}, f32[2,128,128]{2,1,0:T(8,128)S(1)}, bf16[256,128]{1,0:T(8,128)(2,1)S(1)}) custom-call(f32[172,256]{1,0:T(8,128)S(1)} %shard_map.143.refs_0_.refs_5_, s32[23]{0:T(128)S(1)} %concatenate.3.refs_0_.refs_1_.refs_5_, f32[2,128,128]{2,1,0:T(8,128)S(1)} %get-tuple-element.39.refs_0_.refs_2_, ...), custom_call_target="tpu_custom_call" | custom-call | flops 201326592 | bytes 1376256 | tf_op jit(solution)/shard_map/pallas_call | solution.py:534
  24.8 0.1 collective-permute-start.11
  24.8 4.7 %collective-permute-start.12 = (f32[2,128,128]{2,1,0:T(8,128)S(1)}, f32[2,128,128]{2,1,0:T(8,128)S(1)}, u32[]{:S(2)}, u32[]{:S(2)}) collective-permute-start(f32[2,128,128]{2,1,0:T(8,128)S(1)} %get-tuple-element.48), channel_id=1, source_target_pairs={{0,28},{4,0},{8,4},{12,8},{16,12},{20,16},{24,20},{28,24},{1,29},{... | collective-permute-start | bytes 393224 | tf_op jit(solution)/shard_map/ppermute | solution.py:30
  29.6 0.5 collective-permute-start.9
  30.1 0.1 collective-permute-start.10
  30.2 0.7 collective-permute-done.8.refs_4_.refs_2_
  30.8 1.5 %collective-permute-start.4 = (bf16[256,128]{1,0:T(8,128)(2,1)S(1)}, bf16[256,128]{1,0:T(8,128)(2,1)S(1)}, u32[]{:S(2)}, u32[]{:S(2)}) collective-permute-start(bf16[256,128]{1,0:T(8,128)(2,1)S(1)} %get-tuple-element.43.refs_4_), channel_id=1, source_target_pairs={{0,2},{1,3},{2,0},{3,1},{4,6},{5,7},{6,4},{7,5},{8,10},{9,11},{10,... | collective-permute-start | bytes 196616 | tf_op jit(solution)/shard_map/ppermute | solution.py:35
  32.3 0.4 shard_map.146.refs_1_.refs_6_
  32.7 0.6 shard_map.145.refs_0_.refs_2_
  33.3 0.6 collective-permute-done.12.refs_8_
  34.0 1.2 %shard_map.147.refs_1_.refs_6_ = bf16[128,256]{1,0:T(8,128)(2,1)S(1)} custom-call(f32[172,256]{1,0:T(8,128)S(1)} %shard_map.145.refs_0_.refs_2_, s32[1,256]{1,0:T(1,128)S(1)} %shard_map.146.refs_1_.refs_6_, bf16[256,128]{1,0:T(8,128)(2,1)S(1)} %collective-permute-done.9.refs_2_.refs_3_, bf16[256,128]{1,0:T(8,128)(2,1)S(1)} %collective-permute-done.6.refs_1_.refs_3_, ...), custom_call_target="tpu_custom_call" | custom-call | flops 201326592 | bytes 196608 | tf_op jit(solution)/shard_map/pallas_call | solution.py:561
  35.2 0.8 %shard_map.148.refs_8_.refs_0_ = bf16[192,256]{1,0:T(8,128)(2,1)S(1)} custom-call(bf16[256,128]{1,0:T(8,128)(2,1)S(1)} %collective-permute-done.4.refs_0_.refs_5_, bf16[128,256]{1,0:T(8,128)(2,1)S(1)} %shard_map.147.refs_1_.refs_6_, f32[172,256]{1,0:T(8,128)S(1)} %shard_map.145.refs_0_.refs_2_, bf16[4,128,1024]{2,1,0:T(8,128)(2,1)S(1)} %copy-done, ...), custom_call_target="tpu_custom_call" | custom-call | flops 1000 | bytes 1000 | tf_op jit(solution)/shard_map/pallas_call | solution.py:569
  36.0 1.5 %collective-permute-start.14 = (bf16[192,256]{1,0:T(8,128)(2,1)S(1)}, bf16[192,256]{1,0:T(8,128)(2,1)S(1)}, u32[]{:S(2)}, u32[]{:S(2)}) collective-permute-start(bf16[192,256]{1,0:T(8,128)(2,1)S(1)} %shard_map.148.refs_8_.refs_0_), channel_id=1, source_target_pairs={{0,2},{1,3},{2,0},{3,1},{4,6},{5,7},{6,4},{7,5},{8,10},{9,11},{10,... | collective-permute-start | bytes 294920 | tf_op jit(solution)/shard_map/ppermute | solution.py:35
  37.5 0.2 collective-permute-start.16
  37.7 0.3 collective-permute-start.17
  38.0 0.5 collective-permute-start.15
  38.6 0.3 shard_map.149
  38.9 0.1 collective-permute-done.17.refs_7_
  39.0 1.7 %shard_map.150.refs_0_ = f32[8,304,128]{2,1,0:T(8,128)S(1)} custom-call(bf16[272,128]{1,0:T(8,128)(2,1)S(1)} %copy-done.3, bf16[272,128]{1,0:T(8,128)(2,1)S(1)} %collective-permute-done.7.refs_2_.refs_1_, bf16[256,128]{1,0:T(8,128)(2,1)S(1)} %get-tuple-element.45.refs_2_, bf16[256,128]{1,0:T(8,128)(2,1)S(1)} %collective-permute-done.9.refs_2_.refs_3_, ...), custom_call_target="tpu_custom_call" | custom-call | flops 1000 | bytes 1000 | tf_op jit(solution)/shard_map/pallas_call | solution.py:586
  40.7 1.9 %collective-permute-done.15.refs_7_ = bf16[128,256]{1,0:T(8,128)(2,1)S(1)} collective-permute-done((bf16[128,256]{1,0:T(8,128)(2,1)S(1)}, bf16[128,256]{1,0:T(8,128)(2,1)S(1)}, u32[]{:S(2)}, u32[]{:S(2)}) %collective-permute-start.15) | collective-permute-done | bytes 65568 | tf_op jit(solution)/shard_map/ppermute | solution.py:35
  42.6 0.5 collective-permute-start.19
  43.1 0.9 %collective-permute-done.19.refs_6_ = bf16[256,128]{1,0:T(8,128)(2,1)S(1)} collective-permute-done((bf16[256,128]{1,0:T(8,128)(2,1)S(1)}, bf16[256,128]{1,0:T(8,128)(2,1)S(1)}, u32[]{:S(2)}, u32[]{:S(2)}) %collective-permute-start.19) | collective-permute-done | bytes 65568 | tf_op jit(solution)/shard_map/ppermute | solution.py:35
  44.0 0.4 collective-permute-done.20.refs_8_
  44.4 1.9 %shard_map.152 = (f32[304,128]{1,0:T(8,128)S(1)}, f32[304,128]{1,0:T(8,128)S(1)}, f32[304,128]{1,0:T(8,128)S(1)}, f32[304,128]{1,0:T(8,128)S(1)}, bf16[2,304,128...) custom-call(f32[8,304,128]{2,1,0:T(8,128)S(1)} %shard_map.150.refs_0_, ...), custom_call_target="tpu_custom_call" | custom-call | flops 771751936 | bytes 2801664 | tf_op jit(solution)/shard_map/pallas_call | solution.py:614
  46.3 0.1 collective-permute-start.22
  46.3 2.0 %collective-permute-start.21 = (bf16[2,304,128]{2,1,0:T(8,128)(2,1)S(1)}, bf16[2,304,128]{2,1,0:T(8,128)(2,1)S(1)}, u32[]{:S(2)}, u32[]{:S(2)}) collective-permute-start(bf16[2,304,128]{2,1,0:T(8,128)(2,1)S(1)} %get-tuple-element.55), channel_id=1, source_target_pairs={{0,4},{4,0},{8,12},{12,8},{16,20},{20,16},{24,28},{28,24},{1,5},{5... | collective-permute-start | bytes 466952 | tf_op jit(solution)/shard_map/ppermute | solution.py:35
  48.3 0.1 collective-permute-start.24
  48.4 3.1 %collective-permute-done.22 = bf16[304,128]{1,0:T(8,128)(2,1)S(1)} collective-permute-done((bf16[304,128]{1,0:T(8,128)(2,1)S(1)}, bf16[304,128]{1,0:T(8,128)(2,1)S(1)}, u32[]{:S(2)}, u32[]{:S(2)}) %collective-permute-start.22) | collective-permute-done | bytes 77856 | tf_op jit(solution)/shard_map/ppermute | solution.py:35
  51.5 1.6 %collective-permute-start.23 = (bf16[304,128]{1,0:T(8,128)(2,1)S(1)}, bf16[304,128]{1,0:T(8,128)(2,1)S(1)}, u32[]{:S(2)}, u32[]{:S(2)}) collective-permute-start(bf16[304,128]{1,0:T(8,128)(2,1)S(1)} %add_convert_fusion.1), channel_id=1, source_target_pairs={{0,24},{4,28},{8,16},{12,20},{16,8},{20,12},{24,0},{28,4},{1,25},{... | collective-permute-start | bytes 233480 | tf_op jit(solution)/shard_map/ppermute | solution.py:35
  53.1 2.6 %collective-permute-done.24 = bf16[304,128]{1,0:T(8,128)(2,1)S(1)} collective-permute-done((bf16[304,128]{1,0:T(8,128)(2,1)S(1)}, bf16[304,128]{1,0:T(8,128)(2,1)S(1)}, u32[]{:S(2)}, u32[]{:S(2)}) %collective-permute-start.24) | collective-permute-done | bytes 77856 | tf_op jit(solution)/shard_map/ppermute | solution.py:35
  55.8 1.7 %collective-permute-start.25 = (bf16[304,128]{1,0:T(8,128)(2,1)S(1)}, bf16[304,128]{1,0:T(8,128)(2,1)S(1)}, u32[]{:S(2)}, u32[]{:S(2)}) collective-permute-start(bf16[304,128]{1,0:T(8,128)(2,1)S(1)} %add_convert_fusion), channel_id=1, source_target_pairs={{0,16},{4,20},{8,24},{12,28},{16,0},{20,4},{24,8},{28,12},{1,17},{... | collective-permute-start | bytes 233480 | tf_op jit(solution)/shard_map/ppermute | solution.py:35
  57.5 0.3 collective-permute-done.23
  57.9 0.7 collective-permute-start.26
  58.6 2.6 %collective-permute-done.25 = bf16[304,128]{1,0:T(8,128)(2,1)S(1)} collective-permute-done((bf16[304,128]{1,0:T(8,128)(2,1)S(1)}, bf16[304,128]{1,0:T(8,128)(2,1)S(1)}, u32[]{:S(2)}, u32[]{:S(2)}) %collective-permute-start.25) | collective-permute-done | bytes 77856 | tf_op jit(solution)/shard_map/ppermute | solution.py:35
  61.2 1.1 %collective-permute-done.26 = bf16[304,128]{1,0:T(8,128)(2,1)S(1)} collective-permute-done((bf16[304,128]{1,0:T(8,128)(2,1)S(1)}, bf16[304,128]{1,0:T(8,128)(2,1)S(1)}, u32[]{:S(2)}, u32[]{:S(2)}) %collective-permute-start.26) | collective-permute-done | bytes 77856 | tf_op jit(solution)/shard_map/ppermute | solution.py:35
  62.3 0.7 collective-permute-start.27
  63.1 2.0 %collective-permute-start.28 = (bf16[304,128]{1,0:T(8,128)(2,1)S(1)}, bf16[304,128]{1,0:T(8,128)(2,1)S(1)}, u32[]{:S(2)}, u32[]{:S(2)}) collective-permute-start(bf16[304,128]{1,0:T(8,128)(2,1)S(1)} %convert_add_fusion.2.refs_0_), channel_id=1, source_target_pairs={{0,16},{4,20},{8,24},{12,28},{16,0},{20,4},{24,8},{28,12},{1,17},{... | collective-permute-start | bytes 233480 | tf_op jit(solution)/shard_map/ppermute | solution.py:35
  65.1 1.7 %collective-permute-start.29 = (bf16[304,128]{1,0:T(8,128)(2,1)S(1)}, bf16[304,128]{1,0:T(8,128)(2,1)S(1)}, u32[]{:S(2)}, u32[]{:S(2)}) collective-permute-start(bf16[304,128]{1,0:T(8,128)(2,1)S(1)} %convert_add_fusion.2.refs_0_), channel_id=1, source_target_pairs={{0,24},{4,28},{8,16},{12,20},{16,8},{20,12},{24,0},{28,4},{1,25},{... | collective-permute-start | bytes 233480 | tf_op jit(solution)/shard_map/ppermute | solution.py:35
  66.8 0.5 collective-permute-start.30
  67.3 1.6 %collective-permute-start.31 = (bf16[304,128]{1,0:T(8,128)(2,1)S(1)}, bf16[304,128]{1,0:T(8,128)(2,1)S(1)}, u32[]{:S(2)}, u32[]{:S(2)}) collective-permute-start(bf16[304,128]{1,0:T(8,128)(2,1)S(1)} %collective-permute-done.27.refs_1_), channel_id=1, source_target_pairs={{0,4},{4,0},{8,12},{12,8},{16,20},{20,16},{24,28},{28,24},{1,5},{5... | collective-permute-start | bytes 233480 | tf_op jit(solution)/shard_map/ppermute | solution.py:35
  68.8 1.0 %collective-permute-done.28.refs_2_ = bf16[304,128]{1,0:T(8,128)(2,1)S(1)} collective-permute-done((bf16[304,128]{1,0:T(8,128)(2,1)S(1)}, bf16[304,128]{1,0:T(8,128)(2,1)S(1)}, u32[]{:S(2)}, u32[]{:S(2)}) %collective-permute-start.28) | collective-permute-done | bytes 77856 | tf_op jit(solution)/shard_map/ppermute | solution.py:35
  69.9 1.5 %collective-permute-start.32 = (bf16[304,128]{1,0:T(8,128)(2,1)S(1)}, bf16[304,128]{1,0:T(8,128)(2,1)S(1)}, u32[]{:S(2)}, u32[]{:S(2)}) collective-permute-start(bf16[304,128]{1,0:T(8,128)(2,1)S(1)} %collective-permute-done.28.refs_2_), channel_id=1, source_target_pairs={{0,4},{4,0},{8,12},{12,8},{16,20},{20,16},{24,28},{28,24},{1,5},{5... | collective-permute-start | bytes 233480 | tf_op jit(solution)/shard_map/ppermute | solution.py:35
  71.4 1.9 %collective-permute-start.33 = (bf16[304,128]{1,0:T(8,128)(2,1)S(1)}, bf16[304,128]{1,0:T(8,128)(2,1)S(1)}, u32[]{:S(2)}, u32[]{:S(2)}) collective-permute-start(bf16[304,128]{1,0:T(8,128)(2,1)S(1)} %collective-permute-done.29.refs_3_), channel_id=1, source_target_pairs={{0,4},{4,0},{8,12},{12,8},{16,20},{20,16},{24,28},{28,24},{1,5},{5... | collective-permute-start | bytes 233480 | tf_op jit(solution)/shard_map/ppermute | solution.py:35
  73.3 0.8 %shard_map.151 = f32[1,256]{1,0:T(1,128)} custom-call(bf16[192,256]{1,0:T(8,128)(2,1)S(1)} %shard_map.148.refs_8_.refs_0_, bf16[192,256]{1,0:T(8,128)(2,1)S(1)} %collective-permute-done.13.refs_9_.refs_1_, bf16[192,256]{1,0:T(8,128)(2,1)S(1)} %collective-permute-done.14.refs_2_.refs_9_, bf16[192,256]{1,0:T(8,128)(2,1)S(1)} %collective-permute-done.18.refs_3_.refs_10_), custom_call_target="tpu_custom_call" | custom-call | flops 1000 | bytes 1000 | tf_op jit(solution)/shard_map/pallas_call | solution.py:603
  74.1 1.1 %shard_map.153 = (f32[4,128,256]{2,1,0:T(8,128)}, f32[172,1024]{1,0:T(8,128)}) custom-call(bf16[304,128]{1,0:T(8,128)(2,1)S(1)} %convert_add_fusion.2.refs_0_, bf16[304,128]{1,0:T(8,128)(2,1)S(1)} %collective-permute-done.27.refs_1_, bf16[304,128]{1,0:T(8,128)(2,1)S(1)} %collective-permute-done.28.refs_2_, ...), custom_call_target="tpu_custom_call" | custom-call | flops 1000 | bytes 1000 | tf_op jit(solution)/shard_map/pallas_call | solution.py:424
  75.2 0.5 collective-permute-done.33.refs_3_
  75.8 0.8 %shard_map.154 = (f32[4,128,256]{2,1,0:T(8,128)}, f32[172,1024]{1,0:T(8,128)}) custom-call(f32[4,128,256]{2,1,0:T(8,128)} %get-tuple-element.61.refs_0_, f32[172,1024]{1,0:T(8,128)} %get-tuple-element.62.refs_1_, bf16[304,128]{1,0:T(8,128)(2,1)S(1)} %collective-permute-done.32.refs_2_, ...), custom_call_target="tpu_custom_call", output_to_operand_aliasing={{0}: (0, {}), {1}: (1, {})} | custom-call | flops 1000 | bytes 1000 | tf_op jit(solution)/shard_map/pallas_call | solution.py:424
  (48 shorter events, 0.3 us)
Async XLA Ops:
  0.6 12.1 %copy-start.6 = (s32[2]{0:T(128)S(1)}, s32[2]{0:T(128)}, u32[]{:S(2)}) copy-start(s32[2]{0:T(128)} %refs_0_.3) | copy-start | bytes 28
  0.6 12.1 %copy-start.7 = (s32[2]{0:T(128)S(1)}, s32[2]{0:T(128)}, u32[]{:S(2)}) copy-start(s32[2]{0:T(128)} %refs_1_.4) | copy-start | bytes 28
  0.7 12.1 %copy-start.8 = (s32[1,2]{1,0:T(1,128)S(1)}, s32[1,2]{1,0:T(1,128)}, u32[]{:S(2)}) copy-start(s32[1,2]{1,0:T(1,128)} %refs_2_.1) | copy-start | bytes 28
  0.7 12.1 %copy-start.9 = (s32[8]{0:T(128)S(1)}, s32[8]{0:T(128)}, u32[]{:S(2)}) copy-start(s32[8]{0:T(128)} %param.14) | copy-start | bytes 100
  0.7 12.1 %copy-start.10 = (s32[8]{0:T(128)S(1)}, s32[8]{0:T(128)}, u32[]{:S(2)}) copy-start(s32[8]{0:T(128)} %param.15) | copy-start | bytes 100
  2.4 10.4 %collective-permute-start = (f32[2,128,128]{2,1,0:T(8,128)}, f32[2,128,128]{2,1,0:T(8,128)S(1)}, u32[]{:S(2)}, u32[]{:S(2)}) collective-permute-start(f32[2,128,128]{2,1,0:T(8,128)} %get-tuple-element.36), channel_id=1, source_target_pairs={{0,4},{4,8},{8,12},{12,16},{16,20},{20,24},{24,28},{28,0},{1,5},{5... | collective-permute-start | bytes 393224 | tf_op jit(solution)/shard_map/ppermute | solution.py:30
  5.5 8.0 %collective-permute-start.1 = (f32[2,128,128]{2,1,0:T(8,128)}, f32[2,128,128]{2,1,0:T(8,128)S(1)}, u32[]{:S(2)}, u32[]{:S(2)}) collective-permute-start(f32[2,128,128]{2,1,0:T(8,128)} %get-tuple-element.37), channel_id=1, source_target_pairs={{0,28},{4,0},{8,4},{12,8},{16,12},{20,16},{24,20},{28,24},{1,29},{... | collective-permute-start | bytes 393224 | tf_op jit(solution)/shard_map/ppermute | solution.py:30
  8.6 1.4 %copy-start.1 = (bf16[4096,172]{0,1:T(8,128)(2,1)S(1)}, bf16[4096,172]{0,1:T(8,128)(2,1)}, u32[]{:S(2)}) copy-start(bf16[4096,172]{0,1:T(8,128)(2,1)} %param.23) | copy-start | bytes 4227076
  9.9 1.0 %copy-start.2 = (f32[8,128,128]{2,1,0:T(8,128)S(1)}, f32[8,128,128]{2,1,0:T(8,128)}, u32[]{:S(2)}) copy-start(f32[8,128,128]{2,1,0:T(8,128)} %refs_1_.5) | copy-start | bytes 1572868
  11.0 0.9 %copy-start.4 = (f32[2,128,128]{2,1,0:T(8,128)S(1)}, f32[2,128,128]{2,1,0:T(8,128)}, u32[]{:S(2)}) copy-start(f32[2,128,128]{2,1,0:T(8,128)} %get-tuple-element.34.refs_0_) | copy-start | bytes 393220
  11.9 7.5 %copy-start.3 = (bf16[272,128]{1,0:T(8,128)(2,1)S(1)}, bf16[272,128]{1,0:T(8,128)(2,1)}, u32[]{:S(2)}) copy-start(bf16[272,128]{1,0:T(8,128)(2,1)} %get-tuple-element.44.refs_1_.refs_0_) | copy-start | bytes 208900
  11.9 9.0 %copy-start = (bf16[4,128,1024]{2,1,0:T(8,128)(2,1)S(1)}, bf16[4,128,1024]{2,1,0:T(8,128)(2,1)}, u32[]{:S(2)}) copy-start(bf16[4,128,1024]{2,1,0:T(8,128)(2,1)} %refs_11_.1) | copy-start | bytes 3145732
  14.6 8.1 %collective-permute-start.2 = (f32[2,128,128]{2,1,0:T(8,128)S(1)}, f32[2,128,128]{2,1,0:T(8,128)S(1)}, u32[]{:S(2)}, u32[]{:S(2)}) collective-permute-start(f32[2,128,128]{2,1,0:T(8,128)S(1)} %get-tuple-element.41), channel_id=1, source_target_pairs={{0,4},{4,8},{8,12},{12,16},{16,20},{20,24},{24,28},{28,0},{1,5},{5... | collective-permute-start | bytes 393224 | tf_op jit(solution)/shard_map/ppermute | solution.py:30
  15.0 8.6 %collective-permute-start.3 = (f32[2,128,128]{2,1,0:T(8,128)S(1)}, f32[2,128,128]{2,1,0:T(8,128)S(1)}, u32[]{:S(2)}, u32[]{:S(2)}) collective-permute-start(f32[2,128,128]{2,1,0:T(8,128)S(1)} %get-tuple-element.42), channel_id=1, source_target_pairs={{0,28},{4,0},{8,4},{12,8},{16,12},{20,16},{24,20},{28,24},{1,29},{... | collective-permute-start | bytes 393224 | tf_op jit(solution)/shard_map/ppermute | solution.py:30
  19.4 10.1 %collective-permute-start.5 = (bf16[272,128]{1,0:T(8,128)(2,1)S(1)}, bf16[272,128]{1,0:T(8,128)(2,1)S(1)}, u32[]{:S(2)}, u32[]{:S(2)}) collective-permute-start(bf16[272,128]{1,0:T(8,128)(2,1)S(1)} %copy-done.3), channel_id=1, source_target_pairs={{0,2},{1,3},{2,0},{3,1},{4,6},{5,7},{6,4},{7,5},{8,10},{9,11},{10,... | collective-permute-start | bytes 208904 | tf_op jit(solution)/shard_map/ppermute | solution.py:35
  20.9 8.7 %collective-permute-start.7 = (bf16[272,128]{1,0:T(8,128)(2,1)S(1)}, bf16[272,128]{1,0:T(8,128)(2,1)S(1)}, u32[]{:S(2)}, u32[]{:S(2)}) collective-permute-start(bf16[272,128]{1,0:T(8,128)(2,1)S(1)} %copy-done.3), channel_id=1, source_target_pairs={{0,1},{1,0},{2,3},{3,2},{4,5},{5,4},{6,7},{7,6},{8,9},{9,8},{10,11... | collective-permute-start | bytes 208904 | tf_op jit(solution)/shard_map/ppermute | solution.py:35
  21.5 8.6 %collective-permute-start.6 = (bf16[256,128]{1,0:T(8,128)(2,1)S(1)}, bf16[256,128]{1,0:T(8,128)(2,1)S(1)}, u32[]{:S(2)}, u32[]{:S(2)}) collective-permute-start(bf16[256,128]{1,0:T(8,128)(2,1)S(1)} %get-tuple-element.45.refs_2_), channel_id=1, source_target_pairs={{0,2},{1,3},{2,0},{3,1},{4,6},{5,7},{6,4},{7,5},{8,10},{9,11},{10,... | collective-permute-start | bytes 196616 | tf_op jit(solution)/shard_map/ppermute | solution.py:35
  22.1 10.2 %copy-start.5 = (s32[1,256]{1,0:T(1,128)S(1)}, s32[1,256]{1,0:T(1,128)}, u32[]{:S(2)}) copy-start(s32[1,256]{1,0:T(1,128)} %refs_5_.1) | copy-start | bytes 3076
  24.8 8.6 %collective-permute-start.11 = (f32[2,128,128]{2,1,0:T(8,128)S(1)}, f32[2,128,128]{2,1,0:T(8,128)S(1)}, u32[]{:S(2)}, u32[]{:S(2)}) collective-permute-start(f32[2,128,128]{2,1,0:T(8,128)S(1)} %get-tuple-element.47), channel_id=1, source_target_pairs={{0,4},{4,8},{8,12},{12,16},{16,20},{20,24},{24,28},{28,0},{1,5},{5... | collective-permute-start | bytes 393224 | tf_op jit(solution)/shard_map/ppermute | solution.py:30
  24.8 9.1 %collective-permute-start.12 = (f32[2,128,128]{2,1,0:T(8,128)S(1)}, f32[2,128,128]{2,1,0:T(8,128)S(1)}, u32[]{:S(2)}, u32[]{:S(2)}) collective-permute-start(f32[2,128,128]{2,1,0:T(8,128)S(1)} %get-tuple-element.48), channel_id=1, source_target_pairs={{0,28},{4,0},{8,4},{12,8},{16,12},{20,16},{24,20},{28,24},{1,29},{... | collective-permute-start | bytes 393224 | tf_op jit(solution)/shard_map/ppermute | solution.py:30
  29.6 1.3 %collective-permute-start.8 = (bf16[272,128]{1,0:T(8,128)(2,1)S(1)}, bf16[272,128]{1,0:T(8,128)(2,1)S(1)}, u32[]{:S(2)}, u32[]{:S(2)}) collective-permute-start(bf16[272,128]{1,0:T(8,128)(2,1)S(1)} %collective-permute-done.5.refs_0_.refs_3_.refs_1_), channel_id=1, source_target_pairs={{0,1},{1,0},{2,3},{3,2},{4,5},{5,4},{6,7},{7,6},{8,9},{9,8},{10,11... | collective-permute-start | bytes 208904 | tf_op jit(solution)/shard_map/ppermute | solution.py:35
  29.6 3.7 %collective-permute-start.9 = (bf16[256,128]{1,0:T(8,128)(2,1)S(1)}, bf16[256,128]{1,0:T(8,128)(2,1)S(1)}, u32[]{:S(2)}, u32[]{:S(2)}) collective-permute-start(bf16[256,128]{1,0:T(8,128)(2,1)S(1)} %get-tuple-element.45.refs_2_), channel_id=1, source_target_pairs={{0,1},{1,0},{2,3},{3,2},{4,5},{5,4},{6,7},{7,6},{8,9},{9,8},{10,11... | collective-permute-start | bytes 196616 | tf_op jit(solution)/shard_map/ppermute | solution.py:35
  30.1 3.2 %collective-permute-start.10 = (bf16[256,128]{1,0:T(8,128)(2,1)S(1)}, bf16[256,128]{1,0:T(8,128)(2,1)S(1)}, u32[]{:S(2)}, u32[]{:S(2)}) collective-permute-start(bf16[256,128]{1,0:T(8,128)(2,1)S(1)} %collective-permute-done.6.refs_1_.refs_3_), channel_id=1, source_target_pairs={{0,1},{1,0},{2,3},{3,2},{4,5},{5,4},{6,7},{7,6},{8,9},{9,8},{10,11... | collective-permute-start | bytes 196616 | tf_op jit(solution)/shard_map/ppermute | solution.py:35
  30.8 4.3 %collective-permute-start.4 = (bf16[256,128]{1,0:T(8,128)(2,1)S(1)}, bf16[256,128]{1,0:T(8,128)(2,1)S(1)}, u32[]{:S(2)}, u32[]{:S(2)}) collective-permute-start(bf16[256,128]{1,0:T(8,128)(2,1)S(1)} %get-tuple-element.43.refs_4_), channel_id=1, source_target_pairs={{0,2},{1,3},{2,0},{3,1},{4,6},{5,7},{6,4},{7,5},{8,10},{9,11},{10,... | collective-permute-start | bytes 196616 | tf_op jit(solution)/shard_map/ppermute | solution.py:35
  36.0 3.0 %collective-permute-start.13 = (bf16[192,256]{1,0:T(8,128)(2,1)S(1)}, bf16[192,256]{1,0:T(8,128)(2,1)S(1)}, u32[]{:S(2)}, u32[]{:S(2)}) collective-permute-start(bf16[192,256]{1,0:T(8,128)(2,1)S(1)} %shard_map.148.refs_8_.refs_0_), channel_id=1, source_target_pairs={{0,1},{1,0},{2,3},{3,2},{4,5},{5,4},{6,7},{7,6},{8,9},{9,8},{10,11... | collective-permute-start | bytes 294920 | tf_op jit(solution)/shard_map/ppermute | solution.py:35
  36.0 6.6 %collective-permute-start.14 = (bf16[192,256]{1,0:T(8,128)(2,1)S(1)}, bf16[192,256]{1,0:T(8,128)(2,1)S(1)}, u32[]{:S(2)}, u32[]{:S(2)}) collective-permute-start(bf16[192,256]{1,0:T(8,128)(2,1)S(1)} %shard_map.148.refs_8_.refs_0_), channel_id=1, source_target_pairs={{0,2},{1,3},{2,0},{3,1},{4,6},{5,7},{6,4},{7,5},{8,10},{9,11},{10,... | collective-permute-start | bytes 294920 | tf_op jit(solution)/shard_map/ppermute | solution.py:35
  37.5 1.3 %collective-permute-start.16 = (bf16[256,128]{1,0:T(8,128)(2,1)S(1)}, bf16[256,128]{1,0:T(8,128)(2,1)S(1)}, u32[]{:S(2)}, u32[]{:S(2)}) collective-permute-start(bf16[256,128]{1,0:T(8,128)(2,1)S(1)} %get-tuple-element.43.refs_4_), channel_id=1, source_target_pairs={{0,1},{1,0},{2,3},{3,2},{4,5},{5,4},{6,7},{7,6},{8,9},{9,8},{10,11... | collective-permute-start | bytes 196616 | tf_op jit(solution)/shard_map/ppermute | solution.py:35
  37.7 1.3 %collective-permute-start.17 = (bf16[128,256]{1,0:T(8,128)(2,1)S(1)}, bf16[128,256]{1,0:T(8,128)(2,1)S(1)}, u32[]{:S(2)}, u32[]{:S(2)}) collective-permute-start(bf16[128,256]{1,0:T(8,128)(2,1)S(1)} %shard_map.147.refs_1_.refs_6_), channel_id=1, source_target_pairs={{0,1},{1,0},{2,3},{3,2},{4,5},{5,4},{6,7},{7,6},{8,9},{9,8},{10,11... | collective-permute-start | bytes 196616 | tf_op jit(solution)/shard_map/ppermute | solution.py:35
  38.0 4.6 %collective-permute-start.15 = (bf16[128,256]{1,0:T(8,128)(2,1)S(1)}, bf16[128,256]{1,0:T(8,128)(2,1)S(1)}, u32[]{:S(2)}, u32[]{:S(2)}) collective-permute-start(bf16[128,256]{1,0:T(8,128)(2,1)S(1)} %shard_map.147.refs_1_.refs_6_), channel_id=1, source_target_pairs={{0,2},{1,3},{2,0},{3,1},{4,6},{5,7},{6,4},{7,5},{8,10},{9,11},{10,... | collective-permute-start | bytes 196616 | tf_op jit(solution)/shard_map/ppermute | solution.py:35
  42.6 1.8 %collective-permute-start.18 = (bf16[192,256]{1,0:T(8,128)(2,1)S(1)}, bf16[192,256]{1,0:T(8,128)(2,1)S(1)}, u32[]{:S(2)}, u32[]{:S(2)}) collective-permute-start(bf16[192,256]{1,0:T(8,128)(2,1)S(1)} %collective-permute-done.14.refs_2_.refs_9_), channel_id=1, source_target_pairs={{0,1},{1,0},{2,3},{3,2},{4,5},{5,4},{6,7},{7,6},{8,9},{9,8},{10,11... | collective-permute-start | bytes 294920 | tf_op jit(solution)/shard_map/ppermute | solution.py:35
  42.6 1.4 %collective-permute-start.19 = (bf16[256,128]{1,0:T(8,128)(2,1)S(1)}, bf16[256,128]{1,0:T(8,128)(2,1)S(1)}, u32[]{:S(2)}, u32[]{:S(2)}) collective-permute-start(bf16[256,128]{1,0:T(8,128)(2,1)S(1)} %collective-permute-done.4.refs_0_.refs_5_), channel_id=1, source_target_pairs={{0,1},{1,0},{2,3},{3,2},{4,5},{5,4},{6,7},{7,6},{8,9},{9,8},{10,11... | collective-permute-start | bytes 196616 | tf_op jit(solution)/shard_map/ppermute | solution.py:35
  43.1 1.3 %collective-permute-start.20 = (bf16[128,256]{1,0:T(8,128)(2,1)S(1)}, bf16[128,256]{1,0:T(8,128)(2,1)S(1)}, u32[]{:S(2)}, u32[]{:S(2)}) collective-permute-start(bf16[128,256]{1,0:T(8,128)(2,1)S(1)} %collective-permute-done.15.refs_7_), channel_id=1, source_target_pairs={{0,1},{1,0},{2,3},{3,2},{4,5},{5,4},{6,7},{7,6},{8,9},{9,8},{10,11... | collective-permute-start | bytes 196616 | tf_op jit(solution)/shard_map/ppermute | solution.py:35
  46.3 5.3 %collective-permute-start.22 = (bf16[304,128]{1,0:T(8,128)(2,1)S(1)}, bf16[304,128]{1,0:T(8,128)(2,1)S(1)}, u32[]{:S(2)}, u32[]{:S(2)}) collective-permute-start(bf16[304,128]{1,0:T(8,128)(2,1)S(1)} %get-tuple-element.57), channel_id=1, source_target_pairs={{0,4},{4,0},{8,12},{12,8},{16,20},{20,16},{24,28},{28,24},{1,5},{5... | collective-permute-start | bytes 233480 | tf_op jit(solution)/shard_map/ppermute | solution.py:35
  46.3 11.1 %collective-permute-start.21 = (bf16[2,304,128]{2,1,0:T(8,128)(2,1)S(1)}, bf16[2,304,128]{2,1,0:T(8,128)(2,1)S(1)}, u32[]{:S(2)}, u32[]{:S(2)}) collective-permute-start(bf16[2,304,128]{2,1,0:T(8,128)(2,1)S(1)} %get-tuple-element.55), channel_id=1, source_target_pairs={{0,4},{4,0},{8,12},{12,8},{16,20},{20,16},{24,28},{28,24},{1,5},{5... | collective-permute-start | bytes 466952 | tf_op jit(solution)/shard_map/ppermute | solution.py:35
  48.3 7.4 %collective-permute-start.24 = (bf16[304,128]{1,0:T(8,128)(2,1)S(1)}, bf16[304,128]{1,0:T(8,128)(2,1)S(1)}, u32[]{:S(2)}, u32[]{:S(2)}) collective-permute-start(bf16[304,128]{1,0:T(8,128)(2,1)S(1)} %get-tuple-element.59), channel_id=1, source_target_pairs={{0,4},{4,0},{8,12},{12,8},{16,20},{20,16},{24,28},{28,24},{1,5},{5... | collective-permute-start | bytes 233480 | tf_op jit(solution)/shard_map/ppermute | solution.py:35
  51.5 6.3 %collective-permute-start.23 = (bf16[304,128]{1,0:T(8,128)(2,1)S(1)}, bf16[304,128]{1,0:T(8,128)(2,1)S(1)}, u32[]{:S(2)}, u32[]{:S(2)}) collective-permute-start(bf16[304,128]{1,0:T(8,128)(2,1)S(1)} %add_convert_fusion.1), channel_id=1, source_target_pairs={{0,24},{4,28},{8,16},{12,20},{16,8},{20,12},{24,0},{28,4},{1,25},{... | collective-permute-start | bytes 233480 | tf_op jit(solution)/shard_map/ppermute | solution.py:35
  55.8 5.4 %collective-permute-start.25 = (bf16[304,128]{1,0:T(8,128)(2,1)S(1)}, bf16[304,128]{1,0:T(8,128)(2,1)S(1)}, u32[]{:S(2)}, u32[]{:S(2)}) collective-permute-start(bf16[304,128]{1,0:T(8,128)(2,1)S(1)} %add_convert_fusion), channel_id=1, source_target_pairs={{0,16},{4,20},{8,24},{12,28},{16,0},{20,4},{24,8},{28,12},{1,17},{... | collective-permute-start | bytes 233480 | tf_op jit(solution)/shard_map/ppermute | solution.py:35
  57.9 4.5 %collective-permute-start.26 = (bf16[304,128]{1,0:T(8,128)(2,1)S(1)}, bf16[304,128]{1,0:T(8,128)(2,1)S(1)}, u32[]{:S(2)}, u32[]{:S(2)}) collective-permute-start(bf16[304,128]{1,0:T(8,128)(2,1)S(1)} %get-tuple-element.65), channel_id=1, source_target_pairs={{0,8},{4,12},{8,0},{12,4},{16,24},{20,28},{24,16},{28,20},{1,9},{5... | collective-permute-start | bytes 233480 | tf_op jit(solution)/shard_map/ppermute | solution.py:35
  62.3 4.9 %collective-permute-start.27 = (bf16[304,128]{1,0:T(8,128)(2,1)S(1)}, bf16[304,128]{1,0:T(8,128)(2,1)S(1)}, u32[]{:S(2)}, u32[]{:S(2)}) collective-permute-start(bf16[304,128]{1,0:T(8,128)(2,1)S(1)} %convert_add_fusion.2.refs_0_), channel_id=1, source_target_pairs={{0,8},{4,12},{8,0},{12,4},{16,24},{20,28},{24,16},{28,20},{1,9},{5... | collective-permute-start | bytes 233480 | tf_op jit(solution)/shard_map/ppermute | solution.py:35
  63.1 6.8 %collective-permute-start.28 = (bf16[304,128]{1,0:T(8,128)(2,1)S(1)}, bf16[304,128]{1,0:T(8,128)(2,1)S(1)}, u32[]{:S(2)}, u32[]{:S(2)}) collective-permute-start(bf16[304,128]{1,0:T(8,128)(2,1)S(1)} %convert_add_fusion.2.refs_0_), channel_id=1, source_target_pairs={{0,16},{4,20},{8,24},{12,28},{16,0},{20,4},{24,8},{28,12},{1,17},{... | collective-permute-start | bytes 233480 | tf_op jit(solution)/shard_map/ppermute | solution.py:35
  65.1 6.3 %collective-permute-start.29 = (bf16[304,128]{1,0:T(8,128)(2,1)S(1)}, bf16[304,128]{1,0:T(8,128)(2,1)S(1)}, u32[]{:S(2)}, u32[]{:S(2)}) collective-permute-start(bf16[304,128]{1,0:T(8,128)(2,1)S(1)} %convert_add_fusion.2.refs_0_), channel_id=1, source_target_pairs={{0,24},{4,28},{8,16},{12,20},{16,8},{20,12},{24,0},{28,4},{1,25},{... | collective-permute-start | bytes 233480 | tf_op jit(solution)/shard_map/ppermute | solution.py:35
  66.8 7.3 %collective-permute-start.30 = (bf16[304,128]{1,0:T(8,128)(2,1)S(1)}, bf16[304,128]{1,0:T(8,128)(2,1)S(1)}, u32[]{:S(2)}, u32[]{:S(2)}) collective-permute-start(bf16[304,128]{1,0:T(8,128)(2,1)S(1)} %convert_add_fusion.2.refs_0_), channel_id=1, source_target_pairs={{0,4},{4,0},{8,12},{12,8},{16,20},{20,16},{24,28},{28,24},{1,5},{5... | collective-permute-start | bytes 233480 | tf_op jit(solution)/shard_map/ppermute | solution.py:35
  67.3 6.8 %collective-permute-start.31 = (bf16[304,128]{1,0:T(8,128)(2,1)S(1)}, bf16[304,128]{1,0:T(8,128)(2,1)S(1)}, u32[]{:S(2)}, u32[]{:S(2)}) collective-permute-start(bf16[304,128]{1,0:T(8,128)(2,1)S(1)} %collective-permute-done.27.refs_1_), channel_id=1, source_target_pairs={{0,4},{4,0},{8,12},{12,8},{16,20},{20,16},{24,28},{28,24},{1,5},{5... | collective-permute-start | bytes 233480 | tf_op jit(solution)/shard_map/ppermute | solution.py:35
  69.9 5.4 %collective-permute-start.32 = (bf16[304,128]{1,0:T(8,128)(2,1)S(1)}, bf16[304,128]{1,0:T(8,128)(2,1)S(1)}, u32[]{:S(2)}, u32[]{:S(2)}) collective-permute-start(bf16[304,128]{1,0:T(8,128)(2,1)S(1)} %collective-permute-done.28.refs_2_), channel_id=1, source_target_pairs={{0,4},{4,0},{8,12},{12,8},{16,20},{20,16},{24,28},{28,24},{1,5},{5... | collective-permute-start | bytes 233480 | tf_op jit(solution)/shard_map/ppermute | solution.py:35
  71.4 4.4 %collective-permute-start.33 = (bf16[304,128]{1,0:T(8,128)(2,1)S(1)}, bf16[304,128]{1,0:T(8,128)(2,1)S(1)}, u32[]{:S(2)}, u32[]{:S(2)}) collective-permute-start(bf16[304,128]{1,0:T(8,128)(2,1)S(1)} %collective-permute-done.29.refs_3_), channel_id=1, source_target_pairs={{0,4},{4,0},{8,12},{12,8},{16,20},{20,16},{24,28},{28,24},{1,5},{5... | collective-permute-start | bytes 233480 | tf_op jit(solution)/shard_map/ppermute | solution.py:35

commit v13 on v11

--- a/solution.py
+++ b/solution.py
@@ -24,10 +24,13 @@
     return -(-value // multiple) * multiple
 
 
-def passed_along(value, axis, steps):
-    count = lax.axis_size(axis)
-    pairs = [(source, (source + steps) % count) for source in range(count)]
-    return lax.ppermute(value, axis, pairs)
+def exchanged(to_wrap, to_right, to_left):
+    last = lax.axis_size("dom") - 1
+    return (
+        lax.ppermute(to_wrap, "dom", [(0, last), (last, 0)]),
+        lax.ppermute(to_right, "dom", [(d, d + 1) for d in range(last)]),
+        lax.ppermute(to_left, "dom", [(d + 1, d) for d in range(last)]),
+    )
 
 
 def swapped(value, distance, axis="dom"):
@@ -76,14 +79,18 @@
         self.sent = self.right + slots
 
 
-def write_sends(blocks, left_ref, right_ref, ids, counts):
+def write_sends(blocks, left_ref, right_ref, wrap_ref, ids, counts):
+    start = lax.axis_index("dom") == 0
     for slot in range(left_ref.shape[0]):
+        values = []
         for side, out_ref in enumerate((left_ref, right_ref)):
             index = ids(side, slot)
             picked = blocks[0]
             for number in range(1, len(blocks)):
                 picked = jnp.where(index == number, blocks[number], picked)
-            out_ref[slot] = jnp.where(slot < counts(side), picked, 0.0)
+            values.append(jnp.where(slot < counts(side), picked, 0.0))
+            out_ref[slot] = values[-1]
+        wrap_ref[slot] = jnp.where(start, values[0], values[1])
 
 
 def copied(sources, targets, sems):
@@ -99,7 +106,7 @@
 
 def first_kernel(
     sl_ref, sr_ref, sc_ref, feat_ref, label_from,
-    left_ref, right_ref, held_ref, b_ref,
+    left_ref, right_ref, wrap_ref, held_ref, b_ref,
     sl_here, sr_here, sc_here, label_ref, sems,
 ):
     copied(
@@ -112,6 +119,7 @@
         blocks,
         left_ref,
         right_ref,
+        wrap_ref,
         lambda side, slot: (sl_here, sr_here)[side][slot],
         lambda side: sc_here[0, side],
     )
@@ -156,23 +164,27 @@
     return totals
 
 
-def extend(cur_ref, low_ref, high_ref, ext_ref):
+def extend(cur_ref, wrap_ref, low_ref, high_ref, ext_ref):
     local = cur_ref.shape[0]
     slots = low_ref.shape[0]
-    ext_ref[local : local + slots] = low_ref[...]
-    ext_ref[local + slots :] = high_ref[...]
+    dom = lax.axis_index("dom")
+    last = lax.axis_size("dom") - 1
+    ext_ref[local : local + slots] = jnp.where(dom == 0, wrap_ref[...], low_ref[...])
+    ext_ref[local + slots :] = jnp.where(dom == last, wrap_ref[...], high_ref[...])
 
 
 def hop_kernel(
-    plan, plan_ref, cur_ref, low_ref, high_ref, tiles_ref, next_ref, left_ref, right_ref, *refs
+    plan, plan_ref, cur_ref, wrap_in_ref, low_ref, high_ref, tiles_ref,
+    next_ref, left_ref, right_ref, wrap_ref, *refs
 ):
     ext_ref = refs[-1]
-    extend(cur_ref, low_ref, high_ref, ext_ref)
+    extend(cur_ref, wrap_in_ref, low_ref, high_ref, ext_ref)
     blocks = next_blocks(plan, plan_ref, cur_ref, tiles_ref, ext_ref)
     write_sends(
         blocks,
         left_ref,
         right_ref,
+        wrap_ref,
         lambda side, slot: plan_ref[(plan.left, plan.right)[side] + slot],
         lambda side: plan_ref[plan.sent + side],
     )
@@ -248,8 +260,10 @@
     refs[-1][...] = total[0:1] + total[1:2] + total[2:3]
 
 
-def last_hop_kernel(plan, plan_ref, cur_ref, low_ref, high_ref, tiles_ref, out_ref, ext_ref):
-    extend(cur_ref, low_ref, high_ref, ext_ref)
+def last_hop_kernel(
+    plan, plan_ref, cur_ref, wrap_ref, low_ref, high_ref, tiles_ref, out_ref, ext_ref
+):
+    extend(cur_ref, wrap_ref, low_ref, high_ref, ext_ref)
     blocks = next_blocks(plan, plan_ref, cur_ref, tiles_ref, ext_ref)
     for number, block in enumerate(blocks):
         width = block.shape[1]
@@ -484,9 +498,9 @@
     hop_flops = 12 * tiles * block * block * width
     forward_flops = 2 * nodes * hid * (width + classes)
     ext = pltpu.VMEM((local + 2 * slots, block, width), F32)
-    to_left, to_right, current, *rows = call(
+    to_left, to_right, to_wrap, current, *rows = call(
         first_kernel,
-        [slots_f32, slots_f32, blocks_f32, first_b16],
+        [slots_f32, slots_f32, slots_f32, blocks_f32, first_b16],
         [ANYWHERE] * 5,
         1000,
         [
@@ -508,11 +522,19 @@
         [IN_VMEM] * 3,
         1000,
     )(current, tile_values, w_class_t)
+    crossing = []
     for hop in range(HOPS):
-        from_lower = passed_along(to_right, "dom", 1)
-        from_upper = passed_along(to_left, "dom", -1)
+        came = exchanged(to_wrap, to_right, to_left)
         for value in rows:
-            gathered.append(in_group(value))
+            if hop < HOPS - 1:
+                crossing.append((value, swapped(value, shuf // 2, "shuf")))
+            else:
+                crossing, _ = lax.optimization_barrier((crossing, current))
+                for mine_here, across in crossing:
+                    gathered.append(
+                        in_group(mine_here, shuf // 4) + in_group(across, shuf // 4)
+                    )
+                gathered.append(in_group(value))
         before = [] if logits is None else [logits]
         logits = call(
             functools.partial(forward_kernel, hop),
@@ -527,14 +549,14 @@
         else:
             after = [first_logits]
         if hop < HOPS - 1:
-            current, to_left, to_right, *rows = call(
+            current, to_left, to_right, to_wrap, *rows = call(
                 functools.partial(hop_kernel, plan),
-                [blocks_f32, slots_f32, slots_f32, rows_b16],
-                [IN_SMEM] + [IN_VMEM] * 4,
+                [blocks_f32, slots_f32, slots_f32, slots_f32, rows_b16],
+                [IN_SMEM] + [IN_VMEM] * 5,
                 hop_flops,
                 [ext],
                 after,
-            )(small, current, from_lower, from_upper, tile_values)
+            )(small, current, *came, tile_values)
 
     label_mine = call(
         label_kernel,
@@ -557,11 +579,11 @@
     last_rows = call(
         functools.partial(last_hop_kernel, plan),
         jax.ShapeDtypeStruct((block, local * width), BF16),
-        [IN_SMEM] + [IN_VMEM] * 4,
+        [IN_SMEM] + [IN_VMEM] * 5,
         hop_flops,
         [ext],
         [logits, label_mine, *gathered[1][1:]],
-    )(small, current, from_lower, from_upper, tile_values)
+    )(small, current, *came, tile_values)
     dlogits = call(
         functools.partial(loss_and_gradient_kernel, row_scale),
         jax.ShapeDtypeStruct((kept + 16, nodes), BF16),

time: 75.9 us -> 92.1 us (1.21)
  waiting for transfers between devices: 14.2 us -> 22.5 us
  starting transfers between devices: 41.1 us -> 48.2 us
    ppermute x6 -> x9, starting transfers between devices: 15.7 us -> 26.4 us  [the longest x3 18.7 us: exchanged(): lax.ppermute(to_wrap, 'dom', [(0, last), (last, 0)])]
    ppermute x6 -> x9, waiting for transfers between devices: 2.04 us -> 6.36 us  [the longest x3 5.12 us: exchanged(): lax.ppermute(to_left, 'dom', [(d + 1, d) for d in range(last)])]
    ppermute x29, waiting for transfers between devices: 12.2 us -> 16.2 us  [swapped(): return lax.ppermute(value, axis, pairs)]
    ppermute x29, starting transfers between devices: 25.5 us -> 21.7 us  [swapped(): return lax.ppermute(value, axis, pairs)]
  transfers between devices with their start and end apart: 35 -> 38, of which waited for: 16 -> 18; matrix products, arithmetic and copies ran while one was open for 0% -> 0% of each run, Pallas kernels for 11% -> 9%
where the time goes in v13:
time: 92.1 us; the launch traced here: 91.6 us
  starting transfers between devices  48.2 us (52%)
  waiting for transfers between devices  22.5 us (24%)
  Pallas kernels  15.5 us (17%)
  local copies, waits for them, and re-layouts  3.47 us (4%)
  between operations  1.79 us (2%)
    ppermute x29, starting transfers between devices, swapped(): return lax.ppermute(value, axis, pairs)  21.7 us
    ppermute x3, starting transfers between devices, exchanged(): lax.ppermute(to_wrap, 'dom', [(0, last), (last, 0)])  18.7 us
    ppermute x29, waiting for transfers between devices, swapped(): return lax.ppermute(value, axis, pairs)  16.2 us
    ppermute x3, waiting for transfers between devices, exchanged(): lax.ppermute(to_left, 'dom', [(d + 1, d) for d in range(last)])  5.12 us
    ppermute x3, starting transfers between devices, exchanged(): lax.ppermute(to_right, 'dom', [(d, d + 1) for d in range(last)])  3.89 us
    ppermute x3, starting transfers between devices, exchanged(): lax.ppermute(to_left, 'dom', [(d + 1, d) for d in range(last)])  3.88 us
    unnamed x22, local copies, waits for them, and re-layouts  3.39 us
    pallas_call x2, Pallas kernels, body(): call(functools.partial(hop_kernel, plan), [blocks_f32, slots_f32, slots_f...  2.79 us
  transfers between devices with their start and end apart: 38, of which 18 were waited for; matrix products, arithmetic and copies ran while one was open for 0% of the time, Pallas kernels for 9%

profile of v13, /device:TPU:0, one launch (start us, length us, event | category | flops | bytes accessed | tf_op | source)
XLA Modules:
  0.0 91.6 jit_solution(13196057455172986721)
XLA Ops:
  0.7 1.8 %shard_map.139 = (f32[2,128,128]{2,1,0:T(8,128)}, f32[2,128,128]{2,1,0:T(8,128)}, f32[2,128,128]{2,1,0:T(8,128)}, f32[2,128,128]{2,1,0:T(8,128)}, bf16[272,128]{1,0:T(8,128)(2,1)}) custom-call(s32[2]{0:T(128)} %refs_0_.3, s32[2]{0:T(128)} %refs_1_.4, s32[1,2]{1,0:T(1,128)} %refs_2_.1, f32[2,128,128]{2,1,0:T(8,128)} %bitcast.8, s32[1,256]{1,0:T(1,128)} %bitcast.10), custom_call_target="tpu_custom_call" | custom-call | flops 1000 | bytes 1000 | tf_op jit(solution)/shard_map/pallas_call | solution.py:501
  2.5 7.9 %collective-permute-start = (f32[2,128,128]{2,1,0:T(8,128)}, f32[2,128,128]{2,1,0:T(8,128)S(1)}, u32[]{:S(2)}, u32[]{:S(2)}) collective-permute-start(f32[2,128,128]{2,1,0:T(8,128)} %get-tuple-element.45), channel_id=1, source_target_pairs={{0,28},{28,0},{1,29},{29,1},{2,30},{30,2},{3,31},{31,3}} | collective-permute-start | bytes 393224 | tf_op jit(solution)/shard_map/ppermute | solution.py:30
  10.4 1.3 %collective-permute-start.1 = (f32[2,128,128]{2,1,0:T(8,128)}, f32[2,128,128]{2,1,0:T(8,128)S(1)}, u32[]{:S(2)}, u32[]{:S(2)}) collective-permute-start(f32[2,128,128]{2,1,0:T(8,128)} %get-tuple-element.46), channel_id=1, source_target_pairs={{0,4},{4,8},{8,12},{12,16},{16,20},{20,24},{24,28},{1,5},{5,9},{9,... | collective-permute-start | bytes 393224 | tf_op jit(solution)/shard_map/ppermute | solution.py:31
  11.7 1.3 %collective-permute-start.2 = (f32[2,128,128]{2,1,0:T(8,128)}, f32[2,128,128]{2,1,0:T(8,128)}, u32[]{:S(2)}, u32[]{:S(2)}) collective-permute-start(f32[2,128,128]{2,1,0:T(8,128)} %get-tuple-element.47), channel_id=1, source_target_pairs={{4,0},{8,4},{12,8},{16,12},{20,16},{24,20},{28,24},{5,1},{9,5},{13... | collective-permute-start | bytes 393224 | tf_op jit(solution)/shard_map/ppermute | solution.py:32
  13.0 1.4 %copy-done.1 = bf16[4096,172]{0,1:T(8,128)(2,1)S(1)} copy-done((bf16[4096,172]{0,1:T(8,128)(2,1)S(1)}, bf16[4096,172]{0,1:T(8,128)(2,1)}, u32[]{:S(2)}) %copy-start.1) | copy-done | bytes 1409048
  14.4 1.0 %copy-done.2 = f32[8,128,128]{2,1,0:T(8,128)S(1)} copy-done((f32[8,128,128]{2,1,0:T(8,128)S(1)}, f32[8,128,128]{2,1,0:T(8,128)}, u32[]{:S(2)}) %copy-start.2) | copy-done | bytes 524312
  15.4 0.9 copy-done.4
  17.6 1.3 %collective-permute-done.2.refs_4_ = f32[2,128,128]{2,1,0:T(8,128)} collective-permute-done((f32[2,128,128]{2,1,0:T(8,128)}, f32[2,128,128]{2,1,0:T(8,128)}, u32[]{:S(2)}, u32[]{:S(2)}) %collective-permute-start.2) | collective-permute-done | bytes 131104 | tf_op jit(solution)/shard_map/ppermute | solution.py:32
  18.9 1.6 %shard_map.142 = (f32[2,128,128]{2,1,0:T(8,128)S(1)}, f32[2,128,128]{2,1,0:T(8,128)S(1)}, f32[2,128,128]{2,1,0:T(8,128)S(1)}, f32[2,128,128]{2,1,0:T(8,128)S(1)}, bf16[256,128]{1,0:T(8,128)(2,1)S(1)}) custom-call(s32[23]{0:T(128)S(1)} %concatenate.3.refs_0_.refs_1_.refs_5_, f32[2,128,128]{2,1,0:T(8,128)S(1)} %get-tuple-element.43.refs_0_.refs_1_, ...), custom_call_target="tpu_custom_call" | custom-call | flops 201326592 | bytes 1769472 | tf_op jit(solution)/shard_map/pallas_call | solution.py:552
  20.5 4.3 %collective-permute-start.3 = (f32[2,128,128]{2,1,0:T(8,128)S(1)}, f32[2,128,128]{2,1,0:T(8,128)S(1)}, u32[]{:S(2)}, u32[]{:S(2)}) collective-permute-start(f32[2,128,128]{2,1,0:T(8,128)S(1)} %get-tuple-element.50), channel_id=1, source_target_pairs={{0,28},{28,0},{1,29},{29,1},{2,30},{30,2},{3,31},{31,3}} | collective-permute-start | bytes 393224 | tf_op jit(solution)/shard_map/ppermute | solution.py:30
  24.8 1.3 %collective-permute-start.4 = (f32[2,128,128]{2,1,0:T(8,128)S(1)}, f32[2,128,128]{2,1,0:T(8,128)S(1)}, u32[]{:S(2)}, u32[]{:S(2)}) collective-permute-start(f32[2,128,128]{2,1,0:T(8,128)S(1)} %get-tuple-element.51), channel_id=1, source_target_pairs={{0,4},{4,8},{8,12},{12,16},{16,20},{20,24},{24,28},{1,5},{5,9},{9,... | collective-permute-start | bytes 393224 | tf_op jit(solution)/shard_map/ppermute | solution.py:31
  26.1 1.3 %collective-permute-start.5 = (f32[2,128,128]{2,1,0:T(8,128)S(1)}, f32[2,128,128]{2,1,0:T(8,128)S(1)}, u32[]{:S(2)}, u32[]{:S(2)}) collective-permute-start(f32[2,128,128]{2,1,0:T(8,128)S(1)} %get-tuple-element.52), channel_id=1, source_target_pairs={{4,0},{8,4},{12,8},{16,12},{20,16},{24,20},{28,24},{5,1},{9,5},{13... | collective-permute-start | bytes 393224 | tf_op jit(solution)/shard_map/ppermute | solution.py:32
  27.4 1.7 %collective-permute-start.7 = (bf16[272,128]{1,0:T(8,128)(2,1)S(1)}, bf16[272,128]{1,0:T(8,128)(2,1)S(1)}, u32[]{:S(2)}, u32[]{:S(2)}) collective-permute-start(bf16[272,128]{1,0:T(8,128)(2,1)S(1)} %copy-done.3), channel_id=1, source_target_pairs={{0,2},{1,3},{2,0},{3,1},{4,6},{5,7},{6,4},{7,5},{8,10},{9,11},{10,... | collective-permute-start | bytes 208904 | tf_op jit(solution)/shard_map/ppermute | solution.py:38
  29.1 0.4 collective-permute-start.8
  29.5 0.6 shard_map.141.refs_0_.refs_3_
  30.1 1.0 %collective-permute-done.4.refs_4_ = f32[2,128,128]{2,1,0:T(8,128)S(1)} collective-permute-done((f32[2,128,128]{2,1,0:T(8,128)S(1)}, f32[2,128,128]{2,1,0:T(8,128)S(1)}, u32[]{:S(2)}, u32[]{:S(2)}) %collective-permute-start.4) | collective-permute-done | bytes 131104 | tf_op jit(solution)/shard_map/ppermute | solution.py:31
  31.1 1.9 %collective-permute-done.5.refs_5_ = f32[2,128,128]{2,1,0:T(8,128)S(1)} collective-permute-done((f32[2,128,128]{2,1,0:T(8,128)S(1)}, f32[2,128,128]{2,1,0:T(8,128)S(1)}, u32[]{:S(2)}, u32[]{:S(2)}) %collective-permute-start.5) | collective-permute-done | bytes 131104 | tf_op jit(solution)/shard_map/ppermute | solution.py:32
  32.9 1.2 %shard_map.143 = (f32[2,128,128]{2,1,0:T(8,128)S(1)}, f32[2,128,128]{2,1,0:T(8,128)S(1)}, f32[2,128,128]{2,1,0:T(8,128)S(1)}, f32[2,128,128]{2,1,0:T(8,128)S(1)}, bf16[256,128]{1,0:T(8,128)(2,1)S(1)}) custom-call(f32[172,256]{1,0:T(8,128)S(1)} %shard_map.141.refs_0_.refs_3_, s32[23]{0:T(128)S(1)} %concatenate.3.refs_0_.refs_1_.refs_5_, ...), custom_call_target="tpu_custom_call" | custom-call | flops 201326592 | bytes 1769472 | tf_op jit(solution)/shard_map/pallas_call | solution.py:552
  34.3 0.5 collective-permute-start.9
  34.8 6.4 %collective-permute-start.13 = (f32[2,128,128]{2,1,0:T(8,128)S(1)}, f32[2,128,128]{2,1,0:T(8,128)S(1)}, u32[]{:S(2)}, u32[]{:S(2)}) collective-permute-start(f32[2,128,128]{2,1,0:T(8,128)S(1)} %get-tuple-element.61), channel_id=1, source_target_pairs={{0,28},{28,0},{1,29},{29,1},{2,30},{30,2},{3,31},{31,3}} | collective-permute-start | bytes 393224 | tf_op jit(solution)/shard_map/ppermute | solution.py:30
  41.2 1.3 %collective-permute-start.14 = (f32[2,128,128]{2,1,0:T(8,128)S(1)}, f32[2,128,128]{2,1,0:T(8,128)S(1)}, u32[]{:S(2)}, u32[]{:S(2)}) collective-permute-start(f32[2,128,128]{2,1,0:T(8,128)S(1)} %get-tuple-element.62), channel_id=1, source_target_pairs={{0,4},{4,8},{8,12},{12,16},{16,20},{20,24},{24,28},{1,5},{5,9},{9,... | collective-permute-start | bytes 393224 | tf_op jit(solution)/shard_map/ppermute | solution.py:31
  42.5 1.3 %collective-permute-start.15 = (f32[2,128,128]{2,1,0:T(8,128)S(1)}, f32[2,128,128]{2,1,0:T(8,128)S(1)}, u32[]{:S(2)}, u32[]{:S(2)}) collective-permute-start(f32[2,128,128]{2,1,0:T(8,128)S(1)} %get-tuple-element.63), channel_id=1, source_target_pairs={{4,0},{8,4},{12,8},{16,12},{20,16},{24,20},{28,24},{5,1},{9,5},{13... | collective-permute-start | bytes 393224 | tf_op jit(solution)/shard_map/ppermute | solution.py:32
  43.9 0.5 collective-permute-start.12
  44.4 0.7 collective-permute-done.10.refs_4_.refs_2_
  45.2 0.7 collective-permute-start.6
  45.9 0.6 shard_map.144.refs_5_
  46.5 0.6 shard_map.145.refs_0_.refs_2_
  47.2 0.4 shard_map.146.refs_1_.refs_6_
  47.6 1.9 %collective-permute-done.15.refs_9_ = f32[2,128,128]{2,1,0:T(8,128)S(1)} collective-permute-done((f32[2,128,128]{2,1,0:T(8,128)S(1)}, f32[2,128,128]{2,1,0:T(8,128)S(1)}, u32[]{:S(2)}, u32[]{:S(2)}) %collective-permute-start.15) | collective-permute-done | bytes 131104 | tf_op jit(solution)/shard_map/ppermute | solution.py:32
  49.5 1.2 %shard_map.147.refs_1_.refs_6_ = bf16[128,256]{1,0:T(8,128)(2,1)S(1)} custom-call(f32[172,256]{1,0:T(8,128)S(1)} %shard_map.145.refs_0_.refs_2_, s32[1,256]{1,0:T(1,128)S(1)} %shard_map.146.refs_1_.refs_6_, bf16[256,128]{1,0:T(8,128)(2,1)S(1)} %collective-permute-done.11.refs_2_.refs_3_, bf16[256,128]{1,0:T(8,128)(2,1)S(1)} %collective-permute-done.8.refs_1_.refs_3_, ...), custom_call_target="tpu_custom_call" | custom-call | flops 201326592 | bytes 196608 | tf_op jit(solution)/shard_map/pallas_call | solution.py:579
  50.8 0.8 shard_map.148.refs_8_.refs_0_
  51.6 0.8 collective-permute-start.17
  52.6 0.3 collective-permute-start.20
  52.9 1.3 %collective-permute-start.18 = (bf16[128,256]{1,0:T(8,128)(2,1)S(1)}, bf16[128,256]{1,0:T(8,128)(2,1)S(1)}, u32[]{:S(2)}, u32[]{:S(2)}) collective-permute-start(bf16[128,256]{1,0:T(8,128)(2,1)S(1)} %shard_map.147.refs_1_.refs_6_), channel_id=1, source_target_pairs={{0,2},{1,3},{2,0},{3,1},{4,6},{5,7},{6,4},{7,5},{8,10},{9,11},{10,... | collective-permute-start | bytes 196616 | tf_op jit(solution)/shard_map/ppermute | solution.py:38
  54.2 0.3 shard_map.149
  54.5 1.8 %shard_map.150.refs_0_ = f32[8,304,128]{2,1,0:T(8,128)S(1)} custom-call(bf16[272,128]{1,0:T(8,128)(2,1)S(1)} %copy-done.3, bf16[272,128]{1,0:T(8,128)(2,1)S(1)} %collective-permute-done.9.refs_2_.refs_1_, bf16[256,128]{1,0:T(8,128)(2,1)S(1)} %get-tuple-element.60.refs_2_, bf16[256,128]{1,0:T(8,128)(2,1)S(1)} %collective-permute-done.11.refs_2_.refs_3_, ...), custom_call_target="tpu_custom_call" | custom-call | flops 1000 | bytes 1000 | tf_op jit(solution)/shard_map/pallas_call | solution.py:604
  56.2 2.0 %collective-permute-done.18.refs_7_ = bf16[128,256]{1,0:T(8,128)(2,1)S(1)} collective-permute-done((bf16[128,256]{1,0:T(8,128)(2,1)S(1)}, bf16[128,256]{1,0:T(8,128)(2,1)S(1)}, u32[]{:S(2)}, u32[]{:S(2)}) %collective-permute-start.18) | collective-permute-done | bytes 65568 | tf_op jit(solution)/shard_map/ppermute | solution.py:38
  58.2 0.5 collective-permute-start.22
  58.7 0.9 collective-permute-done.22.refs_6_
  59.6 0.4 collective-permute-done.23.refs_8_
  60.0 1.9 %shard_map.152 = (f32[304,128]{1,0:T(8,128)S(1)}, f32[304,128]{1,0:T(8,128)S(1)}, f32[304,128]{1,0:T(8,128)S(1)}, f32[304,128]{1,0:T(8,128)S(1)}, bf16[304,128]{...) custom-call(f32[8,304,128]{2,1,0:T(8,128)S(1)} %shard_map.150.refs_0, ...), custom_call_target="tpu_custom_call" | custom-call | flops 771751936 | bytes 2801664 | tf_op jit(solution)/shard_map/pallas_call | solution.py:632
  61.8 1.4 %collective-permute-start.25 = (bf16[304,128]{1,0:T(8,128)(2,1)S(1)}, bf16[304,128]{1,0:T(8,128)(2,1)S(1)}, u32[]{:S(2)}, u32[]{:S(2)}) collective-permute-start(bf16[304,128]{1,0:T(8,128)(2,1)S(1)} %get-tuple-element.72), channel_id=1, source_target_pairs={{0,4},{4,0},{8,12},{12,8},{16,20},{20,16},{24,28},{28,24},{1,5},{5... | collective-permute-start | bytes 233480 | tf_op jit(solution)/shard_map/ppermute | solution.py:38
  63.2 0.7 collective-permute-start.24
  63.9 1.3 %collective-permute-start.27 = (bf16[304,128]{1,0:T(8,128)(2,1)S(1)}, bf16[304,128]{1,0:T(8,128)(2,1)S(1)}, u32[]{:S(2)}, u32[]{:S(2)}) collective-permute-start(bf16[304,128]{1,0:T(8,128)(2,1)S(1)} %get-tuple-element.74), channel_id=1, source_target_pairs={{0,4},{4,0},{8,12},{12,8},{16,20},{20,16},{24,28},{28,24},{1,5},{5... | collective-permute-start | bytes 233480 | tf_op jit(solution)/shard_map/ppermute | solution.py:38
  65.2 0.7 collective-permute-start.29
  66.0 1.0 %collective-permute-done.25 = bf16[304,128]{1,0:T(8,128)(2,1)S(1)} collective-permute-done((bf16[304,128]{1,0:T(8,128)(2,1)S(1)}, bf16[304,128]{1,0:T(8,128)(2,1)S(1)}, u32[]{:S(2)}, u32[]{:S(2)}) %collective-permute-start.25) | collective-permute-done | bytes 77856 | tf_op jit(solution)/shard_map/ppermute | solution.py:38
  67.0 0.9 collective-permute-start.26
  67.9 2.4 %collective-permute-done.27 = bf16[304,128]{1,0:T(8,128)(2,1)S(1)} collective-permute-done((bf16[304,128]{1,0:T(8,128)(2,1)S(1)}, bf16[304,128]{1,0:T(8,128)(2,1)S(1)}, u32[]{:S(2)}, u32[]{:S(2)}) %collective-permute-start.27) | collective-permute-done | bytes 77856 | tf_op jit(solution)/shard_map/ppermute | solution.py:38
  70.4 0.9 %collective-permute-done.29 = bf16[304,128]{1,0:T(8,128)(2,1)S(1)} collective-permute-done((bf16[304,128]{1,0:T(8,128)(2,1)S(1)}, bf16[304,128]{1,0:T(8,128)(2,1)S(1)}, u32[]{:S(2)}, u32[]{:S(2)}) %collective-permute-start.29) | collective-permute-done | bytes 77856 | tf_op jit(solution)/shard_map/ppermute | solution.py:38
  71.4 1.1 %collective-permute-start.30 = (bf16[304,128]{1,0:T(8,128)(2,1)S(1)}, bf16[304,128]{1,0:T(8,128)(2,1)S(1)}, u32[]{:S(2)}, u32[]{:S(2)}) collective-permute-start(bf16[304,128]{1,0:T(8,128)(2,1)S(1)} %add_convert_fusion), channel_id=1, source_target_pairs={{0,8},{4,12},{8,0},{12,4},{16,24},{20,28},{24,16},{28,20},{1,9},{5... | collective-permute-start | bytes 233480 | tf_op jit(solution)/shard_map/ppermute | solution.py:38
  72.4 0.9 collective-permute-done.26
  73.3 2.5 %collective-permute-done.28 = bf16[304,128]{1,0:T(8,128)(2,1)S(1)} collective-permute-done((bf16[304,128]{1,0:T(8,128)(2,1)S(1)}, bf16[304,128]{1,0:T(8,128)(2,1)S(1)}, u32[]{:S(2)}, u32[]{:S(2)}) %collective-permute-start.28) | collective-permute-done | bytes 77856 | tf_op jit(solution)/shard_map/ppermute | solution.py:38
  75.8 0.9 collective-permute-done.30
  76.9 1.7 %collective-permute-start.32 = (bf16[304,128]{1,0:T(8,128)(2,1)S(1)}, bf16[304,128]{1,0:T(8,128)(2,1)S(1)}, u32[]{:S(2)}, u32[]{:S(2)}) collective-permute-start(bf16[304,128]{1,0:T(8,128)(2,1)S(1)} %convert_add_fusion.refs_0_), channel_id=1, source_target_pairs={{0,16},{4,20},{8,24},{12,28},{16,0},{20,4},{24,8},{28,12},{1,17},{... | collective-permute-start | bytes 233480 | tf_op jit(solution)/shard_map/ppermute | solution.py:38
  78.6 2.6 %collective-permute-start.33 = (bf16[304,128]{1,0:T(8,128)(2,1)S(1)}, bf16[304,128]{1,0:T(8,128)(2,1)S(1)}, u32[]{:S(2)}, u32[]{:S(2)}) collective-permute-start(bf16[304,128]{1,0:T(8,128)(2,1)S(1)} %convert_add_fusion.refs_0_), channel_id=1, source_target_pairs={{0,24},{4,28},{8,16},{12,20},{16,8},{20,12},{24,0},{28,4},{1,25},{... | collective-permute-start | bytes 233480 | tf_op jit(solution)/shard_map/ppermute | solution.py:38
  81.2 1.3 %collective-permute-start.34 = (bf16[304,128]{1,0:T(8,128)(2,1)S(1)}, bf16[304,128]{1,0:T(8,128)(2,1)S(1)}, u32[]{:S(2)}, u32[]{:S(2)}) collective-permute-start(bf16[304,128]{1,0:T(8,128)(2,1)S(1)} %convert_add_fusion.refs_0_), channel_id=1, source_target_pairs={{0,4},{4,0},{8,12},{12,8},{16,20},{20,16},{24,28},{28,24},{1,5},{5... | collective-permute-start | bytes 233480 | tf_op jit(solution)/shard_map/ppermute | solution.py:38
  82.5 0.7 collective-permute-start.35
  83.2 2.3 %collective-permute-done.32.refs_2_ = bf16[304,128]{1,0:T(8,128)(2,1)S(1)} collective-permute-done((bf16[304,128]{1,0:T(8,128)(2,1)S(1)}, bf16[304,128]{1,0:T(8,128)(2,1)S(1)}, u32[]{:S(2)}, u32[]{:S(2)}) %collective-permute-start.32) | collective-permute-done | bytes 77856 | tf_op jit(solution)/shard_map/ppermute | solution.py:38
  85.5 2.0 %collective-permute-start.37 = (bf16[304,128]{1,0:T(8,128)(2,1)S(1)}, bf16[304,128]{1,0:T(8,128)(2,1)S(1)}, u32[]{:S(2)}, u32[]{:S(2)}) collective-permute-start(bf16[304,128]{1,0:T(8,128)(2,1)S(1)} %collective-permute-done.33.refs_3_), channel_id=1, source_target_pairs={{0,4},{4,0},{8,12},{12,8},{16,20},{20,16},{24,28},{28,24},{1,5},{5... | collective-permute-start | bytes 233480 | tf_op jit(solution)/shard_map/ppermute | solution.py:38
  87.6 0.8 shard_map.151
  88.4 1.1 %shard_map.153 = (f32[4,128,256]{2,1,0:T(8,128)}, f32[172,1024]{1,0:T(8,128)}) custom-call(bf16[304,128]{1,0:T(8,128)(2,1)S(1)} %convert_add_fusion.refs_0_, bf16[304,128]{1,0:T(8,128)(2,1)S(1)} %collective-permute-done.31.refs_1_, bf16[304,128]{1,0:T(8,128)(2,1)S(1)} %collective-permute-done.32.refs_2_, ...), custom_call_target="tpu_custom_call" | custom-call | flops 1000 | bytes 1000 | tf_op jit(solution)/shard_map/pallas_call | solution.py:433
  89.5 0.4 collective-permute-done.36.refs_2_
  89.9 0.8 collective-permute-done.37.refs_3_
  90.8 0.8 shard_map.154
  (57 shorter events, 1.4 us)
Async XLA Ops:
  0.6 16.6 %copy-start.6 = (s32[2]{0:T(128)S(1)}, s32[2]{0:T(128)}, u32[]{:S(2)}) copy-start(s32[2]{0:T(128)} %refs_0_.3) | copy-start | bytes 28
  0.6 16.6 %copy-start.7 = (s32[2]{0:T(128)S(1)}, s32[2]{0:T(128)}, u32[]{:S(2)}) copy-start(s32[2]{0:T(128)} %refs_1_.4) | copy-start | bytes 28
  0.7 16.6 %copy-start.8 = (s32[1,2]{1,0:T(1,128)S(1)}, s32[1,2]{1,0:T(1,128)}, u32[]{:S(2)}) copy-start(s32[1,2]{1,0:T(1,128)} %refs_2_.1) | copy-start | bytes 28
  0.7 16.6 %copy-start.9 = (s32[8]{0:T(128)S(1)}, s32[8]{0:T(128)}, u32[]{:S(2)}) copy-start(s32[8]{0:T(128)} %param.14) | copy-start | bytes 100
  0.7 16.6 %copy-start.10 = (s32[8]{0:T(128)S(1)}, s32[8]{0:T(128)}, u32[]{:S(2)}) copy-start(s32[8]{0:T(128)} %param.15) | copy-start | bytes 100
  2.5 14.9 %collective-permute-start = (f32[2,128,128]{2,1,0:T(8,128)}, f32[2,128,128]{2,1,0:T(8,128)S(1)}, u32[]{:S(2)}, u32[]{:S(2)}) collective-permute-start(f32[2,128,128]{2,1,0:T(8,128)} %get-tuple-element.45), channel_id=1, source_target_pairs={{0,28},{28,0},{1,29},{29,1},{2,30},{30,2},{3,31},{31,3}} | collective-permute-start | bytes 393224 | tf_op jit(solution)/shard_map/ppermute | solution.py:30
  10.4 7.2 %collective-permute-start.1 = (f32[2,128,128]{2,1,0:T(8,128)}, f32[2,128,128]{2,1,0:T(8,128)S(1)}, u32[]{:S(2)}, u32[]{:S(2)}) collective-permute-start(f32[2,128,128]{2,1,0:T(8,128)} %get-tuple-element.46), channel_id=1, source_target_pairs={{0,4},{4,8},{8,12},{12,16},{16,20},{20,24},{24,28},{1,5},{5,9},{9,... | collective-permute-start | bytes 393224 | tf_op jit(solution)/shard_map/ppermute | solution.py:31
  11.7 7.2 %collective-permute-start.2 = (f32[2,128,128]{2,1,0:T(8,128)}, f32[2,128,128]{2,1,0:T(8,128)}, u32[]{:S(2)}, u32[]{:S(2)}) collective-permute-start(f32[2,128,128]{2,1,0:T(8,128)} %get-tuple-element.47), channel_id=1, source_target_pairs={{4,0},{8,4},{12,8},{16,12},{20,16},{24,20},{28,24},{5,1},{9,5},{13... | collective-permute-start | bytes 393224 | tf_op jit(solution)/shard_map/ppermute | solution.py:32
  13.0 1.4 %copy-start.1 = (bf16[4096,172]{0,1:T(8,128)(2,1)S(1)}, bf16[4096,172]{0,1:T(8,128)(2,1)}, u32[]{:S(2)}) copy-start(bf16[4096,172]{0,1:T(8,128)(2,1)} %param.23) | copy-start | bytes 4227076
  14.4 1.0 %copy-start.2 = (f32[8,128,128]{2,1,0:T(8,128)S(1)}, f32[8,128,128]{2,1,0:T(8,128)}, u32[]{:S(2)}) copy-start(f32[8,128,128]{2,1,0:T(8,128)} %refs_1_.5) | copy-start | bytes 1572868
  15.4 0.9 copy-start.4
  16.3 11.1 %copy-start.3 = (bf16[272,128]{1,0:T(8,128)(2,1)S(1)}, bf16[272,128]{1,0:T(8,128)(2,1)}, u32[]{:S(2)}) copy-start(bf16[272,128]{1,0:T(8,128)(2,1)} %get-tuple-element.59.refs_1_.refs_0_) | copy-start | bytes 208900
  16.3 13.2 %copy-start = (bf16[4,128,1024]{2,1,0:T(8,128)(2,1)S(1)}, bf16[4,128,1024]{2,1,0:T(8,128)(2,1)}, u32[]{:S(2)}) copy-start(bf16[4,128,1024]{2,1,0:T(8,128)(2,1)} %refs_11_.1) | copy-start | bytes 3145732
  20.5 9.6 %collective-permute-start.3 = (f32[2,128,128]{2,1,0:T(8,128)S(1)}, f32[2,128,128]{2,1,0:T(8,128)S(1)}, u32[]{:S(2)}, u32[]{:S(2)}) collective-permute-start(f32[2,128,128]{2,1,0:T(8,128)S(1)} %get-tuple-element.50), channel_id=1, source_target_pairs={{0,28},{28,0},{1,29},{29,1},{2,30},{30,2},{3,31},{31,3}} | collective-permute-start | bytes 393224 | tf_op jit(solution)/shard_map/ppermute | solution.py:30
  24.8 6.3 %collective-permute-start.4 = (f32[2,128,128]{2,1,0:T(8,128)S(1)}, f32[2,128,128]{2,1,0:T(8,128)S(1)}, u32[]{:S(2)}, u32[]{:S(2)}) collective-permute-start(f32[2,128,128]{2,1,0:T(8,128)S(1)} %get-tuple-element.51), channel_id=1, source_target_pairs={{0,4},{4,8},{8,12},{12,16},{16,20},{20,24},{24,28},{1,5},{5,9},{9,... | collective-permute-start | bytes 393224 | tf_op jit(solution)/shard_map/ppermute | solution.py:31
  26.1 6.9 %collective-permute-start.5 = (f32[2,128,128]{2,1,0:T(8,128)S(1)}, f32[2,128,128]{2,1,0:T(8,128)S(1)}, u32[]{:S(2)}, u32[]{:S(2)}) collective-permute-start(f32[2,128,128]{2,1,0:T(8,128)S(1)} %get-tuple-element.52), channel_id=1, source_target_pairs={{4,0},{8,4},{12,8},{16,12},{20,16},{24,20},{28,24},{5,1},{9,5},{13... | collective-permute-start | bytes 393224 | tf_op jit(solution)/shard_map/ppermute | solution.py:32
  27.4 6.8 %collective-permute-start.7 = (bf16[272,128]{1,0:T(8,128)(2,1)S(1)}, bf16[272,128]{1,0:T(8,128)(2,1)S(1)}, u32[]{:S(2)}, u32[]{:S(2)}) collective-permute-start(bf16[272,128]{1,0:T(8,128)(2,1)S(1)} %copy-done.3), channel_id=1, source_target_pairs={{0,2},{1,3},{2,0},{3,1},{4,6},{5,7},{6,4},{7,5},{8,10},{9,11},{10,... | collective-permute-start | bytes 208904 | tf_op jit(solution)/shard_map/ppermute | solution.py:38
  29.1 5.1 %collective-permute-start.8 = (bf16[256,128]{1,0:T(8,128)(2,1)S(1)}, bf16[256,128]{1,0:T(8,128)(2,1)S(1)}, u32[]{:S(2)}, u32[]{:S(2)}) collective-permute-start(bf16[256,128]{1,0:T(8,128)(2,1)S(1)} %get-tuple-element.60.refs_2_), channel_id=1, source_target_pairs={{0,2},{1,3},{2,0},{3,1},{4,6},{5,7},{6,4},{7,5},{8,10},{9,11},{10,... | collective-permute-start | bytes 196616 | tf_op jit(solution)/shard_map/ppermute | solution.py:38
  34.2 9.6 %collective-permute-start.11 = (bf16[256,128]{1,0:T(8,128)(2,1)S(1)}, bf16[256,128]{1,0:T(8,128)(2,1)S(1)}, u32[]{:S(2)}, u32[]{:S(2)}) collective-permute-start(bf16[256,128]{1,0:T(8,128)(2,1)S(1)} %get-tuple-element.60.refs_2_), channel_id=1, source_target_pairs={{0,1},{1,0},{2,3},{3,2},{4,5},{5,4},{6,7},{7,6},{8,9},{9,8},{10,11... | collective-permute-start | bytes 196616 | tf_op jit(solution)/shard_map/ppermute | solution.py:38
  34.3 9.7 %collective-permute-start.9 = (bf16[272,128]{1,0:T(8,128)(2,1)S(1)}, bf16[272,128]{1,0:T(8,128)(2,1)S(1)}, u32[]{:S(2)}, u32[]{:S(2)}) collective-permute-start(bf16[272,128]{1,0:T(8,128)(2,1)S(1)} %copy-done.3), channel_id=1, source_target_pairs={{0,1},{1,0},{2,3},{3,2},{4,5},{5,4},{6,7},{7,6},{8,9},{9,8},{10,11... | collective-permute-start | bytes 208904 | tf_op jit(solution)/shard_map/ppermute | solution.py:38
  34.8 12.8 %collective-permute-start.13 = (f32[2,128,128]{2,1,0:T(8,128)S(1)}, f32[2,128,128]{2,1,0:T(8,128)S(1)}, u32[]{:S(2)}, u32[]{:S(2)}) collective-permute-start(f32[2,128,128]{2,1,0:T(8,128)S(1)} %get-tuple-element.61), channel_id=1, source_target_pairs={{0,28},{28,0},{1,29},{29,1},{2,30},{30,2},{3,31},{31,3}} | collective-permute-start | bytes 393224 | tf_op jit(solution)/shard_map/ppermute | solution.py:30
  41.2 6.4 %collective-permute-start.14 = (f32[2,128,128]{2,1,0:T(8,128)S(1)}, f32[2,128,128]{2,1,0:T(8,128)S(1)}, u32[]{:S(2)}, u32[]{:S(2)}) collective-permute-start(f32[2,128,128]{2,1,0:T(8,128)S(1)} %get-tuple-element.62), channel_id=1, source_target_pairs={{0,4},{4,8},{8,12},{12,16},{16,20},{20,24},{24,28},{1,5},{5,9},{9,... | collective-permute-start | bytes 393224 | tf_op jit(solution)/shard_map/ppermute | solution.py:31
  42.5 7.0 %collective-permute-start.15 = (f32[2,128,128]{2,1,0:T(8,128)S(1)}, f32[2,128,128]{2,1,0:T(8,128)S(1)}, u32[]{:S(2)}, u32[]{:S(2)}) collective-permute-start(f32[2,128,128]{2,1,0:T(8,128)S(1)} %get-tuple-element.63), channel_id=1, source_target_pairs={{4,0},{8,4},{12,8},{16,12},{20,16},{24,20},{28,24},{5,1},{9,5},{13... | collective-permute-start | bytes 393224 | tf_op jit(solution)/shard_map/ppermute | solution.py:32
  43.8 1.3 %collective-permute-start.10 = (bf16[272,128]{1,0:T(8,128)(2,1)S(1)}, bf16[272,128]{1,0:T(8,128)(2,1)S(1)}, u32[]{:S(2)}, u32[]{:S(2)}) collective-permute-start(bf16[272,128]{1,0:T(8,128)(2,1)S(1)} %collective-permute-done.7.refs_0_.refs_3_.refs_1_), channel_id=1, source_target_pairs={{0,1},{1,0},{2,3},{3,2},{4,5},{5,4},{6,7},{7,6},{8,9},{9,8},{10,11... | collective-permute-start | bytes 208904 | tf_op jit(solution)/shard_map/ppermute | solution.py:38
  43.9 3.6 %collective-permute-start.12 = (bf16[256,128]{1,0:T(8,128)(2,1)S(1)}, bf16[256,128]{1,0:T(8,128)(2,1)S(1)}, u32[]{:S(2)}, u32[]{:S(2)}) collective-permute-start(bf16[256,128]{1,0:T(8,128)(2,1)S(1)} %collective-permute-done.8.refs_1_.refs_3_), channel_id=1, source_target_pairs={{0,1},{1,0},{2,3},{3,2},{4,5},{5,4},{6,7},{7,6},{8,9},{9,8},{10,11... | collective-permute-start | bytes 196616 | tf_op jit(solution)/shard_map/ppermute | solution.py:38
  45.2 5.6 %collective-permute-start.6 = (bf16[256,128]{1,0:T(8,128)(2,1)S(1)}, bf16[256,128]{1,0:T(8,128)(2,1)S(1)}, u32[]{:S(2)}, u32[]{:S(2)}) collective-permute-start(bf16[256,128]{1,0:T(8,128)(2,1)S(1)} %get-tuple-element.53.refs_4_), channel_id=1, source_target_pairs={{0,2},{1,3},{2,0},{3,1},{4,6},{5,7},{6,4},{7,5},{8,10},{9,11},{10,... | collective-permute-start | bytes 196616 | tf_op jit(solution)/shard_map/ppermute | solution.py:38
  46.5 0.7 copy-start.5
  51.6 2.9 %collective-permute-start.16 = (bf16[192,256]{1,0:T(8,128)(2,1)S(1)}, bf16[192,256]{1,0:T(8,128)(2,1)S(1)}, u32[]{:S(2)}, u32[]{:S(2)}) collective-permute-start(bf16[192,256]{1,0:T(8,128)(2,1)S(1)} %shard_map.148.refs_8_.refs_0_), channel_id=1, source_target_pairs={{0,1},{1,0},{2,3},{3,2},{4,5},{5,4},{6,7},{7,6},{8,9},{9,8},{10,11... | collective-permute-start | bytes 294920 | tf_op jit(solution)/shard_map/ppermute | solution.py:38
  51.6 6.6 %collective-permute-start.17 = (bf16[192,256]{1,0:T(8,128)(2,1)S(1)}, bf16[192,256]{1,0:T(8,128)(2,1)S(1)}, u32[]{:S(2)}, u32[]{:S(2)}) collective-permute-start(bf16[192,256]{1,0:T(8,128)(2,1)S(1)} %shard_map.148.refs_8_.refs_0_), channel_id=1, source_target_pairs={{0,2},{1,3},{2,0},{3,1},{4,6},{5,7},{6,4},{7,5},{8,10},{9,11},{10,... | collective-permute-start | bytes 294920 | tf_op jit(solution)/shard_map/ppermute | solution.py:38
  52.4 2.1 %collective-permute-start.19 = (bf16[256,128]{1,0:T(8,128)(2,1)S(1)}, bf16[256,128]{1,0:T(8,128)(2,1)S(1)}, u32[]{:S(2)}, u32[]{:S(2)}) collective-permute-start(bf16[256,128]{1,0:T(8,128)(2,1)S(1)} %get-tuple-element.53.refs_4_), channel_id=1, source_target_pairs={{0,1},{1,0},{2,3},{3,2},{4,5},{5,4},{6,7},{7,6},{8,9},{9,8},{10,11... | collective-permute-start | bytes 196616 | tf_op jit(solution)/shard_map/ppermute | solution.py:38
  52.6 1.9 %collective-permute-start.20 = (bf16[128,256]{1,0:T(8,128)(2,1)S(1)}, bf16[128,256]{1,0:T(8,128)(2,1)S(1)}, u32[]{:S(2)}, u32[]{:S(2)}) collective-permute-start(bf16[128,256]{1,0:T(8,128)(2,1)S(1)} %shard_map.147.refs_1_.refs_6_), channel_id=1, source_target_pairs={{0,1},{1,0},{2,3},{3,2},{4,5},{5,4},{6,7},{7,6},{8,9},{9,8},{10,11... | collective-permute-start | bytes 196616 | tf_op jit(solution)/shard_map/ppermute | solution.py:38
  52.9 5.3 %collective-permute-start.18 = (bf16[128,256]{1,0:T(8,128)(2,1)S(1)}, bf16[128,256]{1,0:T(8,128)(2,1)S(1)}, u32[]{:S(2)}, u32[]{:S(2)}) collective-permute-start(bf16[128,256]{1,0:T(8,128)(2,1)S(1)} %shard_map.147.refs_1_.refs_6_), channel_id=1, source_target_pairs={{0,2},{1,3},{2,0},{3,1},{4,6},{5,7},{6,4},{7,5},{8,10},{9,11},{10,... | collective-permute-start | bytes 196616 | tf_op jit(solution)/shard_map/ppermute | solution.py:38
  58.2 1.8 %collective-permute-start.21 = (bf16[192,256]{1,0:T(8,128)(2,1)S(1)}, bf16[192,256]{1,0:T(8,128)(2,1)S(1)}, u32[]{:S(2)}, u32[]{:S(2)}) collective-permute-start(bf16[192,256]{1,0:T(8,128)(2,1)S(1)} %collective-permute-done.17.refs_2_.refs_9_), channel_id=1, source_target_pairs={{0,1},{1,0},{2,3},{3,2},{4,5},{5,4},{6,7},{7,6},{8,9},{9,8},{10,11... | collective-permute-start | bytes 294920 | tf_op jit(solution)/shard_map/ppermute | solution.py:38
  58.2 1.4 %collective-permute-start.22 = (bf16[256,128]{1,0:T(8,128)(2,1)S(1)}, bf16[256,128]{1,0:T(8,128)(2,1)S(1)}, u32[]{:S(2)}, u32[]{:S(2)}) collective-permute-start(bf16[256,128]{1,0:T(8,128)(2,1)S(1)} %collective-permute-done.6.refs_0_.refs_5_), channel_id=1, source_target_pairs={{0,1},{1,0},{2,3},{3,2},{4,5},{5,4},{6,7},{7,6},{8,9},{9,8},{10,11... | collective-permute-start | bytes 196616 | tf_op jit(solution)/shard_map/ppermute | solution.py:38
  58.7 1.3 %collective-permute-start.23 = (bf16[128,256]{1,0:T(8,128)(2,1)S(1)}, bf16[128,256]{1,0:T(8,128)(2,1)S(1)}, u32[]{:S(2)}, u32[]{:S(2)}) collective-permute-start(bf16[128,256]{1,0:T(8,128)(2,1)S(1)} %collective-permute-done.18.refs_7_), channel_id=1, source_target_pairs={{0,1},{1,0},{2,3},{3,2},{4,5},{5,4},{6,7},{7,6},{8,9},{9,8},{10,11... | collective-permute-start | bytes 196616 | tf_op jit(solution)/shard_map/ppermute | solution.py:38
  61.8 5.1 %collective-permute-start.25 = (bf16[304,128]{1,0:T(8,128)(2,1)S(1)}, bf16[304,128]{1,0:T(8,128)(2,1)S(1)}, u32[]{:S(2)}, u32[]{:S(2)}) collective-permute-start(bf16[304,128]{1,0:T(8,128)(2,1)S(1)} %get-tuple-element.72), channel_id=1, source_target_pairs={{0,4},{4,0},{8,12},{12,8},{16,20},{20,16},{24,28},{28,24},{1,5},{5... | collective-permute-start | bytes 233480 | tf_op jit(solution)/shard_map/ppermute | solution.py:38
  63.2 9.2 %collective-permute-start.24 = (bf16[304,128]{1,0:T(8,128)(2,1)S(1)}, bf16[304,128]{1,0:T(8,128)(2,1)S(1)}, u32[]{:S(2)}, u32[]{:S(2)}) collective-permute-start(bf16[304,128]{1,0:T(8,128)(2,1)S(1)} %get-tuple-element.70), channel_id=1, source_target_pairs={{0,4},{4,0},{8,12},{12,8},{16,20},{20,16},{24,28},{28,24},{1,5},{5... | collective-permute-start | bytes 233480 | tf_op jit(solution)/shard_map/ppermute | solution.py:38
  63.9 6.4 %collective-permute-start.27 = (bf16[304,128]{1,0:T(8,128)(2,1)S(1)}, bf16[304,128]{1,0:T(8,128)(2,1)S(1)}, u32[]{:S(2)}, u32[]{:S(2)}) collective-permute-start(bf16[304,128]{1,0:T(8,128)(2,1)S(1)} %get-tuple-element.74), channel_id=1, source_target_pairs={{0,4},{4,0},{8,12},{12,8},{16,20},{20,16},{24,28},{28,24},{1,5},{5... | collective-permute-start | bytes 233480 | tf_op jit(solution)/shard_map/ppermute | solution.py:38
  65.2 6.1 %collective-permute-start.29 = (bf16[304,128]{1,0:T(8,128)(2,1)S(1)}, bf16[304,128]{1,0:T(8,128)(2,1)S(1)}, u32[]{:S(2)}, u32[]{:S(2)}) collective-permute-start(bf16[304,128]{1,0:T(8,128)(2,1)S(1)} %get-tuple-element.76), channel_id=1, source_target_pairs={{0,4},{4,0},{8,12},{12,8},{16,20},{20,16},{24,28},{28,24},{1,5},{5... | collective-permute-start | bytes 233480 | tf_op jit(solution)/shard_map/ppermute | solution.py:38
  67.0 6.3 %collective-permute-start.26 = (bf16[304,128]{1,0:T(8,128)(2,1)S(1)}, bf16[304,128]{1,0:T(8,128)(2,1)S(1)}, u32[]{:S(2)}, u32[]{:S(2)}) collective-permute-start(bf16[304,128]{1,0:T(8,128)(2,1)S(1)} %add_convert_fusion.2), channel_id=1, source_target_pairs={{0,24},{4,28},{8,16},{12,20},{16,8},{20,12},{24,0},{28,4},{1,25},{... | collective-permute-start | bytes 233480 | tf_op jit(solution)/shard_map/ppermute | solution.py:38
  70.3 5.5 %collective-permute-start.28 = (bf16[304,128]{1,0:T(8,128)(2,1)S(1)}, bf16[304,128]{1,0:T(8,128)(2,1)S(1)}, u32[]{:S(2)}, u32[]{:S(2)}) collective-permute-start(bf16[304,128]{1,0:T(8,128)(2,1)S(1)} %add_convert_fusion.1), channel_id=1, source_target_pairs={{0,16},{4,20},{8,24},{12,28},{16,0},{20,4},{24,8},{28,12},{1,17},{... | collective-permute-start | bytes 233480 | tf_op jit(solution)/shard_map/ppermute | solution.py:38
  71.4 5.4 %collective-permute-start.30 = (bf16[304,128]{1,0:T(8,128)(2,1)S(1)}, bf16[304,128]{1,0:T(8,128)(2,1)S(1)}, u32[]{:S(2)}, u32[]{:S(2)}) collective-permute-start(bf16[304,128]{1,0:T(8,128)(2,1)S(1)} %add_convert_fusion), channel_id=1, source_target_pairs={{0,8},{4,12},{8,0},{12,4},{16,24},{20,28},{24,16},{28,20},{1,9},{5... | collective-permute-start | bytes 233480 | tf_op jit(solution)/shard_map/ppermute | solution.py:38
  76.8 5.8 %collective-permute-start.31 = (bf16[304,128]{1,0:T(8,128)(2,1)S(1)}, bf16[304,128]{1,0:T(8,128)(2,1)S(1)}, u32[]{:S(2)}, u32[]{:S(2)}) collective-permute-start(bf16[304,128]{1,0:T(8,128)(2,1)S(1)} %convert_add_fusion.refs_0_), channel_id=1, source_target_pairs={{0,8},{4,12},{8,0},{12,4},{16,24},{20,28},{24,16},{28,20},{1,9},{5... | collective-permute-start | bytes 233480 | tf_op jit(solution)/shard_map/ppermute | solution.py:38
  76.9 8.6 %collective-permute-start.32 = (bf16[304,128]{1,0:T(8,128)(2,1)S(1)}, bf16[304,128]{1,0:T(8,128)(2,1)S(1)}, u32[]{:S(2)}, u32[]{:S(2)}) collective-permute-start(bf16[304,128]{1,0:T(8,128)(2,1)S(1)} %convert_add_fusion.refs_0_), channel_id=1, source_target_pairs={{0,16},{4,20},{8,24},{12,28},{16,0},{20,4},{24,8},{28,12},{1,17},{... | collective-permute-start | bytes 233480 | tf_op jit(solution)/shard_map/ppermute | solution.py:38
  78.6 6.9 %collective-permute-start.33 = (bf16[304,128]{1,0:T(8,128)(2,1)S(1)}, bf16[304,128]{1,0:T(8,128)(2,1)S(1)}, u32[]{:S(2)}, u32[]{:S(2)}) collective-permute-start(bf16[304,128]{1,0:T(8,128)(2,1)S(1)} %convert_add_fusion.refs_0_), channel_id=1, source_target_pairs={{0,24},{4,28},{8,16},{12,20},{16,8},{20,12},{24,0},{28,4},{1,25},{... | collective-permute-start | bytes 233480 | tf_op jit(solution)/shard_map/ppermute | solution.py:38
  81.2 7.2 %collective-permute-start.34 = (bf16[304,128]{1,0:T(8,128)(2,1)S(1)}, bf16[304,128]{1,0:T(8,128)(2,1)S(1)}, u32[]{:S(2)}, u32[]{:S(2)}) collective-permute-start(bf16[304,128]{1,0:T(8,128)(2,1)S(1)} %convert_add_fusion.refs_0_), channel_id=1, source_target_pairs={{0,4},{4,0},{8,12},{12,8},{16,20},{20,16},{24,28},{28,24},{1,5},{5... | collective-permute-start | bytes 233480 | tf_op jit(solution)/shard_map/ppermute | solution.py:38
  82.5 5.9 %collective-permute-start.35 = (bf16[304,128]{1,0:T(8,128)(2,1)S(1)}, bf16[304,128]{1,0:T(8,128)(2,1)S(1)}, u32[]{:S(2)}, u32[]{:S(2)}) collective-permute-start(bf16[304,128]{1,0:T(8,128)(2,1)S(1)} %collective-permute-done.31.refs_1_), channel_id=1, source_target_pairs={{0,4},{4,0},{8,12},{12,8},{16,20},{20,16},{24,28},{28,24},{1,5},{5... | collective-permute-start | bytes 233480 | tf_op jit(solution)/shard_map/ppermute | solution.py:38
  85.5 4.4 %collective-permute-start.36 = (bf16[304,128]{1,0:T(8,128)(2,1)S(1)}, bf16[304,128]{1,0:T(8,128)(2,1)S(1)}, u32[]{:S(2)}, u32[]{:S(2)}) collective-permute-start(bf16[304,128]{1,0:T(8,128)(2,1)S(1)} %collective-permute-done.32.refs_2_), channel_id=1, source_target_pairs={{0,4},{4,0},{8,12},{12,8},{16,20},{20,16},{24,28},{28,24},{1,5},{5... | collective-permute-start | bytes 233480 | tf_op jit(solution)/shard_map/ppermute | solution.py:38
  85.5 5.2 %collective-permute-start.37 = (bf16[304,128]{1,0:T(8,128)(2,1)S(1)}, bf16[304,128]{1,0:T(8,128)(2,1)S(1)}, u32[]{:S(2)}, u32[]{:S(2)}) collective-permute-start(bf16[304,128]{1,0:T(8,128)(2,1)S(1)} %collective-permute-done.33.refs_3_), channel_id=1, source_target_pairs={{0,4},{4,0},{8,12},{12,8},{16,20},{20,16},{24,28},{28,24},{1,5},{5... | collective-permute-start | bytes 233480 | tf_op jit(solution)/shard_map/ppermute | solution.py:38

commit v14 on v11

--- a/solution.py
+++ b/solution.py
@@ -522,10 +522,9 @@
             after=[members[shuf // 2] for members in gathered[:2]] if hop == HOPS - 1 else [],
         )(current, w_branch, w_class_t, *before)
         if hop == 0:
-            first_logits = logits
             after = []
         else:
-            after = [first_logits]
+            after = [logits]
         if hop < HOPS - 1:
             current, to_left, to_right, *rows = call(
                 functools.partial(hop_kernel, plan),

time: 75.9 us -> 75.9 us (level)
  no operation moved by 1% of the time
where the time goes in v14:
time: 75.9 us; the launch traced here: 75.7 us
  starting transfers between devices  41.1 us (54%)
  Pallas kernels  15.1 us (20%)
  waiting for transfers between devices  14.3 us (19%)
  local copies, waits for them, and re-layouts  3.42 us (5%)
  between operations  1.66 us (2%)
    ppermute x29, starting transfers between devices, swapped(): return lax.ppermute(value, axis, pairs)  25.4 us
    ppermute x6, starting transfers between devices, passed_along(): return lax.ppermute(value, axis, pairs)  15.7 us
    ppermute x29, waiting for transfers between devices, swapped(): return lax.ppermute(value, axis, pairs)  12.2 us
    unnamed x22, local copies, waits for them, and re-layouts  3.34 us
    pallas_call x2, Pallas kernels, body(): call(functools.partial(hop_kernel, plan), [blocks_f32, slots_f32, slots_f...  2.38 us
    ppermute x6, waiting for transfers between devices, passed_along(): return lax.ppermute(value, axis, pairs)  2.04 us
    pallas_call x2, Pallas kernels, write_out(): pl.pallas_call(functools.partial(out_kernel, kept, distances), out_shape=...  1.93 us
    pallas_call x1, Pallas kernels, body(): call(functools.partial(late_kernel, kept, ahead, half), [one_f32] * half...  1.85 us
  transfers between devices with their start and end apart: 35, of which 16 were waited for; matrix products, arithmetic and copies ran while one was open for 0% of the time, Pallas kernels for 11%

profile of v14, /device:TPU:0, one launch (start us, length us, event | category | flops | bytes accessed | tf_op | source)
XLA Modules:
  0.0 75.7 jit_solution(13498614269934151727)
XLA Ops:
  0.7 1.7 %shard_map.139 = (f32[2,128,128]{2,1,0:T(8,128)}, f32[2,128,128]{2,1,0:T(8,128)}, f32[2,128,128]{2,1,0:T(8,128)}, bf16[272,128]{1,0:T(8,128)(2,1)}) custom-call(s32[2]{0:T(128)} %refs_0_.3, s32[2]{0:T(128)} %refs_1_.4, s32[1,2]{1,0:T(1,128)} %refs_2_.1, f32[2,128,128]{2,1,0:T(8,128)} %bitcast.8, s32[1,256]{1,0:T(1,128)} %bitcast.10), custom_call_target="tpu_custom_call" | custom-call | flops 1000 | bytes 1000 | tf_op jit(solution)/shard_map/pallas_call | solution.py:487
  2.4 3.0 %collective-permute-start = (f32[2,128,128]{2,1,0:T(8,128)}, f32[2,128,128]{2,1,0:T(8,128)S(1)}, u32[]{:S(2)}, u32[]{:S(2)}) collective-permute-start(f32[2,128,128]{2,1,0:T(8,128)} %get-tuple-element.37), channel_id=1, source_target_pairs={{0,4},{4,8},{8,12},{12,16},{16,20},{20,24},{24,28},{28,0},{1,5},{5... | collective-permute-start | bytes 393224 | tf_op jit(solution)/shard_map/ppermute | solution.py:30
  5.5 3.1 %collective-permute-start.1 = (f32[2,128,128]{2,1,0:T(8,128)}, f32[2,128,128]{2,1,0:T(8,128)S(1)}, u32[]{:S(2)}, u32[]{:S(2)}) collective-permute-start(f32[2,128,128]{2,1,0:T(8,128)} %get-tuple-element.38), channel_id=1, source_target_pairs={{0,28},{4,0},{8,4},{12,8},{16,12},{20,16},{24,20},{28,24},{1,29},{... | collective-permute-start | bytes 393224 | tf_op jit(solution)/shard_map/ppermute | solution.py:30
  8.6 1.4 %copy-done.1 = bf16[4096,172]{0,1:T(8,128)(2,1)S(1)} copy-done((bf16[4096,172]{0,1:T(8,128)(2,1)S(1)}, bf16[4096,172]{0,1:T(8,128)(2,1)}, u32[]{:S(2)}) %copy-start.1) | copy-done | bytes 1409048
  9.9 1.0 %copy-done.2 = f32[8,128,128]{2,1,0:T(8,128)S(1)} copy-done((f32[8,128,128]{2,1,0:T(8,128)S(1)}, f32[8,128,128]{2,1,0:T(8,128)}, u32[]{:S(2)}) %copy-start.2) | copy-done | bytes 524312
  11.0 0.9 %copy-done.4 = f32[2,128,128]{2,1,0:T(8,128)S(1)} copy-done((f32[2,128,128]{2,1,0:T(8,128)S(1)}, f32[2,128,128]{2,1,0:T(8,128)}, u32[]{:S(2)}) %copy-start.4) | copy-done | bytes 131096
  11.9 0.1 shard_map.140
  12.8 0.1 concatenate.3.refs_0_.refs_1_.refs_5_
  12.9 0.6 collective-permute-done.1.refs_3_
  13.4 1.2 %shard_map.141 = (f32[2,128,128]{2,1,0:T(8,128)S(1)}, f32[2,128,128]{2,1,0:T(8,128)S(1)}, f32[2,128,128]{2,1,0:T(8,128)S(1)}, bf16[256,128]{1,0:T(8,128)(2,1)S(1)}) custom-call(s32[23]{0:T(128)S(1)} %concatenate.3.refs_0_.refs_1_.refs_5_, f32[2,128,128]{2,1,0:T(8,128)S(1)} %get-tuple-element.36.refs_1_.refs_0_, ...), custom_call_target="tpu_custom_call" | custom-call | flops 201326592 | bytes 1376256 | tf_op jit(solution)/shard_map/pallas_call | solution.py:529
  14.6 0.3 collective-permute-start.2
  15.0 4.4 %collective-permute-start.3 = (f32[2,128,128]{2,1,0:T(8,128)S(1)}, f32[2,128,128]{2,1,0:T(8,128)S(1)}, u32[]{:S(2)}, u32[]{:S(2)}) collective-permute-start(f32[2,128,128]{2,1,0:T(8,128)S(1)} %get-tuple-element.43), channel_id=1, source_target_pairs={{0,28},{4,0},{8,4},{12,8},{16,12},{20,16},{24,20},{28,24},{1,29},{... | collective-permute-start | bytes 393224 | tf_op jit(solution)/shard_map/ppermute | solution.py:30
  19.4 1.5 %collective-permute-start.5 = (bf16[272,128]{1,0:T(8,128)(2,1)S(1)}, bf16[272,128]{1,0:T(8,128)(2,1)S(1)}, u32[]{:S(2)}, u32[]{:S(2)}) collective-permute-start(bf16[272,128]{1,0:T(8,128)(2,1)S(1)} %copy-done.3), channel_id=1, source_target_pairs={{0,2},{1,3},{2,0},{3,1},{4,6},{5,7},{6,4},{7,5},{8,10},{9,11},{10,... | collective-permute-start | bytes 208904 | tf_op jit(solution)/shard_map/ppermute | solution.py:35
  20.9 0.6 shard_map.142.refs_3_
  21.5 0.6 collective-permute-start.6
  22.1 0.6 shard_map.143.refs_0_.refs_5_
  22.7 0.9 %collective-permute-done.3.refs_4_ = f32[2,128,128]{2,1,0:T(8,128)S(1)} collective-permute-done((f32[2,128,128]{2,1,0:T(8,128)S(1)}, f32[2,128,128]{2,1,0:T(8,128)S(1)}, u32[]{:S(2)}, u32[]{:S(2)}) %collective-permute-start.3) | collective-permute-done | bytes 131104 | tf_op jit(solution)/shard_map/ppermute | solution.py:30
  23.6 1.2 %shard_map.144 = (f32[2,128,128]{2,1,0:T(8,128)S(1)}, f32[2,128,128]{2,1,0:T(8,128)S(1)}, f32[2,128,128]{2,1,0:T(8,128)S(1)}, bf16[256,128]{1,0:T(8,128)(2,1)S(1)}) custom-call(f32[172,256]{1,0:T(8,128)S(1)} %shard_map.143.refs_0_.refs_5_, s32[23]{0:T(128)S(1)} %concatenate.3.refs_0_.refs_1_.refs_5_, f32[2,128,128]{2,1,0:T(8,128)S(1)} %get-tuple-element.40.refs_0_.refs_2_, ...), custom_call_target="tpu_custom_call" | custom-call | flops 201326592 | bytes 1376256 | tf_op jit(solution)/shard_map/pallas_call | solution.py:529
  24.8 4.7 %collective-permute-start.12 = (f32[2,128,128]{2,1,0:T(8,128)S(1)}, f32[2,128,128]{2,1,0:T(8,128)S(1)}, u32[]{:S(2)}, u32[]{:S(2)}) collective-permute-start(f32[2,128,128]{2,1,0:T(8,128)S(1)} %get-tuple-element.49), channel_id=1, source_target_pairs={{0,28},{4,0},{8,4},{12,8},{16,12},{20,16},{24,20},{28,24},{1,29},{... | collective-permute-start | bytes 393224 | tf_op jit(solution)/shard_map/ppermute | solution.py:30
  29.6 0.5 collective-permute-start.9
  30.1 0.1 collective-permute-start.10
  30.2 0.7 collective-permute-done.8.refs_4_.refs_2_
  30.8 1.5 %collective-permute-start.4 = (bf16[256,128]{1,0:T(8,128)(2,1)S(1)}, bf16[256,128]{1,0:T(8,128)(2,1)S(1)}, u32[]{:S(2)}, u32[]{:S(2)}) collective-permute-start(bf16[256,128]{1,0:T(8,128)(2,1)S(1)} %get-tuple-element.44.refs_4_), channel_id=1, source_target_pairs={{0,2},{1,3},{2,0},{3,1},{4,6},{5,7},{6,4},{7,5},{8,10},{9,11},{10,... | collective-permute-start | bytes 196616 | tf_op jit(solution)/shard_map/ppermute | solution.py:35
  32.3 0.4 shard_map.146.refs_1_.refs_6_
  32.7 0.6 shard_map.145.refs_0_.refs_2_
  33.3 0.6 collective-permute-done.12.refs_8_
  34.0 1.2 %shard_map.147.refs_1_.refs_6_ = bf16[128,256]{1,0:T(8,128)(2,1)S(1)} custom-call(f32[172,256]{1,0:T(8,128)S(1)} %shard_map.145.refs_0_.refs_2_, s32[1,256]{1,0:T(1,128)S(1)} %shard_map.146.refs_1_.refs_6_, bf16[256,128]{1,0:T(8,128)(2,1)S(1)} %collective-permute-done.9.refs_2_.refs_3_, bf16[256,128]{1,0:T(8,128)(2,1)S(1)} %collective-permute-done.6.refs_1_.refs_3_, ...), custom_call_target="tpu_custom_call" | custom-call | flops 201326592 | bytes 196608 | tf_op jit(solution)/shard_map/pallas_call | solution.py:556
  35.2 0.8 %shard_map.148.refs_8_.refs_0_ = bf16[192,256]{1,0:T(8,128)(2,1)S(1)} custom-call(bf16[256,128]{1,0:T(8,128)(2,1)S(1)} %collective-permute-done.4.refs_0_.refs_5_, bf16[128,256]{1,0:T(8,128)(2,1)S(1)} %shard_map.147.refs_1_.refs_6_, f32[172,256]{1,0:T(8,128)S(1)} %shard_map.145.refs_0_.refs_2_, bf16[4,128,1024]{2,1,0:T(8,128)(2,1)S(1)} %copy-done, ...), custom_call_target="tpu_custom_call" | custom-call | flops 1000 | bytes 1000 | tf_op jit(solution)/shard_map/pallas_call | solution.py:564
  36.0 1.5 %collective-permute-start.14 = (bf16[192,256]{1,0:T(8,128)(2,1)S(1)}, bf16[192,256]{1,0:T(8,128)(2,1)S(1)}, u32[]{:S(2)}, u32[]{:S(2)}) collective-permute-start(bf16[192,256]{1,0:T(8,128)(2,1)S(1)} %shard_map.148.refs_8_.refs_0_), channel_id=1, source_target_pairs={{0,2},{1,3},{2,0},{3,1},{4,6},{5,7},{6,4},{7,5},{8,10},{9,11},{10,... | collective-permute-start | bytes 294920 | tf_op jit(solution)/shard_map/ppermute | solution.py:35
  37.5 0.2 collective-permute-start.16
  37.7 0.3 collective-permute-start.17
  38.0 0.5 collective-permute-start.15
  38.6 0.3 shard_map.149
  38.9 0.1 collective-permute-done.17.refs_7_
  39.0 1.7 %shard_map.150.refs_0_ = f32[8,304,128]{2,1,0:T(8,128)S(1)} custom-call(bf16[272,128]{1,0:T(8,128)(2,1)S(1)} %copy-done.3, bf16[272,128]{1,0:T(8,128)(2,1)S(1)} %collective-permute-done.7.refs_2_.refs_1_, bf16[256,128]{1,0:T(8,128)(2,1)S(1)} %get-tuple-element.46.refs_2_, bf16[256,128]{1,0:T(8,128)(2,1)S(1)} %collective-permute-done.9.refs_2_.refs_3_, ...), custom_call_target="tpu_custom_call" | custom-call | flops 1000 | bytes 1000 | tf_op jit(solution)/shard_map/pallas_call | solution.py:581
  40.7 1.9 %collective-permute-done.15.refs_7_ = bf16[128,256]{1,0:T(8,128)(2,1)S(1)} collective-permute-done((bf16[128,256]{1,0:T(8,128)(2,1)S(1)}, bf16[128,256]{1,0:T(8,128)(2,1)S(1)}, u32[]{:S(2)}, u32[]{:S(2)}) %collective-permute-start.15) | collective-permute-done | bytes 65568 | tf_op jit(solution)/shard_map/ppermute | solution.py:35
  42.6 0.5 collective-permute-start.19
  43.1 0.9 %collective-permute-done.19.refs_6_ = bf16[256,128]{1,0:T(8,128)(2,1)S(1)} collective-permute-done((bf16[256,128]{1,0:T(8,128)(2,1)S(1)}, bf16[256,128]{1,0:T(8,128)(2,1)S(1)}, u32[]{:S(2)}, u32[]{:S(2)}) %collective-permute-start.19) | collective-permute-done | bytes 65568 | tf_op jit(solution)/shard_map/ppermute | solution.py:35
  44.0 0.4 collective-permute-done.20.refs_8_
  44.4 1.9 %shard_map.152 = (f32[304,128]{1,0:T(8,128)S(1)}, f32[304,128]{1,0:T(8,128)S(1)}, f32[304,128]{1,0:T(8,128)S(1)}, f32[304,128]{1,0:T(8,128)S(1)}, bf16[304,128]{...) custom-call(f32[8,304,128]{2,1,0:T(8,128)S(1)} %shard_map.150.refs_0, ...), custom_call_target="tpu_custom_call" | custom-call | flops 771751936 | bytes 2801664 | tf_op jit(solution)/shard_map/pallas_call | solution.py:609
  46.3 0.1 collective-permute-start.22
  46.3 2.0 %collective-permute-start.21 = (bf16[304,128]{1,0:T(8,128)(2,1)S(1)}, bf16[304,128]{1,0:T(8,128)(2,1)S(1)}, u32[]{:S(2)}, u32[]{:S(2)}) collective-permute-start(bf16[304,128]{1,0:T(8,128)(2,1)S(1)} %get-tuple-element.56), channel_id=1, source_target_pairs={{0,4},{4,0},{8,12},{12,8},{16,20},{20,16},{24,28},{28,24},{1,5},{5... | collective-permute-start | bytes 233480 | tf_op jit(solution)/shard_map/ppermute | solution.py:35
  48.3 0.1 collective-permute-start.24
  48.4 1.9 %collective-permute-start.26 = (bf16[304,128]{1,0:T(8,128)(2,1)S(1)}, bf16[304,128]{1,0:T(8,128)(2,1)S(1)}, u32[]{:S(2)}, u32[]{:S(2)}) collective-permute-start(bf16[304,128]{1,0:T(8,128)(2,1)S(1)} %get-tuple-element.62), channel_id=1, source_target_pairs={{0,4},{4,0},{8,12},{12,8},{16,20},{20,16},{24,28},{28,24},{1,5},{5... | collective-permute-start | bytes 233480 | tf_op jit(solution)/shard_map/ppermute | solution.py:35
  50.4 1.1 %collective-permute-done.22 = bf16[304,128]{1,0:T(8,128)(2,1)S(1)} collective-permute-done((bf16[304,128]{1,0:T(8,128)(2,1)S(1)}, bf16[304,128]{1,0:T(8,128)(2,1)S(1)}, u32[]{:S(2)}, u32[]{:S(2)}) %collective-permute-start.22) | collective-permute-done | bytes 77856 | tf_op jit(solution)/shard_map/ppermute | solution.py:35
  51.5 1.6 %collective-permute-start.23 = (bf16[304,128]{1,0:T(8,128)(2,1)S(1)}, bf16[304,128]{1,0:T(8,128)(2,1)S(1)}, u32[]{:S(2)}, u32[]{:S(2)}) collective-permute-start(bf16[304,128]{1,0:T(8,128)(2,1)S(1)} %add_convert_fusion.2), channel_id=1, source_target_pairs={{0,24},{4,28},{8,16},{12,20},{16,8},{20,12},{24,0},{28,4},{1,25},{... | collective-permute-start | bytes 233480 | tf_op jit(solution)/shard_map/ppermute | solution.py:35
  53.1 1.7 %collective-permute-done.24 = bf16[304,128]{1,0:T(8,128)(2,1)S(1)} collective-permute-done((bf16[304,128]{1,0:T(8,128)(2,1)S(1)}, bf16[304,128]{1,0:T(8,128)(2,1)S(1)}, u32[]{:S(2)}, u32[]{:S(2)}) %collective-permute-start.24) | collective-permute-done | bytes 77856 | tf_op jit(solution)/shard_map/ppermute | solution.py:35
  54.9 1.7 %collective-permute-start.25 = (bf16[304,128]{1,0:T(8,128)(2,1)S(1)}, bf16[304,128]{1,0:T(8,128)(2,1)S(1)}, u32[]{:S(2)}, u32[]{:S(2)}) collective-permute-start(bf16[304,128]{1,0:T(8,128)(2,1)S(1)} %add_convert_fusion.1), channel_id=1, source_target_pairs={{0,16},{4,20},{8,24},{12,28},{16,0},{20,4},{24,8},{28,12},{1,17},{... | collective-permute-start | bytes 233480 | tf_op jit(solution)/shard_map/ppermute | solution.py:35
  56.6 1.1 %collective-permute-start.27 = (bf16[304,128]{1,0:T(8,128)(2,1)S(1)}, bf16[304,128]{1,0:T(8,128)(2,1)S(1)}, u32[]{:S(2)}, u32[]{:S(2)}) collective-permute-start(bf16[304,128]{1,0:T(8,128)(2,1)S(1)} %add_convert_fusion), channel_id=1, source_target_pairs={{0,8},{4,12},{8,0},{12,4},{16,24},{20,28},{24,16},{28,20},{1,9},{5... | collective-permute-start | bytes 233480 | tf_op jit(solution)/shard_map/ppermute | solution.py:35
  57.7 0.2 collective-permute-done.23
  57.9 2.4 %collective-permute-done.25 = bf16[304,128]{1,0:T(8,128)(2,1)S(1)} collective-permute-done((bf16[304,128]{1,0:T(8,128)(2,1)S(1)}, bf16[304,128]{1,0:T(8,128)(2,1)S(1)}, u32[]{:S(2)}, u32[]{:S(2)}) %collective-permute-start.25) | collective-permute-done | bytes 77856 | tf_op jit(solution)/shard_map/ppermute | solution.py:35
  60.3 0.8 %collective-permute-done.27 = bf16[304,128]{1,0:T(8,128)(2,1)S(1)} collective-permute-done((bf16[304,128]{1,0:T(8,128)(2,1)S(1)}, bf16[304,128]{1,0:T(8,128)(2,1)S(1)}, u32[]{:S(2)}, u32[]{:S(2)}) %collective-permute-start.27) | collective-permute-done | bytes 77856 | tf_op jit(solution)/shard_map/ppermute | solution.py:35
  61.2 1.1 %collective-permute-start.28 = (bf16[304,128]{1,0:T(8,128)(2,1)S(1)}, bf16[304,128]{1,0:T(8,128)(2,1)S(1)}, u32[]{:S(2)}, u32[]{:S(2)}) collective-permute-start(bf16[304,128]{1,0:T(8,128)(2,1)S(1)} %convert_add_fusion.refs_0_), channel_id=1, source_target_pairs={{0,8},{4,12},{8,0},{12,4},{16,24},{20,28},{24,16},{28,20},{1,9},{5... | collective-permute-start | bytes 233480 | tf_op jit(solution)/shard_map/ppermute | solution.py:35
  62.2 2.0 %collective-permute-start.29 = (bf16[304,128]{1,0:T(8,128)(2,1)S(1)}, bf16[304,128]{1,0:T(8,128)(2,1)S(1)}, u32[]{:S(2)}, u32[]{:S(2)}) collective-permute-start(bf16[304,128]{1,0:T(8,128)(2,1)S(1)} %convert_add_fusion.refs_0_), channel_id=1, source_target_pairs={{0,16},{4,20},{8,24},{12,28},{16,0},{20,4},{24,8},{28,12},{1,17},{... | collective-permute-start | bytes 233480 | tf_op jit(solution)/shard_map/ppermute | solution.py:35
  64.2 1.4 %collective-permute-start.30 = (bf16[304,128]{1,0:T(8,128)(2,1)S(1)}, bf16[304,128]{1,0:T(8,128)(2,1)S(1)}, u32[]{:S(2)}, u32[]{:S(2)}) collective-permute-start(bf16[304,128]{1,0:T(8,128)(2,1)S(1)} %convert_add_fusion.refs_0_), channel_id=1, source_target_pairs={{0,24},{4,28},{8,16},{12,20},{16,8},{20,12},{24,0},{28,4},{1,25},{... | collective-permute-start | bytes 233480 | tf_op jit(solution)/shard_map/ppermute | solution.py:35
  65.6 0.7 collective-permute-start.31
  66.4 1.3 %collective-permute-start.32 = (bf16[304,128]{1,0:T(8,128)(2,1)S(1)}, bf16[304,128]{1,0:T(8,128)(2,1)S(1)}, u32[]{:S(2)}, u32[]{:S(2)}) collective-permute-start(bf16[304,128]{1,0:T(8,128)(2,1)S(1)} %collective-permute-done.28.refs_1_), channel_id=1, source_target_pairs={{0,4},{4,0},{8,12},{12,8},{16,20},{20,16},{24,28},{28,24},{1,5},{5... | collective-permute-start | bytes 233480 | tf_op jit(solution)/shard_map/ppermute | solution.py:35
  67.7 1.0 %collective-permute-done.29.refs_2_ = bf16[304,128]{1,0:T(8,128)(2,1)S(1)} collective-permute-done((bf16[304,128]{1,0:T(8,128)(2,1)S(1)}, bf16[304,128]{1,0:T(8,128)(2,1)S(1)}, u32[]{:S(2)}, u32[]{:S(2)}) %collective-permute-start.29) | collective-permute-done | bytes 77856 | tf_op jit(solution)/shard_map/ppermute | solution.py:35
  68.6 1.8 %collective-permute-start.33 = (bf16[304,128]{1,0:T(8,128)(2,1)S(1)}, bf16[304,128]{1,0:T(8,128)(2,1)S(1)}, u32[]{:S(2)}, u32[]{:S(2)}) collective-permute-start(bf16[304,128]{1,0:T(8,128)(2,1)S(1)} %collective-permute-done.29.refs_2_), channel_id=1, source_target_pairs={{0,4},{4,0},{8,12},{12,8},{16,20},{20,16},{24,28},{28,24},{1,5},{5... | collective-permute-start | bytes 233480 | tf_op jit(solution)/shard_map/ppermute | solution.py:35
  70.4 1.5 %collective-permute-start.34 = (bf16[304,128]{1,0:T(8,128)(2,1)S(1)}, bf16[304,128]{1,0:T(8,128)(2,1)S(1)}, u32[]{:S(2)}, u32[]{:S(2)}) collective-permute-start(bf16[304,128]{1,0:T(8,128)(2,1)S(1)} %collective-permute-done.30.refs_3_), channel_id=1, source_target_pairs={{0,4},{4,0},{8,12},{12,8},{16,20},{20,16},{24,28},{28,24},{1,5},{5... | collective-permute-start | bytes 233480 | tf_op jit(solution)/shard_map/ppermute | solution.py:35
  71.9 0.8 %shard_map.151 = f32[1,256]{1,0:T(1,128)} custom-call(bf16[192,256]{1,0:T(8,128)(2,1)S(1)} %shard_map.148.refs_8_.refs_0_, bf16[192,256]{1,0:T(8,128)(2,1)S(1)} %collective-permute-done.13.refs_9_.refs_1_, bf16[192,256]{1,0:T(8,128)(2,1)S(1)} %collective-permute-done.14.refs_2_.refs_9_, bf16[192,256]{1,0:T(8,128)(2,1)S(1)} %collective-permute-done.18.refs_3_.refs_10_), custom_call_target="tpu_custom_call" | custom-call | flops 1000 | bytes 1000 | tf_op jit(solution)/shard_map/pallas_call | solution.py:598
  72.7 1.1 %shard_map.153 = (f32[4,128,256]{2,1,0:T(8,128)}, f32[172,1024]{1,0:T(8,128)}) custom-call(bf16[304,128]{1,0:T(8,128)(2,1)S(1)} %convert_add_fusion.refs_0_, bf16[304,128]{1,0:T(8,128)(2,1)S(1)} %collective-permute-done.28.refs_1_, bf16[304,128]{1,0:T(8,128)(2,1)S(1)} %collective-permute-done.29.refs_2_, ...), custom_call_target="tpu_custom_call" | custom-call | flops 1000 | bytes 1000 | tf_op jit(solution)/shard_map/pallas_call | solution.py:419
  73.9 1.0 %collective-permute-done.34.refs_3_ = bf16[304,128]{1,0:T(8,128)(2,1)S(1)} collective-permute-done((bf16[304,128]{1,0:T(8,128)(2,1)S(1)}, bf16[304,128]{1,0:T(8,128)(2,1)S(1)}, u32[]{:S(2)}, u32[]{:S(2)}) %collective-permute-start.34) | collective-permute-done | bytes 77856 | tf_op jit(solution)/shard_map/ppermute | solution.py:35
  74.8 0.8 %shard_map.154 = (f32[4,128,256]{2,1,0:T(8,128)}, f32[172,1024]{1,0:T(8,128)}) custom-call(f32[4,128,256]{2,1,0:T(8,128)} %get-tuple-element.63.refs_0_, f32[172,1024]{1,0:T(8,128)} %get-tuple-element.64.refs_1_, bf16[304,128]{1,0:T(8,128)(2,1)S(1)} %collective-permute-done.33.refs_2_, ...), custom_call_target="tpu_custom_call", output_to_operand_aliasing={{0}: (0, {}), {1}: (1, {})} | custom-call | flops 1000 | bytes 1000 | tf_op jit(solution)/shard_map/pallas_call | solution.py:419
  (51 shorter events, 0.3 us)
Async XLA Ops:
  0.6 12.1 %copy-start.6 = (s32[2]{0:T(128)S(1)}, s32[2]{0:T(128)}, u32[]{:S(2)}) copy-start(s32[2]{0:T(128)} %refs_0_.3) | copy-start | bytes 28
  0.6 12.1 %copy-start.7 = (s32[2]{0:T(128)S(1)}, s32[2]{0:T(128)}, u32[]{:S(2)}) copy-start(s32[2]{0:T(128)} %refs_1_.4) | copy-start | bytes 28
  0.7 12.1 %copy-start.8 = (s32[1,2]{1,0:T(1,128)S(1)}, s32[1,2]{1,0:T(1,128)}, u32[]{:S(2)}) copy-start(s32[1,2]{1,0:T(1,128)} %refs_2_.1) | copy-start | bytes 28
  0.7 12.1 %copy-start.9 = (s32[8]{0:T(128)S(1)}, s32[8]{0:T(128)}, u32[]{:S(2)}) copy-start(s32[8]{0:T(128)} %param.14) | copy-start | bytes 100
  0.7 12.1 %copy-start.10 = (s32[8]{0:T(128)S(1)}, s32[8]{0:T(128)}, u32[]{:S(2)}) copy-start(s32[8]{0:T(128)} %param.15) | copy-start | bytes 100
  2.4 10.4 %collective-permute-start = (f32[2,128,128]{2,1,0:T(8,128)}, f32[2,128,128]{2,1,0:T(8,128)S(1)}, u32[]{:S(2)}, u32[]{:S(2)}) collective-permute-start(f32[2,128,128]{2,1,0:T(8,128)} %get-tuple-element.37), channel_id=1, source_target_pairs={{0,4},{4,8},{8,12},{12,16},{16,20},{20,24},{24,28},{28,0},{1,5},{5... | collective-permute-start | bytes 393224 | tf_op jit(solution)/shard_map/ppermute | solution.py:30
  5.5 8.0 %collective-permute-start.1 = (f32[2,128,128]{2,1,0:T(8,128)}, f32[2,128,128]{2,1,0:T(8,128)S(1)}, u32[]{:S(2)}, u32[]{:S(2)}) collective-permute-start(f32[2,128,128]{2,1,0:T(8,128)} %get-tuple-element.38), channel_id=1, source_target_pairs={{0,28},{4,0},{8,4},{12,8},{16,12},{20,16},{24,20},{28,24},{1,29},{... | collective-permute-start | bytes 393224 | tf_op jit(solution)/shard_map/ppermute | solution.py:30
  8.6 1.4 %copy-start.1 = (bf16[4096,172]{0,1:T(8,128)(2,1)S(1)}, bf16[4096,172]{0,1:T(8,128)(2,1)}, u32[]{:S(2)}) copy-start(bf16[4096,172]{0,1:T(8,128)(2,1)} %param.23) | copy-start | bytes 4227076
  9.9 1.0 %copy-start.2 = (f32[8,128,128]{2,1,0:T(8,128)S(1)}, f32[8,128,128]{2,1,0:T(8,128)}, u32[]{:S(2)}) copy-start(f32[8,128,128]{2,1,0:T(8,128)} %refs_1_.5) | copy-start | bytes 1572868
  11.0 0.9 %copy-start.4 = (f32[2,128,128]{2,1,0:T(8,128)S(1)}, f32[2,128,128]{2,1,0:T(8,128)}, u32[]{:S(2)}) copy-start(f32[2,128,128]{2,1,0:T(8,128)} %get-tuple-element.35.refs_0_) | copy-start | bytes 393220
  11.9 7.5 %copy-start.3 = (bf16[272,128]{1,0:T(8,128)(2,1)S(1)}, bf16[272,128]{1,0:T(8,128)(2,1)}, u32[]{:S(2)}) copy-start(bf16[272,128]{1,0:T(8,128)(2,1)} %get-tuple-element.45.refs_1_.refs_0_) | copy-start | bytes 208900
  11.9 9.0 %copy-start = (bf16[4,128,1024]{2,1,0:T(8,128)(2,1)S(1)}, bf16[4,128,1024]{2,1,0:T(8,128)(2,1)}, u32[]{:S(2)}) copy-start(bf16[4,128,1024]{2,1,0:T(8,128)(2,1)} %refs_11_.1) | copy-start | bytes 3145732
  14.6 8.1 %collective-permute-start.2 = (f32[2,128,128]{2,1,0:T(8,128)S(1)}, f32[2,128,128]{2,1,0:T(8,128)S(1)}, u32[]{:S(2)}, u32[]{:S(2)}) collective-permute-start(f32[2,128,128]{2,1,0:T(8,128)S(1)} %get-tuple-element.42), channel_id=1, source_target_pairs={{0,4},{4,8},{8,12},{12,16},{16,20},{20,24},{24,28},{28,0},{1,5},{5... | collective-permute-start | bytes 393224 | tf_op jit(solution)/shard_map/ppermute | solution.py:30
  15.0 8.6 %collective-permute-start.3 = (f32[2,128,128]{2,1,0:T(8,128)S(1)}, f32[2,128,128]{2,1,0:T(8,128)S(1)}, u32[]{:S(2)}, u32[]{:S(2)}) collective-permute-start(f32[2,128,128]{2,1,0:T(8,128)S(1)} %get-tuple-element.43), channel_id=1, source_target_pairs={{0,28},{4,0},{8,4},{12,8},{16,12},{20,16},{24,20},{28,24},{1,29},{... | collective-permute-start | bytes 393224 | tf_op jit(solution)/shard_map/ppermute | solution.py:30
  19.4 10.1 %collective-permute-start.5 = (bf16[272,128]{1,0:T(8,128)(2,1)S(1)}, bf16[272,128]{1,0:T(8,128)(2,1)S(1)}, u32[]{:S(2)}, u32[]{:S(2)}) collective-permute-start(bf16[272,128]{1,0:T(8,128)(2,1)S(1)} %copy-done.3), channel_id=1, source_target_pairs={{0,2},{1,3},{2,0},{3,1},{4,6},{5,7},{6,4},{7,5},{8,10},{9,11},{10,... | collective-permute-start | bytes 208904 | tf_op jit(solution)/shard_map/ppermute | solution.py:35
  20.9 8.7 %collective-permute-start.7 = (bf16[272,128]{1,0:T(8,128)(2,1)S(1)}, bf16[272,128]{1,0:T(8,128)(2,1)S(1)}, u32[]{:S(2)}, u32[]{:S(2)}) collective-permute-start(bf16[272,128]{1,0:T(8,128)(2,1)S(1)} %copy-done.3), channel_id=1, source_target_pairs={{0,1},{1,0},{2,3},{3,2},{4,5},{5,4},{6,7},{7,6},{8,9},{9,8},{10,11... | collective-permute-start | bytes 208904 | tf_op jit(solution)/shard_map/ppermute | solution.py:35
  21.5 8.6 %collective-permute-start.6 = (bf16[256,128]{1,0:T(8,128)(2,1)S(1)}, bf16[256,128]{1,0:T(8,128)(2,1)S(1)}, u32[]{:S(2)}, u32[]{:S(2)}) collective-permute-start(bf16[256,128]{1,0:T(8,128)(2,1)S(1)} %get-tuple-element.46.refs_2_), channel_id=1, source_target_pairs={{0,2},{1,3},{2,0},{3,1},{4,6},{5,7},{6,4},{7,5},{8,10},{9,11},{10,... | collective-permute-start | bytes 196616 | tf_op jit(solution)/shard_map/ppermute | solution.py:35
  22.1 10.2 %copy-start.5 = (s32[1,256]{1,0:T(1,128)S(1)}, s32[1,256]{1,0:T(1,128)}, u32[]{:S(2)}) copy-start(s32[1,256]{1,0:T(1,128)} %refs_5_.1) | copy-start | bytes 3076
  24.8 8.6 %collective-permute-start.11 = (f32[2,128,128]{2,1,0:T(8,128)S(1)}, f32[2,128,128]{2,1,0:T(8,128)S(1)}, u32[]{:S(2)}, u32[]{:S(2)}) collective-permute-start(f32[2,128,128]{2,1,0:T(8,128)S(1)} %get-tuple-element.48), channel_id=1, source_target_pairs={{0,4},{4,8},{8,12},{12,16},{16,20},{20,24},{24,28},{28,0},{1,5},{5... | collective-permute-start | bytes 393224 | tf_op jit(solution)/shard_map/ppermute | solution.py:30
  24.8 9.1 %collective-permute-start.12 = (f32[2,128,128]{2,1,0:T(8,128)S(1)}, f32[2,128,128]{2,1,0:T(8,128)S(1)}, u32[]{:S(2)}, u32[]{:S(2)}) collective-permute-start(f32[2,128,128]{2,1,0:T(8,128)S(1)} %get-tuple-element.49), channel_id=1, source_target_pairs={{0,28},{4,0},{8,4},{12,8},{16,12},{20,16},{24,20},{28,24},{1,29},{... | collective-permute-start | bytes 393224 | tf_op jit(solution)/shard_map/ppermute | solution.py:30
  29.6 1.3 %collective-permute-start.8 = (bf16[272,128]{1,0:T(8,128)(2,1)S(1)}, bf16[272,128]{1,0:T(8,128)(2,1)S(1)}, u32[]{:S(2)}, u32[]{:S(2)}) collective-permute-start(bf16[272,128]{1,0:T(8,128)(2,1)S(1)} %collective-permute-done.5.refs_0_.refs_3_.refs_1_), channel_id=1, source_target_pairs={{0,1},{1,0},{2,3},{3,2},{4,5},{5,4},{6,7},{7,6},{8,9},{9,8},{10,11... | collective-permute-start | bytes 208904 | tf_op jit(solution)/shard_map/ppermute | solution.py:35
  29.6 3.7 %collective-permute-start.9 = (bf16[256,128]{1,0:T(8,128)(2,1)S(1)}, bf16[256,128]{1,0:T(8,128)(2,1)S(1)}, u32[]{:S(2)}, u32[]{:S(2)}) collective-permute-start(bf16[256,128]{1,0:T(8,128)(2,1)S(1)} %get-tuple-element.46.refs_2_), channel_id=1, source_target_pairs={{0,1},{1,0},{2,3},{3,2},{4,5},{5,4},{6,7},{7,6},{8,9},{9,8},{10,11... | collective-permute-start | bytes 196616 | tf_op jit(solution)/shard_map/ppermute | solution.py:35
  30.1 3.2 %collective-permute-start.10 = (bf16[256,128]{1,0:T(8,128)(2,1)S(1)}, bf16[256,128]{1,0:T(8,128)(2,1)S(1)}, u32[]{:S(2)}, u32[]{:S(2)}) collective-permute-start(bf16[256,128]{1,0:T(8,128)(2,1)S(1)} %collective-permute-done.6.refs_1_.refs_3_), channel_id=1, source_target_pairs={{0,1},{1,0},{2,3},{3,2},{4,5},{5,4},{6,7},{7,6},{8,9},{9,8},{10,11... | collective-permute-start | bytes 196616 | tf_op jit(solution)/shard_map/ppermute | solution.py:35
  30.8 4.3 %collective-permute-start.4 = (bf16[256,128]{1,0:T(8,128)(2,1)S(1)}, bf16[256,128]{1,0:T(8,128)(2,1)S(1)}, u32[]{:S(2)}, u32[]{:S(2)}) collective-permute-start(bf16[256,128]{1,0:T(8,128)(2,1)S(1)} %get-tuple-element.44.refs_4_), channel_id=1, source_target_pairs={{0,2},{1,3},{2,0},{3,1},{4,6},{5,7},{6,4},{7,5},{8,10},{9,11},{10,... | collective-permute-start | bytes 196616 | tf_op jit(solution)/shard_map/ppermute | solution.py:35
  36.0 3.0 %collective-permute-start.13 = (bf16[192,256]{1,0:T(8,128)(2,1)S(1)}, bf16[192,256]{1,0:T(8,128)(2,1)S(1)}, u32[]{:S(2)}, u32[]{:S(2)}) collective-permute-start(bf16[192,256]{1,0:T(8,128)(2,1)S(1)} %shard_map.148.refs_8_.refs_0_), channel_id=1, source_target_pairs={{0,1},{1,0},{2,3},{3,2},{4,5},{5,4},{6,7},{7,6},{8,9},{9,8},{10,11... | collective-permute-start | bytes 294920 | tf_op jit(solution)/shard_map/ppermute | solution.py:35
  36.0 6.6 %collective-permute-start.14 = (bf16[192,256]{1,0:T(8,128)(2,1)S(1)}, bf16[192,256]{1,0:T(8,128)(2,1)S(1)}, u32[]{:S(2)}, u32[]{:S(2)}) collective-permute-start(bf16[192,256]{1,0:T(8,128)(2,1)S(1)} %shard_map.148.refs_8_.refs_0_), channel_id=1, source_target_pairs={{0,2},{1,3},{2,0},{3,1},{4,6},{5,7},{6,4},{7,5},{8,10},{9,11},{10,... | collective-permute-start | bytes 294920 | tf_op jit(solution)/shard_map/ppermute | solution.py:35
  37.5 1.3 %collective-permute-start.16 = (bf16[256,128]{1,0:T(8,128)(2,1)S(1)}, bf16[256,128]{1,0:T(8,128)(2,1)S(1)}, u32[]{:S(2)}, u32[]{:S(2)}) collective-permute-start(bf16[256,128]{1,0:T(8,128)(2,1)S(1)} %get-tuple-element.44.refs_4_), channel_id=1, source_target_pairs={{0,1},{1,0},{2,3},{3,2},{4,5},{5,4},{6,7},{7,6},{8,9},{9,8},{10,11... | collective-permute-start | bytes 196616 | tf_op jit(solution)/shard_map/ppermute | solution.py:35
  37.7 1.3 %collective-permute-start.17 = (bf16[128,256]{1,0:T(8,128)(2,1)S(1)}, bf16[128,256]{1,0:T(8,128)(2,1)S(1)}, u32[]{:S(2)}, u32[]{:S(2)}) collective-permute-start(bf16[128,256]{1,0:T(8,128)(2,1)S(1)} %shard_map.147.refs_1_.refs_6_), channel_id=1, source_target_pairs={{0,1},{1,0},{2,3},{3,2},{4,5},{5,4},{6,7},{7,6},{8,9},{9,8},{10,11... | collective-permute-start | bytes 196616 | tf_op jit(solution)/shard_map/ppermute | solution.py:35
  38.0 4.6 %collective-permute-start.15 = (bf16[128,256]{1,0:T(8,128)(2,1)S(1)}, bf16[128,256]{1,0:T(8,128)(2,1)S(1)}, u32[]{:S(2)}, u32[]{:S(2)}) collective-permute-start(bf16[128,256]{1,0:T(8,128)(2,1)S(1)} %shard_map.147.refs_1_.refs_6_), channel_id=1, source_target_pairs={{0,2},{1,3},{2,0},{3,1},{4,6},{5,7},{6,4},{7,5},{8,10},{9,11},{10,... | collective-permute-start | bytes 196616 | tf_op jit(solution)/shard_map/ppermute | solution.py:35
  42.6 1.8 %collective-permute-start.18 = (bf16[192,256]{1,0:T(8,128)(2,1)S(1)}, bf16[192,256]{1,0:T(8,128)(2,1)S(1)}, u32[]{:S(2)}, u32[]{:S(2)}) collective-permute-start(bf16[192,256]{1,0:T(8,128)(2,1)S(1)} %collective-permute-done.14.refs_2_.refs_9_), channel_id=1, source_target_pairs={{0,1},{1,0},{2,3},{3,2},{4,5},{5,4},{6,7},{7,6},{8,9},{9,8},{10,11... | collective-permute-start | bytes 294920 | tf_op jit(solution)/shard_map/ppermute | solution.py:35
  42.6 1.4 %collective-permute-start.19 = (bf16[256,128]{1,0:T(8,128)(2,1)S(1)}, bf16[256,128]{1,0:T(8,128)(2,1)S(1)}, u32[]{:S(2)}, u32[]{:S(2)}) collective-permute-start(bf16[256,128]{1,0:T(8,128)(2,1)S(1)} %collective-permute-done.4.refs_0_.refs_5_), channel_id=1, source_target_pairs={{0,1},{1,0},{2,3},{3,2},{4,5},{5,4},{6,7},{7,6},{8,9},{9,8},{10,11... | collective-permute-start | bytes 196616 | tf_op jit(solution)/shard_map/ppermute | solution.py:35
  43.1 1.3 %collective-permute-start.20 = (bf16[128,256]{1,0:T(8,128)(2,1)S(1)}, bf16[128,256]{1,0:T(8,128)(2,1)S(1)}, u32[]{:S(2)}, u32[]{:S(2)}) collective-permute-start(bf16[128,256]{1,0:T(8,128)(2,1)S(1)} %collective-permute-done.15.refs_7_), channel_id=1, source_target_pairs={{0,1},{1,0},{2,3},{3,2},{4,5},{5,4},{6,7},{7,6},{8,9},{9,8},{10,11... | collective-permute-start | bytes 196616 | tf_op jit(solution)/shard_map/ppermute | solution.py:35
  46.3 5.3 %collective-permute-start.22 = (bf16[304,128]{1,0:T(8,128)(2,1)S(1)}, bf16[304,128]{1,0:T(8,128)(2,1)S(1)}, u32[]{:S(2)}, u32[]{:S(2)}) collective-permute-start(bf16[304,128]{1,0:T(8,128)(2,1)S(1)} %get-tuple-element.58), channel_id=1, source_target_pairs={{0,4},{4,0},{8,12},{12,8},{16,20},{20,16},{24,28},{28,24},{1,5},{5... | collective-permute-start | bytes 233480 | tf_op jit(solution)/shard_map/ppermute | solution.py:35
  46.3 11.4 %collective-permute-start.21 = (bf16[304,128]{1,0:T(8,128)(2,1)S(1)}, bf16[304,128]{1,0:T(8,128)(2,1)S(1)}, u32[]{:S(2)}, u32[]{:S(2)}) collective-permute-start(bf16[304,128]{1,0:T(8,128)(2,1)S(1)} %get-tuple-element.56), channel_id=1, source_target_pairs={{0,4},{4,0},{8,12},{12,8},{16,20},{20,16},{24,28},{28,24},{1,5},{5... | collective-permute-start | bytes 233480 | tf_op jit(solution)/shard_map/ppermute | solution.py:35
  48.3 6.5 %collective-permute-start.24 = (bf16[304,128]{1,0:T(8,128)(2,1)S(1)}, bf16[304,128]{1,0:T(8,128)(2,1)S(1)}, u32[]{:S(2)}, u32[]{:S(2)}) collective-permute-start(bf16[304,128]{1,0:T(8,128)(2,1)S(1)} %get-tuple-element.60), channel_id=1, source_target_pairs={{0,4},{4,0},{8,12},{12,8},{16,20},{20,16},{24,28},{28,24},{1,5},{5... | collective-permute-start | bytes 233480 | tf_op jit(solution)/shard_map/ppermute | solution.py:35
  48.4 8.2 %collective-permute-start.26 = (bf16[304,128]{1,0:T(8,128)(2,1)S(1)}, bf16[304,128]{1,0:T(8,128)(2,1)S(1)}, u32[]{:S(2)}, u32[]{:S(2)}) collective-permute-start(bf16[304,128]{1,0:T(8,128)(2,1)S(1)} %get-tuple-element.62), channel_id=1, source_target_pairs={{0,4},{4,0},{8,12},{12,8},{16,20},{20,16},{24,28},{28,24},{1,5},{5... | collective-permute-start | bytes 233480 | tf_op jit(solution)/shard_map/ppermute | solution.py:35
  51.5 6.4 %collective-permute-start.23 = (bf16[304,128]{1,0:T(8,128)(2,1)S(1)}, bf16[304,128]{1,0:T(8,128)(2,1)S(1)}, u32[]{:S(2)}, u32[]{:S(2)}) collective-permute-start(bf16[304,128]{1,0:T(8,128)(2,1)S(1)} %add_convert_fusion.2), channel_id=1, source_target_pairs={{0,24},{4,28},{8,16},{12,20},{16,8},{20,12},{24,0},{28,4},{1,25},{... | collective-permute-start | bytes 233480 | tf_op jit(solution)/shard_map/ppermute | solution.py:35
  54.9 5.4 %collective-permute-start.25 = (bf16[304,128]{1,0:T(8,128)(2,1)S(1)}, bf16[304,128]{1,0:T(8,128)(2,1)S(1)}, u32[]{:S(2)}, u32[]{:S(2)}) collective-permute-start(bf16[304,128]{1,0:T(8,128)(2,1)S(1)} %add_convert_fusion.1), channel_id=1, source_target_pairs={{0,16},{4,20},{8,24},{12,28},{16,0},{20,4},{24,8},{28,12},{1,17},{... | collective-permute-start | bytes 233480 | tf_op jit(solution)/shard_map/ppermute | solution.py:35
  56.6 4.5 %collective-permute-start.27 = (bf16[304,128]{1,0:T(8,128)(2,1)S(1)}, bf16[304,128]{1,0:T(8,128)(2,1)S(1)}, u32[]{:S(2)}, u32[]{:S(2)}) collective-permute-start(bf16[304,128]{1,0:T(8,128)(2,1)S(1)} %add_convert_fusion), channel_id=1, source_target_pairs={{0,8},{4,12},{8,0},{12,4},{16,24},{20,28},{24,16},{28,20},{1,9},{5... | collective-permute-start | bytes 233480 | tf_op jit(solution)/shard_map/ppermute | solution.py:35
  61.2 5.2 %collective-permute-start.28 = (bf16[304,128]{1,0:T(8,128)(2,1)S(1)}, bf16[304,128]{1,0:T(8,128)(2,1)S(1)}, u32[]{:S(2)}, u32[]{:S(2)}) collective-permute-start(bf16[304,128]{1,0:T(8,128)(2,1)S(1)} %convert_add_fusion.refs_0_), channel_id=1, source_target_pairs={{0,8},{4,12},{8,0},{12,4},{16,24},{20,28},{24,16},{28,20},{1,9},{5... | collective-permute-start | bytes 233480 | tf_op jit(solution)/shard_map/ppermute | solution.py:35
  62.2 6.4 %collective-permute-start.29 = (bf16[304,128]{1,0:T(8,128)(2,1)S(1)}, bf16[304,128]{1,0:T(8,128)(2,1)S(1)}, u32[]{:S(2)}, u32[]{:S(2)}) collective-permute-start(bf16[304,128]{1,0:T(8,128)(2,1)S(1)} %convert_add_fusion.refs_0_), channel_id=1, source_target_pairs={{0,16},{4,20},{8,24},{12,28},{16,0},{20,4},{24,8},{28,12},{1,17},{... | collective-permute-start | bytes 233480 | tf_op jit(solution)/shard_map/ppermute | solution.py:35
  64.2 6.2 %collective-permute-start.30 = (bf16[304,128]{1,0:T(8,128)(2,1)S(1)}, bf16[304,128]{1,0:T(8,128)(2,1)S(1)}, u32[]{:S(2)}, u32[]{:S(2)}) collective-permute-start(bf16[304,128]{1,0:T(8,128)(2,1)S(1)} %convert_add_fusion.refs_0_), channel_id=1, source_target_pairs={{0,24},{4,28},{8,16},{12,20},{16,8},{20,12},{24,0},{28,4},{1,25},{... | collective-permute-start | bytes 233480 | tf_op jit(solution)/shard_map/ppermute | solution.py:35
  65.6 7.1 %collective-permute-start.31 = (bf16[304,128]{1,0:T(8,128)(2,1)S(1)}, bf16[304,128]{1,0:T(8,128)(2,1)S(1)}, u32[]{:S(2)}, u32[]{:S(2)}) collective-permute-start(bf16[304,128]{1,0:T(8,128)(2,1)S(1)} %convert_add_fusion.refs_0_), channel_id=1, source_target_pairs={{0,4},{4,0},{8,12},{12,8},{16,20},{20,16},{24,28},{28,24},{1,5},{5... | collective-permute-start | bytes 233480 | tf_op jit(solution)/shard_map/ppermute | solution.py:35
  66.4 6.4 %collective-permute-start.32 = (bf16[304,128]{1,0:T(8,128)(2,1)S(1)}, bf16[304,128]{1,0:T(8,128)(2,1)S(1)}, u32[]{:S(2)}, u32[]{:S(2)}) collective-permute-start(bf16[304,128]{1,0:T(8,128)(2,1)S(1)} %collective-permute-done.28.refs_1_), channel_id=1, source_target_pairs={{0,4},{4,0},{8,12},{12,8},{16,20},{20,16},{24,28},{28,24},{1,5},{5... | collective-permute-start | bytes 233480 | tf_op jit(solution)/shard_map/ppermute | solution.py:35
  68.6 5.2 %collective-permute-start.33 = (bf16[304,128]{1,0:T(8,128)(2,1)S(1)}, bf16[304,128]{1,0:T(8,128)(2,1)S(1)}, u32[]{:S(2)}, u32[]{:S(2)}) collective-permute-start(bf16[304,128]{1,0:T(8,128)(2,1)S(1)} %collective-permute-done.29.refs_2_), channel_id=1, source_target_pairs={{0,4},{4,0},{8,12},{12,8},{16,20},{20,16},{24,28},{28,24},{1,5},{5... | collective-permute-start | bytes 233480 | tf_op jit(solution)/shard_map/ppermute | solution.py:35
  70.4 4.4 %collective-permute-start.34 = (bf16[304,128]{1,0:T(8,128)(2,1)S(1)}, bf16[304,128]{1,0:T(8,128)(2,1)S(1)}, u32[]{:S(2)}, u32[]{:S(2)}) collective-permute-start(bf16[304,128]{1,0:T(8,128)(2,1)S(1)} %collective-permute-done.30.refs_3_), channel_id=1, source_target_pairs={{0,4},{4,0},{8,12},{12,8},{16,20},{20,16},{24,28},{28,24},{1,5},{5... | collective-permute-start | bytes 233480 | tf_op jit(solution)/shard_map/ppermute | solution.py:35

commit v15 on v11

--- a/solution.py
+++ b/solution.py
@@ -626,7 +626,7 @@
         other = [swapped(value, 1) for value in near]
         results = []
         places = [2 * step for step in range(half)] + [2 * step + 1 for step in range(half)]
-        for part in (slice(0, -half // 2), slice(-half // 2, None)):
+        for part in (slice(0, -2), slice(-2, -1), slice(-1, None)):
             results = write_out(kept, places[part], (near + other)[part], outs, results)
         grad_branch, grad_class_t = results
     else:

time: 75.9 us -> 75.8 us (level)
    pallas_call x2 -> x3, Pallas kernels: 1.93 us -> 2.6 us  [write_out(): pl.pallas_call(functools.partial(out_kernel, kept, distances), out_shape=...]
  transfers between devices with their start and end apart: 35 -> 35, of which waited for: 16 -> 16; matrix products, arithmetic and copies ran while one was open for 0% -> 0% of each run, Pallas kernels for 11% -> 12%
where the time goes in v15:
time: 75.8 us; the launch traced here: 75.6 us
  starting transfers between devices  41.1 us (54%)
  Pallas kernels  15.7 us (21%)
  waiting for transfers between devices  13.5 us (18%)
  local copies, waits for them, and re-layouts  3.42 us (5%)
  between operations  1.67 us (2%)
    ppermute x29, starting transfers between devices, swapped(): return lax.ppermute(value, axis, pairs)  25.4 us
    ppermute x6, starting transfers between devices, passed_along(): return lax.ppermute(value, axis, pairs)  15.7 us
    ppermute x29, waiting for transfers between devices, swapped(): return lax.ppermute(value, axis, pairs)  11.4 us
    unnamed x22, local copies, waits for them, and re-layouts  3.34 us
    pallas_call x3, Pallas kernels, write_out(): pl.pallas_call(functools.partial(out_kernel, kept, distances), out_shape=...  2.6 us
    pallas_call x2, Pallas kernels, body(): call(functools.partial(hop_kernel, plan), [blocks_f32, slots_f32, slots_f...  2.37 us
    ppermute x6, waiting for transfers between devices, passed_along(): return lax.ppermute(value, axis, pairs)  2.07 us
    pallas_call x1, Pallas kernels, body(): call(functools.partial(late_kernel, kept, ahead, half), [one_f32] * half...  1.86 us
  transfers between devices with their start and end apart: 35, of which 16 were waited for; matrix products, arithmetic and copies ran while one was open for 0% of the time, Pallas kernels for 12%

profile of v15, /device:TPU:0, one launch (start us, length us, event | category | flops | bytes accessed | tf_op | source)
XLA Modules:
  0.0 75.6 jit_solution(16837944459354223378)
XLA Ops:
  0.7 1.7 %shard_map.139 = (f32[2,128,128]{2,1,0:T(8,128)}, f32[2,128,128]{2,1,0:T(8,128)}, f32[2,128,128]{2,1,0:T(8,128)}, bf16[272,128]{1,0:T(8,128)(2,1)}) custom-call(s32[2]{0:T(128)} %refs_0_.3, s32[2]{0:T(128)} %refs_1_.4, s32[1,2]{1,0:T(1,128)} %refs_2_.1, f32[2,128,128]{2,1,0:T(8,128)} %bitcast.8, s32[1,256]{1,0:T(1,128)} %bitcast.10), custom_call_target="tpu_custom_call" | custom-call | flops 1000 | bytes 1000 | tf_op jit(solution)/shard_map/pallas_call | solution.py:487
  2.4 3.0 %collective-permute-start = (f32[2,128,128]{2,1,0:T(8,128)}, f32[2,128,128]{2,1,0:T(8,128)S(1)}, u32[]{:S(2)}, u32[]{:S(2)}) collective-permute-start(f32[2,128,128]{2,1,0:T(8,128)} %get-tuple-element.40), channel_id=1, source_target_pairs={{0,4},{4,8},{8,12},{12,16},{16,20},{20,24},{24,28},{28,0},{1,5},{5... | collective-permute-start | bytes 393224 | tf_op jit(solution)/shard_map/ppermute | solution.py:30
  5.5 3.1 %collective-permute-start.1 = (f32[2,128,128]{2,1,0:T(8,128)}, f32[2,128,128]{2,1,0:T(8,128)S(1)}, u32[]{:S(2)}, u32[]{:S(2)}) collective-permute-start(f32[2,128,128]{2,1,0:T(8,128)} %get-tuple-element.41), channel_id=1, source_target_pairs={{0,28},{4,0},{8,4},{12,8},{16,12},{20,16},{24,20},{28,24},{1,29},{... | collective-permute-start | bytes 393224 | tf_op jit(solution)/shard_map/ppermute | solution.py:30
  8.6 1.4 %copy-done.1 = bf16[4096,172]{0,1:T(8,128)(2,1)S(1)} copy-done((bf16[4096,172]{0,1:T(8,128)(2,1)S(1)}, bf16[4096,172]{0,1:T(8,128)(2,1)}, u32[]{:S(2)}) %copy-start.1) | copy-done | bytes 1409048
  9.9 1.0 %copy-done.2 = f32[8,128,128]{2,1,0:T(8,128)S(1)} copy-done((f32[8,128,128]{2,1,0:T(8,128)S(1)}, f32[8,128,128]{2,1,0:T(8,128)}, u32[]{:S(2)}) %copy-start.2) | copy-done | bytes 524312
  11.0 0.9 %copy-done.4 = f32[2,128,128]{2,1,0:T(8,128)S(1)} copy-done((f32[2,128,128]{2,1,0:T(8,128)S(1)}, f32[2,128,128]{2,1,0:T(8,128)}, u32[]{:S(2)}) %copy-start.4) | copy-done | bytes 131096
  11.9 0.1 shard_map.140
  12.8 0.1 concatenate.3.refs_0_.refs_1_.refs_5_
  12.9 0.6 collective-permute-done.1.refs_3_
  13.4 1.2 %shard_map.142 = (f32[2,128,128]{2,1,0:T(8,128)S(1)}, f32[2,128,128]{2,1,0:T(8,128)S(1)}, f32[2,128,128]{2,1,0:T(8,128)S(1)}, bf16[256,128]{1,0:T(8,128)(2,1)S(1)}) custom-call(s32[23]{0:T(128)S(1)} %concatenate.3.refs_0_.refs_1_.refs_5_, f32[2,128,128]{2,1,0:T(8,128)S(1)} %get-tuple-element.38.refs_0_.refs_1_, ...), custom_call_target="tpu_custom_call" | custom-call | flops 201326592 | bytes 1376256 | tf_op jit(solution)/shard_map/pallas_call | solution.py:530
  14.6 0.3 collective-permute-start.2
  15.0 4.4 %collective-permute-start.3 = (f32[2,128,128]{2,1,0:T(8,128)S(1)}, f32[2,128,128]{2,1,0:T(8,128)S(1)}, u32[]{:S(2)}, u32[]{:S(2)}) collective-permute-start(f32[2,128,128]{2,1,0:T(8,128)S(1)} %get-tuple-element.45), channel_id=1, source_target_pairs={{0,28},{4,0},{8,4},{12,8},{16,12},{20,16},{24,20},{28,24},{1,29},{... | collective-permute-start | bytes 393224 | tf_op jit(solution)/shard_map/ppermute | solution.py:30
  19.4 1.5 %collective-permute-start.5 = (bf16[272,128]{1,0:T(8,128)(2,1)S(1)}, bf16[272,128]{1,0:T(8,128)(2,1)S(1)}, u32[]{:S(2)}, u32[]{:S(2)}) collective-permute-start(bf16[272,128]{1,0:T(8,128)(2,1)S(1)} %copy-done.3), channel_id=1, source_target_pairs={{0,2},{1,3},{2,0},{3,1},{4,6},{5,7},{6,4},{7,5},{8,10},{9,11},{10,... | collective-permute-start | bytes 208904 | tf_op jit(solution)/shard_map/ppermute | solution.py:35
  20.9 0.6 shard_map.141.refs_0_.refs_3_
  21.5 0.6 collective-permute-start.6
  22.1 0.3 collective-permute-done.2.refs_3_
  22.5 1.1 %collective-permute-done.3.refs_4_ = f32[2,128,128]{2,1,0:T(8,128)S(1)} collective-permute-done((f32[2,128,128]{2,1,0:T(8,128)S(1)}, f32[2,128,128]{2,1,0:T(8,128)S(1)}, u32[]{:S(2)}, u32[]{:S(2)}) %collective-permute-start.3) | collective-permute-done | bytes 131104 | tf_op jit(solution)/shard_map/ppermute | solution.py:30
  23.6 1.2 %shard_map.143 = (f32[2,128,128]{2,1,0:T(8,128)S(1)}, f32[2,128,128]{2,1,0:T(8,128)S(1)}, f32[2,128,128]{2,1,0:T(8,128)S(1)}, bf16[256,128]{1,0:T(8,128)(2,1)S(1)}) custom-call(f32[172,256]{1,0:T(8,128)S(1)} %shard_map.141.refs_0_.refs_3_, s32[23]{0:T(128)S(1)} %concatenate.3.refs_0_.refs_1_.refs_5_, f32[2,128,128]{2,1,0:T(8,128)S(1)} %get-tuple-element.43.refs_2_.refs_0_, ...), custom_call_target="tpu_custom_call" | custom-call | flops 201326592 | bytes 1376256 | tf_op jit(solution)/shard_map/pallas_call | solution.py:530
  24.9 4.7 %collective-permute-start.12 = (f32[2,128,128]{2,1,0:T(8,128)S(1)}, f32[2,128,128]{2,1,0:T(8,128)S(1)}, u32[]{:S(2)}, u32[]{:S(2)}) collective-permute-start(f32[2,128,128]{2,1,0:T(8,128)S(1)} %get-tuple-element.51), channel_id=1, source_target_pairs={{0,28},{4,0},{8,4},{12,8},{16,12},{20,16},{24,20},{28,24},{1,29},{... | collective-permute-start | bytes 393224 | tf_op jit(solution)/shard_map/ppermute | solution.py:30
  29.6 0.5 collective-permute-start.9
  30.2 0.7 collective-permute-done.8.refs_4_.refs_2_
  30.8 1.5 %collective-permute-start.4 = (bf16[256,128]{1,0:T(8,128)(2,1)S(1)}, bf16[256,128]{1,0:T(8,128)(2,1)S(1)}, u32[]{:S(2)}, u32[]{:S(2)}) collective-permute-start(bf16[256,128]{1,0:T(8,128)(2,1)S(1)} %get-tuple-element.46.refs_4_), channel_id=1, source_target_pairs={{0,2},{1,3},{2,0},{3,1},{4,6},{5,7},{6,4},{7,5},{8,10},{9,11},{10,... | collective-permute-start | bytes 196616 | tf_op jit(solution)/shard_map/ppermute | solution.py:35
  32.3 0.6 shard_map.144.refs_5_
  32.9 0.4 shard_map.146.refs_1_.refs_6_
  33.3 0.6 shard_map.145.refs_0_.refs_2_
  34.0 1.2 %shard_map.147.refs_1_.refs_6_ = bf16[128,256]{1,0:T(8,128)(2,1)S(1)} custom-call(f32[172,256]{1,0:T(8,128)S(1)} %shard_map.145.refs_0_.refs_2_, s32[1,256]{1,0:T(1,128)S(1)} %shard_map.146.refs_1_.refs_6_, bf16[256,128]{1,0:T(8,128)(2,1)S(1)} %collective-permute-done.9.refs_2_.refs_3_, bf16[256,128]{1,0:T(8,128)(2,1)S(1)} %collective-permute-done.6.refs_1_.refs_3_, ...), custom_call_target="tpu_custom_call" | custom-call | flops 201326592 | bytes 196608 | tf_op jit(solution)/shard_map/pallas_call | solution.py:557
  35.2 0.8 %shard_map.148.refs_8_.refs_0_ = bf16[192,256]{1,0:T(8,128)(2,1)S(1)} custom-call(bf16[256,128]{1,0:T(8,128)(2,1)S(1)} %collective-permute-done.4.refs_0_.refs_5_, bf16[128,256]{1,0:T(8,128)(2,1)S(1)} %shard_map.147.refs_1_.refs_6_, f32[172,256]{1,0:T(8,128)S(1)} %shard_map.145.refs_0_.refs_2_, bf16[4,128,1024]{2,1,0:T(8,128)(2,1)S(1)} %copy-done, ...), custom_call_target="tpu_custom_call" | custom-call | flops 1000 | bytes 1000 | tf_op jit(solution)/shard_map/pallas_call | solution.py:565
  36.0 1.5 %collective-permute-start.14 = (bf16[192,256]{1,0:T(8,128)(2,1)S(1)}, bf16[192,256]{1,0:T(8,128)(2,1)S(1)}, u32[]{:S(2)}, u32[]{:S(2)}) collective-permute-start(bf16[192,256]{1,0:T(8,128)(2,1)S(1)} %shard_map.148.refs_8_.refs_0_), channel_id=1, source_target_pairs={{0,2},{1,3},{2,0},{3,1},{4,6},{5,7},{6,4},{7,5},{8,10},{9,11},{10,... | collective-permute-start | bytes 294920 | tf_op jit(solution)/shard_map/ppermute | solution.py:35
  37.5 0.2 collective-permute-start.16
  37.7 0.3 collective-permute-start.17
  38.0 0.5 collective-permute-start.15
  38.6 0.3 shard_map.149
  38.9 0.1 collective-permute-done.17.refs_7_
  39.0 1.8 %shard_map.150.refs_0_ = f32[8,304,128]{2,1,0:T(8,128)S(1)} custom-call(bf16[272,128]{1,0:T(8,128)(2,1)S(1)} %copy-done.3, bf16[272,128]{1,0:T(8,128)(2,1)S(1)} %collective-permute-done.7.refs_2_.refs_1_, bf16[256,128]{1,0:T(8,128)(2,1)S(1)} %get-tuple-element.48.refs_2_, bf16[256,128]{1,0:T(8,128)(2,1)S(1)} %collective-permute-done.9.refs_2_.refs_3_, ...), custom_call_target="tpu_custom_call" | custom-call | flops 1000 | bytes 1000 | tf_op jit(solution)/shard_map/pallas_call | solution.py:582
  40.7 1.9 %collective-permute-done.15.refs_7_ = bf16[128,256]{1,0:T(8,128)(2,1)S(1)} collective-permute-done((bf16[128,256]{1,0:T(8,128)(2,1)S(1)}, bf16[128,256]{1,0:T(8,128)(2,1)S(1)}, u32[]{:S(2)}, u32[]{:S(2)}) %collective-permute-start.15) | collective-permute-done | bytes 65568 | tf_op jit(solution)/shard_map/ppermute | solution.py:35
  42.6 0.5 collective-permute-start.19
  43.1 0.9 %collective-permute-done.19.refs_6_ = bf16[256,128]{1,0:T(8,128)(2,1)S(1)} collective-permute-done((bf16[256,128]{1,0:T(8,128)(2,1)S(1)}, bf16[256,128]{1,0:T(8,128)(2,1)S(1)}, u32[]{:S(2)}, u32[]{:S(2)}) %collective-permute-start.19) | collective-permute-done | bytes 65568 | tf_op jit(solution)/shard_map/ppermute | solution.py:35
  44.0 0.4 collective-permute-done.20.refs_8_
  44.4 1.9 %shard_map.152 = (f32[304,128]{1,0:T(8,128)S(1)}, f32[304,128]{1,0:T(8,128)S(1)}, f32[304,128]{1,0:T(8,128)S(1)}, f32[304,128]{1,0:T(8,128)S(1)}, bf16[304,128]{...) custom-call(f32[8,304,128]{2,1,0:T(8,128)S(1)} %shard_map.150.refs_0, ...), custom_call_target="tpu_custom_call" | custom-call | flops 771751936 | bytes 2801664 | tf_op jit(solution)/shard_map/pallas_call | solution.py:610
  46.3 0.1 collective-permute-start.22
  46.3 2.0 %collective-permute-start.21 = (bf16[304,128]{1,0:T(8,128)(2,1)S(1)}, bf16[304,128]{1,0:T(8,128)(2,1)S(1)}, u32[]{:S(2)}, u32[]{:S(2)}) collective-permute-start(bf16[304,128]{1,0:T(8,128)(2,1)S(1)} %get-tuple-element.58), channel_id=1, source_target_pairs={{0,4},{4,0},{8,12},{12,8},{16,20},{20,16},{24,28},{28,24},{1,5},{5... | collective-permute-start | bytes 233480 | tf_op jit(solution)/shard_map/ppermute | solution.py:35
  48.4 0.1 collective-permute-start.24
  48.4 1.9 %collective-permute-start.26 = (bf16[304,128]{1,0:T(8,128)(2,1)S(1)}, bf16[304,128]{1,0:T(8,128)(2,1)S(1)}, u32[]{:S(2)}, u32[]{:S(2)}) collective-permute-start(bf16[304,128]{1,0:T(8,128)(2,1)S(1)} %get-tuple-element.64), channel_id=1, source_target_pairs={{0,4},{4,0},{8,12},{12,8},{16,20},{20,16},{24,28},{28,24},{1,5},{5... | collective-permute-start | bytes 233480 | tf_op jit(solution)/shard_map/ppermute | solution.py:35
  50.4 1.1 %collective-permute-done.22 = bf16[304,128]{1,0:T(8,128)(2,1)S(1)} collective-permute-done((bf16[304,128]{1,0:T(8,128)(2,1)S(1)}, bf16[304,128]{1,0:T(8,128)(2,1)S(1)}, u32[]{:S(2)}, u32[]{:S(2)}) %collective-permute-start.22) | collective-permute-done | bytes 77856 | tf_op jit(solution)/shard_map/ppermute | solution.py:35
  51.6 1.6 %collective-permute-start.23 = (bf16[304,128]{1,0:T(8,128)(2,1)S(1)}, bf16[304,128]{1,0:T(8,128)(2,1)S(1)}, u32[]{:S(2)}, u32[]{:S(2)}) collective-permute-start(bf16[304,128]{1,0:T(8,128)(2,1)S(1)} %add_convert_fusion.2), channel_id=1, source_target_pairs={{0,24},{4,28},{8,16},{12,20},{16,8},{20,12},{24,0},{28,4},{1,25},{... | collective-permute-start | bytes 233480 | tf_op jit(solution)/shard_map/ppermute | solution.py:35
  53.1 1.7 %collective-permute-done.24 = bf16[304,128]{1,0:T(8,128)(2,1)S(1)} collective-permute-done((bf16[304,128]{1,0:T(8,128)(2,1)S(1)}, bf16[304,128]{1,0:T(8,128)(2,1)S(1)}, u32[]{:S(2)}, u32[]{:S(2)}) %collective-permute-start.24) | collective-permute-done | bytes 77856 | tf_op jit(solution)/shard_map/ppermute | solution.py:35
  54.9 1.7 %collective-permute-start.25 = (bf16[304,128]{1,0:T(8,128)(2,1)S(1)}, bf16[304,128]{1,0:T(8,128)(2,1)S(1)}, u32[]{:S(2)}, u32[]{:S(2)}) collective-permute-start(bf16[304,128]{1,0:T(8,128)(2,1)S(1)} %add_convert_fusion.1), channel_id=1, source_target_pairs={{0,16},{4,20},{8,24},{12,28},{16,0},{20,4},{24,8},{28,12},{1,17},{... | collective-permute-start | bytes 233480 | tf_op jit(solution)/shard_map/ppermute | solution.py:35
  56.6 1.1 %collective-permute-start.27 = (bf16[304,128]{1,0:T(8,128)(2,1)S(1)}, bf16[304,128]{1,0:T(8,128)(2,1)S(1)}, u32[]{:S(2)}, u32[]{:S(2)}) collective-permute-start(bf16[304,128]{1,0:T(8,128)(2,1)S(1)} %add_convert_fusion), channel_id=1, source_target_pairs={{0,8},{4,12},{8,0},{12,4},{16,24},{20,28},{24,16},{28,20},{1,9},{5... | collective-permute-start | bytes 233480 | tf_op jit(solution)/shard_map/ppermute | solution.py:35
  57.7 0.2 collective-permute-done.23
  57.9 2.4 %collective-permute-done.25 = bf16[304,128]{1,0:T(8,128)(2,1)S(1)} collective-permute-done((bf16[304,128]{1,0:T(8,128)(2,1)S(1)}, bf16[304,128]{1,0:T(8,128)(2,1)S(1)}, u32[]{:S(2)}, u32[]{:S(2)}) %collective-permute-start.25) | collective-permute-done | bytes 77856 | tf_op jit(solution)/shard_map/ppermute | solution.py:35
  60.3 0.8 %collective-permute-done.27 = bf16[304,128]{1,0:T(8,128)(2,1)S(1)} collective-permute-done((bf16[304,128]{1,0:T(8,128)(2,1)S(1)}, bf16[304,128]{1,0:T(8,128)(2,1)S(1)}, u32[]{:S(2)}, u32[]{:S(2)}) %collective-permute-start.27) | collective-permute-done | bytes 77856 | tf_op jit(solution)/shard_map/ppermute | solution.py:35
  61.2 1.0 %collective-permute-start.28 = (bf16[304,128]{1,0:T(8,128)(2,1)S(1)}, bf16[304,128]{1,0:T(8,128)(2,1)S(1)}, u32[]{:S(2)}, u32[]{:S(2)}) collective-permute-start(bf16[304,128]{1,0:T(8,128)(2,1)S(1)} %convert_add_fusion.refs_0_), channel_id=1, source_target_pairs={{0,8},{4,12},{8,0},{12,4},{16,24},{20,28},{24,16},{28,20},{1,9},{5... | collective-permute-start | bytes 233480 | tf_op jit(solution)/shard_map/ppermute | solution.py:35
  62.2 2.0 %collective-permute-start.29 = (bf16[304,128]{1,0:T(8,128)(2,1)S(1)}, bf16[304,128]{1,0:T(8,128)(2,1)S(1)}, u32[]{:S(2)}, u32[]{:S(2)}) collective-permute-start(bf16[304,128]{1,0:T(8,128)(2,1)S(1)} %convert_add_fusion.refs_0_), channel_id=1, source_target_pairs={{0,16},{4,20},{8,24},{12,28},{16,0},{20,4},{24,8},{28,12},{1,17},{... | collective-permute-start | bytes 233480 | tf_op jit(solution)/shard_map/ppermute | solution.py:35
  64.2 1.4 %collective-permute-start.30 = (bf16[304,128]{1,0:T(8,128)(2,1)S(1)}, bf16[304,128]{1,0:T(8,128)(2,1)S(1)}, u32[]{:S(2)}, u32[]{:S(2)}) collective-permute-start(bf16[304,128]{1,0:T(8,128)(2,1)S(1)} %convert_add_fusion.refs_0_), channel_id=1, source_target_pairs={{0,24},{4,28},{8,16},{12,20},{16,8},{20,12},{24,0},{28,4},{1,25},{... | collective-permute-start | bytes 233480 | tf_op jit(solution)/shard_map/ppermute | solution.py:35
  65.6 0.7 collective-permute-start.31
  66.3 1.3 %collective-permute-start.32 = (bf16[304,128]{1,0:T(8,128)(2,1)S(1)}, bf16[304,128]{1,0:T(8,128)(2,1)S(1)}, u32[]{:S(2)}, u32[]{:S(2)}) collective-permute-start(bf16[304,128]{1,0:T(8,128)(2,1)S(1)} %collective-permute-done.28.refs_1_), channel_id=1, source_target_pairs={{0,4},{4,0},{8,12},{12,8},{16,20},{20,16},{24,28},{28,24},{1,5},{5... | collective-permute-start | bytes 233480 | tf_op jit(solution)/shard_map/ppermute | solution.py:35
  67.7 1.0 %collective-permute-done.29.refs_2_ = bf16[304,128]{1,0:T(8,128)(2,1)S(1)} collective-permute-done((bf16[304,128]{1,0:T(8,128)(2,1)S(1)}, bf16[304,128]{1,0:T(8,128)(2,1)S(1)}, u32[]{:S(2)}, u32[]{:S(2)}) %collective-permute-start.29) | collective-permute-done | bytes 77856 | tf_op jit(solution)/shard_map/ppermute | solution.py:35
  68.6 1.7 %collective-permute-start.33 = (bf16[304,128]{1,0:T(8,128)(2,1)S(1)}, bf16[304,128]{1,0:T(8,128)(2,1)S(1)}, u32[]{:S(2)}, u32[]{:S(2)}) collective-permute-start(bf16[304,128]{1,0:T(8,128)(2,1)S(1)} %collective-permute-done.29.refs_2_), channel_id=1, source_target_pairs={{0,4},{4,0},{8,12},{12,8},{16,20},{20,16},{24,28},{28,24},{1,5},{5... | collective-permute-start | bytes 233480 | tf_op jit(solution)/shard_map/ppermute | solution.py:35
  70.4 1.5 %collective-permute-start.34 = (bf16[304,128]{1,0:T(8,128)(2,1)S(1)}, bf16[304,128]{1,0:T(8,128)(2,1)S(1)}, u32[]{:S(2)}, u32[]{:S(2)}) collective-permute-start(bf16[304,128]{1,0:T(8,128)(2,1)S(1)} %collective-permute-done.30.refs_3_), channel_id=1, source_target_pairs={{0,4},{4,0},{8,12},{12,8},{16,20},{20,16},{24,28},{28,24},{1,5},{5... | collective-permute-start | bytes 233480 | tf_op jit(solution)/shard_map/ppermute | solution.py:35
  71.9 0.8 %shard_map.151 = f32[1,256]{1,0:T(1,128)} custom-call(bf16[192,256]{1,0:T(8,128)(2,1)S(1)} %shard_map.148.refs_8_.refs_0_, bf16[192,256]{1,0:T(8,128)(2,1)S(1)} %collective-permute-done.13.refs_9_.refs_1_, bf16[192,256]{1,0:T(8,128)(2,1)S(1)} %collective-permute-done.14.refs_2_.refs_9_, bf16[192,256]{1,0:T(8,128)(2,1)S(1)} %collective-permute-done.18.refs_3_.refs_10_), custom_call_target="tpu_custom_call" | custom-call | flops 1000 | bytes 1000 | tf_op jit(solution)/shard_map/pallas_call | solution.py:599
  72.7 1.1 %shard_map.153 = (f32[4,128,256]{2,1,0:T(8,128)}, f32[172,1024]{1,0:T(8,128)}) custom-call(bf16[304,128]{1,0:T(8,128)(2,1)S(1)} %convert_add_fusion.refs_0_, bf16[304,128]{1,0:T(8,128)(2,1)S(1)} %collective-permute-done.28.refs_1_, bf16[304,128]{1,0:T(8,128)(2,1)S(1)} %collective-permute-done.29.refs_2_, ...), custom_call_target="tpu_custom_call" | custom-call | flops 1000 | bytes 1000 | tf_op jit(solution)/shard_map/pallas_call | solution.py:419
  73.9 0.8 shard_map.154
  74.6 0.2 collective-permute-done.34.refs_2_
  74.8 0.7 shard_map.155
  (52 shorter events, 0.4 us)
Async XLA Ops:
  0.6 12.1 %copy-start.6 = (s32[2]{0:T(128)S(1)}, s32[2]{0:T(128)}, u32[]{:S(2)}) copy-start(s32[2]{0:T(128)} %refs_0_.3) | copy-start | bytes 28
  0.6 12.1 %copy-start.7 = (s32[2]{0:T(128)S(1)}, s32[2]{0:T(128)}, u32[]{:S(2)}) copy-start(s32[2]{0:T(128)} %refs_1_.4) | copy-start | bytes 28
  0.7 12.1 %copy-start.8 = (s32[1,2]{1,0:T(1,128)S(1)}, s32[1,2]{1,0:T(1,128)}, u32[]{:S(2)}) copy-start(s32[1,2]{1,0:T(1,128)} %refs_2_.1) | copy-start | bytes 28
  0.7 12.1 %copy-start.9 = (s32[8]{0:T(128)S(1)}, s32[8]{0:T(128)}, u32[]{:S(2)}) copy-start(s32[8]{0:T(128)} %param.14) | copy-start | bytes 100
  0.7 12.1 %copy-start.10 = (s32[8]{0:T(128)S(1)}, s32[8]{0:T(128)}, u32[]{:S(2)}) copy-start(s32[8]{0:T(128)} %param.15) | copy-start | bytes 100
  2.4 10.4 %collective-permute-start = (f32[2,128,128]{2,1,0:T(8,128)}, f32[2,128,128]{2,1,0:T(8,128)S(1)}, u32[]{:S(2)}, u32[]{:S(2)}) collective-permute-start(f32[2,128,128]{2,1,0:T(8,128)} %get-tuple-element.40), channel_id=1, source_target_pairs={{0,4},{4,8},{8,12},{12,16},{16,20},{20,24},{24,28},{28,0},{1,5},{5... | collective-permute-start | bytes 393224 | tf_op jit(solution)/shard_map/ppermute | solution.py:30
  5.5 8.0 %collective-permute-start.1 = (f32[2,128,128]{2,1,0:T(8,128)}, f32[2,128,128]{2,1,0:T(8,128)S(1)}, u32[]{:S(2)}, u32[]{:S(2)}) collective-permute-start(f32[2,128,128]{2,1,0:T(8,128)} %get-tuple-element.41), channel_id=1, source_target_pairs={{0,28},{4,0},{8,4},{12,8},{16,12},{20,16},{24,20},{28,24},{1,29},{... | collective-permute-start | bytes 393224 | tf_op jit(solution)/shard_map/ppermute | solution.py:30
  8.6 1.4 %copy-start.1 = (bf16[4096,172]{0,1:T(8,128)(2,1)S(1)}, bf16[4096,172]{0,1:T(8,128)(2,1)}, u32[]{:S(2)}) copy-start(bf16[4096,172]{0,1:T(8,128)(2,1)} %param.23) | copy-start | bytes 4227076
  9.9 1.0 %copy-start.2 = (f32[8,128,128]{2,1,0:T(8,128)S(1)}, f32[8,128,128]{2,1,0:T(8,128)}, u32[]{:S(2)}) copy-start(f32[8,128,128]{2,1,0:T(8,128)} %refs_1_.5) | copy-start | bytes 1572868
  11.0 0.9 %copy-start.4 = (f32[2,128,128]{2,1,0:T(8,128)S(1)}, f32[2,128,128]{2,1,0:T(8,128)}, u32[]{:S(2)}) copy-start(f32[2,128,128]{2,1,0:T(8,128)} %get-tuple-element.37.refs_0_) | copy-start | bytes 393220
  11.9 7.5 %copy-start.3 = (bf16[272,128]{1,0:T(8,128)(2,1)S(1)}, bf16[272,128]{1,0:T(8,128)(2,1)}, u32[]{:S(2)}) copy-start(bf16[272,128]{1,0:T(8,128)(2,1)} %get-tuple-element.47.refs_1_.refs_0_) | copy-start | bytes 208900
  11.9 9.0 %copy-start = (bf16[4,128,1024]{2,1,0:T(8,128)(2,1)S(1)}, bf16[4,128,1024]{2,1,0:T(8,128)(2,1)}, u32[]{:S(2)}) copy-start(bf16[4,128,1024]{2,1,0:T(8,128)(2,1)} %refs_11_.1) | copy-start | bytes 3145732
  14.6 7.8 %collective-permute-start.2 = (f32[2,128,128]{2,1,0:T(8,128)S(1)}, f32[2,128,128]{2,1,0:T(8,128)S(1)}, u32[]{:S(2)}, u32[]{:S(2)}) collective-permute-start(f32[2,128,128]{2,1,0:T(8,128)S(1)} %get-tuple-element.44), channel_id=1, source_target_pairs={{0,4},{4,8},{8,12},{12,16},{16,20},{20,24},{24,28},{28,0},{1,5},{5... | collective-permute-start | bytes 393224 | tf_op jit(solution)/shard_map/ppermute | solution.py:30
  15.0 8.6 %collective-permute-start.3 = (f32[2,128,128]{2,1,0:T(8,128)S(1)}, f32[2,128,128]{2,1,0:T(8,128)S(1)}, u32[]{:S(2)}, u32[]{:S(2)}) collective-permute-start(f32[2,128,128]{2,1,0:T(8,128)S(1)} %get-tuple-element.45), channel_id=1, source_target_pairs={{0,28},{4,0},{8,4},{12,8},{16,12},{20,16},{24,20},{28,24},{1,29},{... | collective-permute-start | bytes 393224 | tf_op jit(solution)/shard_map/ppermute | solution.py:30
  19.4 10.1 %collective-permute-start.5 = (bf16[272,128]{1,0:T(8,128)(2,1)S(1)}, bf16[272,128]{1,0:T(8,128)(2,1)S(1)}, u32[]{:S(2)}, u32[]{:S(2)}) collective-permute-start(bf16[272,128]{1,0:T(8,128)(2,1)S(1)} %copy-done.3), channel_id=1, source_target_pairs={{0,2},{1,3},{2,0},{3,1},{4,6},{5,7},{6,4},{7,5},{8,10},{9,11},{10,... | collective-permute-start | bytes 208904 | tf_op jit(solution)/shard_map/ppermute | solution.py:35
  20.9 8.7 %collective-permute-start.7 = (bf16[272,128]{1,0:T(8,128)(2,1)S(1)}, bf16[272,128]{1,0:T(8,128)(2,1)S(1)}, u32[]{:S(2)}, u32[]{:S(2)}) collective-permute-start(bf16[272,128]{1,0:T(8,128)(2,1)S(1)} %copy-done.3), channel_id=1, source_target_pairs={{0,1},{1,0},{2,3},{3,2},{4,5},{5,4},{6,7},{7,6},{8,9},{9,8},{10,11... | collective-permute-start | bytes 208904 | tf_op jit(solution)/shard_map/ppermute | solution.py:35
  21.5 8.6 %collective-permute-start.6 = (bf16[256,128]{1,0:T(8,128)(2,1)S(1)}, bf16[256,128]{1,0:T(8,128)(2,1)S(1)}, u32[]{:S(2)}, u32[]{:S(2)}) collective-permute-start(bf16[256,128]{1,0:T(8,128)(2,1)S(1)} %get-tuple-element.48.refs_2_), channel_id=1, source_target_pairs={{0,2},{1,3},{2,0},{3,1},{4,6},{5,7},{6,4},{7,5},{8,10},{9,11},{10,... | collective-permute-start | bytes 196616 | tf_op jit(solution)/shard_map/ppermute | solution.py:35
  24.8 9.2 %collective-permute-start.11 = (f32[2,128,128]{2,1,0:T(8,128)S(1)}, f32[2,128,128]{2,1,0:T(8,128)S(1)}, u32[]{:S(2)}, u32[]{:S(2)}) collective-permute-start(f32[2,128,128]{2,1,0:T(8,128)S(1)} %get-tuple-element.50), channel_id=1, source_target_pairs={{0,4},{4,8},{8,12},{12,16},{16,20},{20,24},{24,28},{28,0},{1,5},{5... | collective-permute-start | bytes 393224 | tf_op jit(solution)/shard_map/ppermute | solution.py:30
  24.9 9.1 %collective-permute-start.12 = (f32[2,128,128]{2,1,0:T(8,128)S(1)}, f32[2,128,128]{2,1,0:T(8,128)S(1)}, u32[]{:S(2)}, u32[]{:S(2)}) collective-permute-start(f32[2,128,128]{2,1,0:T(8,128)S(1)} %get-tuple-element.51), channel_id=1, source_target_pairs={{0,28},{4,0},{8,4},{12,8},{16,12},{20,16},{24,20},{28,24},{1,29},{... | collective-permute-start | bytes 393224 | tf_op jit(solution)/shard_map/ppermute | solution.py:30
  29.6 1.3 %collective-permute-start.8 = (bf16[272,128]{1,0:T(8,128)(2,1)S(1)}, bf16[272,128]{1,0:T(8,128)(2,1)S(1)}, u32[]{:S(2)}, u32[]{:S(2)}) collective-permute-start(bf16[272,128]{1,0:T(8,128)(2,1)S(1)} %collective-permute-done.5.refs_0_.refs_3_.refs_1_), channel_id=1, source_target_pairs={{0,1},{1,0},{2,3},{3,2},{4,5},{5,4},{6,7},{7,6},{8,9},{9,8},{10,11... | collective-permute-start | bytes 208904 | tf_op jit(solution)/shard_map/ppermute | solution.py:35
  29.6 4.3 %collective-permute-start.9 = (bf16[256,128]{1,0:T(8,128)(2,1)S(1)}, bf16[256,128]{1,0:T(8,128)(2,1)S(1)}, u32[]{:S(2)}, u32[]{:S(2)}) collective-permute-start(bf16[256,128]{1,0:T(8,128)(2,1)S(1)} %get-tuple-element.48.refs_2_), channel_id=1, source_target_pairs={{0,1},{1,0},{2,3},{3,2},{4,5},{5,4},{6,7},{7,6},{8,9},{9,8},{10,11... | collective-permute-start | bytes 196616 | tf_op jit(solution)/shard_map/ppermute | solution.py:35
  30.1 3.8 %collective-permute-start.10 = (bf16[256,128]{1,0:T(8,128)(2,1)S(1)}, bf16[256,128]{1,0:T(8,128)(2,1)S(1)}, u32[]{:S(2)}, u32[]{:S(2)}) collective-permute-start(bf16[256,128]{1,0:T(8,128)(2,1)S(1)} %collective-permute-done.6.refs_1_.refs_3_), channel_id=1, source_target_pairs={{0,1},{1,0},{2,3},{3,2},{4,5},{5,4},{6,7},{7,6},{8,9},{9,8},{10,11... | collective-permute-start | bytes 196616 | tf_op jit(solution)/shard_map/ppermute | solution.py:35
  30.8 2.1 %copy-start.5 = (s32[1,256]{1,0:T(1,128)S(1)}, s32[1,256]{1,0:T(1,128)}, u32[]{:S(2)}) copy-start(s32[1,256]{1,0:T(1,128)} %refs_5_.1) | copy-start | bytes 3076
  30.8 4.3 %collective-permute-start.4 = (bf16[256,128]{1,0:T(8,128)(2,1)S(1)}, bf16[256,128]{1,0:T(8,128)(2,1)S(1)}, u32[]{:S(2)}, u32[]{:S(2)}) collective-permute-start(bf16[256,128]{1,0:T(8,128)(2,1)S(1)} %get-tuple-element.46.refs_4_), channel_id=1, source_target_pairs={{0,2},{1,3},{2,0},{3,1},{4,6},{5,7},{6,4},{7,5},{8,10},{9,11},{10,... | collective-permute-start | bytes 196616 | tf_op jit(solution)/shard_map/ppermute | solution.py:35
  36.0 3.0 %collective-permute-start.13 = (bf16[192,256]{1,0:T(8,128)(2,1)S(1)}, bf16[192,256]{1,0:T(8,128)(2,1)S(1)}, u32[]{:S(2)}, u32[]{:S(2)}) collective-permute-start(bf16[192,256]{1,0:T(8,128)(2,1)S(1)} %shard_map.148.refs_8_.refs_0_), channel_id=1, source_target_pairs={{0,1},{1,0},{2,3},{3,2},{4,5},{5,4},{6,7},{7,6},{8,9},{9,8},{10,11... | collective-permute-start | bytes 294920 | tf_op jit(solution)/shard_map/ppermute | solution.py:35
  36.0 6.6 %collective-permute-start.14 = (bf16[192,256]{1,0:T(8,128)(2,1)S(1)}, bf16[192,256]{1,0:T(8,128)(2,1)S(1)}, u32[]{:S(2)}, u32[]{:S(2)}) collective-permute-start(bf16[192,256]{1,0:T(8,128)(2,1)S(1)} %shard_map.148.refs_8_.refs_0_), channel_id=1, source_target_pairs={{0,2},{1,3},{2,0},{3,1},{4,6},{5,7},{6,4},{7,5},{8,10},{9,11},{10,... | collective-permute-start | bytes 294920 | tf_op jit(solution)/shard_map/ppermute | solution.py:35
  37.5 1.3 %collective-permute-start.16 = (bf16[256,128]{1,0:T(8,128)(2,1)S(1)}, bf16[256,128]{1,0:T(8,128)(2,1)S(1)}, u32[]{:S(2)}, u32[]{:S(2)}) collective-permute-start(bf16[256,128]{1,0:T(8,128)(2,1)S(1)} %get-tuple-element.46.refs_4_), channel_id=1, source_target_pairs={{0,1},{1,0},{2,3},{3,2},{4,5},{5,4},{6,7},{7,6},{8,9},{9,8},{10,11... | collective-permute-start | bytes 196616 | tf_op jit(solution)/shard_map/ppermute | solution.py:35
  37.7 1.3 %collective-permute-start.17 = (bf16[128,256]{1,0:T(8,128)(2,1)S(1)}, bf16[128,256]{1,0:T(8,128)(2,1)S(1)}, u32[]{:S(2)}, u32[]{:S(2)}) collective-permute-start(bf16[128,256]{1,0:T(8,128)(2,1)S(1)} %shard_map.147.refs_1_.refs_6_), channel_id=1, source_target_pairs={{0,1},{1,0},{2,3},{3,2},{4,5},{5,4},{6,7},{7,6},{8,9},{9,8},{10,11... | collective-permute-start | bytes 196616 | tf_op jit(solution)/shard_map/ppermute | solution.py:35
  38.0 4.6 %collective-permute-start.15 = (bf16[128,256]{1,0:T(8,128)(2,1)S(1)}, bf16[128,256]{1,0:T(8,128)(2,1)S(1)}, u32[]{:S(2)}, u32[]{:S(2)}) collective-permute-start(bf16[128,256]{1,0:T(8,128)(2,1)S(1)} %shard_map.147.refs_1_.refs_6_), channel_id=1, source_target_pairs={{0,2},{1,3},{2,0},{3,1},{4,6},{5,7},{6,4},{7,5},{8,10},{9,11},{10,... | collective-permute-start | bytes 196616 | tf_op jit(solution)/shard_map/ppermute | solution.py:35
  42.6 1.8 %collective-permute-start.18 = (bf16[192,256]{1,0:T(8,128)(2,1)S(1)}, bf16[192,256]{1,0:T(8,128)(2,1)S(1)}, u32[]{:S(2)}, u32[]{:S(2)}) collective-permute-start(bf16[192,256]{1,0:T(8,128)(2,1)S(1)} %collective-permute-done.14.refs_2_.refs_9_), channel_id=1, source_target_pairs={{0,1},{1,0},{2,3},{3,2},{4,5},{5,4},{6,7},{7,6},{8,9},{9,8},{10,11... | collective-permute-start | bytes 294920 | tf_op jit(solution)/shard_map/ppermute | solution.py:35
  42.6 1.4 %collective-permute-start.19 = (bf16[256,128]{1,0:T(8,128)(2,1)S(1)}, bf16[256,128]{1,0:T(8,128)(2,1)S(1)}, u32[]{:S(2)}, u32[]{:S(2)}) collective-permute-start(bf16[256,128]{1,0:T(8,128)(2,1)S(1)} %collective-permute-done.4.refs_0_.refs_5_), channel_id=1, source_target_pairs={{0,1},{1,0},{2,3},{3,2},{4,5},{5,4},{6,7},{7,6},{8,9},{9,8},{10,11... | collective-permute-start | bytes 196616 | tf_op jit(solution)/shard_map/ppermute | solution.py:35
  43.1 1.3 %collective-permute-start.20 = (bf16[128,256]{1,0:T(8,128)(2,1)S(1)}, bf16[128,256]{1,0:T(8,128)(2,1)S(1)}, u32[]{:S(2)}, u32[]{:S(2)}) collective-permute-start(bf16[128,256]{1,0:T(8,128)(2,1)S(1)} %collective-permute-done.15.refs_7_), channel_id=1, source_target_pairs={{0,1},{1,0},{2,3},{3,2},{4,5},{5,4},{6,7},{7,6},{8,9},{9,8},{10,11... | collective-permute-start | bytes 196616 | tf_op jit(solution)/shard_map/ppermute | solution.py:35
  46.3 5.3 %collective-permute-start.22 = (bf16[304,128]{1,0:T(8,128)(2,1)S(1)}, bf16[304,128]{1,0:T(8,128)(2,1)S(1)}, u32[]{:S(2)}, u32[]{:S(2)}) collective-permute-start(bf16[304,128]{1,0:T(8,128)(2,1)S(1)} %get-tuple-element.60), channel_id=1, source_target_pairs={{0,4},{4,0},{8,12},{12,8},{16,20},{20,16},{24,28},{28,24},{1,5},{5... | collective-permute-start | bytes 233480 | tf_op jit(solution)/shard_map/ppermute | solution.py:35
  46.3 11.4 %collective-permute-start.21 = (bf16[304,128]{1,0:T(8,128)(2,1)S(1)}, bf16[304,128]{1,0:T(8,128)(2,1)S(1)}, u32[]{:S(2)}, u32[]{:S(2)}) collective-permute-start(bf16[304,128]{1,0:T(8,128)(2,1)S(1)} %get-tuple-element.58), channel_id=1, source_target_pairs={{0,4},{4,0},{8,12},{12,8},{16,20},{20,16},{24,28},{28,24},{1,5},{5... | collective-permute-start | bytes 233480 | tf_op jit(solution)/shard_map/ppermute | solution.py:35
  48.4 6.5 %collective-permute-start.24 = (bf16[304,128]{1,0:T(8,128)(2,1)S(1)}, bf16[304,128]{1,0:T(8,128)(2,1)S(1)}, u32[]{:S(2)}, u32[]{:S(2)}) collective-permute-start(bf16[304,128]{1,0:T(8,128)(2,1)S(1)} %get-tuple-element.62), channel_id=1, source_target_pairs={{0,4},{4,0},{8,12},{12,8},{16,20},{20,16},{24,28},{28,24},{1,5},{5... | collective-permute-start | bytes 233480 | tf_op jit(solution)/shard_map/ppermute | solution.py:35
  48.4 8.2 %collective-permute-start.26 = (bf16[304,128]{1,0:T(8,128)(2,1)S(1)}, bf16[304,128]{1,0:T(8,128)(2,1)S(1)}, u32[]{:S(2)}, u32[]{:S(2)}) collective-permute-start(bf16[304,128]{1,0:T(8,128)(2,1)S(1)} %get-tuple-element.64), channel_id=1, source_target_pairs={{0,4},{4,0},{8,12},{12,8},{16,20},{20,16},{24,28},{28,24},{1,5},{5... | collective-permute-start | bytes 233480 | tf_op jit(solution)/shard_map/ppermute | solution.py:35
  51.6 6.4 %collective-permute-start.23 = (bf16[304,128]{1,0:T(8,128)(2,1)S(1)}, bf16[304,128]{1,0:T(8,128)(2,1)S(1)}, u32[]{:S(2)}, u32[]{:S(2)}) collective-permute-start(bf16[304,128]{1,0:T(8,128)(2,1)S(1)} %add_convert_fusion.2), channel_id=1, source_target_pairs={{0,24},{4,28},{8,16},{12,20},{16,8},{20,12},{24,0},{28,4},{1,25},{... | collective-permute-start | bytes 233480 | tf_op jit(solution)/shard_map/ppermute | solution.py:35
  54.9 5.4 %collective-permute-start.25 = (bf16[304,128]{1,0:T(8,128)(2,1)S(1)}, bf16[304,128]{1,0:T(8,128)(2,1)S(1)}, u32[]{:S(2)}, u32[]{:S(2)}) collective-permute-start(bf16[304,128]{1,0:T(8,128)(2,1)S(1)} %add_convert_fusion.1), channel_id=1, source_target_pairs={{0,16},{4,20},{8,24},{12,28},{16,0},{20,4},{24,8},{28,12},{1,17},{... | collective-permute-start | bytes 233480 | tf_op jit(solution)/shard_map/ppermute | solution.py:35
  56.6 4.5 %collective-permute-start.27 = (bf16[304,128]{1,0:T(8,128)(2,1)S(1)}, bf16[304,128]{1,0:T(8,128)(2,1)S(1)}, u32[]{:S(2)}, u32[]{:S(2)}) collective-permute-start(bf16[304,128]{1,0:T(8,128)(2,1)S(1)} %add_convert_fusion), channel_id=1, source_target_pairs={{0,8},{4,12},{8,0},{12,4},{16,24},{20,28},{24,16},{28,20},{1,9},{5... | collective-permute-start | bytes 233480 | tf_op jit(solution)/shard_map/ppermute | solution.py:35
  61.2 5.2 %collective-permute-start.28 = (bf16[304,128]{1,0:T(8,128)(2,1)S(1)}, bf16[304,128]{1,0:T(8,128)(2,1)S(1)}, u32[]{:S(2)}, u32[]{:S(2)}) collective-permute-start(bf16[304,128]{1,0:T(8,128)(2,1)S(1)} %convert_add_fusion.refs_0_), channel_id=1, source_target_pairs={{0,8},{4,12},{8,0},{12,4},{16,24},{20,28},{24,16},{28,20},{1,9},{5... | collective-permute-start | bytes 233480 | tf_op jit(solution)/shard_map/ppermute | solution.py:35
  62.2 6.4 %collective-permute-start.29 = (bf16[304,128]{1,0:T(8,128)(2,1)S(1)}, bf16[304,128]{1,0:T(8,128)(2,1)S(1)}, u32[]{:S(2)}, u32[]{:S(2)}) collective-permute-start(bf16[304,128]{1,0:T(8,128)(2,1)S(1)} %convert_add_fusion.refs_0_), channel_id=1, source_target_pairs={{0,16},{4,20},{8,24},{12,28},{16,0},{20,4},{24,8},{28,12},{1,17},{... | collective-permute-start | bytes 233480 | tf_op jit(solution)/shard_map/ppermute | solution.py:35
  64.2 6.2 %collective-permute-start.30 = (bf16[304,128]{1,0:T(8,128)(2,1)S(1)}, bf16[304,128]{1,0:T(8,128)(2,1)S(1)}, u32[]{:S(2)}, u32[]{:S(2)}) collective-permute-start(bf16[304,128]{1,0:T(8,128)(2,1)S(1)} %convert_add_fusion.refs_0_), channel_id=1, source_target_pairs={{0,24},{4,28},{8,16},{12,20},{16,8},{20,12},{24,0},{28,4},{1,25},{... | collective-permute-start | bytes 233480 | tf_op jit(solution)/shard_map/ppermute | solution.py:35
  65.6 7.1 %collective-permute-start.31 = (bf16[304,128]{1,0:T(8,128)(2,1)S(1)}, bf16[304,128]{1,0:T(8,128)(2,1)S(1)}, u32[]{:S(2)}, u32[]{:S(2)}) collective-permute-start(bf16[304,128]{1,0:T(8,128)(2,1)S(1)} %convert_add_fusion.refs_0_), channel_id=1, source_target_pairs={{0,4},{4,0},{8,12},{12,8},{16,20},{20,16},{24,28},{28,24},{1,5},{5... | collective-permute-start | bytes 233480 | tf_op jit(solution)/shard_map/ppermute | solution.py:35
  66.3 6.4 %collective-permute-start.32 = (bf16[304,128]{1,0:T(8,128)(2,1)S(1)}, bf16[304,128]{1,0:T(8,128)(2,1)S(1)}, u32[]{:S(2)}, u32[]{:S(2)}) collective-permute-start(bf16[304,128]{1,0:T(8,128)(2,1)S(1)} %collective-permute-done.28.refs_1_), channel_id=1, source_target_pairs={{0,4},{4,0},{8,12},{12,8},{16,20},{20,16},{24,28},{28,24},{1,5},{5... | collective-permute-start | bytes 233480 | tf_op jit(solution)/shard_map/ppermute | solution.py:35
  68.6 5.2 %collective-permute-start.33 = (bf16[304,128]{1,0:T(8,128)(2,1)S(1)}, bf16[304,128]{1,0:T(8,128)(2,1)S(1)}, u32[]{:S(2)}, u32[]{:S(2)}) collective-permute-start(bf16[304,128]{1,0:T(8,128)(2,1)S(1)} %collective-permute-done.29.refs_2_), channel_id=1, source_target_pairs={{0,4},{4,0},{8,12},{12,8},{16,20},{20,16},{24,28},{28,24},{1,5},{5... | collective-permute-start | bytes 233480 | tf_op jit(solution)/shard_map/ppermute | solution.py:35
  70.4 4.4 %collective-permute-start.34 = (bf16[304,128]{1,0:T(8,128)(2,1)S(1)}, bf16[304,128]{1,0:T(8,128)(2,1)S(1)}, u32[]{:S(2)}, u32[]{:S(2)}) collective-permute-start(bf16[304,128]{1,0:T(8,128)(2,1)S(1)} %collective-permute-done.30.refs_3_), channel_id=1, source_target_pairs={{0,4},{4,0},{8,12},{12,8},{16,20},{20,16},{24,28},{28,24},{1,5},{5... | collective-permute-start | bytes 233480 | tf_op jit(solution)/shard_map/ppermute | solution.py:35
